TPU v7x, 32 devices: a whole 2x2x4 slice. The times are simulated.
32 devices in a mesh: grp: 2 (over y), row: 4 (over z), col: 2 (over x), pair: 2 (over core).
Axes of the slice: x: 2, y: 2, z: 4, core: 2. Of those that a mesh axis runs over, the one named last changes fastest.
Arguments:
- features_in: bfloat16 [128, 32, 512], P('grp', 'row', ('col', 'pair')), parts along dimension 0, may hold values from -8 to 8
- filters_one: bfloat16 [64, 3, 3, 64], replicated, may hold values from -0.25 to 0.25
- filters_two: bfloat16 [512, 3, 3, 256], P('row'), may hold values from -0.125 to 0.125
- out_grad: bfloat16 [1024, 128, 8], P(('grp', 'row'), ('col', 'pair')), parts along dimension 0, may hold values from -24 to 24
Outputs:
- input_grad: bfloat16 [128, 32, 512], P('grp', 'row', ('col', 'pair')), parts along dimension 0
- grad_one: float32 [128, 3, 3, 64], P('grp'), parts along dimension 0
- grad_two: float32 [1024, 3, 3, 256], P(('grp', 'row')), parts along dimension 0
There are 2 independent parts, one for each index of `grp`. A program takes and returns all parts, laid end to end along the dimension named above; an argument that names none is the same for every part. Nothing has to cross between parts.
All inputs are finite; a program needn't handle non-finite values.
Results may differ from a plain program's by a relative error of at most 0.015.
Values may be sent and summed in bfloat16 or wider, within the bound.
No kernel may reach another device: no remote copies, remote signals or barrier semaphores. Data moves between devices by JAX's collectives and lax.ppermute only.
A program may use at most 64 MiB of HBM per device.

v0:
```python
import math

import jax
import jax.numpy as jnp
from jax import lax
from jax.sharding import PartitionSpec as P


def padded_2(cells, sides, width):
    for axis, dim in sides:
        count = lax.axis_size(axis)
        ends = count - 1
        head = lax.slice_in_dim(cells, 0, width, axis=dim)
        tail = lax.slice_in_dim(cells, cells.shape[dim] - width, cells.shape[dim], axis=dim)
        cells = jnp.concatenate(
            [
                lax.ppermute(tail, axis, [(i, (i + 1) % count) for i in range(ends)]),
                cells,
                lax.ppermute(head, axis, [((i + 1) % count, i) for i in range(ends)]),
            ],
            axis=dim,
        )
    return cells


def conv_valid(padded, kernel):
    return lax.conv_general_dilated(
        padded[None],
        kernel,
        (1, 1),
        "VALID",
        dimension_numbers=("NCHW", "OHWI", "NCHW"),
        preferred_element_type=jnp.float32,
    )[0]


def flip_kernel(kernel):
    return jnp.transpose(kernel[:, ::-1, ::-1, :], (3, 1, 2, 0))


def silu_slope(values):
    sigmoid_value = jax.nn.sigmoid(values)
    return sigmoid_value * (1.0 + values * (1.0 - sigmoid_value))


def tap_grads(gradient, padded):
    row_count, col_count = (gradient.shape[1], gradient.shape[2])
    tap_list = []
    for first_tap in range(3):
        tap_row = []
        for second_tap in range(3):
            window = padded[
                :, first_tap : first_tap + row_count, second_tap : second_tap + col_count
            ]
            tap_row.append(
                jnp.einsum("ohw,chw->oc", gradient, window, preferred_element_type=jnp.float32)
            )
        tap_list.append(jnp.stack(tap_row, 1))
    return jnp.stack(tap_list, 1)


def pool_columns(active):
    channels, row_count, col_count = active.shape
    folded = active.reshape(channels, row_count // 4, 2, 2, col_count // 4, 2, 2).mean(axis=(3, 6))
    return jnp.transpose(folded, (0, 2, 4, 3, 1)).reshape(
        channels * 4, col_count // 4, row_count // 4
    )


def unpool_columns(gradient):
    quad_count, col_count, row_count = gradient.shape
    ordered = jnp.transpose(
        gradient.reshape(quad_count // 4, 2, 2, col_count, row_count), (0, 4, 1, 3, 2)
    )
    spread = (
        jnp.broadcast_to(
            ordered[:, :, :, None, :, :, None], (quad_count // 4, row_count, 2, 2, col_count, 2, 2)
        )
        * 0.25
    )
    return spread.reshape(quad_count // 4, row_count * 4, col_count * 4)


def local(features_in, filters_one, filters_two, out_grad):
    band_rows = features_in.shape[1]
    strip_cols = features_in.shape[2]
    height = band_rows * lax.axis_size("row")
    width = strip_cols * lax.axis_size(("col", "pair"))
    padded_in = padded_2(features_in, (("row", 1), (("col", "pair"), 2)), 1)
    pre_one = conv_valid(padded_in, filters_one)
    pooled = pool_columns(jax.nn.silu(pre_one)).astype(jnp.bfloat16)
    with_edges = padded_2(pooled, ((("col", "pair"), 1),), 1)
    column_strip = lax.all_gather(with_edges, "row", axis=2, tiled=True)
    strip_padded = jnp.pad(column_strip, ((0, 0), (0, 0), (1, 1)))
    swapped = jnp.transpose(filters_two, (0, 2, 1, 3))
    pre_two = conv_valid(strip_padded, swapped)
    grad_pre_two = (out_grad.astype(jnp.float32) * silu_slope(pre_two)).astype(jnp.bfloat16)
    pooled_height = column_strip.shape[2]
    pooled_width = strip_cols // 4 * lax.axis_size(("col", "pair"))
    local_two = jnp.transpose(tap_grads(grad_pre_two, strip_padded), (0, 2, 1, 3))
    grad_two = lax.psum(local_two, ("col", "pair")) / math.sqrt(pooled_height * pooled_width)
    padded_grad = jnp.pad(grad_pre_two, ((0, 0), (2, 2), (1, 1)))
    spread_grad = conv_valid(padded_grad, flip_kernel(swapped))
    with_ghosts = padded_2(spread_grad, ((("col", "pair"), 1),), 1)
    real_columns = spread_grad[:, 1:-1, :]
    real_columns = real_columns.at[:, 0, :].add(with_ghosts[:, 0, :])
    real_columns = real_columns.at[:, -1, :].add(with_ghosts[:, -1, :])
    grad_pooled = lax.psum_scatter(real_columns, "row", scatter_dimension=2, tiled=True)
    grad_pre_one = (unpool_columns(grad_pooled) * silu_slope(pre_one)).astype(jnp.bfloat16)
    local_one = tap_grads(grad_pre_one, padded_in)
    grad_one = lax.psum(local_one, ("row", "col", "pair")) / math.sqrt(height * width)
    rimmed_one = padded_2(grad_pre_one, (("row", 1), (("col", "pair"), 2)), 1)
    input_grad = conv_valid(rimmed_one, flip_kernel(filters_one)).astype(jnp.bfloat16)
    return (input_grad, grad_one, grad_two)


def solution(mesh):
    in_specs = (
        P("grp", "row", ("col", "pair")),
        P(),
        P("row", None, None, None),
        P(("grp", "row"), ("col", "pair"), None),
    )
    out_specs = (
        P("grp", "row", ("col", "pair")),
        P("grp", None, None, None),
        P(("grp", "row"), None, None, None),
    )
    return jax.shard_map(local, mesh=mesh, in_specs=in_specs, out_specs=out_specs, check_vma=False)
```

profile of v0, /device:TPU:0, one launch (start us, length us, event | category | flops | bytes accessed | tf_op | source)
XLA Modules:
  0.0 211.8 jit_solution(14888131075437018906)
XLA Ops:
  9.1 4.9 %collective-permute-start = (bf16[64,1,128]{2,0,1:T(8,128)(2,1)S(1)}, bf16[64,1,128]{2,0,1:T(8,128)(2,1)S(1)}, u32[]{:S(2)}, u32[]{:S(2)}) collective-permute-start(bf16[64,1,128]{2,0,1:T(8,128)(2,1)S(1)} %get-tuple-element.58), channel_id=1, source_target_pairs={{0,4},{4,8},{8,12},{1,5},{5,9},{9,13},{2,6},{6,10},{10,14},{3,7},{... | collective-permute-start | bytes 49160 | tf_op jit(solution)/shard_map/ppermute | solution.py:17
  14.0 1.3 collective-permute-start.1
  16.4 3.3 %collective-permute-done.1 = bf16[64,1,128]{2,0,1:T(8,128)(2,1)S(1)} collective-permute-done((bf16[64,1,128]{2,0,1:T(8,128)(2,1)S(1)}, bf16[64,1,128]{2,0,1:T(8,128)(2,1)S(1)}, u32[]{:S(2)}, u32[]{:S(2)}) %collective-permute-start.1) | collective-permute-done | bytes 16416 | tf_op jit(solution)/shard_map/ppermute | solution.py:19
  19.7 1.3 collective-permute-start.3
  21.0 3.0 %collective-permute-start.2 = (bf16[64,10,1]{2,0,1:T(8,128)(2,1)S(1)}, bf16[64,10,1]{2,0,1:T(8,128)(2,1)S(1)}, u32[]{:S(2)}, u32[]{:S(2)}) collective-permute-start(bf16[64,10,1]{2,0,1:T(8,128)(2,1)S(1)} %get-tuple-element.51), channel_id=1, source_target_pairs={{0,1},{1,2},{2,3},{4,5},{5,6},{6,7},{8,9},{9,10},{10,11},{12,13},{... | collective-permute-start | bytes 3848 | tf_op jit(solution)/shard_map/ppermute | solution.py:17
  28.8 1.3 collective-permute-start.5
  30.1 4.9 %collective-permute-start.4 = (bf16[256,1,2]{1,0,2:T(8,128)(2,1)S(1)}, bf16[256,1,2]{1,0,2:T(8,128)(2,1)S(1)}, u32[]{:S(2)}, u32[]{:S(2)}) collective-permute-start(bf16[256,1,2]{1,0,2:T(8,128)(2,1)S(1)} %get-tuple-element.55), channel_id=1, source_target_pairs={{0,1},{1,2},{2,3},{4,5},{5,6},{6,7},{8,9},{9,10},{10,11},{12,13},{... | collective-permute-start | bytes 3080 | tf_op jit(solution)/shard_map/ppermute | solution.py:17
  36.2 13.7 %all_gather.3 = bf16[256,34,8]{0,1,2:T(8,128)(2,1)S(1)} all-gather(bf16[256,34,2]{0,1,2:T(8,128)(2,1)S(1)} %copy.226), channel_id=1, replica_groups=mesh['grp'=2,'row'=4,'col'=2,'pair'=2] {'row'}, dimensions={2}, use_global_device_ids=true | all-gather | bytes 174080 | tf_op jit(solution)/shard_map/all_gather | solution.py:93
  50.1 1.0 fusion.6
  53.9 2.4 %collective-permute-start.6 = (f32[256,1,8]{0,2,1:T(8,128)S(1)}, f32[256,1,8]{0,2,1:T(8,128)S(1)}, u32[]{:S(2)}, u32[]{:S(2)}) collective-permute-start(f32[256,1,8]{0,2,1:T(8,128)S(1)} %get-tuple-element.48), channel_id=1, source_target_pairs={{0,1},{1,2},{2,3},{4,5},{5,6},{6,7},{8,9},{9,10},{10,11},{12,13},{... | collective-permute-start | bytes 24584 | tf_op jit(solution)/shard_map/ppermute | solution.py:17
  56.6 1.3 collective-permute-start.7
  57.9 6.6 %collective-permute-done.7 = f32[256,1,8]{0,2,1:T(8,128)S(1)} collective-permute-done((f32[256,1,8]{0,2,1:T(8,128)S(1)}, f32[256,1,8]{0,2,1:T(8,128)S(1)}, u32[]{:S(2)}, u32[]{:S(2)}) %collective-permute-start.7) | collective-permute-done | bytes 8224 | tf_op jit(solution)/shard_map/ppermute | solution.py:19
  65.7 1.1 maximum_bitcast_fusion
  66.8 18.7 %reduce-scatter.2.cloned.1.call-done = f32[256,32,2]{0,1,2:T(8,128)} async-done(((f32[256,32,8]{0,1,2:T(8,128)}), f32[256,32,2]{0,1,2:T(8,128)}) %reduce-scatter.2.cloned.1.call-update) | async-done | bytes 65552 | tf_op jit(solution)/shard_map/reduce_scatter | solution.py:108
  87.7 1.3 collective-permute-start.8
  89.0 1.3 collective-permute-start.9
  92.4 2.4 %collective-permute-done.9 = bf16[64,1,128]{2,1,0:T(2,128)(2,1)S(1)} collective-permute-done((bf16[64,1,128]{2,1,0:T(2,128)(2,1)S(1)}, bf16[64,1,128]{2,1,0:T(2,128)(2,1)S(1)}, u32[]{:S(2)}, u32[]{:S(2)}) %collective-permute-start.9) | collective-permute-done | bytes 16416 | tf_op jit(solution)/shard_map/ppermute | solution.py:19
  94.9 1.3 collective-permute-start.11
  96.2 3.0 %collective-permute-start.10 = (bf16[64,10,1]{2,0,1:T(8,128)(2,1)S(1)}, bf16[64,10,1]{2,0,1:T(8,128)(2,1)S(1)}, u32[]{:S(2)}, u32[]{:S(2)}) collective-permute-start(bf16[64,10,1]{2,0,1:T(8,128)(2,1)S(1)} %get-tuple-element.49), channel_id=1, source_target_pairs={{0,1},{1,2},{2,3},{4,5},{5,6},{6,7},{8,9},{9,10},{10,11},{12,13},{... | collective-permute-start | bytes 3848 | tf_op jit(solution)/shard_map/ppermute | solution.py:17
  102.6 5.7 %all-reduce.7.cloned.1.call-done = f32[128,3,3,256]{3,0,1,2:T(8,128)} async-done(((f32[128,3,3,256]{3,0,1,2:T(8,128)}), f32[128,3,3,256]{3,0,1,2:T(8,128)}) %all-reduce.7.cloned.1.call-update) | async-done | bytes 1179664 | tf_op jit(solution)/shard_map/psum | solution.py:101
  108.3 1.4 broadcast_multiply_fusion
  109.7 1.1 copy.260
  110.8 91.9 %all-reduce.5.cloned.1.call-done = f32[64,3,3,64]{3,0,2,1:T(8,128)} async-done(((f32[64,3,3,64]{3,0,2,1:T(8,128)}), f32[64,3,3,64]{3,0,2,1:T(8,128)}) %all-reduce.5.cloned.1.call-update) | async-done | bytes 147472 | tf_op jit(solution)/shard_map/psum | solution.py:111
  202.6 1.7 broadcast_multiply_fusion.1
  (103 shorter events, 19.8 us)
Async XLA Ops:
  8.0 42.1 %copy-start = (bf16[128,3,3,256]{3,0,2,1:T(8,128)(2,1)S(1)}, bf16[128,3,3,256]{3,0,2,1:T(8,128)(2,1)}, u32[]{:S(2)}) copy-start(bf16[128,3,3,256]{3,0,2,1:T(8,128)(2,1)} %param.10) | copy-start | bytes 1769476
  8.0 77.5 %reduce-scatter.2.cloned.1.call-start = ((), (), s32[]{:S(2)}) async-start(), calls=%async_computation.1 | async-start | bytes 327680 | tf_op jit(solution)/shard_map/reduce_scatter | solution.py:108
  9.1 6.4 %collective-permute-start = (bf16[64,1,128]{2,0,1:T(8,128)(2,1)S(1)}, bf16[64,1,128]{2,0,1:T(8,128)(2,1)S(1)}, u32[]{:S(2)}, u32[]{:S(2)}) collective-permute-start(bf16[64,1,128]{2,0,1:T(8,128)(2,1)S(1)} %get-tuple-element.58), channel_id=1, source_target_pairs={{0,4},{4,8},{8,12},{1,5},{5,9},{9,13},{2,6},{6,10},{10,14},{3,7},{... | collective-permute-start | bytes 49160 | tf_op jit(solution)/shard_map/ppermute | solution.py:17
  14.0 5.6 %collective-permute-start.1 = (bf16[64,1,128]{2,0,1:T(8,128)(2,1)S(1)}, bf16[64,1,128]{2,0,1:T(8,128)(2,1)S(1)}, u32[]{:S(2)}, u32[]{:S(2)}) collective-permute-start(bf16[64,1,128]{2,0,1:T(8,128)(2,1)S(1)} %get-tuple-element.57), channel_id=1, source_target_pairs={{4,0},{8,4},{12,8},{5,1},{9,5},{13,9},{6,2},{10,6},{14,10},{7,3},{... | collective-permute-start | bytes 49160 | tf_op jit(solution)/shard_map/ppermute | solution.py:19
  19.7 4.4 %collective-permute-start.3 = (bf16[64,10,1]{2,0,1:T(8,128)(2,1)S(1)}, bf16[64,10,1]{2,0,1:T(8,128)(2,1)S(1)}, u32[]{:S(2)}, u32[]{:S(2)}) collective-permute-start(bf16[64,10,1]{2,0,1:T(8,128)(2,1)S(1)} %get-tuple-element.52), channel_id=1, source_target_pairs={{1,0},{2,1},{3,2},{5,4},{6,5},{7,6},{9,8},{10,9},{11,10},{13,12},{... | collective-permute-start | bytes 3848 | tf_op jit(solution)/shard_map/ppermute | solution.py:19
  21.0 4.0 %collective-permute-start.2 = (bf16[64,10,1]{2,0,1:T(8,128)(2,1)S(1)}, bf16[64,10,1]{2,0,1:T(8,128)(2,1)S(1)}, u32[]{:S(2)}, u32[]{:S(2)}) collective-permute-start(bf16[64,10,1]{2,0,1:T(8,128)(2,1)S(1)} %get-tuple-element.51), channel_id=1, source_target_pairs={{0,1},{1,2},{2,3},{4,5},{5,6},{6,7},{8,9},{9,10},{10,11},{12,13},{... | collective-permute-start | bytes 3848 | tf_op jit(solution)/shard_map/ppermute | solution.py:17
  25.6 0.9 copy-start.3
  25.6 0.9 copy-start.4
  28.8 6.4 %collective-permute-start.5 = (bf16[256,1,2]{1,0,2:T(8,128)(2,1)S(1)}, bf16[256,1,2]{1,0,2:T(8,128)(2,1)S(1)}, u32[]{:S(2)}, u32[]{:S(2)}) collective-permute-start(bf16[256,1,2]{1,0,2:T(8,128)(2,1)S(1)} %get-tuple-element.56), channel_id=1, source_target_pairs={{1,0},{2,1},{3,2},{5,4},{6,5},{7,6},{9,8},{10,9},{11,10},{13,12},{... | collective-permute-start | bytes 3080 | tf_op jit(solution)/shard_map/ppermute | solution.py:19
  30.1 5.9 %collective-permute-start.4 = (bf16[256,1,2]{1,0,2:T(8,128)(2,1)S(1)}, bf16[256,1,2]{1,0,2:T(8,128)(2,1)S(1)}, u32[]{:S(2)}, u32[]{:S(2)}) collective-permute-start(bf16[256,1,2]{1,0,2:T(8,128)(2,1)S(1)} %get-tuple-element.55), channel_id=1, source_target_pairs={{0,1},{1,2},{2,3},{4,5},{5,6},{6,7},{8,9},{9,10},{10,11},{12,13},{... | collective-permute-start | bytes 3080 | tf_op jit(solution)/shard_map/ppermute | solution.py:17
  50.1 1.0 copy-start.2
  53.9 4.0 %collective-permute-start.6 = (f32[256,1,8]{0,2,1:T(8,128)S(1)}, f32[256,1,8]{0,2,1:T(8,128)S(1)}, u32[]{:S(2)}, u32[]{:S(2)}) collective-permute-start(f32[256,1,8]{0,2,1:T(8,128)S(1)} %get-tuple-element.48), channel_id=1, source_target_pairs={{0,1},{1,2},{2,3},{4,5},{5,6},{6,7},{8,9},{9,10},{10,11},{12,13},{... | collective-permute-start | bytes 24584 | tf_op jit(solution)/shard_map/ppermute | solution.py:17
  56.6 7.9 %collective-permute-start.7 = (f32[256,1,8]{0,2,1:T(8,128)S(1)}, f32[256,1,8]{0,2,1:T(8,128)S(1)}, u32[]{:S(2)}, u32[]{:S(2)}) collective-permute-start(f32[256,1,8]{0,2,1:T(8,128)S(1)} %get-tuple-element.47), channel_id=1, source_target_pairs={{1,0},{2,1},{3,2},{5,4},{6,5},{7,6},{9,8},{10,9},{11,10},{13,12},{... | collective-permute-start | bytes 24584 | tf_op jit(solution)/shard_map/ppermute | solution.py:19
  65.3 43.0 %all-reduce.7.cloned.1.call-start = ((), (), s32[]{:S(2)}) async-start(), calls=%async_computation.3 | async-start | bytes 2359296 | tf_op jit(solution)/shard_map/psum | solution.py:101
  66.8 135.9 %all-reduce.5.cloned.1.call-start = ((), (), s32[]{:S(2)}) async-start(), calls=%async_computation.2 | async-start | bytes 589824 | tf_op jit(solution)/shard_map/psum | solution.py:111
  86.6 0.9 copy-start.1
  87.7 4.6 %collective-permute-start.8 = (bf16[64,1,128]{2,1,0:T(2,128)(2,1)S(1)}, bf16[64,1,128]{2,1,0:T(2,128)(2,1)S(1)}, u32[]{:S(2)}, u32[]{:S(2)}) collective-permute-start(bf16[64,1,128]{2,1,0:T(2,128)(2,1)S(1)} %get-tuple-element.54), channel_id=1, source_target_pairs={{0,4},{4,8},{8,12},{1,5},{5,9},{9,13},{2,6},{6,10},{10,14},{3,7},{... | collective-permute-start | bytes 49160 | tf_op jit(solution)/shard_map/ppermute | solution.py:17
  89.0 5.8 %collective-permute-start.9 = (bf16[64,1,128]{2,1,0:T(2,128)(2,1)S(1)}, bf16[64,1,128]{2,1,0:T(2,128)(2,1)S(1)}, u32[]{:S(2)}, u32[]{:S(2)}) collective-permute-start(bf16[64,1,128]{2,1,0:T(2,128)(2,1)S(1)} %get-tuple-element.53), channel_id=1, source_target_pairs={{4,0},{8,4},{12,8},{5,1},{9,5},{13,9},{6,2},{10,6},{14,10},{7,3},{... | collective-permute-start | bytes 49160 | tf_op jit(solution)/shard_map/ppermute | solution.py:19
  94.9 5.1 %collective-permute-start.11 = (bf16[64,10,1]{2,0,1:T(8,128)(2,1)S(1)}, bf16[64,10,1]{2,0,1:T(8,128)(2,1)S(1)}, u32[]{:S(2)}, u32[]{:S(2)}) collective-permute-start(bf16[64,10,1]{2,0,1:T(8,128)(2,1)S(1)} %get-tuple-element.50), channel_id=1, source_target_pairs={{1,0},{2,1},{3,2},{5,4},{6,5},{7,6},{9,8},{10,9},{11,10},{13,12},{... | collective-permute-start | bytes 3848 | tf_op jit(solution)/shard_map/ppermute | solution.py:19
  96.2 4.0 %collective-permute-start.10 = (bf16[64,10,1]{2,0,1:T(8,128)(2,1)S(1)}, bf16[64,10,1]{2,0,1:T(8,128)(2,1)S(1)}, u32[]{:S(2)}, u32[]{:S(2)}) collective-permute-start(bf16[64,10,1]{2,0,1:T(8,128)(2,1)S(1)} %get-tuple-element.49), channel_id=1, source_target_pairs={{0,1},{1,2},{2,3},{4,5},{5,6},{6,7},{8,9},{9,10},{10,11},{12,13},{... | collective-permute-start | bytes 3848 | tf_op jit(solution)/shard_map/ppermute | solution.py:17
Sparse Core Ops, SparseCore 0:
  65.4 20.0 reduce-scatter.1
Sparse Core Ops, SparseCore 1:
  68.8 39.4 all-reduce.6
  112.5 90.1 all-reduce.4
where the time goes:
time: 212 us
  waiting for transfers between devices  131 us (62%)
  starting transfers between devices  27.5 us (13%)
  between operations  16.1 us (8%)
  blocking collectives  13.7 us (6%)
  local copies, waits for them, and re-layouts  8.75 us (4%)
  other arithmetic  7.58 us (4%)
  matrix products  7.49 us (4%)
    psum x1, waiting for transfers between devices, local(): lax.psum(local_one, ('row', 'col', 'pair')) / math.sqrt(height * width)  91.9 us
    ppermute x6, starting transfers between devices, padded_2(): lax.ppermute(tail, axis, [(i, (i + 1) % count) for i in range(ends)])  19.6 us
    reduce_scatter x1, waiting for transfers between devices, local(): lax.psum_scatter(real_columns, 'row', scatter_dimension=2, tiled=True)  18.7 us
    all_gather x1, blocking collectives, local(): column_strip = lax.all_gather(with_edges, 'row', axis=2, tiled=True)  13.7 us
    ppermute x6, waiting for transfers between devices, padded_2(): lax.ppermute(head, axis, [((i + 1) % count, i) for i in range(ends)])  12.2 us
    ppermute x6, starting transfers between devices, padded_2(): lax.ppermute(head, axis, [((i + 1) % count, i) for i in range(ends)])  7.75 us
    psum x1, waiting for transfers between devices, local(): lax.psum(local_two, ('col', 'pair'))  5.73 us
    unnamed x21, local copies, waits for them, and re-layouts  5.7 us
  transfers between devices with their start and end apart: 15, of which 10 were waited for; matrix products, arithmetic and copies ran while one was open for 6% of the time, Pallas kernels for 0%

commit v1 on v0

v1 whole, which is shorter than its diff:
```python
import functools
import math

import jax
import jax.numpy as jnp
from jax import lax
from jax.experimental import pallas as pl
from jax.experimental.pallas import tpu as pltpu
from jax.sharding import PartitionSpec as P

BF16 = jnp.bfloat16
F32 = jnp.float32
COLS = ("col", "pair")
EVERY = ("row", "col", "pair")
REACH = 3
PITCH = 48
SENT = 40


def dot(a, b, contract):
    return lax.dot_general(a, b, ((contract[:1], contract[1:]), ((), ())), preferred_element_type=F32)


def whole_call(body, outs, operands, flops, scalars=1, scratch=()):
    specs = [
        pl.BlockSpec(memory_space=pltpu.SMEM if n < scalars else pltpu.VMEM)
        for n in range(len(operands))
    ]
    moved = sum(math.prod(a.shape) * a.dtype.itemsize for a in tuple(operands[scalars:]) + tuple(outs))
    return pl.pallas_call(
        body,
        out_shape=outs,
        in_specs=specs,
        out_specs=[pl.BlockSpec(memory_space=pltpu.VMEM) for _ in outs],
        scratch_shapes=list(scratch),
        cost_estimate=pl.CostEstimate(flops=flops, bytes_accessed=moved, transcendentals=0),
        compiler_params=pltpu.CompilerParams(vmem_limit_bytes=40 * 1024 * 1024),
    )(*operands)


def shaped(shape, dtype=BF16):
    return jax.ShapeDtypeStruct(shape, dtype)


def roll(values, amount, axis):
    return pltpu.roll(values, amount % values.shape[axis], axis)


def sigmoid(values):
    return 1.0 / (1.0 + jnp.exp(-values))


def slope_of(values, sig):
    return sig * (1.0 + values * (1.0 - sig))


def pool_matrix(strip, total):
    row = lax.broadcasted_iota(jnp.int32, (2 * PITCH, 256), 0)
    lane = lax.broadcasted_iota(jnp.int32, (2 * PITCH, 256), 1)
    half = (row >= PITCH).astype(jnp.int32)
    v = row - half * PITCH
    first = 4 * (v - REACH) + 2 * half
    near = jnp.bitwise_and(lane - first, 255) < 2
    place = strip * 32 + v - REACH
    keep = near & (v < 32 + 2 * REACH) & (place >= 0) & (place < total)
    return jnp.where(keep, 0.25, 0.0).astype(BF16)


def order_matrix():
    row = lax.broadcasted_iota(jnp.int32, (256, 256), 0)
    lane = lax.broadcasted_iota(jnp.int32, (256, 256), 1)
    j, i, c = row >> 7, (row >> 6) & 1, row & 63
    return jnp.where(lane == 4 * c + 2 * i + j, 1.0, 0.0).astype(BF16)


def layer_one(info, x_ref, a_ref, b_ref, w_ref, pooled_ref, slope_ref, wide_ref, *, total):
    strip = info[0]
    lane = lax.broadcasted_iota(jnp.int32, x_ref.shape, 2)
    from_a = (lane >= 64).astype(jnp.int32) == (strip & 1)
    halo = jnp.where(from_a, a_ref[...].astype(F32), b_ref[...].astype(F32))
    wide_ref[:, :, :128] = x_ref[...]
    wide_ref[:, :, 128:] = halo.astype(BF16)
    weights = jnp.concatenate([w_ref[0], w_ref[1], w_ref[2]], axis=1)
    rows = slope_ref.shape[0]
    halves, held = [], None
    for h in range(rows):
        y = dot(weights, wide_ref[h : h + 3].reshape(192, 256), (1, 0))
        pre = roll(y[:64], 1, 1) + y[64:128] + roll(y[128:], -1, 1)
        sig = sigmoid(pre)
        slope_ref[h] = slope_of(pre, sig).astype(BF16)
        if 1 <= h <= rows - 2:
            active = pre * sig
            if h % 2:
                held = active
            else:
                halves.append((held + active).astype(BF16))
    pooled = dot(pool_matrix(strip, total), jnp.concatenate(halves, 0), (1, 1))
    stacked = jnp.concatenate(
        [
            jnp.concatenate(
                [pooled[:PITCH, u * 128 : u * 128 + 128], pooled[PITCH:, u * 128 : u * 128 + 128]], 1
            )
            for u in range(2)
        ],
        0,
    ).astype(BF16)
    ordered = dot(stacked, order_matrix(), (1, 0)).astype(BF16)
    for u in range(2):
        pooled_ref[u] = ordered[u * PITCH : u * PITCH + SENT]


def layer_two(info, og_ref, w_ref, *refs, bands):
    pieces, refs = refs[:bands], refs[bands:]
    terms, refs = refs[:bands], refs[bands:]
    map_ref, cat_ref, grad_ref, spread_ref = refs
    band = info[0]
    rows, _, filters = og_ref.shape
    count = rows * PITCH
    map_ref[0] = jnp.zeros((PITCH, 256), BF16)
    map_ref[rows + 1] = jnp.zeros((PITCH, 256), BF16)
    blank = jnp.zeros((PITCH - SENT, 256), BF16)
    for k in range(bands):
        for t in range(2):
            map_ref[1 + 2 * (band ^ k) + t] = jnp.concatenate([pieces[k][t], blank], 0)
    y = None
    for i in range(3):
        part = dot(map_ref[i : i + rows].reshape(count, 256), w_ref[i], (1, 1))
        y = part if y is None else y + part
    pre = roll(y[:, :filters], 1, 0) + y[:, filters : 2 * filters] + roll(y[:, 2 * filters :], -1, 0)
    grad = og_ref[...].reshape(count, filters).astype(F32) * slope_of(pre, sigmoid(pre))
    grad = grad.astype(BF16)
    grad_ref[0] = jnp.zeros((PITCH, filters), BF16)
    grad_ref[rows + 1] = jnp.zeros((PITCH, filters), BF16)
    grad_ref[1 : rows + 1] = grad.reshape(rows, PITCH, filters)
    z = None
    for i in range(3):
        weights = jnp.concatenate([w_ref[i, j * filters : (j + 1) * filters] for j in range(3)], 1)
        part = dot(grad_ref[2 - i : 2 - i + rows].reshape(count, filters), weights, (1, 0))
        z = part if z is None else z + part
    spread = roll(z[:, :256], -1, 0) + z[:, 256:512] + roll(z[:, 512:], 1, 0)
    spread_ref[0] = jnp.zeros((PITCH, 256), F32)
    spread_ref[rows + 1] = jnp.zeros((PITCH, 256), F32)
    spread_ref[1 : rows + 1] = spread.reshape(rows, PITCH, 256)
    lower = (lax.broadcasted_iota(jnp.int32, (PITCH, 256), 1) & 2) == 0
    for k in range(bands):
        first = 2 * (band ^ k)
        for t in range(2):
            terms[k][t] = spread_ref[first + 1 + t][:SENT].astype(BF16)
        edge = jnp.where(lower, spread_ref[first + 3], spread_ref[first])
        terms[k][2] = edge[:SENT].astype(BF16)
    wide = grad.astype(F32)
    v = lax.broadcasted_iota(jnp.int32, (rows, PITCH, filters), 1).reshape(count, filters)
    wide = jnp.where((v >= REACH) & (v < REACH + 32), wide, 0.0)
    cat_ref[...] = jnp.concatenate([roll(wide, -1, 0), wide, roll(wide, 1, 0)], 1).astype(BF16)


def filter_two_grads(info, map_ref, cat_ref, keep_ref, send_ref, all_ref):
    pair = info[0]
    rows = map_ref.shape[0] - 2
    taps = cat_ref.shape[1]
    for i in range(3):
        part = dot(cat_ref[...], map_ref[i : i + rows].reshape(rows * PITCH, 256), (0, 0))
        all_ref[i * taps : (i + 1) * taps] = part.astype(BF16)
    half = keep_ref.shape[0]
    keep_ref[...] = all_ref[pl.ds(pl.multiple_of(pair * half, 16), half)]
    send_ref[...] = all_ref[pl.ds(pl.multiple_of((1 - pair) * half, 16), half)]


def grad_pre_one(info, *refs, bands, total):
    terms, (slope_ref, wide_ref, g_ref, part_ref) = refs[:bands], refs[bands:]
    strip = info[0]
    summed = terms[0][...].astype(F32)
    for k in range(1, bands):
        summed = summed + terms[k][...].astype(F32)
    blank = jnp.zeros((PITCH - SENT, 256), F32)
    stacked = jnp.concatenate([p for t in range(3) for p in (summed[t], blank)], 0).astype(BF16)
    ordered = dot(stacked, order_matrix(), (1, 1)).astype(BF16)
    pool = pool_matrix(strip, total)
    ups = []
    for t in range(3):
        block = ordered[t * PITCH : (t + 1) * PITCH]
        ups.append(dot(jnp.concatenate([block[:, :128], block[:, 128:]], 0), pool, (0, 0)))
    quads = [ups[0][:64], ups[0][64:], ups[1][:64], ups[1][64:]]
    rows = [ups[2][64:]] + [quads[h // 2] for h in range(8)] + [ups[2][:64]]
    acc = None
    own = lax.broadcasted_iota(jnp.int32, (64, 256), 1) < 128
    for h in range(10):
        g = (rows[h] * slope_ref[h].astype(F32)).astype(BF16)
        g_ref[h] = g
        if 1 <= h <= 8:
            mine = jnp.where(own, g.astype(F32), 0.0)
            cat = jnp.concatenate([roll(mine, -1, 1), mine, roll(mine, 1, 1)], 0).astype(BF16)
            part = dot(cat, wide_ref[h : h + 3].reshape(192, 256), (1, 1))
            acc = part if acc is None else acc + part
    part_ref[:192] = acc[:, :128].astype(BF16)
    tail = jnp.concatenate([acc[:96, 128:], acc[96:, 128:]], 1)
    part_ref[192:288] = tail.astype(BF16)
    rest = part_ref.shape[0] - 288
    if rest:
        part_ref[288:] = jnp.zeros((rest, 128), BF16)


def layer_one_back(g_ref, w_ref, out_ref):
    rows = []
    for h in range(8):
        z = dot(w_ref[...], g_ref[h : h + 3].reshape(192, 256), (1, 0))
        rows.append((roll(z[:64], -1, 1) + z[64:128] + roll(z[128:], 1, 1))[:, :128])
    out_ref[...] = jnp.swapaxes(jnp.stack(rows, 0), 0, 1).astype(BF16)


def sum_and_copy(parts_ref, out_ref):
    count = parts_ref.shape[0]
    total = parts_ref[0].astype(F32)
    for n in range(1, count):
        total = total + parts_ref[n].astype(F32)
    for n in range(count):
        out_ref[n] = total.astype(BF16)


def unpack_one(flat_ref, out_ref, *, scale):
    out_ref[0] = flat_ref[:192, :64].astype(F32) * scale
    out_ref[1] = flat_ref[:192, 64:].astype(F32) * scale
    out_ref[2, :96] = flat_ref[192:288, :64].astype(F32) * scale
    out_ref[2, 96:] = flat_ref[192:288, 64:].astype(F32) * scale


def even_swap(values, axis, count):
    return lax.ppermute(values, axis, [(n, n ^ 1) for n in range(count)])


def odd_swap(values, axis, count):
    steps = [(n, n + 1) for n in range(1, count - 1, 2)]
    return lax.ppermute(values, axis, steps + [(b, a) for a, b in steps])


def xor_swap(values, axis, count, k):
    return lax.ppermute(values, axis, [(n, n ^ k) for n in range(count)])


def border_swap(head, tail, axis, place):
    count = lax.axis_size(axis)
    even = place % 2 == 0
    first = even_swap(jnp.where(even, tail, head), axis, count)
    second = odd_swap(jnp.where(even, head, tail), axis, count)
    return jnp.where(even, second, first), jnp.where(even, first, second)


def local(features_in, filters_one, filters_two, out_grad):
    channels, band_rows, strip_cols = features_in.shape
    filters, own_cols, pooled_rows = out_grad.shape
    bands = lax.axis_size("row")
    strips = lax.axis_size(COLS)
    band = lax.axis_index("row")
    strip = lax.axis_index(COLS)
    pair = lax.axis_index("pair")
    height, width = band_rows * bands, strip_cols * strips
    total = own_cols * strips
    at_strip = jnp.stack([strip]).astype(jnp.int32)
    at_band = jnp.stack([band]).astype(jnp.int32)
    at_pair = jnp.stack([pair]).astype(jnp.int32)

    taps_one = jnp.transpose(filters_one, (1, 2, 0, 3)).reshape(3, 3 * channels, channels)
    back_one = jnp.transpose(filters_one[:, ::-1], (2, 3, 1, 0)).reshape(3 * channels, 3 * channels)
    taps_two = jnp.transpose(filters_two, (1, 2, 0, 3)).reshape(3, 3 * filters, 4 * channels)

    x = jnp.transpose(features_in, (1, 0, 2))
    above, below = border_swap(x[:2], x[-2:], "row", band)
    x = jnp.concatenate([above, x, below], 0)
    side_a = even_swap(x, COLS, strips)
    side_b = odd_swap(x, COLS, strips)
    rows_wide = band_rows + 2
    pooled, slope, wide = whole_call(
        functools.partial(layer_one, total=total),
        [
            shaped((2, SENT, 4 * channels)),
            shaped((rows_wide, channels, 256)),
            shaped((rows_wide + 2, channels, 256)),
        ],
        [at_strip, x, side_a, side_b, taps_one],
        2 * rows_wide * 192 * 192 * 256,
    )
    pieces = [pooled] + [xor_swap(pooled, "row", bands, k) for k in range(1, bands)]

    og = jnp.transpose(out_grad, (1, 2, 0))
    before, after = border_swap(og[: REACH - 1], og[-(REACH - 1) :], COLS, strip)
    og = jnp.concatenate([before, og, after], 0)
    og = jnp.pad(og, ((1, PITCH - own_cols - 2 * REACH + 1), (0, 0), (0, 0)))
    og = jnp.transpose(og, (1, 0, 2))

    count = pooled_rows * PITCH
    *terms, pooled_map, grad_cat = whole_call(
        functools.partial(layer_two, bands=bands),
        [shaped((3, SENT, 4 * channels))] * bands
        + [shaped((pooled_rows + 2, PITCH, 4 * channels)), shaped((count, 3 * filters))],
        [at_band, og, taps_two] + pieces,
        4 * count * 9 * filters * 4 * channels,
        scratch=[
            pltpu.VMEM((pooled_rows + 2, PITCH, filters), BF16),
            pltpu.VMEM((pooled_rows + 2, PITCH, 4 * channels), F32),
        ],
    )
    received = [terms[0]] + [xor_swap(terms[k], "row", bands, k) for k in range(1, bands)]

    half = 9 * filters // 2
    keep, send = whole_call(
        filter_two_grads,
        [shaped((half, 4 * channels))] * 2,
        [at_pair, pooled_map, grad_cat],
        2 * count * 9 * filters * 4 * channels,
        scratch=[pltpu.VMEM((2 * half, 4 * channels), BF16)],
    )
    part = keep.astype(F32) + even_swap(send, "pair", 2).astype(F32)
    step = 1
    while step < lax.axis_size("col"):
        sent = part.astype(BF16)
        part = sent.astype(F32) + xor_swap(sent, "col", lax.axis_size("col"), step).astype(F32)
        step *= 2
    mine = part.astype(BF16)
    other = even_swap(mine, "pair", 2)
    grad_two = jnp.concatenate([jnp.where(pair == 0, mine, other), jnp.where(pair == 0, other, mine)], 0)
    grad_two = grad_two.astype(F32) * (1.0 / math.sqrt(pooled_rows * total))
    grad_two = jnp.transpose(grad_two.reshape(3, 3, filters, 4 * channels), (2, 0, 1, 3))

    devices = lax.axis_size(EVERY)
    share = -(-288 // (8 * devices)) * 8
    g, part_one = whole_call(
        functools.partial(grad_pre_one, bands=bands, total=total),
        [shaped((rows_wide, channels, 256)), shaped((devices * share, 128))],
        [at_strip] + received + [slope, wide],
        2 * 8 * 192 * 192 * 256,
    )
    parts = lax.all_to_all(part_one.reshape(devices, share, 128), EVERY, 0, 0, tiled=True)
    (copies,) = whole_call(sum_and_copy, [shaped((devices, share, 128))], [parts], 1, scalars=0)
    flat = lax.all_to_all(copies, EVERY, 0, 0, tiled=True).reshape(devices * share, 128)
    (grad_one,) = whole_call(
        functools.partial(unpack_one, scale=1.0 / math.sqrt(height * width)),
        [shaped((3, 3 * channels, channels), F32)],
        [flat],
        1,
        scalars=0,
    )
    grad_one = jnp.transpose(grad_one.reshape(3, 3, channels, channels), (2, 0, 1, 3))
    (input_grad,) = whole_call(
        layer_one_back, [shaped(features_in.shape)], [g, back_one], 2 * 8 * 192 * 192 * 256, scalars=0
    )
    return (input_grad, grad_one, grad_two)


def solution(mesh):
    in_specs = (
        P("grp", "row", ("col", "pair")),
        P(),
        P("row", None, None, None),
        P(("grp", "row"), ("col", "pair"), None),
    )
    out_specs = (
        P("grp", "row", ("col", "pair")),
        P("grp", None, None, None),
        P(("grp", "row"), None, None, None),
    )
    return jax.shard_map(local, mesh=mesh, in_specs=in_specs, out_specs=out_specs, check_vma=False)
```

time: 212 us -> 66.9 us (0.32)
  waiting for transfers between devices: 131 us -> 22.5 us
  between operations: 16.1 us -> 0.83 us
  blocking collectives: 13.7 us -> 0 us
  matrix products: 7.49 us -> 0 us
  Pallas kernels: 0 us -> 7.15 us
  local copies, waits for them, and re-layouts: 8.75 us -> 2.19 us
  other arithmetic: 7.58 us -> 1.41 us
  starting transfers between devices: 27.5 us -> 32.5 us
    psum x2 -> x0, waiting for transfers between devices: 97.6 us -> none  [the longest x1 91.9 us: local(): lax.psum(local_one, ('row', 'col', 'pair')) / math.sqrt(height * width)]
    reduce_scatter x1 -> x0, waiting for transfers between devices: 18.7 us -> none  [local(): lax.psum_scatter(real_columns, 'row', scatter_dimension=2, tiled=True)]
    all_gather x1 -> x0, blocking collectives: 13.7 us -> none  [local(): column_strip = lax.all_gather(with_edges, 'row', axis=2, tiled=True)]
    all_to_all x0 -> x2, waiting for transfers between devices: none -> 12.8 us  [the longest x1 6.93 us: local(): lax.all_to_all(part_one.reshape(devices, share, 128), EVERY, 0, 0, tiled=...]
    pallas_call x0 -> x7, Pallas kernels: none -> 7.15 us  [whole_call(): pl.pallas_call(body, out_shape=outs, in_specs=specs, out_specs=[pl.BlockS...]
    all_to_all x0 -> x2, starting transfers between devices: none -> 7.01 us  [the longest x1 3.51 us: local(): lax.all_to_all(copies, EVERY, 0, 0, tiled=True)]
    ppermute x12 -> x15, waiting for transfers between devices: 14.3 us -> 9.7 us  [the longest x7 7.43 us: xor_swap(): return lax.ppermute(values, axis, [(n, n ^ k) for n in range(count)])]
    dot_general x18 -> x0, matrix products: 4.1 us -> none  [tap_grads(): jnp.einsum('ohw,chw->oc', gradient, window, preferred_element_type=jnp.fl...]
  transfers between devices with their start and end apart: 15 -> 17, of which waited for: 10 -> 7; matrix products, arithmetic and copies ran while one was open for 6% -> 2% of each run, Pallas kernels for 0% -> 6%
where the time goes in v1:
time: 66.9 us; the launch traced here: 66.5 us
  starting transfers between devices  32.5 us (49%)
  waiting for transfers between devices  22.5 us (34%)
  Pallas kernels  7.15 us (11%)
  local copies, waits for them, and re-layouts  2.19 us (3%)
  other arithmetic  1.41 us (2%)
  between operations  0.83 us (1%)
    ppermute x5, starting transfers between devices, even_swap(): return lax.ppermute(values, axis, [(n, n ^ 1) for n in range(count)])  12.9 us
    ppermute x7, starting transfers between devices, xor_swap(): return lax.ppermute(values, axis, [(n, n ^ k) for n in range(count)])  10.5 us
    ppermute x7, waiting for transfers between devices, xor_swap(): return lax.ppermute(values, axis, [(n, n ^ k) for n in range(count)])  7.43 us
    pallas_call x7, Pallas kernels, whole_call(): pl.pallas_call(body, out_shape=outs, in_specs=specs, out_specs=[pl.BlockS...  7.15 us
    all_to_all x1, waiting for transfers between devices, local(): lax.all_to_all(part_one.reshape(devices, share, 128), EVERY, 0, 0, tiled=...  6.93 us
    all_to_all x1, waiting for transfers between devices, local(): lax.all_to_all(copies, EVERY, 0, 0, tiled=True)  5.83 us
    all_to_all x1, starting transfers between devices, local(): lax.all_to_all(copies, EVERY, 0, 0, tiled=True)  3.51 us
    all_to_all x1, starting transfers between devices, local(): lax.all_to_all(part_one.reshape(devices, share, 128), EVERY, 0, 0, tiled=...  3.51 us
  transfers between devices with their start and end apart: 17, of which 7 were waited for; matrix products, arithmetic and copies ran while one was open for 2% of the time, Pallas kernels for 6%

profile of v1, /device:TPU:0, one launch (start us, length us, event | category | flops | bytes accessed | tf_op | source)
XLA Modules:
  0.0 66.5 jit_solution(8483497692590453806)
XLA Ops:
  0.7 1.0 %copy.15 = bf16[64,8,128]{2,0,1:T(8,128)(2,1)S(1)} copy(bf16[64,8,128]{2,1,0:T(8,128)(2,1)} %param.4) | data formatting | bytes 262144 | tf_op args[0]
  2.3 5.9 %collective-permute-start.3 = (bf16[2,64,128]{2,1,0:T(8,128)(2,1)S(1)}, bf16[2,64,128]{2,1,0:T(8,128)(2,1)S(1)}, u32[]{:S(2)}, u32[]{:S(2)}) collective-permute-start(bf16[2,64,128]{2,1,0:T(8,128)(2,1)S(1)} %get-tuple-element.32), channel_id=1, source_target_pairs={{0,4},{4,0},{8,12},{12,8},{1,5},{5,1},{9,13},{13,9},{2,6},{6,2},{1... | collective-permute-start | bytes 98312 | tf_op jit(solution)/shard_map/ppermute | solution.py:228
  9.8 2.9 %collective-permute-start.1 = (bf16[2,8,128]{2,0,1:T(2,128)(2,1)S(1)}, bf16[2,8,128]{2,0,1:T(2,128)(2,1)S(1)}, u32[]{:S(2)}, u32[]{:S(2)}) collective-permute-start(bf16[2,8,128]{2,0,1:T(2,128)(2,1)S(1)} %get-tuple-element.36), channel_id=1, source_target_pairs={{0,1},{1,0},{2,3},{3,2},{4,5},{5,4},{6,7},{7,6},{8,9},{9,8},{10,11... | collective-permute-start | bytes 12296 | tf_op jit(solution)/shard_map/ppermute | solution.py:228
  13.5 1.3 %collective-permute-start.4 = (bf16[12,64,128]{2,1,0:T(8,128)(2,1)S(1)}, bf16[12,64,128]{2,1,0:T(8,128)(2,1)S(1)}, u32[]{:S(2)}, u32[]{:S(2)}) collective-permute-start(bf16[12,64,128]{2,1,0:T(8,128)(2,1)S(1)} %pad_maximum_fusion.x_ref), channel_id=1, source_target_pairs={{0,1},{1,0},{2,3},{3,2},{4,5},{5,4},{6,7},{7,6},{8,9},{9,8},{10,11... | collective-permute-start | bytes 589832 | tf_op jit(solution)/shard_map/ppermute | solution.py:228
  14.8 1.0 %collective-permute-done.4.a_ref = bf16[12,64,128]{2,1,0:T(8,128)(2,1)S(1)} collective-permute-done((bf16[12,64,128]{2,1,0:T(8,128)(2,1)S(1)}, bf16[12,64,128]{2,1,0:T(8,128)(2,1)S(1)}, u32[]{:S(2)}, u32[]{:S(2)}) %collective-permute-start.4) | collective-permute-done | bytes 196640 | tf_op jit(solution)/shard_map/ppermute | solution.py:228
  16.8 1.4 %collective-permute-start.8 = (bf16[2,40,256]{2,1,0:T(8,128)(2,1)S(1)}, bf16[2,40,256]{2,1,0:T(8,128)(2,1)S(1)}, u32[]{:S(2)}, u32[]{:S(2)}) collective-permute-start(bf16[2,40,256]{2,1,0:T(8,128)(2,1)S(1)} %get-tuple-element.16.refs_0_), channel_id=1, source_target_pairs={{0,12},{4,8},{8,4},{12,0},{1,13},{5,9},{9,5},{13,1},{2,14},{6,10},... | collective-permute-start | bytes 122888 | tf_op jit(solution)/shard_map/ppermute | solution.py:237
  18.2 1.1 %collective-permute-start.7 = (bf16[2,40,256]{2,1,0:T(8,128)(2,1)S(1)}, bf16[2,40,256]{2,1,0:T(8,128)(2,1)S(1)}, u32[]{:S(2)}, u32[]{:S(2)}) collective-permute-start(bf16[2,40,256]{2,1,0:T(8,128)(2,1)S(1)} %get-tuple-element.16.refs_0_), channel_id=1, source_target_pairs={{0,8},{4,12},{8,0},{12,4},{1,9},{5,13},{9,1},{13,5},{2,10},{6,14},... | collective-permute-start | bytes 122888 | tf_op jit(solution)/shard_map/ppermute | solution.py:237
  19.3 1.9 %collective-permute-start.6 = (bf16[2,40,256]{2,1,0:T(8,128)(2,1)S(1)}, bf16[2,40,256]{2,1,0:T(8,128)(2,1)S(1)}, u32[]{:S(2)}, u32[]{:S(2)}) collective-permute-start(bf16[2,40,256]{2,1,0:T(8,128)(2,1)S(1)} %get-tuple-element.16.refs_0_), channel_id=1, source_target_pairs={{0,4},{4,0},{8,12},{12,8},{1,5},{5,1},{9,13},{13,9},{2,6},{6,2},{1... | collective-permute-start | bytes 122888 | tf_op jit(solution)/shard_map/ppermute | solution.py:237
  21.3 1.4 %collective-permute-done.8.refs_3_ = bf16[2,40,256]{2,1,0:T(8,128)(2,1)S(1)} collective-permute-done((bf16[2,40,256]{2,1,0:T(8,128)(2,1)S(1)}, bf16[2,40,256]{2,1,0:T(8,128)(2,1)S(1)}, u32[]{:S(2)}, u32[]{:S(2)}) %collective-permute-start.8) | collective-permute-done | bytes 40992 | tf_op jit(solution)/shard_map/ppermute | solution.py:237
  22.6 1.3 %collective-permute-done.7.refs_2_ = bf16[2,40,256]{2,1,0:T(8,128)(2,1)S(1)} collective-permute-done((bf16[2,40,256]{2,1,0:T(8,128)(2,1)S(1)}, bf16[2,40,256]{2,1,0:T(8,128)(2,1)S(1)}, u32[]{:S(2)}, u32[]{:S(2)}) %collective-permute-start.7) | collective-permute-done | bytes 40992 | tf_op jit(solution)/shard_map/ppermute | solution.py:237
  23.9 1.5 %shard_map.68 = (bf16[3,40,256]{2,1,0:T(8,128)(2,1)S(1)}, bf16[3,40,256]{2,1,0:T(8,128)(2,1)S(1)}, bf16[3,40,256]{2,1,0:T(8,128)(2,1)S(1)}, bf16[3,40,256]{2,1,0...) custom-call(s32[1]{0:T(128)} %bitcast.1.info, bf16[8,48,128]{2,1,0:T(8,128)(2,1)S(1)} %fusion.6.og_ref, ...), custom_call_target="tpu_custom_call" | custom-call | flops 452984832 | bytes 1638400 | tf_op jit(solution)/shard_map/pallas_call | solution.py:30
  26.0 2.4 %collective-permute-start.12 = (bf16[576,256]{1,0:T(8,128)(2,1)S(1)}, bf16[576,256]{1,0:T(8,128)(2,1)S(1)}, u32[]{:S(2)}, u32[]{:S(2)}) collective-permute-start(bf16[576,256]{1,0:T(8,128)(2,1)S(1)} %get-tuple-element.28), channel_id=1, source_target_pairs={{0,1},{1,0},{2,3},{3,2},{4,5},{5,4},{6,7},{7,6},{8,9},{9,8},{10,11... | collective-permute-start | bytes 884744 | tf_op jit(solution)/shard_map/ppermute | solution.py:228
  28.4 1.2 %collective-permute-done.12 = bf16[576,256]{1,0:T(8,128)(2,1)S(1)} collective-permute-done((bf16[576,256]{1,0:T(8,128)(2,1)S(1)}, bf16[576,256]{1,0:T(8,128)(2,1)S(1)}, u32[]{:S(2)}, u32[]{:S(2)}) %collective-permute-start.12) | collective-permute-done | bytes 294944 | tf_op jit(solution)/shard_map/ppermute | solution.py:228
  29.7 1.7 %collective-permute-start.13 = (bf16[576,256]{1,0:T(8,128)(2,1)S(1)}, bf16[576,256]{1,0:T(8,128)(2,1)S(1)}, u32[]{:S(2)}, u32[]{:S(2)}) collective-permute-start(bf16[576,256]{1,0:T(8,128)(2,1)S(1)} %add_convert_fusion.1), channel_id=1, source_target_pairs={{0,2},{2,0},{1,3},{3,1},{4,6},{6,4},{5,7},{7,5},{8,10},{10,8},{9,1... | collective-permute-start | bytes 884744 | tf_op jit(solution)/shard_map/ppermute | solution.py:237
  31.4 1.5 %collective-permute-start.9 = (bf16[3,40,256]{2,1,0:T(8,128)(2,1)S(1)}, bf16[3,40,256]{2,1,0:T(8,128)(2,1)S(1)}, u32[]{:S(2)}, u32[]{:S(2)}) collective-permute-start(bf16[3,40,256]{2,1,0:T(8,128)(2,1)S(1)} %get-tuple-element.18), channel_id=1, source_target_pairs={{0,4},{4,0},{8,12},{12,8},{1,5},{5,1},{9,13},{13,9},{2,6},{6,2},{1... | collective-permute-start | bytes 184328 | tf_op jit(solution)/shard_map/ppermute | solution.py:237
  33.8 2.0 %collective-permute-start.11 = (bf16[3,40,256]{2,1,0:T(8,128)(2,1)S(1)}, bf16[3,40,256]{2,1,0:T(8,128)(2,1)S(1)}, u32[]{:S(2)}, u32[]{:S(2)}) collective-permute-start(bf16[3,40,256]{2,1,0:T(8,128)(2,1)S(1)} %get-tuple-element.20), channel_id=1, source_target_pairs={{0,12},{4,8},{8,4},{12,0},{1,13},{5,9},{9,5},{13,1},{2,14},{6,10},... | collective-permute-start | bytes 184328 | tf_op jit(solution)/shard_map/ppermute | solution.py:237
  35.8 4.8 %collective-permute-done.10.refs_2_ = bf16[3,40,256]{2,1,0:T(8,128)(2,1)S(1)} collective-permute-done((bf16[3,40,256]{2,1,0:T(8,128)(2,1)S(1)}, bf16[3,40,256]{2,1,0:T(8,128)(2,1)S(1)}, u32[]{:S(2)}, u32[]{:S(2)}) %collective-permute-start.10) | collective-permute-done | bytes 61472 | tf_op jit(solution)/shard_map/ppermute | solution.py:237
  40.5 1.6 %shard_map.69 = (bf16[10,64,256]{2,1,0:T(8,128)(2,1)S(1)}, bf16[384,128]{1,0:T(8,128)(2,1)}) custom-call(s32[1]{0:T(128)} %bitcast.info, bf16[3,40,256]{2,1,0:T(8,128)(2,1)S(1)} %get-tuple-element.17.refs_0_, bf16[3,40,256]{2,1,0:T(8,128)(2,1)S(1)} %collective-permute-done.9.refs_1_, bf16[3,40,256]{2,1,0:T(8,128)(2,1)S(1)} %collective-permute-done.10.refs_2_, ...), custom_call_target="tpu_custom_call" | custom-call | flops 150994944 | bytes 1392640 | tf_op jit(solution)/shard_map/pallas_call | solution.py:30
  42.1 3.5 %all-to-all-start = ((bf16[16,24,128]{2,1,0:T(8,128)(2,1)}), bf16[16,24,128]{2,1,0:T(8,128)(2,1)S(1)}, u32[]{:S(2)}, u32[]{:S(2)}) async-start(bf16[16,24,128]{2,1,0:T(8,128)(2,1)} %bitcast.10), calls=%async_computation | async-start | bytes 196608 | tf_op jit(solution)/shard_map/all_to_all | solution.py:332
  46.1 6.9 %all-to-all-done.parts_ref = bf16[16,24,128]{2,1,0:T(8,128)(2,1)S(1)} async-done(((bf16[16,24,128]{2,1,0:T(8,128)(2,1)}), bf16[16,24,128]{2,1,0:T(8,128)(2,1)S(1)}, u32[]{:S(2)}, u32[]{:S(2)}) %all-to-all-start) | async-done | bytes 98336 | tf_op jit(solution)/shard_map/all_to_all | solution.py:332
  53.7 3.5 %all-to-all-start.1 = ((bf16[16,24,128]{2,1,0:T(8,128)(2,1)}), bf16[16,24,128]{2,1,0:T(8,128)(2,1)S(1)}, u32[]{:S(2)}, u32[]{:S(2)}) async-start(bf16[16,24,128]{2,1,0:T(8,128)(2,1)} %shard_map.71), calls=%async_computation.1 | async-start | bytes 196608 | tf_op jit(solution)/shard_map/all_to_all | solution.py:334
  57.6 1.2 %shard_map.70 = bf16[64,8,128]{2,1,0:T(8,128)(2,1)} custom-call(bf16[10,64,256]{2,1,0:T(8,128)(2,1)S(1)} %get-tuple-element.23.g_ref, bf16[192,192]{1,0:T(8,128)(2,1)S(1)} %reshape.31.w_ref), custom_call_target="tpu_custom_call" | custom-call | flops 150994944 | bytes 532480 | tf_op jit(solution)/shard_map/pallas_call | solution.py:30
  58.7 5.8 %all-to-all-done.1 = bf16[16,24,128]{2,1,0:T(8,128)(2,1)S(1)} async-done(((bf16[16,24,128]{2,1,0:T(8,128)(2,1)}), bf16[16,24,128]{2,1,0:T(8,128)(2,1)S(1)}, u32[]{:S(2)}, u32[]{:S(2)}) %all-to-all-start.1) | async-done | bytes 98336 | tf_op jit(solution)/shard_map/all_to_all | solution.py:334
  65.4 1.1 %convert_multiply_fusion = f32[1152,256]{1,0:T(8,128)} fusion(bf16[576,256]{1,0:T(8,128)(2,1)S(1)} %get-tuple-element.30, bf16[576,256]{1,0:T(8,128)(2,1)S(1)} %get-tuple-element.29), kind=kLoop, calls=%fused_computation | loop fusion | flops 1474560 | bytes 1769472 | tf_op jit(solution)/shard_map/mul | solution.py:321
  (36 shorter events, 7.7 us)
Async XLA Ops:
  0.6 15.2 %copy-start = (bf16[64,3,3,64]{3,0,2,1:T(8,128)(2,1)S(1)}, bf16[64,3,3,64]{3,0,2,1:T(8,128)(2,1)}, u32[]{:S(2)}) copy-start(bf16[64,3,3,64]{3,0,2,1:T(8,128)(2,1)} %param.5) | copy-start | bytes 221188
  0.6 23.3 %copy-start.1 = (bf16[128,3,3,256]{3,0,2,1:T(8,128)(2,1)S(1)}, bf16[128,3,3,256]{3,0,2,1:T(8,128)(2,1)}, u32[]{:S(2)}) copy-start(bf16[128,3,3,256]{3,0,2,1:T(8,128)(2,1)} %param.6) | copy-start | bytes 1769476
  1.7 11.0 %collective-permute-start.2 = (bf16[2,64,128]{2,1,0:T(8,128)(2,1)S(1)}, bf16[2,64,128]{2,1,0:T(8,128)(2,1)S(1)}, u32[]{:S(2)}, u32[]{:S(2)}) collective-permute-start(bf16[2,64,128]{2,1,0:T(8,128)(2,1)S(1)} %get-tuple-element.31), channel_id=1, source_target_pairs={{4,8},{8,4},{5,9},{9,5},{6,10},{10,6},{7,11},{11,7},{20,24},{24,20... | collective-permute-start | bytes 98312 | tf_op jit(solution)/shard_map/ppermute | solution.py:233
  2.3 10.4 %collective-permute-start.3 = (bf16[2,64,128]{2,1,0:T(8,128)(2,1)S(1)}, bf16[2,64,128]{2,1,0:T(8,128)(2,1)S(1)}, u32[]{:S(2)}, u32[]{:S(2)}) collective-permute-start(bf16[2,64,128]{2,1,0:T(8,128)(2,1)S(1)} %get-tuple-element.32), channel_id=1, source_target_pairs={{0,4},{4,0},{8,12},{12,8},{1,5},{5,1},{9,13},{13,9},{2,6},{6,2},{1... | collective-permute-start | bytes 98312 | tf_op jit(solution)/shard_map/ppermute | solution.py:228
  9.1 5.7 %collective-permute-start = (bf16[2,8,128]{2,0,1:T(2,128)(2,1)S(1)}, bf16[2,8,128]{2,0,1:T(2,128)(2,1)S(1)}, u32[]{:S(2)}, u32[]{:S(2)}) collective-permute-start(bf16[2,8,128]{2,0,1:T(2,128)(2,1)S(1)} %get-tuple-element.35), channel_id=1, source_target_pairs={{1,2},{2,1},{5,6},{6,5},{9,10},{10,9},{13,14},{14,13},{17,18},{18,... | collective-permute-start | bytes 12296 | tf_op jit(solution)/shard_map/ppermute | solution.py:233
  9.8 5.0 %collective-permute-start.1 = (bf16[2,8,128]{2,0,1:T(2,128)(2,1)S(1)}, bf16[2,8,128]{2,0,1:T(2,128)(2,1)S(1)}, u32[]{:S(2)}, u32[]{:S(2)}) collective-permute-start(bf16[2,8,128]{2,0,1:T(2,128)(2,1)S(1)} %get-tuple-element.36), channel_id=1, source_target_pairs={{0,1},{1,0},{2,3},{3,2},{4,5},{5,4},{6,7},{7,6},{8,9},{9,8},{10,11... | collective-permute-start | bytes 12296 | tf_op jit(solution)/shard_map/ppermute | solution.py:228
  12.8 2.0 %collective-permute-start.5 = (bf16[12,64,128]{2,1,0:T(8,128)(2,1)S(1)}, bf16[12,64,128]{2,1,0:T(8,128)(2,1)S(1)}, u32[]{:S(2)}, u32[]{:S(2)}) collective-permute-start(bf16[12,64,128]{2,1,0:T(8,128)(2,1)S(1)} %pad_maximum_fusion.x_ref), channel_id=1, source_target_pairs={{1,2},{2,1},{5,6},{6,5},{9,10},{10,9},{13,14},{14,13},{17,18},{18,... | collective-permute-start | bytes 589832 | tf_op jit(solution)/shard_map/ppermute | solution.py:233
  13.5 2.4 %collective-permute-start.4 = (bf16[12,64,128]{2,1,0:T(8,128)(2,1)S(1)}, bf16[12,64,128]{2,1,0:T(8,128)(2,1)S(1)}, u32[]{:S(2)}, u32[]{:S(2)}) collective-permute-start(bf16[12,64,128]{2,1,0:T(8,128)(2,1)S(1)} %pad_maximum_fusion.x_ref), channel_id=1, source_target_pairs={{0,1},{1,0},{2,3},{3,2},{4,5},{5,4},{6,7},{7,6},{8,9},{9,8},{10,11... | collective-permute-start | bytes 589832 | tf_op jit(solution)/shard_map/ppermute | solution.py:228
  16.8 5.9 %collective-permute-start.8 = (bf16[2,40,256]{2,1,0:T(8,128)(2,1)S(1)}, bf16[2,40,256]{2,1,0:T(8,128)(2,1)S(1)}, u32[]{:S(2)}, u32[]{:S(2)}) collective-permute-start(bf16[2,40,256]{2,1,0:T(8,128)(2,1)S(1)} %get-tuple-element.16.refs_0_), channel_id=1, source_target_pairs={{0,12},{4,8},{8,4},{12,0},{1,13},{5,9},{9,5},{13,1},{2,14},{6,10},... | collective-permute-start | bytes 122888 | tf_op jit(solution)/shard_map/ppermute | solution.py:237
  18.2 5.8 %collective-permute-start.7 = (bf16[2,40,256]{2,1,0:T(8,128)(2,1)S(1)}, bf16[2,40,256]{2,1,0:T(8,128)(2,1)S(1)}, u32[]{:S(2)}, u32[]{:S(2)}) collective-permute-start(bf16[2,40,256]{2,1,0:T(8,128)(2,1)S(1)} %get-tuple-element.16.refs_0_), channel_id=1, source_target_pairs={{0,8},{4,12},{8,0},{12,4},{1,9},{5,13},{9,1},{13,5},{2,10},{6,14},... | collective-permute-start | bytes 122888 | tf_op jit(solution)/shard_map/ppermute | solution.py:237
  19.3 4.6 %collective-permute-start.6 = (bf16[2,40,256]{2,1,0:T(8,128)(2,1)S(1)}, bf16[2,40,256]{2,1,0:T(8,128)(2,1)S(1)}, u32[]{:S(2)}, u32[]{:S(2)}) collective-permute-start(bf16[2,40,256]{2,1,0:T(8,128)(2,1)S(1)} %get-tuple-element.16.refs_0_), channel_id=1, source_target_pairs={{0,4},{4,0},{8,12},{12,8},{1,5},{5,1},{9,13},{13,9},{2,6},{6,2},{1... | collective-permute-start | bytes 122888 | tf_op jit(solution)/shard_map/ppermute | solution.py:237
  26.0 3.6 %collective-permute-start.12 = (bf16[576,256]{1,0:T(8,128)(2,1)S(1)}, bf16[576,256]{1,0:T(8,128)(2,1)S(1)}, u32[]{:S(2)}, u32[]{:S(2)}) collective-permute-start(bf16[576,256]{1,0:T(8,128)(2,1)S(1)} %get-tuple-element.28), channel_id=1, source_target_pairs={{0,1},{1,0},{2,3},{3,2},{4,5},{5,4},{6,7},{7,6},{8,9},{9,8},{10,11... | collective-permute-start | bytes 884744 | tf_op jit(solution)/shard_map/ppermute | solution.py:228
  29.7 16.0 %collective-permute-start.13 = (bf16[576,256]{1,0:T(8,128)(2,1)S(1)}, bf16[576,256]{1,0:T(8,128)(2,1)S(1)}, u32[]{:S(2)}, u32[]{:S(2)}) collective-permute-start(bf16[576,256]{1,0:T(8,128)(2,1)S(1)} %add_convert_fusion.1), channel_id=1, source_target_pairs={{0,2},{2,0},{1,3},{3,1},{4,6},{6,4},{5,7},{7,5},{8,10},{10,8},{9,1... | collective-permute-start | bytes 884744 | tf_op jit(solution)/shard_map/ppermute | solution.py:237
  31.4 4.4 %collective-permute-start.9 = (bf16[3,40,256]{2,1,0:T(8,128)(2,1)S(1)}, bf16[3,40,256]{2,1,0:T(8,128)(2,1)S(1)}, u32[]{:S(2)}, u32[]{:S(2)}) collective-permute-start(bf16[3,40,256]{2,1,0:T(8,128)(2,1)S(1)} %get-tuple-element.18), channel_id=1, source_target_pairs={{0,4},{4,0},{8,12},{12,8},{1,5},{5,1},{9,13},{13,9},{2,6},{6,2},{1... | collective-permute-start | bytes 184328 | tf_op jit(solution)/shard_map/ppermute | solution.py:237
  32.9 7.7 %collective-permute-start.10 = (bf16[3,40,256]{2,1,0:T(8,128)(2,1)S(1)}, bf16[3,40,256]{2,1,0:T(8,128)(2,1)S(1)}, u32[]{:S(2)}, u32[]{:S(2)}) collective-permute-start(bf16[3,40,256]{2,1,0:T(8,128)(2,1)S(1)} %get-tuple-element.19), channel_id=1, source_target_pairs={{0,8},{4,12},{8,0},{12,4},{1,9},{5,13},{9,1},{13,5},{2,10},{6,14},... | collective-permute-start | bytes 184328 | tf_op jit(solution)/shard_map/ppermute | solution.py:237
  33.8 6.8 %collective-permute-start.11 = (bf16[3,40,256]{2,1,0:T(8,128)(2,1)S(1)}, bf16[3,40,256]{2,1,0:T(8,128)(2,1)S(1)}, u32[]{:S(2)}, u32[]{:S(2)}) collective-permute-start(bf16[3,40,256]{2,1,0:T(8,128)(2,1)S(1)} %get-tuple-element.20), channel_id=1, source_target_pairs={{0,12},{4,8},{8,4},{12,0},{1,13},{5,9},{9,5},{13,1},{2,14},{6,10},... | collective-permute-start | bytes 184328 | tf_op jit(solution)/shard_map/ppermute | solution.py:237
  42.1 10.9 %all-to-all-start = ((bf16[16,24,128]{2,1,0:T(8,128)(2,1)}), bf16[16,24,128]{2,1,0:T(8,128)(2,1)S(1)}, u32[]{:S(2)}, u32[]{:S(2)}) async-start(bf16[16,24,128]{2,1,0:T(8,128)(2,1)} %bitcast.10), calls=%async_computation | async-start | bytes 196608 | tf_op jit(solution)/shard_map/all_to_all | solution.py:332
  45.7 19.7 %collective-permute-start.14 = (bf16[576,256]{1,0:T(8,128)(2,1)S(1)}, bf16[576,256]{1,0:T(8,128)(2,1)S(1)}, u32[]{:S(2)}, u32[]{:S(2)}) collective-permute-start(bf16[576,256]{1,0:T(8,128)(2,1)S(1)} %add_convert_fusion), channel_id=1, source_target_pairs={{0,1},{1,0},{2,3},{3,2},{4,5},{5,4},{6,7},{7,6},{8,9},{9,8},{10,11... | collective-permute-start | bytes 884744 | tf_op jit(solution)/shard_map/ppermute | solution.py:228
  53.7 10.9 %all-to-all-start.1 = ((bf16[16,24,128]{2,1,0:T(8,128)(2,1)}), bf16[16,24,128]{2,1,0:T(8,128)(2,1)S(1)}, u32[]{:S(2)}, u32[]{:S(2)}) async-start(bf16[16,24,128]{2,1,0:T(8,128)(2,1)} %shard_map.71), calls=%async_computation.1 | async-start | bytes 196608 | tf_op jit(solution)/shard_map/all_to_all | solution.py:334

commit v2 on v1

--- a/solution.py
+++ b/solution.py
@@ -11,7 +11,6 @@
 BF16 = jnp.bfloat16
 F32 = jnp.float32
 COLS = ("col", "pair")
-EVERY = ("row", "col", "pair")
 REACH = 3
 PITCH = 48
 SENT = 40
@@ -26,7 +25,8 @@
         pl.BlockSpec(memory_space=pltpu.SMEM if n < scalars else pltpu.VMEM)
         for n in range(len(operands))
     ]
-    moved = sum(math.prod(a.shape) * a.dtype.itemsize for a in tuple(operands[scalars:]) + tuple(outs))
+    sizes = [math.prod(a.shape) * a.dtype.itemsize for a in tuple(operands[scalars:]) + tuple(outs)]
+    moved = sum(sizes) if flops else 0
     return pl.pallas_call(
         body,
         out_shape=outs,
@@ -73,12 +73,18 @@
     return jnp.where(lane == 4 * c + 2 * i + j, 1.0, 0.0).astype(BF16)
 
 
-def layer_one(info, x_ref, a_ref, b_ref, w_ref, pooled_ref, slope_ref, wide_ref, *, total):
+def layer_one(
+    info, x_ref, above_ref, below_ref, a_ref, b_ref, w_ref, pooled_ref, slope_ref, wide_ref, *, total
+):
     strip = info[0]
-    lane = lax.broadcasted_iota(jnp.int32, x_ref.shape, 2)
+    band_rows = x_ref.shape[0]
+    lane = lax.broadcasted_iota(jnp.int32, wide_ref.shape[:2] + (128,), 2)
     from_a = (lane >= 64).astype(jnp.int32) == (strip & 1)
-    halo = jnp.where(from_a, a_ref[...].astype(F32), b_ref[...].astype(F32))
-    wide_ref[:, :, :128] = x_ref[...]
+    sides = a_ref[: band_rows + 4].astype(F32), b_ref[: band_rows + 4].astype(F32)
+    halo = jnp.where(from_a, *sides)
+    wide_ref[:2, :, :128] = above_ref[...]
+    wide_ref[2 : band_rows + 2, :, :128] = x_ref[...]
+    wide_ref[band_rows + 2 :, :, :128] = below_ref[...]
     wide_ref[:, :, 128:] = halo.astype(BF16)
     weights = jnp.concatenate([w_ref[0], w_ref[1], w_ref[2]], axis=1)
     rows = slope_ref.shape[0]
@@ -166,9 +172,14 @@
     send_ref[...] = all_ref[pl.ds(pl.multiple_of((1 - pair) * half, 16), half)]
 
 
+def add_after(a_ref, b_ref, after_ref, out_ref):
+    out_ref[...] = (a_ref[...].astype(F32) + b_ref[...].astype(F32)).astype(BF16)
+
+
 def grad_pre_one(info, *refs, bands, total):
-    terms, (slope_ref, wide_ref, g_ref, part_ref) = refs[:bands], refs[bands:]
-    strip = info[0]
+    terms, refs = refs[:bands], refs[bands:]
+    slope_ref, wide_ref, g_ref, keep_ref, send_ref, part_ref = refs
+    strip, pair = info[0], info[1]
     summed = terms[0][...].astype(F32)
     for k in range(1, bands):
         summed = summed + terms[k][...].astype(F32)
@@ -194,10 +205,10 @@
             acc = part if acc is None else acc + part
     part_ref[:192] = acc[:, :128].astype(BF16)
     tail = jnp.concatenate([acc[:96, 128:], acc[96:, 128:]], 1)
-    part_ref[192:288] = tail.astype(BF16)
-    rest = part_ref.shape[0] - 288
-    if rest:
-        part_ref[288:] = jnp.zeros((rest, 128), BF16)
+    part_ref[192:] = tail.astype(BF16)
+    half = keep_ref.shape[0]
+    keep_ref[...] = part_ref[pl.ds(pl.multiple_of(pair * half, 16), half)]
+    send_ref[...] = part_ref[pl.ds(pl.multiple_of((1 - pair) * half, 16), half)]
 
 
 def layer_one_back(g_ref, w_ref, out_ref):
@@ -208,20 +219,15 @@
     out_ref[...] = jnp.swapaxes(jnp.stack(rows, 0), 0, 1).astype(BF16)
 
 
-def sum_and_copy(parts_ref, out_ref):
-    count = parts_ref.shape[0]
-    total = parts_ref[0].astype(F32)
-    for n in range(1, count):
-        total = total + parts_ref[n].astype(F32)
-    for n in range(count):
-        out_ref[n] = total.astype(BF16)
-
-
-def unpack_one(flat_ref, out_ref, *, scale):
-    out_ref[0] = flat_ref[:192, :64].astype(F32) * scale
-    out_ref[1] = flat_ref[:192, 64:].astype(F32) * scale
-    out_ref[2, :96] = flat_ref[192:288, :64].astype(F32) * scale
-    out_ref[2, 96:] = flat_ref[192:288, 64:].astype(F32) * scale
+def unpack_one(info, mine_ref, other_ref, out_ref, flat_ref, *, scale):
+    pair, half = info[1], mine_ref.shape[0]
+    flat_ref[pl.ds(pl.multiple_of(pair * half, 16), half)] = mine_ref[...]
+    flat_ref[pl.ds(pl.multiple_of((1 - pair) * half, 16), half)] = other_ref[...]
+    flat = flat_ref[...].astype(F32) * scale
+    out_ref[0] = flat[:192, :64]
+    out_ref[1] = flat[:192, 64:]
+    out_ref[2, :96] = flat[192:, :64]
+    out_ref[2, 96:] = flat[192:, 64:]
 
 
 def even_swap(values, axis, count):
@@ -243,6 +249,15 @@
     first = even_swap(jnp.where(even, tail, head), axis, count)
     second = odd_swap(jnp.where(even, head, tail), axis, count)
     return jnp.where(even, second, first), jnp.where(even, first, second)
+
+
+def sum_cols(part):
+    count, step = lax.axis_size("col"), 1
+    while step < count:
+        sent = part.astype(BF16)
+        part = sent.astype(F32) + xor_swap(sent, "col", count, step).astype(F32)
+        step *= 2
+    return part
 
 
 def local(features_in, filters_one, filters_two, out_grad):
@@ -258,6 +273,7 @@
     at_strip = jnp.stack([strip]).astype(jnp.int32)
     at_band = jnp.stack([band]).astype(jnp.int32)
     at_pair = jnp.stack([pair]).astype(jnp.int32)
+    at_place = jnp.stack([strip, pair]).astype(jnp.int32)
 
     taps_one = jnp.transpose(filters_one, (1, 2, 0, 3)).reshape(3, 3 * channels, channels)
     back_one = jnp.transpose(filters_one[:, ::-1], (2, 3, 1, 0)).reshape(3 * channels, 3 * channels)
@@ -265,9 +281,15 @@
 
     x = jnp.transpose(features_in, (1, 0, 2))
     above, below = border_swap(x[:2], x[-2:], "row", band)
-    x = jnp.concatenate([above, x, below], 0)
-    side_a = even_swap(x, COLS, strips)
-    side_b = odd_swap(x, COLS, strips)
+    og = jnp.transpose(out_grad, (1, 2, 0))
+    edge = REACH - 1
+    head, tail = (
+        jnp.pad(e.reshape(-1, 128), ((0, channels - e.size // 128), (0, 0)))[None]
+        for e in (og[:edge], og[-edge:])
+    )
+    even = strip % 2 == 0
+    side_a = even_swap(jnp.concatenate([above, x, below, jnp.where(even, tail, head)], 0), COLS, strips)
+    side_b = odd_swap(jnp.concatenate([above, x, below, jnp.where(even, head, tail)], 0), COLS, strips)
     rows_wide = band_rows + 2
     pooled, slope, wide = whole_call(
         functools.partial(layer_one, total=total),
@@ -276,13 +298,13 @@
             shaped((rows_wide, channels, 256)),
             shaped((rows_wide + 2, channels, 256)),
         ],
-        [at_strip, x, side_a, side_b, taps_one],
+        [at_strip, x, above, below, side_a, side_b, taps_one],
         2 * rows_wide * 192 * 192 * 256,
     )
     pieces = [pooled] + [xor_swap(pooled, "row", bands, k) for k in range(1, bands)]
 
-    og = jnp.transpose(out_grad, (1, 2, 0))
-    before, after = border_swap(og[: REACH - 1], og[-(REACH - 1) :], COLS, strip)
+    ends = [side[-1].reshape(-1)[: og[:edge].size].reshape(og[:edge].shape) for side in (side_a, side_b)]
+    before, after = jnp.where(even, ends[1], ends[0]), jnp.where(even, ends[0], ends[1])
     og = jnp.concatenate([before, og, after], 0)
     og = jnp.pad(og, ((1, PITCH - own_cols - 2 * REACH + 1), (0, 0), (0, 0)))
     og = jnp.transpose(og, (1, 0, 2))
@@ -302,42 +324,43 @@
     received = [terms[0]] + [xor_swap(terms[k], "row", bands, k) for k in range(1, bands)]
 
     half = 9 * filters // 2
-    keep, send = whole_call(
+    keep_two, send_two = whole_call(
         filter_two_grads,
         [shaped((half, 4 * channels))] * 2,
         [at_pair, pooled_map, grad_cat],
-        2 * count * 9 * filters * 4 * channels,
+        0,
         scratch=[pltpu.VMEM((2 * half, 4 * channels), BF16)],
     )
-    part = keep.astype(F32) + even_swap(send, "pair", 2).astype(F32)
-    step = 1
-    while step < lax.axis_size("col"):
-        sent = part.astype(BF16)
-        part = sent.astype(F32) + xor_swap(sent, "col", lax.axis_size("col"), step).astype(F32)
-        step *= 2
-    mine = part.astype(BF16)
+    swapped = even_swap(send_two, "pair", 2)
+    share = 9 * channels * channels // 256
+    g, keep, send = whole_call(
+        functools.partial(grad_pre_one, bands=bands, total=total),
+        [shaped((rows_wide, channels, 256))] + [shaped((share, 128))] * 2,
+        [at_place] + received + [slope, wide],
+        2 * 8 * 192 * 192 * 256,
+        scratch=[pltpu.VMEM((2 * share, 128), BF16)],
+    )
+    (part_two,) = whole_call(
+        add_after, [shaped(keep_two.shape)], [keep_two, swapped, keep], 0, scalars=0
+    )
+    mine = sum_cols(part_two).astype(BF16)
     other = even_swap(mine, "pair", 2)
     grad_two = jnp.concatenate([jnp.where(pair == 0, mine, other), jnp.where(pair == 0, other, mine)], 0)
     grad_two = grad_two.astype(F32) * (1.0 / math.sqrt(pooled_rows * total))
     grad_two = jnp.transpose(grad_two.reshape(3, 3, filters, 4 * channels), (2, 0, 1, 3))
 
-    devices = lax.axis_size(EVERY)
-    share = -(-288 // (8 * devices)) * 8
-    g, part_one = whole_call(
-        functools.partial(grad_pre_one, bands=bands, total=total),
-        [shaped((rows_wide, channels, 256)), shaped((devices * share, 128))],
-        [at_strip] + received + [slope, wide],
-        2 * 8 * 192 * 192 * 256,
-    )
-    parts = lax.all_to_all(part_one.reshape(devices, share, 128), EVERY, 0, 0, tiled=True)
-    (copies,) = whole_call(sum_and_copy, [shaped((devices, share, 128))], [parts], 1, scalars=0)
-    flat = lax.all_to_all(copies, EVERY, 0, 0, tiled=True).reshape(devices * share, 128)
+    part = sum_cols(keep.astype(F32) + even_swap(send, "pair", 2).astype(F32)).astype(BF16)
+    terms = [part.astype(F32)] + [xor_swap(part, "row", bands, k).astype(F32) for k in range(1, bands)]
+    while len(terms) > 1:
+        terms = [a + b for a, b in zip(terms[::2], terms[1::2])]
+    mine = terms[0].astype(BF16)
+    other = even_swap(mine, "pair", 2)
     (grad_one,) = whole_call(
         functools.partial(unpack_one, scale=1.0 / math.sqrt(height * width)),
         [shaped((3, 3 * channels, channels), F32)],
-        [flat],
+        [at_place, mine, other],
         1,
-        scalars=0,
+        scratch=[pltpu.VMEM((2 * share, 128), BF16)],
     )
     grad_one = jnp.transpose(grad_one.reshape(3, 3, channels, channels), (2, 0, 1, 3))
     (input_grad,) = whole_call(

time: 66.9 us -> 61.8 us (0.924)
  starting transfers between devices: 32.5 us -> 28.6 us
  waiting for transfers between devices: 22.5 us -> 21.4 us
    all_to_all x2 -> x0, waiting for transfers between devices: 12.8 us -> none  [the longest x1 6.93 us: local(): lax.all_to_all(part_one.reshape(devices, share, 128), EVERY, 0, 0, tiled=...]
    ppermute x7 -> x11, waiting for transfers between devices: 7.43 us -> 19.3 us  [xor_swap(): return lax.ppermute(values, axis, [(n, n ^ k) for n in range(count)])]
    all_to_all x2 -> x0, starting transfers between devices: 7.01 us -> none  [the longest x1 3.51 us: local(): lax.all_to_all(copies, EVERY, 0, 0, tiled=True)]
    ppermute x7 -> x11, starting transfers between devices: 10.5 us -> 17.5 us  [xor_swap(): return lax.ppermute(values, axis, [(n, n ^ k) for n in range(count)])]
    ppermute x5 -> x6, starting transfers between devices: 12.9 us -> 9.73 us  [even_swap(): return lax.ppermute(values, axis, [(n, n ^ 1) for n in range(count)])]
    ppermute x3 -> x2, starting transfers between devices: 2 us -> 1.34 us  [odd_swap(): return lax.ppermute(values, axis, steps + [(b, a) for a, b in steps])]
    ppermute x5 -> x6, waiting for transfers between devices: 2.26 us -> 2.08 us  [even_swap(): return lax.ppermute(values, axis, [(n, n ^ 1) for n in range(count)])]
  transfers between devices with their start and end apart: 17 -> 19, of which waited for: 7 -> 9; matrix products, arithmetic and copies ran while one was open for 2% -> 2% of each run, Pallas kernels for 6% -> 7%
where the time goes in v2:
time: 61.8 us; the launch traced here: 61.5 us
  starting transfers between devices  28.6 us (46%)
  waiting for transfers between devices  21.4 us (35%)
  Pallas kernels  6.99 us (11%)
  local copies, waits for them, and re-layouts  2.22 us (4%)
  other arithmetic  1.46 us (2%)
  between operations  0.89 us (1%)
    ppermute x11, waiting for transfers between devices, xor_swap(): return lax.ppermute(values, axis, [(n, n ^ k) for n in range(count)])  19.3 us
    ppermute x11, starting transfers between devices, xor_swap(): return lax.ppermute(values, axis, [(n, n ^ k) for n in range(count)])  17.5 us
    ppermute x6, starting transfers between devices, even_swap(): return lax.ppermute(values, axis, [(n, n ^ 1) for n in range(count)])  9.73 us
    pallas_call x7, Pallas kernels, whole_call(): pl.pallas_call(body, out_shape=outs, in_specs=specs, out_specs=[pl.BlockS...  6.99 us
    ppermute x6, waiting for transfers between devices, even_swap(): return lax.ppermute(values, axis, [(n, n ^ 1) for n in range(count)])  2.08 us
    unnamed x6, local copies, waits for them, and re-layouts  1.85 us
    ppermute x2, starting transfers between devices, odd_swap(): return lax.ppermute(values, axis, steps + [(b, a) for a, b in steps])  1.34 us
  transfers between devices with their start and end apart: 19, of which 9 were waited for; matrix products, arithmetic and copies ran while one was open for 2% of the time, Pallas kernels for 7%

profile of v2, /device:TPU:0, one launch (start us, length us, event | category | flops | bytes accessed | tf_op | source)
XLA Modules:
  0.0 61.5 jit_solution(10494895671343856763)
XLA Ops:
  0.7 1.0 %copy.21 = bf16[64,8,128]{2,0,1:T(8,128)(2,1)S(1)} copy(bf16[64,8,128]{2,1,0:T(8,128)(2,1)} %param.4) | data formatting | bytes 262144 | tf_op args[0]
  2.3 5.9 %collective-permute-start.1 = (bf16[2,64,128]{2,1,0:T(8,128)(2,1)S(1)}, bf16[2,64,128]{2,1,0:T(8,128)(2,1)S(1)}, u32[]{:S(2)}, u32[]{:S(2)}) collective-permute-start(bf16[2,64,128]{2,1,0:T(8,128)(2,1)S(1)} %get-tuple-element.38), channel_id=1, source_target_pairs={{0,4},{4,0},{8,12},{12,8},{1,5},{5,1},{9,13},{13,9},{2,6},{6,2},{1... | collective-permute-start | bytes 98312 | tf_op jit(solution)/shard_map/ppermute | solution.py:234
  10.9 2.9 %collective-permute-start.3 = (bf16[13,64,128]{2,1,0:T(8,128)(2,1)S(1)}, bf16[13,64,128]{2,1,0:T(8,128)(2,1)S(1)}, u32[]{:S(2)}, u32[]{:S(2)}) collective-permute-start(bf16[13,64,128]{2,1,0:T(8,128)(2,1)S(1)} %get-tuple-element.36), channel_id=1, source_target_pairs={{0,1},{1,0},{2,3},{3,2},{4,5},{5,4},{6,7},{7,6},{8,9},{9,8},{10,11... | collective-permute-start | bytes 638984 | tf_op jit(solution)/shard_map/ppermute | solution.py:234
  13.8 1.1 %collective-permute-done.3.a_ref = bf16[13,64,128]{2,1,0:T(8,128)(2,1)S(1)} collective-permute-done((bf16[13,64,128]{2,1,0:T(8,128)(2,1)S(1)}, bf16[13,64,128]{2,1,0:T(8,128)(2,1)S(1)}, u32[]{:S(2)}, u32[]{:S(2)}) %collective-permute-start.3) | collective-permute-done | bytes 213024 | tf_op jit(solution)/shard_map/ppermute | solution.py:234
  15.8 2.1 %collective-permute-start.4 = (bf16[2,40,256]{2,1,0:T(8,128)(2,1)S(1)}, bf16[2,40,256]{2,1,0:T(8,128)(2,1)S(1)}, u32[]{:S(2)}, u32[]{:S(2)}) collective-permute-start(bf16[2,40,256]{2,1,0:T(8,128)(2,1)S(1)} %get-tuple-element.17.refs_0_), channel_id=1, source_target_pairs={{0,4},{4,0},{8,12},{12,8},{1,5},{5,1},{9,13},{13,9},{2,6},{6,2},{1... | collective-permute-start | bytes 122888 | tf_op jit(solution)/shard_map/ppermute | solution.py:243
  17.9 2.4 %collective-permute-start.6 = (bf16[2,40,256]{2,1,0:T(8,128)(2,1)S(1)}, bf16[2,40,256]{2,1,0:T(8,128)(2,1)S(1)}, u32[]{:S(2)}, u32[]{:S(2)}) collective-permute-start(bf16[2,40,256]{2,1,0:T(8,128)(2,1)S(1)} %get-tuple-element.17.refs_0_), channel_id=1, source_target_pairs={{0,12},{4,8},{8,4},{12,0},{1,13},{5,9},{9,5},{13,1},{2,14},{6,10},... | collective-permute-start | bytes 122888 | tf_op jit(solution)/shard_map/ppermute | solution.py:243
  20.4 2.4 %collective-permute-done.5.refs_2_ = bf16[2,40,256]{2,1,0:T(8,128)(2,1)S(1)} collective-permute-done((bf16[2,40,256]{2,1,0:T(8,128)(2,1)S(1)}, bf16[2,40,256]{2,1,0:T(8,128)(2,1)S(1)}, u32[]{:S(2)}, u32[]{:S(2)}) %collective-permute-start.5) | collective-permute-done | bytes 40992 | tf_op jit(solution)/shard_map/ppermute | solution.py:243
  22.8 1.4 %collective-permute-done.6.refs_3_ = bf16[2,40,256]{2,1,0:T(8,128)(2,1)S(1)} collective-permute-done((bf16[2,40,256]{2,1,0:T(8,128)(2,1)S(1)}, bf16[2,40,256]{2,1,0:T(8,128)(2,1)S(1)}, u32[]{:S(2)}, u32[]{:S(2)}) %collective-permute-start.6) | collective-permute-done | bytes 40992 | tf_op jit(solution)/shard_map/ppermute | solution.py:243
  24.2 1.5 %shard_map.68 = (bf16[3,40,256]{2,1,0:T(8,128)(2,1)S(1)}, bf16[3,40,256]{2,1,0:T(8,128)(2,1)S(1)}, bf16[3,40,256]{2,1,0:T(8,128)(2,1)S(1)}, bf16[3,40,256]{2,1,0...) custom-call(s32[1]{0:T(128)} %bitcast.2.info, bf16[8,48,128]{2,1,0:T(8,128)(2,1)S(1)} %fusion.6.og_ref, ...), custom_call_target="tpu_custom_call" | custom-call | flops 452984832 | bytes 1638400 | tf_op jit(solution)/shard_map/pallas_call | solution.py:30
  26.9 1.0 %collective-permute-start.7 = (bf16[3,40,256]{2,1,0:T(8,128)(2,1)S(1)}, bf16[3,40,256]{2,1,0:T(8,128)(2,1)S(1)}, u32[]{:S(2)}, u32[]{:S(2)}) collective-permute-start(bf16[3,40,256]{2,1,0:T(8,128)(2,1)S(1)} %get-tuple-element.19), channel_id=1, source_target_pairs={{0,4},{4,0},{8,12},{12,8},{1,5},{5,1},{9,13},{13,9},{2,6},{6,2},{1... | collective-permute-start | bytes 184328 | tf_op jit(solution)/shard_map/ppermute | solution.py:243
  27.9 1.9 %collective-permute-start.8 = (bf16[3,40,256]{2,1,0:T(8,128)(2,1)S(1)}, bf16[3,40,256]{2,1,0:T(8,128)(2,1)S(1)}, u32[]{:S(2)}, u32[]{:S(2)}) collective-permute-start(bf16[3,40,256]{2,1,0:T(8,128)(2,1)S(1)} %get-tuple-element.20), channel_id=1, source_target_pairs={{0,8},{4,12},{8,0},{12,4},{1,9},{5,13},{9,1},{13,5},{2,10},{6,14},... | collective-permute-start | bytes 184328 | tf_op jit(solution)/shard_map/ppermute | solution.py:243
  29.8 1.5 %collective-permute-start.9 = (bf16[3,40,256]{2,1,0:T(8,128)(2,1)S(1)}, bf16[3,40,256]{2,1,0:T(8,128)(2,1)S(1)}, u32[]{:S(2)}, u32[]{:S(2)}) collective-permute-start(bf16[3,40,256]{2,1,0:T(8,128)(2,1)S(1)} %get-tuple-element.21), channel_id=1, source_target_pairs={{0,12},{4,8},{8,4},{12,0},{1,13},{5,9},{9,5},{13,1},{2,14},{6,10},... | collective-permute-start | bytes 184328 | tf_op jit(solution)/shard_map/ppermute | solution.py:243
  31.4 3.8 %collective-permute-done.8.refs_2_ = bf16[3,40,256]{2,1,0:T(8,128)(2,1)S(1)} collective-permute-done((bf16[3,40,256]{2,1,0:T(8,128)(2,1)S(1)}, bf16[3,40,256]{2,1,0:T(8,128)(2,1)S(1)}, u32[]{:S(2)}, u32[]{:S(2)}) %collective-permute-start.8) | collective-permute-done | bytes 61472 | tf_op jit(solution)/shard_map/ppermute | solution.py:243
  35.9 1.5 %shard_map.69 = (bf16[10,64,256]{2,1,0:T(8,128)(2,1)S(1)}, bf16[144,128]{1,0:T(8,128)(2,1)S(1)}, bf16[144,128]{1,0:T(8,128)(2,1)S(1)}) custom-call(s32[2]{0:T(128)S(1)} %pad_add_fusion.info, bf16[3,40,256]{2,1,0:T(8,128)(2,1)S(1)} %get-tuple-element.18.refs_0_, bf16[3,40,256]{2,1,0:T(8,128)(2,1)S(1)} %collective-permute-done.7.refs_1_, ...), custom_call_target="tpu_custom_call" | custom-call | flops 150994944 | bytes 1368064 | tf_op jit(solution)/shard_map/pallas_call | solution.py:30
  37.6 3.1 %collective-permute-start.17 = (bf16[576,256]{1,0:T(8,128)(2,1)S(1)}, bf16[576,256]{1,0:T(8,128)(2,1)S(1)}, u32[]{:S(2)}, u32[]{:S(2)}) collective-permute-start(bf16[576,256]{1,0:T(8,128)(2,1)S(1)} %shard_map.73), channel_id=1, source_target_pairs={{0,2},{2,0},{1,3},{3,1},{4,6},{6,4},{5,7},{7,5},{8,10},{10,8},{9,1... | collective-permute-start | bytes 884744 | tf_op jit(solution)/shard_map/ppermute | solution.py:243
  40.7 1.1 %collective-permute-start.11 = (bf16[144,128]{1,0:T(8,128)(2,1)S(1)}, bf16[144,128]{1,0:T(8,128)(2,1)S(1)}, u32[]{:S(2)}, u32[]{:S(2)}) collective-permute-start(bf16[144,128]{1,0:T(8,128)(2,1)S(1)} %add_convert_fusion.3), channel_id=1, source_target_pairs={{0,2},{2,0},{1,3},{3,1},{4,6},{6,4},{5,7},{7,5},{8,10},{10,8},{9,1... | collective-permute-start | bytes 110600 | tf_op jit(solution)/shard_map/ppermute | solution.py:243
  41.8 7.3 %collective-permute-done.11 = bf16[144,128]{1,0:T(8,128)(2,1)S(1)} collective-permute-done((bf16[144,128]{1,0:T(8,128)(2,1)S(1)}, bf16[144,128]{1,0:T(8,128)(2,1)S(1)}, u32[]{:S(2)}, u32[]{:S(2)}) %collective-permute-start.11) | collective-permute-done | bytes 36896 | tf_op jit(solution)/shard_map/ppermute | solution.py:243
  50.0 1.6 %collective-permute-start.13 = (bf16[144,128]{1,0:T(8,128)(2,1)S(1)}, bf16[144,128]{1,0:T(8,128)(2,1)S(1)}, u32[]{:S(2)}, u32[]{:S(2)}) collective-permute-start(bf16[144,128]{1,0:T(8,128)(2,1)S(1)} %add_convert_fusion.2), channel_id=1, source_target_pairs={{0,8},{4,12},{8,0},{12,4},{1,9},{5,13},{9,1},{13,5},{2,10},{6,14},... | collective-permute-start | bytes 110600 | tf_op jit(solution)/shard_map/ppermute | solution.py:243
  51.6 2.0 %collective-permute-start.14 = (bf16[144,128]{1,0:T(8,128)(2,1)S(1)}, bf16[144,128]{1,0:T(8,128)(2,1)S(1)}, u32[]{:S(2)}, u32[]{:S(2)}) collective-permute-start(bf16[144,128]{1,0:T(8,128)(2,1)S(1)} %add_convert_fusion.2), channel_id=1, source_target_pairs={{0,12},{4,8},{8,4},{12,0},{1,13},{5,9},{9,5},{13,1},{2,14},{6,10},... | collective-permute-start | bytes 110600 | tf_op jit(solution)/shard_map/ppermute | solution.py:243
  53.7 1.4 %collective-permute-done.13 = bf16[144,128]{1,0:T(8,128)(2,1)S(1)} collective-permute-done((bf16[144,128]{1,0:T(8,128)(2,1)S(1)}, bf16[144,128]{1,0:T(8,128)(2,1)S(1)}, u32[]{:S(2)}, u32[]{:S(2)}) %collective-permute-start.13) | collective-permute-done | bytes 36896 | tf_op jit(solution)/shard_map/ppermute | solution.py:243
  55.2 2.2 %collective-permute-done.14 = bf16[144,128]{1,0:T(8,128)(2,1)S(1)} collective-permute-done((bf16[144,128]{1,0:T(8,128)(2,1)S(1)}, bf16[144,128]{1,0:T(8,128)(2,1)S(1)}, u32[]{:S(2)}, u32[]{:S(2)}) %collective-permute-start.14) | collective-permute-done | bytes 36896 | tf_op jit(solution)/shard_map/ppermute | solution.py:243
  57.8 1.2 %shard_map.70 = bf16[64,8,128]{2,1,0:T(8,128)(2,1)} custom-call(bf16[10,64,256]{2,1,0:T(8,128)(2,1)S(1)} %get-tuple-element.24.g_ref, bf16[192,192]{1,0:T(8,128)(2,1)S(1)} %reshape.45.w_ref), custom_call_target="tpu_custom_call" | custom-call | flops 150994944 | bytes 532480 | tf_op jit(solution)/shard_map/pallas_call | solution.py:30
  59.0 1.4 %shard_map.71 = f32[3,192,64]{2,1,0:T(8,128)} custom-call(s32[2]{0:T(128)S(1)} %pad_add_fusion.info, bf16[144,128]{1,0:T(8,128)(2,1)S(1)} %add_convert_fusion.1.mine_ref, bf16[144,128]{1,0:T(8,128)(2,1)S(1)} %collective-permute-done.15.other_ref), custom_call_target="tpu_custom_call" | custom-call | flops 1 | bytes 221184 | tf_op jit(solution)/shard_map/pallas_call | solution.py:30
  60.4 1.1 %convert_multiply_fusion = f32[1152,256]{1,0:T(8,128)} fusion(bf16[576,256]{1,0:T(8,128)(2,1)S(1)} %get-tuple-element.32, bf16[576,256]{1,0:T(8,128)(2,1)S(1)} %get-tuple-element.31), kind=kLoop, calls=%fused_computation | loop fusion | flops 1474560 | bytes 1769472 | tf_op jit(solution)/shard_map/mul | solution.py:349
  (47 shorter events, 8.0 us)
Async XLA Ops:
  0.6 14.3 %copy-start = (bf16[64,3,3,64]{3,0,2,1:T(8,128)(2,1)S(1)}, bf16[64,3,3,64]{3,0,2,1:T(8,128)(2,1)}, u32[]{:S(2)}) copy-start(bf16[64,3,3,64]{3,0,2,1:T(8,128)(2,1)} %param.5) | copy-start | bytes 221188
  0.7 23.6 %copy-start.1 = (bf16[128,3,3,256]{3,0,2,1:T(8,128)(2,1)S(1)}, bf16[128,3,3,256]{3,0,2,1:T(8,128)(2,1)}, u32[]{:S(2)}) copy-start(bf16[128,3,3,256]{3,0,2,1:T(8,128)(2,1)} %param.6) | copy-start | bytes 1769476
  1.7 7.5 %collective-permute-start = (bf16[2,64,128]{2,1,0:T(8,128)(2,1)S(1)}, bf16[2,64,128]{2,1,0:T(8,128)(2,1)S(1)}, u32[]{:S(2)}, u32[]{:S(2)}) collective-permute-start(bf16[2,64,128]{2,1,0:T(8,128)(2,1)S(1)} %get-tuple-element.37), channel_id=1, source_target_pairs={{4,8},{8,4},{5,9},{9,5},{6,10},{10,6},{7,11},{11,7},{20,24},{24,20... | collective-permute-start | bytes 98312 | tf_op jit(solution)/shard_map/ppermute | solution.py:239
  2.3 7.8 %collective-permute-start.1 = (bf16[2,64,128]{2,1,0:T(8,128)(2,1)S(1)}, bf16[2,64,128]{2,1,0:T(8,128)(2,1)S(1)}, u32[]{:S(2)}, u32[]{:S(2)}) collective-permute-start(bf16[2,64,128]{2,1,0:T(8,128)(2,1)S(1)} %get-tuple-element.38), channel_id=1, source_target_pairs={{0,4},{4,0},{8,12},{12,8},{1,5},{5,1},{9,13},{13,9},{2,6},{6,2},{1... | collective-permute-start | bytes 98312 | tf_op jit(solution)/shard_map/ppermute | solution.py:234
  10.2 3.6 %collective-permute-start.2 = (bf16[13,64,128]{2,1,0:T(8,128)(2,1)S(1)}, bf16[13,64,128]{2,1,0:T(8,128)(2,1)S(1)}, u32[]{:S(2)}, u32[]{:S(2)}) collective-permute-start(bf16[13,64,128]{2,1,0:T(8,128)(2,1)S(1)} %get-tuple-element.35), channel_id=1, source_target_pairs={{1,2},{2,1},{5,6},{6,5},{9,10},{10,9},{13,14},{14,13},{17,18},{18,... | collective-permute-start | bytes 638984 | tf_op jit(solution)/shard_map/ppermute | solution.py:239
  10.9 4.0 %collective-permute-start.3 = (bf16[13,64,128]{2,1,0:T(8,128)(2,1)S(1)}, bf16[13,64,128]{2,1,0:T(8,128)(2,1)S(1)}, u32[]{:S(2)}, u32[]{:S(2)}) collective-permute-start(bf16[13,64,128]{2,1,0:T(8,128)(2,1)S(1)} %get-tuple-element.36), channel_id=1, source_target_pairs={{0,1},{1,0},{2,3},{3,2},{4,5},{5,4},{6,7},{7,6},{8,9},{9,8},{10,11... | collective-permute-start | bytes 638984 | tf_op jit(solution)/shard_map/ppermute | solution.py:234
  15.8 4.6 %collective-permute-start.4 = (bf16[2,40,256]{2,1,0:T(8,128)(2,1)S(1)}, bf16[2,40,256]{2,1,0:T(8,128)(2,1)S(1)}, u32[]{:S(2)}, u32[]{:S(2)}) collective-permute-start(bf16[2,40,256]{2,1,0:T(8,128)(2,1)S(1)} %get-tuple-element.17.refs_0_), channel_id=1, source_target_pairs={{0,4},{4,0},{8,12},{12,8},{1,5},{5,1},{9,13},{13,9},{2,6},{6,2},{1... | collective-permute-start | bytes 122888 | tf_op jit(solution)/shard_map/ppermute | solution.py:243
  17.9 4.9 %collective-permute-start.5 = (bf16[2,40,256]{2,1,0:T(8,128)(2,1)S(1)}, bf16[2,40,256]{2,1,0:T(8,128)(2,1)S(1)}, u32[]{:S(2)}, u32[]{:S(2)}) collective-permute-start(bf16[2,40,256]{2,1,0:T(8,128)(2,1)S(1)} %get-tuple-element.17.refs_0_), channel_id=1, source_target_pairs={{0,8},{4,12},{8,0},{12,4},{1,9},{5,13},{9,1},{13,5},{2,10},{6,14},... | collective-permute-start | bytes 122888 | tf_op jit(solution)/shard_map/ppermute | solution.py:243
  17.9 6.3 %collective-permute-start.6 = (bf16[2,40,256]{2,1,0:T(8,128)(2,1)S(1)}, bf16[2,40,256]{2,1,0:T(8,128)(2,1)S(1)}, u32[]{:S(2)}, u32[]{:S(2)}) collective-permute-start(bf16[2,40,256]{2,1,0:T(8,128)(2,1)S(1)} %get-tuple-element.17.refs_0_), channel_id=1, source_target_pairs={{0,12},{4,8},{8,4},{12,0},{1,13},{5,9},{9,5},{13,1},{2,14},{6,10},... | collective-permute-start | bytes 122888 | tf_op jit(solution)/shard_map/ppermute | solution.py:243
  26.2 11.3 %collective-permute-start.16 = (bf16[576,256]{1,0:T(8,128)(2,1)S(1)}, bf16[576,256]{1,0:T(8,128)(2,1)S(1)}, u32[]{:S(2)}, u32[]{:S(2)}) collective-permute-start(bf16[576,256]{1,0:T(8,128)(2,1)S(1)} %get-tuple-element.30), channel_id=1, source_target_pairs={{0,1},{1,0},{2,3},{3,2},{4,5},{5,4},{6,7},{7,6},{8,9},{9,8},{10,11... | collective-permute-start | bytes 884744 | tf_op jit(solution)/shard_map/ppermute | solution.py:234
  26.9 4.5 %collective-permute-start.7 = (bf16[3,40,256]{2,1,0:T(8,128)(2,1)S(1)}, bf16[3,40,256]{2,1,0:T(8,128)(2,1)S(1)}, u32[]{:S(2)}, u32[]{:S(2)}) collective-permute-start(bf16[3,40,256]{2,1,0:T(8,128)(2,1)S(1)} %get-tuple-element.19), channel_id=1, source_target_pairs={{0,4},{4,0},{8,12},{12,8},{1,5},{5,1},{9,13},{13,9},{2,6},{6,2},{1... | collective-permute-start | bytes 184328 | tf_op jit(solution)/shard_map/ppermute | solution.py:243
  27.9 7.2 %collective-permute-start.8 = (bf16[3,40,256]{2,1,0:T(8,128)(2,1)S(1)}, bf16[3,40,256]{2,1,0:T(8,128)(2,1)S(1)}, u32[]{:S(2)}, u32[]{:S(2)}) collective-permute-start(bf16[3,40,256]{2,1,0:T(8,128)(2,1)S(1)} %get-tuple-element.20), channel_id=1, source_target_pairs={{0,8},{4,12},{8,0},{12,4},{1,9},{5,13},{9,1},{13,5},{2,10},{6,14},... | collective-permute-start | bytes 184328 | tf_op jit(solution)/shard_map/ppermute | solution.py:243
  29.8 6.1 %collective-permute-start.9 = (bf16[3,40,256]{2,1,0:T(8,128)(2,1)S(1)}, bf16[3,40,256]{2,1,0:T(8,128)(2,1)S(1)}, u32[]{:S(2)}, u32[]{:S(2)}) collective-permute-start(bf16[3,40,256]{2,1,0:T(8,128)(2,1)S(1)} %get-tuple-element.21), channel_id=1, source_target_pairs={{0,12},{4,8},{8,4},{12,0},{1,13},{5,9},{9,5},{13,1},{2,14},{6,10},... | collective-permute-start | bytes 184328 | tf_op jit(solution)/shard_map/ppermute | solution.py:243
  37.4 3.2 %collective-permute-start.10 = (bf16[144,128]{1,0:T(8,128)(2,1)S(1)}, bf16[144,128]{1,0:T(8,128)(2,1)S(1)}, u32[]{:S(2)}, u32[]{:S(2)}) collective-permute-start(bf16[144,128]{1,0:T(8,128)(2,1)S(1)} %get-tuple-element.26), channel_id=1, source_target_pairs={{0,1},{1,0},{2,3},{3,2},{4,5},{5,4},{6,7},{7,6},{8,9},{9,8},{10,11... | collective-permute-start | bytes 110600 | tf_op jit(solution)/shard_map/ppermute | solution.py:234
  37.6 16.0 %collective-permute-start.17 = (bf16[576,256]{1,0:T(8,128)(2,1)S(1)}, bf16[576,256]{1,0:T(8,128)(2,1)S(1)}, u32[]{:S(2)}, u32[]{:S(2)}) collective-permute-start(bf16[576,256]{1,0:T(8,128)(2,1)S(1)} %shard_map.73), channel_id=1, source_target_pairs={{0,2},{2,0},{1,3},{3,1},{4,6},{6,4},{5,7},{7,5},{8,10},{10,8},{9,1... | collective-permute-start | bytes 884744 | tf_op jit(solution)/shard_map/ppermute | solution.py:243
  40.7 8.4 %collective-permute-start.11 = (bf16[144,128]{1,0:T(8,128)(2,1)S(1)}, bf16[144,128]{1,0:T(8,128)(2,1)S(1)}, u32[]{:S(2)}, u32[]{:S(2)}) collective-permute-start(bf16[144,128]{1,0:T(8,128)(2,1)S(1)} %add_convert_fusion.3), channel_id=1, source_target_pairs={{0,2},{2,0},{1,3},{3,1},{4,6},{6,4},{5,7},{7,5},{8,10},{10,8},{9,1... | collective-permute-start | bytes 110600 | tf_op jit(solution)/shard_map/ppermute | solution.py:243
  49.1 4.6 %collective-permute-start.12 = (bf16[144,128]{1,0:T(8,128)(2,1)S(1)}, bf16[144,128]{1,0:T(8,128)(2,1)S(1)}, u32[]{:S(2)}, u32[]{:S(2)}) collective-permute-start(bf16[144,128]{1,0:T(8,128)(2,1)S(1)} %add_convert_fusion.2), channel_id=1, source_target_pairs={{0,4},{4,0},{8,12},{12,8},{1,5},{5,1},{9,13},{13,9},{2,6},{6,2},{1... | collective-permute-start | bytes 110600 | tf_op jit(solution)/shard_map/ppermute | solution.py:243
  50.0 5.2 %collective-permute-start.13 = (bf16[144,128]{1,0:T(8,128)(2,1)S(1)}, bf16[144,128]{1,0:T(8,128)(2,1)S(1)}, u32[]{:S(2)}, u32[]{:S(2)}) collective-permute-start(bf16[144,128]{1,0:T(8,128)(2,1)S(1)} %add_convert_fusion.2), channel_id=1, source_target_pairs={{0,8},{4,12},{8,0},{12,4},{1,9},{5,13},{9,1},{13,5},{2,10},{6,14},... | collective-permute-start | bytes 110600 | tf_op jit(solution)/shard_map/ppermute | solution.py:243
  51.6 5.8 %collective-permute-start.14 = (bf16[144,128]{1,0:T(8,128)(2,1)S(1)}, bf16[144,128]{1,0:T(8,128)(2,1)S(1)}, u32[]{:S(2)}, u32[]{:S(2)}) collective-permute-start(bf16[144,128]{1,0:T(8,128)(2,1)S(1)} %add_convert_fusion.2), channel_id=1, source_target_pairs={{0,12},{4,8},{8,4},{12,0},{1,13},{5,9},{9,5},{13,1},{2,14},{6,10},... | collective-permute-start | bytes 110600 | tf_op jit(solution)/shard_map/ppermute | solution.py:243
  53.7 6.7 %collective-permute-start.18 = (bf16[576,256]{1,0:T(8,128)(2,1)S(1)}, bf16[576,256]{1,0:T(8,128)(2,1)S(1)}, u32[]{:S(2)}, u32[]{:S(2)}) collective-permute-start(bf16[576,256]{1,0:T(8,128)(2,1)S(1)} %add_convert_fusion), channel_id=1, source_target_pairs={{0,1},{1,0},{2,3},{3,2},{4,5},{5,4},{6,7},{7,6},{8,9},{9,8},{10,11... | collective-permute-start | bytes 884744 | tf_op jit(solution)/shard_map/ppermute | solution.py:234
  57.4 1.6 %collective-permute-start.15 = (bf16[144,128]{1,0:T(8,128)(2,1)S(1)}, bf16[144,128]{1,0:T(8,128)(2,1)S(1)}, u32[]{:S(2)}, u32[]{:S(2)}) collective-permute-start(bf16[144,128]{1,0:T(8,128)(2,1)S(1)} %add_convert_fusion.1.mine_ref), channel_id=1, source_target_pairs={{0,1},{1,0},{2,3},{3,2},{4,5},{5,4},{6,7},{7,6},{8,9},{9,8},{10,11... | collective-permute-start | bytes 110600 | tf_op jit(solution)/shard_map/ppermute | solution.py:234

commit v3 on v2

--- a/solution.py
+++ b/solution.py
@@ -54,15 +54,18 @@
     return sig * (1.0 + values * (1.0 - sig))
 
 
-def pool_matrix(strip, total):
+def pool_matrix(strip, total, back=False):
     row = lax.broadcasted_iota(jnp.int32, (2 * PITCH, 256), 0)
     lane = lax.broadcasted_iota(jnp.int32, (2 * PITCH, 256), 1)
     half = (row >= PITCH).astype(jnp.int32)
-    v = row - half * PITCH
-    first = 4 * (v - REACH) + 2 * half
-    near = jnp.bitwise_and(lane - first, 255) < 2
-    place = strip * 32 + v - REACH
-    keep = near & (v < 32 + 2 * REACH) & (place >= 0) & (place < total)
+    n = row - half * PITCH
+    if back:
+        v, most = jnp.where((n == 32) & (half == 1), -1, n), 33
+    else:
+        v, most = n - REACH, 32 + 2 * REACH
+    near = jnp.bitwise_and(lane - 4 * v - 2 * half, 255) < 2
+    place = strip * 32 + v
+    keep = near & (n < most) & (place >= 0) & (place < total)
     return jnp.where(keep, 0.25, 0.0).astype(BF16)
 
 
@@ -73,19 +76,43 @@
     return jnp.where(lane == 4 * c + 2 * i + j, 1.0, 0.0).astype(BF16)
 
 
+def pack_sides(info, x_ref, above_ref, below_ref, head_ref, tail_ref, a_ref, b_ref):
+    even = (info[0] & 1) == 0
+    rows = [above_ref[...]] + [x_ref[h] for h in range(x_ref.shape[0])] + [below_ref[...]]
+    lane = lax.broadcasted_iota(jnp.int32, (64, 128), 1)
+    tiles = [[jnp.zeros((64, 128), F32)] * 2 for _ in range(2)]
+    for r, row in enumerate(rows):
+        wide, slot = row.astype(F32), r % 8
+        for side, shift in enumerate((16 * slot, 16 * slot + 16)):
+            here = (lane >> 4) == slot
+            tiles[side][r // 8] = jnp.where(here, roll(wide, shift, 1), tiles[side][r // 8])
+    head, tail = tiles
+    for t in range(2):
+        a_ref[64 * t : 64 * t + 64] = jnp.where(even, tail[t], head[t]).astype(BF16)
+        b_ref[64 * t : 64 * t + 64] = jnp.where(even, head[t], tail[t]).astype(BF16)
+    first, last = head_ref[...].astype(F32), tail_ref[...].astype(F32)
+    a_ref[128:] = jnp.where(even, last, first).astype(BF16)
+    b_ref[128:] = jnp.where(even, first, last).astype(BF16)
+
+
 def layer_one(
     info, x_ref, above_ref, below_ref, a_ref, b_ref, w_ref, pooled_ref, slope_ref, wide_ref, *, total
 ):
     strip = info[0]
     band_rows = x_ref.shape[0]
-    lane = lax.broadcasted_iota(jnp.int32, wide_ref.shape[:2] + (128,), 2)
-    from_a = (lane >= 64).astype(jnp.int32) == (strip & 1)
-    sides = a_ref[: band_rows + 4].astype(F32), b_ref[: band_rows + 4].astype(F32)
-    halo = jnp.where(from_a, *sides)
-    wide_ref[:2, :, :128] = above_ref[...]
-    wide_ref[2 : band_rows + 2, :, :128] = x_ref[...]
-    wide_ref[band_rows + 2 :, :, :128] = below_ref[...]
-    wide_ref[:, :, 128:] = halo.astype(BF16)
+    even = (strip & 1) == 0
+    lane = lax.broadcasted_iota(jnp.int32, (64, 128), 1)
+    sides = [ref[:128].astype(F32) for ref in (a_ref, b_ref)]
+    after, before = jnp.where(even, *sides), jnp.where(even, *sides[::-1])
+    for r in range(band_rows + 2):
+        tile, slot = 64 * (r // 8), r % 8
+        right = roll(after[tile : tile + 64], -16 * slot, 1)
+        left = roll(before[tile : tile + 64], -16 * slot - 16, 1)
+        halo = jnp.where(lane < 16, right, jnp.where(lane >= 112, left, 0.0))
+        wide_ref[r, :, 128:] = halo.astype(BF16)
+    wide_ref[0, :, :128] = above_ref[...]
+    wide_ref[1 : band_rows + 1, :, :128] = x_ref[...]
+    wide_ref[band_rows + 1, :, :128] = below_ref[...]
     weights = jnp.concatenate([w_ref[0], w_ref[1], w_ref[2]], axis=1)
     rows = slope_ref.shape[0]
     halves, held = [], None
@@ -94,12 +121,11 @@
         pre = roll(y[:64], 1, 1) + y[64:128] + roll(y[128:], -1, 1)
         sig = sigmoid(pre)
         slope_ref[h] = slope_of(pre, sig).astype(BF16)
-        if 1 <= h <= rows - 2:
-            active = pre * sig
-            if h % 2:
-                held = active
-            else:
-                halves.append((held + active).astype(BF16))
+        active = pre * sig
+        if h % 2:
+            halves.append((held + active).astype(BF16))
+        else:
+            held = active
     pooled = dot(pool_matrix(strip, total), jnp.concatenate(halves, 0), (1, 1))
     stacked = jnp.concatenate(
         [
@@ -143,17 +169,15 @@
         weights = jnp.concatenate([w_ref[i, j * filters : (j + 1) * filters] for j in range(3)], 1)
         part = dot(grad_ref[2 - i : 2 - i + rows].reshape(count, filters), weights, (1, 0))
         z = part if z is None else z + part
-    spread = roll(z[:, :256], -1, 0) + z[:, 256:512] + roll(z[:, 512:], 1, 0)
-    spread_ref[0] = jnp.zeros((PITCH, 256), F32)
-    spread_ref[rows + 1] = jnp.zeros((PITCH, 256), F32)
-    spread_ref[1 : rows + 1] = spread.reshape(rows, PITCH, 256)
-    lower = (lax.broadcasted_iota(jnp.int32, (PITCH, 256), 1) & 2) == 0
+    spread = roll(z[:, :256], -1 - REACH, 0) + roll(z[:, 256:512], -REACH, 0) + roll(z[:, 512:], 1 - REACH, 0)
+    n = lax.broadcasted_iota(jnp.int32, (rows, PITCH, 256), 1).reshape(count, 256)
+    odd = (lax.broadcasted_iota(jnp.int32, (count, 256), 1) & 1) == 1
+    spread = jnp.where((n == 32) & odd, roll(spread, 33, 0), spread)
+    spread = jnp.where(n == 33, roll(spread, 33 - 32 - PITCH, 0), spread)
+    spread_ref[...] = spread.astype(BF16).reshape(rows, PITCH, 256)
     for k in range(bands):
         first = 2 * (band ^ k)
-        for t in range(2):
-            terms[k][t] = spread_ref[first + 1 + t][:SENT].astype(BF16)
-        edge = jnp.where(lower, spread_ref[first + 3], spread_ref[first])
-        terms[k][2] = edge[:SENT].astype(BF16)
+        terms[k][...] = jnp.concatenate([spread_ref[first, :40], spread_ref[first + 1, :32]], 0)
     wide = grad.astype(F32)
     v = lax.broadcasted_iota(jnp.int32, (rows, PITCH, filters), 1).reshape(count, filters)
     wide = jnp.where((v >= REACH) & (v < REACH + 32), wide, 0.0)
@@ -172,37 +196,40 @@
     send_ref[...] = all_ref[pl.ds(pl.multiple_of((1 - pair) * half, 16), half)]
 
 
-def add_after(a_ref, b_ref, after_ref, out_ref):
+def add_after(a_ref, b_ref, *refs):
+    out_ref = refs[-1]
     out_ref[...] = (a_ref[...].astype(F32) + b_ref[...].astype(F32)).astype(BF16)
 
 
 def grad_pre_one(info, *refs, bands, total):
     terms, refs = refs[:bands], refs[bands:]
-    slope_ref, wide_ref, g_ref, keep_ref, send_ref, part_ref = refs
+    slope_ref, wide_ref, g_ref, a_ref, b_ref, keep_ref, send_ref, part_ref = refs
     strip, pair = info[0], info[1]
     summed = terms[0][...].astype(F32)
     for k in range(1, bands):
         summed = summed + terms[k][...].astype(F32)
-    blank = jnp.zeros((PITCH - SENT, 256), F32)
-    stacked = jnp.concatenate([p for t in range(3) for p in (summed[t], blank)], 0).astype(BF16)
-    ordered = dot(stacked, order_matrix(), (1, 1)).astype(BF16)
-    pool = pool_matrix(strip, total)
-    ups = []
-    for t in range(3):
-        block = ordered[t * PITCH : (t + 1) * PITCH]
-        ups.append(dot(jnp.concatenate([block[:, :128], block[:, 128:]], 0), pool, (0, 0)))
-    quads = [ups[0][:64], ups[0][64:], ups[1][:64], ups[1][64:]]
-    rows = [ups[2][64:]] + [quads[h // 2] for h in range(8)] + [ups[2][:64]]
+    blank = jnp.zeros((8, 256), F32)
+    ends = summed[32:40]
+    blocks = [summed[:32], ends, blank, summed[40:], roll(ends, -1, 0), blank]
+    ordered = dot(jnp.concatenate(blocks, 0).astype(BF16), order_matrix(), (1, 1)).astype(BF16)
+    pool = pool_matrix(strip, total, back=True)
     acc = None
     own = lax.broadcasted_iota(jnp.int32, (64, 256), 1) < 128
-    for h in range(10):
-        g = (rows[h] * slope_ref[h].astype(F32)).astype(BF16)
-        g_ref[h] = g
-        if 1 <= h <= 8:
+    for u in range(2):
+        block = ordered[u * PITCH : (u + 1) * PITCH]
+        up = dot(jnp.concatenate([block[:, :128], block[:, 128:]], 0), pool, (0, 0))
+        for i in range(4):
+            h = 4 * u + i
+            g = (up[64 * (i // 2) : 64 * (i // 2) + 64] * slope_ref[h].astype(F32)).astype(BF16)
+            g_ref[h] = g
             mine = jnp.where(own, g.astype(F32), 0.0)
             cat = jnp.concatenate([roll(mine, -1, 1), mine, roll(mine, 1, 1)], 0).astype(BF16)
             part = dot(cat, wide_ref[h : h + 3].reshape(192, 256), (1, 1))
             acc = part if acc is None else acc + part
+    even = (info[2] & 1) == 0
+    first, last = g_ref[0].astype(F32), g_ref[7].astype(F32)
+    a_ref[...] = jnp.where(even, last, first).astype(BF16)
+    b_ref[...] = jnp.where(even, first, last).astype(BF16)
     part_ref[:192] = acc[:, :128].astype(BF16)
     tail = jnp.concatenate([acc[:96, 128:], acc[96:, 128:]], 1)
     part_ref[192:] = tail.astype(BF16)
@@ -211,10 +238,14 @@
     send_ref[...] = part_ref[pl.ds(pl.multiple_of((1 - pair) * half, 16), half)]
 
 
-def layer_one_back(g_ref, w_ref, out_ref):
+def layer_one_back(info, g_ref, a_ref, b_ref, w_ref, out_ref):
+    even = (info[2] & 1) == 0
+    sides = a_ref[...].astype(F32), b_ref[...].astype(F32)
+    below, above = jnp.where(even, *sides).astype(BF16), jnp.where(even, *sides[::-1]).astype(BF16)
+    lines = [above] + [g_ref[h] for h in range(8)] + [below]
     rows = []
     for h in range(8):
-        z = dot(w_ref[...], g_ref[h : h + 3].reshape(192, 256), (1, 0))
+        z = dot(w_ref[...], jnp.concatenate(lines[h : h + 3], 0), (1, 0))
         rows.append((roll(z[:64], -1, 1) + z[64:128] + roll(z[128:], 1, 1))[:, :128])
     out_ref[...] = jnp.swapaxes(jnp.stack(rows, 0), 0, 1).astype(BF16)
 
@@ -251,12 +282,20 @@
     return jnp.where(even, second, first), jnp.where(even, first, second)
 
 
-def sum_cols(part):
+def added(a, b, *after):
+    (total,) = whole_call(add_after, [shaped(a.shape)], [a, b, *after], 0, scalars=0)
+    return total
+
+
+def sum_cols(part, after=()):
     count, step = lax.axis_size("col"), 1
     while step < count:
-        sent = part.astype(BF16)
-        part = sent.astype(F32) + xor_swap(sent, "col", count, step).astype(F32)
+        other = xor_swap(part, "col", count, step)
         step *= 2
+        if after and step >= count:
+            part = added(part, other, *after)
+        else:
+            part = (part.astype(F32) + other.astype(F32)).astype(BF16)
     return part
 
 
@@ -270,40 +309,40 @@
     pair = lax.axis_index("pair")
     height, width = band_rows * bands, strip_cols * strips
     total = own_cols * strips
-    at_strip = jnp.stack([strip]).astype(jnp.int32)
     at_band = jnp.stack([band]).astype(jnp.int32)
     at_pair = jnp.stack([pair]).astype(jnp.int32)
-    at_place = jnp.stack([strip, pair]).astype(jnp.int32)
+    at_place = jnp.stack([strip, pair, band]).astype(jnp.int32)
 
     taps_one = jnp.transpose(filters_one, (1, 2, 0, 3)).reshape(3, 3 * channels, channels)
     back_one = jnp.transpose(filters_one[:, ::-1], (2, 3, 1, 0)).reshape(3 * channels, 3 * channels)
     taps_two = jnp.transpose(filters_two, (1, 2, 0, 3)).reshape(3, 3 * filters, 4 * channels)
 
+    above, below = border_swap(features_in[:, 0], features_in[:, -1], "row", band)
     x = jnp.transpose(features_in, (1, 0, 2))
-    above, below = border_swap(x[:2], x[-2:], "row", band)
     og = jnp.transpose(out_grad, (1, 2, 0))
     edge = REACH - 1
-    head, tail = (
-        jnp.pad(e.reshape(-1, 128), ((0, channels - e.size // 128), (0, 0)))[None]
-        for e in (og[:edge], og[-edge:])
-    )
-    even = strip % 2 == 0
-    side_a = even_swap(jnp.concatenate([above, x, below, jnp.where(even, tail, head)], 0), COLS, strips)
-    side_b = odd_swap(jnp.concatenate([above, x, below, jnp.where(even, head, tail)], 0), COLS, strips)
-    rows_wide = band_rows + 2
+    head, tail = (e.reshape(-1, 128) for e in (og[:edge], og[-edge:]))
+    to_a, to_b = whole_call(
+        pack_sides,
+        [shaped((2 * channels + head.shape[0], 128))] * 2,
+        [at_place, x, above, below, head, tail],
+        1,
+    )
+    side_a, side_b = even_swap(to_a, COLS, strips), odd_swap(to_b, COLS, strips)
     pooled, slope, wide = whole_call(
         functools.partial(layer_one, total=total),
         [
             shaped((2, SENT, 4 * channels)),
-            shaped((rows_wide, channels, 256)),
-            shaped((rows_wide + 2, channels, 256)),
+            shaped((band_rows, channels, 256)),
+            shaped((band_rows + 2, channels, 256)),
         ],
-        [at_strip, x, above, below, side_a, side_b, taps_one],
-        2 * rows_wide * 192 * 192 * 256,
+        [at_place, x, above, below, side_a, side_b, taps_one],
+        2 * band_rows * 192 * 192 * 256,
     )
     pieces = [pooled] + [xor_swap(pooled, "row", bands, k) for k in range(1, bands)]
 
-    ends = [side[-1].reshape(-1)[: og[:edge].size].reshape(og[:edge].shape) for side in (side_a, side_b)]
+    even = strip % 2 == 0
+    ends = [side[2 * channels :].reshape(og[:edge].shape) for side in (side_a, side_b)]
     before, after = jnp.where(even, ends[1], ends[0]), jnp.where(even, ends[0], ends[1])
     og = jnp.concatenate([before, og, after], 0)
     og = jnp.pad(og, ((1, PITCH - own_cols - 2 * REACH + 1), (0, 0), (0, 0)))
@@ -312,13 +351,13 @@
     count = pooled_rows * PITCH
     *terms, pooled_map, grad_cat = whole_call(
         functools.partial(layer_two, bands=bands),
-        [shaped((3, SENT, 4 * channels))] * bands
+        [shaped((72, 4 * channels))] * bands
         + [shaped((pooled_rows + 2, PITCH, 4 * channels)), shaped((count, 3 * filters))],
         [at_band, og, taps_two] + pieces,
         4 * count * 9 * filters * 4 * channels,
         scratch=[
             pltpu.VMEM((pooled_rows + 2, PITCH, filters), BF16),
-            pltpu.VMEM((pooled_rows + 2, PITCH, 4 * channels), F32),
+            pltpu.VMEM((pooled_rows, PITCH, 4 * channels), BF16),
         ],
     )
     received = [terms[0]] + [xor_swap(terms[k], "row", bands, k) for k in range(1, bands)]
@@ -333,28 +372,34 @@
     )
     swapped = even_swap(send_two, "pair", 2)
     share = 9 * channels * channels // 256
-    g, keep, send = whole_call(
+    g, up_a, up_b, keep, send = whole_call(
         functools.partial(grad_pre_one, bands=bands, total=total),
-        [shaped((rows_wide, channels, 256))] + [shaped((share, 128))] * 2,
+        [shaped((band_rows, channels, 256))]
+        + [shaped((channels, 256))] * 2
+        + [shaped((share, 128))] * 2,
         [at_place] + received + [slope, wide],
         2 * 8 * 192 * 192 * 256,
         scratch=[pltpu.VMEM((2 * share, 128), BF16)],
     )
-    (part_two,) = whole_call(
-        add_after, [shaped(keep_two.shape)], [keep_two, swapped, keep], 0, scalars=0
-    )
-    mine = sum_cols(part_two).astype(BF16)
-    other = even_swap(mine, "pair", 2)
-    grad_two = jnp.concatenate([jnp.where(pair == 0, mine, other), jnp.where(pair == 0, other, mine)], 0)
-    grad_two = grad_two.astype(F32) * (1.0 / math.sqrt(pooled_rows * total))
-    grad_two = jnp.transpose(grad_two.reshape(3, 3, filters, 4 * channels), (2, 0, 1, 3))
-
-    part = sum_cols(keep.astype(F32) + even_swap(send, "pair", 2).astype(F32)).astype(BF16)
+    part = sum_cols((keep.astype(F32) + even_swap(send, "pair", 2).astype(F32)).astype(BF16))
+    part_two = added(keep_two, swapped, part)
     terms = [part.astype(F32)] + [xor_swap(part, "row", bands, k).astype(F32) for k in range(1, bands)]
     while len(terms) > 1:
         terms = [a + b for a, b in zip(terms[::2], terms[1::2])]
     mine = terms[0].astype(BF16)
     other = even_swap(mine, "pair", 2)
+    (input_grad,) = whole_call(
+        layer_one_back,
+        [shaped(features_in.shape)],
+        [at_place, g, even_swap(up_a, "row", bands), odd_swap(up_b, "row", bands), back_one],
+        2 * band_rows * 192 * 192 * 256,
+    )
+    mine_two = sum_cols(part_two, after=(mine, input_grad))
+    other_two = even_swap(mine_two, "pair", 2)
+    first, second = jnp.where(pair == 0, mine_two, other_two), jnp.where(pair == 0, other_two, mine_two)
+    grad_two = jnp.concatenate([first, second], 0)
+    grad_two = grad_two.astype(F32) * (1.0 / math.sqrt(pooled_rows * total))
+    grad_two = jnp.transpose(grad_two.reshape(3, 3, filters, 4 * channels), (2, 0, 1, 3))
     (grad_one,) = whole_call(
         functools.partial(unpack_one, scale=1.0 / math.sqrt(height * width)),
         [shaped((3, 3 * channels, channels), F32)],
@@ -363,9 +408,6 @@
         scratch=[pltpu.VMEM((2 * share, 128), BF16)],
     )
     grad_one = jnp.transpose(grad_one.reshape(3, 3, channels, channels), (2, 0, 1, 3))
-    (input_grad,) = whole_call(
-        layer_one_back, [shaped(features_in.shape)], [g, back_one], 2 * 8 * 192 * 192 * 256, scalars=0
-    )
     return (input_grad, grad_one, grad_two)
 
 

time: 61.8 us -> 61.4 us (level)
  waiting for transfers between devices: 21.4 us -> 15.9 us
  Pallas kernels: 6.99 us -> 9.09 us
  local copies, waits for them, and re-layouts: 2.22 us -> 4.02 us
  starting transfers between devices: 28.6 us -> 29.9 us
    ppermute x11, waiting for transfers between devices: 19.3 us -> 13.1 us  [xor_swap(): return lax.ppermute(values, axis, [(n, n ^ k) for n in range(count)])]
    pallas_call x7 -> x9, Pallas kernels: 6.99 us -> 9.09 us  [whole_call(): pl.pallas_call(body, out_shape=outs, in_specs=specs, out_specs=[pl.BlockS...]
    unnamed x6 -> x10, local copies, waits for them, and re-layouts: 1.85 us -> 3.65 us
    ppermute x6 -> x7, waiting for transfers between devices: 2.08 us -> 2.83 us  [even_swap(): return lax.ppermute(values, axis, [(n, n ^ 1) for n in range(count)])]
    ppermute x2 -> x3, starting transfers between devices: 1.34 us -> 1.98 us  [odd_swap(): return lax.ppermute(values, axis, steps + [(b, a) for a, b in steps])]
    ppermute x6 -> x7, starting transfers between devices: 9.73 us -> 10 us  [even_swap(): return lax.ppermute(values, axis, [(n, n ^ 1) for n in range(count)])]
  transfers between devices with their start and end apart: 19 -> 21, of which waited for: 9 -> 10; matrix products, arithmetic and copies ran while one was open for 2% -> 2% of each run, Pallas kernels for 7% -> 6%
where the time goes in v3:
time: 61.4 us; the launch traced here: 61.1 us
  starting transfers between devices  29.9 us (49%)
  waiting for transfers between devices  15.9 us (26%)
  Pallas kernels  9.09 us (15%)
  local copies, waits for them, and re-layouts  4.02 us (7%)
  other arithmetic  1.36 us (2%)
  between operations  0.85 us (1%)
    ppermute x11, starting transfers between devices, xor_swap(): return lax.ppermute(values, axis, [(n, n ^ k) for n in range(count)])  17.9 us
    ppermute x11, waiting for transfers between devices, xor_swap(): return lax.ppermute(values, axis, [(n, n ^ k) for n in range(count)])  13.1 us
    ppermute x7, starting transfers between devices, even_swap(): return lax.ppermute(values, axis, [(n, n ^ 1) for n in range(count)])  10 us
    pallas_call x9, Pallas kernels, whole_call(): pl.pallas_call(body, out_shape=outs, in_specs=specs, out_specs=[pl.BlockS...  9.09 us
    unnamed x10, local copies, waits for them, and re-layouts  3.65 us
    ppermute x7, waiting for transfers between devices, even_swap(): return lax.ppermute(values, axis, [(n, n ^ 1) for n in range(count)])  2.83 us
    ppermute x3, starting transfers between devices, odd_swap(): return lax.ppermute(values, axis, steps + [(b, a) for a, b in steps])  1.98 us
  transfers between devices with their start and end apart: 21, of which 10 were waited for; matrix products, arithmetic and copies ran while one was open for 2% of the time, Pallas kernels for 6%

profile of v3, /device:TPU:0, one launch (start us, length us, event | category | flops | bytes accessed | tf_op | source)
XLA Modules:
  0.0 61.1 jit_solution(5590887937986408636)
XLA Ops:
  2.3 5.9 %collective-permute-start.1 = (bf16[64,128]{1,0:T(8,128)(2,1)S(1)}, bf16[64,128]{1,0:T(8,128)(2,1)S(1)}, u32[]{:S(2)}, u32[]{:S(2)}) collective-permute-start(bf16[64,128]{1,0:T(8,128)(2,1)S(1)} %get-tuple-element.41), channel_id=1, source_target_pairs={{0,4},{4,0},{8,12},{12,8},{1,5},{5,1},{9,13},{13,9},{2,6},{6,2},{1... | collective-permute-start | bytes 49160 | tf_op jit(solution)/shard_map/ppermute | solution.py:265
  11.3 2.9 %collective-permute-start.3 = (bf16[144,128]{1,0:T(8,128)(2,1)S(1)}, bf16[144,128]{1,0:T(8,128)(2,1)S(1)}, u32[]{:S(2)}, u32[]{:S(2)}) collective-permute-start(bf16[144,128]{1,0:T(8,128)(2,1)S(1)} %get-tuple-element.22), channel_id=1, source_target_pairs={{0,1},{1,0},{2,3},{3,2},{4,5},{5,4},{6,7},{7,6},{8,9},{9,8},{10,11... | collective-permute-start | bytes 110600 | tf_op jit(solution)/shard_map/ppermute | solution.py:265
  16.0 1.5 %shard_map.68 = (bf16[2,40,256]{2,1,0:T(8,128)(2,1)S(1)}, bf16[8,64,256]{2,1,0:T(8,128)(2,1)S(1)}, bf16[10,64,256]{2,1,0:T(8,128)(2,1)S(1)}) custom-call(s32[3]{0:T(128)S(1)} %pad_add_fusion.info, bf16[8,64,128]{2,1,0:T(8,128)(2,1)S(1)} %bitcast.37, bf16[64,128]{1,0:T(8,128)(2,1)S(1)} %get-tuple-element.50.above_ref, ...), custom_call_target="tpu_custom_call" | custom-call | flops 150994944 | bytes 942080 | tf_op jit(solution)/shard_map/pallas_call | solution.py:30
  17.5 2.1 %collective-permute-start.4 = (bf16[2,40,256]{2,1,0:T(8,128)(2,1)S(1)}, bf16[2,40,256]{2,1,0:T(8,128)(2,1)S(1)}, u32[]{:S(2)}, u32[]{:S(2)}) collective-permute-start(bf16[2,40,256]{2,1,0:T(8,128)(2,1)S(1)} %get-tuple-element.23.refs_0_), channel_id=1, source_target_pairs={{0,4},{4,0},{8,12},{12,8},{1,5},{5,1},{9,13},{13,9},{2,6},{6,2},{1... | collective-permute-start | bytes 122888 | tf_op jit(solution)/shard_map/ppermute | solution.py:274
  19.6 2.4 %collective-permute-start.6 = (bf16[2,40,256]{2,1,0:T(8,128)(2,1)S(1)}, bf16[2,40,256]{2,1,0:T(8,128)(2,1)S(1)}, u32[]{:S(2)}, u32[]{:S(2)}) collective-permute-start(bf16[2,40,256]{2,1,0:T(8,128)(2,1)S(1)} %get-tuple-element.23.refs_0_), channel_id=1, source_target_pairs={{0,12},{4,8},{8,4},{12,0},{1,13},{5,9},{9,5},{13,1},{2,14},{6,10},... | collective-permute-start | bytes 122888 | tf_op jit(solution)/shard_map/ppermute | solution.py:274
  22.1 3.9 %collective-permute-done.5.refs_2_ = bf16[2,40,256]{2,1,0:T(8,128)(2,1)S(1)} collective-permute-done((bf16[2,40,256]{2,1,0:T(8,128)(2,1)S(1)}, bf16[2,40,256]{2,1,0:T(8,128)(2,1)S(1)}, u32[]{:S(2)}, u32[]{:S(2)}) %collective-permute-start.5) | collective-permute-done | bytes 40992 | tf_op jit(solution)/shard_map/ppermute | solution.py:274
  26.0 1.4 %shard_map.69 = (bf16[72,256]{1,0:T(8,128)(2,1)S(1)}, bf16[72,256]{1,0:T(8,128)(2,1)S(1)}, bf16[72,256]{1,0:T(8,128)(2,1)S(1)}, bf16[72,256]{1,0:T(8,128)(2,1)S(...) custom-call(s32[1]{0:T(128)} %bitcast.2.info, bf16[8,48,128]{2,1,0:T(8,128)(2,1)S(1)} %fusion.6.og_ref, ...), custom_call_target="tpu_custom_call" | custom-call | flops 452984832 | bytes 1540096 | tf_op jit(solution)/shard_map/pallas_call | solution.py:30
  27.4 1.5 %collective-permute-start.7 = (bf16[72,256]{1,0:T(8,128)(2,1)S(1)}, bf16[72,256]{1,0:T(8,128)(2,1)S(1)}, u32[]{:S(2)}, u32[]{:S(2)}) collective-permute-start(bf16[72,256]{1,0:T(8,128)(2,1)S(1)} %get-tuple-element.25), channel_id=1, source_target_pairs={{0,4},{4,0},{8,12},{12,8},{1,5},{5,1},{9,13},{13,9},{2,6},{6,2},{1... | collective-permute-start | bytes 110600 | tf_op jit(solution)/shard_map/ppermute | solution.py:274
  28.9 1.1 %collective-permute-start.8 = (bf16[72,256]{1,0:T(8,128)(2,1)S(1)}, bf16[72,256]{1,0:T(8,128)(2,1)S(1)}, u32[]{:S(2)}, u32[]{:S(2)}) collective-permute-start(bf16[72,256]{1,0:T(8,128)(2,1)S(1)} %get-tuple-element.26), channel_id=1, source_target_pairs={{0,8},{4,12},{8,0},{12,4},{1,9},{5,13},{9,1},{13,5},{2,10},{6,14},... | collective-permute-start | bytes 110600 | tf_op jit(solution)/shard_map/ppermute | solution.py:274
  29.9 1.9 %collective-permute-start.9 = (bf16[72,256]{1,0:T(8,128)(2,1)S(1)}, bf16[72,256]{1,0:T(8,128)(2,1)S(1)}, u32[]{:S(2)}, u32[]{:S(2)}) collective-permute-start(bf16[72,256]{1,0:T(8,128)(2,1)S(1)} %get-tuple-element.27), channel_id=1, source_target_pairs={{0,12},{4,8},{8,4},{12,0},{1,13},{5,9},{9,5},{13,1},{2,14},{6,10},... | collective-permute-start | bytes 110600 | tf_op jit(solution)/shard_map/ppermute | solution.py:274
  31.9 2.6 %collective-permute-done.8.refs_2_ = bf16[72,256]{1,0:T(8,128)(2,1)S(1)} collective-permute-done((bf16[72,256]{1,0:T(8,128)(2,1)S(1)}, bf16[72,256]{1,0:T(8,128)(2,1)S(1)}, u32[]{:S(2)}, u32[]{:S(2)}) %collective-permute-start.8) | collective-permute-done | bytes 36896 | tf_op jit(solution)/shard_map/ppermute | solution.py:274
  34.5 1.2 %collective-permute-done.9.refs_3_ = bf16[72,256]{1,0:T(8,128)(2,1)S(1)} collective-permute-done((bf16[72,256]{1,0:T(8,128)(2,1)S(1)}, bf16[72,256]{1,0:T(8,128)(2,1)S(1)}, u32[]{:S(2)}, u32[]{:S(2)}) %collective-permute-start.9) | collective-permute-done | bytes 36896 | tf_op jit(solution)/shard_map/ppermute | solution.py:274
  35.7 1.7 %shard_map.70 = (bf16[8,64,256]{2,1,0:T(8,128)(2,1)S(1)}, bf16[64,256]{1,0:T(8,128)(2,1)S(1)}, bf16[64,256]{1,0:T(8,128)(2,1)S(1)}, bf16[144,128]{1,0:T(8,128)(2,1)S(1)}, bf16[144,128]{1,0:T(8,128)(2,1)S(1)}) custom-call(s32[3]{0:T(128)S(1)} %pad_add_fusion.info, bf16[72,256]{1,0:T(8,128)(2,1)S(1)} %get-tuple-element.24.refs_0_, ...), custom_call_target="tpu_custom_call" | custom-call | flops 150994944 | bytes 1138688 | tf_op jit(solution)/shard_map/pallas_call | solution.py:30
  38.7 2.4 %collective-permute-start.13 = (bf16[144,128]{1,0:T(8,128)(2,1)S(1)}, bf16[144,128]{1,0:T(8,128)(2,1)S(1)}, u32[]{:S(2)}, u32[]{:S(2)}) collective-permute-start(bf16[144,128]{1,0:T(8,128)(2,1)S(1)} %add_convert_fusion.2), channel_id=1, source_target_pairs={{0,2},{2,0},{1,3},{3,1},{4,6},{6,4},{5,7},{7,5},{8,10},{10,8},{9,1... | collective-permute-start | bytes 110600 | tf_op jit(solution)/shard_map/ppermute | solution.py:274
  41.7 1.3 %collective-permute-done.13 = bf16[144,128]{1,0:T(8,128)(2,1)S(1)} collective-permute-done((bf16[144,128]{1,0:T(8,128)(2,1)S(1)}, bf16[144,128]{1,0:T(8,128)(2,1)S(1)}, u32[]{:S(2)}, u32[]{:S(2)}) %collective-permute-start.13) | collective-permute-done | bytes 36896 | tf_op jit(solution)/shard_map/ppermute | solution.py:274
  43.0 2.5 %collective-permute-start.14 = (bf16[144,128]{1,0:T(8,128)(2,1)S(1)}, bf16[144,128]{1,0:T(8,128)(2,1)S(1)}, u32[]{:S(2)}, u32[]{:S(2)}) collective-permute-start(bf16[144,128]{1,0:T(8,128)(2,1)S(1)} %add_convert_fusion.1.refs_0_), channel_id=1, source_target_pairs={{0,4},{4,0},{8,12},{12,8},{1,5},{5,1},{9,13},{13,9},{2,6},{6,2},{1... | collective-permute-start | bytes 110600 | tf_op jit(solution)/shard_map/ppermute | solution.py:274
  45.6 1.1 %collective-permute-start.15 = (bf16[144,128]{1,0:T(8,128)(2,1)S(1)}, bf16[144,128]{1,0:T(8,128)(2,1)S(1)}, u32[]{:S(2)}, u32[]{:S(2)}) collective-permute-start(bf16[144,128]{1,0:T(8,128)(2,1)S(1)} %add_convert_fusion.1.refs_0_), channel_id=1, source_target_pairs={{0,8},{4,12},{8,0},{12,4},{1,9},{5,13},{9,1},{13,5},{2,10},{6,14},... | collective-permute-start | bytes 110600 | tf_op jit(solution)/shard_map/ppermute | solution.py:274
  46.7 1.4 %collective-permute-start.16 = (bf16[144,128]{1,0:T(8,128)(2,1)S(1)}, bf16[144,128]{1,0:T(8,128)(2,1)S(1)}, u32[]{:S(2)}, u32[]{:S(2)}) collective-permute-start(bf16[144,128]{1,0:T(8,128)(2,1)S(1)} %add_convert_fusion.1.refs_0_), channel_id=1, source_target_pairs={{0,12},{4,8},{8,4},{12,0},{1,13},{5,9},{9,5},{13,1},{2,14},{6,10},... | collective-permute-start | bytes 110600 | tf_op jit(solution)/shard_map/ppermute | solution.py:274
  48.1 1.5 %collective-permute-start.19 = (bf16[576,256]{1,0:T(8,128)(2,1)S(1)}, bf16[576,256]{1,0:T(8,128)(2,1)S(1)}, u32[]{:S(2)}, u32[]{:S(2)}) collective-permute-start(bf16[576,256]{1,0:T(8,128)(2,1)S(1)} %shard_map.74.a_ref), channel_id=1, source_target_pairs={{0,2},{2,0},{1,3},{3,1},{4,6},{6,4},{5,7},{7,5},{8,10},{10,8},{9,1... | collective-permute-start | bytes 884744 | tf_op jit(solution)/shard_map/ppermute | solution.py:274
  50.0 1.7 %shard_map.71.refs_1_ = bf16[64,8,128]{2,1,0:T(8,128)(2,1)} custom-call(s32[3]{0:T(128)S(1)} %pad_add_fusion.info, bf16[8,64,256]{2,1,0:T(8,128)(2,1)S(1)} %get-tuple-element.30.g_ref, bf16[64,256]{1,0:T(8,128)(2,1)S(1)} %collective-permute-done.10.a_ref, bf16[64,256]{1,0:T(8,128)(2,1)S(1)} %collective-permute-done.11.b_ref, bf16[192,192]{1,0:T(8,128)(2,1)S(1)} %reshape.43.w_ref), custom_call_target="tpu_custom_call" | custom-call | flops 150994944 | bytes 532480 | tf_op jit(solution)/shard_map/pallas_call | solution.py:30
  52.4 3.4 %collective-permute-done.19.b_ref = bf16[576,256]{1,0:T(8,128)(2,1)S(1)} collective-permute-done((bf16[576,256]{1,0:T(8,128)(2,1)S(1)}, bf16[576,256]{1,0:T(8,128)(2,1)S(1)}, u32[]{:S(2)}, u32[]{:S(2)}) %collective-permute-start.19) | collective-permute-done | bytes 294944 | tf_op jit(solution)/shard_map/ppermute | solution.py:274
  57.4 1.1 %collective-permute-done.17.other_ref = bf16[144,128]{1,0:T(8,128)(2,1)S(1)} collective-permute-done((bf16[144,128]{1,0:T(8,128)(2,1)S(1)}, bf16[144,128]{1,0:T(8,128)(2,1)S(1)}, u32[]{:S(2)}, u32[]{:S(2)}) %collective-permute-start.17) | collective-permute-done | bytes 36896 | tf_op jit(solution)/shard_map/ppermute | solution.py:265
  58.6 1.4 %shard_map.72 = f32[3,192,64]{2,1,0:T(8,128)} custom-call(s32[3]{0:T(128)S(1)} %pad_add_fusion.info, bf16[144,128]{1,0:T(8,128)(2,1)S(1)} %add_convert_fusion.mine_ref.refs_0_, bf16[144,128]{1,0:T(8,128)(2,1)S(1)} %collective-permute-done.17.other_ref), custom_call_target="tpu_custom_call" | custom-call | flops 1 | bytes 221184 | tf_op jit(solution)/shard_map/pallas_call | solution.py:30
  60.0 1.1 %convert_multiply_fusion = f32[1152,256]{1,0:T(8,128)} fusion(bf16[576,256]{1,0:T(8,128)(2,1)S(1)} %get-tuple-element.40, bf16[576,256]{1,0:T(8,128)(2,1)S(1)} %get-tuple-element.39), kind=kLoop, calls=%fused_computation | loop fusion | flops 1474560 | bytes 1769472 | tf_op jit(solution)/shard_map/mul | solution.py:401
  (54 shorter events, 11.2 us)
Async XLA Ops:
  0.6 25.3 %copy-start.3 = (bf16[128,3,3,256]{3,0,2,1:T(8,128)(2,1)S(1)}, bf16[128,3,3,256]{3,0,2,1:T(8,128)(2,1)}, u32[]{:S(2)}) copy-start(bf16[128,3,3,256]{3,0,2,1:T(8,128)(2,1)} %param.6) | copy-start | bytes 1769476
  1.7 7.6 %collective-permute-start = (bf16[64,128]{1,0:T(8,128)(2,1)S(1)}, bf16[64,128]{1,0:T(8,128)(2,1)S(1)}, u32[]{:S(2)}, u32[]{:S(2)}) collective-permute-start(bf16[64,128]{1,0:T(8,128)(2,1)S(1)} %get-tuple-element.42), channel_id=1, source_target_pairs={{4,8},{8,4},{5,9},{9,5},{6,10},{10,6},{7,11},{11,7},{20,24},{24,20... | collective-permute-start | bytes 49160 | tf_op jit(solution)/shard_map/ppermute | solution.py:270
  2.3 7.6 %collective-permute-start.1 = (bf16[64,128]{1,0:T(8,128)(2,1)S(1)}, bf16[64,128]{1,0:T(8,128)(2,1)S(1)}, u32[]{:S(2)}, u32[]{:S(2)}) collective-permute-start(bf16[64,128]{1,0:T(8,128)(2,1)S(1)} %get-tuple-element.41), channel_id=1, source_target_pairs={{0,4},{4,0},{8,12},{12,8},{1,5},{5,1},{9,13},{13,9},{2,6},{6,2},{1... | collective-permute-start | bytes 49160 | tf_op jit(solution)/shard_map/ppermute | solution.py:265
  10.7 3.6 %collective-permute-start.2 = (bf16[144,128]{1,0:T(8,128)(2,1)S(1)}, bf16[144,128]{1,0:T(8,128)(2,1)S(1)}, u32[]{:S(2)}, u32[]{:S(2)}) collective-permute-start(bf16[144,128]{1,0:T(8,128)(2,1)S(1)} %get-tuple-element.21), channel_id=1, source_target_pairs={{1,2},{2,1},{5,6},{6,5},{9,10},{10,9},{13,14},{14,13},{17,18},{18,... | collective-permute-start | bytes 110600 | tf_op jit(solution)/shard_map/ppermute | solution.py:270
  11.3 3.8 %collective-permute-start.3 = (bf16[144,128]{1,0:T(8,128)(2,1)S(1)}, bf16[144,128]{1,0:T(8,128)(2,1)S(1)}, u32[]{:S(2)}, u32[]{:S(2)}) collective-permute-start(bf16[144,128]{1,0:T(8,128)(2,1)S(1)} %get-tuple-element.22), channel_id=1, source_target_pairs={{0,1},{1,0},{2,3},{3,2},{4,5},{5,4},{6,7},{7,6},{8,9},{9,8},{10,11... | collective-permute-start | bytes 110600 | tf_op jit(solution)/shard_map/ppermute | solution.py:265
  15.1 0.9 %copy-start = (bf16[64,3,3,64]{3,0,2,1:T(8,128)(2,1)S(1)}, bf16[64,3,3,64]{3,0,2,1:T(8,128)(2,1)}, u32[]{:S(2)}) copy-start(bf16[64,3,3,64]{3,0,2,1:T(8,128)(2,1)} %param.5) | copy-start | bytes 221188
  17.5 4.6 %collective-permute-start.4 = (bf16[2,40,256]{2,1,0:T(8,128)(2,1)S(1)}, bf16[2,40,256]{2,1,0:T(8,128)(2,1)S(1)}, u32[]{:S(2)}, u32[]{:S(2)}) collective-permute-start(bf16[2,40,256]{2,1,0:T(8,128)(2,1)S(1)} %get-tuple-element.23.refs_0_), channel_id=1, source_target_pairs={{0,4},{4,0},{8,12},{12,8},{1,5},{5,1},{9,13},{13,9},{2,6},{6,2},{1... | collective-permute-start | bytes 122888 | tf_op jit(solution)/shard_map/ppermute | solution.py:274
  19.6 6.4 %collective-permute-start.5 = (bf16[2,40,256]{2,1,0:T(8,128)(2,1)S(1)}, bf16[2,40,256]{2,1,0:T(8,128)(2,1)S(1)}, u32[]{:S(2)}, u32[]{:S(2)}) collective-permute-start(bf16[2,40,256]{2,1,0:T(8,128)(2,1)S(1)} %get-tuple-element.23.refs_0_), channel_id=1, source_target_pairs={{0,8},{4,12},{8,0},{12,4},{1,9},{5,13},{9,1},{13,5},{2,10},{6,14},... | collective-permute-start | bytes 122888 | tf_op jit(solution)/shard_map/ppermute | solution.py:274
  19.6 6.4 %collective-permute-start.6 = (bf16[2,40,256]{2,1,0:T(8,128)(2,1)S(1)}, bf16[2,40,256]{2,1,0:T(8,128)(2,1)S(1)}, u32[]{:S(2)}, u32[]{:S(2)}) collective-permute-start(bf16[2,40,256]{2,1,0:T(8,128)(2,1)S(1)} %get-tuple-element.23.refs_0_), channel_id=1, source_target_pairs={{0,12},{4,8},{8,4},{12,0},{1,13},{5,9},{9,5},{13,1},{2,14},{6,10},... | collective-permute-start | bytes 122888 | tf_op jit(solution)/shard_map/ppermute | solution.py:274
  27.4 4.5 %collective-permute-start.7 = (bf16[72,256]{1,0:T(8,128)(2,1)S(1)}, bf16[72,256]{1,0:T(8,128)(2,1)S(1)}, u32[]{:S(2)}, u32[]{:S(2)}) collective-permute-start(bf16[72,256]{1,0:T(8,128)(2,1)S(1)} %get-tuple-element.25), channel_id=1, source_target_pairs={{0,4},{4,0},{8,12},{12,8},{1,5},{5,1},{9,13},{13,9},{2,6},{6,2},{1... | collective-permute-start | bytes 110600 | tf_op jit(solution)/shard_map/ppermute | solution.py:274
  28.9 5.6 %collective-permute-start.8 = (bf16[72,256]{1,0:T(8,128)(2,1)S(1)}, bf16[72,256]{1,0:T(8,128)(2,1)S(1)}, u32[]{:S(2)}, u32[]{:S(2)}) collective-permute-start(bf16[72,256]{1,0:T(8,128)(2,1)S(1)} %get-tuple-element.26), channel_id=1, source_target_pairs={{0,8},{4,12},{8,0},{12,4},{1,9},{5,13},{9,1},{13,5},{2,10},{6,14},... | collective-permute-start | bytes 110600 | tf_op jit(solution)/shard_map/ppermute | solution.py:274
  29.9 5.8 %collective-permute-start.9 = (bf16[72,256]{1,0:T(8,128)(2,1)S(1)}, bf16[72,256]{1,0:T(8,128)(2,1)S(1)}, u32[]{:S(2)}, u32[]{:S(2)}) collective-permute-start(bf16[72,256]{1,0:T(8,128)(2,1)S(1)} %get-tuple-element.27), channel_id=1, source_target_pairs={{0,12},{4,8},{8,4},{12,0},{1,13},{5,9},{9,5},{13,1},{2,14},{6,10},... | collective-permute-start | bytes 110600 | tf_op jit(solution)/shard_map/ppermute | solution.py:274
  35.7 14.0 %copy-start.1 = (bf16[64,3,3,64]{3,0,2,1:T(8,128)(2,1)S(1)}, bf16[64,3,3,64]{3,0,2,1:T(8,128)(2,1)}, u32[]{:S(2)}) copy-start(bf16[64,3,3,64]{3,0,2,1:T(8,128)(2,1)} %param.5) | copy-start | bytes 221188
  37.4 1.3 %collective-permute-start.12 = (bf16[144,128]{1,0:T(8,128)(2,1)S(1)}, bf16[144,128]{1,0:T(8,128)(2,1)S(1)}, u32[]{:S(2)}, u32[]{:S(2)}) collective-permute-start(bf16[144,128]{1,0:T(8,128)(2,1)S(1)} %get-tuple-element.34), channel_id=1, source_target_pairs={{0,1},{1,0},{2,3},{3,2},{4,5},{5,4},{6,7},{7,6},{8,9},{9,8},{10,11... | collective-permute-start | bytes 110600 | tf_op jit(solution)/shard_map/ppermute | solution.py:265
  38.1 8.6 %collective-permute-start.18 = (bf16[576,256]{1,0:T(8,128)(2,1)S(1)}, bf16[576,256]{1,0:T(8,128)(2,1)S(1)}, u32[]{:S(2)}, u32[]{:S(2)}) collective-permute-start(bf16[576,256]{1,0:T(8,128)(2,1)S(1)} %get-tuple-element.38), channel_id=1, source_target_pairs={{0,1},{1,0},{2,3},{3,2},{4,5},{5,4},{6,7},{7,6},{8,9},{9,8},{10,11... | collective-permute-start | bytes 884744 | tf_op jit(solution)/shard_map/ppermute | solution.py:265
  38.7 4.3 %collective-permute-start.13 = (bf16[144,128]{1,0:T(8,128)(2,1)S(1)}, bf16[144,128]{1,0:T(8,128)(2,1)S(1)}, u32[]{:S(2)}, u32[]{:S(2)}) collective-permute-start(bf16[144,128]{1,0:T(8,128)(2,1)S(1)} %add_convert_fusion.2), channel_id=1, source_target_pairs={{0,2},{2,0},{1,3},{3,1},{4,6},{6,4},{5,7},{7,5},{8,10},{10,8},{9,1... | collective-permute-start | bytes 110600 | tf_op jit(solution)/shard_map/ppermute | solution.py:274
  41.1 7.0 %collective-permute-start.10 = (bf16[64,256]{1,0:T(8,128)(2,1)S(1)}, bf16[64,256]{1,0:T(8,128)(2,1)S(1)}, u32[]{:S(2)}, u32[]{:S(2)}) collective-permute-start(bf16[64,256]{1,0:T(8,128)(2,1)S(1)} %get-tuple-element.31), channel_id=1, source_target_pairs={{0,4},{4,0},{8,12},{12,8},{1,5},{5,1},{9,13},{13,9},{2,6},{6,2},{1... | collective-permute-start | bytes 98312 | tf_op jit(solution)/shard_map/ppermute | solution.py:265
  41.1 8.9 %collective-permute-start.11 = (bf16[64,256]{1,0:T(8,128)(2,1)S(1)}, bf16[64,256]{1,0:T(8,128)(2,1)S(1)}, u32[]{:S(2)}, u32[]{:S(2)}) collective-permute-start(bf16[64,256]{1,0:T(8,128)(2,1)S(1)} %get-tuple-element.32), channel_id=1, source_target_pairs={{4,8},{8,4},{5,9},{9,5},{6,10},{10,6},{7,11},{11,7},{20,24},{24,20... | collective-permute-start | bytes 98312 | tf_op jit(solution)/shard_map/ppermute | solution.py:270
  43.0 8.7 %collective-permute-start.14 = (bf16[144,128]{1,0:T(8,128)(2,1)S(1)}, bf16[144,128]{1,0:T(8,128)(2,1)S(1)}, u32[]{:S(2)}, u32[]{:S(2)}) collective-permute-start(bf16[144,128]{1,0:T(8,128)(2,1)S(1)} %add_convert_fusion.1.refs_0_), channel_id=1, source_target_pairs={{0,4},{4,0},{8,12},{12,8},{1,5},{5,1},{9,13},{13,9},{2,6},{6,2},{1... | collective-permute-start | bytes 110600 | tf_op jit(solution)/shard_map/ppermute | solution.py:274
  45.6 6.2 %collective-permute-start.15 = (bf16[144,128]{1,0:T(8,128)(2,1)S(1)}, bf16[144,128]{1,0:T(8,128)(2,1)S(1)}, u32[]{:S(2)}, u32[]{:S(2)}) collective-permute-start(bf16[144,128]{1,0:T(8,128)(2,1)S(1)} %add_convert_fusion.1.refs_0_), channel_id=1, source_target_pairs={{0,8},{4,12},{8,0},{12,4},{1,9},{5,13},{9,1},{13,5},{2,10},{6,14},... | collective-permute-start | bytes 110600 | tf_op jit(solution)/shard_map/ppermute | solution.py:274
  46.7 5.8 %collective-permute-start.16 = (bf16[144,128]{1,0:T(8,128)(2,1)S(1)}, bf16[144,128]{1,0:T(8,128)(2,1)S(1)}, u32[]{:S(2)}, u32[]{:S(2)}) collective-permute-start(bf16[144,128]{1,0:T(8,128)(2,1)S(1)} %add_convert_fusion.1.refs_0_), channel_id=1, source_target_pairs={{0,12},{4,8},{8,4},{12,0},{1,13},{5,9},{9,5},{13,1},{2,14},{6,10},... | collective-permute-start | bytes 110600 | tf_op jit(solution)/shard_map/ppermute | solution.py:274
  48.1 7.7 %collective-permute-start.19 = (bf16[576,256]{1,0:T(8,128)(2,1)S(1)}, bf16[576,256]{1,0:T(8,128)(2,1)S(1)}, u32[]{:S(2)}, u32[]{:S(2)}) collective-permute-start(bf16[576,256]{1,0:T(8,128)(2,1)S(1)} %shard_map.74.a_ref), channel_id=1, source_target_pairs={{0,2},{2,0},{1,3},{3,1},{4,6},{6,4},{5,7},{7,5},{8,10},{10,8},{9,1... | collective-permute-start | bytes 884744 | tf_op jit(solution)/shard_map/ppermute | solution.py:274
  56.9 3.1 %collective-permute-start.20 = (bf16[576,256]{1,0:T(8,128)(2,1)S(1)}, bf16[576,256]{1,0:T(8,128)(2,1)S(1)}, u32[]{:S(2)}, u32[]{:S(2)}) collective-permute-start(bf16[576,256]{1,0:T(8,128)(2,1)S(1)} %shard_map.75), channel_id=1, source_target_pairs={{0,1},{1,0},{2,3},{3,2},{4,5},{5,4},{6,7},{7,6},{8,9},{9,8},{10,11... | collective-permute-start | bytes 884744 | tf_op jit(solution)/shard_map/ppermute | solution.py:265
  56.9 1.6 %collective-permute-start.17 = (bf16[144,128]{1,0:T(8,128)(2,1)S(1)}, bf16[144,128]{1,0:T(8,128)(2,1)S(1)}, u32[]{:S(2)}, u32[]{:S(2)}) collective-permute-start(bf16[144,128]{1,0:T(8,128)(2,1)S(1)} %add_convert_fusion.mine_ref.refs_0_), channel_id=1, source_target_pairs={{0,1},{1,0},{2,3},{3,2},{4,5},{5,4},{6,7},{7,6},{8,9},{9,8},{10,11... | collective-permute-start | bytes 110600 | tf_op jit(solution)/shard_map/ppermute | solution.py:265
  (1 other events, 0.9 us)

commit v4 on v3

--- a/solution.py
+++ b/solution.py
@@ -20,11 +20,11 @@
     return lax.dot_general(a, b, ((contract[:1], contract[1:]), ((), ())), preferred_element_type=F32)
 
 
-def whole_call(body, outs, operands, flops, scalars=1, scratch=()):
+def whole_call(body, outs, operands, flops, scalars=1, scratch=(), after=0):
     specs = [
         pl.BlockSpec(memory_space=pltpu.SMEM if n < scalars else pltpu.VMEM)
-        for n in range(len(operands))
-    ]
+        for n in range(len(operands) - after)
+    ] + [pl.BlockSpec(memory_space=pl.ANY)] * after
     sizes = [math.prod(a.shape) * a.dtype.itemsize for a in tuple(operands[scalars:]) + tuple(outs)]
     moved = sum(sizes) if flops else 0
     return pl.pallas_call(
@@ -76,20 +76,29 @@
     return jnp.where(lane == 4 * c + 2 * i + j, 1.0, 0.0).astype(BF16)
 
 
+def split_rows(info, x_ref, w_ref, rows_ref, a_ref, b_ref, joined_ref):
+    even = (info[2] & 1) == 0
+    rows = jnp.swapaxes(x_ref[...].astype(F32), 0, 1)
+    rows_ref[...] = rows.astype(BF16)
+    first, last = rows[0], rows[-1]
+    a_ref[...] = jnp.where(even, last, first).astype(BF16)
+    b_ref[...] = jnp.where(even, first, last).astype(BF16)
+    joined_ref[...] = jnp.concatenate([w_ref[0], w_ref[1], w_ref[2]], axis=1)
+
+
 def pack_sides(info, x_ref, above_ref, below_ref, head_ref, tail_ref, a_ref, b_ref):
     even = (info[0] & 1) == 0
     rows = [above_ref[...]] + [x_ref[h] for h in range(x_ref.shape[0])] + [below_ref[...]]
-    lane = lax.broadcasted_iota(jnp.int32, (64, 128), 1)
-    tiles = [[jnp.zeros((64, 128), F32)] * 2 for _ in range(2)]
+    slot = lax.broadcasted_iota(jnp.int32, (64, 128), 1) >> 4
+    blank = jnp.zeros((64, 128), F32)
+    heads, tails = [blank, blank], [blank, blank]
     for r, row in enumerate(rows):
-        wide, slot = row.astype(F32), r % 8
-        for side, shift in enumerate((16 * slot, 16 * slot + 16)):
-            here = (lane >> 4) == slot
-            tiles[side][r // 8] = jnp.where(here, roll(wide, shift, 1), tiles[side][r // 8])
-    head, tail = tiles
+        turned = roll(row.astype(F32), 16 * (r % 8), 1)
+        heads[r // 8] = jnp.where(slot == r % 8, turned, heads[r // 8])
+        tails[r // 8] = jnp.where(slot == (r - 1) % 8, turned, tails[r // 8])
     for t in range(2):
-        a_ref[64 * t : 64 * t + 64] = jnp.where(even, tail[t], head[t]).astype(BF16)
-        b_ref[64 * t : 64 * t + 64] = jnp.where(even, head[t], tail[t]).astype(BF16)
+        a_ref[64 * t : 64 * t + 64] = jnp.where(even, tails[t], heads[t]).astype(BF16)
+        b_ref[64 * t : 64 * t + 64] = jnp.where(even, heads[t], tails[t]).astype(BF16)
     first, last = head_ref[...].astype(F32), tail_ref[...].astype(F32)
     a_ref[128:] = jnp.where(even, last, first).astype(BF16)
     b_ref[128:] = jnp.where(even, first, last).astype(BF16)
@@ -100,20 +109,17 @@
 ):
     strip = info[0]
     band_rows = x_ref.shape[0]
-    even = (strip & 1) == 0
-    lane = lax.broadcasted_iota(jnp.int32, (64, 128), 1)
+    slot = lax.broadcasted_iota(jnp.int32, (128, 128), 1) >> 4
     sides = [ref[:128].astype(F32) for ref in (a_ref, b_ref)]
-    after, before = jnp.where(even, *sides), jnp.where(even, *sides[::-1])
+    from_a = ((slot ^ strip) & 1) == 0
+    packed = jnp.where(from_a, *sides), jnp.where(from_a, *sides[::-1])
     for r in range(band_rows + 2):
-        tile, slot = 64 * (r // 8), r % 8
-        right = roll(after[tile : tile + 64], -16 * slot, 1)
-        left = roll(before[tile : tile + 64], -16 * slot - 16, 1)
-        halo = jnp.where(lane < 16, right, jnp.where(lane >= 112, left, 0.0))
-        wide_ref[r, :, 128:] = halo.astype(BF16)
+        tile = 64 * (r // 8)
+        wide_ref[r, :, 128:] = roll(packed[r % 2][tile : tile + 64], -16 * (r % 8), 1).astype(BF16)
     wide_ref[0, :, :128] = above_ref[...]
     wide_ref[1 : band_rows + 1, :, :128] = x_ref[...]
     wide_ref[band_rows + 1, :, :128] = below_ref[...]
-    weights = jnp.concatenate([w_ref[0], w_ref[1], w_ref[2]], axis=1)
+    weights = w_ref[...]
     rows = slope_ref.shape[0]
     halves, held = [], None
     for h in range(rows):
@@ -144,8 +150,8 @@
 def layer_two(info, og_ref, w_ref, *refs, bands):
     pieces, refs = refs[:bands], refs[bands:]
     terms, refs = refs[:bands], refs[bands:]
-    map_ref, cat_ref, grad_ref, spread_ref = refs
-    band = info[0]
+    map_ref, own_ref, grad_ref, spread_ref = refs
+    band = info[2]
     rows, _, filters = og_ref.shape
     count = rows * PITCH
     map_ref[0] = jnp.zeros((PITCH, 256), BF16)
@@ -161,6 +167,7 @@
     pre = roll(y[:, :filters], 1, 0) + y[:, filters : 2 * filters] + roll(y[:, 2 * filters :], -1, 0)
     grad = og_ref[...].reshape(count, filters).astype(F32) * slope_of(pre, sigmoid(pre))
     grad = grad.astype(BF16)
+    own_ref[...] = grad
     grad_ref[0] = jnp.zeros((PITCH, filters), BF16)
     grad_ref[rows + 1] = jnp.zeros((PITCH, filters), BF16)
     grad_ref[1 : rows + 1] = grad.reshape(rows, PITCH, filters)
@@ -178,18 +185,18 @@
     for k in range(bands):
         first = 2 * (band ^ k)
         terms[k][...] = jnp.concatenate([spread_ref[first, :40], spread_ref[first + 1, :32]], 0)
-    wide = grad.astype(F32)
+
+
+def filter_two_grads(info, map_ref, own_ref, keep_ref, send_ref, all_ref):
+    pair = info[1]
+    rows = map_ref.shape[0] - 2
+    count, filters = own_ref.shape
     v = lax.broadcasted_iota(jnp.int32, (rows, PITCH, filters), 1).reshape(count, filters)
-    wide = jnp.where((v >= REACH) & (v < REACH + 32), wide, 0.0)
-    cat_ref[...] = jnp.concatenate([roll(wide, -1, 0), wide, roll(wide, 1, 0)], 1).astype(BF16)
-
-
-def filter_two_grads(info, map_ref, cat_ref, keep_ref, send_ref, all_ref):
-    pair = info[0]
-    rows = map_ref.shape[0] - 2
-    taps = cat_ref.shape[1]
+    wide = jnp.where((v >= REACH) & (v < REACH + 32), own_ref[...].astype(F32), 0.0)
+    cat = jnp.concatenate([roll(wide, -1, 0), wide, roll(wide, 1, 0)], 1).astype(BF16)
+    taps = 3 * filters
     for i in range(3):
-        part = dot(cat_ref[...], map_ref[i : i + rows].reshape(rows * PITCH, 256), (0, 0))
+        part = dot(cat, map_ref[i : i + rows].reshape(rows * PITCH, 256), (0, 0))
         all_ref[i * taps : (i + 1) * taps] = part.astype(BF16)
     half = keep_ref.shape[0]
     keep_ref[...] = all_ref[pl.ds(pl.multiple_of(pair * half, 16), half)]
@@ -238,9 +245,11 @@
     send_ref[...] = part_ref[pl.ds(pl.multiple_of((1 - pair) * half, 16), half)]
 
 
-def layer_one_back(info, g_ref, a_ref, b_ref, w_ref, out_ref):
-    even = (info[2] & 1) == 0
-    sides = a_ref[...].astype(F32), b_ref[...].astype(F32)
+def layer_one_back(info, g_ref, a_ref, b_ref, w_ref, out_ref, *, bands):
+    band = info[2]
+    even = (band & 1) == 0
+    inner = (band > 0) & (band < bands - 1)
+    sides = a_ref[...].astype(F32), jnp.where(inner, b_ref[...].astype(F32), 0.0)
     below, above = jnp.where(even, *sides).astype(BF16), jnp.where(even, *sides[::-1]).astype(BF16)
     lines = [above] + [g_ref[h] for h in range(8)] + [below]
     rows = []
@@ -266,24 +275,26 @@
 
 
 def odd_swap(values, axis, count):
-    steps = [(n, n + 1) for n in range(1, count - 1, 2)]
-    return lax.ppermute(values, axis, steps + [(b, a) for a, b in steps])
+    return lax.ppermute(values, axis, [(n, (n - 1 if n % 2 == 0 else n + 1) % count) for n in range(count)])
+
+
+def inner_swap(values, axis, count):
+    steps = [(n, n - 1 if n % 2 == 0 else n + 1) for n in range(1, count - 1)]
+    return lax.ppermute(values, axis, steps + [(0, 0), (count - 1, count - 1)])
 
 
 def xor_swap(values, axis, count, k):
     return lax.ppermute(values, axis, [(n, n ^ k) for n in range(count)])
 
 
-def border_swap(head, tail, axis, place):
-    count = lax.axis_size(axis)
-    even = place % 2 == 0
-    first = even_swap(jnp.where(even, tail, head), axis, count)
-    second = odd_swap(jnp.where(even, head, tail), axis, count)
-    return jnp.where(even, second, first), jnp.where(even, first, second)
+def row_swaps(values, bands):
+    order = sorted(range(1, bands), key=lambda k: (k < bands // 2, k))
+    moved = {k: xor_swap(values[k], "row", bands, k) for k in order}
+    return [moved[k] for k in range(1, bands)]
 
 
 def added(a, b, *after):
-    (total,) = whole_call(add_after, [shaped(a.shape)], [a, b, *after], 0, scalars=0)
+    (total,) = whole_call(add_after, [shaped(a.shape)], [a, b, *after], 0, scalars=0, after=len(after))
     return total
 
 
@@ -309,16 +320,24 @@
     pair = lax.axis_index("pair")
     height, width = band_rows * bands, strip_cols * strips
     total = own_cols * strips
-    at_band = jnp.stack([band]).astype(jnp.int32)
-    at_pair = jnp.stack([pair]).astype(jnp.int32)
     at_place = jnp.stack([strip, pair, band]).astype(jnp.int32)
 
     taps_one = jnp.transpose(filters_one, (1, 2, 0, 3)).reshape(3, 3 * channels, channels)
     back_one = jnp.transpose(filters_one[:, ::-1], (2, 3, 1, 0)).reshape(3 * channels, 3 * channels)
     taps_two = jnp.transpose(filters_two, (1, 2, 0, 3)).reshape(3, 3 * filters, 4 * channels)
 
-    above, below = border_swap(features_in[:, 0], features_in[:, -1], "row", band)
-    x = jnp.transpose(features_in, (1, 0, 2))
+    x, to_a, to_b, joined_one = whole_call(
+        split_rows,
+        [shaped((band_rows, channels, strip_cols))]
+        + [shaped((channels, strip_cols))] * 2
+        + [shaped((3 * channels, 3 * channels))],
+        [at_place, features_in, taps_one],
+        1,
+    )
+    side_a, side_b = even_swap(to_a, "row", bands), inner_swap(to_b, "row", bands)
+    even = band % 2 == 0
+    above, below = jnp.where(even, side_b, side_a), jnp.where(even, side_a, side_b)
+    above, below = jnp.where(band == 0, 0, above), jnp.where(band == bands - 1, 0, below)
     og = jnp.transpose(out_grad, (1, 2, 0))
     edge = REACH - 1
     head, tail = (e.reshape(-1, 128) for e in (og[:edge], og[-edge:]))
@@ -329,6 +348,7 @@
         1,
     )
     side_a, side_b = even_swap(to_a, COLS, strips), odd_swap(to_b, COLS, strips)
+    side_b = jnp.where((strip == 0) | (strip == strips - 1), 0, side_b)
     pooled, slope, wide = whole_call(
         functools.partial(layer_one, total=total),
         [
@@ -336,10 +356,10 @@
             shaped((band_rows, channels, 256)),
             shaped((band_rows + 2, channels, 256)),
         ],
-        [at_place, x, above, below, side_a, side_b, taps_one],
+        [at_place, x, above, below, side_a, side_b, joined_one],
         2 * band_rows * 192 * 192 * 256,
     )
-    pieces = [pooled] + [xor_swap(pooled, "row", bands, k) for k in range(1, bands)]
+    pieces = [pooled] + row_swaps([pooled] * bands, bands)
 
     even = strip % 2 == 0
     ends = [side[2 * channels :].reshape(og[:edge].shape) for side in (side_a, side_b)]
@@ -349,24 +369,24 @@
     og = jnp.transpose(og, (1, 0, 2))
 
     count = pooled_rows * PITCH
-    *terms, pooled_map, grad_cat = whole_call(
+    *terms, pooled_map, own_grad = whole_call(
         functools.partial(layer_two, bands=bands),
         [shaped((72, 4 * channels))] * bands
-        + [shaped((pooled_rows + 2, PITCH, 4 * channels)), shaped((count, 3 * filters))],
-        [at_band, og, taps_two] + pieces,
+        + [shaped((pooled_rows + 2, PITCH, 4 * channels)), shaped((count, filters))],
+        [at_place, og, taps_two] + pieces,
         4 * count * 9 * filters * 4 * channels,
         scratch=[
             pltpu.VMEM((pooled_rows + 2, PITCH, filters), BF16),
             pltpu.VMEM((pooled_rows, PITCH, 4 * channels), BF16),
         ],
     )
-    received = [terms[0]] + [xor_swap(terms[k], "row", bands, k) for k in range(1, bands)]
+    received = [terms[0]] + row_swaps(terms, bands)
 
     half = 9 * filters // 2
     keep_two, send_two = whole_call(
         filter_two_grads,
         [shaped((half, 4 * channels))] * 2,
-        [at_pair, pooled_map, grad_cat],
+        [at_place, pooled_map, own_grad],
         0,
         scratch=[pltpu.VMEM((2 * half, 4 * channels), BF16)],
     )
@@ -381,20 +401,21 @@
         2 * 8 * 192 * 192 * 256,
         scratch=[pltpu.VMEM((2 * share, 128), BF16)],
     )
-    part = sum_cols((keep.astype(F32) + even_swap(send, "pair", 2).astype(F32)).astype(BF16))
-    part_two = added(keep_two, swapped, part)
-    terms = [part.astype(F32)] + [xor_swap(part, "row", bands, k).astype(F32) for k in range(1, bands)]
+    part_two = added(keep_two, swapped, keep)
+    part = added(keep, even_swap(send, "pair", 2), part_two)
+    terms = [t.astype(F32) for t in [part] + row_swaps([part] * bands, bands)]
     while len(terms) > 1:
         terms = [a + b for a, b in zip(terms[::2], terms[1::2])]
-    mine = terms[0].astype(BF16)
+    part = terms[0].astype(BF16)
+    (input_grad,) = whole_call(
+        functools.partial(layer_one_back, bands=bands),
+        [shaped(features_in.shape)],
+        [at_place, g, even_swap(up_a, "row", bands), inner_swap(up_b, "row", bands), back_one],
+        2 * band_rows * 192 * 192 * 256,
+    )
+    mine = sum_cols(part)
     other = even_swap(mine, "pair", 2)
-    (input_grad,) = whole_call(
-        layer_one_back,
-        [shaped(features_in.shape)],
-        [at_place, g, even_swap(up_a, "row", bands), odd_swap(up_b, "row", bands), back_one],
-        2 * band_rows * 192 * 192 * 256,
-    )
-    mine_two = sum_cols(part_two, after=(mine, input_grad))
+    mine_two = sum_cols(part_two, after=(part, input_grad))
     other_two = even_swap(mine_two, "pair", 2)
     first, second = jnp.where(pair == 0, mine_two, other_two), jnp.where(pair == 0, other_two, mine_two)
     grad_two = jnp.concatenate([first, second], 0)

time: 61.4 us -> 57.6 us (0.938)
  the two profiles are of different devices: /device:TPU:0 before, /device:TPU:13 now
where the time goes in v4:
time: 57.6 us; the launch traced here: 57.3 us
  starting transfers between devices  26 us (45%)
  waiting for transfers between devices  14.5 us (25%)
  Pallas kernels  10.7 us (19%)
  local copies, waits for them, and re-layouts  3.95 us (7%)
  other arithmetic  1.32 us (2%)
  between operations  0.85 us (1%)
    pallas_call x11, Pallas kernels, whole_call(): pl.pallas_call(body, out_shape=outs, in_specs=specs, out_specs=[pl.BlockS...  10.7 us
    ppermute x11, starting transfers between devices, xor_swap(): return lax.ppermute(values, axis, [(n, n ^ k) for n in range(count)])  9.78 us
    ppermute x7, starting transfers between devices, even_swap(): return lax.ppermute(values, axis, [(n, n ^ 1) for n in range(count)])  7.5 us
    ppermute x11, waiting for transfers between devices, xor_swap(): return lax.ppermute(values, axis, [(n, n ^ k) for n in range(count)])  7.16 us
    ppermute x2, starting transfers between devices, inner_swap(): return lax.ppermute(values, axis, steps + [(0, 0), (count - 1, count - 1)])  5.51 us
    unnamed x11, local copies, waits for them, and re-layouts  3.58 us
    ppermute x7, waiting for transfers between devices, even_swap(): return lax.ppermute(values, axis, [(n, n ^ 1) for n in range(count)])  3.34 us
    ppermute x1, starting transfers between devices, odd_swap(): lax.ppermute(values, axis, [(n, (n - 1 if n % 2 == 0 else n + 1) % count)...  3.22 us
  transfers between devices with their start and end apart: 21, of which 12 were waited for; matrix products, arithmetic and copies ran while one was open for 2% of the time, Pallas kernels for 9%

profile of v4, /device:TPU:13, one launch (start us, length us, event | category | flops | bytes accessed | tf_op | source)
XLA Modules:
  0.0 57.3 jit_solution(2297535987567402632)
XLA Ops:
  3.2 3.2 %collective-permute-start = (bf16[64,128]{1,0:T(8,128)(2,1)S(1)}, bf16[64,128]{1,0:T(8,128)(2,1)S(1)}, u32[]{:S(2)}, u32[]{:S(2)}) collective-permute-start(bf16[64,128]{1,0:T(8,128)(2,1)S(1)} %get-tuple-element.26), channel_id=1, source_target_pairs={{4,8},{8,4},{0,0},{12,12},{5,9},{9,5},{1,1},{13,13},{6,10},{10,6},... | collective-permute-start | bytes 49160 | tf_op jit(solution)/shard_map/ppermute | solution.py:283
  7.7 1.4 %collective-permute-done.1 = bf16[64,128]{1,0:T(8,128)(2,1)S(1)} collective-permute-done((bf16[64,128]{1,0:T(8,128)(2,1)S(1)}, bf16[64,128]{1,0:T(8,128)(2,1)S(1)}, u32[]{:S(2)}, u32[]{:S(2)}) %collective-permute-start.1) | collective-permute-done | bytes 16416 | tf_op jit(solution)/shard_map/ppermute | solution.py:274
  9.7 3.2 %collective-permute-start.2 = (bf16[144,128]{1,0:T(8,128)(2,1)S(1)}, bf16[144,128]{1,0:T(8,128)(2,1)S(1)}, u32[]{:S(2)}, u32[]{:S(2)}) collective-permute-start(bf16[144,128]{1,0:T(8,128)(2,1)S(1)} %get-tuple-element.28), channel_id=1, source_target_pairs={{0,3},{1,2},{2,1},{3,0},{4,7},{5,6},{6,5},{7,4},{8,11},{9,10},{10,... | collective-permute-start | bytes 110600 | tf_op jit(solution)/shard_map/ppermute | solution.py:278
  13.0 2.2 %collective-permute-done.2 = bf16[144,128]{1,0:T(8,128)(2,1)S(1)} collective-permute-done((bf16[144,128]{1,0:T(8,128)(2,1)S(1)}, bf16[144,128]{1,0:T(8,128)(2,1)S(1)}, u32[]{:S(2)}, u32[]{:S(2)}) %collective-permute-start.2) | collective-permute-done | bytes 36896 | tf_op jit(solution)/shard_map/ppermute | solution.py:278
  15.2 1.4 %shard_map.69 = (bf16[2,40,256]{2,1,0:T(8,128)(2,1)S(1)}, bf16[8,64,256]{2,1,0:T(8,128)(2,1)S(1)}, bf16[10,64,256]{2,1,0:T(8,128)(2,1)S(1)}) custom-call(s32[3]{0:T(128)S(1)} %pad_add_fusion.info, bf16[8,64,128]{2,1,0:T(8,128)(2,1)S(1)} %get-tuple-element.25.x_ref, bf16[64,128]{1,0:T(8,128)(2,1)S(1)} %get-tuple-element.54.above_ref, ...), custom_call_target="tpu_custom_call" | custom-call | flops 150994944 | bytes 942080 | tf_op jit(solution)/shard_map/pallas_call | solution.py:30
  16.7 1.3 %collective-permute-start.5 = (bf16[2,40,256]{2,1,0:T(8,128)(2,1)S(1)}, bf16[2,40,256]{2,1,0:T(8,128)(2,1)S(1)}, u32[]{:S(2)}, u32[]{:S(2)}) collective-permute-start(bf16[2,40,256]{2,1,0:T(8,128)(2,1)S(1)} %get-tuple-element.31.refs_0_), channel_id=1, source_target_pairs={{0,8},{4,12},{8,0},{12,4},{1,9},{5,13},{9,1},{13,5},{2,10},{6,14},... | collective-permute-start | bytes 122888 | tf_op jit(solution)/shard_map/ppermute | solution.py:287
  18.1 1.3 %collective-permute-start.6 = (bf16[2,40,256]{2,1,0:T(8,128)(2,1)S(1)}, bf16[2,40,256]{2,1,0:T(8,128)(2,1)S(1)}, u32[]{:S(2)}, u32[]{:S(2)}) collective-permute-start(bf16[2,40,256]{2,1,0:T(8,128)(2,1)S(1)} %get-tuple-element.31.refs_0_), channel_id=1, source_target_pairs={{0,12},{4,8},{8,4},{12,0},{1,13},{5,9},{9,5},{13,1},{2,14},{6,10},... | collective-permute-start | bytes 122888 | tf_op jit(solution)/shard_map/ppermute | solution.py:287
  19.6 1.3 %collective-permute-done.5.refs_2_ = bf16[2,40,256]{2,1,0:T(8,128)(2,1)S(1)} collective-permute-done((bf16[2,40,256]{2,1,0:T(8,128)(2,1)S(1)}, bf16[2,40,256]{2,1,0:T(8,128)(2,1)S(1)}, u32[]{:S(2)}, u32[]{:S(2)}) %collective-permute-start.5) | collective-permute-done | bytes 40992 | tf_op jit(solution)/shard_map/ppermute | solution.py:287
  20.9 2.9 %collective-permute-done.6.refs_3_ = bf16[2,40,256]{2,1,0:T(8,128)(2,1)S(1)} collective-permute-done((bf16[2,40,256]{2,1,0:T(8,128)(2,1)S(1)}, bf16[2,40,256]{2,1,0:T(8,128)(2,1)S(1)}, u32[]{:S(2)}, u32[]{:S(2)}) %collective-permute-start.6) | collective-permute-done | bytes 40992 | tf_op jit(solution)/shard_map/ppermute | solution.py:287
  23.7 1.9 %shard_map.70 = (bf16[72,256]{1,0:T(8,128)(2,1)S(1)}, bf16[72,256]{1,0:T(8,128)(2,1)S(1)}, bf16[72,256]{1,0:T(8,128)(2,1)S(1)}, bf16[72,256]{1,0:T(8,128)(2,1)S(...) custom-call(s32[3]{0:T(128)S(1)} %pad_add_fusion.info, bf16[8,48,128]{2,1,0:T(8,128)(2,1)S(1)} %fusion.6.og_ref, ...), custom_call_target="tpu_custom_call" | custom-call | flops 452984832 | bytes 1343488 | tf_op jit(solution)/shard_map/pallas_call | solution.py:30
  25.7 1.1 %shard_map.73 = (bf16[576,256]{1,0:T(8,128)(2,1)S(1)}, bf16[576,256]{1,0:T(8,128)(2,1)S(1)}) custom-call(s32[3]{0:T(128)S(1)} %pad_add_fusion.info, bf16[10,48,256]{2,1,0:T(8,128)(2,1)S(1)} %get-tuple-element.43.map_ref, bf16[384,128]{1,0:T(8,128)(2,1)S(1)} %get-tuple-element.44.own_ref), custom_call_target="tpu_custom_call" | custom-call | tf_op jit(solution)/shard_map/pallas_call | solution.py:30
  30.4 1.6 %collective-permute-done.8.refs_2_ = bf16[72,256]{1,0:T(8,128)(2,1)S(1)} collective-permute-done((bf16[72,256]{1,0:T(8,128)(2,1)S(1)}, bf16[72,256]{1,0:T(8,128)(2,1)S(1)}, u32[]{:S(2)}, u32[]{:S(2)}) %collective-permute-start.8) | collective-permute-done | bytes 36896 | tf_op jit(solution)/shard_map/ppermute | solution.py:287
  32.0 1.1 %collective-permute-done.9.refs_3_ = bf16[72,256]{1,0:T(8,128)(2,1)S(1)} collective-permute-done((bf16[72,256]{1,0:T(8,128)(2,1)S(1)}, bf16[72,256]{1,0:T(8,128)(2,1)S(1)}, u32[]{:S(2)}, u32[]{:S(2)}) %collective-permute-start.9) | collective-permute-done | bytes 36896 | tf_op jit(solution)/shard_map/ppermute | solution.py:287
  33.1 1.7 %shard_map.71 = (bf16[8,64,256]{2,1,0:T(8,128)(2,1)S(1)}, bf16[64,256]{1,0:T(8,128)(2,1)S(1)}, bf16[64,256]{1,0:T(8,128)(2,1)S(1)}, bf16[144,128]{1,0:T(8,128)(2,1)S(1)}, bf16[144,128]{1,0:T(8,128)(2,1)S(1)}) custom-call(s32[3]{0:T(128)S(1)} %pad_add_fusion.info, bf16[72,256]{1,0:T(8,128)(2,1)S(1)} %get-tuple-element.32.refs_0_, ...), custom_call_target="tpu_custom_call" | custom-call | flops 150994944 | bytes 1138688 | tf_op jit(solution)/shard_map/pallas_call | solution.py:30
  34.8 1.6 %collective-permute-start.12 = (bf16[144,128]{1,0:T(8,128)(2,1)S(1)}, bf16[144,128]{1,0:T(8,128)(2,1)S(1)}, u32[]{:S(2)}, u32[]{:S(2)}) collective-permute-start(bf16[144,128]{1,0:T(8,128)(2,1)S(1)} %get-tuple-element.42), channel_id=1, source_target_pairs={{0,1},{1,0},{2,3},{3,2},{4,5},{5,4},{6,7},{7,6},{8,9},{9,8},{10,11... | collective-permute-start | bytes 110600 | tf_op jit(solution)/shard_map/ppermute | solution.py:274
  37.3 2.3 %collective-permute-start.14 = (bf16[144,128]{1,0:T(8,128)(2,1)S(1)}, bf16[144,128]{1,0:T(8,128)(2,1)S(1)}, u32[]{:S(2)}, u32[]{:S(2)}) collective-permute-start(bf16[144,128]{1,0:T(8,128)(2,1)S(1)} %shard_map.75), channel_id=1, source_target_pairs={{0,4},{4,0},{8,12},{12,8},{1,5},{5,1},{9,13},{13,9},{2,6},{6,2},{1... | collective-permute-start | bytes 110600 | tf_op jit(solution)/shard_map/ppermute | solution.py:287
  41.2 2.3 %collective-permute-start.10 = (bf16[64,256]{1,0:T(8,128)(2,1)S(1)}, bf16[64,256]{1,0:T(8,128)(2,1)S(1)}, u32[]{:S(2)}, u32[]{:S(2)}) collective-permute-start(bf16[64,256]{1,0:T(8,128)(2,1)S(1)} %get-tuple-element.39), channel_id=1, source_target_pairs={{0,4},{4,0},{8,12},{12,8},{1,5},{5,1},{9,13},{13,9},{2,6},{6,2},{1... | collective-permute-start | bytes 98312 | tf_op jit(solution)/shard_map/ppermute | solution.py:274
  43.5 2.3 %collective-permute-start.11 = (bf16[64,256]{1,0:T(8,128)(2,1)S(1)}, bf16[64,256]{1,0:T(8,128)(2,1)S(1)}, u32[]{:S(2)}, u32[]{:S(2)}) collective-permute-start(bf16[64,256]{1,0:T(8,128)(2,1)S(1)} %get-tuple-element.40), channel_id=1, source_target_pairs={{4,8},{8,4},{0,0},{12,12},{5,9},{9,5},{1,1},{13,13},{6,10},{10,6},... | collective-permute-start | bytes 98312 | tf_op jit(solution)/shard_map/ppermute | solution.py:283
  46.7 1.5 %collective-permute-done.11.b_ref = bf16[64,256]{1,0:T(8,128)(2,1)S(1)} collective-permute-done((bf16[64,256]{1,0:T(8,128)(2,1)S(1)}, bf16[64,256]{1,0:T(8,128)(2,1)S(1)}, u32[]{:S(2)}, u32[]{:S(2)}) %collective-permute-start.11) | collective-permute-done | bytes 32800 | tf_op jit(solution)/shard_map/ppermute | solution.py:283
  48.2 1.7 %shard_map.72.refs_1_ = bf16[64,8,128]{2,1,0:T(8,128)(2,1)} custom-call(s32[3]{0:T(128)S(1)} %pad_add_fusion.info, bf16[8,64,256]{2,1,0:T(8,128)(2,1)S(1)} %get-tuple-element.38.g_ref, bf16[64,256]{1,0:T(8,128)(2,1)S(1)} %collective-permute-done.10.a_ref, bf16[64,256]{1,0:T(8,128)(2,1)S(1)} %collective-permute-done.11.b_ref, bf16[192,192]{1,0:T(8,128)(2,1)S(1)} %reshape.39.w_ref), custom_call_target="tpu_custom_call" | custom-call | flops 150994944 | bytes 532480 | tf_op jit(solution)/shard_map/pallas_call | solution.py:30
  50.9 2.6 %collective-permute-start.20 = (bf16[576,256]{1,0:T(8,128)(2,1)S(1)}, bf16[576,256]{1,0:T(8,128)(2,1)S(1)}, u32[]{:S(2)}, u32[]{:S(2)}) collective-permute-start(bf16[576,256]{1,0:T(8,128)(2,1)S(1)} %shard_map.77), channel_id=1, source_target_pairs={{0,1},{1,0},{2,3},{3,2},{4,5},{5,4},{6,7},{7,6},{8,9},{9,8},{10,11... | collective-permute-start | bytes 884744 | tf_op jit(solution)/shard_map/ppermute | solution.py:274
  53.6 1.2 %collective-permute-done.18.other_ref = bf16[144,128]{1,0:T(8,128)(2,1)S(1)} collective-permute-done((bf16[144,128]{1,0:T(8,128)(2,1)S(1)}, bf16[144,128]{1,0:T(8,128)(2,1)S(1)}, u32[]{:S(2)}, u32[]{:S(2)}) %collective-permute-start.18) | collective-permute-done | bytes 36896 | tf_op jit(solution)/shard_map/ppermute | solution.py:274
  54.8 1.4 %shard_map.76 = f32[3,192,64]{2,1,0:T(8,128)} custom-call(s32[3]{0:T(128)S(1)} %pad_add_fusion.info, bf16[144,128]{1,0:T(8,128)(2,1)S(1)} %add_convert_fusion.mine_ref, bf16[144,128]{1,0:T(8,128)(2,1)S(1)} %collective-permute-done.18.other_ref), custom_call_target="tpu_custom_call" | custom-call | flops 1 | bytes 221184 | tf_op jit(solution)/shard_map/pallas_call | solution.py:30
  56.2 1.1 %convert_multiply_fusion = f32[1152,256]{1,0:T(8,128)} fusion(bf16[576,256]{1,0:T(8,128)(2,1)S(1)} %get-tuple-element.48, bf16[576,256]{1,0:T(8,128)(2,1)S(1)} %get-tuple-element.47), kind=kLoop, calls=%fused_computation | loop fusion | flops 1474560 | bytes 1769472 | tf_op jit(solution)/shard_map/mul | solution.py:422
  (56 shorter events, 12.7 us)
Async XLA Ops:
  0.7 0.9 %copy-start = (bf16[64,3,3,64]{3,0,2,1:T(8,128)(2,1)S(1)}, bf16[64,3,3,64]{3,0,2,1:T(8,128)(2,1)}, u32[]{:S(2)}) copy-start(bf16[64,3,3,64]{3,0,2,1:T(8,128)(2,1)} %param.5) | copy-start | bytes 221188
  2.5 21.2 %copy-start.4 = (bf16[128,3,3,256]{3,0,2,1:T(8,128)(2,1)S(1)}, bf16[128,3,3,256]{3,0,2,1:T(8,128)(2,1)}, u32[]{:S(2)}) copy-start(bf16[128,3,3,256]{3,0,2,1:T(8,128)(2,1)} %param.6) | copy-start | bytes 1769476
  3.2 4.5 %collective-permute-start = (bf16[64,128]{1,0:T(8,128)(2,1)S(1)}, bf16[64,128]{1,0:T(8,128)(2,1)S(1)}, u32[]{:S(2)}, u32[]{:S(2)}) collective-permute-start(bf16[64,128]{1,0:T(8,128)(2,1)S(1)} %get-tuple-element.26), channel_id=1, source_target_pairs={{4,8},{8,4},{0,0},{12,12},{5,9},{9,5},{1,1},{13,13},{6,10},{10,6},... | collective-permute-start | bytes 49160 | tf_op jit(solution)/shard_map/ppermute | solution.py:283
  6.4 2.7 %collective-permute-start.1 = (bf16[64,128]{1,0:T(8,128)(2,1)S(1)}, bf16[64,128]{1,0:T(8,128)(2,1)S(1)}, u32[]{:S(2)}, u32[]{:S(2)}) collective-permute-start(bf16[64,128]{1,0:T(8,128)(2,1)S(1)} %get-tuple-element.27), channel_id=1, source_target_pairs={{0,4},{4,0},{8,12},{12,8},{1,5},{5,1},{9,13},{13,9},{2,6},{6,2},{1... | collective-permute-start | bytes 49160 | tf_op jit(solution)/shard_map/ppermute | solution.py:274
  9.7 5.5 %collective-permute-start.2 = (bf16[144,128]{1,0:T(8,128)(2,1)S(1)}, bf16[144,128]{1,0:T(8,128)(2,1)S(1)}, u32[]{:S(2)}, u32[]{:S(2)}) collective-permute-start(bf16[144,128]{1,0:T(8,128)(2,1)S(1)} %get-tuple-element.28), channel_id=1, source_target_pairs={{0,3},{1,2},{2,1},{3,0},{4,7},{5,6},{6,5},{7,4},{8,11},{9,10},{10,... | collective-permute-start | bytes 110600 | tf_op jit(solution)/shard_map/ppermute | solution.py:278
  13.0 2.2 %collective-permute-start.3 = (bf16[144,128]{1,0:T(8,128)(2,1)S(1)}, bf16[144,128]{1,0:T(8,128)(2,1)S(1)}, u32[]{:S(2)}, u32[]{:S(2)}) collective-permute-start(bf16[144,128]{1,0:T(8,128)(2,1)S(1)} %get-tuple-element.29), channel_id=1, source_target_pairs={{0,1},{1,0},{2,3},{3,2},{4,5},{5,4},{6,7},{7,6},{8,9},{9,8},{10,11... | collective-permute-start | bytes 110600 | tf_op jit(solution)/shard_map/ppermute | solution.py:274
  16.7 2.9 %collective-permute-start.4 = (bf16[2,40,256]{2,1,0:T(8,128)(2,1)S(1)}, bf16[2,40,256]{2,1,0:T(8,128)(2,1)S(1)}, u32[]{:S(2)}, u32[]{:S(2)}) collective-permute-start(bf16[2,40,256]{2,1,0:T(8,128)(2,1)S(1)} %get-tuple-element.31.refs_0_), channel_id=1, source_target_pairs={{0,4},{4,0},{8,12},{12,8},{1,5},{5,1},{9,13},{13,9},{2,6},{6,2},{1... | collective-permute-start | bytes 122888 | tf_op jit(solution)/shard_map/ppermute | solution.py:287
  16.7 4.1 %collective-permute-start.5 = (bf16[2,40,256]{2,1,0:T(8,128)(2,1)S(1)}, bf16[2,40,256]{2,1,0:T(8,128)(2,1)S(1)}, u32[]{:S(2)}, u32[]{:S(2)}) collective-permute-start(bf16[2,40,256]{2,1,0:T(8,128)(2,1)S(1)} %get-tuple-element.31.refs_0_), channel_id=1, source_target_pairs={{0,8},{4,12},{8,0},{12,4},{1,9},{5,13},{9,1},{13,5},{2,10},{6,14},... | collective-permute-start | bytes 122888 | tf_op jit(solution)/shard_map/ppermute | solution.py:287
  18.1 5.6 %collective-permute-start.6 = (bf16[2,40,256]{2,1,0:T(8,128)(2,1)S(1)}, bf16[2,40,256]{2,1,0:T(8,128)(2,1)S(1)}, u32[]{:S(2)}, u32[]{:S(2)}) collective-permute-start(bf16[2,40,256]{2,1,0:T(8,128)(2,1)S(1)} %get-tuple-element.31.refs_0_), channel_id=1, source_target_pairs={{0,12},{4,8},{8,4},{12,0},{1,13},{5,9},{9,5},{13,1},{2,14},{6,10},... | collective-permute-start | bytes 122888 | tf_op jit(solution)/shard_map/ppermute | solution.py:287
  25.7 15.2 %copy-start.1 = (bf16[64,3,3,64]{3,0,2,1:T(8,128)(2,1)S(1)}, bf16[64,3,3,64]{3,0,2,1:T(8,128)(2,1)}, u32[]{:S(2)}) copy-start(bf16[64,3,3,64]{3,0,2,1:T(8,128)(2,1)} %param.5) | copy-start | bytes 221188
  26.8 9.6 %collective-permute-start.13 = (bf16[576,256]{1,0:T(8,128)(2,1)S(1)}, bf16[576,256]{1,0:T(8,128)(2,1)S(1)}, u32[]{:S(2)}, u32[]{:S(2)}) collective-permute-start(bf16[576,256]{1,0:T(8,128)(2,1)S(1)} %get-tuple-element.46), channel_id=1, source_target_pairs={{0,1},{1,0},{2,3},{3,2},{4,5},{5,4},{6,7},{7,6},{8,9},{9,8},{10,11... | collective-permute-start | bytes 884744 | tf_op jit(solution)/shard_map/ppermute | solution.py:274
  27.6 2.8 %collective-permute-start.7 = (bf16[72,256]{1,0:T(8,128)(2,1)S(1)}, bf16[72,256]{1,0:T(8,128)(2,1)S(1)}, u32[]{:S(2)}, u32[]{:S(2)}) collective-permute-start(bf16[72,256]{1,0:T(8,128)(2,1)S(1)} %get-tuple-element.33), channel_id=1, source_target_pairs={{0,4},{4,0},{8,12},{12,8},{1,5},{5,1},{9,13},{13,9},{2,6},{6,2},{1... | collective-permute-start | bytes 110600 | tf_op jit(solution)/shard_map/ppermute | solution.py:287
  28.2 3.8 %collective-permute-start.8 = (bf16[72,256]{1,0:T(8,128)(2,1)S(1)}, bf16[72,256]{1,0:T(8,128)(2,1)S(1)}, u32[]{:S(2)}, u32[]{:S(2)}) collective-permute-start(bf16[72,256]{1,0:T(8,128)(2,1)S(1)} %get-tuple-element.34), channel_id=1, source_target_pairs={{0,8},{4,12},{8,0},{12,4},{1,9},{5,13},{9,1},{13,5},{2,10},{6,14},... | collective-permute-start | bytes 110600 | tf_op jit(solution)/shard_map/ppermute | solution.py:287
  29.3 3.8 %collective-permute-start.9 = (bf16[72,256]{1,0:T(8,128)(2,1)S(1)}, bf16[72,256]{1,0:T(8,128)(2,1)S(1)}, u32[]{:S(2)}, u32[]{:S(2)}) collective-permute-start(bf16[72,256]{1,0:T(8,128)(2,1)S(1)} %get-tuple-element.35), channel_id=1, source_target_pairs={{0,12},{4,8},{8,4},{12,0},{1,13},{5,9},{9,5},{13,1},{2,14},{6,10},... | collective-permute-start | bytes 110600 | tf_op jit(solution)/shard_map/ppermute | solution.py:287
  34.8 2.4 %collective-permute-start.12 = (bf16[144,128]{1,0:T(8,128)(2,1)S(1)}, bf16[144,128]{1,0:T(8,128)(2,1)S(1)}, u32[]{:S(2)}, u32[]{:S(2)}) collective-permute-start(bf16[144,128]{1,0:T(8,128)(2,1)S(1)} %get-tuple-element.42), channel_id=1, source_target_pairs={{0,1},{1,0},{2,3},{3,2},{4,5},{5,4},{6,7},{7,6},{8,9},{9,8},{10,11... | collective-permute-start | bytes 110600 | tf_op jit(solution)/shard_map/ppermute | solution.py:274
  36.5 13.4 %collective-permute-start.19 = (bf16[576,256]{1,0:T(8,128)(2,1)S(1)}, bf16[576,256]{1,0:T(8,128)(2,1)S(1)}, u32[]{:S(2)}, u32[]{:S(2)}) collective-permute-start(bf16[576,256]{1,0:T(8,128)(2,1)S(1)} %shard_map.74.refs_0_.a_ref), channel_id=1, source_target_pairs={{0,2},{2,0},{1,3},{3,1},{4,6},{6,4},{5,7},{7,5},{8,10},{10,8},{9,1... | collective-permute-start | bytes 884744 | tf_op jit(solution)/shard_map/ppermute | solution.py:287
  37.3 6.2 %collective-permute-start.14 = (bf16[144,128]{1,0:T(8,128)(2,1)S(1)}, bf16[144,128]{1,0:T(8,128)(2,1)S(1)}, u32[]{:S(2)}, u32[]{:S(2)}) collective-permute-start(bf16[144,128]{1,0:T(8,128)(2,1)S(1)} %shard_map.75), channel_id=1, source_target_pairs={{0,4},{4,0},{8,12},{12,8},{1,5},{5,1},{9,13},{13,9},{2,6},{6,2},{1... | collective-permute-start | bytes 110600 | tf_op jit(solution)/shard_map/ppermute | solution.py:287
  39.6 6.3 %collective-permute-start.15 = (bf16[144,128]{1,0:T(8,128)(2,1)S(1)}, bf16[144,128]{1,0:T(8,128)(2,1)S(1)}, u32[]{:S(2)}, u32[]{:S(2)}) collective-permute-start(bf16[144,128]{1,0:T(8,128)(2,1)S(1)} %shard_map.75), channel_id=1, source_target_pairs={{0,8},{4,12},{8,0},{12,4},{1,9},{5,13},{9,1},{13,5},{2,10},{6,14},... | collective-permute-start | bytes 110600 | tf_op jit(solution)/shard_map/ppermute | solution.py:287
  39.8 6.1 %collective-permute-start.16 = (bf16[144,128]{1,0:T(8,128)(2,1)S(1)}, bf16[144,128]{1,0:T(8,128)(2,1)S(1)}, u32[]{:S(2)}, u32[]{:S(2)}) collective-permute-start(bf16[144,128]{1,0:T(8,128)(2,1)S(1)} %shard_map.75), channel_id=1, source_target_pairs={{0,12},{4,8},{8,4},{12,0},{1,13},{5,9},{9,5},{13,1},{2,14},{6,10},... | collective-permute-start | bytes 110600 | tf_op jit(solution)/shard_map/ppermute | solution.py:287
  41.2 5.5 %collective-permute-start.10 = (bf16[64,256]{1,0:T(8,128)(2,1)S(1)}, bf16[64,256]{1,0:T(8,128)(2,1)S(1)}, u32[]{:S(2)}, u32[]{:S(2)}) collective-permute-start(bf16[64,256]{1,0:T(8,128)(2,1)S(1)} %get-tuple-element.39), channel_id=1, source_target_pairs={{0,4},{4,0},{8,12},{12,8},{1,5},{5,1},{9,13},{13,9},{2,6},{6,2},{1... | collective-permute-start | bytes 98312 | tf_op jit(solution)/shard_map/ppermute | solution.py:274
  43.5 4.6 %collective-permute-start.11 = (bf16[64,256]{1,0:T(8,128)(2,1)S(1)}, bf16[64,256]{1,0:T(8,128)(2,1)S(1)}, u32[]{:S(2)}, u32[]{:S(2)}) collective-permute-start(bf16[64,256]{1,0:T(8,128)(2,1)S(1)} %get-tuple-element.40), channel_id=1, source_target_pairs={{4,8},{8,4},{0,0},{12,12},{5,9},{9,5},{1,1},{13,13},{6,10},{10,6},... | collective-permute-start | bytes 98312 | tf_op jit(solution)/shard_map/ppermute | solution.py:283
  45.9 7.6 %collective-permute-start.17 = (bf16[144,128]{1,0:T(8,128)(2,1)S(1)}, bf16[144,128]{1,0:T(8,128)(2,1)S(1)}, u32[]{:S(2)}, u32[]{:S(2)}) collective-permute-start(bf16[144,128]{1,0:T(8,128)(2,1)S(1)} %add_convert_fusion.1.refs_0_), channel_id=1, source_target_pairs={{0,2},{2,0},{1,3},{3,1},{4,6},{6,4},{5,7},{7,5},{8,10},{10,8},{9,1... | collective-permute-start | bytes 110600 | tf_op jit(solution)/shard_map/ppermute | solution.py:287
  50.9 5.3 %collective-permute-start.20 = (bf16[576,256]{1,0:T(8,128)(2,1)S(1)}, bf16[576,256]{1,0:T(8,128)(2,1)S(1)}, u32[]{:S(2)}, u32[]{:S(2)}) collective-permute-start(bf16[576,256]{1,0:T(8,128)(2,1)S(1)} %shard_map.77), channel_id=1, source_target_pairs={{0,1},{1,0},{2,3},{3,2},{4,5},{5,4},{6,7},{7,6},{8,9},{9,8},{10,11... | collective-permute-start | bytes 884744 | tf_op jit(solution)/shard_map/ppermute | solution.py:274
  53.5 1.3 %collective-permute-start.18 = (bf16[144,128]{1,0:T(8,128)(2,1)S(1)}, bf16[144,128]{1,0:T(8,128)(2,1)S(1)}, u32[]{:S(2)}, u32[]{:S(2)}) collective-permute-start(bf16[144,128]{1,0:T(8,128)(2,1)S(1)} %add_convert_fusion.mine_ref), channel_id=1, source_target_pairs={{0,1},{1,0},{2,3},{3,2},{4,5},{5,4},{6,7},{7,6},{8,9},{9,8},{10,11... | collective-permute-start | bytes 110600 | tf_op jit(solution)/shard_map/ppermute | solution.py:274
  (2 other events, 1.8 us)

commit v5 on v4

--- a/solution.py
+++ b/solution.py
@@ -20,9 +20,9 @@
     return lax.dot_general(a, b, ((contract[:1], contract[1:]), ((), ())), preferred_element_type=F32)
 
 
-def whole_call(body, outs, operands, flops, scalars=1, scratch=(), after=0):
+def whole_call(body, outs, operands, flops, scalars=1, scratch=(), after=0, held=0):
     specs = [
-        pl.BlockSpec(memory_space=pltpu.SMEM if n < scalars else pltpu.VMEM)
+        pl.BlockSpec(memory_space=pltpu.SMEM if n < scalars else pltpu.HBM if n < scalars + held else pltpu.VMEM)
         for n in range(len(operands) - after)
     ] + [pl.BlockSpec(memory_space=pl.ANY)] * after
     sizes = [math.prod(a.shape) * a.dtype.itemsize for a in tuple(operands[scalars:]) + tuple(outs)]
@@ -76,18 +76,53 @@
     return jnp.where(lane == 4 * c + 2 * i + j, 1.0, 0.0).astype(BF16)
 
 
-def split_rows(info, x_ref, w_ref, rows_ref, a_ref, b_ref, joined_ref):
+def matrices(info, _, pool_ref, back_ref, order_ref, *, total):
+    pool_ref[...] = pool_matrix(info[0], total)
+    back_ref[...] = pool_matrix(info[0], total, back=True)
+    order_ref[...] = order_matrix()
+
+
+def split_rows(
+    info, x_hbm, w_hbm, og_hbm, rows_ref, a_ref, b_ref, joined_ref, head_ref, tail_ref, x_ref, w_ref, sems
+):
+    edge = head_ref.shape[0]
+    copies = [
+        pltpu.make_async_copy(source, target, sems.at[n])
+        for n, (source, target) in enumerate(
+            [
+                (x_hbm, x_ref),
+                (w_hbm, w_ref),
+                (og_hbm.at[pl.ds(0, edge)], head_ref),
+                (og_hbm.at[pl.ds(og_hbm.shape[0] - edge, edge)], tail_ref),
+            ]
+        )
+    ]
+    for copy in copies:
+        copy.start()
+    copies[0].wait()
     even = (info[2] & 1) == 0
     rows = jnp.swapaxes(x_ref[...].astype(F32), 0, 1)
     rows_ref[...] = rows.astype(BF16)
     first, last = rows[0], rows[-1]
     a_ref[...] = jnp.where(even, last, first).astype(BF16)
     b_ref[...] = jnp.where(even, first, last).astype(BF16)
+    for copy in copies[1:]:
+        copy.wait()
     joined_ref[...] = jnp.concatenate([w_ref[0], w_ref[1], w_ref[2]], axis=1)
 
 
-def pack_sides(info, x_ref, above_ref, below_ref, head_ref, tail_ref, a_ref, b_ref):
+def beside(a_ref, b_ref, place, count):
+    even = (place & 1) == 0
+    a = a_ref[...].astype(F32)
+    b = jnp.where((place > 0) & (place < count - 1), b_ref[...].astype(F32), 0.0)
+    return jnp.where(even, b, a).astype(BF16), jnp.where(even, a, b).astype(BF16)
+
+
+def pack_sides(
+    info, x_ref, up_a_ref, up_b_ref, head_ref, tail_ref, a_ref, b_ref, above_ref, below_ref, *, bands
+):
     even = (info[0] & 1) == 0
+    above_ref[...], below_ref[...] = beside(up_a_ref, up_b_ref, info[2], bands)
     rows = [above_ref[...]] + [x_ref[h] for h in range(x_ref.shape[0])] + [below_ref[...]]
     slot = lax.broadcasted_iota(jnp.int32, (64, 128), 1) >> 4
     blank = jnp.zeros((64, 128), F32)
@@ -105,12 +140,26 @@
 
 
 def layer_one(
-    info, x_ref, above_ref, below_ref, a_ref, b_ref, w_ref, pooled_ref, slope_ref, wide_ref, *, total
+    info,
+    x_ref,
+    above_ref,
+    below_ref,
+    a_ref,
+    b_ref,
+    w_ref,
+    pool_ref,
+    order_ref,
+    pooled_ref,
+    slope_ref,
+    wide_ref,
+    *,
+    strips,
 ):
     strip = info[0]
     band_rows = x_ref.shape[0]
     slot = lax.broadcasted_iota(jnp.int32, (128, 128), 1) >> 4
-    sides = [ref[:128].astype(F32) for ref in (a_ref, b_ref)]
+    inner = (strip > 0) & (strip < strips - 1)
+    sides = a_ref[:128].astype(F32), jnp.where(inner, b_ref[:128].astype(F32), 0.0)
     from_a = ((slot ^ strip) & 1) == 0
     packed = jnp.where(from_a, *sides), jnp.where(from_a, *sides[::-1])
     for r in range(band_rows + 2):
@@ -132,7 +181,7 @@
             halves.append((held + active).astype(BF16))
         else:
             held = active
-    pooled = dot(pool_matrix(strip, total), jnp.concatenate(halves, 0), (1, 1))
+    pooled = dot(pool_ref[...], jnp.concatenate(halves, 0), (1, 1))
     stacked = jnp.concatenate(
         [
             jnp.concatenate(
@@ -142,7 +191,7 @@
         ],
         0,
     ).astype(BF16)
-    ordered = dot(stacked, order_matrix(), (1, 0)).astype(BF16)
+    ordered = dot(stacked, order_ref[...], (1, 0)).astype(BF16)
     for u in range(2):
         pooled_ref[u] = ordered[u * PITCH : u * PITCH + SENT]
 
@@ -150,7 +199,7 @@
 def layer_two(info, og_ref, w_ref, *refs, bands):
     pieces, refs = refs[:bands], refs[bands:]
     terms, refs = refs[:bands], refs[bands:]
-    map_ref, own_ref, grad_ref, spread_ref = refs
+    map_ref, grad_ref, pack_ref = refs
     band = info[2]
     rows, _, filters = og_ref.shape
     count = rows * PITCH
@@ -167,7 +216,6 @@
     pre = roll(y[:, :filters], 1, 0) + y[:, filters : 2 * filters] + roll(y[:, 2 * filters :], -1, 0)
     grad = og_ref[...].reshape(count, filters).astype(F32) * slope_of(pre, sigmoid(pre))
     grad = grad.astype(BF16)
-    own_ref[...] = grad
     grad_ref[0] = jnp.zeros((PITCH, filters), BF16)
     grad_ref[rows + 1] = jnp.zeros((PITCH, filters), BF16)
     grad_ref[1 : rows + 1] = grad.reshape(rows, PITCH, filters)
@@ -177,22 +225,24 @@
         part = dot(grad_ref[2 - i : 2 - i + rows].reshape(count, filters), weights, (1, 0))
         z = part if z is None else z + part
     spread = roll(z[:, :256], -1 - REACH, 0) + roll(z[:, 256:512], -REACH, 0) + roll(z[:, 512:], 1 - REACH, 0)
-    n = lax.broadcasted_iota(jnp.int32, (rows, PITCH, 256), 1).reshape(count, 256)
-    odd = (lax.broadcasted_iota(jnp.int32, (count, 256), 1) & 1) == 1
-    spread = jnp.where((n == 32) & odd, roll(spread, 33, 0), spread)
-    spread = jnp.where(n == 33, roll(spread, 33 - 32 - PITCH, 0), spread)
-    spread_ref[...] = spread.astype(BF16).reshape(rows, PITCH, 256)
+    spread = spread.reshape(rows, PITCH, 256)
+    odd = (lax.broadcasted_iota(jnp.int32, (8, 256), 1) & 1) == 1
+    row = lax.broadcasted_iota(jnp.int32, (8, 256), 0)
+    ends = [jnp.where(odd, spread[u - 1, 47:48], spread[u, 32:33]) for u in range(rows)]
+    for p in range(rows // 2):
+        shared = jnp.where(row == 0, ends[2 * p], jnp.where(row == 1, ends[2 * p + 1], 0.0))
+        pack_ref[p] = jnp.concatenate([spread[2 * p, :32], shared, spread[2 * p + 1, :32]], 0).astype(BF16)
     for k in range(bands):
-        first = 2 * (band ^ k)
-        terms[k][...] = jnp.concatenate([spread_ref[first, :40], spread_ref[first + 1, :32]], 0)
-
-
-def filter_two_grads(info, map_ref, own_ref, keep_ref, send_ref, all_ref):
+        terms[k][...] = pack_ref[band ^ k]
+
+
+def filter_two_grads(info, map_ref, grad_ref, _, keep_ref, send_ref, all_ref):
     pair = info[1]
     rows = map_ref.shape[0] - 2
-    count, filters = own_ref.shape
-    v = lax.broadcasted_iota(jnp.int32, (rows, PITCH, filters), 1).reshape(count, filters)
-    wide = jnp.where((v >= REACH) & (v < REACH + 32), own_ref[...].astype(F32), 0.0)
+    filters = grad_ref.shape[2]
+    v = lax.broadcasted_iota(jnp.int32, (rows, PITCH, filters), 1)
+    own = (v >= REACH) & (v < REACH + 32)
+    wide = jnp.where(own, grad_ref[1 : rows + 1].astype(F32), 0.0).reshape(rows * PITCH, filters)
     cat = jnp.concatenate([roll(wide, -1, 0), wide, roll(wide, 1, 0)], 1).astype(BF16)
     taps = 3 * filters
     for i in range(3):
@@ -204,22 +254,34 @@
 
 
 def add_after(a_ref, b_ref, *refs):
-    out_ref = refs[-1]
+    refs[-1][...] = (a_ref[...].astype(F32) + b_ref[...].astype(F32)).astype(BF16)
+
+
+def add_and_pass(a_ref, b_ref, other_ref, out_ref, passed_ref):
     out_ref[...] = (a_ref[...].astype(F32) + b_ref[...].astype(F32)).astype(BF16)
-
-
-def grad_pre_one(info, *refs, bands, total):
+    passed_ref[...] = other_ref[...]
+
+
+def sum_rows(*refs):
+    *terms, _, out_ref = refs
+    terms = [t[...].astype(F32) for t in terms]
+    while len(terms) > 1:
+        terms = [a + b for a, b in zip(terms[::2], terms[1::2])]
+    out_ref[...] = terms[0].astype(BF16)
+
+
+def grad_pre_one(info, *refs, bands):
     terms, refs = refs[:bands], refs[bands:]
-    slope_ref, wide_ref, g_ref, a_ref, b_ref, keep_ref, send_ref, part_ref = refs
-    strip, pair = info[0], info[1]
+    slope_ref, wide_ref, pool_ref, order_ref, g_ref, a_ref, b_ref, keep_ref, send_ref, part_ref = refs
+    pair = info[1]
     summed = terms[0][...].astype(F32)
     for k in range(1, bands):
         summed = summed + terms[k][...].astype(F32)
     blank = jnp.zeros((8, 256), F32)
     ends = summed[32:40]
     blocks = [summed[:32], ends, blank, summed[40:], roll(ends, -1, 0), blank]
-    ordered = dot(jnp.concatenate(blocks, 0).astype(BF16), order_matrix(), (1, 1)).astype(BF16)
-    pool = pool_matrix(strip, total, back=True)
+    ordered = dot(jnp.concatenate(blocks, 0).astype(BF16), order_ref[...], (1, 1)).astype(BF16)
+    pool = pool_ref[...]
     acc = None
     own = lax.broadcasted_iota(jnp.int32, (64, 256), 1) < 128
     for u in range(2):
@@ -245,12 +307,9 @@
     send_ref[...] = part_ref[pl.ds(pl.multiple_of((1 - pair) * half, 16), half)]
 
 
-def layer_one_back(info, g_ref, a_ref, b_ref, w_ref, out_ref, *, bands):
-    band = info[2]
-    even = (band & 1) == 0
-    inner = (band > 0) & (band < bands - 1)
-    sides = a_ref[...].astype(F32), jnp.where(inner, b_ref[...].astype(F32), 0.0)
-    below, above = jnp.where(even, *sides).astype(BF16), jnp.where(even, *sides[::-1]).astype(BF16)
+def layer_one_back(info, g_ref, a_ref, b_ref, w_ref, out_ref, done_ref, *, bands):
+    above, below = beside(a_ref, b_ref, info[2], bands)
+    done_ref[...] = jnp.zeros(done_ref.shape, F32)
     lines = [above] + [g_ref[h] for h in range(8)] + [below]
     rows = []
     for h in range(8):
@@ -259,7 +318,7 @@
     out_ref[...] = jnp.swapaxes(jnp.stack(rows, 0), 0, 1).astype(BF16)
 
 
-def unpack_one(info, mine_ref, other_ref, out_ref, flat_ref, *, scale):
+def unpack_one(info, mine_ref, other_ref, _, out_ref, flat_ref, *, scale):
     pair, half = info[1], mine_ref.shape[0]
     flat_ref[pl.ds(pl.multiple_of(pair * half, 16), half)] = mine_ref[...]
     flat_ref[pl.ds(pl.multiple_of((1 - pair) * half, 16), half)] = other_ref[...]
@@ -276,11 +335,6 @@
 
 def odd_swap(values, axis, count):
     return lax.ppermute(values, axis, [(n, (n - 1 if n % 2 == 0 else n + 1) % count) for n in range(count)])
-
-
-def inner_swap(values, axis, count):
-    steps = [(n, n - 1 if n % 2 == 0 else n + 1) for n in range(1, count - 1)]
-    return lax.ppermute(values, axis, steps + [(0, 0), (count - 1, count - 1)])
 
 
 def xor_swap(values, axis, count, k):
@@ -326,96 +380,107 @@
     back_one = jnp.transpose(filters_one[:, ::-1], (2, 3, 1, 0)).reshape(3 * channels, 3 * channels)
     taps_two = jnp.transpose(filters_two, (1, 2, 0, 3)).reshape(3, 3 * filters, 4 * channels)
 
-    x, to_a, to_b, joined_one = whole_call(
+    og = jnp.transpose(out_grad, (1, 2, 0))
+    edge = REACH - 1
+    x, to_a, to_b, joined_one, head, tail = whole_call(
         split_rows,
         [shaped((band_rows, channels, strip_cols))]
         + [shaped((channels, strip_cols))] * 2
-        + [shaped((3 * channels, 3 * channels))],
-        [at_place, features_in, taps_one],
+        + [shaped((3 * channels, 3 * channels))]
+        + [shaped((edge, pooled_rows, filters))] * 2,
+        [at_place, features_in, taps_one, og],
         1,
-    )
-    side_a, side_b = even_swap(to_a, "row", bands), inner_swap(to_b, "row", bands)
-    even = band % 2 == 0
-    above, below = jnp.where(even, side_b, side_a), jnp.where(even, side_a, side_b)
-    above, below = jnp.where(band == 0, 0, above), jnp.where(band == bands - 1, 0, below)
-    og = jnp.transpose(out_grad, (1, 2, 0))
-    edge = REACH - 1
-    head, tail = (e.reshape(-1, 128) for e in (og[:edge], og[-edge:]))
-    to_a, to_b = whole_call(
-        pack_sides,
-        [shaped((2 * channels + head.shape[0], 128))] * 2,
-        [at_place, x, above, below, head, tail],
+        scratch=[
+            pltpu.VMEM(features_in.shape, BF16),
+            pltpu.VMEM(taps_one.shape, BF16),
+            pltpu.SemaphoreType.DMA((4,)),
+        ],
+        held=3,
+    )
+    pool, pool_back, order = whole_call(
+        functools.partial(matrices, total=total),
+        [shaped((2 * PITCH, 256))] * 2 + [shaped((256, 256))],
+        [at_place, to_a],
+        10**8,
+        after=1,
+    )
+    up_a, up_b = even_swap(to_a, "row", bands), odd_swap(to_b, "row", bands)
+    head, tail = head.reshape(-1, 128), tail.reshape(-1, 128)
+    to_a, to_b, above, below = whole_call(
+        functools.partial(pack_sides, bands=bands),
+        [shaped((2 * channels + head.shape[0], 128))] * 2 + [shaped((channels, strip_cols))] * 2,
+        [at_place, x, up_a, up_b, head, tail],
         1,
     )
     side_a, side_b = even_swap(to_a, COLS, strips), odd_swap(to_b, COLS, strips)
-    side_b = jnp.where((strip == 0) | (strip == strips - 1), 0, side_b)
     pooled, slope, wide = whole_call(
-        functools.partial(layer_one, total=total),
+        functools.partial(layer_one, strips=strips),
         [
             shaped((2, SENT, 4 * channels)),
             shaped((band_rows, channels, 256)),
             shaped((band_rows + 2, channels, 256)),
         ],
-        [at_place, x, above, below, side_a, side_b, joined_one],
+        [at_place, x, above, below, side_a, side_b, joined_one, pool, order],
         2 * band_rows * 192 * 192 * 256,
     )
     pieces = [pooled] + row_swaps([pooled] * bands, bands)
 
     even = strip % 2 == 0
     ends = [side[2 * channels :].reshape(og[:edge].shape) for side in (side_a, side_b)]
+    ends[1] = jnp.where((strip == 0) | (strip == strips - 1), 0, ends[1])
     before, after = jnp.where(even, ends[1], ends[0]), jnp.where(even, ends[0], ends[1])
     og = jnp.concatenate([before, og, after], 0)
     og = jnp.pad(og, ((1, PITCH - own_cols - 2 * REACH + 1), (0, 0), (0, 0)))
     og = jnp.transpose(og, (1, 0, 2))
 
     count = pooled_rows * PITCH
-    *terms, pooled_map, own_grad = whole_call(
+    *terms, pooled_map, grad_map = whole_call(
         functools.partial(layer_two, bands=bands),
         [shaped((72, 4 * channels))] * bands
-        + [shaped((pooled_rows + 2, PITCH, 4 * channels)), shaped((count, filters))],
+        + [shaped((pooled_rows + 2, PITCH, 4 * channels)), shaped((pooled_rows + 2, PITCH, filters))],
         [at_place, og, taps_two] + pieces,
         4 * count * 9 * filters * 4 * channels,
-        scratch=[
-            pltpu.VMEM((pooled_rows + 2, PITCH, filters), BF16),
-            pltpu.VMEM((pooled_rows, PITCH, 4 * channels), BF16),
-        ],
+        scratch=[pltpu.VMEM((bands, 72, 4 * channels), BF16)],
     )
     received = [terms[0]] + row_swaps(terms, bands)
 
+    share = 9 * channels * channels // 256
+    g, up_a, up_b, keep, send = whole_call(
+        functools.partial(grad_pre_one, bands=bands),
+        [shaped((band_rows, channels, 256))]
+        + [shaped((channels, 256))] * 2
+        + [shaped((share, 128))] * 2,
+        [at_place] + received + [slope, wide, pool_back, order],
+        2 * 8 * 192 * 192 * 256,
+        scratch=[pltpu.VMEM((2 * share, 128), BF16)],
+    )
     half = 9 * filters // 2
     keep_two, send_two = whole_call(
         filter_two_grads,
         [shaped((half, 4 * channels))] * 2,
-        [at_place, pooled_map, own_grad],
+        [at_place, pooled_map, grad_map, keep],
         0,
         scratch=[pltpu.VMEM((2 * half, 4 * channels), BF16)],
-    )
-    swapped = even_swap(send_two, "pair", 2)
-    share = 9 * channels * channels // 256
-    g, up_a, up_b, keep, send = whole_call(
-        functools.partial(grad_pre_one, bands=bands, total=total),
-        [shaped((band_rows, channels, 256))]
-        + [shaped((channels, 256))] * 2
-        + [shaped((share, 128))] * 2,
-        [at_place] + received + [slope, wide],
-        2 * 8 * 192 * 192 * 256,
-        scratch=[pltpu.VMEM((2 * share, 128), BF16)],
-    )
-    part_two = added(keep_two, swapped, keep)
-    part = added(keep, even_swap(send, "pair", 2), part_two)
-    terms = [t.astype(F32) for t in [part] + row_swaps([part] * bands, bands)]
-    while len(terms) > 1:
-        terms = [a + b for a, b in zip(terms[::2], terms[1::2])]
-    part = terms[0].astype(BF16)
-    (input_grad,) = whole_call(
+        after=1,
+    )
+    part = sum_cols(added(keep, even_swap(send, "pair", 2)))
+    part_two, part = whole_call(
+        add_and_pass,
+        [shaped(keep_two.shape), shaped(part.shape)],
+        [keep_two, even_swap(send_two, "pair", 2), part],
+        0,
+        scalars=0,
+    )
+    terms = [part] + row_swaps([part] * bands, bands)
+    input_grad, done = whole_call(
         functools.partial(layer_one_back, bands=bands),
-        [shaped(features_in.shape)],
-        [at_place, g, even_swap(up_a, "row", bands), inner_swap(up_b, "row", bands), back_one],
+        [shaped(features_in.shape), shaped((8, 128), F32)],
+        [at_place, g, even_swap(up_a, "row", bands), odd_swap(up_b, "row", bands), back_one],
         2 * band_rows * 192 * 192 * 256,
     )
-    mine = sum_cols(part)
+    (mine,) = whole_call(sum_rows, [shaped(part.shape)], terms + [done], 0, scalars=0, after=1)
     other = even_swap(mine, "pair", 2)
-    mine_two = sum_cols(part_two, after=(part, input_grad))
+    mine_two = sum_cols(part_two, after=(mine,))
     other_two = even_swap(mine_two, "pair", 2)
     first, second = jnp.where(pair == 0, mine_two, other_two), jnp.where(pair == 0, other_two, mine_two)
     grad_two = jnp.concatenate([first, second], 0)
@@ -424,9 +489,10 @@
     (grad_one,) = whole_call(
         functools.partial(unpack_one, scale=1.0 / math.sqrt(height * width)),
         [shaped((3, 3 * channels, channels), F32)],
-        [at_place, mine, other],
+        [at_place, mine, other, other_two],
         1,
         scratch=[pltpu.VMEM((2 * share, 128), BF16)],
+        after=1,
     )
     grad_one = jnp.transpose(grad_one.reshape(3, 3, channels, channels), (2, 0, 1, 3))
     return (input_grad, grad_one, grad_two)

time: 57.6 us -> 58.6 us (1.017)
  the two profiles are of different devices: /device:TPU:13 before, /device:TPU:0 now
where the time goes in v5:
time: 58.6 us; the launch traced here: 58.4 us
  starting transfers between devices  25.3 us (43%)
  waiting for transfers between devices  15.3 us (26%)
  Pallas kernels  11.9 us (20%)
  local copies, waits for them, and re-layouts  3.87 us (7%)
  other arithmetic  1.28 us (2%)
  between operations  0.84 us (1%)
    ppermute x11, starting transfers between devices, xor_swap(): return lax.ppermute(values, axis, [(n, n ^ k) for n in range(count)])  15.5 us
    pallas_call x13, Pallas kernels, whole_call(): pl.pallas_call(body, out_shape=outs, in_specs=specs, out_specs=[pl.BlockS...  11.9 us
    ppermute x11, waiting for transfers between devices, xor_swap(): return lax.ppermute(values, axis, [(n, n ^ k) for n in range(count)])  9.86 us
    ppermute x3, starting transfers between devices, odd_swap(): lax.ppermute(values, axis, [(n, (n - 1 if n % 2 == 0 else n + 1) % count)...  6.98 us
    unnamed x11, local copies, waits for them, and re-layouts  3.51 us
    ppermute x7, waiting for transfers between devices, even_swap(): return lax.ppermute(values, axis, [(n, n ^ 1) for n in range(count)])  3.1 us
    ppermute x7, starting transfers between devices, even_swap(): return lax.ppermute(values, axis, [(n, n ^ 1) for n in range(count)])  2.79 us
    ppermute x3, waiting for transfers between devices, odd_swap(): lax.ppermute(values, axis, [(n, (n - 1 if n % 2 == 0 else n + 1) % count)...  2.31 us
  transfers between devices with their start and end apart: 21, of which 10 were waited for; matrix products, arithmetic and copies ran while one was open for 4% of the time, Pallas kernels for 6%

profile of v5, /device:TPU:0, one launch (start us, length us, event | category | flops | bytes accessed | tf_op | source)
XLA Modules:
  0.0 58.4 jit_solution(3223987222400252674)
XLA Ops:
  4.5 5.1 %collective-permute-start.1 = (bf16[64,128]{1,0:T(8,128)(2,1)S(1)}, bf16[64,128]{1,0:T(8,128)(2,1)S(1)}, u32[]{:S(2)}, u32[]{:S(2)}) collective-permute-start(bf16[64,128]{1,0:T(8,128)(2,1)S(1)} %get-tuple-element.38), channel_id=1, source_target_pairs={{0,12},{4,8},{8,4},{12,0},{1,13},{5,9},{9,5},{13,1},{2,14},{6,10},... | collective-permute-start | bytes 49160 | tf_op jit(solution)/shard_map/ppermute | solution.py:337
  9.6 1.7 %collective-permute-done.1.up_b_ref = bf16[64,128]{1,0:T(8,128)(2,1)S(1)} collective-permute-done((bf16[64,128]{1,0:T(8,128)(2,1)S(1)}, bf16[64,128]{1,0:T(8,128)(2,1)S(1)}, u32[]{:S(2)}, u32[]{:S(2)}) %collective-permute-start.1) | collective-permute-done | bytes 16416 | tf_op jit(solution)/shard_map/ppermute | solution.py:337
  11.3 2.0 %collective-permute-done.up_a_ref = bf16[64,128]{1,0:T(8,128)(2,1)S(1)} collective-permute-done((bf16[64,128]{1,0:T(8,128)(2,1)S(1)}, bf16[64,128]{1,0:T(8,128)(2,1)S(1)}, u32[]{:S(2)}, u32[]{:S(2)}) %collective-permute-start) | collective-permute-done | bytes 16416 | tf_op jit(solution)/shard_map/ppermute | solution.py:333
  14.1 1.6 %collective-permute-start.3 = (bf16[144,128]{1,0:T(8,128)(2,1)S(1)}, bf16[144,128]{1,0:T(8,128)(2,1)S(1)}, u32[]{:S(2)}, u32[]{:S(2)}) collective-permute-start(bf16[144,128]{1,0:T(8,128)(2,1)S(1)} %get-tuple-element.42), channel_id=1, source_target_pairs={{0,1},{1,0},{2,3},{3,2},{4,5},{5,4},{6,7},{7,6},{8,9},{9,8},{10,11... | collective-permute-start | bytes 110600 | tf_op jit(solution)/shard_map/ppermute | solution.py:333
  17.8 1.5 %shard_map.70 = (bf16[2,40,256]{2,1,0:T(8,128)(2,1)S(1)}, bf16[8,64,256]{2,1,0:T(8,128)(2,1)S(1)}, bf16[10,64,256]{2,1,0:T(8,128)(2,1)S(1)}) custom-call(s32[3]{0:T(128)S(1)} %pad_add_fusion.info, bf16[8,64,128]{2,1,0:T(8,128)(2,1)S(1)} %get-tuple-element.36.x_ref, bf16[64,128]{1,0:T(8,128)(2,1)S(1)} %get-tuple-element.43.above_ref, ...), custom_call_target="tpu_custom_call" | custom-call | flops 150994944 | bytes 1122304 | tf_op jit(solution)/shard_map/pallas_call | solution.py:30
  19.2 1.9 %collective-permute-start.6 = (bf16[2,40,256]{2,1,0:T(8,128)(2,1)S(1)}, bf16[2,40,256]{2,1,0:T(8,128)(2,1)S(1)}, u32[]{:S(2)}, u32[]{:S(2)}) collective-permute-start(bf16[2,40,256]{2,1,0:T(8,128)(2,1)S(1)} %get-tuple-element.48.refs_0_), channel_id=1, source_target_pairs={{0,12},{4,8},{8,4},{12,0},{1,13},{5,9},{9,5},{13,1},{2,14},{6,10},... | collective-permute-start | bytes 122888 | tf_op jit(solution)/shard_map/ppermute | solution.py:341
  21.1 2.6 %collective-permute-start.4 = (bf16[2,40,256]{2,1,0:T(8,128)(2,1)S(1)}, bf16[2,40,256]{2,1,0:T(8,128)(2,1)S(1)}, u32[]{:S(2)}, u32[]{:S(2)}) collective-permute-start(bf16[2,40,256]{2,1,0:T(8,128)(2,1)S(1)} %get-tuple-element.48.refs_0_), channel_id=1, source_target_pairs={{0,4},{4,0},{8,12},{12,8},{1,5},{5,1},{9,13},{13,9},{2,6},{6,2},{1... | collective-permute-start | bytes 122888 | tf_op jit(solution)/shard_map/ppermute | solution.py:341
  23.8 1.4 %collective-permute-done.6.refs_3_ = bf16[2,40,256]{2,1,0:T(8,128)(2,1)S(1)} collective-permute-done((bf16[2,40,256]{2,1,0:T(8,128)(2,1)S(1)}, bf16[2,40,256]{2,1,0:T(8,128)(2,1)S(1)}, u32[]{:S(2)}, u32[]{:S(2)}) %collective-permute-start.6) | collective-permute-done | bytes 40992 | tf_op jit(solution)/shard_map/ppermute | solution.py:341
  25.2 1.3 %collective-permute-done.5.refs_2_ = bf16[2,40,256]{2,1,0:T(8,128)(2,1)S(1)} collective-permute-done((bf16[2,40,256]{2,1,0:T(8,128)(2,1)S(1)}, bf16[2,40,256]{2,1,0:T(8,128)(2,1)S(1)}, u32[]{:S(2)}, u32[]{:S(2)}) %collective-permute-start.5) | collective-permute-done | bytes 40992 | tf_op jit(solution)/shard_map/ppermute | solution.py:341
  26.5 1.9 %shard_map.71 = (bf16[72,256]{1,0:T(8,128)(2,1)S(1)}, bf16[72,256]{1,0:T(8,128)(2,1)S(1)}, bf16[72,256]{1,0:T(8,128)(2,1)S(1)}, bf16[72,256]{1,0:T(8,128)(2,1)S(...) custom-call(s32[3]{0:T(128)S(1)} %pad_add_fusion.info, bf16[8,48,128]{2,1,0:T(8,128)(2,1)S(1)} %fusion.6.og_ref, ...), custom_call_target="tpu_custom_call" | custom-call | flops 452984832 | bytes 1368064 | tf_op jit(solution)/shard_map/pallas_call | solution.py:30
  28.4 1.3 %collective-permute-start.7 = (bf16[72,256]{1,0:T(8,128)(2,1)S(1)}, bf16[72,256]{1,0:T(8,128)(2,1)S(1)}, u32[]{:S(2)}, u32[]{:S(2)}) collective-permute-start(bf16[72,256]{1,0:T(8,128)(2,1)S(1)} %get-tuple-element.50), channel_id=1, source_target_pairs={{0,4},{4,0},{8,12},{12,8},{1,5},{5,1},{9,13},{13,9},{2,6},{6,2},{1... | collective-permute-start | bytes 110600 | tf_op jit(solution)/shard_map/ppermute | solution.py:341
  29.7 1.2 %collective-permute-start.8 = (bf16[72,256]{1,0:T(8,128)(2,1)S(1)}, bf16[72,256]{1,0:T(8,128)(2,1)S(1)}, u32[]{:S(2)}, u32[]{:S(2)}) collective-permute-start(bf16[72,256]{1,0:T(8,128)(2,1)S(1)} %get-tuple-element.51), channel_id=1, source_target_pairs={{0,8},{4,12},{8,0},{12,4},{1,9},{5,13},{9,1},{13,5},{2,10},{6,14},... | collective-permute-start | bytes 110600 | tf_op jit(solution)/shard_map/ppermute | solution.py:341
  30.9 2.0 %collective-permute-start.9 = (bf16[72,256]{1,0:T(8,128)(2,1)S(1)}, bf16[72,256]{1,0:T(8,128)(2,1)S(1)}, u32[]{:S(2)}, u32[]{:S(2)}) collective-permute-start(bf16[72,256]{1,0:T(8,128)(2,1)S(1)} %get-tuple-element.52), channel_id=1, source_target_pairs={{0,12},{4,8},{8,4},{12,0},{1,13},{5,9},{9,5},{13,1},{2,14},{6,10},... | collective-permute-start | bytes 110600 | tf_op jit(solution)/shard_map/ppermute | solution.py:341
  32.9 2.5 %collective-permute-done.8.refs_2_ = bf16[72,256]{1,0:T(8,128)(2,1)S(1)} collective-permute-done((bf16[72,256]{1,0:T(8,128)(2,1)S(1)}, bf16[72,256]{1,0:T(8,128)(2,1)S(1)}, u32[]{:S(2)}, u32[]{:S(2)}) %collective-permute-start.8) | collective-permute-done | bytes 36896 | tf_op jit(solution)/shard_map/ppermute | solution.py:341
  35.4 1.3 %collective-permute-done.9.refs_3_ = bf16[72,256]{1,0:T(8,128)(2,1)S(1)} collective-permute-done((bf16[72,256]{1,0:T(8,128)(2,1)S(1)}, bf16[72,256]{1,0:T(8,128)(2,1)S(1)}, u32[]{:S(2)}, u32[]{:S(2)}) %collective-permute-start.9) | collective-permute-done | bytes 36896 | tf_op jit(solution)/shard_map/ppermute | solution.py:341
  36.7 1.7 %shard_map.72 = (bf16[8,64,256]{2,1,0:T(8,128)(2,1)S(1)}, bf16[64,256]{1,0:T(8,128)(2,1)S(1)}, bf16[64,256]{1,0:T(8,128)(2,1)S(1)}, bf16[144,128]{1,0:T(8,128)(2,1)S(1)}, bf16[144,128]{1,0:T(8,128)(2,1)S(1)}) custom-call(s32[3]{0:T(128)S(1)} %pad_add_fusion.info, bf16[72,256]{1,0:T(8,128)(2,1)S(1)} %get-tuple-element.49.refs_0_, ...), custom_call_target="tpu_custom_call" | custom-call | flops 150994944 | bytes 1318912 | tf_op jit(solution)/shard_map/pallas_call | solution.py:30
  40.1 1.1 %collective-permute-start.14 = (bf16[144,128]{1,0:T(8,128)(2,1)S(1)}, bf16[144,128]{1,0:T(8,128)(2,1)S(1)}, u32[]{:S(2)}, u32[]{:S(2)}) collective-permute-start(bf16[144,128]{1,0:T(8,128)(2,1)S(1)} %shard_map.75), channel_id=1, source_target_pairs={{0,2},{2,0},{1,3},{3,1},{4,6},{6,4},{5,7},{7,5},{8,10},{10,8},{9,1... | collective-permute-start | bytes 110600 | tf_op jit(solution)/shard_map/ppermute | solution.py:341
  41.2 2.9 %collective-permute-done.14 = bf16[144,128]{1,0:T(8,128)(2,1)S(1)} collective-permute-done((bf16[144,128]{1,0:T(8,128)(2,1)S(1)}, bf16[144,128]{1,0:T(8,128)(2,1)S(1)}, u32[]{:S(2)}, u32[]{:S(2)}) %collective-permute-start.14) | collective-permute-done | bytes 36896 | tf_op jit(solution)/shard_map/ppermute | solution.py:341
  44.3 1.1 %collective-permute-start.19 = (bf16[576,256]{1,0:T(8,128)(2,1)S(1)}, bf16[576,256]{1,0:T(8,128)(2,1)S(1)}, u32[]{:S(2)}, u32[]{:S(2)}) collective-permute-start(bf16[576,256]{1,0:T(8,128)(2,1)S(1)} %get-tuple-element.68.a_ref), channel_id=1, source_target_pairs={{0,2},{2,0},{1,3},{3,1},{4,6},{6,4},{5,7},{7,5},{8,10},{10,8},{9,1... | collective-permute-start | bytes 884744 | tf_op jit(solution)/shard_map/ppermute | solution.py:341
  45.4 1.8 %collective-permute-start.11 = (bf16[64,256]{1,0:T(8,128)(2,1)S(1)}, bf16[64,256]{1,0:T(8,128)(2,1)S(1)}, u32[]{:S(2)}, u32[]{:S(2)}) collective-permute-start(bf16[64,256]{1,0:T(8,128)(2,1)S(1)} %get-tuple-element.58), channel_id=1, source_target_pairs={{0,12},{4,8},{8,4},{12,0},{1,13},{5,9},{9,5},{13,1},{2,14},{6,10},... | collective-permute-start | bytes 98312 | tf_op jit(solution)/shard_map/ppermute | solution.py:337
  47.2 2.0 %collective-permute-start.17 = (bf16[144,128]{1,0:T(8,128)(2,1)S(1)}, bf16[144,128]{1,0:T(8,128)(2,1)S(1)}, u32[]{:S(2)}, u32[]{:S(2)}) collective-permute-start(bf16[144,128]{1,0:T(8,128)(2,1)S(1)} %get-tuple-element.66.refs_0_), channel_id=1, source_target_pairs={{0,12},{4,8},{8,4},{12,0},{1,13},{5,9},{9,5},{13,1},{2,14},{6,10},... | collective-permute-start | bytes 110600 | tf_op jit(solution)/shard_map/ppermute | solution.py:341
  49.8 1.8 %collective-permute-start.15 = (bf16[144,128]{1,0:T(8,128)(2,1)S(1)}, bf16[144,128]{1,0:T(8,128)(2,1)S(1)}, u32[]{:S(2)}, u32[]{:S(2)}) collective-permute-start(bf16[144,128]{1,0:T(8,128)(2,1)S(1)} %get-tuple-element.66.refs_0_), channel_id=1, source_target_pairs={{0,4},{4,0},{8,12},{12,8},{1,5},{5,1},{9,13},{13,9},{2,6},{6,2},{1... | collective-permute-start | bytes 110600 | tf_op jit(solution)/shard_map/ppermute | solution.py:341
  51.9 1.7 %shard_map.73 = (bf16[64,8,128]{2,1,0:T(8,128)(2,1)}, f32[8,128]{1,0:T(8,128)S(1)}) custom-call(s32[3]{0:T(128)S(1)} %pad_add_fusion.info, bf16[8,64,256]{2,1,0:T(8,128)(2,1)S(1)} %get-tuple-element.56.g_ref, bf16[64,256]{1,0:T(8,128)(2,1)S(1)} %collective-permute-done.10.a_ref, bf16[64,256]{1,0:T(8,128)(2,1)S(1)} %collective-permute-done.11.b_ref, ...), custom_call_target="tpu_custom_call" | custom-call | flops 150994944 | bytes 536576 | tf_op jit(solution)/shard_map/pallas_call | solution.py:30
  57.0 1.4 %shard_map.79 = f32[3,192,64]{2,1,0:T(8,128)} custom-call(s32[3]{0:T(128)S(1)} %pad_add_fusion.info, bf16[144,128]{1,0:T(8,128)(2,1)S(1)} %shard_map.77.refs_0_.mine_ref, bf16[144,128]{1,0:T(8,128)(2,1)S(1)} %collective-permute-done.18.other_ref, bf16[576,256]{1,0:T(8,128)(2,1)S(1)} %collective-permute-done.20._), custom_call_target="tpu_custom_call" | custom-call | flops 1 | bytes 516096 | tf_op jit(solution)/shard_map/pallas_call | solution.py:30
  (53 shorter events, 12.8 us)
Async XLA Ops:
  0.7 0.9 %copy-start = (bf16[64,3,3,64]{3,0,2,1:T(8,128)(2,1)S(1)}, bf16[64,3,3,64]{3,0,2,1:T(8,128)(2,1)}, u32[]{:S(2)}) copy-start(bf16[64,3,3,64]{3,0,2,1:T(8,128)(2,1)} %param.5) | copy-start | bytes 221188
  3.4 23.1 %copy-start.4 = (bf16[128,3,3,256]{3,0,2,1:T(8,128)(2,1)S(1)}, bf16[128,3,3,256]{3,0,2,1:T(8,128)(2,1)}, u32[]{:S(2)}) copy-start(bf16[128,3,3,256]{3,0,2,1:T(8,128)(2,1)} %param.6) | copy-start | bytes 1769476
  4.5 6.8 %collective-permute-start.1 = (bf16[64,128]{1,0:T(8,128)(2,1)S(1)}, bf16[64,128]{1,0:T(8,128)(2,1)S(1)}, u32[]{:S(2)}, u32[]{:S(2)}) collective-permute-start(bf16[64,128]{1,0:T(8,128)(2,1)S(1)} %get-tuple-element.38), channel_id=1, source_target_pairs={{0,12},{4,8},{8,4},{12,0},{1,13},{5,9},{9,5},{13,1},{2,14},{6,10},... | collective-permute-start | bytes 49160 | tf_op jit(solution)/shard_map/ppermute | solution.py:337
  9.6 3.7 %collective-permute-start = (bf16[64,128]{1,0:T(8,128)(2,1)S(1)}, bf16[64,128]{1,0:T(8,128)(2,1)S(1)}, u32[]{:S(2)}, u32[]{:S(2)}) collective-permute-start(bf16[64,128]{1,0:T(8,128)(2,1)S(1)} %get-tuple-element.37._), channel_id=1, source_target_pairs={{0,4},{4,0},{8,12},{12,8},{1,5},{5,1},{9,13},{13,9},{2,6},{6,2},{1... | collective-permute-start | bytes 49160 | tf_op jit(solution)/shard_map/ppermute | solution.py:333
  14.0 3.8 %collective-permute-start.2 = (bf16[144,128]{1,0:T(8,128)(2,1)S(1)}, bf16[144,128]{1,0:T(8,128)(2,1)S(1)}, u32[]{:S(2)}, u32[]{:S(2)}) collective-permute-start(bf16[144,128]{1,0:T(8,128)(2,1)S(1)} %get-tuple-element.41), channel_id=1, source_target_pairs={{0,3},{1,2},{2,1},{3,0},{4,7},{5,6},{6,5},{7,4},{8,11},{9,10},{10,... | collective-permute-start | bytes 110600 | tf_op jit(solution)/shard_map/ppermute | solution.py:337
  14.1 3.7 %collective-permute-start.3 = (bf16[144,128]{1,0:T(8,128)(2,1)S(1)}, bf16[144,128]{1,0:T(8,128)(2,1)S(1)}, u32[]{:S(2)}, u32[]{:S(2)}) collective-permute-start(bf16[144,128]{1,0:T(8,128)(2,1)S(1)} %get-tuple-element.42), channel_id=1, source_target_pairs={{0,1},{1,0},{2,3},{3,2},{4,5},{5,4},{6,7},{7,6},{8,9},{9,8},{10,11... | collective-permute-start | bytes 110600 | tf_op jit(solution)/shard_map/ppermute | solution.py:333
  19.2 6.0 %collective-permute-start.6 = (bf16[2,40,256]{2,1,0:T(8,128)(2,1)S(1)}, bf16[2,40,256]{2,1,0:T(8,128)(2,1)S(1)}, u32[]{:S(2)}, u32[]{:S(2)}) collective-permute-start(bf16[2,40,256]{2,1,0:T(8,128)(2,1)S(1)} %get-tuple-element.48.refs_0_), channel_id=1, source_target_pairs={{0,12},{4,8},{8,4},{12,0},{1,13},{5,9},{9,5},{13,1},{2,14},{6,10},... | collective-permute-start | bytes 122888 | tf_op jit(solution)/shard_map/ppermute | solution.py:341
  21.1 5.4 %collective-permute-start.5 = (bf16[2,40,256]{2,1,0:T(8,128)(2,1)S(1)}, bf16[2,40,256]{2,1,0:T(8,128)(2,1)S(1)}, u32[]{:S(2)}, u32[]{:S(2)}) collective-permute-start(bf16[2,40,256]{2,1,0:T(8,128)(2,1)S(1)} %get-tuple-element.48.refs_0_), channel_id=1, source_target_pairs={{0,8},{4,12},{8,0},{12,4},{1,9},{5,13},{9,1},{13,5},{2,10},{6,14},... | collective-permute-start | bytes 122888 | tf_op jit(solution)/shard_map/ppermute | solution.py:341
  21.1 5.4 %collective-permute-start.4 = (bf16[2,40,256]{2,1,0:T(8,128)(2,1)S(1)}, bf16[2,40,256]{2,1,0:T(8,128)(2,1)S(1)}, u32[]{:S(2)}, u32[]{:S(2)}) collective-permute-start(bf16[2,40,256]{2,1,0:T(8,128)(2,1)S(1)} %get-tuple-element.48.refs_0_), channel_id=1, source_target_pairs={{0,4},{4,0},{8,12},{12,8},{1,5},{5,1},{9,13},{13,9},{2,6},{6,2},{1... | collective-permute-start | bytes 122888 | tf_op jit(solution)/shard_map/ppermute | solution.py:341
  28.4 23.1 %copy-start.1 = (bf16[64,3,3,64]{3,0,2,1:T(8,128)(2,1)S(1)}, bf16[64,3,3,64]{3,0,2,1:T(8,128)(2,1)}, u32[]{:S(2)}) copy-start(bf16[64,3,3,64]{3,0,2,1:T(8,128)(2,1)} %param.5) | copy-start | bytes 221188
  28.4 4.5 %collective-permute-start.7 = (bf16[72,256]{1,0:T(8,128)(2,1)S(1)}, bf16[72,256]{1,0:T(8,128)(2,1)S(1)}, u32[]{:S(2)}, u32[]{:S(2)}) collective-permute-start(bf16[72,256]{1,0:T(8,128)(2,1)S(1)} %get-tuple-element.50), channel_id=1, source_target_pairs={{0,4},{4,0},{8,12},{12,8},{1,5},{5,1},{9,13},{13,9},{2,6},{6,2},{1... | collective-permute-start | bytes 110600 | tf_op jit(solution)/shard_map/ppermute | solution.py:341
  29.7 5.6 %collective-permute-start.8 = (bf16[72,256]{1,0:T(8,128)(2,1)S(1)}, bf16[72,256]{1,0:T(8,128)(2,1)S(1)}, u32[]{:S(2)}, u32[]{:S(2)}) collective-permute-start(bf16[72,256]{1,0:T(8,128)(2,1)S(1)} %get-tuple-element.51), channel_id=1, source_target_pairs={{0,8},{4,12},{8,0},{12,4},{1,9},{5,13},{9,1},{13,5},{2,10},{6,14},... | collective-permute-start | bytes 110600 | tf_op jit(solution)/shard_map/ppermute | solution.py:341
  30.9 5.8 %collective-permute-start.9 = (bf16[72,256]{1,0:T(8,128)(2,1)S(1)}, bf16[72,256]{1,0:T(8,128)(2,1)S(1)}, u32[]{:S(2)}, u32[]{:S(2)}) collective-permute-start(bf16[72,256]{1,0:T(8,128)(2,1)S(1)} %get-tuple-element.52), channel_id=1, source_target_pairs={{0,12},{4,8},{8,4},{12,0},{1,13},{5,9},{9,5},{13,1},{2,14},{6,10},... | collective-permute-start | bytes 110600 | tf_op jit(solution)/shard_map/ppermute | solution.py:341
  38.4 1.7 %collective-permute-start.13 = (bf16[144,128]{1,0:T(8,128)(2,1)S(1)}, bf16[144,128]{1,0:T(8,128)(2,1)S(1)}, u32[]{:S(2)}, u32[]{:S(2)}) collective-permute-start(bf16[144,128]{1,0:T(8,128)(2,1)S(1)} %get-tuple-element.65), channel_id=1, source_target_pairs={{0,1},{1,0},{2,3},{3,2},{4,5},{5,4},{6,7},{7,6},{8,9},{9,8},{10,11... | collective-permute-start | bytes 110600 | tf_op jit(solution)/shard_map/ppermute | solution.py:333
  39.6 4.6 %collective-permute-start.12 = (bf16[576,256]{1,0:T(8,128)(2,1)S(1)}, bf16[576,256]{1,0:T(8,128)(2,1)S(1)}, u32[]{:S(2)}, u32[]{:S(2)}) collective-permute-start(bf16[576,256]{1,0:T(8,128)(2,1)S(1)} %get-tuple-element.64), channel_id=1, source_target_pairs={{0,1},{1,0},{2,3},{3,2},{4,5},{5,4},{6,7},{7,6},{8,9},{9,8},{10,11... | collective-permute-start | bytes 884744 | tf_op jit(solution)/shard_map/ppermute | solution.py:333
  40.1 4.0 %collective-permute-start.14 = (bf16[144,128]{1,0:T(8,128)(2,1)S(1)}, bf16[144,128]{1,0:T(8,128)(2,1)S(1)}, u32[]{:S(2)}, u32[]{:S(2)}) collective-permute-start(bf16[144,128]{1,0:T(8,128)(2,1)S(1)} %shard_map.75), channel_id=1, source_target_pairs={{0,2},{2,0},{1,3},{3,1},{4,6},{6,4},{5,7},{7,5},{8,10},{10,8},{9,1... | collective-permute-start | bytes 110600 | tf_op jit(solution)/shard_map/ppermute | solution.py:341
  44.3 9.9 %collective-permute-start.19 = (bf16[576,256]{1,0:T(8,128)(2,1)S(1)}, bf16[576,256]{1,0:T(8,128)(2,1)S(1)}, u32[]{:S(2)}, u32[]{:S(2)}) collective-permute-start(bf16[576,256]{1,0:T(8,128)(2,1)S(1)} %get-tuple-element.68.a_ref), channel_id=1, source_target_pairs={{0,2},{2,0},{1,3},{3,1},{4,6},{6,4},{5,7},{7,5},{8,10},{10,8},{9,1... | collective-permute-start | bytes 884744 | tf_op jit(solution)/shard_map/ppermute | solution.py:341
  45.4 4.4 %collective-permute-start.10 = (bf16[64,256]{1,0:T(8,128)(2,1)S(1)}, bf16[64,256]{1,0:T(8,128)(2,1)S(1)}, u32[]{:S(2)}, u32[]{:S(2)}) collective-permute-start(bf16[64,256]{1,0:T(8,128)(2,1)S(1)} %get-tuple-element.57), channel_id=1, source_target_pairs={{0,4},{4,0},{8,12},{12,8},{1,5},{5,1},{9,13},{13,9},{2,6},{6,2},{1... | collective-permute-start | bytes 98312 | tf_op jit(solution)/shard_map/ppermute | solution.py:333
  45.4 6.5 %collective-permute-start.11 = (bf16[64,256]{1,0:T(8,128)(2,1)S(1)}, bf16[64,256]{1,0:T(8,128)(2,1)S(1)}, u32[]{:S(2)}, u32[]{:S(2)}) collective-permute-start(bf16[64,256]{1,0:T(8,128)(2,1)S(1)} %get-tuple-element.58), channel_id=1, source_target_pairs={{0,12},{4,8},{8,4},{12,0},{1,13},{5,9},{9,5},{13,1},{2,14},{6,10},... | collective-permute-start | bytes 98312 | tf_op jit(solution)/shard_map/ppermute | solution.py:337
  47.2 6.5 %collective-permute-start.17 = (bf16[144,128]{1,0:T(8,128)(2,1)S(1)}, bf16[144,128]{1,0:T(8,128)(2,1)S(1)}, u32[]{:S(2)}, u32[]{:S(2)}) collective-permute-start(bf16[144,128]{1,0:T(8,128)(2,1)S(1)} %get-tuple-element.66.refs_0_), channel_id=1, source_target_pairs={{0,12},{4,8},{8,4},{12,0},{1,13},{5,9},{9,5},{13,1},{2,14},{6,10},... | collective-permute-start | bytes 110600 | tf_op jit(solution)/shard_map/ppermute | solution.py:341
  49.2 4.9 %collective-permute-start.16 = (bf16[144,128]{1,0:T(8,128)(2,1)S(1)}, bf16[144,128]{1,0:T(8,128)(2,1)S(1)}, u32[]{:S(2)}, u32[]{:S(2)}) collective-permute-start(bf16[144,128]{1,0:T(8,128)(2,1)S(1)} %get-tuple-element.66.refs_0_), channel_id=1, source_target_pairs={{0,8},{4,12},{8,0},{12,4},{1,9},{5,13},{9,1},{13,5},{2,10},{6,14},... | collective-permute-start | bytes 110600 | tf_op jit(solution)/shard_map/ppermute | solution.py:341
  49.8 4.4 %collective-permute-start.15 = (bf16[144,128]{1,0:T(8,128)(2,1)S(1)}, bf16[144,128]{1,0:T(8,128)(2,1)S(1)}, u32[]{:S(2)}, u32[]{:S(2)}) collective-permute-start(bf16[144,128]{1,0:T(8,128)(2,1)S(1)} %get-tuple-element.66.refs_0_), channel_id=1, source_target_pairs={{0,4},{4,0},{8,12},{12,8},{1,5},{5,1},{9,13},{13,9},{2,6},{6,2},{1... | collective-permute-start | bytes 110600 | tf_op jit(solution)/shard_map/ppermute | solution.py:341
  54.2 1.6 %collective-permute-start.20 = (bf16[576,256]{1,0:T(8,128)(2,1)S(1)}, bf16[576,256]{1,0:T(8,128)(2,1)S(1)}, u32[]{:S(2)}, u32[]{:S(2)}) collective-permute-start(bf16[576,256]{1,0:T(8,128)(2,1)S(1)} %shard_map.78), channel_id=1, source_target_pairs={{0,1},{1,0},{2,3},{3,2},{4,5},{5,4},{6,7},{7,6},{8,9},{9,8},{10,11... | collective-permute-start | bytes 884744 | tf_op jit(solution)/shard_map/ppermute | solution.py:333
  54.3 2.7 %collective-permute-start.18 = (bf16[144,128]{1,0:T(8,128)(2,1)S(1)}, bf16[144,128]{1,0:T(8,128)(2,1)S(1)}, u32[]{:S(2)}, u32[]{:S(2)}) collective-permute-start(bf16[144,128]{1,0:T(8,128)(2,1)S(1)} %shard_map.77.refs_0_.mine_ref), channel_id=1, source_target_pairs={{0,1},{1,0},{2,3},{3,2},{4,5},{5,4},{6,7},{7,6},{8,9},{9,8},{10,11... | collective-permute-start | bytes 110600 | tf_op jit(solution)/shard_map/ppermute | solution.py:333
  (2 other events, 1.7 us)

commit v6 on v5

--- a/solution.py
+++ b/solution.py
@@ -12,6 +12,7 @@
 F32 = jnp.float32
 COLS = ("col", "pair")
 REACH = 3
+TAIL = 80
 PITCH = 48
 SENT = 40
 
@@ -20,9 +21,9 @@
     return lax.dot_general(a, b, ((contract[:1], contract[1:]), ((), ())), preferred_element_type=F32)
 
 
-def whole_call(body, outs, operands, flops, scalars=1, scratch=(), after=0, held=0):
+def whole_call(body, outs, operands, flops, scalars=1, scratch=(), after=0, out_space=pltpu.VMEM):
     specs = [
-        pl.BlockSpec(memory_space=pltpu.SMEM if n < scalars else pltpu.HBM if n < scalars + held else pltpu.VMEM)
+        pl.BlockSpec(memory_space=pltpu.SMEM if n < scalars else pltpu.VMEM)
         for n in range(len(operands) - after)
     ] + [pl.BlockSpec(memory_space=pl.ANY)] * after
     sizes = [math.prod(a.shape) * a.dtype.itemsize for a in tuple(operands[scalars:]) + tuple(outs)]
@@ -31,7 +32,7 @@
         body,
         out_shape=outs,
         in_specs=specs,
-        out_specs=[pl.BlockSpec(memory_space=pltpu.VMEM) for _ in outs],
+        out_specs=[pl.BlockSpec(memory_space=out_space) for _ in outs],
         scratch_shapes=list(scratch),
         cost_estimate=pl.CostEstimate(flops=flops, bytes_accessed=moved, transcendentals=0),
         compiler_params=pltpu.CompilerParams(vmem_limit_bytes=40 * 1024 * 1024),
@@ -76,39 +77,11 @@
     return jnp.where(lane == 4 * c + 2 * i + j, 1.0, 0.0).astype(BF16)
 
 
-def matrices(info, _, pool_ref, back_ref, order_ref, *, total):
+def constants(info, w_ref, joined_ref, pool_ref, back_ref, order_ref, *, total):
+    joined_ref[...] = jnp.concatenate([w_ref[0], w_ref[1], w_ref[2]], axis=1)
     pool_ref[...] = pool_matrix(info[0], total)
     back_ref[...] = pool_matrix(info[0], total, back=True)
     order_ref[...] = order_matrix()
-
-
-def split_rows(
-    info, x_hbm, w_hbm, og_hbm, rows_ref, a_ref, b_ref, joined_ref, head_ref, tail_ref, x_ref, w_ref, sems
-):
-    edge = head_ref.shape[0]
-    copies = [
-        pltpu.make_async_copy(source, target, sems.at[n])
-        for n, (source, target) in enumerate(
-            [
-                (x_hbm, x_ref),
-                (w_hbm, w_ref),
-                (og_hbm.at[pl.ds(0, edge)], head_ref),
-                (og_hbm.at[pl.ds(og_hbm.shape[0] - edge, edge)], tail_ref),
-            ]
-        )
-    ]
-    for copy in copies:
-        copy.start()
-    copies[0].wait()
-    even = (info[2] & 1) == 0
-    rows = jnp.swapaxes(x_ref[...].astype(F32), 0, 1)
-    rows_ref[...] = rows.astype(BF16)
-    first, last = rows[0], rows[-1]
-    a_ref[...] = jnp.where(even, last, first).astype(BF16)
-    b_ref[...] = jnp.where(even, first, last).astype(BF16)
-    for copy in copies[1:]:
-        copy.wait()
-    joined_ref[...] = jnp.concatenate([w_ref[0], w_ref[1], w_ref[2]], axis=1)
 
 
 def beside(a_ref, b_ref, place, count):
@@ -236,7 +209,7 @@
         terms[k][...] = pack_ref[band ^ k]
 
 
-def filter_two_grads(info, map_ref, grad_ref, _, keep_ref, send_ref, all_ref):
+def filter_two_grads(info, map_ref, grad_ref, keep_ref, send_ref, all_ref):
     pair = info[1]
     rows = map_ref.shape[0] - 2
     filters = grad_ref.shape[2]
@@ -257,22 +230,23 @@
     refs[-1][...] = (a_ref[...].astype(F32) + b_ref[...].astype(F32)).astype(BF16)
 
 
-def add_and_pass(a_ref, b_ref, other_ref, out_ref, passed_ref):
-    out_ref[...] = (a_ref[...].astype(F32) + b_ref[...].astype(F32)).astype(BF16)
-    passed_ref[...] = other_ref[...]
-
-
-def sum_rows(*refs):
-    *terms, _, out_ref = refs
-    terms = [t[...].astype(F32) for t in terms]
-    while len(terms) > 1:
-        terms = [a + b for a, b in zip(terms[::2], terms[1::2])]
-    out_ref[...] = terms[0].astype(BF16)
+def add_halves(a_ref, b_ref, two_ref, one_ref):
+    half = two_ref.shape[0]
+    total = (a_ref[...].astype(F32) + b_ref[...].astype(F32)).astype(BF16)
+    two_ref[...] = total[:half]
+    one_ref[...] = total[half:]
+
+
+def add_joined(a_ref, b_ref, c_ref, d_ref, out_ref):
+    half = a_ref.shape[0]
+    out_ref[:half] = (a_ref[...].astype(F32) + b_ref[...].astype(F32)).astype(BF16)
+    out_ref[half:] = (c_ref[...].astype(F32) + d_ref[...].astype(F32)).astype(BF16)
 
 
 def grad_pre_one(info, *refs, bands):
     terms, refs = refs[:bands], refs[bands:]
-    slope_ref, wide_ref, pool_ref, order_ref, g_ref, a_ref, b_ref, keep_ref, send_ref, part_ref = refs
+    slope_ref, wide_ref, pool_ref, order_ref, keep_two_ref, send_two_ref, *refs = refs
+    g_ref, a_ref, b_ref, keep_ref, send_ref, part_ref = refs
     pair = info[1]
     summed = terms[0][...].astype(F32)
     for k in range(1, bands):
@@ -299,12 +273,14 @@
     first, last = g_ref[0].astype(F32), g_ref[7].astype(F32)
     a_ref[...] = jnp.where(even, last, first).astype(BF16)
     b_ref[...] = jnp.where(even, first, last).astype(BF16)
-    part_ref[:192] = acc[:, :128].astype(BF16)
-    tail = jnp.concatenate([acc[:96, 128:], acc[96:, 128:]], 1)
-    part_ref[192:] = tail.astype(BF16)
-    half = keep_ref.shape[0]
-    keep_ref[...] = part_ref[pl.ds(pl.multiple_of(pair * half, 16), half)]
-    send_ref[...] = part_ref[pl.ds(pl.multiple_of((1 - pair) * half, 16), half)]
+    part_ref[:96] = jnp.concatenate([acc[:96, :128], acc[96:, :128]], 1)
+    part_ref[96:] = jnp.concatenate([acc[48 * q : 48 * q + 48, 128:] for q in range(4)], 1)
+    half = keep_two_ref.shape[0]
+    blank = jnp.zeros((TAIL - 72, 256), F32)
+    for ref, two_ref, place in ((keep_ref, keep_two_ref, pair), (send_ref, send_two_ref, 1 - pair)):
+        ref[:half] = two_ref[...]
+        mine = part_ref[pl.ds(pl.multiple_of(place * 72, 8), 72)]
+        ref[half:] = jnp.concatenate([mine, blank], 0).astype(BF16)
 
 
 def layer_one_back(info, g_ref, a_ref, b_ref, w_ref, out_ref, done_ref, *, bands):
@@ -318,15 +294,25 @@
     out_ref[...] = jnp.swapaxes(jnp.stack(rows, 0), 0, 1).astype(BF16)
 
 
-def unpack_one(info, mine_ref, other_ref, _, out_ref, flat_ref, *, scale):
-    pair, half = info[1], mine_ref.shape[0]
-    flat_ref[pl.ds(pl.multiple_of(pair * half, 16), half)] = mine_ref[...]
-    flat_ref[pl.ds(pl.multiple_of((1 - pair) * half, 16), half)] = other_ref[...]
-    flat = flat_ref[...].astype(F32) * scale
-    out_ref[0] = flat[:192, :64]
-    out_ref[1] = flat[:192, 64:]
-    out_ref[2, :96] = flat[192:, :64]
-    out_ref[2, 96:] = flat[192:, 64:]
+def finish(info, mine_ref, other_ref, one_hbm, two_hbm, one_ref, two_ref, flat_ref, sems, *, scales):
+    pair, half = info[1], mine_ref.shape[0] - TAIL
+    copies = [pltpu.make_async_copy(one_ref, one_hbm, sems.at[0])]
+    for ref, place in ((mine_ref, pair), (other_ref, 1 - pair)):
+        flat_ref[pl.ds(pl.multiple_of(place * 72, 8), 72)] = ref[half : half + 72].astype(F32) * scales[0]
+    one_ref[0, :96] = flat_ref[:96, :64]
+    one_ref[1, :96] = flat_ref[:96, 64:128]
+    one_ref[0, 96:] = flat_ref[:96, 128:192]
+    one_ref[1, 96:] = flat_ref[:96, 192:]
+    for q in range(4):
+        one_ref[2, 48 * q : 48 * q + 48] = flat_ref[96:, 64 * q : 64 * q + 64]
+    copies[0].start()
+    for n, (ref, place) in enumerate(((mine_ref, pair), (other_ref, 1 - pair))):
+        rows = pl.ds(pl.multiple_of(place * half, 16), half)
+        two_ref[n] = ref[:half].astype(F32) * scales[1]
+        copies.append(pltpu.make_async_copy(two_ref.at[n], two_hbm.at[rows], sems.at[1 + n]))
+        copies[-1].start()
+    for copy in copies:
+        copy.wait()
 
 
 def even_swap(values, axis, count):
@@ -352,16 +338,12 @@
     return total
 
 
-def sum_cols(part, after=()):
-    count, step = lax.axis_size("col"), 1
-    while step < count:
-        other = xor_swap(part, "col", count, step)
+def sum_but_last(part, axis, count):
+    step = 1
+    while 2 * step < count:
+        part = added(part, xor_swap(part, axis, count, step))
         step *= 2
-        if after and step >= count:
-            part = added(part, other, *after)
-        else:
-            part = (part.astype(F32) + other.astype(F32)).astype(BF16)
-    return part
+    return part, xor_swap(part, axis, count, step)
 
 
 def local(features_in, filters_one, filters_two, out_grad):
@@ -382,27 +364,15 @@
 
     og = jnp.transpose(out_grad, (1, 2, 0))
     edge = REACH - 1
-    x, to_a, to_b, joined_one, head, tail = whole_call(
-        split_rows,
-        [shaped((band_rows, channels, strip_cols))]
-        + [shaped((channels, strip_cols))] * 2
-        + [shaped((3 * channels, 3 * channels))]
-        + [shaped((edge, pooled_rows, filters))] * 2,
-        [at_place, features_in, taps_one, og],
-        1,
-        scratch=[
-            pltpu.VMEM(features_in.shape, BF16),
-            pltpu.VMEM(taps_one.shape, BF16),
-            pltpu.SemaphoreType.DMA((4,)),
-        ],
-        held=3,
-    )
-    pool, pool_back, order = whole_call(
-        functools.partial(matrices, total=total),
-        [shaped((2 * PITCH, 256))] * 2 + [shaped((256, 256))],
-        [at_place, to_a],
+    x = jnp.transpose(features_in, (1, 0, 2))
+    even = band % 2 == 0
+    to_a, to_b = jnp.where(even, x[-1], x[0]), jnp.where(even, x[0], x[-1])
+    head, tail = og[:edge], og[-edge:]
+    joined_one, pool, pool_back, order = whole_call(
+        functools.partial(constants, total=total),
+        [shaped((3 * channels, 3 * channels))] + [shaped((2 * PITCH, 256))] * 2 + [shaped((256, 256))],
+        [at_place, taps_one],
         10**8,
-        after=1,
     )
     up_a, up_b = even_swap(to_a, "row", bands), odd_swap(to_b, "row", bands)
     head, tail = head.reshape(-1, 128), tail.reshape(-1, 128)
@@ -444,56 +414,60 @@
     )
     received = [terms[0]] + row_swaps(terms, bands)
 
-    share = 9 * channels * channels // 256
+    half = 9 * filters // 2
+    keep_two, send_two = whole_call(
+        filter_two_grads,
+        [shaped((half, 4 * channels))] * 2,
+        [at_place, pooled_map, grad_map],
+        2 * count * 9 * filters * 4 * channels,
+        scratch=[pltpu.VMEM((2 * half, 4 * channels), BF16)],
+    )
     g, up_a, up_b, keep, send = whole_call(
         functools.partial(grad_pre_one, bands=bands),
         [shaped((band_rows, channels, 256))]
         + [shaped((channels, 256))] * 2
-        + [shaped((share, 128))] * 2,
-        [at_place] + received + [slope, wide, pool_back, order],
+        + [shaped((half + TAIL, 256))] * 2,
+        [at_place] + received + [slope, wide, pool_back, order, keep_two, send_two],
         2 * 8 * 192 * 192 * 256,
-        scratch=[pltpu.VMEM((2 * share, 128), BF16)],
-    )
-    half = 9 * filters // 2
-    keep_two, send_two = whole_call(
-        filter_two_grads,
-        [shaped((half, 4 * channels))] * 2,
-        [at_place, pooled_map, grad_map, keep],
-        0,
-        scratch=[pltpu.VMEM((2 * half, 4 * channels), BF16)],
-        after=1,
-    )
-    part = sum_cols(added(keep, even_swap(send, "pair", 2)))
-    part_two, part = whole_call(
-        add_and_pass,
-        [shaped(keep_two.shape), shaped(part.shape)],
-        [keep_two, even_swap(send_two, "pair", 2), part],
+        scratch=[pltpu.VMEM((144, 256), F32)],
+    )
+    two, one = whole_call(
+        add_halves,
+        [shaped((half, 256)), shaped((TAIL, 256))],
+        [keep, even_swap(send, "pair", 2)],
         0,
         scalars=0,
     )
-    terms = [part] + row_swaps([part] * bands, bands)
+    columns = lax.axis_size("col")
+    two, two_more = sum_but_last(two, "col", columns)
+    one, one_more = sum_but_last(one, "row", bands)
     input_grad, done = whole_call(
         functools.partial(layer_one_back, bands=bands),
         [shaped(features_in.shape), shaped((8, 128), F32)],
         [at_place, g, even_swap(up_a, "row", bands), odd_swap(up_b, "row", bands), back_one],
         2 * band_rows * 192 * 192 * 256,
     )
-    (mine,) = whole_call(sum_rows, [shaped(part.shape)], terms + [done], 0, scalars=0, after=1)
-    other = even_swap(mine, "pair", 2)
-    mine_two = sum_cols(part_two, after=(mine,))
-    other_two = even_swap(mine_two, "pair", 2)
-    first, second = jnp.where(pair == 0, mine_two, other_two), jnp.where(pair == 0, other_two, mine_two)
-    grad_two = jnp.concatenate([first, second], 0)
-    grad_two = grad_two.astype(F32) * (1.0 / math.sqrt(pooled_rows * total))
+    one, one_more = sum_but_last(added(one, one_more, done), "col", columns)
+    (mine,) = whole_call(
+        add_joined, [shaped((half + TAIL, 256))], [two, two_more, one, one_more], 0, scalars=0
+    )
+    grad_one, grad_two = whole_call(
+        functools.partial(
+            finish,
+            scales=(1.0 / math.sqrt(height * width), 1.0 / math.sqrt(pooled_rows * total)),
+        ),
+        [shaped((3, 3 * channels, channels), F32), shaped((2 * half, 256), F32)],
+        [at_place, mine, even_swap(mine, "pair", 2)],
+        1,
+        scratch=[
+            pltpu.VMEM((3, 3 * channels, channels), F32),
+            pltpu.VMEM((2, half, 256), F32),
+            pltpu.VMEM((144, 256), F32),
+            pltpu.SemaphoreType.DMA((3,)),
+        ],
+        out_space=pl.ANY,
+    )
     grad_two = jnp.transpose(grad_two.reshape(3, 3, filters, 4 * channels), (2, 0, 1, 3))
-    (grad_one,) = whole_call(
-        functools.partial(unpack_one, scale=1.0 / math.sqrt(height * width)),
-        [shaped((3, 3 * channels, channels), F32)],
-        [at_place, mine, other, other_two],
-        1,
-        scratch=[pltpu.VMEM((2 * share, 128), BF16)],
-        after=1,
-    )
     grad_one = jnp.transpose(grad_one.reshape(3, 3, channels, channels), (2, 0, 1, 3))
     return (input_grad, grad_one, grad_two)
 

time: 58.6 us -> 56.9 us (0.971)
  waiting for transfers between devices: 15.3 us -> 17.9 us
  starting transfers between devices: 25.3 us -> 23.5 us
  other arithmetic: 1.28 us -> 0.14 us
  local copies, waits for them, and re-layouts: 3.87 us -> 3.12 us
  Pallas kernels: 11.9 us -> 11.2 us
    ppermute x7 -> x5, starting transfers between devices: 2.79 us -> 6.85 us  [even_swap(): return lax.ppermute(values, axis, [(n, n ^ 1) for n in range(count)])]
    ppermute x11 -> x10, starting transfers between devices: 15.5 us -> 11.6 us  [xor_swap(): return lax.ppermute(values, axis, [(n, n ^ k) for n in range(count)])]
    ppermute x3, waiting for transfers between devices: 2.31 us -> 4.99 us  [odd_swap(): lax.ppermute(values, axis, [(n, (n - 1 if n % 2 == 0 else n + 1) % count)...]
    ppermute x3, starting transfers between devices: 6.98 us -> 5.01 us  [odd_swap(): lax.ppermute(values, axis, [(n, (n - 1 if n % 2 == 0 else n + 1) % count)...]
    mul x1 -> x0, other arithmetic: 1.09 us -> none  [local(): grad_two = grad_two.astype(F32) * (1.0 / math.sqrt(pooled_rows * total))]
    unnamed x11 -> x8, local copies, waits for them, and re-layouts: 3.51 us -> 2.75 us
    pallas_call x13 -> x12, Pallas kernels: 11.9 us -> 11.2 us  [whole_call(): pl.pallas_call(body, out_shape=outs, in_specs=specs, out_specs=[pl.BlockS...]
    ppermute x11 -> x10, waiting for transfers between devices: 9.86 us -> 9.65 us  [xor_swap(): return lax.ppermute(values, axis, [(n, n ^ k) for n in range(count)])]
  transfers between devices with their start and end apart: 21 -> 18, of which waited for: 10 -> 9; matrix products, arithmetic and copies ran while one was open for 4% -> 2% of each run, Pallas kernels for 6% -> 6%
where the time goes in v6:
time: 56.9 us; the launch traced here: 56.7 us
  starting transfers between devices  23.5 us (41%)
  waiting for transfers between devices  17.9 us (31%)
  Pallas kernels  11.2 us (20%)
  local copies, waits for them, and re-layouts  3.12 us (5%)
  between operations  0.86 us (2%)
    ppermute x10, starting transfers between devices, xor_swap(): return lax.ppermute(values, axis, [(n, n ^ k) for n in range(count)])  11.6 us
    pallas_call x12, Pallas kernels, whole_call(): pl.pallas_call(body, out_shape=outs, in_specs=specs, out_specs=[pl.BlockS...  11.2 us
    ppermute x10, waiting for transfers between devices, xor_swap(): return lax.ppermute(values, axis, [(n, n ^ k) for n in range(count)])  9.65 us
    ppermute x5, starting transfers between devices, even_swap(): return lax.ppermute(values, axis, [(n, n ^ 1) for n in range(count)])  6.85 us
    ppermute x3, starting transfers between devices, odd_swap(): lax.ppermute(values, axis, [(n, (n - 1 if n % 2 == 0 else n + 1) % count)...  5.01 us
    ppermute x3, waiting for transfers between devices, odd_swap(): lax.ppermute(values, axis, [(n, (n - 1 if n % 2 == 0 else n + 1) % count)...  4.99 us
    ppermute x5, waiting for transfers between devices, even_swap(): return lax.ppermute(values, axis, [(n, n ^ 1) for n in range(count)])  3.26 us
    unnamed x8, local copies, waits for them, and re-layouts  2.75 us
  transfers between devices with their start and end apart: 18, of which 9 were waited for; matrix products, arithmetic and copies ran while one was open for 2% of the time, Pallas kernels for 6%

profile of v6, /device:TPU:0, one launch (start us, length us, event | category | flops | bytes accessed | tf_op | source)
XLA Modules:
  0.0 56.7 jit_solution(11527343547188170832)
XLA Ops:
  1.7 3.1 %collective-permute-start = (bf16[64,128]{1,0:T(8,128)(2,1)S(1)}, bf16[64,128]{1,0:T(8,128)(2,1)S(1)}, u32[]{:S(2)}, u32[]{:S(2)}) collective-permute-start(bf16[64,128]{1,0:T(8,128)(2,1)S(1)} %get-tuple-element.64), channel_id=1, source_target_pairs={{0,4},{4,0},{8,12},{12,8},{1,5},{5,1},{9,13},{13,9},{2,6},{6,2},{1... | collective-permute-start | bytes 49160 | tf_op jit(solution)/shard_map/ppermute | solution.py:319
  4.7 2.5 %collective-permute-start.1 = (bf16[64,128]{1,0:T(8,128)(2,1)S(1)}, bf16[64,128]{1,0:T(8,128)(2,1)S(1)}, u32[]{:S(2)}, u32[]{:S(2)}) collective-permute-start(bf16[64,128]{1,0:T(8,128)(2,1)S(1)} %get-tuple-element.63), channel_id=1, source_target_pairs={{0,12},{4,8},{8,4},{12,0},{1,13},{5,9},{9,5},{13,1},{2,14},{6,10},... | collective-permute-start | bytes 49160 | tf_op jit(solution)/shard_map/ppermute | solution.py:323
  8.2 2.1 %collective-permute-done.1.up_b_ref = bf16[64,128]{1,0:T(8,128)(2,1)S(1)} collective-permute-done((bf16[64,128]{1,0:T(8,128)(2,1)S(1)}, bf16[64,128]{1,0:T(8,128)(2,1)S(1)}, u32[]{:S(2)}, u32[]{:S(2)}) %collective-permute-start.1) | collective-permute-done | bytes 16416 | tf_op jit(solution)/shard_map/ppermute | solution.py:323
  11.0 1.6 %collective-permute-start.3 = (bf16[144,128]{1,0:T(8,128)(2,1)S(1)}, bf16[144,128]{1,0:T(8,128)(2,1)S(1)}, u32[]{:S(2)}, u32[]{:S(2)}) collective-permute-start(bf16[144,128]{1,0:T(8,128)(2,1)S(1)} %get-tuple-element.34), channel_id=1, source_target_pairs={{0,1},{1,0},{2,3},{3,2},{4,5},{5,4},{6,7},{7,6},{8,9},{9,8},{10,11... | collective-permute-start | bytes 110600 | tf_op jit(solution)/shard_map/ppermute | solution.py:319
  14.7 1.5 %shard_map.69 = (bf16[2,40,256]{2,1,0:T(8,128)(2,1)S(1)}, bf16[8,64,256]{2,1,0:T(8,128)(2,1)S(1)}, bf16[10,64,256]{2,1,0:T(8,128)(2,1)S(1)}) custom-call(s32[3]{0:T(128)S(1)} %pad_add_fusion.info, bf16[8,64,128]{2,1,0:T(8,128)(2,1)S(1)} %bitcast.39, bf16[64,128]{1,0:T(8,128)(2,1)S(1)} %get-tuple-element.35.above_ref, ...), custom_call_target="tpu_custom_call" | custom-call | flops 150994944 | bytes 1122304 | tf_op jit(solution)/shard_map/pallas_call | solution.py:31
  16.3 3.0 %collective-permute-start.5 = (bf16[2,40,256]{2,1,0:T(8,128)(2,1)S(1)}, bf16[2,40,256]{2,1,0:T(8,128)(2,1)S(1)}, u32[]{:S(2)}, u32[]{:S(2)}) collective-permute-start(bf16[2,40,256]{2,1,0:T(8,128)(2,1)S(1)} %get-tuple-element.40.refs_0_), channel_id=1, source_target_pairs={{0,8},{4,12},{8,0},{12,4},{1,9},{5,13},{9,1},{13,5},{2,10},{6,14},... | collective-permute-start | bytes 122888 | tf_op jit(solution)/shard_map/ppermute | solution.py:327
  19.3 1.3 %collective-permute-start.6 = (bf16[2,40,256]{2,1,0:T(8,128)(2,1)S(1)}, bf16[2,40,256]{2,1,0:T(8,128)(2,1)S(1)}, u32[]{:S(2)}, u32[]{:S(2)}) collective-permute-start(bf16[2,40,256]{2,1,0:T(8,128)(2,1)S(1)} %get-tuple-element.40.refs_0_), channel_id=1, source_target_pairs={{0,12},{4,8},{8,4},{12,0},{1,13},{5,9},{9,5},{13,1},{2,14},{6,10},... | collective-permute-start | bytes 122888 | tf_op jit(solution)/shard_map/ppermute | solution.py:327
  20.7 1.1 %collective-permute-done.5.refs_2_ = bf16[2,40,256]{2,1,0:T(8,128)(2,1)S(1)} collective-permute-done((bf16[2,40,256]{2,1,0:T(8,128)(2,1)S(1)}, bf16[2,40,256]{2,1,0:T(8,128)(2,1)S(1)}, u32[]{:S(2)}, u32[]{:S(2)}) %collective-permute-start.5) | collective-permute-done | bytes 40992 | tf_op jit(solution)/shard_map/ppermute | solution.py:327
  21.8 3.3 %collective-permute-done.6.refs_3_ = bf16[2,40,256]{2,1,0:T(8,128)(2,1)S(1)} collective-permute-done((bf16[2,40,256]{2,1,0:T(8,128)(2,1)S(1)}, bf16[2,40,256]{2,1,0:T(8,128)(2,1)S(1)}, u32[]{:S(2)}, u32[]{:S(2)}) %collective-permute-start.6) | collective-permute-done | bytes 40992 | tf_op jit(solution)/shard_map/ppermute | solution.py:327
  25.1 1.9 %shard_map.70 = (bf16[72,256]{1,0:T(8,128)(2,1)S(1)}, bf16[72,256]{1,0:T(8,128)(2,1)S(1)}, bf16[72,256]{1,0:T(8,128)(2,1)S(1)}, bf16[72,256]{1,0:T(8,128)(2,1)S(...) custom-call(s32[3]{0:T(128)S(1)} %pad_add_fusion.info, bf16[8,48,128]{2,1,0:T(8,128)(2,1)S(1)} %fusion.6.og_ref, ...), custom_call_target="tpu_custom_call" | custom-call | flops 452984832 | bytes 1368064 | tf_op jit(solution)/shard_map/pallas_call | solution.py:31
  27.1 1.9 %collective-permute-start.8 = (bf16[72,256]{1,0:T(8,128)(2,1)S(1)}, bf16[72,256]{1,0:T(8,128)(2,1)S(1)}, u32[]{:S(2)}, u32[]{:S(2)}) collective-permute-start(bf16[72,256]{1,0:T(8,128)(2,1)S(1)} %get-tuple-element.43), channel_id=1, source_target_pairs={{0,8},{4,12},{8,0},{12,4},{1,9},{5,13},{9,1},{13,5},{2,10},{6,14},... | collective-permute-start | bytes 110600 | tf_op jit(solution)/shard_map/ppermute | solution.py:327
  29.0 2.5 %collective-permute-start.9 = (bf16[72,256]{1,0:T(8,128)(2,1)S(1)}, bf16[72,256]{1,0:T(8,128)(2,1)S(1)}, u32[]{:S(2)}, u32[]{:S(2)}) collective-permute-start(bf16[72,256]{1,0:T(8,128)(2,1)S(1)} %get-tuple-element.44), channel_id=1, source_target_pairs={{0,12},{4,8},{8,4},{12,0},{1,13},{5,9},{9,5},{13,1},{2,14},{6,10},... | collective-permute-start | bytes 110600 | tf_op jit(solution)/shard_map/ppermute | solution.py:327
  31.5 1.1 %shard_map.71 = (bf16[576,256]{1,0:T(8,128)(2,1)S(1)}, bf16[576,256]{1,0:T(8,128)(2,1)S(1)}) custom-call(s32[3]{0:T(128)S(1)} %pad_add_fusion.info, bf16[10,48,256]{2,1,0:T(8,128)(2,1)S(1)} %get-tuple-element.48.map_ref, bf16[10,48,128]{2,1,0:T(8,128)(2,1)S(1)} %get-tuple-element.49.grad_ref), custom_call_target="tpu_custom_call" | custom-call | flops 226492416 | bytes 958464 | tf_op jit(solution)/shard_map/pallas_call | solution.py:31
  32.6 2.2 %collective-permute-done.9.refs_3_ = bf16[72,256]{1,0:T(8,128)(2,1)S(1)} collective-permute-done((bf16[72,256]{1,0:T(8,128)(2,1)S(1)}, bf16[72,256]{1,0:T(8,128)(2,1)S(1)}, u32[]{:S(2)}, u32[]{:S(2)}) %collective-permute-start.9) | collective-permute-done | bytes 36896 | tf_op jit(solution)/shard_map/ppermute | solution.py:327
  34.8 1.7 %shard_map.72 = (bf16[8,64,256]{2,1,0:T(8,128)(2,1)S(1)}, bf16[64,256]{1,0:T(8,128)(2,1)S(1)}, bf16[64,256]{1,0:T(8,128)(2,1)S(1)}, bf16[656,256]{1,0:T(8,128)(2,1)S(1)}, bf16[656,256]{1,0:T(8,128)(2,1)S(1)}) custom-call(s32[3]{0:T(128)S(1)} %pad_add_fusion.info, bf16[72,256]{1,0:T(8,128)(2,1)S(1)} %get-tuple-element.41.refs_0_, ...), custom_call_target="tpu_custom_call" | custom-call | flops 150994944 | bytes 2506752 | tf_op jit(solution)/shard_map/pallas_call | solution.py:31
  36.6 1.6 %collective-permute-done.12.b_ref = bf16[656,256]{1,0:T(8,128)(2,1)S(1)} collective-permute-done((bf16[656,256]{1,0:T(8,128)(2,1)S(1)}, bf16[656,256]{1,0:T(8,128)(2,1)S(1)}, u32[]{:S(2)}, u32[]{:S(2)}) %collective-permute-start.12) | collective-permute-done | bytes 335904 | tf_op jit(solution)/shard_map/ppermute | solution.py:319
  38.3 1.2 %collective-permute-start.13 = (bf16[576,256]{1,0:T(8,128)(2,1)S(1)}, bf16[576,256]{1,0:T(8,128)(2,1)S(1)}, u32[]{:S(2)}, u32[]{:S(2)}) collective-permute-start(bf16[576,256]{1,0:T(8,128)(2,1)S(1)} %get-tuple-element.58.a_ref), channel_id=1, source_target_pairs={{0,2},{2,0},{1,3},{3,1},{4,6},{6,4},{5,7},{7,5},{8,10},{10,8},{9,1... | collective-permute-start | bytes 884744 | tf_op jit(solution)/shard_map/ppermute | solution.py:327
  39.5 2.0 %collective-permute-start.10 = (bf16[64,256]{1,0:T(8,128)(2,1)S(1)}, bf16[64,256]{1,0:T(8,128)(2,1)S(1)}, u32[]{:S(2)}, u32[]{:S(2)}) collective-permute-start(bf16[64,256]{1,0:T(8,128)(2,1)S(1)} %get-tuple-element.53), channel_id=1, source_target_pairs={{0,4},{4,0},{8,12},{12,8},{1,5},{5,1},{9,13},{13,9},{2,6},{6,2},{1... | collective-permute-start | bytes 98312 | tf_op jit(solution)/shard_map/ppermute | solution.py:319
  41.5 2.5 %collective-permute-start.11 = (bf16[64,256]{1,0:T(8,128)(2,1)S(1)}, bf16[64,256]{1,0:T(8,128)(2,1)S(1)}, u32[]{:S(2)}, u32[]{:S(2)}) collective-permute-start(bf16[64,256]{1,0:T(8,128)(2,1)S(1)} %get-tuple-element.54), channel_id=1, source_target_pairs={{0,12},{4,8},{8,4},{12,0},{1,13},{5,9},{9,5},{13,1},{2,14},{6,10},... | collective-permute-start | bytes 98312 | tf_op jit(solution)/shard_map/ppermute | solution.py:323
  45.0 2.4 %collective-permute-done.11.b_ref = bf16[64,256]{1,0:T(8,128)(2,1)S(1)} collective-permute-done((bf16[64,256]{1,0:T(8,128)(2,1)S(1)}, bf16[64,256]{1,0:T(8,128)(2,1)S(1)}, u32[]{:S(2)}, u32[]{:S(2)}) %collective-permute-start.11) | collective-permute-done | bytes 32800 | tf_op jit(solution)/shard_map/ppermute | solution.py:323
  47.3 1.7 %shard_map.73 = (bf16[64,8,128]{2,1,0:T(8,128)(2,1)}, f32[8,128]{1,0:T(8,128)S(1)}) custom-call(s32[3]{0:T(128)S(1)} %pad_add_fusion.info, bf16[8,64,256]{2,1,0:T(8,128)(2,1)S(1)} %get-tuple-element.52.g_ref, bf16[64,256]{1,0:T(8,128)(2,1)S(1)} %collective-permute-done.10.a_ref, bf16[64,256]{1,0:T(8,128)(2,1)S(1)} %collective-permute-done.11.b_ref, ...), custom_call_target="tpu_custom_call" | custom-call | flops 150994944 | bytes 536576 | tf_op jit(solution)/shard_map/pallas_call | solution.py:31
  50.0 3.1 %collective-permute-done.16.d_ref = bf16[80,256]{1,0:T(8,128)(2,1)S(1)} collective-permute-done((bf16[80,256]{1,0:T(8,128)(2,1)S(1)}, bf16[80,256]{1,0:T(8,128)(2,1)S(1)}, u32[]{:S(2)}, u32[]{:S(2)}) %collective-permute-start.16) | collective-permute-done | bytes 40992 | tf_op jit(solution)/shard_map/ppermute | solution.py:327
  53.3 1.6 %collective-permute-done.17.other_ref = bf16[656,256]{1,0:T(8,128)(2,1)S(1)} collective-permute-done((bf16[656,256]{1,0:T(8,128)(2,1)S(1)}, bf16[656,256]{1,0:T(8,128)(2,1)S(1)}, u32[]{:S(2)}, u32[]{:S(2)}) %collective-permute-start.17) | collective-permute-done | bytes 335904 | tf_op jit(solution)/shard_map/ppermute | solution.py:319
  54.9 1.8 %shard_map.78 = (f32[3,192,64]{2,1,0:T(8,128)}, f32[1152,256]{1,0:T(8,128)}) custom-call(s32[3]{0:T(128)S(1)} %pad_add_fusion.info, bf16[656,256]{1,0:T(8,128)(2,1)S(1)} %shard_map.77.mine_ref, bf16[656,256]{1,0:T(8,128)(2,1)S(1)} %collective-permute-done.17.other_ref), custom_call_target="tpu_custom_call" | custom-call | flops 1 | bytes 1998848 | tf_op jit(solution)/shard_map/pallas_call | solution.py:31
  (43 shorter events, 7.2 us)
Async XLA Ops:
  0.6 24.5 %copy-start.2 = (bf16[128,3,3,256]{3,0,2,1:T(8,128)(2,1)S(1)}, bf16[128,3,3,256]{3,0,2,1:T(8,128)(2,1)}, u32[]{:S(2)}) copy-start(bf16[128,3,3,256]{3,0,2,1:T(8,128)(2,1)} %param.6) | copy-start | bytes 1769476
  1.7 6.5 %collective-permute-start = (bf16[64,128]{1,0:T(8,128)(2,1)S(1)}, bf16[64,128]{1,0:T(8,128)(2,1)S(1)}, u32[]{:S(2)}, u32[]{:S(2)}) collective-permute-start(bf16[64,128]{1,0:T(8,128)(2,1)S(1)} %get-tuple-element.64), channel_id=1, source_target_pairs={{0,4},{4,0},{8,12},{12,8},{1,5},{5,1},{9,13},{13,9},{2,6},{6,2},{1... | collective-permute-start | bytes 49160 | tf_op jit(solution)/shard_map/ppermute | solution.py:319
  4.7 5.5 %collective-permute-start.1 = (bf16[64,128]{1,0:T(8,128)(2,1)S(1)}, bf16[64,128]{1,0:T(8,128)(2,1)S(1)}, u32[]{:S(2)}, u32[]{:S(2)}) collective-permute-start(bf16[64,128]{1,0:T(8,128)(2,1)S(1)} %get-tuple-element.63), channel_id=1, source_target_pairs={{0,12},{4,8},{8,4},{12,0},{1,13},{5,9},{9,5},{13,1},{2,14},{6,10},... | collective-permute-start | bytes 49160 | tf_op jit(solution)/shard_map/ppermute | solution.py:323
  10.9 3.8 %collective-permute-start.2 = (bf16[144,128]{1,0:T(8,128)(2,1)S(1)}, bf16[144,128]{1,0:T(8,128)(2,1)S(1)}, u32[]{:S(2)}, u32[]{:S(2)}) collective-permute-start(bf16[144,128]{1,0:T(8,128)(2,1)S(1)} %get-tuple-element.33), channel_id=1, source_target_pairs={{0,3},{1,2},{2,1},{3,0},{4,7},{5,6},{6,5},{7,4},{8,11},{9,10},{10,... | collective-permute-start | bytes 110600 | tf_op jit(solution)/shard_map/ppermute | solution.py:323
  11.0 3.7 %collective-permute-start.3 = (bf16[144,128]{1,0:T(8,128)(2,1)S(1)}, bf16[144,128]{1,0:T(8,128)(2,1)S(1)}, u32[]{:S(2)}, u32[]{:S(2)}) collective-permute-start(bf16[144,128]{1,0:T(8,128)(2,1)S(1)} %get-tuple-element.34), channel_id=1, source_target_pairs={{0,1},{1,0},{2,3},{3,2},{4,5},{5,4},{6,7},{7,6},{8,9},{9,8},{10,11... | collective-permute-start | bytes 110600 | tf_op jit(solution)/shard_map/ppermute | solution.py:319
  12.6 0.9 %copy-start = (bf16[64,3,3,64]{3,0,2,1:T(8,128)(2,1)S(1)}, bf16[64,3,3,64]{3,0,2,1:T(8,128)(2,1)}, u32[]{:S(2)}) copy-start(bf16[64,3,3,64]{3,0,2,1:T(8,128)(2,1)} %param.5) | copy-start | bytes 221188
  16.2 4.5 %collective-permute-start.4 = (bf16[2,40,256]{2,1,0:T(8,128)(2,1)S(1)}, bf16[2,40,256]{2,1,0:T(8,128)(2,1)S(1)}, u32[]{:S(2)}, u32[]{:S(2)}) collective-permute-start(bf16[2,40,256]{2,1,0:T(8,128)(2,1)S(1)} %get-tuple-element.40.refs_0_), channel_id=1, source_target_pairs={{0,4},{4,0},{8,12},{12,8},{1,5},{5,1},{9,13},{13,9},{2,6},{6,2},{1... | collective-permute-start | bytes 122888 | tf_op jit(solution)/shard_map/ppermute | solution.py:327
  16.3 5.6 %collective-permute-start.5 = (bf16[2,40,256]{2,1,0:T(8,128)(2,1)S(1)}, bf16[2,40,256]{2,1,0:T(8,128)(2,1)S(1)}, u32[]{:S(2)}, u32[]{:S(2)}) collective-permute-start(bf16[2,40,256]{2,1,0:T(8,128)(2,1)S(1)} %get-tuple-element.40.refs_0_), channel_id=1, source_target_pairs={{0,8},{4,12},{8,0},{12,4},{1,9},{5,13},{9,1},{13,5},{2,10},{6,14},... | collective-permute-start | bytes 122888 | tf_op jit(solution)/shard_map/ppermute | solution.py:327
  19.3 5.8 %collective-permute-start.6 = (bf16[2,40,256]{2,1,0:T(8,128)(2,1)S(1)}, bf16[2,40,256]{2,1,0:T(8,128)(2,1)S(1)}, u32[]{:S(2)}, u32[]{:S(2)}) collective-permute-start(bf16[2,40,256]{2,1,0:T(8,128)(2,1)S(1)} %get-tuple-element.40.refs_0_), channel_id=1, source_target_pairs={{0,12},{4,8},{8,4},{12,0},{1,13},{5,9},{9,5},{13,1},{2,14},{6,10},... | collective-permute-start | bytes 122888 | tf_op jit(solution)/shard_map/ppermute | solution.py:327
  27.0 5.6 %collective-permute-start.7 = (bf16[72,256]{1,0:T(8,128)(2,1)S(1)}, bf16[72,256]{1,0:T(8,128)(2,1)S(1)}, u32[]{:S(2)}, u32[]{:S(2)}) collective-permute-start(bf16[72,256]{1,0:T(8,128)(2,1)S(1)} %get-tuple-element.42), channel_id=1, source_target_pairs={{0,4},{4,0},{8,12},{12,8},{1,5},{5,1},{9,13},{13,9},{2,6},{6,2},{1... | collective-permute-start | bytes 110600 | tf_op jit(solution)/shard_map/ppermute | solution.py:327
  27.1 5.5 %collective-permute-start.8 = (bf16[72,256]{1,0:T(8,128)(2,1)S(1)}, bf16[72,256]{1,0:T(8,128)(2,1)S(1)}, u32[]{:S(2)}, u32[]{:S(2)}) collective-permute-start(bf16[72,256]{1,0:T(8,128)(2,1)S(1)} %get-tuple-element.43), channel_id=1, source_target_pairs={{0,8},{4,12},{8,0},{12,4},{1,9},{5,13},{9,1},{13,5},{2,10},{6,14},... | collective-permute-start | bytes 110600 | tf_op jit(solution)/shard_map/ppermute | solution.py:327
  29.0 5.8 %collective-permute-start.9 = (bf16[72,256]{1,0:T(8,128)(2,1)S(1)}, bf16[72,256]{1,0:T(8,128)(2,1)S(1)}, u32[]{:S(2)}, u32[]{:S(2)}) collective-permute-start(bf16[72,256]{1,0:T(8,128)(2,1)S(1)} %get-tuple-element.44), channel_id=1, source_target_pairs={{0,12},{4,8},{8,4},{12,0},{1,13},{5,9},{9,5},{13,1},{2,14},{6,10},... | collective-permute-start | bytes 110600 | tf_op jit(solution)/shard_map/ppermute | solution.py:327
  32.6 12.0 %copy-start.1 = (bf16[64,3,3,64]{3,0,2,1:T(8,128)(2,1)S(1)}, bf16[64,3,3,64]{3,0,2,1:T(8,128)(2,1)}, u32[]{:S(2)}) copy-start(bf16[64,3,3,64]{3,0,2,1:T(8,128)(2,1)} %param.5) | copy-start | bytes 221188
  36.5 1.7 %collective-permute-start.12 = (bf16[656,256]{1,0:T(8,128)(2,1)S(1)}, bf16[656,256]{1,0:T(8,128)(2,1)S(1)}, u32[]{:S(2)}, u32[]{:S(2)}) collective-permute-start(bf16[656,256]{1,0:T(8,128)(2,1)S(1)} %get-tuple-element.57), channel_id=1, source_target_pairs={{0,1},{1,0},{2,3},{3,2},{4,5},{5,4},{6,7},{7,6},{8,9},{9,8},{10,11... | collective-permute-start | bytes 1007624 | tf_op jit(solution)/shard_map/ppermute | solution.py:319
  38.3 14.9 %collective-permute-start.13 = (bf16[576,256]{1,0:T(8,128)(2,1)S(1)}, bf16[576,256]{1,0:T(8,128)(2,1)S(1)}, u32[]{:S(2)}, u32[]{:S(2)}) collective-permute-start(bf16[576,256]{1,0:T(8,128)(2,1)S(1)} %get-tuple-element.58.a_ref), channel_id=1, source_target_pairs={{0,2},{2,0},{1,3},{3,1},{4,6},{6,4},{5,7},{7,5},{8,10},{10,8},{9,1... | collective-permute-start | bytes 884744 | tf_op jit(solution)/shard_map/ppermute | solution.py:327
  39.5 4.5 %collective-permute-start.14 = (bf16[80,256]{1,0:T(8,128)(2,1)S(1)}, bf16[80,256]{1,0:T(8,128)(2,1)S(1)}, u32[]{:S(2)}, u32[]{:S(2)}) collective-permute-start(bf16[80,256]{1,0:T(8,128)(2,1)S(1)} %get-tuple-element.59.a_ref), channel_id=1, source_target_pairs={{0,4},{4,0},{8,12},{12,8},{1,5},{5,1},{9,13},{13,9},{2,6},{6,2},{1... | collective-permute-start | bytes 122888 | tf_op jit(solution)/shard_map/ppermute | solution.py:327
  39.5 5.4 %collective-permute-start.10 = (bf16[64,256]{1,0:T(8,128)(2,1)S(1)}, bf16[64,256]{1,0:T(8,128)(2,1)S(1)}, u32[]{:S(2)}, u32[]{:S(2)}) collective-permute-start(bf16[64,256]{1,0:T(8,128)(2,1)S(1)} %get-tuple-element.53), channel_id=1, source_target_pairs={{0,4},{4,0},{8,12},{12,8},{1,5},{5,1},{9,13},{13,9},{2,6},{6,2},{1... | collective-permute-start | bytes 98312 | tf_op jit(solution)/shard_map/ppermute | solution.py:319
  41.5 5.8 %collective-permute-start.11 = (bf16[64,256]{1,0:T(8,128)(2,1)S(1)}, bf16[64,256]{1,0:T(8,128)(2,1)S(1)}, u32[]{:S(2)}, u32[]{:S(2)}) collective-permute-start(bf16[64,256]{1,0:T(8,128)(2,1)S(1)} %get-tuple-element.54), channel_id=1, source_target_pairs={{0,12},{4,8},{8,4},{12,0},{1,13},{5,9},{9,5},{13,1},{2,14},{6,10},... | collective-permute-start | bytes 98312 | tf_op jit(solution)/shard_map/ppermute | solution.py:323
  44.0 5.0 %collective-permute-start.15 = (bf16[80,256]{1,0:T(8,128)(2,1)S(1)}, bf16[80,256]{1,0:T(8,128)(2,1)S(1)}, u32[]{:S(2)}, u32[]{:S(2)}) collective-permute-start(bf16[80,256]{1,0:T(8,128)(2,1)S(1)} %shard_map.75.a_ref), channel_id=1, source_target_pairs={{0,8},{4,12},{8,0},{12,4},{1,9},{5,13},{9,1},{13,5},{2,10},{6,14},... | collective-permute-start | bytes 122888 | tf_op jit(solution)/shard_map/ppermute | solution.py:327
  49.1 4.1 %collective-permute-start.16 = (bf16[80,256]{1,0:T(8,128)(2,1)S(1)}, bf16[80,256]{1,0:T(8,128)(2,1)S(1)}, u32[]{:S(2)}, u32[]{:S(2)}) collective-permute-start(bf16[80,256]{1,0:T(8,128)(2,1)S(1)} %shard_map.76.c_ref), channel_id=1, source_target_pairs={{0,2},{2,0},{1,3},{3,1},{4,6},{6,4},{5,7},{7,5},{8,10},{10,8},{9,1... | collective-permute-start | bytes 122888 | tf_op jit(solution)/shard_map/ppermute | solution.py:327
  53.2 1.7 %collective-permute-start.17 = (bf16[656,256]{1,0:T(8,128)(2,1)S(1)}, bf16[656,256]{1,0:T(8,128)(2,1)S(1)}, u32[]{:S(2)}, u32[]{:S(2)}) collective-permute-start(bf16[656,256]{1,0:T(8,128)(2,1)S(1)} %shard_map.77.mine_ref), channel_id=1, source_target_pairs={{0,1},{1,0},{2,3},{3,2},{4,5},{5,4},{6,7},{7,6},{8,9},{9,8},{10,11... | collective-permute-start | bytes 1007624 | tf_op jit(solution)/shard_map/ppermute | solution.py:319

commit v7 on v6

--- a/solution.py
+++ b/solution.py
@@ -48,7 +48,7 @@
 
 
 def sigmoid(values):
-    return 1.0 / (1.0 + jnp.exp(-values))
+    return 0.5 + 0.5 * jnp.tanh(0.5 * values)
 
 
 def slope_of(values, sig):
@@ -91,25 +91,35 @@
     return jnp.where(even, b, a).astype(BF16), jnp.where(even, a, b).astype(BF16)
 
 
-def pack_sides(
-    info, x_ref, up_a_ref, up_b_ref, head_ref, tail_ref, a_ref, b_ref, above_ref, below_ref, *, bands
-):
+def pack_row(row, r, slot, head, tail):
+    turned = roll(row.astype(F32), 16 * r, 1)
+    return jnp.where(slot == r, turned, head), jnp.where(slot == (r - 1) % 8, turned, tail)
+
+
+def pack_own(info, x_ref, head_ref, tail_ref, a_ref, b_ref):
+    even = (info[0] & 1) == 0
+    slot = lax.broadcasted_iota(jnp.int32, (64, 128), 1) >> 4
+    head = tail = jnp.zeros((64, 128), F32)
+    for r in range(x_ref.shape[0]):
+        head, tail = pack_row(x_ref[r], r, slot, head, tail)
+    a_ref[:64] = jnp.where(even, tail, head).astype(BF16)
+    b_ref[:64] = jnp.where(even, head, tail).astype(BF16)
+    first, last = head_ref[...].astype(F32), tail_ref[...].astype(F32)
+    a_ref[64:] = jnp.where(even, last, first).astype(BF16)
+    b_ref[64:] = jnp.where(even, first, last).astype(BF16)
+
+
+def pack_borders(info, up_a_ref, up_b_ref, own_a_ref, own_b_ref, a_ref, b_ref, above_ref, below_ref, *, bands):
     even = (info[0] & 1) == 0
     above_ref[...], below_ref[...] = beside(up_a_ref, up_b_ref, info[2], bands)
-    rows = [above_ref[...]] + [x_ref[h] for h in range(x_ref.shape[0])] + [below_ref[...]]
     slot = lax.broadcasted_iota(jnp.int32, (64, 128), 1) >> 4
-    blank = jnp.zeros((64, 128), F32)
-    heads, tails = [blank, blank], [blank, blank]
-    for r, row in enumerate(rows):
-        turned = roll(row.astype(F32), 16 * (r % 8), 1)
-        heads[r // 8] = jnp.where(slot == r % 8, turned, heads[r // 8])
-        tails[r // 8] = jnp.where(slot == (r - 1) % 8, turned, tails[r // 8])
-    for t in range(2):
-        a_ref[64 * t : 64 * t + 64] = jnp.where(even, tails[t], heads[t]).astype(BF16)
-        b_ref[64 * t : 64 * t + 64] = jnp.where(even, heads[t], tails[t]).astype(BF16)
-    first, last = head_ref[...].astype(F32), tail_ref[...].astype(F32)
-    a_ref[128:] = jnp.where(even, last, first).astype(BF16)
-    b_ref[128:] = jnp.where(even, first, last).astype(BF16)
+    head = tail = jnp.zeros((64, 128), F32)
+    for r, ref in enumerate((above_ref, below_ref)):
+        head, tail = pack_row(ref[...], r, slot, head, tail)
+    a_ref[:64] = jnp.where(even, tail, head).astype(BF16)
+    b_ref[:64] = jnp.where(even, head, tail).astype(BF16)
+    a_ref[64:] = own_a_ref[...]
+    b_ref[64:] = own_b_ref[...]
 
 
 def layer_one(
@@ -135,9 +145,10 @@
     sides = a_ref[:128].astype(F32), jnp.where(inner, b_ref[:128].astype(F32), 0.0)
     from_a = ((slot ^ strip) & 1) == 0
     packed = jnp.where(from_a, *sides), jnp.where(from_a, *sides[::-1])
-    for r in range(band_rows + 2):
-        tile = 64 * (r // 8)
-        wide_ref[r, :, 128:] = roll(packed[r % 2][tile : tile + 64], -16 * (r % 8), 1).astype(BF16)
+    for r in range(band_rows):
+        wide_ref[1 + r, :, 128:] = roll(packed[r % 2][64:], -16 * r, 1).astype(BF16)
+    for r, place in enumerate((0, band_rows + 1)):
+        wide_ref[place, :, 128:] = roll(packed[r][:64], -16 * r, 1).astype(BF16)
     wide_ref[0, :, :128] = above_ref[...]
     wide_ref[1 : band_rows + 1, :, :128] = x_ref[...]
     wide_ref[band_rows + 1, :, :128] = below_ref[...]
@@ -182,21 +193,19 @@
     for k in range(bands):
         for t in range(2):
             map_ref[1 + 2 * (band ^ k) + t] = jnp.concatenate([pieces[k][t], blank], 0)
-    y = None
-    for i in range(3):
-        part = dot(map_ref[i : i + rows].reshape(count, 256), w_ref[i], (1, 1))
-        y = part if y is None else y + part
+    near = jnp.concatenate([map_ref[i : i + rows].reshape(count, 256) for i in range(3)], 1)
+    y = dot(near, jnp.concatenate([w_ref[i] for i in range(3)], 1), (1, 1))
     pre = roll(y[:, :filters], 1, 0) + y[:, filters : 2 * filters] + roll(y[:, 2 * filters :], -1, 0)
     grad = og_ref[...].reshape(count, filters).astype(F32) * slope_of(pre, sigmoid(pre))
     grad = grad.astype(BF16)
     grad_ref[0] = jnp.zeros((PITCH, filters), BF16)
     grad_ref[rows + 1] = jnp.zeros((PITCH, filters), BF16)
     grad_ref[1 : rows + 1] = grad.reshape(rows, PITCH, filters)
-    z = None
-    for i in range(3):
-        weights = jnp.concatenate([w_ref[i, j * filters : (j + 1) * filters] for j in range(3)], 1)
-        part = dot(grad_ref[2 - i : 2 - i + rows].reshape(count, filters), weights, (1, 0))
-        z = part if z is None else z + part
+    near = jnp.concatenate([grad_ref[2 - i : 2 - i + rows].reshape(count, filters) for i in range(3)], 1)
+    weights = [
+        jnp.concatenate([w_ref[i, j * filters : (j + 1) * filters] for j in range(3)], 1) for i in range(3)
+    ]
+    z = dot(near, jnp.concatenate(weights, 0), (1, 0))
     spread = roll(z[:, :256], -1 - REACH, 0) + roll(z[:, 256:512], -REACH, 0) + roll(z[:, 512:], 1 - REACH, 0)
     spread = spread.reshape(rows, PITCH, 256)
     odd = (lax.broadcasted_iota(jnp.int32, (8, 256), 1) & 1) == 1
@@ -237,7 +246,7 @@
     one_ref[...] = total[half:]
 
 
-def add_joined(a_ref, b_ref, c_ref, d_ref, out_ref):
+def add_joined(a_ref, b_ref, c_ref, d_ref, _, out_ref):
     half = a_ref.shape[0]
     out_ref[:half] = (a_ref[...].astype(F32) + b_ref[...].astype(F32)).astype(BF16)
     out_ref[half:] = (c_ref[...].astype(F32) + d_ref[...].astype(F32)).astype(BF16)
@@ -256,7 +265,7 @@
     blocks = [summed[:32], ends, blank, summed[40:], roll(ends, -1, 0), blank]
     ordered = dot(jnp.concatenate(blocks, 0).astype(BF16), order_ref[...], (1, 1)).astype(BF16)
     pool = pool_ref[...]
-    acc = None
+    cats = []
     own = lax.broadcasted_iota(jnp.int32, (64, 256), 1) < 128
     for u in range(2):
         block = ordered[u * PITCH : (u + 1) * PITCH]
@@ -266,9 +275,9 @@
             g = (up[64 * (i // 2) : 64 * (i // 2) + 64] * slope_ref[h].astype(F32)).astype(BF16)
             g_ref[h] = g
             mine = jnp.where(own, g.astype(F32), 0.0)
-            cat = jnp.concatenate([roll(mine, -1, 1), mine, roll(mine, 1, 1)], 0).astype(BF16)
-            part = dot(cat, wide_ref[h : h + 3].reshape(192, 256), (1, 1))
-            acc = part if acc is None else acc + part
+            cats.append(jnp.concatenate([roll(mine, -1, 1), mine, roll(mine, 1, 1)], 0).astype(BF16))
+    around = jnp.concatenate([wide_ref[h : h + 3].reshape(192, 256) for h in range(8)], 1)
+    acc = dot(jnp.concatenate(cats, 1), around, (1, 1))
     even = (info[2] & 1) == 0
     first, last = g_ref[0].astype(F32), g_ref[7].astype(F32)
     a_ref[...] = jnp.where(even, last, first).astype(BF16)
@@ -374,12 +383,14 @@
         [at_place, taps_one],
         10**8,
     )
-    up_a, up_b = even_swap(to_a, "row", bands), odd_swap(to_b, "row", bands)
     head, tail = head.reshape(-1, 128), tail.reshape(-1, 128)
+    own_a, own_b = whole_call(
+        pack_own, [shaped((channels + head.shape[0], 128))] * 2, [at_place, x, head, tail], 10**8
+    )
     to_a, to_b, above, below = whole_call(
-        functools.partial(pack_sides, bands=bands),
+        functools.partial(pack_borders, bands=bands),
         [shaped((2 * channels + head.shape[0], 128))] * 2 + [shaped((channels, strip_cols))] * 2,
-        [at_place, x, up_a, up_b, head, tail],
+        [at_place, even_swap(to_a, "row", bands), odd_swap(to_b, "row", bands), own_a, own_b],
         1,
     )
     side_a, side_b = even_swap(to_a, COLS, strips), odd_swap(to_b, COLS, strips)
@@ -447,9 +458,14 @@
         [at_place, g, even_swap(up_a, "row", bands), odd_swap(up_b, "row", bands), back_one],
         2 * band_rows * 192 * 192 * 256,
     )
-    one, one_more = sum_but_last(added(one, one_more, done), "col", columns)
+    one, one_more = sum_but_last(added(one, one_more), "col", columns)
     (mine,) = whole_call(
-        add_joined, [shaped((half + TAIL, 256))], [two, two_more, one, one_more], 0, scalars=0
+        add_joined,
+        [shaped((half + TAIL, 256))],
+        [two, two_more, one, one_more, done],
+        0,
+        scalars=0,
+        after=1,
     )
     grad_one, grad_two = whole_call(
         functools.partial(

time: 56.9 us -> 57.1 us (level)
  waiting for transfers between devices: 17.9 us -> 18.8 us
  starting transfers between devices: 23.5 us -> 22.9 us
    ppermute x10, waiting for transfers between devices: 9.65 us -> 11.3 us  [xor_swap(): return lax.ppermute(values, axis, [(n, n ^ k) for n in range(count)])]
    ppermute x3, starting transfers between devices: 5.01 us -> 3.9 us  [odd_swap(): lax.ppermute(values, axis, [(n, (n - 1 if n % 2 == 0 else n + 1) % count)...]
    ppermute x3, waiting for transfers between devices: 4.99 us -> 4.25 us  [odd_swap(): lax.ppermute(values, axis, [(n, (n - 1 if n % 2 == 0 else n + 1) % count)...]
    pallas_call x12 -> x13, Pallas kernels: 11.2 us -> 11.1 us  [whole_call(): pl.pallas_call(body, out_shape=outs, in_specs=specs, out_specs=[pl.BlockS...]
  transfers between devices with their start and end apart: 18 -> 18, of which waited for: 9 -> 10; matrix products, arithmetic and copies ran while one was open for 2% -> 2% of each run, Pallas kernels for 6% -> 7%
where the time goes in v7:
time: 57.1 us; the launch traced here: 56.9 us
  starting transfers between devices  22.9 us (40%)
  waiting for transfers between devices  18.8 us (33%)
  Pallas kernels  11.1 us (19%)
  local copies, waits for them, and re-layouts  3.12 us (5%)
  between operations  0.87 us (2%)
    ppermute x10, starting transfers between devices, xor_swap(): return lax.ppermute(values, axis, [(n, n ^ k) for n in range(count)])  12.1 us
    ppermute x10, waiting for transfers between devices, xor_swap(): return lax.ppermute(values, axis, [(n, n ^ k) for n in range(count)])  11.3 us
    pallas_call x13, Pallas kernels, whole_call(): pl.pallas_call(body, out_shape=outs, in_specs=specs, out_specs=[pl.BlockS...  11.1 us
    ppermute x5, starting transfers between devices, even_swap(): return lax.ppermute(values, axis, [(n, n ^ 1) for n in range(count)])  6.85 us
    ppermute x3, waiting for transfers between devices, odd_swap(): lax.ppermute(values, axis, [(n, (n - 1 if n % 2 == 0 else n + 1) % count)...  4.25 us
    ppermute x3, starting transfers between devices, odd_swap(): lax.ppermute(values, axis, [(n, (n - 1 if n % 2 == 0 else n + 1) % count)...  3.9 us
    ppermute x5, waiting for transfers between devices, even_swap(): return lax.ppermute(values, axis, [(n, n ^ 1) for n in range(count)])  3.26 us
    unnamed x8, local copies, waits for them, and re-layouts  2.75 us
  transfers between devices with their start and end apart: 18, of which 10 were waited for; matrix products, arithmetic and copies ran while one was open for 2% of the time, Pallas kernels for 7%

profile of v7, /device:TPU:0, one launch (start us, length us, event | category | flops | bytes accessed | tf_op | source)
XLA Modules:
  0.0 56.9 jit_solution(6017934303913873660)
XLA Ops:
  1.7 3.1 %collective-permute-start = (bf16[64,128]{1,0:T(8,128)(2,1)S(1)}, bf16[64,128]{1,0:T(8,128)(2,1)S(1)}, u32[]{:S(2)}, u32[]{:S(2)}) collective-permute-start(bf16[64,128]{1,0:T(8,128)(2,1)S(1)} %get-tuple-element.68), channel_id=1, source_target_pairs={{0,4},{4,0},{8,12},{12,8},{1,5},{5,1},{9,13},{13,9},{2,6},{6,2},{1... | collective-permute-start | bytes 49160 | tf_op jit(solution)/shard_map/ppermute | solution.py:328
  4.7 2.5 %collective-permute-start.1 = (bf16[64,128]{1,0:T(8,128)(2,1)S(1)}, bf16[64,128]{1,0:T(8,128)(2,1)S(1)}, u32[]{:S(2)}, u32[]{:S(2)}) collective-permute-start(bf16[64,128]{1,0:T(8,128)(2,1)S(1)} %get-tuple-element.67), channel_id=1, source_target_pairs={{0,12},{4,8},{8,4},{12,0},{1,13},{5,9},{9,5},{13,1},{2,14},{6,10},... | collective-permute-start | bytes 49160 | tf_op jit(solution)/shard_map/ppermute | solution.py:332
  8.8 1.4 %collective-permute-done.1.up_b_ref = bf16[64,128]{1,0:T(8,128)(2,1)S(1)} collective-permute-done((bf16[64,128]{1,0:T(8,128)(2,1)S(1)}, bf16[64,128]{1,0:T(8,128)(2,1)S(1)}, u32[]{:S(2)}, u32[]{:S(2)}) %collective-permute-start.1) | collective-permute-done | bytes 16416 | tf_op jit(solution)/shard_map/ppermute | solution.py:332
  11.0 1.6 %collective-permute-start.3 = (bf16[144,128]{1,0:T(8,128)(2,1)S(1)}, bf16[144,128]{1,0:T(8,128)(2,1)S(1)}, u32[]{:S(2)}, u32[]{:S(2)}) collective-permute-start(bf16[144,128]{1,0:T(8,128)(2,1)S(1)} %get-tuple-element.38), channel_id=1, source_target_pairs={{0,1},{1,0},{2,3},{3,2},{4,5},{5,4},{6,7},{7,6},{8,9},{9,8},{10,11... | collective-permute-start | bytes 110600 | tf_op jit(solution)/shard_map/ppermute | solution.py:328
  14.7 1.4 %shard_map.70 = (bf16[2,40,256]{2,1,0:T(8,128)(2,1)S(1)}, bf16[8,64,256]{2,1,0:T(8,128)(2,1)S(1)}, bf16[10,64,256]{2,1,0:T(8,128)(2,1)S(1)}) custom-call(s32[3]{0:T(128)S(1)} %pad_add_fusion.info, bf16[8,64,128]{2,1,0:T(8,128)(2,1)S(1)} %bitcast.39, bf16[64,128]{1,0:T(8,128)(2,1)S(1)} %get-tuple-element.39.above_ref, ...), custom_call_target="tpu_custom_call" | custom-call | flops 150994944 | bytes 1122304 | tf_op jit(solution)/shard_map/pallas_call | solution.py:31
  16.2 3.0 %collective-permute-start.5 = (bf16[2,40,256]{2,1,0:T(8,128)(2,1)S(1)}, bf16[2,40,256]{2,1,0:T(8,128)(2,1)S(1)}, u32[]{:S(2)}, u32[]{:S(2)}) collective-permute-start(bf16[2,40,256]{2,1,0:T(8,128)(2,1)S(1)} %get-tuple-element.44.refs_0_), channel_id=1, source_target_pairs={{0,8},{4,12},{8,0},{12,4},{1,9},{5,13},{9,1},{13,5},{2,10},{6,14},... | collective-permute-start | bytes 122888 | tf_op jit(solution)/shard_map/ppermute | solution.py:336
  19.2 1.3 %collective-permute-start.6 = (bf16[2,40,256]{2,1,0:T(8,128)(2,1)S(1)}, bf16[2,40,256]{2,1,0:T(8,128)(2,1)S(1)}, u32[]{:S(2)}, u32[]{:S(2)}) collective-permute-start(bf16[2,40,256]{2,1,0:T(8,128)(2,1)S(1)} %get-tuple-element.44.refs_0_), channel_id=1, source_target_pairs={{0,12},{4,8},{8,4},{12,0},{1,13},{5,9},{9,5},{13,1},{2,14},{6,10},... | collective-permute-start | bytes 122888 | tf_op jit(solution)/shard_map/ppermute | solution.py:336
  20.7 1.1 %collective-permute-done.5.refs_2_ = bf16[2,40,256]{2,1,0:T(8,128)(2,1)S(1)} collective-permute-done((bf16[2,40,256]{2,1,0:T(8,128)(2,1)S(1)}, bf16[2,40,256]{2,1,0:T(8,128)(2,1)S(1)}, u32[]{:S(2)}, u32[]{:S(2)}) %collective-permute-start.5) | collective-permute-done | bytes 40992 | tf_op jit(solution)/shard_map/ppermute | solution.py:336
  21.8 3.3 %collective-permute-done.6.refs_3_ = bf16[2,40,256]{2,1,0:T(8,128)(2,1)S(1)} collective-permute-done((bf16[2,40,256]{2,1,0:T(8,128)(2,1)S(1)}, bf16[2,40,256]{2,1,0:T(8,128)(2,1)S(1)}, u32[]{:S(2)}, u32[]{:S(2)}) %collective-permute-start.6) | collective-permute-done | bytes 40992 | tf_op jit(solution)/shard_map/ppermute | solution.py:336
  25.0 1.5 %shard_map.71 = (bf16[72,256]{1,0:T(8,128)(2,1)S(1)}, bf16[72,256]{1,0:T(8,128)(2,1)S(1)}, bf16[72,256]{1,0:T(8,128)(2,1)S(1)}, bf16[72,256]{1,0:T(8,128)(2,1)S(...) custom-call(s32[3]{0:T(128)S(1)} %pad_add_fusion.info, bf16[8,48,128]{2,1,0:T(8,128)(2,1)S(1)} %fusion.6.og_ref, ...), custom_call_target="tpu_custom_call" | custom-call | flops 452984832 | bytes 1368064 | tf_op jit(solution)/shard_map/pallas_call | solution.py:31
  26.7 1.9 %collective-permute-start.8 = (bf16[72,256]{1,0:T(8,128)(2,1)S(1)}, bf16[72,256]{1,0:T(8,128)(2,1)S(1)}, u32[]{:S(2)}, u32[]{:S(2)}) collective-permute-start(bf16[72,256]{1,0:T(8,128)(2,1)S(1)} %get-tuple-element.47), channel_id=1, source_target_pairs={{0,8},{4,12},{8,0},{12,4},{1,9},{5,13},{9,1},{13,5},{2,10},{6,14},... | collective-permute-start | bytes 110600 | tf_op jit(solution)/shard_map/ppermute | solution.py:336
  28.6 2.5 %collective-permute-start.9 = (bf16[72,256]{1,0:T(8,128)(2,1)S(1)}, bf16[72,256]{1,0:T(8,128)(2,1)S(1)}, u32[]{:S(2)}, u32[]{:S(2)}) collective-permute-start(bf16[72,256]{1,0:T(8,128)(2,1)S(1)} %get-tuple-element.48), channel_id=1, source_target_pairs={{0,12},{4,8},{8,4},{12,0},{1,13},{5,9},{9,5},{13,1},{2,14},{6,10},... | collective-permute-start | bytes 110600 | tf_op jit(solution)/shard_map/ppermute | solution.py:336
  31.0 1.1 %shard_map.72 = (bf16[576,256]{1,0:T(8,128)(2,1)S(1)}, bf16[576,256]{1,0:T(8,128)(2,1)S(1)}) custom-call(s32[3]{0:T(128)S(1)} %pad_add_fusion.info, bf16[10,48,256]{2,1,0:T(8,128)(2,1)S(1)} %get-tuple-element.52.map_ref, bf16[10,48,128]{2,1,0:T(8,128)(2,1)S(1)} %get-tuple-element.53.grad_ref), custom_call_target="tpu_custom_call" | custom-call | flops 226492416 | bytes 958464 | tf_op jit(solution)/shard_map/pallas_call | solution.py:31
  32.2 2.2 %collective-permute-done.9.refs_3_ = bf16[72,256]{1,0:T(8,128)(2,1)S(1)} collective-permute-done((bf16[72,256]{1,0:T(8,128)(2,1)S(1)}, bf16[72,256]{1,0:T(8,128)(2,1)S(1)}, u32[]{:S(2)}, u32[]{:S(2)}) %collective-permute-start.9) | collective-permute-done | bytes 36896 | tf_op jit(solution)/shard_map/ppermute | solution.py:336
  34.3 1.4 %shard_map.73 = (bf16[8,64,256]{2,1,0:T(8,128)(2,1)S(1)}, bf16[64,256]{1,0:T(8,128)(2,1)S(1)}, bf16[64,256]{1,0:T(8,128)(2,1)S(1)}, bf16[656,256]{1,0:T(8,128)(2,1)S(1)}, bf16[656,256]{1,0:T(8,128)(2,1)S(1)}) custom-call(s32[3]{0:T(128)S(1)} %pad_add_fusion.info, bf16[72,256]{1,0:T(8,128)(2,1)S(1)} %get-tuple-element.45.refs_0_, ...), custom_call_target="tpu_custom_call" | custom-call | flops 150994944 | bytes 2506752 | tf_op jit(solution)/shard_map/pallas_call | solution.py:31
  35.8 1.6 %collective-permute-done.12.b_ref = bf16[656,256]{1,0:T(8,128)(2,1)S(1)} collective-permute-done((bf16[656,256]{1,0:T(8,128)(2,1)S(1)}, bf16[656,256]{1,0:T(8,128)(2,1)S(1)}, u32[]{:S(2)}, u32[]{:S(2)}) %collective-permute-start.12) | collective-permute-done | bytes 335904 | tf_op jit(solution)/shard_map/ppermute | solution.py:328
  37.5 1.2 %collective-permute-start.13 = (bf16[576,256]{1,0:T(8,128)(2,1)S(1)}, bf16[576,256]{1,0:T(8,128)(2,1)S(1)}, u32[]{:S(2)}, u32[]{:S(2)}) collective-permute-start(bf16[576,256]{1,0:T(8,128)(2,1)S(1)} %get-tuple-element.62.a_ref), channel_id=1, source_target_pairs={{0,2},{2,0},{1,3},{3,1},{4,6},{6,4},{5,7},{7,5},{8,10},{10,8},{9,1... | collective-permute-start | bytes 884744 | tf_op jit(solution)/shard_map/ppermute | solution.py:336
  38.7 4.0 %collective-permute-done.14.b_ref = bf16[80,256]{1,0:T(8,128)(2,1)S(1)} collective-permute-done((bf16[80,256]{1,0:T(8,128)(2,1)S(1)}, bf16[80,256]{1,0:T(8,128)(2,1)S(1)}, u32[]{:S(2)}, u32[]{:S(2)}) %collective-permute-start.14) | collective-permute-done | bytes 40992 | tf_op jit(solution)/shard_map/ppermute | solution.py:336
  43.8 2.0 %collective-permute-start.10 = (bf16[64,256]{1,0:T(8,128)(2,1)S(1)}, bf16[64,256]{1,0:T(8,128)(2,1)S(1)}, u32[]{:S(2)}, u32[]{:S(2)}) collective-permute-start(bf16[64,256]{1,0:T(8,128)(2,1)S(1)} %get-tuple-element.57), channel_id=1, source_target_pairs={{0,4},{4,0},{8,12},{12,8},{1,5},{5,1},{9,13},{13,9},{2,6},{6,2},{1... | collective-permute-start | bytes 98312 | tf_op jit(solution)/shard_map/ppermute | solution.py:328
  45.9 1.4 %collective-permute-start.11 = (bf16[64,256]{1,0:T(8,128)(2,1)S(1)}, bf16[64,256]{1,0:T(8,128)(2,1)S(1)}, u32[]{:S(2)}, u32[]{:S(2)}) collective-permute-start(bf16[64,256]{1,0:T(8,128)(2,1)S(1)} %get-tuple-element.58), channel_id=1, source_target_pairs={{0,12},{4,8},{8,4},{12,0},{1,13},{5,9},{9,5},{13,1},{2,14},{6,10},... | collective-permute-start | bytes 98312 | tf_op jit(solution)/shard_map/ppermute | solution.py:332
  49.3 2.3 %collective-permute-done.11.b_ref = bf16[64,256]{1,0:T(8,128)(2,1)S(1)} collective-permute-done((bf16[64,256]{1,0:T(8,128)(2,1)S(1)}, bf16[64,256]{1,0:T(8,128)(2,1)S(1)}, u32[]{:S(2)}, u32[]{:S(2)}) %collective-permute-start.11) | collective-permute-done | bytes 32800 | tf_op jit(solution)/shard_map/ppermute | solution.py:332
  51.6 1.7 %shard_map.74 = (bf16[64,8,128]{2,1,0:T(8,128)(2,1)}, f32[8,128]{1,0:T(8,128)S(1)}) custom-call(s32[3]{0:T(128)S(1)} %pad_add_fusion.info, bf16[8,64,256]{2,1,0:T(8,128)(2,1)S(1)} %get-tuple-element.56.g_ref, bf16[64,256]{1,0:T(8,128)(2,1)S(1)} %collective-permute-done.10.a_ref, bf16[64,256]{1,0:T(8,128)(2,1)S(1)} %collective-permute-done.11.b_ref, ...), custom_call_target="tpu_custom_call" | custom-call | flops 150994944 | bytes 536576 | tf_op jit(solution)/shard_map/pallas_call | solution.py:31
  53.5 1.6 %collective-permute-done.17.other_ref = bf16[656,256]{1,0:T(8,128)(2,1)S(1)} collective-permute-done((bf16[656,256]{1,0:T(8,128)(2,1)S(1)}, bf16[656,256]{1,0:T(8,128)(2,1)S(1)}, u32[]{:S(2)}, u32[]{:S(2)}) %collective-permute-start.17) | collective-permute-done | bytes 335904 | tf_op jit(solution)/shard_map/ppermute | solution.py:328
  55.1 1.8 %shard_map.79 = (f32[3,192,64]{2,1,0:T(8,128)}, f32[1152,256]{1,0:T(8,128)}) custom-call(s32[3]{0:T(128)S(1)} %pad_add_fusion.info, bf16[656,256]{1,0:T(8,128)(2,1)S(1)} %shard_map.78.mine_ref, bf16[656,256]{1,0:T(8,128)(2,1)S(1)} %collective-permute-done.17.other_ref), custom_call_target="tpu_custom_call" | custom-call | flops 1 | bytes 1998848 | tf_op jit(solution)/shard_map/pallas_call | solution.py:31
  (44 shorter events, 9.1 us)
Async XLA Ops:
  0.6 24.4 %copy-start.2 = (bf16[128,3,3,256]{3,0,2,1:T(8,128)(2,1)S(1)}, bf16[128,3,3,256]{3,0,2,1:T(8,128)(2,1)}, u32[]{:S(2)}) copy-start(bf16[128,3,3,256]{3,0,2,1:T(8,128)(2,1)} %param.6) | copy-start | bytes 1769476
  1.7 7.2 %collective-permute-start = (bf16[64,128]{1,0:T(8,128)(2,1)S(1)}, bf16[64,128]{1,0:T(8,128)(2,1)S(1)}, u32[]{:S(2)}, u32[]{:S(2)}) collective-permute-start(bf16[64,128]{1,0:T(8,128)(2,1)S(1)} %get-tuple-element.68), channel_id=1, source_target_pairs={{0,4},{4,0},{8,12},{12,8},{1,5},{5,1},{9,13},{13,9},{2,6},{6,2},{1... | collective-permute-start | bytes 49160 | tf_op jit(solution)/shard_map/ppermute | solution.py:328
  4.7 5.5 %collective-permute-start.1 = (bf16[64,128]{1,0:T(8,128)(2,1)S(1)}, bf16[64,128]{1,0:T(8,128)(2,1)S(1)}, u32[]{:S(2)}, u32[]{:S(2)}) collective-permute-start(bf16[64,128]{1,0:T(8,128)(2,1)S(1)} %get-tuple-element.67), channel_id=1, source_target_pairs={{0,12},{4,8},{8,4},{12,0},{1,13},{5,9},{9,5},{13,1},{2,14},{6,10},... | collective-permute-start | bytes 49160 | tf_op jit(solution)/shard_map/ppermute | solution.py:332
  10.9 3.8 %collective-permute-start.2 = (bf16[144,128]{1,0:T(8,128)(2,1)S(1)}, bf16[144,128]{1,0:T(8,128)(2,1)S(1)}, u32[]{:S(2)}, u32[]{:S(2)}) collective-permute-start(bf16[144,128]{1,0:T(8,128)(2,1)S(1)} %get-tuple-element.37), channel_id=1, source_target_pairs={{0,3},{1,2},{2,1},{3,0},{4,7},{5,6},{6,5},{7,4},{8,11},{9,10},{10,... | collective-permute-start | bytes 110600 | tf_op jit(solution)/shard_map/ppermute | solution.py:332
  11.0 3.7 %collective-permute-start.3 = (bf16[144,128]{1,0:T(8,128)(2,1)S(1)}, bf16[144,128]{1,0:T(8,128)(2,1)S(1)}, u32[]{:S(2)}, u32[]{:S(2)}) collective-permute-start(bf16[144,128]{1,0:T(8,128)(2,1)S(1)} %get-tuple-element.38), channel_id=1, source_target_pairs={{0,1},{1,0},{2,3},{3,2},{4,5},{5,4},{6,7},{7,6},{8,9},{9,8},{10,11... | collective-permute-start | bytes 110600 | tf_op jit(solution)/shard_map/ppermute | solution.py:328
  12.6 0.9 %copy-start = (bf16[64,3,3,64]{3,0,2,1:T(8,128)(2,1)S(1)}, bf16[64,3,3,64]{3,0,2,1:T(8,128)(2,1)}, u32[]{:S(2)}) copy-start(bf16[64,3,3,64]{3,0,2,1:T(8,128)(2,1)} %param.5) | copy-start | bytes 221188
  16.1 4.5 %collective-permute-start.4 = (bf16[2,40,256]{2,1,0:T(8,128)(2,1)S(1)}, bf16[2,40,256]{2,1,0:T(8,128)(2,1)S(1)}, u32[]{:S(2)}, u32[]{:S(2)}) collective-permute-start(bf16[2,40,256]{2,1,0:T(8,128)(2,1)S(1)} %get-tuple-element.44.refs_0_), channel_id=1, source_target_pairs={{0,4},{4,0},{8,12},{12,8},{1,5},{5,1},{9,13},{13,9},{2,6},{6,2},{1... | collective-permute-start | bytes 122888 | tf_op jit(solution)/shard_map/ppermute | solution.py:336
  16.2 5.6 %collective-permute-start.5 = (bf16[2,40,256]{2,1,0:T(8,128)(2,1)S(1)}, bf16[2,40,256]{2,1,0:T(8,128)(2,1)S(1)}, u32[]{:S(2)}, u32[]{:S(2)}) collective-permute-start(bf16[2,40,256]{2,1,0:T(8,128)(2,1)S(1)} %get-tuple-element.44.refs_0_), channel_id=1, source_target_pairs={{0,8},{4,12},{8,0},{12,4},{1,9},{5,13},{9,1},{13,5},{2,10},{6,14},... | collective-permute-start | bytes 122888 | tf_op jit(solution)/shard_map/ppermute | solution.py:336
  19.2 5.8 %collective-permute-start.6 = (bf16[2,40,256]{2,1,0:T(8,128)(2,1)S(1)}, bf16[2,40,256]{2,1,0:T(8,128)(2,1)S(1)}, u32[]{:S(2)}, u32[]{:S(2)}) collective-permute-start(bf16[2,40,256]{2,1,0:T(8,128)(2,1)S(1)} %get-tuple-element.44.refs_0_), channel_id=1, source_target_pairs={{0,12},{4,8},{8,4},{12,0},{1,13},{5,9},{9,5},{13,1},{2,14},{6,10},... | collective-permute-start | bytes 122888 | tf_op jit(solution)/shard_map/ppermute | solution.py:336
  26.6 5.6 %collective-permute-start.7 = (bf16[72,256]{1,0:T(8,128)(2,1)S(1)}, bf16[72,256]{1,0:T(8,128)(2,1)S(1)}, u32[]{:S(2)}, u32[]{:S(2)}) collective-permute-start(bf16[72,256]{1,0:T(8,128)(2,1)S(1)} %get-tuple-element.46), channel_id=1, source_target_pairs={{0,4},{4,0},{8,12},{12,8},{1,5},{5,1},{9,13},{13,9},{2,6},{6,2},{1... | collective-permute-start | bytes 110600 | tf_op jit(solution)/shard_map/ppermute | solution.py:336
  26.7 5.5 %collective-permute-start.8 = (bf16[72,256]{1,0:T(8,128)(2,1)S(1)}, bf16[72,256]{1,0:T(8,128)(2,1)S(1)}, u32[]{:S(2)}, u32[]{:S(2)}) collective-permute-start(bf16[72,256]{1,0:T(8,128)(2,1)S(1)} %get-tuple-element.47), channel_id=1, source_target_pairs={{0,8},{4,12},{8,0},{12,4},{1,9},{5,13},{9,1},{13,5},{2,10},{6,14},... | collective-permute-start | bytes 110600 | tf_op jit(solution)/shard_map/ppermute | solution.py:336
  28.6 5.8 %collective-permute-start.9 = (bf16[72,256]{1,0:T(8,128)(2,1)S(1)}, bf16[72,256]{1,0:T(8,128)(2,1)S(1)}, u32[]{:S(2)}, u32[]{:S(2)}) collective-permute-start(bf16[72,256]{1,0:T(8,128)(2,1)S(1)} %get-tuple-element.48), channel_id=1, source_target_pairs={{0,12},{4,8},{8,4},{12,0},{1,13},{5,9},{9,5},{13,1},{2,14},{6,10},... | collective-permute-start | bytes 110600 | tf_op jit(solution)/shard_map/ppermute | solution.py:336
  34.3 14.6 %copy-start.1 = (bf16[64,3,3,64]{3,0,2,1:T(8,128)(2,1)S(1)}, bf16[64,3,3,64]{3,0,2,1:T(8,128)(2,1)}, u32[]{:S(2)}) copy-start(bf16[64,3,3,64]{3,0,2,1:T(8,128)(2,1)} %param.5) | copy-start | bytes 221188
  35.7 1.7 %collective-permute-start.12 = (bf16[656,256]{1,0:T(8,128)(2,1)S(1)}, bf16[656,256]{1,0:T(8,128)(2,1)S(1)}, u32[]{:S(2)}, u32[]{:S(2)}) collective-permute-start(bf16[656,256]{1,0:T(8,128)(2,1)S(1)} %get-tuple-element.61), channel_id=1, source_target_pairs={{0,1},{1,0},{2,3},{3,2},{4,5},{5,4},{6,7},{7,6},{8,9},{9,8},{10,11... | collective-permute-start | bytes 1007624 | tf_op jit(solution)/shard_map/ppermute | solution.py:328
  37.5 15.8 %collective-permute-start.13 = (bf16[576,256]{1,0:T(8,128)(2,1)S(1)}, bf16[576,256]{1,0:T(8,128)(2,1)S(1)}, u32[]{:S(2)}, u32[]{:S(2)}) collective-permute-start(bf16[576,256]{1,0:T(8,128)(2,1)S(1)} %get-tuple-element.62.a_ref), channel_id=1, source_target_pairs={{0,2},{2,0},{1,3},{3,1},{4,6},{6,4},{5,7},{7,5},{8,10},{10,8},{9,1... | collective-permute-start | bytes 884744 | tf_op jit(solution)/shard_map/ppermute | solution.py:336
  38.7 4.0 %collective-permute-start.14 = (bf16[80,256]{1,0:T(8,128)(2,1)S(1)}, bf16[80,256]{1,0:T(8,128)(2,1)S(1)}, u32[]{:S(2)}, u32[]{:S(2)}) collective-permute-start(bf16[80,256]{1,0:T(8,128)(2,1)S(1)} %get-tuple-element.63.a_ref), channel_id=1, source_target_pairs={{0,4},{4,0},{8,12},{12,8},{1,5},{5,1},{9,13},{13,9},{2,6},{6,2},{1... | collective-permute-start | bytes 122888 | tf_op jit(solution)/shard_map/ppermute | solution.py:336
  42.8 5.2 %collective-permute-start.15 = (bf16[80,256]{1,0:T(8,128)(2,1)S(1)}, bf16[80,256]{1,0:T(8,128)(2,1)S(1)}, u32[]{:S(2)}, u32[]{:S(2)}) collective-permute-start(bf16[80,256]{1,0:T(8,128)(2,1)S(1)} %shard_map.76.a_ref), channel_id=1, source_target_pairs={{0,8},{4,12},{8,0},{12,4},{1,9},{5,13},{9,1},{13,5},{2,10},{6,14},... | collective-permute-start | bytes 122888 | tf_op jit(solution)/shard_map/ppermute | solution.py:336
  43.8 5.4 %collective-permute-start.10 = (bf16[64,256]{1,0:T(8,128)(2,1)S(1)}, bf16[64,256]{1,0:T(8,128)(2,1)S(1)}, u32[]{:S(2)}, u32[]{:S(2)}) collective-permute-start(bf16[64,256]{1,0:T(8,128)(2,1)S(1)} %get-tuple-element.57), channel_id=1, source_target_pairs={{0,4},{4,0},{8,12},{12,8},{1,5},{5,1},{9,13},{13,9},{2,6},{6,2},{1... | collective-permute-start | bytes 98312 | tf_op jit(solution)/shard_map/ppermute | solution.py:328
  45.9 5.7 %collective-permute-start.11 = (bf16[64,256]{1,0:T(8,128)(2,1)S(1)}, bf16[64,256]{1,0:T(8,128)(2,1)S(1)}, u32[]{:S(2)}, u32[]{:S(2)}) collective-permute-start(bf16[64,256]{1,0:T(8,128)(2,1)S(1)} %get-tuple-element.58), channel_id=1, source_target_pairs={{0,12},{4,8},{8,4},{12,0},{1,13},{5,9},{9,5},{13,1},{2,14},{6,10},... | collective-permute-start | bytes 98312 | tf_op jit(solution)/shard_map/ppermute | solution.py:332
  48.0 5.3 %collective-permute-start.16 = (bf16[80,256]{1,0:T(8,128)(2,1)S(1)}, bf16[80,256]{1,0:T(8,128)(2,1)S(1)}, u32[]{:S(2)}, u32[]{:S(2)}) collective-permute-start(bf16[80,256]{1,0:T(8,128)(2,1)S(1)} %shard_map.77.c_ref), channel_id=1, source_target_pairs={{0,2},{2,0},{1,3},{3,1},{4,6},{6,4},{5,7},{7,5},{8,10},{10,8},{9,1... | collective-permute-start | bytes 122888 | tf_op jit(solution)/shard_map/ppermute | solution.py:336
  53.4 1.7 %collective-permute-start.17 = (bf16[656,256]{1,0:T(8,128)(2,1)S(1)}, bf16[656,256]{1,0:T(8,128)(2,1)S(1)}, u32[]{:S(2)}, u32[]{:S(2)}) collective-permute-start(bf16[656,256]{1,0:T(8,128)(2,1)S(1)} %shard_map.78.mine_ref), channel_id=1, source_target_pairs={{0,1},{1,0},{2,3},{3,2},{4,5},{5,4},{6,7},{7,6},{8,9},{9,8},{10,11... | collective-permute-start | bytes 1007624 | tf_op jit(solution)/shard_map/ppermute | solution.py:328

commit v8 on v7

--- a/solution.py
+++ b/solution.py
@@ -21,12 +21,11 @@
     return lax.dot_general(a, b, ((contract[:1], contract[1:]), ((), ())), preferred_element_type=F32)
 
 
-def whole_call(body, outs, operands, flops, scalars=1, scratch=(), after=0, out_space=pltpu.VMEM):
+def whole_call(body, outs, operands, flops, scratch=(), after=0, out_space=pltpu.VMEM):
     specs = [
-        pl.BlockSpec(memory_space=pltpu.SMEM if n < scalars else pltpu.VMEM)
-        for n in range(len(operands) - after)
+        pl.BlockSpec(memory_space=pltpu.VMEM) for _ in range(len(operands) - after)
     ] + [pl.BlockSpec(memory_space=pl.ANY)] * after
-    sizes = [math.prod(a.shape) * a.dtype.itemsize for a in tuple(operands[scalars:]) + tuple(outs)]
+    sizes = [math.prod(a.shape) * a.dtype.itemsize for a in tuple(operands) + tuple(outs)]
     moved = sum(sizes) if flops else 0
     return pl.pallas_call(
         body,
@@ -37,6 +36,10 @@
         cost_estimate=pl.CostEstimate(flops=flops, bytes_accessed=moved, transcendentals=0),
         compiler_params=pltpu.CompilerParams(vmem_limit_bytes=40 * 1024 * 1024),
     )(*operands)
+
+
+def strip_index():
+    return lax.axis_index("col") * lax.axis_size("pair") + lax.axis_index("pair")
 
 
 def shaped(shape, dtype=BF16):
@@ -77,10 +80,10 @@
     return jnp.where(lane == 4 * c + 2 * i + j, 1.0, 0.0).astype(BF16)
 
 
-def constants(info, w_ref, joined_ref, pool_ref, back_ref, order_ref, *, total):
+def constants(w_ref, joined_ref, pool_ref, back_ref, order_ref, *, total):
     joined_ref[...] = jnp.concatenate([w_ref[0], w_ref[1], w_ref[2]], axis=1)
-    pool_ref[...] = pool_matrix(info[0], total)
-    back_ref[...] = pool_matrix(info[0], total, back=True)
+    pool_ref[...] = pool_matrix(strip_index(), total)
+    back_ref[...] = pool_matrix(strip_index(), total, back=True)
     order_ref[...] = order_matrix()
 
 
@@ -96,8 +99,8 @@
     return jnp.where(slot == r, turned, head), jnp.where(slot == (r - 1) % 8, turned, tail)
 
 
-def pack_own(info, x_ref, head_ref, tail_ref, a_ref, b_ref):
-    even = (info[0] & 1) == 0
+def pack_own(x_ref, head_ref, tail_ref, a_ref, b_ref):
+    even = (strip_index() & 1) == 0
     slot = lax.broadcasted_iota(jnp.int32, (64, 128), 1) >> 4
     head = tail = jnp.zeros((64, 128), F32)
     for r in range(x_ref.shape[0]):
@@ -109,9 +112,9 @@
     b_ref[64:] = jnp.where(even, first, last).astype(BF16)
 
 
-def pack_borders(info, up_a_ref, up_b_ref, own_a_ref, own_b_ref, a_ref, b_ref, above_ref, below_ref, *, bands):
-    even = (info[0] & 1) == 0
-    above_ref[...], below_ref[...] = beside(up_a_ref, up_b_ref, info[2], bands)
+def pack_borders(up_a_ref, up_b_ref, own_a_ref, own_b_ref, a_ref, b_ref, above_ref, below_ref, *, bands):
+    even = (strip_index() & 1) == 0
+    above_ref[...], below_ref[...] = beside(up_a_ref, up_b_ref, lax.axis_index("row"), bands)
     slot = lax.broadcasted_iota(jnp.int32, (64, 128), 1) >> 4
     head = tail = jnp.zeros((64, 128), F32)
     for r, ref in enumerate((above_ref, below_ref)):
@@ -123,7 +126,6 @@
 
 
 def layer_one(
-    info,
     x_ref,
     above_ref,
     below_ref,
@@ -138,7 +140,7 @@
     *,
     strips,
 ):
-    strip = info[0]
+    strip = strip_index()
     band_rows = x_ref.shape[0]
     slot = lax.broadcasted_iota(jnp.int32, (128, 128), 1) >> 4
     inner = (strip > 0) & (strip < strips - 1)
@@ -180,11 +182,11 @@
         pooled_ref[u] = ordered[u * PITCH : u * PITCH + SENT]
 
 
-def layer_two(info, og_ref, w_ref, *refs, bands):
+def layer_two(og_ref, w_ref, *refs, bands):
     pieces, refs = refs[:bands], refs[bands:]
     terms, refs = refs[:bands], refs[bands:]
     map_ref, grad_ref, pack_ref = refs
-    band = info[2]
+    band = lax.axis_index("row")
     rows, _, filters = og_ref.shape
     count = rows * PITCH
     map_ref[0] = jnp.zeros((PITCH, 256), BF16)
@@ -218,8 +220,8 @@
         terms[k][...] = pack_ref[band ^ k]
 
 
-def filter_two_grads(info, map_ref, grad_ref, keep_ref, send_ref, all_ref):
-    pair = info[1]
+def filter_two_grads(map_ref, grad_ref, keep_ref, send_ref, all_ref):
+    pair = lax.axis_index("pair")
     rows = map_ref.shape[0] - 2
     filters = grad_ref.shape[2]
     v = lax.broadcasted_iota(jnp.int32, (rows, PITCH, filters), 1)
@@ -252,11 +254,11 @@
     out_ref[half:] = (c_ref[...].astype(F32) + d_ref[...].astype(F32)).astype(BF16)
 
 
-def grad_pre_one(info, *refs, bands):
+def grad_pre_one(*refs, bands):
     terms, refs = refs[:bands], refs[bands:]
     slope_ref, wide_ref, pool_ref, order_ref, keep_two_ref, send_two_ref, *refs = refs
     g_ref, a_ref, b_ref, keep_ref, send_ref, part_ref = refs
-    pair = info[1]
+    pair = lax.axis_index("pair")
     summed = terms[0][...].astype(F32)
     for k in range(1, bands):
         summed = summed + terms[k][...].astype(F32)
@@ -278,7 +280,7 @@
             cats.append(jnp.concatenate([roll(mine, -1, 1), mine, roll(mine, 1, 1)], 0).astype(BF16))
     around = jnp.concatenate([wide_ref[h : h + 3].reshape(192, 256) for h in range(8)], 1)
     acc = dot(jnp.concatenate(cats, 1), around, (1, 1))
-    even = (info[2] & 1) == 0
+    even = (lax.axis_index("row") & 1) == 0
     first, last = g_ref[0].astype(F32), g_ref[7].astype(F32)
     a_ref[...] = jnp.where(even, last, first).astype(BF16)
     b_ref[...] = jnp.where(even, first, last).astype(BF16)
@@ -292,8 +294,8 @@
         ref[half:] = jnp.concatenate([mine, blank], 0).astype(BF16)
 
 
-def layer_one_back(info, g_ref, a_ref, b_ref, w_ref, out_ref, done_ref, *, bands):
-    above, below = beside(a_ref, b_ref, info[2], bands)
+def layer_one_back(g_ref, a_ref, b_ref, w_ref, out_ref, done_ref, *, bands):
+    above, below = beside(a_ref, b_ref, lax.axis_index("row"), bands)
     done_ref[...] = jnp.zeros(done_ref.shape, F32)
     lines = [above] + [g_ref[h] for h in range(8)] + [below]
     rows = []
@@ -303,8 +305,8 @@
     out_ref[...] = jnp.swapaxes(jnp.stack(rows, 0), 0, 1).astype(BF16)
 
 
-def finish(info, mine_ref, other_ref, one_hbm, two_hbm, one_ref, two_ref, flat_ref, sems, *, scales):
-    pair, half = info[1], mine_ref.shape[0] - TAIL
+def finish(mine_ref, other_ref, one_hbm, two_hbm, one_ref, two_ref, flat_ref, sems, *, scales):
+    pair, half = lax.axis_index("pair"), mine_ref.shape[0] - TAIL
     copies = [pltpu.make_async_copy(one_ref, one_hbm, sems.at[0])]
     for ref, place in ((mine_ref, pair), (other_ref, 1 - pair)):
         flat_ref[pl.ds(pl.multiple_of(place * 72, 8), 72)] = ref[half : half + 72].astype(F32) * scales[0]
@@ -343,7 +345,7 @@
 
 
 def added(a, b, *after):
-    (total,) = whole_call(add_after, [shaped(a.shape)], [a, b, *after], 0, scalars=0, after=len(after))
+    (total,) = whole_call(add_after, [shaped(a.shape)], [a, b, *after], 0, after=len(after))
     return total
 
 
@@ -365,7 +367,6 @@
     pair = lax.axis_index("pair")
     height, width = band_rows * bands, strip_cols * strips
     total = own_cols * strips
-    at_place = jnp.stack([strip, pair, band]).astype(jnp.int32)
 
     taps_one = jnp.transpose(filters_one, (1, 2, 0, 3)).reshape(3, 3 * channels, channels)
     back_one = jnp.transpose(filters_one[:, ::-1], (2, 3, 1, 0)).reshape(3 * channels, 3 * channels)
@@ -380,17 +381,17 @@
     joined_one, pool, pool_back, order = whole_call(
         functools.partial(constants, total=total),
         [shaped((3 * channels, 3 * channels))] + [shaped((2 * PITCH, 256))] * 2 + [shaped((256, 256))],
-        [at_place, taps_one],
+        [taps_one],
         10**8,
     )
     head, tail = head.reshape(-1, 128), tail.reshape(-1, 128)
     own_a, own_b = whole_call(
-        pack_own, [shaped((channels + head.shape[0], 128))] * 2, [at_place, x, head, tail], 10**8
+        pack_own, [shaped((channels + head.shape[0], 128))] * 2, [x, head, tail], 10**8
     )
     to_a, to_b, above, below = whole_call(
         functools.partial(pack_borders, bands=bands),
         [shaped((2 * channels + head.shape[0], 128))] * 2 + [shaped((channels, strip_cols))] * 2,
-        [at_place, even_swap(to_a, "row", bands), odd_swap(to_b, "row", bands), own_a, own_b],
+        [even_swap(to_a, "row", bands), odd_swap(to_b, "row", bands), own_a, own_b],
         1,
     )
     side_a, side_b = even_swap(to_a, COLS, strips), odd_swap(to_b, COLS, strips)
@@ -401,7 +402,7 @@
             shaped((band_rows, channels, 256)),
             shaped((band_rows + 2, channels, 256)),
         ],
-        [at_place, x, above, below, side_a, side_b, joined_one, pool, order],
+        [x, above, below, side_a, side_b, joined_one, pool, order],
         2 * band_rows * 192 * 192 * 256,
     )
     pieces = [pooled] + row_swaps([pooled] * bands, bands)
@@ -419,7 +420,7 @@
         functools.partial(layer_two, bands=bands),
         [shaped((72, 4 * channels))] * bands
         + [shaped((pooled_rows + 2, PITCH, 4 * channels)), shaped((pooled_rows + 2, PITCH, filters))],
-        [at_place, og, taps_two] + pieces,
+        [og, taps_two] + pieces,
         4 * count * 9 * filters * 4 * channels,
         scratch=[pltpu.VMEM((bands, 72, 4 * channels), BF16)],
     )
@@ -429,7 +430,7 @@
     keep_two, send_two = whole_call(
         filter_two_grads,
         [shaped((half, 4 * channels))] * 2,
-        [at_place, pooled_map, grad_map],
+        [pooled_map, grad_map],
         2 * count * 9 * filters * 4 * channels,
         scratch=[pltpu.VMEM((2 * half, 4 * channels), BF16)],
     )
@@ -438,7 +439,7 @@
         [shaped((band_rows, channels, 256))]
         + [shaped((channels, 256))] * 2
         + [shaped((half + TAIL, 256))] * 2,
-        [at_place] + received + [slope, wide, pool_back, order, keep_two, send_two],
+        received + [slope, wide, pool_back, order, keep_two, send_two],
         2 * 8 * 192 * 192 * 256,
         scratch=[pltpu.VMEM((144, 256), F32)],
     )
@@ -447,7 +448,6 @@
         [shaped((half, 256)), shaped((TAIL, 256))],
         [keep, even_swap(send, "pair", 2)],
         0,
-        scalars=0,
     )
     columns = lax.axis_size("col")
     two, two_more = sum_but_last(two, "col", columns)
@@ -455,7 +455,7 @@
     input_grad, done = whole_call(
         functools.partial(layer_one_back, bands=bands),
         [shaped(features_in.shape), shaped((8, 128), F32)],
-        [at_place, g, even_swap(up_a, "row", bands), odd_swap(up_b, "row", bands), back_one],
+        [g, even_swap(up_a, "row", bands), odd_swap(up_b, "row", bands), back_one],
         2 * band_rows * 192 * 192 * 256,
     )
     one, one_more = sum_but_last(added(one, one_more), "col", columns)
@@ -464,7 +464,6 @@
         [shaped((half + TAIL, 256))],
         [two, two_more, one, one_more, done],
         0,
-        scalars=0,
         after=1,
     )
     grad_one, grad_two = whole_call(
@@ -473,7 +472,7 @@
             scales=(1.0 / math.sqrt(height * width), 1.0 / math.sqrt(pooled_rows * total)),
         ),
         [shaped((3, 3 * channels, channels), F32), shaped((2 * half, 256), F32)],
-        [at_place, mine, even_swap(mine, "pair", 2)],
+        [mine, even_swap(mine, "pair", 2)],
         1,
         scratch=[
             pltpu.VMEM((3, 3 * channels, channels), F32),

time: 57.1 us -> 53.8 us (0.942)
  Pallas kernels: 11.1 us -> 6.32 us
  waiting for transfers between devices: 18.8 us -> 20.5 us
    pallas_call x13, Pallas kernels: 11.1 us -> 6.32 us  [whole_call(): pl.pallas_call(body, out_shape=outs, in_specs=specs, out_specs=[pl.BlockS...]
    ppermute x3, waiting for transfers between devices: 4.25 us -> 5.41 us  [odd_swap(): lax.ppermute(values, axis, [(n, (n - 1 if n % 2 == 0 else n + 1) % count)...]
  transfers between devices with their start and end apart: 18 -> 18, of which waited for: 10 -> 11; matrix products, arithmetic and copies ran while one was open for 2% -> 2% of each run, Pallas kernels for 7% -> 4%
where the time goes in v8:
time: 53.8 us; the launch traced here: 53.6 us
  starting transfers between devices  22.8 us (42%)
  waiting for transfers between devices  20.5 us (38%)
  Pallas kernels  6.32 us (12%)
  local copies, waits for them, and re-layouts  3.12 us (6%)
  between operations  0.83 us (2%)
    ppermute x10, starting transfers between devices, xor_swap(): return lax.ppermute(values, axis, [(n, n ^ k) for n in range(count)])  12.1 us
    ppermute x10, waiting for transfers between devices, xor_swap(): return lax.ppermute(values, axis, [(n, n ^ k) for n in range(count)])  11.8 us
    ppermute x5, starting transfers between devices, even_swap(): return lax.ppermute(values, axis, [(n, n ^ 1) for n in range(count)])  6.85 us
    pallas_call x13, Pallas kernels, whole_call(): pl.pallas_call(body, out_shape=outs, in_specs=specs, out_specs=[pl.BlockS...  6.32 us
    ppermute x3, waiting for transfers between devices, odd_swap(): lax.ppermute(values, axis, [(n, (n - 1 if n % 2 == 0 else n + 1) % count)...  5.41 us
    ppermute x3, starting transfers between devices, odd_swap(): lax.ppermute(values, axis, [(n, (n - 1 if n % 2 == 0 else n + 1) % count)...  3.88 us
    ppermute x5, waiting for transfers between devices, even_swap(): return lax.ppermute(values, axis, [(n, n ^ 1) for n in range(count)])  3.26 us
    unnamed x8, local copies, waits for them, and re-layouts  2.75 us
  transfers between devices with their start and end apart: 18, of which 11 were waited for; matrix products, arithmetic and copies ran while one was open for 2% of the time, Pallas kernels for 4%

profile of v8, /device:TPU:0, one launch (start us, length us, event | category | flops | bytes accessed | tf_op | source)
XLA Modules:
  0.0 53.6 jit_solution(1458221093369655274)
XLA Ops:
  0.7 1.0 %copy.21 = bf16[64,8,128]{2,0,1:T(8,128)(2,1)S(1)} copy(bf16[64,8,128]{2,1,0:T(8,128)(2,1)} %param.4) | data formatting | bytes 262144 | tf_op args[0]
  1.7 3.1 %collective-permute-start = (bf16[64,128]{1,0:T(8,128)(2,1)S(1)}, bf16[64,128]{1,0:T(8,128)(2,1)S(1)}, u32[]{:S(2)}, u32[]{:S(2)}) collective-permute-start(bf16[64,128]{1,0:T(8,128)(2,1)S(1)} %get-tuple-element.68), channel_id=1, source_target_pairs={{0,4},{4,0},{8,12},{12,8},{1,5},{5,1},{9,13},{13,9},{2,6},{6,2},{1... | collective-permute-start | bytes 49160 | tf_op jit(solution)/shard_map/ppermute | solution.py:330
  4.7 2.5 %collective-permute-start.1 = (bf16[64,128]{1,0:T(8,128)(2,1)S(1)}, bf16[64,128]{1,0:T(8,128)(2,1)S(1)}, u32[]{:S(2)}, u32[]{:S(2)}) collective-permute-start(bf16[64,128]{1,0:T(8,128)(2,1)S(1)} %get-tuple-element.67), channel_id=1, source_target_pairs={{0,12},{4,8},{8,4},{12,0},{1,13},{5,9},{9,5},{13,1},{2,14},{6,10},... | collective-permute-start | bytes 49160 | tf_op jit(solution)/shard_map/ppermute | solution.py:334
  8.2 2.1 %collective-permute-done.1.up_b_ref = bf16[64,128]{1,0:T(8,128)(2,1)S(1)} collective-permute-done((bf16[64,128]{1,0:T(8,128)(2,1)S(1)}, bf16[64,128]{1,0:T(8,128)(2,1)S(1)}, u32[]{:S(2)}, u32[]{:S(2)}) %collective-permute-start.1) | collective-permute-done | bytes 16416 | tf_op jit(solution)/shard_map/ppermute | solution.py:334
  10.4 1.6 %collective-permute-start.3 = (bf16[144,128]{1,0:T(8,128)(2,1)S(1)}, bf16[144,128]{1,0:T(8,128)(2,1)S(1)}, u32[]{:S(2)}, u32[]{:S(2)}) collective-permute-start(bf16[144,128]{1,0:T(8,128)(2,1)S(1)} %get-tuple-element.38), channel_id=1, source_target_pairs={{0,1},{1,0},{2,3},{3,2},{4,5},{5,4},{6,7},{7,6},{8,9},{9,8},{10,11... | collective-permute-start | bytes 110600 | tf_op jit(solution)/shard_map/ppermute | solution.py:330
  13.1 1.1 %collective-permute-done.2.b_ref = bf16[144,128]{1,0:T(8,128)(2,1)S(1)} collective-permute-done((bf16[144,128]{1,0:T(8,128)(2,1)S(1)}, bf16[144,128]{1,0:T(8,128)(2,1)S(1)}, u32[]{:S(2)}, u32[]{:S(2)}) %collective-permute-start.2) | collective-permute-done | bytes 36896 | tf_op jit(solution)/shard_map/ppermute | solution.py:334
  15.1 3.0 %collective-permute-start.5 = (bf16[2,40,256]{2,1,0:T(8,128)(2,1)S(1)}, bf16[2,40,256]{2,1,0:T(8,128)(2,1)S(1)}, u32[]{:S(2)}, u32[]{:S(2)}) collective-permute-start(bf16[2,40,256]{2,1,0:T(8,128)(2,1)S(1)} %get-tuple-element.44.refs_0_), channel_id=1, source_target_pairs={{0,8},{4,12},{8,0},{12,4},{1,9},{5,13},{9,1},{13,5},{2,10},{6,14},... | collective-permute-start | bytes 122888 | tf_op jit(solution)/shard_map/ppermute | solution.py:338
  18.1 1.3 %collective-permute-start.6 = (bf16[2,40,256]{2,1,0:T(8,128)(2,1)S(1)}, bf16[2,40,256]{2,1,0:T(8,128)(2,1)S(1)}, u32[]{:S(2)}, u32[]{:S(2)}) collective-permute-start(bf16[2,40,256]{2,1,0:T(8,128)(2,1)S(1)} %get-tuple-element.44.refs_0_), channel_id=1, source_target_pairs={{0,12},{4,8},{8,4},{12,0},{1,13},{5,9},{9,5},{13,1},{2,14},{6,10},... | collective-permute-start | bytes 122888 | tf_op jit(solution)/shard_map/ppermute | solution.py:338
  19.6 1.1 %collective-permute-done.5.refs_2_ = bf16[2,40,256]{2,1,0:T(8,128)(2,1)S(1)} collective-permute-done((bf16[2,40,256]{2,1,0:T(8,128)(2,1)S(1)}, bf16[2,40,256]{2,1,0:T(8,128)(2,1)S(1)}, u32[]{:S(2)}, u32[]{:S(2)}) %collective-permute-start.5) | collective-permute-done | bytes 40992 | tf_op jit(solution)/shard_map/ppermute | solution.py:338
  20.7 3.3 %collective-permute-done.6.refs_3_ = bf16[2,40,256]{2,1,0:T(8,128)(2,1)S(1)} collective-permute-done((bf16[2,40,256]{2,1,0:T(8,128)(2,1)S(1)}, bf16[2,40,256]{2,1,0:T(8,128)(2,1)S(1)}, u32[]{:S(2)}, u32[]{:S(2)}) %collective-permute-start.6) | collective-permute-done | bytes 40992 | tf_op jit(solution)/shard_map/ppermute | solution.py:338
  23.9 1.0 %shard_map.71 = (bf16[72,256]{1,0:T(8,128)(2,1)S(1)}, bf16[72,256]{1,0:T(8,128)(2,1)S(1)}, bf16[72,256]{1,0:T(8,128)(2,1)S(1)}, bf16[72,256]{1,0:T(8,128)(2,1)S(...) custom-call(bf16[8,48,128]{2,1,0:T(8,128)(2,1)S(1)} %fusion.6.og_ref, ...), custom_call_target="tpu_custom_call" | custom-call | flops 452984832 | bytes 1368064 | tf_op jit(solution)/shard_map/pallas_call | solution.py:30
  25.0 1.9 %collective-permute-start.8 = (bf16[72,256]{1,0:T(8,128)(2,1)S(1)}, bf16[72,256]{1,0:T(8,128)(2,1)S(1)}, u32[]{:S(2)}, u32[]{:S(2)}) collective-permute-start(bf16[72,256]{1,0:T(8,128)(2,1)S(1)} %get-tuple-element.47), channel_id=1, source_target_pairs={{0,8},{4,12},{8,0},{12,4},{1,9},{5,13},{9,1},{13,5},{2,10},{6,14},... | collective-permute-start | bytes 110600 | tf_op jit(solution)/shard_map/ppermute | solution.py:338
  26.9 2.5 %collective-permute-start.9 = (bf16[72,256]{1,0:T(8,128)(2,1)S(1)}, bf16[72,256]{1,0:T(8,128)(2,1)S(1)}, u32[]{:S(2)}, u32[]{:S(2)}) collective-permute-start(bf16[72,256]{1,0:T(8,128)(2,1)S(1)} %get-tuple-element.48), channel_id=1, source_target_pairs={{0,12},{4,8},{8,4},{12,0},{1,13},{5,9},{9,5},{13,1},{2,14},{6,10},... | collective-permute-start | bytes 110600 | tf_op jit(solution)/shard_map/ppermute | solution.py:338
  30.4 2.3 %collective-permute-done.9.refs_3_ = bf16[72,256]{1,0:T(8,128)(2,1)S(1)} collective-permute-done((bf16[72,256]{1,0:T(8,128)(2,1)S(1)}, bf16[72,256]{1,0:T(8,128)(2,1)S(1)}, u32[]{:S(2)}, u32[]{:S(2)}) %collective-permute-start.9) | collective-permute-done | bytes 36896 | tf_op jit(solution)/shard_map/ppermute | solution.py:338
  33.7 1.6 %collective-permute-done.12.b_ref = bf16[656,256]{1,0:T(8,128)(2,1)S(1)} collective-permute-done((bf16[656,256]{1,0:T(8,128)(2,1)S(1)}, bf16[656,256]{1,0:T(8,128)(2,1)S(1)}, u32[]{:S(2)}, u32[]{:S(2)}) %collective-permute-start.12) | collective-permute-done | bytes 335904 | tf_op jit(solution)/shard_map/ppermute | solution.py:330
  35.4 1.2 %collective-permute-start.13 = (bf16[576,256]{1,0:T(8,128)(2,1)S(1)}, bf16[576,256]{1,0:T(8,128)(2,1)S(1)}, u32[]{:S(2)}, u32[]{:S(2)}) collective-permute-start(bf16[576,256]{1,0:T(8,128)(2,1)S(1)} %get-tuple-element.62.a_ref), channel_id=1, source_target_pairs={{0,2},{2,0},{1,3},{3,1},{4,6},{6,4},{5,7},{7,5},{8,10},{10,8},{9,1... | collective-permute-start | bytes 884744 | tf_op jit(solution)/shard_map/ppermute | solution.py:338
  36.6 4.0 %collective-permute-done.14.b_ref = bf16[80,256]{1,0:T(8,128)(2,1)S(1)} collective-permute-done((bf16[80,256]{1,0:T(8,128)(2,1)S(1)}, bf16[80,256]{1,0:T(8,128)(2,1)S(1)}, u32[]{:S(2)}, u32[]{:S(2)}) %collective-permute-start.14) | collective-permute-done | bytes 40992 | tf_op jit(solution)/shard_map/ppermute | solution.py:338
  40.6 1.1 %collective-permute-start.15 = (bf16[80,256]{1,0:T(8,128)(2,1)S(1)}, bf16[80,256]{1,0:T(8,128)(2,1)S(1)}, u32[]{:S(2)}, u32[]{:S(2)}) collective-permute-start(bf16[80,256]{1,0:T(8,128)(2,1)S(1)} %shard_map.76.a_ref), channel_id=1, source_target_pairs={{0,8},{4,12},{8,0},{12,4},{1,9},{5,13},{9,1},{13,5},{2,10},{6,14},... | collective-permute-start | bytes 122888 | tf_op jit(solution)/shard_map/ppermute | solution.py:338
  41.7 2.0 %collective-permute-start.10 = (bf16[64,256]{1,0:T(8,128)(2,1)S(1)}, bf16[64,256]{1,0:T(8,128)(2,1)S(1)}, u32[]{:S(2)}, u32[]{:S(2)}) collective-permute-start(bf16[64,256]{1,0:T(8,128)(2,1)S(1)} %get-tuple-element.57), channel_id=1, source_target_pairs={{0,4},{4,0},{8,12},{12,8},{1,5},{5,1},{9,13},{13,9},{2,6},{6,2},{1... | collective-permute-start | bytes 98312 | tf_op jit(solution)/shard_map/ppermute | solution.py:330
  43.7 1.4 %collective-permute-start.11 = (bf16[64,256]{1,0:T(8,128)(2,1)S(1)}, bf16[64,256]{1,0:T(8,128)(2,1)S(1)}, u32[]{:S(2)}, u32[]{:S(2)}) collective-permute-start(bf16[64,256]{1,0:T(8,128)(2,1)S(1)} %get-tuple-element.58), channel_id=1, source_target_pairs={{0,12},{4,8},{8,4},{12,0},{1,13},{5,9},{9,5},{13,1},{2,14},{6,10},... | collective-permute-start | bytes 98312 | tf_op jit(solution)/shard_map/ppermute | solution.py:334
  47.1 2.3 %collective-permute-done.11.b_ref = bf16[64,256]{1,0:T(8,128)(2,1)S(1)} collective-permute-done((bf16[64,256]{1,0:T(8,128)(2,1)S(1)}, bf16[64,256]{1,0:T(8,128)(2,1)S(1)}, u32[]{:S(2)}, u32[]{:S(2)}) %collective-permute-start.11) | collective-permute-done | bytes 32800 | tf_op jit(solution)/shard_map/ppermute | solution.py:334
  49.4 1.2 %shard_map.74 = (bf16[64,8,128]{2,1,0:T(8,128)(2,1)}, f32[8,128]{1,0:T(8,128)S(1)}) custom-call(bf16[8,64,256]{2,1,0:T(8,128)(2,1)S(1)} %get-tuple-element.56.g_ref, bf16[64,256]{1,0:T(8,128)(2,1)S(1)} %collective-permute-done.10.a_ref, bf16[64,256]{1,0:T(8,128)(2,1)S(1)} %collective-permute-done.11.b_ref, bf16[192,192]{1,0:T(8,128)(2,1)S(1)} %reshape.44.w_ref), custom_call_target="tpu_custom_call" | custom-call | flops 150994944 | bytes 536576 | tf_op jit(solution)/shard_map/pallas_call | solution.py:30
  50.7 1.6 %collective-permute-done.17.other_ref = bf16[656,256]{1,0:T(8,128)(2,1)S(1)} collective-permute-done((bf16[656,256]{1,0:T(8,128)(2,1)S(1)}, bf16[656,256]{1,0:T(8,128)(2,1)S(1)}, u32[]{:S(2)}, u32[]{:S(2)}) %collective-permute-start.17) | collective-permute-done | bytes 335904 | tf_op jit(solution)/shard_map/ppermute | solution.py:330
  52.4 1.3 %shard_map.79 = (f32[3,192,64]{2,1,0:T(8,128)}, f32[1152,256]{1,0:T(8,128)}) custom-call(bf16[656,256]{1,0:T(8,128)(2,1)S(1)} %shard_map.78.mine_ref, bf16[656,256]{1,0:T(8,128)(2,1)S(1)} %collective-permute-done.17.other_ref), custom_call_target="tpu_custom_call" | custom-call | flops 1 | bytes 1998848 | tf_op jit(solution)/shard_map/pallas_call | solution.py:30
  (43 shorter events, 7.4 us)
Async XLA Ops:
  0.6 23.3 %copy-start.2 = (bf16[128,3,3,256]{3,0,2,1:T(8,128)(2,1)S(1)}, bf16[128,3,3,256]{3,0,2,1:T(8,128)(2,1)}, u32[]{:S(2)}) copy-start(bf16[128,3,3,256]{3,0,2,1:T(8,128)(2,1)} %param.6) | copy-start | bytes 1769476
  1.7 6.6 %collective-permute-start = (bf16[64,128]{1,0:T(8,128)(2,1)S(1)}, bf16[64,128]{1,0:T(8,128)(2,1)S(1)}, u32[]{:S(2)}, u32[]{:S(2)}) collective-permute-start(bf16[64,128]{1,0:T(8,128)(2,1)S(1)} %get-tuple-element.68), channel_id=1, source_target_pairs={{0,4},{4,0},{8,12},{12,8},{1,5},{5,1},{9,13},{13,9},{2,6},{6,2},{1... | collective-permute-start | bytes 49160 | tf_op jit(solution)/shard_map/ppermute | solution.py:330
  4.7 5.5 %collective-permute-start.1 = (bf16[64,128]{1,0:T(8,128)(2,1)S(1)}, bf16[64,128]{1,0:T(8,128)(2,1)S(1)}, u32[]{:S(2)}, u32[]{:S(2)}) collective-permute-start(bf16[64,128]{1,0:T(8,128)(2,1)S(1)} %get-tuple-element.67), channel_id=1, source_target_pairs={{0,12},{4,8},{8,4},{12,0},{1,13},{5,9},{9,5},{13,1},{2,14},{6,10},... | collective-permute-start | bytes 49160 | tf_op jit(solution)/shard_map/ppermute | solution.py:334
  10.4 3.8 %collective-permute-start.2 = (bf16[144,128]{1,0:T(8,128)(2,1)S(1)}, bf16[144,128]{1,0:T(8,128)(2,1)S(1)}, u32[]{:S(2)}, u32[]{:S(2)}) collective-permute-start(bf16[144,128]{1,0:T(8,128)(2,1)S(1)} %get-tuple-element.37), channel_id=1, source_target_pairs={{0,3},{1,2},{2,1},{3,0},{4,7},{5,6},{6,5},{7,4},{8,11},{9,10},{10,... | collective-permute-start | bytes 110600 | tf_op jit(solution)/shard_map/ppermute | solution.py:334
  10.4 3.7 %collective-permute-start.3 = (bf16[144,128]{1,0:T(8,128)(2,1)S(1)}, bf16[144,128]{1,0:T(8,128)(2,1)S(1)}, u32[]{:S(2)}, u32[]{:S(2)}) collective-permute-start(bf16[144,128]{1,0:T(8,128)(2,1)S(1)} %get-tuple-element.38), channel_id=1, source_target_pairs={{0,1},{1,0},{2,3},{3,2},{4,5},{5,4},{6,7},{7,6},{8,9},{9,8},{10,11... | collective-permute-start | bytes 110600 | tf_op jit(solution)/shard_map/ppermute | solution.py:330
  12.0 0.9 %copy-start = (bf16[64,3,3,64]{3,0,2,1:T(8,128)(2,1)S(1)}, bf16[64,3,3,64]{3,0,2,1:T(8,128)(2,1)}, u32[]{:S(2)}) copy-start(bf16[64,3,3,64]{3,0,2,1:T(8,128)(2,1)} %param.5) | copy-start | bytes 221188
  15.0 4.5 %collective-permute-start.4 = (bf16[2,40,256]{2,1,0:T(8,128)(2,1)S(1)}, bf16[2,40,256]{2,1,0:T(8,128)(2,1)S(1)}, u32[]{:S(2)}, u32[]{:S(2)}) collective-permute-start(bf16[2,40,256]{2,1,0:T(8,128)(2,1)S(1)} %get-tuple-element.44.refs_0_), channel_id=1, source_target_pairs={{0,4},{4,0},{8,12},{12,8},{1,5},{5,1},{9,13},{13,9},{2,6},{6,2},{1... | collective-permute-start | bytes 122888 | tf_op jit(solution)/shard_map/ppermute | solution.py:338
  15.1 5.6 %collective-permute-start.5 = (bf16[2,40,256]{2,1,0:T(8,128)(2,1)S(1)}, bf16[2,40,256]{2,1,0:T(8,128)(2,1)S(1)}, u32[]{:S(2)}, u32[]{:S(2)}) collective-permute-start(bf16[2,40,256]{2,1,0:T(8,128)(2,1)S(1)} %get-tuple-element.44.refs_0_), channel_id=1, source_target_pairs={{0,8},{4,12},{8,0},{12,4},{1,9},{5,13},{9,1},{13,5},{2,10},{6,14},... | collective-permute-start | bytes 122888 | tf_op jit(solution)/shard_map/ppermute | solution.py:338
  18.1 5.8 %collective-permute-start.6 = (bf16[2,40,256]{2,1,0:T(8,128)(2,1)S(1)}, bf16[2,40,256]{2,1,0:T(8,128)(2,1)S(1)}, u32[]{:S(2)}, u32[]{:S(2)}) collective-permute-start(bf16[2,40,256]{2,1,0:T(8,128)(2,1)S(1)} %get-tuple-element.44.refs_0_), channel_id=1, source_target_pairs={{0,12},{4,8},{8,4},{12,0},{1,13},{5,9},{9,5},{13,1},{2,14},{6,10},... | collective-permute-start | bytes 122888 | tf_op jit(solution)/shard_map/ppermute | solution.py:338
  25.0 5.1 %collective-permute-start.7 = (bf16[72,256]{1,0:T(8,128)(2,1)S(1)}, bf16[72,256]{1,0:T(8,128)(2,1)S(1)}, u32[]{:S(2)}, u32[]{:S(2)}) collective-permute-start(bf16[72,256]{1,0:T(8,128)(2,1)S(1)} %get-tuple-element.46), channel_id=1, source_target_pairs={{0,4},{4,0},{8,12},{12,8},{1,5},{5,1},{9,13},{13,9},{2,6},{6,2},{1... | collective-permute-start | bytes 110600 | tf_op jit(solution)/shard_map/ppermute | solution.py:338
  25.0 5.3 %collective-permute-start.8 = (bf16[72,256]{1,0:T(8,128)(2,1)S(1)}, bf16[72,256]{1,0:T(8,128)(2,1)S(1)}, u32[]{:S(2)}, u32[]{:S(2)}) collective-permute-start(bf16[72,256]{1,0:T(8,128)(2,1)S(1)} %get-tuple-element.47), channel_id=1, source_target_pairs={{0,8},{4,12},{8,0},{12,4},{1,9},{5,13},{9,1},{13,5},{2,10},{6,14},... | collective-permute-start | bytes 110600 | tf_op jit(solution)/shard_map/ppermute | solution.py:338
  26.9 5.8 %collective-permute-start.9 = (bf16[72,256]{1,0:T(8,128)(2,1)S(1)}, bf16[72,256]{1,0:T(8,128)(2,1)S(1)}, u32[]{:S(2)}, u32[]{:S(2)}) collective-permute-start(bf16[72,256]{1,0:T(8,128)(2,1)S(1)} %get-tuple-element.48), channel_id=1, source_target_pairs={{0,12},{4,8},{8,4},{12,0},{1,13},{5,9},{9,5},{13,1},{2,14},{6,10},... | collective-permute-start | bytes 110600 | tf_op jit(solution)/shard_map/ppermute | solution.py:338
  32.7 14.0 %copy-start.1 = (bf16[64,3,3,64]{3,0,2,1:T(8,128)(2,1)S(1)}, bf16[64,3,3,64]{3,0,2,1:T(8,128)(2,1)}, u32[]{:S(2)}) copy-start(bf16[64,3,3,64]{3,0,2,1:T(8,128)(2,1)} %param.5) | copy-start | bytes 221188
  33.6 1.7 %collective-permute-start.12 = (bf16[656,256]{1,0:T(8,128)(2,1)S(1)}, bf16[656,256]{1,0:T(8,128)(2,1)S(1)}, u32[]{:S(2)}, u32[]{:S(2)}) collective-permute-start(bf16[656,256]{1,0:T(8,128)(2,1)S(1)} %get-tuple-element.61), channel_id=1, source_target_pairs={{0,1},{1,0},{2,3},{3,2},{4,5},{5,4},{6,7},{7,6},{8,9},{9,8},{10,11... | collective-permute-start | bytes 1007624 | tf_op jit(solution)/shard_map/ppermute | solution.py:330
  35.4 15.2 %collective-permute-start.13 = (bf16[576,256]{1,0:T(8,128)(2,1)S(1)}, bf16[576,256]{1,0:T(8,128)(2,1)S(1)}, u32[]{:S(2)}, u32[]{:S(2)}) collective-permute-start(bf16[576,256]{1,0:T(8,128)(2,1)S(1)} %get-tuple-element.62.a_ref), channel_id=1, source_target_pairs={{0,2},{2,0},{1,3},{3,1},{4,6},{6,4},{5,7},{7,5},{8,10},{10,8},{9,1... | collective-permute-start | bytes 884744 | tf_op jit(solution)/shard_map/ppermute | solution.py:338
  36.6 4.0 %collective-permute-start.14 = (bf16[80,256]{1,0:T(8,128)(2,1)S(1)}, bf16[80,256]{1,0:T(8,128)(2,1)S(1)}, u32[]{:S(2)}, u32[]{:S(2)}) collective-permute-start(bf16[80,256]{1,0:T(8,128)(2,1)S(1)} %get-tuple-element.63.a_ref), channel_id=1, source_target_pairs={{0,4},{4,0},{8,12},{12,8},{1,5},{5,1},{9,13},{13,9},{2,6},{6,2},{1... | collective-permute-start | bytes 122888 | tf_op jit(solution)/shard_map/ppermute | solution.py:338
  40.6 5.2 %collective-permute-start.15 = (bf16[80,256]{1,0:T(8,128)(2,1)S(1)}, bf16[80,256]{1,0:T(8,128)(2,1)S(1)}, u32[]{:S(2)}, u32[]{:S(2)}) collective-permute-start(bf16[80,256]{1,0:T(8,128)(2,1)S(1)} %shard_map.76.a_ref), channel_id=1, source_target_pairs={{0,8},{4,12},{8,0},{12,4},{1,9},{5,13},{9,1},{13,5},{2,10},{6,14},... | collective-permute-start | bytes 122888 | tf_op jit(solution)/shard_map/ppermute | solution.py:338
  41.7 5.4 %collective-permute-start.10 = (bf16[64,256]{1,0:T(8,128)(2,1)S(1)}, bf16[64,256]{1,0:T(8,128)(2,1)S(1)}, u32[]{:S(2)}, u32[]{:S(2)}) collective-permute-start(bf16[64,256]{1,0:T(8,128)(2,1)S(1)} %get-tuple-element.57), channel_id=1, source_target_pairs={{0,4},{4,0},{8,12},{12,8},{1,5},{5,1},{9,13},{13,9},{2,6},{6,2},{1... | collective-permute-start | bytes 98312 | tf_op jit(solution)/shard_map/ppermute | solution.py:330
  43.7 5.7 %collective-permute-start.11 = (bf16[64,256]{1,0:T(8,128)(2,1)S(1)}, bf16[64,256]{1,0:T(8,128)(2,1)S(1)}, u32[]{:S(2)}, u32[]{:S(2)}) collective-permute-start(bf16[64,256]{1,0:T(8,128)(2,1)S(1)} %get-tuple-element.58), channel_id=1, source_target_pairs={{0,12},{4,8},{8,4},{12,0},{1,13},{5,9},{9,5},{13,1},{2,14},{6,10},... | collective-permute-start | bytes 98312 | tf_op jit(solution)/shard_map/ppermute | solution.py:334
  45.8 4.8 %collective-permute-start.16 = (bf16[80,256]{1,0:T(8,128)(2,1)S(1)}, bf16[80,256]{1,0:T(8,128)(2,1)S(1)}, u32[]{:S(2)}, u32[]{:S(2)}) collective-permute-start(bf16[80,256]{1,0:T(8,128)(2,1)S(1)} %shard_map.77.c_ref), channel_id=1, source_target_pairs={{0,2},{2,0},{1,3},{3,1},{4,6},{6,4},{5,7},{7,5},{8,10},{10,8},{9,1... | collective-permute-start | bytes 122888 | tf_op jit(solution)/shard_map/ppermute | solution.py:338
  50.7 1.7 %collective-permute-start.17 = (bf16[656,256]{1,0:T(8,128)(2,1)S(1)}, bf16[656,256]{1,0:T(8,128)(2,1)S(1)}, u32[]{:S(2)}, u32[]{:S(2)}) collective-permute-start(bf16[656,256]{1,0:T(8,128)(2,1)S(1)} %shard_map.78.mine_ref), channel_id=1, source_target_pairs={{0,1},{1,0},{2,3},{3,2},{4,5},{5,4},{6,7},{7,6},{8,9},{9,8},{10,11... | collective-permute-start | bytes 1007624 | tf_op jit(solution)/shard_map/ppermute | solution.py:330

commit v9 on v8

--- a/solution.py
+++ b/solution.py
@@ -21,7 +21,7 @@
     return lax.dot_general(a, b, ((contract[:1], contract[1:]), ((), ())), preferred_element_type=F32)
 
 
-def whole_call(body, outs, operands, flops, scratch=(), after=0, out_space=pltpu.VMEM):
+def whole_call(body, outs, operands, flops, scratch=(), after=0, out_spaces=None):
     specs = [
         pl.BlockSpec(memory_space=pltpu.VMEM) for _ in range(len(operands) - after)
     ] + [pl.BlockSpec(memory_space=pl.ANY)] * after
@@ -31,7 +31,7 @@
         body,
         out_shape=outs,
         in_specs=specs,
-        out_specs=[pl.BlockSpec(memory_space=out_space) for _ in outs],
+        out_specs=[pl.BlockSpec(memory_space=space) for space in out_spaces or [pltpu.VMEM] * len(outs)],
         scratch_shapes=list(scratch),
         cost_estimate=pl.CostEstimate(flops=flops, bytes_accessed=moved, transcendentals=0),
         compiler_params=pltpu.CompilerParams(vmem_limit_bytes=40 * 1024 * 1024),
@@ -248,12 +248,6 @@
     one_ref[...] = total[half:]
 
 
-def add_joined(a_ref, b_ref, c_ref, d_ref, _, out_ref):
-    half = a_ref.shape[0]
-    out_ref[:half] = (a_ref[...].astype(F32) + b_ref[...].astype(F32)).astype(BF16)
-    out_ref[half:] = (c_ref[...].astype(F32) + d_ref[...].astype(F32)).astype(BF16)
-
-
 def grad_pre_one(*refs, bands):
     terms, refs = refs[:bands], refs[bands:]
     slope_ref, wide_ref, pool_ref, order_ref, keep_two_ref, send_two_ref, *refs = refs
@@ -305,33 +299,57 @@
     out_ref[...] = jnp.swapaxes(jnp.stack(rows, 0), 0, 1).astype(BF16)
 
 
-def finish(mine_ref, other_ref, one_hbm, two_hbm, one_ref, two_ref, flat_ref, sems, *, scales):
-    pair, half = lax.axis_index("pair"), mine_ref.shape[0] - TAIL
-    copies = [pltpu.make_async_copy(one_ref, one_hbm, sems.at[0])]
-    for ref, place in ((mine_ref, pair), (other_ref, 1 - pair)):
-        flat_ref[pl.ds(pl.multiple_of(place * 72, 8), 72)] = ref[half : half + 72].astype(F32) * scales[0]
-    one_ref[0, :96] = flat_ref[:96, :64]
-    one_ref[1, :96] = flat_ref[:96, 64:128]
-    one_ref[0, 96:] = flat_ref[:96, 128:192]
-    one_ref[1, 96:] = flat_ref[:96, 192:]
-    for q in range(4):
-        one_ref[2, 48 * q : 48 * q + 48] = flat_ref[96:, 64 * q : 64 * q + 64]
-    copies[0].start()
+def finish_two(mine_ref, other_ref, two_hbm, done_ref, two_ref, sems, *, scale):
+    pair, half = lax.axis_index("pair"), mine_ref.shape[0]
+    done_ref[...] = jnp.zeros(done_ref.shape, F32)
+    copies = []
     for n, (ref, place) in enumerate(((mine_ref, pair), (other_ref, 1 - pair))):
         rows = pl.ds(pl.multiple_of(place * half, 16), half)
-        two_ref[n] = ref[:half].astype(F32) * scales[1]
-        copies.append(pltpu.make_async_copy(two_ref.at[n], two_hbm.at[rows], sems.at[1 + n]))
+        two_ref[n] = ref[...].astype(F32) * scale
+        copies.append(pltpu.make_async_copy(two_ref.at[n], two_hbm.at[rows], sems.at[n]))
         copies[-1].start()
     for copy in copies:
         copy.wait()
 
 
+def finish_one(mine_ref, other_ref, _, out_ref, flat_ref, *, scale):
+    pair = lax.axis_index("pair")
+    for ref, place in ((mine_ref, pair), (other_ref, 1 - pair)):
+        flat_ref[pl.ds(pl.multiple_of(place * 72, 8), 72)] = ref[:72].astype(F32) * scale
+    out_ref[0, :96] = flat_ref[:96, :64]
+    out_ref[1, :96] = flat_ref[:96, 64:128]
+    out_ref[0, 96:] = flat_ref[:96, 128:192]
+    out_ref[1, 96:] = flat_ref[:96, 192:]
+    for q in range(4):
+        out_ref[2, 48 * q : 48 * q + 48] = flat_ref[96:, 64 * q : 64 * q + 64]
+
+
 def even_swap(values, axis, count):
     return lax.ppermute(values, axis, [(n, n ^ 1) for n in range(count)])
 
 
-def odd_swap(values, axis, count):
-    return lax.ppermute(values, axis, [(n, (n - 1 if n % 2 == 0 else n + 1) % count) for n in range(count)])
+def odd_partner(place):
+    return place - 1 if place % 2 == 0 else place + 1
+
+
+def odd_row_swap(values):
+    bands, cores = lax.axis_size("row"), lax.axis_size("pair")
+    steps = []
+    for n in range(bands):
+        for p in range(cores):
+            to = (n, p ^ 1) if n in (0, bands - 1) else (odd_partner(n), p)
+            steps.append((n * cores + p, to[0] * cores + to[1]))
+    return lax.ppermute(values, ("row", "pair"), steps)
+
+
+def odd_strip_swap(values):
+    groups, strips = lax.axis_size("grp"), lax.axis_size(COLS)
+    steps = []
+    for g in range(groups):
+        for n in range(strips):
+            to = ((g + 1) % groups, n) if n in (0, strips - 1) else (g, odd_partner(n))
+            steps.append((g * strips + n, to[0] * strips + to[1]))
+    return lax.ppermute(values, ("grp",) + COLS, steps)
 
 
 def xor_swap(values, axis, count, k):
@@ -391,10 +409,10 @@
     to_a, to_b, above, below = whole_call(
         functools.partial(pack_borders, bands=bands),
         [shaped((2 * channels + head.shape[0], 128))] * 2 + [shaped((channels, strip_cols))] * 2,
-        [even_swap(to_a, "row", bands), odd_swap(to_b, "row", bands), own_a, own_b],
+        [even_swap(to_a, "row", bands), odd_row_swap(to_b), own_a, own_b],
         1,
     )
-    side_a, side_b = even_swap(to_a, COLS, strips), odd_swap(to_b, COLS, strips)
+    side_a, side_b = even_swap(to_a, COLS, strips), odd_strip_swap(to_b)
     pooled, slope, wide = whole_call(
         functools.partial(layer_one, strips=strips),
         [
@@ -455,32 +473,27 @@
     input_grad, done = whole_call(
         functools.partial(layer_one_back, bands=bands),
         [shaped(features_in.shape), shaped((8, 128), F32)],
-        [g, even_swap(up_a, "row", bands), odd_swap(up_b, "row", bands), back_one],
+        [g, even_swap(up_a, "row", bands), odd_row_swap(up_b), back_one],
         2 * band_rows * 192 * 192 * 256,
     )
-    one, one_more = sum_but_last(added(one, one_more), "col", columns)
-    (mine,) = whole_call(
-        add_joined,
-        [shaped((half + TAIL, 256))],
-        [two, two_more, one, one_more, done],
-        0,
+    one = added(one, one_more, done)
+    mine_two = added(two, two_more, one)
+    grad_two, done = whole_call(
+        functools.partial(finish_two, scale=1.0 / math.sqrt(pooled_rows * total)),
+        [shaped((2 * half, 256), F32), shaped((8, 128), F32)],
+        [mine_two, even_swap(mine_two, "pair", 2)],
+        10**8,
+        scratch=[pltpu.VMEM((2, half, 256), F32), pltpu.SemaphoreType.DMA((2,))],
+        out_spaces=[pl.ANY, pltpu.VMEM],
+    )
+    mine_one = added(*sum_but_last(one, "col", columns))
+    (grad_one,) = whole_call(
+        functools.partial(finish_one, scale=1.0 / math.sqrt(height * width)),
+        [shaped((3, 3 * channels, channels), F32)],
+        [mine_one, even_swap(mine_one, "pair", 2), done],
+        1,
+        scratch=[pltpu.VMEM((144, 256), F32)],
         after=1,
-    )
-    grad_one, grad_two = whole_call(
-        functools.partial(
-            finish,
-            scales=(1.0 / math.sqrt(height * width), 1.0 / math.sqrt(pooled_rows * total)),
-        ),
-        [shaped((3, 3 * channels, channels), F32), shaped((2 * half, 256), F32)],
-        [mine, even_swap(mine, "pair", 2)],
-        1,
-        scratch=[
-            pltpu.VMEM((3, 3 * channels, channels), F32),
-            pltpu.VMEM((2, half, 256), F32),
-            pltpu.VMEM((144, 256), F32),
-            pltpu.SemaphoreType.DMA((3,)),
-        ],
-        out_space=pl.ANY,
     )
     grad_two = jnp.transpose(grad_two.reshape(3, 3, filters, 4 * channels), (2, 0, 1, 3))
     grad_one = jnp.transpose(grad_one.reshape(3, 3, channels, channels), (2, 0, 1, 3))

time: 53.8 us -> 50 us (0.929)
  waiting for transfers between devices: 20.5 us -> 17.6 us
  starting transfers between devices: 22.8 us -> 21.2 us
  Pallas kernels: 6.32 us -> 6.96 us
    ppermute x3, waiting for transfers between devices: 5.41 us -> 0.84 us  [the longest x1 0.84 us: odd_strip_swap(): return lax.ppermute(values, ('grp',) + COLS, steps)]
    ppermute x10, waiting for transfers between devices: 11.8 us -> 14.3 us  [xor_swap(): return lax.ppermute(values, axis, [(n, n ^ k) for n in range(count)])]
    ppermute x3, starting transfers between devices: 3.88 us -> 2.01 us  [the longest x1 2.01 us: odd_strip_swap(): return lax.ppermute(values, ('grp',) + COLS, steps)]
    ppermute x10, starting transfers between devices: 12.1 us -> 13.8 us  [xor_swap(): return lax.ppermute(values, axis, [(n, n ^ k) for n in range(count)])]
    ppermute x5 -> x6, starting transfers between devices: 6.85 us -> 5.41 us  [even_swap(): return lax.ppermute(values, axis, [(n, n ^ 1) for n in range(count)])]
    ppermute x5 -> x6, waiting for transfers between devices: 3.26 us -> 2.48 us  [even_swap(): return lax.ppermute(values, axis, [(n, n ^ 1) for n in range(count)])]
    pallas_call x13 -> x15, Pallas kernels: 6.32 us -> 6.96 us  [whole_call(): pl.pallas_call(body, out_shape=outs, in_specs=specs, out_specs=[pl.BlockS...]
  transfers between devices with their start and end apart: 18 -> 19, of which waited for: 11 -> 10; matrix products, arithmetic and copies ran while one was open for 2% -> 3% of each run, Pallas kernels for 4% -> 6%
where the time goes in v9:
time: 50 us; the launch traced here: 49.8 us
  starting transfers between devices  21.2 us (42%)
  waiting for transfers between devices  17.6 us (35%)
  Pallas kernels  6.96 us (14%)
  local copies, waits for them, and re-layouts  3.12 us (6%)
  between operations  0.86 us (2%)
    ppermute x10, waiting for transfers between devices, xor_swap(): return lax.ppermute(values, axis, [(n, n ^ k) for n in range(count)])  14.3 us
    ppermute x10, starting transfers between devices, xor_swap(): return lax.ppermute(values, axis, [(n, n ^ k) for n in range(count)])  13.8 us
    pallas_call x15, Pallas kernels, whole_call(): pl.pallas_call(body, out_shape=outs, in_specs=specs, out_specs=[pl.BlockS...  6.96 us
    ppermute x6, starting transfers between devices, even_swap(): return lax.ppermute(values, axis, [(n, n ^ 1) for n in range(count)])  5.41 us
    unnamed x8, local copies, waits for them, and re-layouts  2.75 us
    ppermute x6, waiting for transfers between devices, even_swap(): return lax.ppermute(values, axis, [(n, n ^ 1) for n in range(count)])  2.48 us
    ppermute x1, starting transfers between devices, odd_strip_swap(): return lax.ppermute(values, ('grp',) + COLS, steps)  2.01 us
  transfers between devices with their start and end apart: 19, of which 10 were waited for; matrix products, arithmetic and copies ran while one was open for 3% of the time, Pallas kernels for 6%

profile of v9, /device:TPU:0, one launch (start us, length us, event | category | flops | bytes accessed | tf_op | source)
XLA Modules:
  0.0 49.8 jit_solution(15627946358819711201)
XLA Ops:
  0.7 1.0 %copy.21 = bf16[64,8,128]{2,0,1:T(8,128)(2,1)S(1)} copy(bf16[64,8,128]{2,1,0:T(8,128)(2,1)} %param.4) | data formatting | bytes 262144 | tf_op args[0]
  1.7 3.1 %collective-permute-start = (bf16[64,128]{1,0:T(8,128)(2,1)S(1)}, bf16[64,128]{1,0:T(8,128)(2,1)S(1)}, u32[]{:S(2)}, u32[]{:S(2)}) collective-permute-start(bf16[64,128]{1,0:T(8,128)(2,1)S(1)} %get-tuple-element.68), channel_id=1, source_target_pairs={{0,4},{4,0},{8,12},{12,8},{1,5},{5,1},{9,13},{13,9},{2,6},{6,2},{1... | collective-permute-start | bytes 49160 | tf_op jit(solution)/shard_map/ppermute | solution.py:328
  6.6 2.0 %collective-permute-start.2 = (bf16[144,128]{1,0:T(8,128)(2,1)S(1)}, bf16[144,128]{1,0:T(8,128)(2,1)S(1)}, u32[]{:S(2)}, u32[]{:S(2)}) collective-permute-start(bf16[144,128]{1,0:T(8,128)(2,1)S(1)} %get-tuple-element.37), channel_id=1, source_target_pairs={{0,16},{1,2},{2,1},{3,19},{16,0},{17,18},{18,17},{19,3},{4,20},{5,... | collective-permute-start | bytes 110600 | tf_op jit(solution)/shard_map/ppermute | solution.py:352
  8.7 0.9 %copy-done = bf16[64,3,3,64]{3,0,2,1:T(8,128)(2,1)S(1)} copy-done((bf16[64,3,3,64]{3,0,2,1:T(8,128)(2,1)S(1)}, bf16[64,3,3,64]{3,0,2,1:T(8,128)(2,1)}, u32[]{:S(2)}) %copy-start) | copy-done | bytes 73752
  10.6 0.9 %shard_map.70 = (bf16[2,40,256]{2,1,0:T(8,128)(2,1)S(1)}, bf16[8,64,256]{2,1,0:T(8,128)(2,1)S(1)}, bf16[10,64,256]{2,1,0:T(8,128)(2,1)S(1)}) custom-call(bf16[8,64,128]{2,1,0:T(8,128)(2,1)S(1)} %bitcast.36, bf16[64,128]{1,0:T(8,128)(2,1)S(1)} %get-tuple-element.39.above_ref, bf16[64,128]{1,0:T(8,128)(2,1)S(1)} %get-tuple-element.40.below_ref, ...), custom_call_target="tpu_custom_call" | custom-call | flops 150994944 | bytes 1122304 | tf_op jit(solution)/shard_map/pallas_call | solution.py:30
  11.4 3.2 %collective-permute-start.4 = (bf16[2,40,256]{2,1,0:T(8,128)(2,1)S(1)}, bf16[2,40,256]{2,1,0:T(8,128)(2,1)S(1)}, u32[]{:S(2)}, u32[]{:S(2)}) collective-permute-start(bf16[2,40,256]{2,1,0:T(8,128)(2,1)S(1)} %get-tuple-element.44.refs_0_), channel_id=1, source_target_pairs={{0,4},{4,0},{8,12},{12,8},{1,5},{5,1},{9,13},{13,9},{2,6},{6,2},{1... | collective-permute-start | bytes 122888 | tf_op jit(solution)/shard_map/ppermute | solution.py:356
  14.7 1.5 %collective-permute-start.5 = (bf16[2,40,256]{2,1,0:T(8,128)(2,1)S(1)}, bf16[2,40,256]{2,1,0:T(8,128)(2,1)S(1)}, u32[]{:S(2)}, u32[]{:S(2)}) collective-permute-start(bf16[2,40,256]{2,1,0:T(8,128)(2,1)S(1)} %get-tuple-element.44.refs_0_), channel_id=1, source_target_pairs={{0,8},{4,12},{8,0},{12,4},{1,9},{5,13},{9,1},{13,5},{2,10},{6,14},... | collective-permute-start | bytes 122888 | tf_op jit(solution)/shard_map/ppermute | solution.py:356
  16.2 1.4 %collective-permute-start.6 = (bf16[2,40,256]{2,1,0:T(8,128)(2,1)S(1)}, bf16[2,40,256]{2,1,0:T(8,128)(2,1)S(1)}, u32[]{:S(2)}, u32[]{:S(2)}) collective-permute-start(bf16[2,40,256]{2,1,0:T(8,128)(2,1)S(1)} %get-tuple-element.44.refs_0_), channel_id=1, source_target_pairs={{0,12},{4,8},{8,4},{12,0},{1,13},{5,9},{9,5},{13,1},{2,14},{6,10},... | collective-permute-start | bytes 122888 | tf_op jit(solution)/shard_map/ppermute | solution.py:356
  17.7 3.0 %collective-permute-done.5.refs_2_ = bf16[2,40,256]{2,1,0:T(8,128)(2,1)S(1)} collective-permute-done((bf16[2,40,256]{2,1,0:T(8,128)(2,1)S(1)}, bf16[2,40,256]{2,1,0:T(8,128)(2,1)S(1)}, u32[]{:S(2)}, u32[]{:S(2)}) %collective-permute-start.5) | collective-permute-done | bytes 40992 | tf_op jit(solution)/shard_map/ppermute | solution.py:356
  20.7 1.4 %collective-permute-done.6.refs_3_ = bf16[2,40,256]{2,1,0:T(8,128)(2,1)S(1)} collective-permute-done((bf16[2,40,256]{2,1,0:T(8,128)(2,1)S(1)}, bf16[2,40,256]{2,1,0:T(8,128)(2,1)S(1)}, u32[]{:S(2)}, u32[]{:S(2)}) %collective-permute-start.6) | collective-permute-done | bytes 40992 | tf_op jit(solution)/shard_map/ppermute | solution.py:356
  22.0 1.0 %shard_map.71 = (bf16[72,256]{1,0:T(8,128)(2,1)S(1)}, bf16[72,256]{1,0:T(8,128)(2,1)S(1)}, bf16[72,256]{1,0:T(8,128)(2,1)S(1)}, bf16[72,256]{1,0:T(8,128)(2,1)S(...) custom-call(bf16[8,48,128]{2,1,0:T(8,128)(2,1)S(1)} %fusion.6.og_ref, ...), custom_call_target="tpu_custom_call" | custom-call | flops 452984832 | bytes 1368064 | tf_op jit(solution)/shard_map/pallas_call | solution.py:30
  23.2 1.8 %collective-permute-start.8 = (bf16[72,256]{1,0:T(8,128)(2,1)S(1)}, bf16[72,256]{1,0:T(8,128)(2,1)S(1)}, u32[]{:S(2)}, u32[]{:S(2)}) collective-permute-start(bf16[72,256]{1,0:T(8,128)(2,1)S(1)} %get-tuple-element.47), channel_id=1, source_target_pairs={{0,8},{4,12},{8,0},{12,4},{1,9},{5,13},{9,1},{13,5},{2,10},{6,14},... | collective-permute-start | bytes 110600 | tf_op jit(solution)/shard_map/ppermute | solution.py:356
  25.1 2.4 %collective-permute-start.9 = (bf16[72,256]{1,0:T(8,128)(2,1)S(1)}, bf16[72,256]{1,0:T(8,128)(2,1)S(1)}, u32[]{:S(2)}, u32[]{:S(2)}) collective-permute-start(bf16[72,256]{1,0:T(8,128)(2,1)S(1)} %get-tuple-element.48), channel_id=1, source_target_pairs={{0,12},{4,8},{8,4},{12,0},{1,13},{5,9},{9,5},{13,1},{2,14},{6,10},... | collective-permute-start | bytes 110600 | tf_op jit(solution)/shard_map/ppermute | solution.py:356
  28.1 2.7 %collective-permute-done.9.refs_3_ = bf16[72,256]{1,0:T(8,128)(2,1)S(1)} collective-permute-done((bf16[72,256]{1,0:T(8,128)(2,1)S(1)}, bf16[72,256]{1,0:T(8,128)(2,1)S(1)}, u32[]{:S(2)}, u32[]{:S(2)}) %collective-permute-start.9) | collective-permute-done | bytes 36896 | tf_op jit(solution)/shard_map/ppermute | solution.py:356
  31.8 1.6 %collective-permute-done.12.b_ref = bf16[656,256]{1,0:T(8,128)(2,1)S(1)} collective-permute-done((bf16[656,256]{1,0:T(8,128)(2,1)S(1)}, bf16[656,256]{1,0:T(8,128)(2,1)S(1)}, u32[]{:S(2)}, u32[]{:S(2)}) %collective-permute-start.12) | collective-permute-done | bytes 335904 | tf_op jit(solution)/shard_map/ppermute | solution.py:328
  33.5 0.9 %collective-permute-start.17 = (bf16[576,256]{1,0:T(8,128)(2,1)S(1)}, bf16[576,256]{1,0:T(8,128)(2,1)S(1)}, u32[]{:S(2)}, u32[]{:S(2)}) collective-permute-start(bf16[576,256]{1,0:T(8,128)(2,1)S(1)} %get-tuple-element.64.a_ref), channel_id=1, source_target_pairs={{0,2},{2,0},{1,3},{3,1},{4,6},{6,4},{5,7},{7,5},{8,10},{10,8},{9,1... | collective-permute-start | bytes 884744 | tf_op jit(solution)/shard_map/ppermute | solution.py:356
  34.4 2.0 %collective-permute-start.10 = (bf16[64,256]{1,0:T(8,128)(2,1)S(1)}, bf16[64,256]{1,0:T(8,128)(2,1)S(1)}, u32[]{:S(2)}, u32[]{:S(2)}) collective-permute-start(bf16[64,256]{1,0:T(8,128)(2,1)S(1)} %get-tuple-element.57), channel_id=1, source_target_pairs={{0,4},{4,0},{8,12},{12,8},{1,5},{5,1},{9,13},{13,9},{2,6},{6,2},{1... | collective-permute-start | bytes 98312 | tf_op jit(solution)/shard_map/ppermute | solution.py:328
  36.5 2.0 %collective-permute-done.13.b_ref = bf16[80,256]{1,0:T(8,128)(2,1)S(1)} collective-permute-done((bf16[80,256]{1,0:T(8,128)(2,1)S(1)}, bf16[80,256]{1,0:T(8,128)(2,1)S(1)}, u32[]{:S(2)}, u32[]{:S(2)}) %collective-permute-start.13) | collective-permute-done | bytes 40992 | tf_op jit(solution)/shard_map/ppermute | solution.py:356
  38.5 1.1 %collective-permute-start.14 = (bf16[80,256]{1,0:T(8,128)(2,1)S(1)}, bf16[80,256]{1,0:T(8,128)(2,1)S(1)}, u32[]{:S(2)}, u32[]{:S(2)}) collective-permute-start(bf16[80,256]{1,0:T(8,128)(2,1)S(1)} %shard_map.76.a_ref), channel_id=1, source_target_pairs={{0,8},{4,12},{8,0},{12,4},{1,9},{5,13},{9,1},{13,5},{2,10},{6,14},... | collective-permute-start | bytes 122888 | tf_op jit(solution)/shard_map/ppermute | solution.py:356
  39.9 1.2 %shard_map.74 = (bf16[64,8,128]{2,1,0:T(8,128)(2,1)}, f32[8,128]{1,0:T(8,128)S(1)}) custom-call(bf16[8,64,256]{2,1,0:T(8,128)(2,1)S(1)} %get-tuple-element.56.g_ref, bf16[64,256]{1,0:T(8,128)(2,1)S(1)} %collective-permute-done.10.a_ref, bf16[64,256]{1,0:T(8,128)(2,1)S(1)} %collective-permute-done.11.b_ref, bf16[192,192]{1,0:T(8,128)(2,1)S(1)} %reshape.44.w_ref), custom_call_target="tpu_custom_call" | custom-call | flops 150994944 | bytes 536576 | tf_op jit(solution)/shard_map/pallas_call | solution.py:30
  41.1 2.4 %collective-permute-done.14.b_ref = bf16[80,256]{1,0:T(8,128)(2,1)S(1)} collective-permute-done((bf16[80,256]{1,0:T(8,128)(2,1)S(1)}, bf16[80,256]{1,0:T(8,128)(2,1)S(1)}, u32[]{:S(2)}, u32[]{:S(2)}) %collective-permute-start.14) | collective-permute-done | bytes 40992 | tf_op jit(solution)/shard_map/ppermute | solution.py:356
  43.6 1.2 %collective-permute-start.15 = (bf16[80,256]{1,0:T(8,128)(2,1)S(1)}, bf16[80,256]{1,0:T(8,128)(2,1)S(1)}, u32[]{:S(2)}, u32[]{:S(2)}) collective-permute-start(bf16[80,256]{1,0:T(8,128)(2,1)S(1)} %shard_map.77.a_ref.refs_0_), channel_id=1, source_target_pairs={{0,2},{2,0},{1,3},{3,1},{4,6},{6,4},{5,7},{7,5},{8,10},{10,8},{9,1... | collective-permute-start | bytes 122888 | tf_op jit(solution)/shard_map/ppermute | solution.py:356
  44.8 2.9 %collective-permute-done.15.b_ref = bf16[80,256]{1,0:T(8,128)(2,1)S(1)} collective-permute-done((bf16[80,256]{1,0:T(8,128)(2,1)S(1)}, bf16[80,256]{1,0:T(8,128)(2,1)S(1)}, u32[]{:S(2)}, u32[]{:S(2)}) %collective-permute-start.15) | collective-permute-done | bytes 40992 | tf_op jit(solution)/shard_map/ppermute | solution.py:356
  47.8 1.1 %shard_map.80 = (f32[1152,256]{1,0:T(8,128)}, f32[8,128]{1,0:T(8,128)S(1)}) custom-call(bf16[576,256]{1,0:T(8,128)(2,1)S(1)} %shard_map.79.mine_ref, bf16[576,256]{1,0:T(8,128)(2,1)S(1)} %collective-permute-done.18.other_ref), custom_call_target="tpu_custom_call" | custom-call | flops 100000000 | bytes 1773568 | tf_op jit(solution)/shard_map/pallas_call | solution.py:30
  (47 shorter events, 6.4 us)
Async XLA Ops:
  0.6 21.4 %copy-start.2 = (bf16[128,3,3,256]{3,0,2,1:T(8,128)(2,1)S(1)}, bf16[128,3,3,256]{3,0,2,1:T(8,128)(2,1)}, u32[]{:S(2)}) copy-start(bf16[128,3,3,256]{3,0,2,1:T(8,128)(2,1)} %param.6) | copy-start | bytes 1769476
  1.7 4.8 %collective-permute-start = (bf16[64,128]{1,0:T(8,128)(2,1)S(1)}, bf16[64,128]{1,0:T(8,128)(2,1)S(1)}, u32[]{:S(2)}, u32[]{:S(2)}) collective-permute-start(bf16[64,128]{1,0:T(8,128)(2,1)S(1)} %get-tuple-element.68), channel_id=1, source_target_pairs={{0,4},{4,0},{8,12},{12,8},{1,5},{5,1},{9,13},{13,9},{2,6},{6,2},{1... | collective-permute-start | bytes 49160 | tf_op jit(solution)/shard_map/ppermute | solution.py:328
  4.7 1.7 %collective-permute-start.1 = (bf16[64,128]{1,0:T(8,128)(2,1)S(1)}, bf16[64,128]{1,0:T(8,128)(2,1)S(1)}, u32[]{:S(2)}, u32[]{:S(2)}) collective-permute-start(bf16[64,128]{1,0:T(8,128)(2,1)S(1)} %get-tuple-element.67), channel_id=1, source_target_pairs={{0,1},{1,0},{4,8},{5,9},{8,4},{9,5},{12,13},{13,12},{2,3},{3,2},{6... | collective-permute-start | bytes 49160 | tf_op jit(solution)/shard_map/ppermute | solution.py:342
  6.6 4.0 %collective-permute-start.2 = (bf16[144,128]{1,0:T(8,128)(2,1)S(1)}, bf16[144,128]{1,0:T(8,128)(2,1)S(1)}, u32[]{:S(2)}, u32[]{:S(2)}) collective-permute-start(bf16[144,128]{1,0:T(8,128)(2,1)S(1)} %get-tuple-element.37), channel_id=1, source_target_pairs={{0,16},{1,2},{2,1},{3,19},{16,0},{17,18},{18,17},{19,3},{4,20},{5,... | collective-permute-start | bytes 110600 | tf_op jit(solution)/shard_map/ppermute | solution.py:352
  8.6 2.0 %collective-permute-start.3 = (bf16[144,128]{1,0:T(8,128)(2,1)S(1)}, bf16[144,128]{1,0:T(8,128)(2,1)S(1)}, u32[]{:S(2)}, u32[]{:S(2)}) collective-permute-start(bf16[144,128]{1,0:T(8,128)(2,1)S(1)} %get-tuple-element.38), channel_id=1, source_target_pairs={{0,1},{1,0},{2,3},{3,2},{4,5},{5,4},{6,7},{7,6},{8,9},{9,8},{10,11... | collective-permute-start | bytes 110600 | tf_op jit(solution)/shard_map/ppermute | solution.py:328
  8.7 0.9 %copy-start = (bf16[64,3,3,64]{3,0,2,1:T(8,128)(2,1)S(1)}, bf16[64,3,3,64]{3,0,2,1:T(8,128)(2,1)}, u32[]{:S(2)}) copy-start(bf16[64,3,3,64]{3,0,2,1:T(8,128)(2,1)} %param.5) | copy-start | bytes 221188
  11.4 6.2 %collective-permute-start.4 = (bf16[2,40,256]{2,1,0:T(8,128)(2,1)S(1)}, bf16[2,40,256]{2,1,0:T(8,128)(2,1)S(1)}, u32[]{:S(2)}, u32[]{:S(2)}) collective-permute-start(bf16[2,40,256]{2,1,0:T(8,128)(2,1)S(1)} %get-tuple-element.44.refs_0_), channel_id=1, source_target_pairs={{0,4},{4,0},{8,12},{12,8},{1,5},{5,1},{9,13},{13,9},{2,6},{6,2},{1... | collective-permute-start | bytes 122888 | tf_op jit(solution)/shard_map/ppermute | solution.py:356
  14.7 6.0 %collective-permute-start.5 = (bf16[2,40,256]{2,1,0:T(8,128)(2,1)S(1)}, bf16[2,40,256]{2,1,0:T(8,128)(2,1)S(1)}, u32[]{:S(2)}, u32[]{:S(2)}) collective-permute-start(bf16[2,40,256]{2,1,0:T(8,128)(2,1)S(1)} %get-tuple-element.44.refs_0_), channel_id=1, source_target_pairs={{0,8},{4,12},{8,0},{12,4},{1,9},{5,13},{9,1},{13,5},{2,10},{6,14},... | collective-permute-start | bytes 122888 | tf_op jit(solution)/shard_map/ppermute | solution.py:356
  16.2 5.8 %collective-permute-start.6 = (bf16[2,40,256]{2,1,0:T(8,128)(2,1)S(1)}, bf16[2,40,256]{2,1,0:T(8,128)(2,1)S(1)}, u32[]{:S(2)}, u32[]{:S(2)}) collective-permute-start(bf16[2,40,256]{2,1,0:T(8,128)(2,1)S(1)} %get-tuple-element.44.refs_0_), channel_id=1, source_target_pairs={{0,12},{4,8},{8,4},{12,0},{1,13},{5,9},{9,5},{13,1},{2,14},{6,10},... | collective-permute-start | bytes 122888 | tf_op jit(solution)/shard_map/ppermute | solution.py:356
  23.0 5.1 %collective-permute-start.7 = (bf16[72,256]{1,0:T(8,128)(2,1)S(1)}, bf16[72,256]{1,0:T(8,128)(2,1)S(1)}, u32[]{:S(2)}, u32[]{:S(2)}) collective-permute-start(bf16[72,256]{1,0:T(8,128)(2,1)S(1)} %get-tuple-element.46), channel_id=1, source_target_pairs={{0,4},{4,0},{8,12},{12,8},{1,5},{5,1},{9,13},{13,9},{2,6},{6,2},{1... | collective-permute-start | bytes 110600 | tf_op jit(solution)/shard_map/ppermute | solution.py:356
  23.2 4.9 %collective-permute-start.8 = (bf16[72,256]{1,0:T(8,128)(2,1)S(1)}, bf16[72,256]{1,0:T(8,128)(2,1)S(1)}, u32[]{:S(2)}, u32[]{:S(2)}) collective-permute-start(bf16[72,256]{1,0:T(8,128)(2,1)S(1)} %get-tuple-element.47), channel_id=1, source_target_pairs={{0,8},{4,12},{8,0},{12,4},{1,9},{5,13},{9,1},{13,5},{2,10},{6,14},... | collective-permute-start | bytes 110600 | tf_op jit(solution)/shard_map/ppermute | solution.py:356
  25.1 5.8 %collective-permute-start.9 = (bf16[72,256]{1,0:T(8,128)(2,1)S(1)}, bf16[72,256]{1,0:T(8,128)(2,1)S(1)}, u32[]{:S(2)}, u32[]{:S(2)}) collective-permute-start(bf16[72,256]{1,0:T(8,128)(2,1)S(1)} %get-tuple-element.48), channel_id=1, source_target_pairs={{0,12},{4,8},{8,4},{12,0},{1,13},{5,9},{9,5},{13,1},{2,14},{6,10},... | collective-permute-start | bytes 110600 | tf_op jit(solution)/shard_map/ppermute | solution.py:356
  28.1 11.4 %copy-start.1 = (bf16[64,3,3,64]{3,0,2,1:T(8,128)(2,1)S(1)}, bf16[64,3,3,64]{3,0,2,1:T(8,128)(2,1)}, u32[]{:S(2)}) copy-start(bf16[64,3,3,64]{3,0,2,1:T(8,128)(2,1)} %param.5) | copy-start | bytes 221188
  31.7 1.7 %collective-permute-start.12 = (bf16[656,256]{1,0:T(8,128)(2,1)S(1)}, bf16[656,256]{1,0:T(8,128)(2,1)S(1)}, u32[]{:S(2)}, u32[]{:S(2)}) collective-permute-start(bf16[656,256]{1,0:T(8,128)(2,1)S(1)} %get-tuple-element.61), channel_id=1, source_target_pairs={{0,1},{1,0},{2,3},{3,2},{4,5},{5,4},{6,7},{7,6},{8,9},{9,8},{10,11... | collective-permute-start | bytes 1007624 | tf_op jit(solution)/shard_map/ppermute | solution.py:328
  33.5 9.9 %collective-permute-start.17 = (bf16[576,256]{1,0:T(8,128)(2,1)S(1)}, bf16[576,256]{1,0:T(8,128)(2,1)S(1)}, u32[]{:S(2)}, u32[]{:S(2)}) collective-permute-start(bf16[576,256]{1,0:T(8,128)(2,1)S(1)} %get-tuple-element.64.a_ref), channel_id=1, source_target_pairs={{0,2},{2,0},{1,3},{3,1},{4,6},{6,4},{5,7},{7,5},{8,10},{10,8},{9,1... | collective-permute-start | bytes 884744 | tf_op jit(solution)/shard_map/ppermute | solution.py:356
  34.4 4.0 %collective-permute-start.13 = (bf16[80,256]{1,0:T(8,128)(2,1)S(1)}, bf16[80,256]{1,0:T(8,128)(2,1)S(1)}, u32[]{:S(2)}, u32[]{:S(2)}) collective-permute-start(bf16[80,256]{1,0:T(8,128)(2,1)S(1)} %get-tuple-element.62.a_ref), channel_id=1, source_target_pairs={{0,4},{4,0},{8,12},{12,8},{1,5},{5,1},{9,13},{13,9},{2,6},{6,2},{1... | collective-permute-start | bytes 122888 | tf_op jit(solution)/shard_map/ppermute | solution.py:356
  34.4 5.4 %collective-permute-start.10 = (bf16[64,256]{1,0:T(8,128)(2,1)S(1)}, bf16[64,256]{1,0:T(8,128)(2,1)S(1)}, u32[]{:S(2)}, u32[]{:S(2)}) collective-permute-start(bf16[64,256]{1,0:T(8,128)(2,1)S(1)} %get-tuple-element.57), channel_id=1, source_target_pairs={{0,4},{4,0},{8,12},{12,8},{1,5},{5,1},{9,13},{13,9},{2,6},{6,2},{1... | collective-permute-start | bytes 98312 | tf_op jit(solution)/shard_map/ppermute | solution.py:328
  36.5 3.4 %collective-permute-start.11 = (bf16[64,256]{1,0:T(8,128)(2,1)S(1)}, bf16[64,256]{1,0:T(8,128)(2,1)S(1)}, u32[]{:S(2)}, u32[]{:S(2)}) collective-permute-start(bf16[64,256]{1,0:T(8,128)(2,1)S(1)} %get-tuple-element.58), channel_id=1, source_target_pairs={{0,1},{1,0},{4,8},{5,9},{8,4},{9,5},{12,13},{13,12},{2,3},{3,2},{6... | collective-permute-start | bytes 98312 | tf_op jit(solution)/shard_map/ppermute | solution.py:342
  38.5 5.0 %collective-permute-start.14 = (bf16[80,256]{1,0:T(8,128)(2,1)S(1)}, bf16[80,256]{1,0:T(8,128)(2,1)S(1)}, u32[]{:S(2)}, u32[]{:S(2)}) collective-permute-start(bf16[80,256]{1,0:T(8,128)(2,1)S(1)} %shard_map.76.a_ref), channel_id=1, source_target_pairs={{0,8},{4,12},{8,0},{12,4},{1,9},{5,13},{9,1},{13,5},{2,10},{6,14},... | collective-permute-start | bytes 122888 | tf_op jit(solution)/shard_map/ppermute | solution.py:356
  43.5 4.2 %collective-permute-start.18 = (bf16[576,256]{1,0:T(8,128)(2,1)S(1)}, bf16[576,256]{1,0:T(8,128)(2,1)S(1)}, u32[]{:S(2)}, u32[]{:S(2)}) collective-permute-start(bf16[576,256]{1,0:T(8,128)(2,1)S(1)} %shard_map.79.mine_ref), channel_id=1, source_target_pairs={{0,1},{1,0},{2,3},{3,2},{4,5},{5,4},{6,7},{7,6},{8,9},{9,8},{10,11... | collective-permute-start | bytes 884744 | tf_op jit(solution)/shard_map/ppermute | solution.py:328
  43.6 4.1 %collective-permute-start.15 = (bf16[80,256]{1,0:T(8,128)(2,1)S(1)}, bf16[80,256]{1,0:T(8,128)(2,1)S(1)}, u32[]{:S(2)}, u32[]{:S(2)}) collective-permute-start(bf16[80,256]{1,0:T(8,128)(2,1)S(1)} %shard_map.77.a_ref.refs_0_), channel_id=1, source_target_pairs={{0,2},{2,0},{1,3},{3,1},{4,6},{6,4},{5,7},{7,5},{8,10},{10,8},{9,1... | collective-permute-start | bytes 122888 | tf_op jit(solution)/shard_map/ppermute | solution.py:356
  47.7 1.3 %collective-permute-start.16 = (bf16[80,256]{1,0:T(8,128)(2,1)S(1)}, bf16[80,256]{1,0:T(8,128)(2,1)S(1)}, u32[]{:S(2)}, u32[]{:S(2)}) collective-permute-start(bf16[80,256]{1,0:T(8,128)(2,1)S(1)} %shard_map.78.mine_ref), channel_id=1, source_target_pairs={{0,1},{1,0},{2,3},{3,2},{4,5},{5,4},{6,7},{7,6},{8,9},{9,8},{10,11... | collective-permute-start | bytes 122888 | tf_op jit(solution)/shard_map/ppermute | solution.py:328

commit v10 on v9

--- a/solution.py
+++ b/solution.py
@@ -192,9 +192,9 @@
     map_ref[0] = jnp.zeros((PITCH, 256), BF16)
     map_ref[rows + 1] = jnp.zeros((PITCH, 256), BF16)
     blank = jnp.zeros((PITCH - SENT, 256), BF16)
-    for k in range(bands):
+    for k, piece in zip(row_order(bands), pieces):
         for t in range(2):
-            map_ref[1 + 2 * (band ^ k) + t] = jnp.concatenate([pieces[k][t], blank], 0)
+            map_ref[1 + 2 * (band ^ k) + t] = jnp.concatenate([piece[t], blank], 0)
     near = jnp.concatenate([map_ref[i : i + rows].reshape(count, 256) for i in range(3)], 1)
     y = dot(near, jnp.concatenate([w_ref[i] for i in range(3)], 1), (1, 1))
     pre = roll(y[:, :filters], 1, 0) + y[:, filters : 2 * filters] + roll(y[:, 2 * filters :], -1, 0)
@@ -239,6 +239,15 @@
 
 def add_after(a_ref, b_ref, *refs):
     refs[-1][...] = (a_ref[...].astype(F32) + b_ref[...].astype(F32)).astype(BF16)
+
+
+def sum_rows(*refs):
+    *refs, _, _, out_ref = refs
+    terms = dict(zip(row_order(len(refs)), (ref[...].astype(F32) for ref in refs)))
+    terms = [terms[k] for k in range(len(refs))]
+    while len(terms) > 1:
+        terms = [a + b for a, b in zip(terms[::2], terms[1::2])]
+    out_ref[...] = terms[0].astype(BF16)
 
 
 def add_halves(a_ref, b_ref, two_ref, one_ref):
@@ -356,10 +365,13 @@
     return lax.ppermute(values, axis, [(n, n ^ k) for n in range(count)])
 
 
+def row_order(bands):
+    return [0] + sorted(range(1, bands), key=lambda k: (k < bands // 2, k))
+
+
 def row_swaps(values, bands):
-    order = sorted(range(1, bands), key=lambda k: (k < bands // 2, k))
-    moved = {k: xor_swap(values[k], "row", bands, k) for k in order}
-    return [moved[k] for k in range(1, bands)]
+    order = row_order(bands)
+    return [values[0]] + [xor_swap(values[k], "row", bands, k) for k in order[1:]]
 
 
 def added(a, b, *after):
@@ -423,7 +435,7 @@
         [x, above, below, side_a, side_b, joined_one, pool, order],
         2 * band_rows * 192 * 192 * 256,
     )
-    pieces = [pooled] + row_swaps([pooled] * bands, bands)
+    pieces = row_swaps([pooled] * bands, bands)
 
     even = strip % 2 == 0
     ends = [side[2 * channels :].reshape(og[:edge].shape) for side in (side_a, side_b)]
@@ -442,7 +454,7 @@
         4 * count * 9 * filters * 4 * channels,
         scratch=[pltpu.VMEM((bands, 72, 4 * channels), BF16)],
     )
-    received = [terms[0]] + row_swaps(terms, bands)
+    received = row_swaps(terms, bands)
 
     half = 9 * filters // 2
     keep_two, send_two = whole_call(
@@ -469,16 +481,17 @@
     )
     columns = lax.axis_size("col")
     two, two_more = sum_but_last(two, "col", columns)
-    one, one_more = sum_but_last(one, "row", bands)
+    ones = row_swaps([one] * bands, bands)
+    up_a, up_b = even_swap(up_a, "row", bands), odd_row_swap(up_b)
+    (one,) = whole_call(sum_rows, [shaped(one.shape)], ones + [up_a, up_b], 0, after=2)
     input_grad, done = whole_call(
         functools.partial(layer_one_back, bands=bands),
         [shaped(features_in.shape), shaped((8, 128), F32)],
-        [g, even_swap(up_a, "row", bands), odd_row_swap(up_b), back_one],
+        [g, up_a, up_b, back_one],
         2 * band_rows * 192 * 192 * 256,
     )
-    one = added(one, one_more, done)
     mine_two = added(two, two_more, one)
-    grad_two, done = whole_call(
+    grad_two, wrote = whole_call(
         functools.partial(finish_two, scale=1.0 / math.sqrt(pooled_rows * total)),
         [shaped((2 * half, 256), F32), shaped((8, 128), F32)],
         [mine_two, even_swap(mine_two, "pair", 2)],
@@ -486,11 +499,11 @@
         scratch=[pltpu.VMEM((2, half, 256), F32), pltpu.SemaphoreType.DMA((2,))],
         out_spaces=[pl.ANY, pltpu.VMEM],
     )
-    mine_one = added(*sum_but_last(one, "col", columns))
+    mine_one = added(*sum_but_last(one, "col", columns), done)
     (grad_one,) = whole_call(
         functools.partial(finish_one, scale=1.0 / math.sqrt(height * width)),
         [shaped((3, 3 * channels, channels), F32)],
-        [mine_one, even_swap(mine_one, "pair", 2), done],
+        [mine_one, even_swap(mine_one, "pair", 2), wrote],
         1,
         scratch=[pltpu.VMEM((144, 256), F32)],
         after=1,

time: 50 us -> 48.8 us (0.976)
  waiting for transfers between devices: 17.6 us -> 16.6 us
    ppermute x10 -> x11, waiting for transfers between devices: 14.3 us -> 12.1 us  [xor_swap(): return lax.ppermute(values, axis, [(n, n ^ k) for n in range(count)])]
    ppermute x6, starting transfers between devices: 5.41 us -> 4.08 us  [even_swap(): return lax.ppermute(values, axis, [(n, n ^ 1) for n in range(count)])]
    ppermute x2, waiting for transfers between devices: 0.01 us -> 1.2 us  [odd_row_swap(): return lax.ppermute(values, ('row', 'pair'), steps)]
    ppermute x10 -> x11, starting transfers between devices: 13.8 us -> 15 us  [xor_swap(): return lax.ppermute(values, axis, [(n, n ^ k) for n in range(count)])]
    pallas_call x15 -> x14, Pallas kernels: 6.96 us -> 6.95 us  [whole_call(): pl.pallas_call(body, out_shape=outs, in_specs=specs, out_specs=[pl.BlockS...]
  transfers between devices with their start and end apart: 19 -> 20, of which waited for: 10 -> 13; matrix products, arithmetic and copies ran while one was open for 3% -> 3% of each run, Pallas kernels for 6% -> 6%
where the time goes in v10:
time: 48.8 us; the launch traced here: 48.6 us
  starting transfers between devices  21.1 us (43%)
  waiting for transfers between devices  16.6 us (34%)
  Pallas kernels  6.95 us (14%)
  local copies, waits for them, and re-layouts  3.12 us (6%)
  between operations  0.84 us (2%)
    ppermute x11, starting transfers between devices, xor_swap(): return lax.ppermute(values, axis, [(n, n ^ k) for n in range(count)])  15 us
    ppermute x11, waiting for transfers between devices, xor_swap(): return lax.ppermute(values, axis, [(n, n ^ k) for n in range(count)])  12.1 us
    pallas_call x14, Pallas kernels, whole_call(): pl.pallas_call(body, out_shape=outs, in_specs=specs, out_specs=[pl.BlockS...  6.95 us
    ppermute x6, starting transfers between devices, even_swap(): return lax.ppermute(values, axis, [(n, n ^ 1) for n in range(count)])  4.08 us
    unnamed x8, local copies, waits for them, and re-layouts  2.75 us
    ppermute x6, waiting for transfers between devices, even_swap(): return lax.ppermute(values, axis, [(n, n ^ 1) for n in range(count)])  2.48 us
    ppermute x1, starting transfers between devices, odd_strip_swap(): return lax.ppermute(values, ('grp',) + COLS, steps)  2.01 us
    ppermute x2, waiting for transfers between devices, odd_row_swap(): return lax.ppermute(values, ('row', 'pair'), steps)  1.2 us
  transfers between devices with their start and end apart: 20, of which 13 were waited for; matrix products, arithmetic and copies ran while one was open for 3% of the time, Pallas kernels for 6%

profile of v10, /device:TPU:0, one launch (start us, length us, event | category | flops | bytes accessed | tf_op | source)
XLA Modules:
  0.0 48.6 jit_solution(7169780431811296010)
XLA Ops:
  0.7 1.0 %copy.21 = bf16[64,8,128]{2,0,1:T(8,128)(2,1)S(1)} copy(bf16[64,8,128]{2,1,0:T(8,128)(2,1)} %param.4) | data formatting | bytes 262144 | tf_op args[0]
  1.7 3.1 %collective-permute-start = (bf16[64,128]{1,0:T(8,128)(2,1)S(1)}, bf16[64,128]{1,0:T(8,128)(2,1)S(1)}, u32[]{:S(2)}, u32[]{:S(2)}) collective-permute-start(bf16[64,128]{1,0:T(8,128)(2,1)S(1)} %get-tuple-element.68), channel_id=1, source_target_pairs={{0,4},{4,0},{8,12},{12,8},{1,5},{5,1},{9,13},{13,9},{2,6},{6,2},{1... | collective-permute-start | bytes 49160 | tf_op jit(solution)/shard_map/ppermute | solution.py:337
  6.6 2.0 %collective-permute-start.2 = (bf16[144,128]{1,0:T(8,128)(2,1)S(1)}, bf16[144,128]{1,0:T(8,128)(2,1)S(1)}, u32[]{:S(2)}, u32[]{:S(2)}) collective-permute-start(bf16[144,128]{1,0:T(8,128)(2,1)S(1)} %get-tuple-element.37), channel_id=1, source_target_pairs={{0,16},{1,2},{2,1},{3,19},{16,0},{17,18},{18,17},{19,3},{4,20},{5,... | collective-permute-start | bytes 110600 | tf_op jit(solution)/shard_map/ppermute | solution.py:361
  8.7 0.9 %copy-done = bf16[64,3,3,64]{3,0,2,1:T(8,128)(2,1)S(1)} copy-done((bf16[64,3,3,64]{3,0,2,1:T(8,128)(2,1)S(1)}, bf16[64,3,3,64]{3,0,2,1:T(8,128)(2,1)}, u32[]{:S(2)}) %copy-start) | copy-done | bytes 73752
  10.6 0.9 %shard_map.70 = (bf16[2,40,256]{2,1,0:T(8,128)(2,1)S(1)}, bf16[8,64,256]{2,1,0:T(8,128)(2,1)S(1)}, bf16[10,64,256]{2,1,0:T(8,128)(2,1)S(1)}) custom-call(bf16[8,64,128]{2,1,0:T(8,128)(2,1)S(1)} %bitcast.36, bf16[64,128]{1,0:T(8,128)(2,1)S(1)} %get-tuple-element.39.above_ref, bf16[64,128]{1,0:T(8,128)(2,1)S(1)} %get-tuple-element.40.below_ref, ...), custom_call_target="tpu_custom_call" | custom-call | flops 150994944 | bytes 1122304 | tf_op jit(solution)/shard_map/pallas_call | solution.py:30
  11.4 4.7 %collective-permute-start.4 = (bf16[2,40,256]{2,1,0:T(8,128)(2,1)S(1)}, bf16[2,40,256]{2,1,0:T(8,128)(2,1)S(1)}, u32[]{:S(2)}, u32[]{:S(2)}) collective-permute-start(bf16[2,40,256]{2,1,0:T(8,128)(2,1)S(1)} %get-tuple-element.44.refs_0_), channel_id=1, source_target_pairs={{0,8},{4,12},{8,0},{12,4},{1,9},{5,13},{9,1},{13,5},{2,10},{6,14},... | collective-permute-start | bytes 122888 | tf_op jit(solution)/shard_map/ppermute | solution.py:365
  16.1 0.9 %collective-permute-start.5 = (bf16[2,40,256]{2,1,0:T(8,128)(2,1)S(1)}, bf16[2,40,256]{2,1,0:T(8,128)(2,1)S(1)}, u32[]{:S(2)}, u32[]{:S(2)}) collective-permute-start(bf16[2,40,256]{2,1,0:T(8,128)(2,1)S(1)} %get-tuple-element.44.refs_0_), channel_id=1, source_target_pairs={{0,12},{4,8},{8,4},{12,0},{1,13},{5,9},{9,5},{13,1},{2,14},{6,10},... | collective-permute-start | bytes 122888 | tf_op jit(solution)/shard_map/ppermute | solution.py:365
  17.1 1.1 %collective-permute-done.4.refs_1_ = bf16[2,40,256]{2,1,0:T(8,128)(2,1)S(1)} collective-permute-done((bf16[2,40,256]{2,1,0:T(8,128)(2,1)S(1)}, bf16[2,40,256]{2,1,0:T(8,128)(2,1)S(1)}, u32[]{:S(2)}, u32[]{:S(2)}) %collective-permute-start.4) | collective-permute-done | bytes 40992 | tf_op jit(solution)/shard_map/ppermute | solution.py:365
  18.2 3.7 %collective-permute-done.5.refs_2_ = bf16[2,40,256]{2,1,0:T(8,128)(2,1)S(1)} collective-permute-done((bf16[2,40,256]{2,1,0:T(8,128)(2,1)S(1)}, bf16[2,40,256]{2,1,0:T(8,128)(2,1)S(1)}, u32[]{:S(2)}, u32[]{:S(2)}) %collective-permute-start.5) | collective-permute-done | bytes 40992 | tf_op jit(solution)/shard_map/ppermute | solution.py:365
  21.9 1.0 %shard_map.71 = (bf16[72,256]{1,0:T(8,128)(2,1)S(1)}, bf16[72,256]{1,0:T(8,128)(2,1)S(1)}, bf16[72,256]{1,0:T(8,128)(2,1)S(1)}, bf16[72,256]{1,0:T(8,128)(2,1)S(...) custom-call(bf16[8,48,128]{2,1,0:T(8,128)(2,1)S(1)} %fusion.6.og_ref, ...), custom_call_target="tpu_custom_call" | custom-call | flops 452984832 | bytes 1368064 | tf_op jit(solution)/shard_map/pallas_call | solution.py:30
  22.9 1.1 %collective-permute-start.7 = (bf16[72,256]{1,0:T(8,128)(2,1)S(1)}, bf16[72,256]{1,0:T(8,128)(2,1)S(1)}, u32[]{:S(2)}, u32[]{:S(2)}) collective-permute-start(bf16[72,256]{1,0:T(8,128)(2,1)S(1)} %get-tuple-element.46), channel_id=1, source_target_pairs={{0,8},{4,12},{8,0},{12,4},{1,9},{5,13},{9,1},{13,5},{2,10},{6,14},... | collective-permute-start | bytes 110600 | tf_op jit(solution)/shard_map/ppermute | solution.py:365
  24.0 1.1 %collective-permute-start.8 = (bf16[72,256]{1,0:T(8,128)(2,1)S(1)}, bf16[72,256]{1,0:T(8,128)(2,1)S(1)}, u32[]{:S(2)}, u32[]{:S(2)}) collective-permute-start(bf16[72,256]{1,0:T(8,128)(2,1)S(1)} %get-tuple-element.47), channel_id=1, source_target_pairs={{0,12},{4,8},{8,4},{12,0},{1,13},{5,9},{9,5},{13,1},{2,14},{6,10},... | collective-permute-start | bytes 110600 | tf_op jit(solution)/shard_map/ppermute | solution.py:365
  25.1 1.4 %collective-permute-start.9 = (bf16[72,256]{1,0:T(8,128)(2,1)S(1)}, bf16[72,256]{1,0:T(8,128)(2,1)S(1)}, u32[]{:S(2)}, u32[]{:S(2)}) collective-permute-start(bf16[72,256]{1,0:T(8,128)(2,1)S(1)} %get-tuple-element.48), channel_id=1, source_target_pairs={{0,4},{4,0},{8,12},{12,8},{1,5},{5,1},{9,13},{13,9},{2,6},{6,2},{1... | collective-permute-start | bytes 110600 | tf_op jit(solution)/shard_map/ppermute | solution.py:365
  27.9 1.9 %collective-permute-done.8.refs_2_ = bf16[72,256]{1,0:T(8,128)(2,1)S(1)} collective-permute-done((bf16[72,256]{1,0:T(8,128)(2,1)S(1)}, bf16[72,256]{1,0:T(8,128)(2,1)S(1)}, u32[]{:S(2)}, u32[]{:S(2)}) %collective-permute-start.8) | collective-permute-done | bytes 36896 | tf_op jit(solution)/shard_map/ppermute | solution.py:365
  30.7 1.6 %collective-permute-done.12.b_ref = bf16[656,256]{1,0:T(8,128)(2,1)S(1)} collective-permute-done((bf16[656,256]{1,0:T(8,128)(2,1)S(1)}, bf16[656,256]{1,0:T(8,128)(2,1)S(1)}, u32[]{:S(2)}, u32[]{:S(2)}) %collective-permute-start.12) | collective-permute-done | bytes 335904 | tf_op jit(solution)/shard_map/ppermute | solution.py:337
  32.4 1.0 %collective-permute-start.18 = (bf16[576,256]{1,0:T(8,128)(2,1)S(1)}, bf16[576,256]{1,0:T(8,128)(2,1)S(1)}, u32[]{:S(2)}, u32[]{:S(2)}) collective-permute-start(bf16[576,256]{1,0:T(8,128)(2,1)S(1)} %get-tuple-element.64.a_ref), channel_id=1, source_target_pairs={{0,2},{2,0},{1,3},{3,1},{4,6},{6,4},{5,7},{7,5},{8,10},{10,8},{9,1... | collective-permute-start | bytes 884744 | tf_op jit(solution)/shard_map/ppermute | solution.py:365
  34.1 1.9 %collective-permute-start.13 = (bf16[80,256]{1,0:T(8,128)(2,1)S(1)}, bf16[80,256]{1,0:T(8,128)(2,1)S(1)}, u32[]{:S(2)}, u32[]{:S(2)}) collective-permute-start(bf16[80,256]{1,0:T(8,128)(2,1)S(1)} %get-tuple-element.62.refs_0_), channel_id=1, source_target_pairs={{0,8},{4,12},{8,0},{12,4},{1,9},{5,13},{9,1},{13,5},{2,10},{6,14},... | collective-permute-start | bytes 122888 | tf_op jit(solution)/shard_map/ppermute | solution.py:365
  36.0 1.8 %collective-permute-start.14 = (bf16[80,256]{1,0:T(8,128)(2,1)S(1)}, bf16[80,256]{1,0:T(8,128)(2,1)S(1)}, u32[]{:S(2)}, u32[]{:S(2)}) collective-permute-start(bf16[80,256]{1,0:T(8,128)(2,1)S(1)} %get-tuple-element.62.refs_0_), channel_id=1, source_target_pairs={{0,12},{4,8},{8,4},{12,0},{1,13},{5,9},{9,5},{13,1},{2,14},{6,10},... | collective-permute-start | bytes 122888 | tf_op jit(solution)/shard_map/ppermute | solution.py:365
  37.8 1.2 %collective-permute-done.11.b_ref.refs_5_ = bf16[64,256]{1,0:T(8,128)(2,1)S(1)} collective-permute-done((bf16[64,256]{1,0:T(8,128)(2,1)S(1)}, bf16[64,256]{1,0:T(8,128)(2,1)S(1)}, u32[]{:S(2)}, u32[]{:S(2)}) %collective-permute-start.11) | collective-permute-done | bytes 32800 | tf_op jit(solution)/shard_map/ppermute | solution.py:351
  39.3 2.5 %collective-permute-done.14.refs_2_ = bf16[80,256]{1,0:T(8,128)(2,1)S(1)} collective-permute-done((bf16[80,256]{1,0:T(8,128)(2,1)S(1)}, bf16[80,256]{1,0:T(8,128)(2,1)S(1)}, u32[]{:S(2)}, u32[]{:S(2)}) %collective-permute-start.14) | collective-permute-done | bytes 40992 | tf_op jit(solution)/shard_map/ppermute | solution.py:365
  42.4 1.2 %collective-permute-start.16 = (bf16[80,256]{1,0:T(8,128)(2,1)S(1)}, bf16[80,256]{1,0:T(8,128)(2,1)S(1)}, u32[]{:S(2)}, u32[]{:S(2)}) collective-permute-start(bf16[80,256]{1,0:T(8,128)(2,1)S(1)} %shard_map.76.a_ref.refs_0_), channel_id=1, source_target_pairs={{0,2},{2,0},{1,3},{3,1},{4,6},{6,4},{5,7},{7,5},{8,10},{10,8},{9,1... | collective-permute-start | bytes 122888 | tf_op jit(solution)/shard_map/ppermute | solution.py:365
  44.0 1.2 %shard_map.74 = (bf16[64,8,128]{2,1,0:T(8,128)(2,1)}, f32[8,128]{1,0:T(8,128)S(1)}) custom-call(bf16[8,64,256]{2,1,0:T(8,128)(2,1)S(1)} %get-tuple-element.56.g_ref, bf16[64,256]{1,0:T(8,128)(2,1)S(1)} %collective-permute-done.10.a_ref.refs_4_, bf16[64,256]{1,0:T(8,128)(2,1)S(1)} %collective-permute-done.11.b_ref.refs_5_, bf16[192,192]{1,0:T(8,128)(2,1)S(1)} %reshape.44.w_ref), custom_call_target="tpu_custom_call" | custom-call | flops 150994944 | bytes 536576 | tf_op jit(solution)/shard_map/pallas_call | solution.py:30
  45.1 1.4 %collective-permute-done.16.b_ref = bf16[80,256]{1,0:T(8,128)(2,1)S(1)} collective-permute-done((bf16[80,256]{1,0:T(8,128)(2,1)S(1)}, bf16[80,256]{1,0:T(8,128)(2,1)S(1)}, u32[]{:S(2)}, u32[]{:S(2)}) %collective-permute-start.16) | collective-permute-done | bytes 40992 | tf_op jit(solution)/shard_map/ppermute | solution.py:365
  46.6 1.1 %shard_map.79 = (f32[1152,256]{1,0:T(8,128)}, f32[8,128]{1,0:T(8,128)S(1)}) custom-call(bf16[576,256]{1,0:T(8,128)(2,1)S(1)} %shard_map.78.mine_ref, bf16[576,256]{1,0:T(8,128)(2,1)S(1)} %collective-permute-done.19.other_ref), custom_call_target="tpu_custom_call" | custom-call | flops 100000000 | bytes 1773568 | tf_op jit(solution)/shard_map/pallas_call | solution.py:30
  (48 shorter events, 8.3 us)
Async XLA Ops:
  0.6 21.3 %copy-start.2 = (bf16[128,3,3,256]{3,0,2,1:T(8,128)(2,1)S(1)}, bf16[128,3,3,256]{3,0,2,1:T(8,128)(2,1)}, u32[]{:S(2)}) copy-start(bf16[128,3,3,256]{3,0,2,1:T(8,128)(2,1)} %param.6) | copy-start | bytes 1769476
  1.7 4.8 %collective-permute-start = (bf16[64,128]{1,0:T(8,128)(2,1)S(1)}, bf16[64,128]{1,0:T(8,128)(2,1)S(1)}, u32[]{:S(2)}, u32[]{:S(2)}) collective-permute-start(bf16[64,128]{1,0:T(8,128)(2,1)S(1)} %get-tuple-element.68), channel_id=1, source_target_pairs={{0,4},{4,0},{8,12},{12,8},{1,5},{5,1},{9,13},{13,9},{2,6},{6,2},{1... | collective-permute-start | bytes 49160 | tf_op jit(solution)/shard_map/ppermute | solution.py:337
  4.7 1.7 %collective-permute-start.1 = (bf16[64,128]{1,0:T(8,128)(2,1)S(1)}, bf16[64,128]{1,0:T(8,128)(2,1)S(1)}, u32[]{:S(2)}, u32[]{:S(2)}) collective-permute-start(bf16[64,128]{1,0:T(8,128)(2,1)S(1)} %get-tuple-element.67), channel_id=1, source_target_pairs={{0,1},{1,0},{4,8},{5,9},{8,4},{9,5},{12,13},{13,12},{2,3},{3,2},{6... | collective-permute-start | bytes 49160 | tf_op jit(solution)/shard_map/ppermute | solution.py:351
  6.6 4.0 %collective-permute-start.2 = (bf16[144,128]{1,0:T(8,128)(2,1)S(1)}, bf16[144,128]{1,0:T(8,128)(2,1)S(1)}, u32[]{:S(2)}, u32[]{:S(2)}) collective-permute-start(bf16[144,128]{1,0:T(8,128)(2,1)S(1)} %get-tuple-element.37), channel_id=1, source_target_pairs={{0,16},{1,2},{2,1},{3,19},{16,0},{17,18},{18,17},{19,3},{4,20},{5,... | collective-permute-start | bytes 110600 | tf_op jit(solution)/shard_map/ppermute | solution.py:361
  8.6 2.0 %collective-permute-start.3 = (bf16[144,128]{1,0:T(8,128)(2,1)S(1)}, bf16[144,128]{1,0:T(8,128)(2,1)S(1)}, u32[]{:S(2)}, u32[]{:S(2)}) collective-permute-start(bf16[144,128]{1,0:T(8,128)(2,1)S(1)} %get-tuple-element.38), channel_id=1, source_target_pairs={{0,1},{1,0},{2,3},{3,2},{4,5},{5,4},{6,7},{7,6},{8,9},{9,8},{10,11... | collective-permute-start | bytes 110600 | tf_op jit(solution)/shard_map/ppermute | solution.py:337
  8.7 0.9 %copy-start = (bf16[64,3,3,64]{3,0,2,1:T(8,128)(2,1)S(1)}, bf16[64,3,3,64]{3,0,2,1:T(8,128)(2,1)}, u32[]{:S(2)}) copy-start(bf16[64,3,3,64]{3,0,2,1:T(8,128)(2,1)} %param.5) | copy-start | bytes 221188
  11.4 6.8 %collective-permute-start.4 = (bf16[2,40,256]{2,1,0:T(8,128)(2,1)S(1)}, bf16[2,40,256]{2,1,0:T(8,128)(2,1)S(1)}, u32[]{:S(2)}, u32[]{:S(2)}) collective-permute-start(bf16[2,40,256]{2,1,0:T(8,128)(2,1)S(1)} %get-tuple-element.44.refs_0_), channel_id=1, source_target_pairs={{0,8},{4,12},{8,0},{12,4},{1,9},{5,13},{9,1},{13,5},{2,10},{6,14},... | collective-permute-start | bytes 122888 | tf_op jit(solution)/shard_map/ppermute | solution.py:365
  16.1 5.8 %collective-permute-start.5 = (bf16[2,40,256]{2,1,0:T(8,128)(2,1)S(1)}, bf16[2,40,256]{2,1,0:T(8,128)(2,1)S(1)}, u32[]{:S(2)}, u32[]{:S(2)}) collective-permute-start(bf16[2,40,256]{2,1,0:T(8,128)(2,1)S(1)} %get-tuple-element.44.refs_0_), channel_id=1, source_target_pairs={{0,12},{4,8},{8,4},{12,0},{1,13},{5,9},{9,5},{13,1},{2,14},{6,10},... | collective-permute-start | bytes 122888 | tf_op jit(solution)/shard_map/ppermute | solution.py:365
  17.0 4.9 %collective-permute-start.6 = (bf16[2,40,256]{2,1,0:T(8,128)(2,1)S(1)}, bf16[2,40,256]{2,1,0:T(8,128)(2,1)S(1)}, u32[]{:S(2)}, u32[]{:S(2)}) collective-permute-start(bf16[2,40,256]{2,1,0:T(8,128)(2,1)S(1)} %get-tuple-element.44.refs_0_), channel_id=1, source_target_pairs={{0,4},{4,0},{8,12},{12,8},{1,5},{5,1},{9,13},{13,9},{2,6},{6,2},{1... | collective-permute-start | bytes 122888 | tf_op jit(solution)/shard_map/ppermute | solution.py:365
  22.9 4.9 %collective-permute-start.7 = (bf16[72,256]{1,0:T(8,128)(2,1)S(1)}, bf16[72,256]{1,0:T(8,128)(2,1)S(1)}, u32[]{:S(2)}, u32[]{:S(2)}) collective-permute-start(bf16[72,256]{1,0:T(8,128)(2,1)S(1)} %get-tuple-element.46), channel_id=1, source_target_pairs={{0,8},{4,12},{8,0},{12,4},{1,9},{5,13},{9,1},{13,5},{2,10},{6,14},... | collective-permute-start | bytes 110600 | tf_op jit(solution)/shard_map/ppermute | solution.py:365
  24.0 5.8 %collective-permute-start.8 = (bf16[72,256]{1,0:T(8,128)(2,1)S(1)}, bf16[72,256]{1,0:T(8,128)(2,1)S(1)}, u32[]{:S(2)}, u32[]{:S(2)}) collective-permute-start(bf16[72,256]{1,0:T(8,128)(2,1)S(1)} %get-tuple-element.47), channel_id=1, source_target_pairs={{0,12},{4,8},{8,4},{12,0},{1,13},{5,9},{9,5},{13,1},{2,14},{6,10},... | collective-permute-start | bytes 110600 | tf_op jit(solution)/shard_map/ppermute | solution.py:365
  25.1 4.7 %collective-permute-start.9 = (bf16[72,256]{1,0:T(8,128)(2,1)S(1)}, bf16[72,256]{1,0:T(8,128)(2,1)S(1)}, u32[]{:S(2)}, u32[]{:S(2)}) collective-permute-start(bf16[72,256]{1,0:T(8,128)(2,1)S(1)} %get-tuple-element.48), channel_id=1, source_target_pairs={{0,4},{4,0},{8,12},{12,8},{1,5},{5,1},{9,13},{13,9},{2,6},{6,2},{1... | collective-permute-start | bytes 110600 | tf_op jit(solution)/shard_map/ppermute | solution.py:365
  30.6 13.0 %copy-start.1 = (bf16[64,3,3,64]{3,0,2,1:T(8,128)(2,1)S(1)}, bf16[64,3,3,64]{3,0,2,1:T(8,128)(2,1)}, u32[]{:S(2)}) copy-start(bf16[64,3,3,64]{3,0,2,1:T(8,128)(2,1)} %param.5) | copy-start | bytes 221188
  30.6 1.7 %collective-permute-start.12 = (bf16[656,256]{1,0:T(8,128)(2,1)S(1)}, bf16[656,256]{1,0:T(8,128)(2,1)S(1)}, u32[]{:S(2)}, u32[]{:S(2)}) collective-permute-start(bf16[656,256]{1,0:T(8,128)(2,1)S(1)} %get-tuple-element.61), channel_id=1, source_target_pairs={{0,1},{1,0},{2,3},{3,2},{4,5},{5,4},{6,7},{7,6},{8,9},{9,8},{10,11... | collective-permute-start | bytes 1007624 | tf_op jit(solution)/shard_map/ppermute | solution.py:337
  32.4 9.8 %collective-permute-start.18 = (bf16[576,256]{1,0:T(8,128)(2,1)S(1)}, bf16[576,256]{1,0:T(8,128)(2,1)S(1)}, u32[]{:S(2)}, u32[]{:S(2)}) collective-permute-start(bf16[576,256]{1,0:T(8,128)(2,1)S(1)} %get-tuple-element.64.a_ref), channel_id=1, source_target_pairs={{0,2},{2,0},{1,3},{3,1},{4,6},{6,4},{5,7},{7,5},{8,10},{10,8},{9,1... | collective-permute-start | bytes 884744 | tf_op jit(solution)/shard_map/ppermute | solution.py:365
  33.4 4.4 %collective-permute-start.10 = (bf16[64,256]{1,0:T(8,128)(2,1)S(1)}, bf16[64,256]{1,0:T(8,128)(2,1)S(1)}, u32[]{:S(2)}, u32[]{:S(2)}) collective-permute-start(bf16[64,256]{1,0:T(8,128)(2,1)S(1)} %get-tuple-element.57), channel_id=1, source_target_pairs={{0,4},{4,0},{8,12},{12,8},{1,5},{5,1},{9,13},{13,9},{2,6},{6,2},{1... | collective-permute-start | bytes 98312 | tf_op jit(solution)/shard_map/ppermute | solution.py:337
  34.1 5.2 %collective-permute-start.13 = (bf16[80,256]{1,0:T(8,128)(2,1)S(1)}, bf16[80,256]{1,0:T(8,128)(2,1)S(1)}, u32[]{:S(2)}, u32[]{:S(2)}) collective-permute-start(bf16[80,256]{1,0:T(8,128)(2,1)S(1)} %get-tuple-element.62.refs_0_), channel_id=1, source_target_pairs={{0,8},{4,12},{8,0},{12,4},{1,9},{5,13},{9,1},{13,5},{2,10},{6,14},... | collective-permute-start | bytes 122888 | tf_op jit(solution)/shard_map/ppermute | solution.py:365
  36.0 5.8 %collective-permute-start.14 = (bf16[80,256]{1,0:T(8,128)(2,1)S(1)}, bf16[80,256]{1,0:T(8,128)(2,1)S(1)}, u32[]{:S(2)}, u32[]{:S(2)}) collective-permute-start(bf16[80,256]{1,0:T(8,128)(2,1)S(1)} %get-tuple-element.62.refs_0_), channel_id=1, source_target_pairs={{0,12},{4,8},{8,4},{12,0},{1,13},{5,9},{9,5},{13,1},{2,14},{6,10},... | collective-permute-start | bytes 122888 | tf_op jit(solution)/shard_map/ppermute | solution.py:365
  37.8 4.4 %collective-permute-start.15 = (bf16[80,256]{1,0:T(8,128)(2,1)S(1)}, bf16[80,256]{1,0:T(8,128)(2,1)S(1)}, u32[]{:S(2)}, u32[]{:S(2)}) collective-permute-start(bf16[80,256]{1,0:T(8,128)(2,1)S(1)} %get-tuple-element.62.refs_0_), channel_id=1, source_target_pairs={{0,4},{4,0},{8,12},{12,8},{1,5},{5,1},{9,13},{13,9},{2,6},{6,2},{1... | collective-permute-start | bytes 122888 | tf_op jit(solution)/shard_map/ppermute | solution.py:365
  37.8 1.2 %collective-permute-start.11 = (bf16[64,256]{1,0:T(8,128)(2,1)S(1)}, bf16[64,256]{1,0:T(8,128)(2,1)S(1)}, u32[]{:S(2)}, u32[]{:S(2)}) collective-permute-start(bf16[64,256]{1,0:T(8,128)(2,1)S(1)} %get-tuple-element.58), channel_id=1, source_target_pairs={{0,1},{1,0},{4,8},{5,9},{8,4},{9,5},{12,13},{13,12},{2,3},{3,2},{6... | collective-permute-start | bytes 98312 | tf_op jit(solution)/shard_map/ppermute | solution.py:351
  42.4 4.2 %collective-permute-start.19 = (bf16[576,256]{1,0:T(8,128)(2,1)S(1)}, bf16[576,256]{1,0:T(8,128)(2,1)S(1)}, u32[]{:S(2)}, u32[]{:S(2)}) collective-permute-start(bf16[576,256]{1,0:T(8,128)(2,1)S(1)} %shard_map.78.mine_ref), channel_id=1, source_target_pairs={{0,1},{1,0},{2,3},{3,2},{4,5},{5,4},{6,7},{7,6},{8,9},{9,8},{10,11... | collective-permute-start | bytes 884744 | tf_op jit(solution)/shard_map/ppermute | solution.py:337
  42.4 4.1 %collective-permute-start.16 = (bf16[80,256]{1,0:T(8,128)(2,1)S(1)}, bf16[80,256]{1,0:T(8,128)(2,1)S(1)}, u32[]{:S(2)}, u32[]{:S(2)}) collective-permute-start(bf16[80,256]{1,0:T(8,128)(2,1)S(1)} %shard_map.76.a_ref.refs_0_), channel_id=1, source_target_pairs={{0,2},{2,0},{1,3},{3,1},{4,6},{6,4},{5,7},{7,5},{8,10},{10,8},{9,1... | collective-permute-start | bytes 122888 | tf_op jit(solution)/shard_map/ppermute | solution.py:365
  46.5 1.3 %collective-permute-start.17 = (bf16[80,256]{1,0:T(8,128)(2,1)S(1)}, bf16[80,256]{1,0:T(8,128)(2,1)S(1)}, u32[]{:S(2)}, u32[]{:S(2)}) collective-permute-start(bf16[80,256]{1,0:T(8,128)(2,1)S(1)} %shard_map.77.mine_ref), channel_id=1, source_target_pairs={{0,1},{1,0},{2,3},{3,2},{4,5},{5,4},{6,7},{7,6},{8,9},{9,8},{10,11... | collective-permute-start | bytes 122888 | tf_op jit(solution)/shard_map/ppermute | solution.py:337

commit v11 on v10

--- a/solution.py
+++ b/solution.py
@@ -12,7 +12,7 @@
 F32 = jnp.float32
 COLS = ("col", "pair")
 REACH = 3
-TAIL = 80
+HALF_ONE = 72
 PITCH = 48
 SENT = 40
 
@@ -192,7 +192,7 @@
     map_ref[0] = jnp.zeros((PITCH, 256), BF16)
     map_ref[rows + 1] = jnp.zeros((PITCH, 256), BF16)
     blank = jnp.zeros((PITCH - SENT, 256), BF16)
-    for k, piece in zip(row_order(bands), pieces):
+    for k, piece in zip(row_order(bands, near_first=True), pieces):
         for t in range(2):
             map_ref[1 + 2 * (band ^ k) + t] = jnp.concatenate([piece[t], blank], 0)
     near = jnp.concatenate([map_ref[i : i + rows].reshape(count, 256) for i in range(3)], 1)
@@ -242,25 +242,19 @@
 
 
 def sum_rows(*refs):
-    *refs, _, _, out_ref = refs
-    terms = dict(zip(row_order(len(refs)), (ref[...].astype(F32) for ref in refs)))
+    *refs, a_ref, b_ref, out_ref, passed_a_ref, passed_b_ref = refs
+    terms = dict(zip(row_order(len(refs), near_first=True), (ref[...].astype(F32) for ref in refs)))
     terms = [terms[k] for k in range(len(refs))]
     while len(terms) > 1:
         terms = [a + b for a, b in zip(terms[::2], terms[1::2])]
     out_ref[...] = terms[0].astype(BF16)
-
-
-def add_halves(a_ref, b_ref, two_ref, one_ref):
-    half = two_ref.shape[0]
-    total = (a_ref[...].astype(F32) + b_ref[...].astype(F32)).astype(BF16)
-    two_ref[...] = total[:half]
-    one_ref[...] = total[half:]
+    passed_a_ref[...] = a_ref[...]
+    passed_b_ref[...] = b_ref[...]
 
 
 def grad_pre_one(*refs, bands):
     terms, refs = refs[:bands], refs[bands:]
-    slope_ref, wide_ref, pool_ref, order_ref, keep_two_ref, send_two_ref, *refs = refs
-    g_ref, a_ref, b_ref, keep_ref, send_ref, part_ref = refs
+    slope_ref, wide_ref, pool_ref, order_ref, g_ref, a_ref, b_ref, keep_ref, send_ref, part_ref = refs
     pair = lax.axis_index("pair")
     summed = terms[0][...].astype(F32)
     for k in range(1, bands):
@@ -289,12 +283,8 @@
     b_ref[...] = jnp.where(even, first, last).astype(BF16)
     part_ref[:96] = jnp.concatenate([acc[:96, :128], acc[96:, :128]], 1)
     part_ref[96:] = jnp.concatenate([acc[48 * q : 48 * q + 48, 128:] for q in range(4)], 1)
-    half = keep_two_ref.shape[0]
-    blank = jnp.zeros((TAIL - 72, 256), F32)
-    for ref, two_ref, place in ((keep_ref, keep_two_ref, pair), (send_ref, send_two_ref, 1 - pair)):
-        ref[:half] = two_ref[...]
-        mine = part_ref[pl.ds(pl.multiple_of(place * 72, 8), 72)]
-        ref[half:] = jnp.concatenate([mine, blank], 0).astype(BF16)
+    for ref, place in ((keep_ref, pair), (send_ref, 1 - pair)):
+        ref[...] = part_ref[pl.ds(pl.multiple_of(place * HALF_ONE, 8), HALF_ONE)].astype(BF16)
 
 
 def layer_one_back(g_ref, a_ref, b_ref, w_ref, out_ref, done_ref, *, bands):
@@ -321,10 +311,10 @@
         copy.wait()
 
 
-def finish_one(mine_ref, other_ref, _, out_ref, flat_ref, *, scale):
+def finish_one(mine_ref, other_ref, _, __, out_ref, flat_ref, *, scale):
     pair = lax.axis_index("pair")
     for ref, place in ((mine_ref, pair), (other_ref, 1 - pair)):
-        flat_ref[pl.ds(pl.multiple_of(place * 72, 8), 72)] = ref[:72].astype(F32) * scale
+        flat_ref[pl.ds(pl.multiple_of(place * HALF_ONE, 8), HALF_ONE)] = ref[...].astype(F32) * scale
     out_ref[0, :96] = flat_ref[:96, :64]
     out_ref[1, :96] = flat_ref[:96, 64:128]
     out_ref[0, 96:] = flat_ref[:96, 128:192]
@@ -365,12 +355,13 @@
     return lax.ppermute(values, axis, [(n, n ^ k) for n in range(count)])
 
 
-def row_order(bands):
-    return [0] + sorted(range(1, bands), key=lambda k: (k < bands // 2, k))
-
-
-def row_swaps(values, bands):
-    order = row_order(bands)
+def row_order(bands, near_first=False):
+    far_first = sorted(range(1, bands), key=lambda k: (k < bands // 2, k))
+    return [0] + (far_first[::-1] if near_first else far_first)
+
+
+def row_swaps(values, bands, near_first=False):
+    order = row_order(bands, near_first)
     return [values[0]] + [xor_swap(values[k], "row", bands, k) for k in order[1:]]
 
 
@@ -435,7 +426,7 @@
         [x, above, below, side_a, side_b, joined_one, pool, order],
         2 * band_rows * 192 * 192 * 256,
     )
-    pieces = row_swaps([pooled] * bands, bands)
+    pieces = row_swaps([pooled] * bands, bands, near_first=True)
 
     even = strip % 2 == 0
     ends = [side[2 * channels :].reshape(og[:edge].shape) for side in (side_a, side_b)]
@@ -468,26 +459,23 @@
         functools.partial(grad_pre_one, bands=bands),
         [shaped((band_rows, channels, 256))]
         + [shaped((channels, 256))] * 2
-        + [shaped((half + TAIL, 256))] * 2,
-        received + [slope, wide, pool_back, order, keep_two, send_two],
+        + [shaped((HALF_ONE, 256))] * 2,
+        received + [slope, wide, pool_back, order],
         2 * 8 * 192 * 192 * 256,
         scratch=[pltpu.VMEM((144, 256), F32)],
     )
-    two, one = whole_call(
-        add_halves,
-        [shaped((half, 256)), shaped((TAIL, 256))],
-        [keep, even_swap(send, "pair", 2)],
-        0,
-    )
+    one = added(keep, even_swap(send, "pair", 2))
+    two = added(keep_two, even_swap(send_two, "pair", 2), keep)
     columns = lax.axis_size("col")
     two, two_more = sum_but_last(two, "col", columns)
-    ones = row_swaps([one] * bands, bands)
-    up_a, up_b = even_swap(up_a, "row", bands), odd_row_swap(up_b)
-    (one,) = whole_call(sum_rows, [shaped(one.shape)], ones + [up_a, up_b], 0, after=2)
+    ones = row_swaps([one] * bands, bands, near_first=True)
+    one, up_a, up_b = whole_call(
+        sum_rows, [shaped(a.shape) for a in (one, up_a, up_b)], ones + [up_a, up_b], 0
+    )
     input_grad, done = whole_call(
         functools.partial(layer_one_back, bands=bands),
         [shaped(features_in.shape), shaped((8, 128), F32)],
-        [g, up_a, up_b, back_one],
+        [g, even_swap(up_a, "row", bands), odd_row_swap(up_b), back_one],
         2 * band_rows * 192 * 192 * 256,
     )
     mine_two = added(two, two_more, one)
@@ -499,14 +487,14 @@
         scratch=[pltpu.VMEM((2, half, 256), F32), pltpu.SemaphoreType.DMA((2,))],
         out_spaces=[pl.ANY, pltpu.VMEM],
     )
-    mine_one = added(*sum_but_last(one, "col", columns), done)
+    mine_one = added(*sum_but_last(one, "col", columns))
     (grad_one,) = whole_call(
         functools.partial(finish_one, scale=1.0 / math.sqrt(height * width)),
         [shaped((3, 3 * channels, channels), F32)],
-        [mine_one, even_swap(mine_one, "pair", 2), wrote],
+        [mine_one, even_swap(mine_one, "pair", 2), wrote, done],
         1,
         scratch=[pltpu.VMEM((144, 256), F32)],
-        after=1,
+        after=2,
     )
     grad_two = jnp.transpose(grad_two.reshape(3, 3, filters, 4 * channels), (2, 0, 1, 3))
     grad_one = jnp.transpose(grad_one.reshape(3, 3, channels, channels), (2, 0, 1, 3))

time: 48.8 us -> 49.1 us (level)
  waiting for transfers between devices: 16.6 us -> 17.3 us
  starting transfers between devices: 21.1 us -> 20.6 us
    ppermute x11, waiting for transfers between devices: 12.1 us -> 13.4 us  [xor_swap(): return lax.ppermute(values, axis, [(n, n ^ k) for n in range(count)])]
    ppermute x11, starting transfers between devices: 15 us -> 13.7 us  [xor_swap(): return lax.ppermute(values, axis, [(n, n ^ k) for n in range(count)])]
    ppermute x2, waiting for transfers between devices: 1.2 us -> 0.01 us  [odd_row_swap(): return lax.ppermute(values, ('row', 'pair'), steps)]
    ppermute x6 -> x7, starting transfers between devices: 4.08 us -> 4.83 us  [even_swap(): return lax.ppermute(values, axis, [(n, n ^ 1) for n in range(count)])]
    ppermute x2, starting transfers between devices: 0.01 us -> 0.52 us  [odd_row_swap(): return lax.ppermute(values, ('row', 'pair'), steps)]
    ppermute x6 -> x7, waiting for transfers between devices: 2.48 us -> 2.54 us  [even_swap(): return lax.ppermute(values, axis, [(n, n ^ 1) for n in range(count)])]
    pallas_call x14 -> x15, Pallas kernels: 6.95 us -> 6.97 us  [whole_call(): pl.pallas_call(body, out_shape=outs, in_specs=specs, out_specs=[pl.BlockS...]
  transfers between devices with their start and end apart: 20 -> 21, of which waited for: 13 -> 14; matrix products, arithmetic and copies ran while one was open for 3% -> 3% of each run, Pallas kernels for 6% -> 7%
where the time goes in v11:
time: 49.1 us; the launch traced here: 48.9 us
  starting transfers between devices  20.6 us (42%)
  waiting for transfers between devices  17.3 us (35%)
  Pallas kernels  6.97 us (14%)
  local copies, waits for them, and re-layouts  3.12 us (6%)
  between operations  0.87 us (2%)
    ppermute x11, starting transfers between devices, xor_swap(): return lax.ppermute(values, axis, [(n, n ^ k) for n in range(count)])  13.7 us
    ppermute x11, waiting for transfers between devices, xor_swap(): return lax.ppermute(values, axis, [(n, n ^ k) for n in range(count)])  13.4 us
    pallas_call x15, Pallas kernels, whole_call(): pl.pallas_call(body, out_shape=outs, in_specs=specs, out_specs=[pl.BlockS...  6.97 us
    ppermute x7, starting transfers between devices, even_swap(): return lax.ppermute(values, axis, [(n, n ^ 1) for n in range(count)])  4.83 us
    unnamed x8, local copies, waits for them, and re-layouts  2.75 us
    ppermute x7, waiting for transfers between devices, even_swap(): return lax.ppermute(values, axis, [(n, n ^ 1) for n in range(count)])  2.54 us
    ppermute x1, starting transfers between devices, odd_strip_swap(): return lax.ppermute(values, ('grp',) + COLS, steps)  1.56 us
    ppermute x1, waiting for transfers between devices, odd_strip_swap(): return lax.ppermute(values, ('grp',) + COLS, steps)  1.28 us
  transfers between devices with their start and end apart: 21, of which 14 were waited for; matrix products, arithmetic and copies ran while one was open for 3% of the time, Pallas kernels for 7%

profile of v11, /device:TPU:0, one launch (start us, length us, event | category | flops | bytes accessed | tf_op | source)
XLA Modules:
  0.0 48.9 jit_solution(2720340704107188961)
XLA Ops:
  0.7 1.0 %copy.21 = bf16[64,8,128]{2,0,1:T(8,128)(2,1)S(1)} copy(bf16[64,8,128]{2,1,0:T(8,128)(2,1)} %param.4) | data formatting | bytes 262144 | tf_op args[0]
  2.2 4.1 %collective-permute-start = (bf16[64,128]{1,0:T(8,128)(2,1)S(1)}, bf16[64,128]{1,0:T(8,128)(2,1)S(1)}, u32[]{:S(2)}, u32[]{:S(2)}) collective-permute-start(bf16[64,128]{1,0:T(8,128)(2,1)S(1)} %get-tuple-element.70), channel_id=1, source_target_pairs={{0,4},{4,0},{8,12},{12,8},{1,5},{5,1},{9,13},{13,9},{2,6},{6,2},{1... | collective-permute-start | bytes 49160 | tf_op jit(solution)/shard_map/ppermute | solution.py:327
  6.3 0.8 %copy.22 = bf16[128,32,8]{0,1,2:T(8,128)(2,1)S(1)} copy(bf16[128,32,8]{0,2,1:T(8,128)(2,1)} %param.7) | data formatting | bytes 131072 | tf_op args[3]
  8.1 1.6 %collective-permute-start.2 = (bf16[144,128]{1,0:T(8,128)(2,1)S(1)}, bf16[144,128]{1,0:T(8,128)(2,1)S(1)}, u32[]{:S(2)}, u32[]{:S(2)}) collective-permute-start(bf16[144,128]{1,0:T(8,128)(2,1)S(1)} %get-tuple-element.38), channel_id=1, source_target_pairs={{0,16},{1,2},{2,1},{3,19},{16,0},{17,18},{18,17},{19,3},{4,20},{5,... | collective-permute-start | bytes 110600 | tf_op jit(solution)/shard_map/ppermute | solution.py:351
  9.8 0.9 %copy-done = bf16[64,3,3,64]{3,0,2,1:T(8,128)(2,1)S(1)} copy-done((bf16[64,3,3,64]{3,0,2,1:T(8,128)(2,1)S(1)}, bf16[64,3,3,64]{3,0,2,1:T(8,128)(2,1)}, u32[]{:S(2)}) %copy-start) | copy-done | bytes 73752
  10.8 1.3 %collective-permute-done.2.b_ref = bf16[144,128]{1,0:T(8,128)(2,1)S(1)} collective-permute-done((bf16[144,128]{1,0:T(8,128)(2,1)S(1)}, bf16[144,128]{1,0:T(8,128)(2,1)S(1)}, u32[]{:S(2)}, u32[]{:S(2)}) %collective-permute-start.2) | collective-permute-done | bytes 36896 | tf_op jit(solution)/shard_map/ppermute | solution.py:351
  12.1 0.9 %shard_map.70 = (bf16[2,40,256]{2,1,0:T(8,128)(2,1)S(1)}, bf16[8,64,256]{2,1,0:T(8,128)(2,1)S(1)}, bf16[10,64,256]{2,1,0:T(8,128)(2,1)S(1)}) custom-call(bf16[8,64,128]{2,1,0:T(8,128)(2,1)S(1)} %bitcast.36, bf16[64,128]{1,0:T(8,128)(2,1)S(1)} %get-tuple-element.40.above_ref, bf16[64,128]{1,0:T(8,128)(2,1)S(1)} %get-tuple-element.41.below_ref, ...), custom_call_target="tpu_custom_call" | custom-call | flops 150994944 | bytes 1122304 | tf_op jit(solution)/shard_map/pallas_call | solution.py:30
  13.0 2.0 %collective-permute-start.6 = (bf16[2,40,256]{2,1,0:T(8,128)(2,1)S(1)}, bf16[2,40,256]{2,1,0:T(8,128)(2,1)S(1)}, u32[]{:S(2)}, u32[]{:S(2)}) collective-permute-start(bf16[2,40,256]{2,1,0:T(8,128)(2,1)S(1)} %get-tuple-element.45.refs_0_), channel_id=1, source_target_pairs={{0,8},{4,12},{8,0},{12,4},{1,9},{5,13},{9,1},{13,5},{2,10},{6,14},... | collective-permute-start | bytes 122888 | tf_op jit(solution)/shard_map/ppermute | solution.py:355
  15.0 2.5 %collective-permute-start.5 = (bf16[2,40,256]{2,1,0:T(8,128)(2,1)S(1)}, bf16[2,40,256]{2,1,0:T(8,128)(2,1)S(1)}, u32[]{:S(2)}, u32[]{:S(2)}) collective-permute-start(bf16[2,40,256]{2,1,0:T(8,128)(2,1)S(1)} %get-tuple-element.45.refs_0_), channel_id=1, source_target_pairs={{0,12},{4,8},{8,4},{12,0},{1,13},{5,9},{9,5},{13,1},{2,14},{6,10},... | collective-permute-start | bytes 122888 | tf_op jit(solution)/shard_map/ppermute | solution.py:355
  17.6 1.4 %collective-permute-done.6.refs_3_ = bf16[2,40,256]{2,1,0:T(8,128)(2,1)S(1)} collective-permute-done((bf16[2,40,256]{2,1,0:T(8,128)(2,1)S(1)}, bf16[2,40,256]{2,1,0:T(8,128)(2,1)S(1)}, u32[]{:S(2)}, u32[]{:S(2)}) %collective-permute-start.6) | collective-permute-done | bytes 40992 | tf_op jit(solution)/shard_map/ppermute | solution.py:355
  19.0 1.8 %collective-permute-done.5.refs_2_ = bf16[2,40,256]{2,1,0:T(8,128)(2,1)S(1)} collective-permute-done((bf16[2,40,256]{2,1,0:T(8,128)(2,1)S(1)}, bf16[2,40,256]{2,1,0:T(8,128)(2,1)S(1)}, u32[]{:S(2)}, u32[]{:S(2)}) %collective-permute-start.5) | collective-permute-done | bytes 40992 | tf_op jit(solution)/shard_map/ppermute | solution.py:355
  21.5 1.0 %shard_map.71 = (bf16[72,256]{1,0:T(8,128)(2,1)S(1)}, bf16[72,256]{1,0:T(8,128)(2,1)S(1)}, bf16[72,256]{1,0:T(8,128)(2,1)S(1)}, bf16[72,256]{1,0:T(8,128)(2,1)S(...) custom-call(bf16[8,48,128]{2,1,0:T(8,128)(2,1)S(1)} %fusion.6.og_ref, ...), custom_call_target="tpu_custom_call" | custom-call | flops 452984832 | bytes 1368064 | tf_op jit(solution)/shard_map/pallas_call | solution.py:30
  23.5 2.5 %collective-permute-start.8 = (bf16[72,256]{1,0:T(8,128)(2,1)S(1)}, bf16[72,256]{1,0:T(8,128)(2,1)S(1)}, u32[]{:S(2)}, u32[]{:S(2)}) collective-permute-start(bf16[72,256]{1,0:T(8,128)(2,1)S(1)} %get-tuple-element.48), channel_id=1, source_target_pairs={{0,12},{4,8},{8,4},{12,0},{1,13},{5,9},{9,5},{13,1},{2,14},{6,10},... | collective-permute-start | bytes 110600 | tf_op jit(solution)/shard_map/ppermute | solution.py:355
  26.7 2.7 %collective-permute-done.7.refs_1_ = bf16[72,256]{1,0:T(8,128)(2,1)S(1)} collective-permute-done((bf16[72,256]{1,0:T(8,128)(2,1)S(1)}, bf16[72,256]{1,0:T(8,128)(2,1)S(1)}, u32[]{:S(2)}, u32[]{:S(2)}) %collective-permute-start.7) | collective-permute-done | bytes 36896 | tf_op jit(solution)/shard_map/ppermute | solution.py:355
  30.2 0.9 %shard_map.72 = (bf16[8,64,256]{2,1,0:T(8,128)(2,1)S(1)}, bf16[64,256]{1,0:T(8,128)(2,1)S(1)}, bf16[64,256]{1,0:T(8,128)(2,1)S(1)}, bf16[72,256]{1,0:T(8,128)(2,1)S(1)}, bf16[72,256]{1,0:T(8,128)(2,1)S(1)}) custom-call(bf16[72,256]{1,0:T(8,128)(2,1)S(1)} %get-tuple-element.46.refs_0_, bf16[72,256]{1,0:T(8,128)(2,1)S(1)} %collective-permute-done.7.refs_1_, ...), custom_call_target="tpu_custom_call" | custom-call | flops 150994944 | bytes 1318912 | tf_op jit(solution)/shard_map/pallas_call | solution.py:30
  31.2 1.0 %collective-permute-start.19 = (bf16[576,256]{1,0:T(8,128)(2,1)S(1)}, bf16[576,256]{1,0:T(8,128)(2,1)S(1)}, u32[]{:S(2)}, u32[]{:S(2)}) collective-permute-start(bf16[576,256]{1,0:T(8,128)(2,1)S(1)} %shard_map.78.a_ref), channel_id=1, source_target_pairs={{0,2},{2,0},{1,3},{3,1},{4,6},{6,4},{5,7},{7,5},{8,10},{10,8},{9,1... | collective-permute-start | bytes 884744 | tf_op jit(solution)/shard_map/ppermute | solution.py:355
  32.2 1.2 %collective-permute-done.10.b_ref = bf16[72,256]{1,0:T(8,128)(2,1)S(1)} collective-permute-done((bf16[72,256]{1,0:T(8,128)(2,1)S(1)}, bf16[72,256]{1,0:T(8,128)(2,1)S(1)}, u32[]{:S(2)}, u32[]{:S(2)}) %collective-permute-start.10) | collective-permute-done | bytes 36896 | tf_op jit(solution)/shard_map/ppermute | solution.py:327
  33.4 0.9 %collective-permute-start.13 = (bf16[72,256]{1,0:T(8,128)(2,1)S(1)}, bf16[72,256]{1,0:T(8,128)(2,1)S(1)}, u32[]{:S(2)}, u32[]{:S(2)}) collective-permute-start(bf16[72,256]{1,0:T(8,128)(2,1)S(1)} %shard_map.73.refs_0_), channel_id=1, source_target_pairs={{0,8},{4,12},{8,0},{12,4},{1,9},{5,13},{9,1},{13,5},{2,10},{6,14},... | collective-permute-start | bytes 110600 | tf_op jit(solution)/shard_map/ppermute | solution.py:355
  34.3 2.1 %collective-permute-start.12 = (bf16[72,256]{1,0:T(8,128)(2,1)S(1)}, bf16[72,256]{1,0:T(8,128)(2,1)S(1)}, u32[]{:S(2)}, u32[]{:S(2)}) collective-permute-start(bf16[72,256]{1,0:T(8,128)(2,1)S(1)} %shard_map.73.refs_0_), channel_id=1, source_target_pairs={{0,12},{4,8},{8,4},{12,0},{1,13},{5,9},{9,5},{13,1},{2,14},{6,10},... | collective-permute-start | bytes 110600 | tf_op jit(solution)/shard_map/ppermute | solution.py:355
  36.9 2.5 %collective-permute-done.13.refs_3_ = bf16[72,256]{1,0:T(8,128)(2,1)S(1)} collective-permute-done((bf16[72,256]{1,0:T(8,128)(2,1)S(1)}, bf16[72,256]{1,0:T(8,128)(2,1)S(1)}, u32[]{:S(2)}, u32[]{:S(2)}) %collective-permute-start.13) | collective-permute-done | bytes 36896 | tf_op jit(solution)/shard_map/ppermute | solution.py:355
  40.7 1.2 %collective-permute-start.16 = (bf16[72,256]{1,0:T(8,128)(2,1)S(1)}, bf16[72,256]{1,0:T(8,128)(2,1)S(1)}, u32[]{:S(2)}, u32[]{:S(2)}) collective-permute-start(bf16[72,256]{1,0:T(8,128)(2,1)S(1)} %get-tuple-element.61.a_ref.refs_0_), channel_id=1, source_target_pairs={{0,2},{2,0},{1,3},{3,1},{4,6},{6,4},{5,7},{7,5},{8,10},{10,8},{9,1... | collective-permute-start | bytes 110600 | tf_op jit(solution)/shard_map/ppermute | solution.py:355
  42.3 2.5 %collective-permute-done.16.b_ref = bf16[72,256]{1,0:T(8,128)(2,1)S(1)} collective-permute-done((bf16[72,256]{1,0:T(8,128)(2,1)S(1)}, bf16[72,256]{1,0:T(8,128)(2,1)S(1)}, u32[]{:S(2)}, u32[]{:S(2)}) %collective-permute-start.16) | collective-permute-done | bytes 36896 | tf_op jit(solution)/shard_map/ppermute | solution.py:355
  45.8 1.2 %shard_map.75 = (bf16[64,8,128]{2,1,0:T(8,128)(2,1)}, f32[8,128]{1,0:T(8,128)S(1)}) custom-call(bf16[8,64,256]{2,1,0:T(8,128)(2,1)S(1)} %get-tuple-element.53.g_ref, bf16[64,256]{1,0:T(8,128)(2,1)S(1)} %collective-permute-done.14.a_ref, bf16[64,256]{1,0:T(8,128)(2,1)S(1)} %collective-permute-done.15.b_ref, bf16[192,192]{1,0:T(8,128)(2,1)S(1)} %reshape.44.w_ref), custom_call_target="tpu_custom_call" | custom-call | flops 150994944 | bytes 536576 | tf_op jit(solution)/shard_map/pallas_call | solution.py:30
  47.0 1.1 %shard_map.80 = (f32[1152,256]{1,0:T(8,128)}, f32[8,128]{1,0:T(8,128)S(1)}) custom-call(bf16[576,256]{1,0:T(8,128)(2,1)S(1)} %shard_map.79.mine_ref, bf16[576,256]{1,0:T(8,128)(2,1)S(1)} %collective-permute-done.20.other_ref), custom_call_target="tpu_custom_call" | custom-call | flops 100000000 | bytes 1773568 | tf_op jit(solution)/shard_map/pallas_call | solution.py:30
  (51 shorter events, 9.1 us)
Async XLA Ops:
  0.6 20.8 %copy-start.2 = (bf16[128,3,3,256]{3,0,2,1:T(8,128)(2,1)S(1)}, bf16[128,3,3,256]{3,0,2,1:T(8,128)(2,1)}, u32[]{:S(2)}) copy-start(bf16[128,3,3,256]{3,0,2,1:T(8,128)(2,1)} %param.6) | copy-start | bytes 1769476
  1.7 5.7 %collective-permute-start.1 = (bf16[64,128]{1,0:T(8,128)(2,1)S(1)}, bf16[64,128]{1,0:T(8,128)(2,1)S(1)}, u32[]{:S(2)}, u32[]{:S(2)}) collective-permute-start(bf16[64,128]{1,0:T(8,128)(2,1)S(1)} %get-tuple-element.69), channel_id=1, source_target_pairs={{0,1},{1,0},{4,8},{5,9},{8,4},{9,5},{12,13},{13,12},{2,3},{3,2},{6... | collective-permute-start | bytes 49160 | tf_op jit(solution)/shard_map/ppermute | solution.py:341
  2.2 5.9 %collective-permute-start = (bf16[64,128]{1,0:T(8,128)(2,1)S(1)}, bf16[64,128]{1,0:T(8,128)(2,1)S(1)}, u32[]{:S(2)}, u32[]{:S(2)}) collective-permute-start(bf16[64,128]{1,0:T(8,128)(2,1)S(1)} %get-tuple-element.70), channel_id=1, source_target_pairs={{0,4},{4,0},{8,12},{12,8},{1,5},{5,1},{9,13},{13,9},{2,6},{6,2},{1... | collective-permute-start | bytes 49160 | tf_op jit(solution)/shard_map/ppermute | solution.py:327
  8.1 4.0 %collective-permute-start.2 = (bf16[144,128]{1,0:T(8,128)(2,1)S(1)}, bf16[144,128]{1,0:T(8,128)(2,1)S(1)}, u32[]{:S(2)}, u32[]{:S(2)}) collective-permute-start(bf16[144,128]{1,0:T(8,128)(2,1)S(1)} %get-tuple-element.38), channel_id=1, source_target_pairs={{0,16},{1,2},{2,1},{3,19},{16,0},{17,18},{18,17},{19,3},{4,20},{5,... | collective-permute-start | bytes 110600 | tf_op jit(solution)/shard_map/ppermute | solution.py:351
  9.7 2.4 %collective-permute-start.3 = (bf16[144,128]{1,0:T(8,128)(2,1)S(1)}, bf16[144,128]{1,0:T(8,128)(2,1)S(1)}, u32[]{:S(2)}, u32[]{:S(2)}) collective-permute-start(bf16[144,128]{1,0:T(8,128)(2,1)S(1)} %get-tuple-element.39), channel_id=1, source_target_pairs={{0,1},{1,0},{2,3},{3,2},{4,5},{5,4},{6,7},{7,6},{8,9},{9,8},{10,11... | collective-permute-start | bytes 110600 | tf_op jit(solution)/shard_map/ppermute | solution.py:327
  9.8 0.9 %copy-start = (bf16[64,3,3,64]{3,0,2,1:T(8,128)(2,1)S(1)}, bf16[64,3,3,64]{3,0,2,1:T(8,128)(2,1)}, u32[]{:S(2)}) copy-start(bf16[64,3,3,64]{3,0,2,1:T(8,128)(2,1)} %param.5) | copy-start | bytes 221188
  13.0 6.0 %collective-permute-start.6 = (bf16[2,40,256]{2,1,0:T(8,128)(2,1)S(1)}, bf16[2,40,256]{2,1,0:T(8,128)(2,1)S(1)}, u32[]{:S(2)}, u32[]{:S(2)}) collective-permute-start(bf16[2,40,256]{2,1,0:T(8,128)(2,1)S(1)} %get-tuple-element.45.refs_0_), channel_id=1, source_target_pairs={{0,8},{4,12},{8,0},{12,4},{1,9},{5,13},{9,1},{13,5},{2,10},{6,14},... | collective-permute-start | bytes 122888 | tf_op jit(solution)/shard_map/ppermute | solution.py:355
  15.0 5.8 %collective-permute-start.5 = (bf16[2,40,256]{2,1,0:T(8,128)(2,1)S(1)}, bf16[2,40,256]{2,1,0:T(8,128)(2,1)S(1)}, u32[]{:S(2)}, u32[]{:S(2)}) collective-permute-start(bf16[2,40,256]{2,1,0:T(8,128)(2,1)S(1)} %get-tuple-element.45.refs_0_), channel_id=1, source_target_pairs={{0,12},{4,8},{8,4},{12,0},{1,13},{5,9},{9,5},{13,1},{2,14},{6,10},... | collective-permute-start | bytes 122888 | tf_op jit(solution)/shard_map/ppermute | solution.py:355
  17.5 4.0 %collective-permute-start.4 = (bf16[2,40,256]{2,1,0:T(8,128)(2,1)S(1)}, bf16[2,40,256]{2,1,0:T(8,128)(2,1)S(1)}, u32[]{:S(2)}, u32[]{:S(2)}) collective-permute-start(bf16[2,40,256]{2,1,0:T(8,128)(2,1)S(1)} %get-tuple-element.45.refs_0_), channel_id=1, source_target_pairs={{0,4},{4,0},{8,12},{12,8},{1,5},{5,1},{9,13},{13,9},{2,6},{6,2},{1... | collective-permute-start | bytes 122888 | tf_op jit(solution)/shard_map/ppermute | solution.py:355
  23.1 8.0 %collective-permute-start.18 = (bf16[576,256]{1,0:T(8,128)(2,1)S(1)}, bf16[576,256]{1,0:T(8,128)(2,1)S(1)}, u32[]{:S(2)}, u32[]{:S(2)}) collective-permute-start(bf16[576,256]{1,0:T(8,128)(2,1)S(1)} %get-tuple-element.65), channel_id=1, source_target_pairs={{0,1},{1,0},{2,3},{3,2},{4,5},{5,4},{6,7},{7,6},{8,9},{9,8},{10,11... | collective-permute-start | bytes 884744 | tf_op jit(solution)/shard_map/ppermute | solution.py:327
  23.2 6.3 %collective-permute-start.7 = (bf16[72,256]{1,0:T(8,128)(2,1)S(1)}, bf16[72,256]{1,0:T(8,128)(2,1)S(1)}, u32[]{:S(2)}, u32[]{:S(2)}) collective-permute-start(bf16[72,256]{1,0:T(8,128)(2,1)S(1)} %get-tuple-element.47), channel_id=1, source_target_pairs={{0,8},{4,12},{8,0},{12,4},{1,9},{5,13},{9,1},{13,5},{2,10},{6,14},... | collective-permute-start | bytes 110600 | tf_op jit(solution)/shard_map/ppermute | solution.py:355
  23.5 6.1 %collective-permute-start.8 = (bf16[72,256]{1,0:T(8,128)(2,1)S(1)}, bf16[72,256]{1,0:T(8,128)(2,1)S(1)}, u32[]{:S(2)}, u32[]{:S(2)}) collective-permute-start(bf16[72,256]{1,0:T(8,128)(2,1)S(1)} %get-tuple-element.48), channel_id=1, source_target_pairs={{0,12},{4,8},{8,4},{12,0},{1,13},{5,9},{9,5},{13,1},{2,14},{6,10},... | collective-permute-start | bytes 110600 | tf_op jit(solution)/shard_map/ppermute | solution.py:355
  26.0 4.2 %collective-permute-start.9 = (bf16[72,256]{1,0:T(8,128)(2,1)S(1)}, bf16[72,256]{1,0:T(8,128)(2,1)S(1)}, u32[]{:S(2)}, u32[]{:S(2)}) collective-permute-start(bf16[72,256]{1,0:T(8,128)(2,1)S(1)} %get-tuple-element.49), channel_id=1, source_target_pairs={{0,4},{4,0},{8,12},{12,8},{1,5},{5,1},{9,13},{13,9},{2,6},{6,2},{1... | collective-permute-start | bytes 110600 | tf_op jit(solution)/shard_map/ppermute | solution.py:355
  31.1 13.8 %copy-start.1 = (bf16[64,3,3,64]{3,0,2,1:T(8,128)(2,1)S(1)}, bf16[64,3,3,64]{3,0,2,1:T(8,128)(2,1)}, u32[]{:S(2)}) copy-start(bf16[64,3,3,64]{3,0,2,1:T(8,128)(2,1)} %param.5) | copy-start | bytes 221188
  31.2 9.4 %collective-permute-start.19 = (bf16[576,256]{1,0:T(8,128)(2,1)S(1)}, bf16[576,256]{1,0:T(8,128)(2,1)S(1)}, u32[]{:S(2)}, u32[]{:S(2)}) collective-permute-start(bf16[576,256]{1,0:T(8,128)(2,1)S(1)} %shard_map.78.a_ref), channel_id=1, source_target_pairs={{0,2},{2,0},{1,3},{3,1},{4,6},{6,4},{5,7},{7,5},{8,10},{10,8},{9,1... | collective-permute-start | bytes 884744 | tf_op jit(solution)/shard_map/ppermute | solution.py:355
  32.2 1.2 %collective-permute-start.10 = (bf16[72,256]{1,0:T(8,128)(2,1)S(1)}, bf16[72,256]{1,0:T(8,128)(2,1)S(1)}, u32[]{:S(2)}, u32[]{:S(2)}) collective-permute-start(bf16[72,256]{1,0:T(8,128)(2,1)S(1)} %get-tuple-element.55), channel_id=1, source_target_pairs={{0,1},{1,0},{2,3},{3,2},{4,5},{5,4},{6,7},{7,6},{8,9},{9,8},{10,11... | collective-permute-start | bytes 110600 | tf_op jit(solution)/shard_map/ppermute | solution.py:327
  33.4 6.1 %collective-permute-start.13 = (bf16[72,256]{1,0:T(8,128)(2,1)S(1)}, bf16[72,256]{1,0:T(8,128)(2,1)S(1)}, u32[]{:S(2)}, u32[]{:S(2)}) collective-permute-start(bf16[72,256]{1,0:T(8,128)(2,1)S(1)} %shard_map.73.refs_0_), channel_id=1, source_target_pairs={{0,8},{4,12},{8,0},{12,4},{1,9},{5,13},{9,1},{13,5},{2,10},{6,14},... | collective-permute-start | bytes 110600 | tf_op jit(solution)/shard_map/ppermute | solution.py:355
  34.3 5.9 %collective-permute-start.12 = (bf16[72,256]{1,0:T(8,128)(2,1)S(1)}, bf16[72,256]{1,0:T(8,128)(2,1)S(1)}, u32[]{:S(2)}, u32[]{:S(2)}) collective-permute-start(bf16[72,256]{1,0:T(8,128)(2,1)S(1)} %shard_map.73.refs_0_), channel_id=1, source_target_pairs={{0,12},{4,8},{8,4},{12,0},{1,13},{5,9},{9,5},{13,1},{2,14},{6,10},... | collective-permute-start | bytes 110600 | tf_op jit(solution)/shard_map/ppermute | solution.py:355
  36.4 4.1 %collective-permute-start.11 = (bf16[72,256]{1,0:T(8,128)(2,1)S(1)}, bf16[72,256]{1,0:T(8,128)(2,1)S(1)}, u32[]{:S(2)}, u32[]{:S(2)}) collective-permute-start(bf16[72,256]{1,0:T(8,128)(2,1)S(1)} %shard_map.73.refs_0_), channel_id=1, source_target_pairs={{0,4},{4,0},{8,12},{12,8},{1,5},{5,1},{9,13},{13,9},{2,6},{6,2},{1... | collective-permute-start | bytes 110600 | tf_op jit(solution)/shard_map/ppermute | solution.py:355
  40.6 6.3 %collective-permute-start.20 = (bf16[576,256]{1,0:T(8,128)(2,1)S(1)}, bf16[576,256]{1,0:T(8,128)(2,1)S(1)}, u32[]{:S(2)}, u32[]{:S(2)}) collective-permute-start(bf16[576,256]{1,0:T(8,128)(2,1)S(1)} %shard_map.79.mine_ref), channel_id=1, source_target_pairs={{0,1},{1,0},{2,3},{3,2},{4,5},{5,4},{6,7},{7,6},{8,9},{9,8},{10,11... | collective-permute-start | bytes 884744 | tf_op jit(solution)/shard_map/ppermute | solution.py:327
  40.7 4.0 %collective-permute-start.16 = (bf16[72,256]{1,0:T(8,128)(2,1)S(1)}, bf16[72,256]{1,0:T(8,128)(2,1)S(1)}, u32[]{:S(2)}, u32[]{:S(2)}) collective-permute-start(bf16[72,256]{1,0:T(8,128)(2,1)S(1)} %get-tuple-element.61.a_ref.refs_0_), channel_id=1, source_target_pairs={{0,2},{2,0},{1,3},{3,1},{4,6},{6,4},{5,7},{7,5},{8,10},{10,8},{9,1... | collective-permute-start | bytes 110600 | tf_op jit(solution)/shard_map/ppermute | solution.py:355
  41.9 3.9 %collective-permute-start.14 = (bf16[64,256]{1,0:T(8,128)(2,1)S(1)}, bf16[64,256]{1,0:T(8,128)(2,1)S(1)}, u32[]{:S(2)}, u32[]{:S(2)}) collective-permute-start(bf16[64,256]{1,0:T(8,128)(2,1)S(1)} %get-tuple-element.58), channel_id=1, source_target_pairs={{0,4},{4,0},{8,12},{12,8},{1,5},{5,1},{9,13},{13,9},{2,6},{6,2},{1... | collective-permute-start | bytes 98312 | tf_op jit(solution)/shard_map/ppermute | solution.py:327
  42.3 3.5 %collective-permute-start.15 = (bf16[64,256]{1,0:T(8,128)(2,1)S(1)}, bf16[64,256]{1,0:T(8,128)(2,1)S(1)}, u32[]{:S(2)}, u32[]{:S(2)}) collective-permute-start(bf16[64,256]{1,0:T(8,128)(2,1)S(1)} %get-tuple-element.59), channel_id=1, source_target_pairs={{0,1},{1,0},{4,8},{5,9},{8,4},{9,5},{12,13},{13,12},{2,3},{3,2},{6... | collective-permute-start | bytes 98312 | tf_op jit(solution)/shard_map/ppermute | solution.py:341
  44.8 3.3 %collective-permute-start.17 = (bf16[72,256]{1,0:T(8,128)(2,1)S(1)}, bf16[72,256]{1,0:T(8,128)(2,1)S(1)}, u32[]{:S(2)}, u32[]{:S(2)}) collective-permute-start(bf16[72,256]{1,0:T(8,128)(2,1)S(1)} %shard_map.76.mine_ref), channel_id=1, source_target_pairs={{0,1},{1,0},{2,3},{3,2},{4,5},{5,4},{6,7},{7,6},{8,9},{9,8},{10,11... | collective-permute-start | bytes 110600 | tf_op jit(solution)/shard_map/ppermute | solution.py:327

commit v12 on v11

--- a/solution.py
+++ b/solution.py
@@ -80,7 +80,11 @@
     return jnp.where(lane == 4 * c + 2 * i + j, 1.0, 0.0).astype(BF16)
 
 
-def constants(w_ref, joined_ref, pool_ref, back_ref, order_ref, *, total):
+def constants(w_ref, joined_ref, back_w_ref, pool_ref, back_ref, order_ref, *, total):
+    turned = [w_ref[2 - i].astype(F32).T for i in range(3)]
+    back_w_ref[...] = jnp.concatenate(
+        [jnp.concatenate([t[:, 64 * j : 64 * j + 64] for t in turned], 1) for j in range(3)], 0
+    ).astype(BF16)
     joined_ref[...] = jnp.concatenate([w_ref[0], w_ref[1], w_ref[2]], axis=1)
     pool_ref[...] = pool_matrix(strip_index(), total)
     back_ref[...] = pool_matrix(strip_index(), total, back=True)
@@ -241,6 +245,13 @@
     refs[-1][...] = (a_ref[...].astype(F32) + b_ref[...].astype(F32)).astype(BF16)
 
 
+def add_halves(a_ref, b_ref, two_ref, one_ref):
+    half = two_ref.shape[0]
+    total = (a_ref[...].astype(F32) + b_ref[...].astype(F32)).astype(BF16)
+    two_ref[...] = total[:half]
+    one_ref[...] = total[half:]
+
+
 def sum_rows(*refs):
     *refs, a_ref, b_ref, out_ref, passed_a_ref, passed_b_ref = refs
     terms = dict(zip(row_order(len(refs), near_first=True), (ref[...].astype(F32) for ref in refs)))
@@ -254,7 +265,8 @@
 
 def grad_pre_one(*refs, bands):
     terms, refs = refs[:bands], refs[bands:]
-    slope_ref, wide_ref, pool_ref, order_ref, g_ref, a_ref, b_ref, keep_ref, send_ref, part_ref = refs
+    slope_ref, wide_ref, pool_ref, order_ref, keep_two_ref, send_two_ref, *refs = refs
+    g_ref, a_ref, b_ref, keep_ref, send_ref, part_ref = refs
     pair = lax.axis_index("pair")
     summed = terms[0][...].astype(F32)
     for k in range(1, bands):
@@ -283,8 +295,10 @@
     b_ref[...] = jnp.where(even, first, last).astype(BF16)
     part_ref[:96] = jnp.concatenate([acc[:96, :128], acc[96:, :128]], 1)
     part_ref[96:] = jnp.concatenate([acc[48 * q : 48 * q + 48, 128:] for q in range(4)], 1)
-    for ref, place in ((keep_ref, pair), (send_ref, 1 - pair)):
-        ref[...] = part_ref[pl.ds(pl.multiple_of(place * HALF_ONE, 8), HALF_ONE)].astype(BF16)
+    half = keep_two_ref.shape[0]
+    for ref, two_ref, place in ((keep_ref, keep_two_ref, pair), (send_ref, send_two_ref, 1 - pair)):
+        ref[:half] = two_ref[...]
+        ref[half:] = part_ref[pl.ds(pl.multiple_of(place * HALF_ONE, 8), HALF_ONE)].astype(BF16)
 
 
 def layer_one_back(g_ref, a_ref, b_ref, w_ref, out_ref, done_ref, *, bands):
@@ -311,7 +325,7 @@
         copy.wait()
 
 
-def finish_one(mine_ref, other_ref, _, __, out_ref, flat_ref, *, scale):
+def finish_one(mine_ref, other_ref, _, out_ref, flat_ref, *, scale):
     pair = lax.axis_index("pair")
     for ref, place in ((mine_ref, pair), (other_ref, 1 - pair)):
         flat_ref[pl.ds(pl.multiple_of(place * HALF_ONE, 8), HALF_ONE)] = ref[...].astype(F32) * scale
@@ -390,7 +404,6 @@
     total = own_cols * strips
 
     taps_one = jnp.transpose(filters_one, (1, 2, 0, 3)).reshape(3, 3 * channels, channels)
-    back_one = jnp.transpose(filters_one[:, ::-1], (2, 3, 1, 0)).reshape(3 * channels, 3 * channels)
     taps_two = jnp.transpose(filters_two, (1, 2, 0, 3)).reshape(3, 3 * filters, 4 * channels)
 
     og = jnp.transpose(out_grad, (1, 2, 0))
@@ -399,9 +412,9 @@
     even = band % 2 == 0
     to_a, to_b = jnp.where(even, x[-1], x[0]), jnp.where(even, x[0], x[-1])
     head, tail = og[:edge], og[-edge:]
-    joined_one, pool, pool_back, order = whole_call(
+    joined_one, back_one, pool, pool_back, order = whole_call(
         functools.partial(constants, total=total),
-        [shaped((3 * channels, 3 * channels))] + [shaped((2 * PITCH, 256))] * 2 + [shaped((256, 256))],
+        [shaped((3 * channels, 3 * channels))] * 2 + [shaped((2 * PITCH, 256))] * 2 + [shaped((256, 256))],
         [taps_one],
         10**8,
     )
@@ -459,13 +472,17 @@
         functools.partial(grad_pre_one, bands=bands),
         [shaped((band_rows, channels, 256))]
         + [shaped((channels, 256))] * 2
-        + [shaped((HALF_ONE, 256))] * 2,
-        received + [slope, wide, pool_back, order],
+        + [shaped((half + HALF_ONE, 256))] * 2,
+        received + [slope, wide, pool_back, order, keep_two, send_two],
         2 * 8 * 192 * 192 * 256,
         scratch=[pltpu.VMEM((144, 256), F32)],
     )
-    one = added(keep, even_swap(send, "pair", 2))
-    two = added(keep_two, even_swap(send_two, "pair", 2), keep)
+    two, one = whole_call(
+        add_halves,
+        [shaped((half, 256)), shaped((HALF_ONE, 256))],
+        [keep, even_swap(send, "pair", 2)],
+        0,
+    )
     columns = lax.axis_size("col")
     two, two_more = sum_but_last(two, "col", columns)
     ones = row_swaps([one] * bands, bands, near_first=True)
@@ -487,14 +504,14 @@
         scratch=[pltpu.VMEM((2, half, 256), F32), pltpu.SemaphoreType.DMA((2,))],
         out_spaces=[pl.ANY, pltpu.VMEM],
     )
-    mine_one = added(*sum_but_last(one, "col", columns))
+    mine_one = added(*sum_but_last(one, "col", columns), wrote)
     (grad_one,) = whole_call(
         functools.partial(finish_one, scale=1.0 / math.sqrt(height * width)),
         [shaped((3, 3 * channels, channels), F32)],
-        [mine_one, even_swap(mine_one, "pair", 2), wrote, done],
+        [mine_one, even_swap(mine_one, "pair", 2), done],
         1,
         scratch=[pltpu.VMEM((144, 256), F32)],
-        after=2,
+        after=1,
     )
     grad_two = jnp.transpose(grad_two.reshape(3, 3, filters, 4 * channels), (2, 0, 1, 3))
     grad_one = jnp.transpose(grad_one.reshape(3, 3, channels, channels), (2, 0, 1, 3))

time: 49.1 us -> 48.3 us (0.984)
  waiting for transfers between devices: 17.3 us -> 16.8 us
    ppermute x11, waiting for transfers between devices: 13.4 us -> 12.5 us  [xor_swap(): return lax.ppermute(values, axis, [(n, n ^ k) for n in range(count)])]
    ppermute x7 -> x6, waiting for transfers between devices: 2.54 us -> 3.12 us  [even_swap(): return lax.ppermute(values, axis, [(n, n ^ 1) for n in range(count)])]
    ppermute x7 -> x6, starting transfers between devices: 4.83 us -> 5.13 us  [even_swap(): return lax.ppermute(values, axis, [(n, n ^ 1) for n in range(count)])]
    pallas_call x15 -> x14, Pallas kernels: 6.97 us -> 7.05 us  [whole_call(): pl.pallas_call(body, out_shape=outs, in_specs=specs, out_specs=[pl.BlockS...]
    unnamed x8 -> x6, local copies, waits for them, and re-layouts: 2.75 us -> 2.75 us
  transfers between devices with their start and end apart: 21 -> 20, of which waited for: 14 -> 15; matrix products, arithmetic and copies ran while one was open for 3% -> 2% of each run, Pallas kernels for 7% -> 7%
where the time goes in v12:
time: 48.3 us; the launch traced here: 48.1 us
  starting transfers between devices  20.7 us (43%)
  waiting for transfers between devices  16.8 us (35%)
  Pallas kernels  7.05 us (15%)
  local copies, waits for them, and re-layouts  2.77 us (6%)
  between operations  0.81 us (2%)
    ppermute x11, starting transfers between devices, xor_swap(): return lax.ppermute(values, axis, [(n, n ^ k) for n in range(count)])  13.5 us
    ppermute x11, waiting for transfers between devices, xor_swap(): return lax.ppermute(values, axis, [(n, n ^ k) for n in range(count)])  12.5 us
    pallas_call x14, Pallas kernels, whole_call(): pl.pallas_call(body, out_shape=outs, in_specs=specs, out_specs=[pl.BlockS...  7.05 us
    ppermute x6, starting transfers between devices, even_swap(): return lax.ppermute(values, axis, [(n, n ^ 1) for n in range(count)])  5.13 us
    ppermute x6, waiting for transfers between devices, even_swap(): return lax.ppermute(values, axis, [(n, n ^ 1) for n in range(count)])  3.12 us
    unnamed x6, local copies, waits for them, and re-layouts  2.75 us
    ppermute x1, starting transfers between devices, odd_strip_swap(): return lax.ppermute(values, ('grp',) + COLS, steps)  1.56 us
    ppermute x1, waiting for transfers between devices, odd_strip_swap(): return lax.ppermute(values, ('grp',) + COLS, steps)  1.18 us
  transfers between devices with their start and end apart: 20, of which 15 were waited for; matrix products, arithmetic and copies ran while one was open for 2% of the time, Pallas kernels for 7%

profile of v12, /device:TPU:0, one launch (start us, length us, event | category | flops | bytes accessed | tf_op | source)
XLA Modules:
  0.0 48.1 jit_solution(16718565269892697025)
XLA Ops:
  0.7 1.0 %copy.19 = bf16[64,8,128]{2,0,1:T(8,128)(2,1)S(1)} copy(bf16[64,8,128]{2,1,0:T(8,128)(2,1)} %param.4) | data formatting | bytes 262144 | tf_op args[0]
  2.2 4.1 %collective-permute-start = (bf16[64,128]{1,0:T(8,128)(2,1)S(1)}, bf16[64,128]{1,0:T(8,128)(2,1)S(1)}, u32[]{:S(2)}, u32[]{:S(2)}) collective-permute-start(bf16[64,128]{1,0:T(8,128)(2,1)S(1)} %get-tuple-element.76), channel_id=1, source_target_pairs={{0,4},{4,0},{8,12},{12,8},{1,5},{5,1},{9,13},{13,9},{2,6},{6,2},{1... | collective-permute-start | bytes 49160 | tf_op jit(solution)/shard_map/ppermute | solution.py:341
  8.1 1.6 %collective-permute-start.2 = (bf16[144,128]{1,0:T(8,128)(2,1)S(1)}, bf16[144,128]{1,0:T(8,128)(2,1)S(1)}, u32[]{:S(2)}, u32[]{:S(2)}) collective-permute-start(bf16[144,128]{1,0:T(8,128)(2,1)S(1)} %get-tuple-element.41), channel_id=1, source_target_pairs={{0,16},{1,2},{2,1},{3,19},{16,0},{17,18},{18,17},{19,3},{4,20},{5,... | collective-permute-start | bytes 110600 | tf_op jit(solution)/shard_map/ppermute | solution.py:365
  9.8 0.9 %copy-done.1 = bf16[64,3,3,64]{3,0,2,1:T(8,128)(2,1)S(1)} copy-done((bf16[64,3,3,64]{3,0,2,1:T(8,128)(2,1)S(1)}, bf16[64,3,3,64]{3,0,2,1:T(8,128)(2,1)}, u32[]{:S(2)}) %copy-start.1) | copy-done | bytes 73752
  10.9 1.2 %collective-permute-done.2.b_ref = bf16[144,128]{1,0:T(8,128)(2,1)S(1)} collective-permute-done((bf16[144,128]{1,0:T(8,128)(2,1)S(1)}, bf16[144,128]{1,0:T(8,128)(2,1)S(1)}, u32[]{:S(2)}, u32[]{:S(2)}) %collective-permute-start.2) | collective-permute-done | bytes 36896 | tf_op jit(solution)/shard_map/ppermute | solution.py:365
  13.0 2.0 %collective-permute-start.6 = (bf16[2,40,256]{2,1,0:T(8,128)(2,1)S(1)}, bf16[2,40,256]{2,1,0:T(8,128)(2,1)S(1)}, u32[]{:S(2)}, u32[]{:S(2)}) collective-permute-start(bf16[2,40,256]{2,1,0:T(8,128)(2,1)S(1)} %get-tuple-element.48.refs_0_), channel_id=1, source_target_pairs={{0,8},{4,12},{8,0},{12,4},{1,9},{5,13},{9,1},{13,5},{2,10},{6,14},... | collective-permute-start | bytes 122888 | tf_op jit(solution)/shard_map/ppermute | solution.py:369
  15.0 2.5 %collective-permute-start.5 = (bf16[2,40,256]{2,1,0:T(8,128)(2,1)S(1)}, bf16[2,40,256]{2,1,0:T(8,128)(2,1)S(1)}, u32[]{:S(2)}, u32[]{:S(2)}) collective-permute-start(bf16[2,40,256]{2,1,0:T(8,128)(2,1)S(1)} %get-tuple-element.48.refs_0_), channel_id=1, source_target_pairs={{0,12},{4,8},{8,4},{12,0},{1,13},{5,9},{9,5},{13,1},{2,14},{6,10},... | collective-permute-start | bytes 122888 | tf_op jit(solution)/shard_map/ppermute | solution.py:369
  17.6 1.4 %collective-permute-done.6.refs_3_ = bf16[2,40,256]{2,1,0:T(8,128)(2,1)S(1)} collective-permute-done((bf16[2,40,256]{2,1,0:T(8,128)(2,1)S(1)}, bf16[2,40,256]{2,1,0:T(8,128)(2,1)S(1)}, u32[]{:S(2)}, u32[]{:S(2)}) %collective-permute-start.6) | collective-permute-done | bytes 40992 | tf_op jit(solution)/shard_map/ppermute | solution.py:369
  19.0 1.8 %collective-permute-done.5.refs_2_ = bf16[2,40,256]{2,1,0:T(8,128)(2,1)S(1)} collective-permute-done((bf16[2,40,256]{2,1,0:T(8,128)(2,1)S(1)}, bf16[2,40,256]{2,1,0:T(8,128)(2,1)S(1)}, u32[]{:S(2)}, u32[]{:S(2)}) %collective-permute-start.5) | collective-permute-done | bytes 40992 | tf_op jit(solution)/shard_map/ppermute | solution.py:369
  21.5 1.0 %shard_map.71 = (bf16[72,256]{1,0:T(8,128)(2,1)S(1)}, bf16[72,256]{1,0:T(8,128)(2,1)S(1)}, bf16[72,256]{1,0:T(8,128)(2,1)S(1)}, bf16[72,256]{1,0:T(8,128)(2,1)S(...) custom-call(bf16[8,48,128]{2,1,0:T(8,128)(2,1)S(1)} %fusion.6.og_ref, ...), custom_call_target="tpu_custom_call" | custom-call | flops 452984832 | bytes 1368064 | tf_op jit(solution)/shard_map/pallas_call | solution.py:30
  22.9 2.5 %collective-permute-start.8 = (bf16[72,256]{1,0:T(8,128)(2,1)S(1)}, bf16[72,256]{1,0:T(8,128)(2,1)S(1)}, u32[]{:S(2)}, u32[]{:S(2)}) collective-permute-start(bf16[72,256]{1,0:T(8,128)(2,1)S(1)} %get-tuple-element.51), channel_id=1, source_target_pairs={{0,12},{4,8},{8,4},{12,0},{1,13},{5,9},{9,5},{13,1},{2,14},{6,10},... | collective-permute-start | bytes 110600 | tf_op jit(solution)/shard_map/ppermute | solution.py:369
  26.6 1.0 %collective-permute-done.7.refs_1_ = bf16[72,256]{1,0:T(8,128)(2,1)S(1)} collective-permute-done((bf16[72,256]{1,0:T(8,128)(2,1)S(1)}, bf16[72,256]{1,0:T(8,128)(2,1)S(1)}, u32[]{:S(2)}, u32[]{:S(2)}) %collective-permute-start.7) | collective-permute-done | bytes 36896 | tf_op jit(solution)/shard_map/ppermute | solution.py:369
  27.7 1.0 %collective-permute-done.8.refs_2_ = bf16[72,256]{1,0:T(8,128)(2,1)S(1)} collective-permute-done((bf16[72,256]{1,0:T(8,128)(2,1)S(1)}, bf16[72,256]{1,0:T(8,128)(2,1)S(1)}, u32[]{:S(2)}, u32[]{:S(2)}) %collective-permute-start.8) | collective-permute-done | bytes 36896 | tf_op jit(solution)/shard_map/ppermute | solution.py:369
  30.3 1.6 %collective-permute-done.10.b_ref = bf16[648,256]{1,0:T(8,128)(2,1)S(1)} collective-permute-done((bf16[648,256]{1,0:T(8,128)(2,1)S(1)}, bf16[648,256]{1,0:T(8,128)(2,1)S(1)}, u32[]{:S(2)}, u32[]{:S(2)}) %collective-permute-start.10) | collective-permute-done | bytes 331808 | tf_op jit(solution)/shard_map/ppermute | solution.py:341
  32.0 1.0 %collective-permute-start.17 = (bf16[576,256]{1,0:T(8,128)(2,1)S(1)}, bf16[576,256]{1,0:T(8,128)(2,1)S(1)}, u32[]{:S(2)}, u32[]{:S(2)}) collective-permute-start(bf16[576,256]{1,0:T(8,128)(2,1)S(1)} %get-tuple-element.71.a_ref), channel_id=1, source_target_pairs={{0,2},{2,0},{1,3},{3,1},{4,6},{6,4},{5,7},{7,5},{8,10},{10,8},{9,1... | collective-permute-start | bytes 884744 | tf_op jit(solution)/shard_map/ppermute | solution.py:369
  33.0 1.0 %collective-permute-start.13 = (bf16[72,256]{1,0:T(8,128)(2,1)S(1)}, bf16[72,256]{1,0:T(8,128)(2,1)S(1)}, u32[]{:S(2)}, u32[]{:S(2)}) collective-permute-start(bf16[72,256]{1,0:T(8,128)(2,1)S(1)} %get-tuple-element.63.refs_0_), channel_id=1, source_target_pairs={{0,8},{4,12},{8,0},{12,4},{1,9},{5,13},{9,1},{13,5},{2,10},{6,14},... | collective-permute-start | bytes 110600 | tf_op jit(solution)/shard_map/ppermute | solution.py:369
  34.0 2.0 %collective-permute-start.12 = (bf16[72,256]{1,0:T(8,128)(2,1)S(1)}, bf16[72,256]{1,0:T(8,128)(2,1)S(1)}, u32[]{:S(2)}, u32[]{:S(2)}) collective-permute-start(bf16[72,256]{1,0:T(8,128)(2,1)S(1)} %get-tuple-element.63.refs_0_), channel_id=1, source_target_pairs={{0,12},{4,8},{8,4},{12,0},{1,13},{5,9},{9,5},{13,1},{2,14},{6,10},... | collective-permute-start | bytes 110600 | tf_op jit(solution)/shard_map/ppermute | solution.py:369
  36.4 2.3 %collective-permute-done.13.refs_3_ = bf16[72,256]{1,0:T(8,128)(2,1)S(1)} collective-permute-done((bf16[72,256]{1,0:T(8,128)(2,1)S(1)}, bf16[72,256]{1,0:T(8,128)(2,1)S(1)}, u32[]{:S(2)}, u32[]{:S(2)}) %collective-permute-start.13) | collective-permute-done | bytes 36896 | tf_op jit(solution)/shard_map/ppermute | solution.py:369
  38.8 1.0 %collective-permute-done.12.refs_2_ = bf16[72,256]{1,0:T(8,128)(2,1)S(1)} collective-permute-done((bf16[72,256]{1,0:T(8,128)(2,1)S(1)}, bf16[72,256]{1,0:T(8,128)(2,1)S(1)}, u32[]{:S(2)}, u32[]{:S(2)}) %collective-permute-start.12) | collective-permute-done | bytes 36896 | tf_op jit(solution)/shard_map/ppermute | solution.py:369
  40.2 0.9 %collective-permute-done.17.b_ref = bf16[576,256]{1,0:T(8,128)(2,1)S(1)} collective-permute-done((bf16[576,256]{1,0:T(8,128)(2,1)S(1)}, bf16[576,256]{1,0:T(8,128)(2,1)S(1)}, u32[]{:S(2)}, u32[]{:S(2)}) %collective-permute-start.17) | collective-permute-done | bytes 294944 | tf_op jit(solution)/shard_map/ppermute | solution.py:369
  41.2 1.0 %collective-permute-start.16 = (bf16[72,256]{1,0:T(8,128)(2,1)S(1)}, bf16[72,256]{1,0:T(8,128)(2,1)S(1)}, u32[]{:S(2)}, u32[]{:S(2)}) collective-permute-start(bf16[72,256]{1,0:T(8,128)(2,1)S(1)} %get-tuple-element.70.refs_0_.a_ref), channel_id=1, source_target_pairs={{0,2},{2,0},{1,3},{3,1},{4,6},{6,4},{5,7},{7,5},{8,10},{10,8},{9,1... | collective-permute-start | bytes 110600 | tf_op jit(solution)/shard_map/ppermute | solution.py:369
  42.9 1.1 %shard_map.78 = (f32[1152,256]{1,0:T(8,128)}, f32[8,128]{1,0:T(8,128)S(1)}) custom-call(bf16[576,256]{1,0:T(8,128)(2,1)S(1)} %shard_map.77.mine_ref, bf16[576,256]{1,0:T(8,128)(2,1)S(1)} %collective-permute-done.18.other_ref), custom_call_target="tpu_custom_call" | custom-call | flops 100000000 | bytes 1773568 | tf_op jit(solution)/shard_map/pallas_call | solution.py:30
  44.0 1.3 %collective-permute-done.16.b_ref = bf16[72,256]{1,0:T(8,128)(2,1)S(1)} collective-permute-done((bf16[72,256]{1,0:T(8,128)(2,1)S(1)}, bf16[72,256]{1,0:T(8,128)(2,1)S(1)}, u32[]{:S(2)}, u32[]{:S(2)}) %collective-permute-start.16) | collective-permute-done | bytes 36896 | tf_op jit(solution)/shard_map/ppermute | solution.py:369
  46.1 1.2 %shard_map.76 = (bf16[64,8,128]{2,1,0:T(8,128)(2,1)}, f32[8,128]{1,0:T(8,128)S(1)}) custom-call(bf16[8,64,256]{2,1,0:T(8,128)(2,1)S(1)} %get-tuple-element.60.g_ref, bf16[64,256]{1,0:T(8,128)(2,1)S(1)} %collective-permute-done.14.a_ref, bf16[64,256]{1,0:T(8,128)(2,1)S(1)} %collective-permute-done.15.b_ref, bf16[192,192]{1,0:T(8,128)(2,1)S(1)} %get-tuple-element.68.w_ref), custom_call_target="tpu_custom_call" | custom-call | flops 150994944 | bytes 536576 | tf_op jit(solution)/shard_map/pallas_call | solution.py:30
  (43 shorter events, 11.0 us)
Async XLA Ops:
  0.6 20.8 %copy-start = (bf16[128,3,3,256]{3,0,2,1:T(8,128)(2,1)S(1)}, bf16[128,3,3,256]{3,0,2,1:T(8,128)(2,1)}, u32[]{:S(2)}) copy-start(bf16[128,3,3,256]{3,0,2,1:T(8,128)(2,1)} %param.6) | copy-start | bytes 1769476
  1.7 5.7 %collective-permute-start.1 = (bf16[64,128]{1,0:T(8,128)(2,1)S(1)}, bf16[64,128]{1,0:T(8,128)(2,1)S(1)}, u32[]{:S(2)}, u32[]{:S(2)}) collective-permute-start(bf16[64,128]{1,0:T(8,128)(2,1)S(1)} %get-tuple-element.75), channel_id=1, source_target_pairs={{0,1},{1,0},{4,8},{5,9},{8,4},{9,5},{12,13},{13,12},{2,3},{3,2},{6... | collective-permute-start | bytes 49160 | tf_op jit(solution)/shard_map/ppermute | solution.py:355
  2.2 5.9 %collective-permute-start = (bf16[64,128]{1,0:T(8,128)(2,1)S(1)}, bf16[64,128]{1,0:T(8,128)(2,1)S(1)}, u32[]{:S(2)}, u32[]{:S(2)}) collective-permute-start(bf16[64,128]{1,0:T(8,128)(2,1)S(1)} %get-tuple-element.76), channel_id=1, source_target_pairs={{0,4},{4,0},{8,12},{12,8},{1,5},{5,1},{9,13},{13,9},{2,6},{6,2},{1... | collective-permute-start | bytes 49160 | tf_op jit(solution)/shard_map/ppermute | solution.py:341
  8.1 4.0 %collective-permute-start.2 = (bf16[144,128]{1,0:T(8,128)(2,1)S(1)}, bf16[144,128]{1,0:T(8,128)(2,1)S(1)}, u32[]{:S(2)}, u32[]{:S(2)}) collective-permute-start(bf16[144,128]{1,0:T(8,128)(2,1)S(1)} %get-tuple-element.41), channel_id=1, source_target_pairs={{0,16},{1,2},{2,1},{3,19},{16,0},{17,18},{18,17},{19,3},{4,20},{5,... | collective-permute-start | bytes 110600 | tf_op jit(solution)/shard_map/ppermute | solution.py:365
  9.7 2.4 %collective-permute-start.3 = (bf16[144,128]{1,0:T(8,128)(2,1)S(1)}, bf16[144,128]{1,0:T(8,128)(2,1)S(1)}, u32[]{:S(2)}, u32[]{:S(2)}) collective-permute-start(bf16[144,128]{1,0:T(8,128)(2,1)S(1)} %get-tuple-element.42), channel_id=1, source_target_pairs={{0,1},{1,0},{2,3},{3,2},{4,5},{5,4},{6,7},{7,6},{8,9},{9,8},{10,11... | collective-permute-start | bytes 110600 | tf_op jit(solution)/shard_map/ppermute | solution.py:341
  9.8 0.9 %copy-start.1 = (bf16[64,3,3,64]{3,0,2,1:T(8,128)(2,1)S(1)}, bf16[64,3,3,64]{3,0,2,1:T(8,128)(2,1)}, u32[]{:S(2)}) copy-start(bf16[64,3,3,64]{3,0,2,1:T(8,128)(2,1)} %param.5) | copy-start | bytes 221188
  13.0 6.0 %collective-permute-start.6 = (bf16[2,40,256]{2,1,0:T(8,128)(2,1)S(1)}, bf16[2,40,256]{2,1,0:T(8,128)(2,1)S(1)}, u32[]{:S(2)}, u32[]{:S(2)}) collective-permute-start(bf16[2,40,256]{2,1,0:T(8,128)(2,1)S(1)} %get-tuple-element.48.refs_0_), channel_id=1, source_target_pairs={{0,8},{4,12},{8,0},{12,4},{1,9},{5,13},{9,1},{13,5},{2,10},{6,14},... | collective-permute-start | bytes 122888 | tf_op jit(solution)/shard_map/ppermute | solution.py:369
  15.0 5.8 %collective-permute-start.5 = (bf16[2,40,256]{2,1,0:T(8,128)(2,1)S(1)}, bf16[2,40,256]{2,1,0:T(8,128)(2,1)S(1)}, u32[]{:S(2)}, u32[]{:S(2)}) collective-permute-start(bf16[2,40,256]{2,1,0:T(8,128)(2,1)S(1)} %get-tuple-element.48.refs_0_), channel_id=1, source_target_pairs={{0,12},{4,8},{8,4},{12,0},{1,13},{5,9},{9,5},{13,1},{2,14},{6,10},... | collective-permute-start | bytes 122888 | tf_op jit(solution)/shard_map/ppermute | solution.py:369
  17.5 4.0 %collective-permute-start.4 = (bf16[2,40,256]{2,1,0:T(8,128)(2,1)S(1)}, bf16[2,40,256]{2,1,0:T(8,128)(2,1)S(1)}, u32[]{:S(2)}, u32[]{:S(2)}) collective-permute-start(bf16[2,40,256]{2,1,0:T(8,128)(2,1)S(1)} %get-tuple-element.48.refs_0_), channel_id=1, source_target_pairs={{0,4},{4,0},{8,12},{12,8},{1,5},{5,1},{9,13},{13,9},{2,6},{6,2},{1... | collective-permute-start | bytes 122888 | tf_op jit(solution)/shard_map/ppermute | solution.py:369
  22.5 5.2 %collective-permute-start.7 = (bf16[72,256]{1,0:T(8,128)(2,1)S(1)}, bf16[72,256]{1,0:T(8,128)(2,1)S(1)}, u32[]{:S(2)}, u32[]{:S(2)}) collective-permute-start(bf16[72,256]{1,0:T(8,128)(2,1)S(1)} %get-tuple-element.50), channel_id=1, source_target_pairs={{0,8},{4,12},{8,0},{12,4},{1,9},{5,13},{9,1},{13,5},{2,10},{6,14},... | collective-permute-start | bytes 110600 | tf_op jit(solution)/shard_map/ppermute | solution.py:369
  22.9 5.8 %collective-permute-start.8 = (bf16[72,256]{1,0:T(8,128)(2,1)S(1)}, bf16[72,256]{1,0:T(8,128)(2,1)S(1)}, u32[]{:S(2)}, u32[]{:S(2)}) collective-permute-start(bf16[72,256]{1,0:T(8,128)(2,1)S(1)} %get-tuple-element.51), channel_id=1, source_target_pairs={{0,12},{4,8},{8,4},{12,0},{1,13},{5,9},{9,5},{13,1},{2,14},{6,10},... | collective-permute-start | bytes 110600 | tf_op jit(solution)/shard_map/ppermute | solution.py:369
  25.3 4.0 %collective-permute-start.9 = (bf16[72,256]{1,0:T(8,128)(2,1)S(1)}, bf16[72,256]{1,0:T(8,128)(2,1)S(1)}, u32[]{:S(2)}, u32[]{:S(2)}) collective-permute-start(bf16[72,256]{1,0:T(8,128)(2,1)S(1)} %get-tuple-element.52), channel_id=1, source_target_pairs={{0,4},{4,0},{8,12},{12,8},{1,5},{5,1},{9,13},{13,9},{2,6},{6,2},{1... | collective-permute-start | bytes 110600 | tf_op jit(solution)/shard_map/ppermute | solution.py:369
  30.2 1.7 %collective-permute-start.10 = (bf16[648,256]{1,0:T(8,128)(2,1)S(1)}, bf16[648,256]{1,0:T(8,128)(2,1)S(1)}, u32[]{:S(2)}, u32[]{:S(2)}) collective-permute-start(bf16[648,256]{1,0:T(8,128)(2,1)S(1)} %get-tuple-element.62), channel_id=1, source_target_pairs={{0,1},{1,0},{2,3},{3,2},{4,5},{5,4},{6,7},{7,6},{8,9},{9,8},{10,11... | collective-permute-start | bytes 995336 | tf_op jit(solution)/shard_map/ppermute | solution.py:341
  32.0 9.1 %collective-permute-start.17 = (bf16[576,256]{1,0:T(8,128)(2,1)S(1)}, bf16[576,256]{1,0:T(8,128)(2,1)S(1)}, u32[]{:S(2)}, u32[]{:S(2)}) collective-permute-start(bf16[576,256]{1,0:T(8,128)(2,1)S(1)} %get-tuple-element.71.a_ref), channel_id=1, source_target_pairs={{0,2},{2,0},{1,3},{3,1},{4,6},{6,4},{5,7},{7,5},{8,10},{10,8},{9,1... | collective-permute-start | bytes 884744 | tf_op jit(solution)/shard_map/ppermute | solution.py:369
  33.0 5.8 %collective-permute-start.13 = (bf16[72,256]{1,0:T(8,128)(2,1)S(1)}, bf16[72,256]{1,0:T(8,128)(2,1)S(1)}, u32[]{:S(2)}, u32[]{:S(2)}) collective-permute-start(bf16[72,256]{1,0:T(8,128)(2,1)S(1)} %get-tuple-element.63.refs_0_), channel_id=1, source_target_pairs={{0,8},{4,12},{8,0},{12,4},{1,9},{5,13},{9,1},{13,5},{2,10},{6,14},... | collective-permute-start | bytes 110600 | tf_op jit(solution)/shard_map/ppermute | solution.py:369
  34.0 5.8 %collective-permute-start.12 = (bf16[72,256]{1,0:T(8,128)(2,1)S(1)}, bf16[72,256]{1,0:T(8,128)(2,1)S(1)}, u32[]{:S(2)}, u32[]{:S(2)}) collective-permute-start(bf16[72,256]{1,0:T(8,128)(2,1)S(1)} %get-tuple-element.63.refs_0_), channel_id=1, source_target_pairs={{0,12},{4,8},{8,4},{12,0},{1,13},{5,9},{9,5},{13,1},{2,14},{6,10},... | collective-permute-start | bytes 110600 | tf_op jit(solution)/shard_map/ppermute | solution.py:369
  36.0 4.1 %collective-permute-start.11 = (bf16[72,256]{1,0:T(8,128)(2,1)S(1)}, bf16[72,256]{1,0:T(8,128)(2,1)S(1)}, u32[]{:S(2)}, u32[]{:S(2)}) collective-permute-start(bf16[72,256]{1,0:T(8,128)(2,1)S(1)} %get-tuple-element.63.refs_0_), channel_id=1, source_target_pairs={{0,4},{4,0},{8,12},{12,8},{1,5},{5,1},{9,13},{13,9},{2,6},{6,2},{1... | collective-permute-start | bytes 110600 | tf_op jit(solution)/shard_map/ppermute | solution.py:369
  41.2 1.8 %collective-permute-start.18 = (bf16[576,256]{1,0:T(8,128)(2,1)S(1)}, bf16[576,256]{1,0:T(8,128)(2,1)S(1)}, u32[]{:S(2)}, u32[]{:S(2)}) collective-permute-start(bf16[576,256]{1,0:T(8,128)(2,1)S(1)} %shard_map.77.mine_ref), channel_id=1, source_target_pairs={{0,1},{1,0},{2,3},{3,2},{4,5},{5,4},{6,7},{7,6},{8,9},{9,8},{10,11... | collective-permute-start | bytes 884744 | tf_op jit(solution)/shard_map/ppermute | solution.py:341
  41.2 4.0 %collective-permute-start.16 = (bf16[72,256]{1,0:T(8,128)(2,1)S(1)}, bf16[72,256]{1,0:T(8,128)(2,1)S(1)}, u32[]{:S(2)}, u32[]{:S(2)}) collective-permute-start(bf16[72,256]{1,0:T(8,128)(2,1)S(1)} %get-tuple-element.70.refs_0_.a_ref), channel_id=1, source_target_pairs={{0,2},{2,0},{1,3},{3,1},{4,6},{6,4},{5,7},{7,5},{8,10},{10,8},{9,1... | collective-permute-start | bytes 110600 | tf_op jit(solution)/shard_map/ppermute | solution.py:369
  42.2 3.9 %collective-permute-start.14 = (bf16[64,256]{1,0:T(8,128)(2,1)S(1)}, bf16[64,256]{1,0:T(8,128)(2,1)S(1)}, u32[]{:S(2)}, u32[]{:S(2)}) collective-permute-start(bf16[64,256]{1,0:T(8,128)(2,1)S(1)} %get-tuple-element.66), channel_id=1, source_target_pairs={{0,4},{4,0},{8,12},{12,8},{1,5},{5,1},{9,13},{13,9},{2,6},{6,2},{1... | collective-permute-start | bytes 98312 | tf_op jit(solution)/shard_map/ppermute | solution.py:341
  42.9 3.2 %collective-permute-start.15 = (bf16[64,256]{1,0:T(8,128)(2,1)S(1)}, bf16[64,256]{1,0:T(8,128)(2,1)S(1)}, u32[]{:S(2)}, u32[]{:S(2)}) collective-permute-start(bf16[64,256]{1,0:T(8,128)(2,1)S(1)} %get-tuple-element.67), channel_id=1, source_target_pairs={{0,1},{1,0},{4,8},{5,9},{8,4},{9,5},{12,13},{13,12},{2,3},{3,2},{6... | collective-permute-start | bytes 98312 | tf_op jit(solution)/shard_map/ppermute | solution.py:355
  45.3 2.0 %collective-permute-start.19 = (bf16[72,256]{1,0:T(8,128)(2,1)S(1)}, bf16[72,256]{1,0:T(8,128)(2,1)S(1)}, u32[]{:S(2)}, u32[]{:S(2)}) collective-permute-start(bf16[72,256]{1,0:T(8,128)(2,1)S(1)} %shard_map.79.mine_ref), channel_id=1, source_target_pairs={{0,1},{1,0},{2,3},{3,2},{4,5},{5,4},{6,7},{7,6},{8,9},{9,8},{10,11... | collective-permute-start | bytes 110600 | tf_op jit(solution)/shard_map/ppermute | solution.py:341

commit v13 on v12

--- a/solution.py
+++ b/solution.py
@@ -252,6 +252,12 @@
     one_ref[...] = total[half:]
 
 
+def add_joined(a_ref, b_ref, c_ref, d_ref, _, __, out_ref):
+    half = a_ref.shape[0]
+    out_ref[:half] = (a_ref[...].astype(F32) + b_ref[...].astype(F32)).astype(BF16)
+    out_ref[half:] = (c_ref[...].astype(F32) + d_ref[...].astype(F32)).astype(BF16)
+
+
 def sum_rows(*refs):
     *refs, a_ref, b_ref, out_ref, passed_a_ref, passed_b_ref = refs
     terms = dict(zip(row_order(len(refs), near_first=True), (ref[...].astype(F32) for ref in refs)))
@@ -312,29 +318,28 @@
     out_ref[...] = jnp.swapaxes(jnp.stack(rows, 0), 0, 1).astype(BF16)
 
 
-def finish_two(mine_ref, other_ref, two_hbm, done_ref, two_ref, sems, *, scale):
-    pair, half = lax.axis_index("pair"), mine_ref.shape[0]
-    done_ref[...] = jnp.zeros(done_ref.shape, F32)
+def finish(mine_ref, other_ref, _, one_hbm, two_hbm, one_ref, two_ref, flat_ref, sems, *, scales):
+    pair, half = lax.axis_index("pair"), mine_ref.shape[0] - HALF_ONE
+    halves = ((mine_ref, pair), (other_ref, 1 - pair))
     copies = []
-    for n, (ref, place) in enumerate(((mine_ref, pair), (other_ref, 1 - pair))):
+    for n, (ref, place) in enumerate(halves):
         rows = pl.ds(pl.multiple_of(place * half, 16), half)
-        two_ref[n] = ref[...].astype(F32) * scale
+        two_ref[n] = ref[:half].astype(F32) * scales[1]
         copies.append(pltpu.make_async_copy(two_ref.at[n], two_hbm.at[rows], sems.at[n]))
         copies[-1].start()
+    for ref, place in halves:
+        rows = pl.ds(pl.multiple_of(place * HALF_ONE, 8), HALF_ONE)
+        flat_ref[rows] = ref[half:].astype(F32) * scales[0]
+    one_ref[0, :96] = flat_ref[:96, :64]
+    one_ref[1, :96] = flat_ref[:96, 64:128]
+    one_ref[0, 96:] = flat_ref[:96, 128:192]
+    one_ref[1, 96:] = flat_ref[:96, 192:]
+    for q in range(4):
+        one_ref[2, 48 * q : 48 * q + 48] = flat_ref[96:, 64 * q : 64 * q + 64]
+    copies.append(pltpu.make_async_copy(one_ref, one_hbm, sems.at[2]))
+    copies[-1].start()
     for copy in copies:
         copy.wait()
-
-
-def finish_one(mine_ref, other_ref, _, out_ref, flat_ref, *, scale):
-    pair = lax.axis_index("pair")
-    for ref, place in ((mine_ref, pair), (other_ref, 1 - pair)):
-        flat_ref[pl.ds(pl.multiple_of(place * HALF_ONE, 8), HALF_ONE)] = ref[...].astype(F32) * scale
-    out_ref[0, :96] = flat_ref[:96, :64]
-    out_ref[1, :96] = flat_ref[:96, 64:128]
-    out_ref[0, 96:] = flat_ref[:96, 128:192]
-    out_ref[1, 96:] = flat_ref[:96, 192:]
-    for q in range(4):
-        out_ref[2, 48 * q : 48 * q + 48] = flat_ref[96:, 64 * q : 64 * q + 64]
 
 
 def even_swap(values, axis, count):
@@ -489,29 +494,36 @@
     one, up_a, up_b = whole_call(
         sum_rows, [shaped(a.shape) for a in (one, up_a, up_b)], ones + [up_a, up_b], 0
     )
+    up_a, up_b = even_swap(up_a, "row", bands), odd_row_swap(up_b)
     input_grad, done = whole_call(
         functools.partial(layer_one_back, bands=bands),
         [shaped(features_in.shape), shaped((8, 128), F32)],
-        [g, even_swap(up_a, "row", bands), odd_row_swap(up_b), back_one],
+        [g, up_a, up_b, back_one],
         2 * band_rows * 192 * 192 * 256,
     )
-    mine_two = added(two, two_more, one)
-    grad_two, wrote = whole_call(
-        functools.partial(finish_two, scale=1.0 / math.sqrt(pooled_rows * total)),
-        [shaped((2 * half, 256), F32), shaped((8, 128), F32)],
-        [mine_two, even_swap(mine_two, "pair", 2)],
-        10**8,
-        scratch=[pltpu.VMEM((2, half, 256), F32), pltpu.SemaphoreType.DMA((2,))],
-        out_spaces=[pl.ANY, pltpu.VMEM],
-    )
-    mine_one = added(*sum_but_last(one, "col", columns), wrote)
-    (grad_one,) = whole_call(
-        functools.partial(finish_one, scale=1.0 / math.sqrt(height * width)),
-        [shaped((3, 3 * channels, channels), F32)],
-        [mine_one, even_swap(mine_one, "pair", 2), done],
+    one, one_more = sum_but_last(one, "col", columns)
+    (mine,) = whole_call(
+        add_joined,
+        [shaped((half + HALF_ONE, 256))],
+        [two, two_more, one, one_more, up_a, up_b],
+        0,
+        after=2,
+    )
+    grad_one, grad_two = whole_call(
+        functools.partial(
+            finish, scales=(1.0 / math.sqrt(height * width), 1.0 / math.sqrt(pooled_rows * total))
+        ),
+        [shaped((3, 3 * channels, channels), F32), shaped((2 * half, 256), F32)],
+        [mine, even_swap(mine, "pair", 2), done],
         1,
-        scratch=[pltpu.VMEM((144, 256), F32)],
+        scratch=[
+            pltpu.VMEM((3, 3 * channels, channels), F32),
+            pltpu.VMEM((2, half, 256), F32),
+            pltpu.VMEM((144, 256), F32),
+            pltpu.SemaphoreType.DMA((3,)),
+        ],
         after=1,
+        out_spaces=[pl.ANY] * 2,
     )
     grad_two = jnp.transpose(grad_two.reshape(3, 3, filters, 4 * channels), (2, 0, 1, 3))
     grad_one = jnp.transpose(grad_one.reshape(3, 3, channels, channels), (2, 0, 1, 3))

time: 48.3 us -> 48.5 us (level)
  waiting for transfers between devices: 16.8 us -> 17.9 us
  Pallas kernels: 7.05 us -> 6.37 us
    ppermute x6 -> x5, waiting for transfers between devices: 3.12 us -> 6.43 us  [even_swap(): return lax.ppermute(values, axis, [(n, n ^ 1) for n in range(count)])]
    ppermute x11, waiting for transfers between devices: 12.5 us -> 10.3 us  [xor_swap(): return lax.ppermute(values, axis, [(n, n ^ k) for n in range(count)])]
    pallas_call x14 -> x12, Pallas kernels: 7.05 us -> 6.37 us  [whole_call(): pl.pallas_call(body, out_shape=outs, in_specs=specs, out_specs=[pl.BlockS...]
    ppermute x6 -> x5, starting transfers between devices: 5.13 us -> 4.64 us  [even_swap(): return lax.ppermute(values, axis, [(n, n ^ 1) for n in range(count)])]
  transfers between devices with their start and end apart: 20 -> 19, of which waited for: 15 -> 14; matrix products, arithmetic and copies ran while one was open for 2% -> 2% of each run, Pallas kernels for 7% -> 4%
where the time goes in v13:
time: 48.5 us; the launch traced here: 48.3 us
  starting transfers between devices  20.4 us (42%)
  waiting for transfers between devices  17.9 us (37%)
  Pallas kernels  6.37 us (13%)
  local copies, waits for them, and re-layouts  2.77 us (6%)
  between operations  0.79 us (2%)
    ppermute x11, starting transfers between devices, xor_swap(): return lax.ppermute(values, axis, [(n, n ^ k) for n in range(count)])  13.7 us
    ppermute x11, waiting for transfers between devices, xor_swap(): return lax.ppermute(values, axis, [(n, n ^ k) for n in range(count)])  10.3 us
    ppermute x5, waiting for transfers between devices, even_swap(): return lax.ppermute(values, axis, [(n, n ^ 1) for n in range(count)])  6.43 us
    pallas_call x12, Pallas kernels, whole_call(): pl.pallas_call(body, out_shape=outs, in_specs=specs, out_specs=[pl.BlockS...  6.37 us
    ppermute x5, starting transfers between devices, even_swap(): return lax.ppermute(values, axis, [(n, n ^ 1) for n in range(count)])  4.64 us
    unnamed x6, local copies, waits for them, and re-layouts  2.75 us
    ppermute x1, starting transfers between devices, odd_strip_swap(): return lax.ppermute(values, ('grp',) + COLS, steps)  1.56 us
    ppermute x1, waiting for transfers between devices, odd_strip_swap(): return lax.ppermute(values, ('grp',) + COLS, steps)  1.18 us
  transfers between devices with their start and end apart: 19, of which 14 were waited for; matrix products, arithmetic and copies ran while one was open for 2% of the time, Pallas kernels for 4%

profile of v13, /device:TPU:0, one launch (start us, length us, event | category | flops | bytes accessed | tf_op | source)
XLA Modules:
  0.0 48.3 jit_solution(4004627182041902604)
XLA Ops:
  0.7 1.0 %copy.19 = bf16[64,8,128]{2,0,1:T(8,128)(2,1)S(1)} copy(bf16[64,8,128]{2,1,0:T(8,128)(2,1)} %param.4) | data formatting | bytes 262144 | tf_op args[0]
  2.2 4.1 %collective-permute-start = (bf16[64,128]{1,0:T(8,128)(2,1)S(1)}, bf16[64,128]{1,0:T(8,128)(2,1)S(1)}, u32[]{:S(2)}, u32[]{:S(2)}) collective-permute-start(bf16[64,128]{1,0:T(8,128)(2,1)S(1)} %get-tuple-element.76), channel_id=1, source_target_pairs={{0,4},{4,0},{8,12},{12,8},{1,5},{5,1},{9,13},{13,9},{2,6},{6,2},{1... | collective-permute-start | bytes 49160 | tf_op jit(solution)/shard_map/ppermute | solution.py:346
  8.1 1.6 %collective-permute-start.2 = (bf16[144,128]{1,0:T(8,128)(2,1)S(1)}, bf16[144,128]{1,0:T(8,128)(2,1)S(1)}, u32[]{:S(2)}, u32[]{:S(2)}) collective-permute-start(bf16[144,128]{1,0:T(8,128)(2,1)S(1)} %get-tuple-element.41), channel_id=1, source_target_pairs={{0,16},{1,2},{2,1},{3,19},{16,0},{17,18},{18,17},{19,3},{4,20},{5,... | collective-permute-start | bytes 110600 | tf_op jit(solution)/shard_map/ppermute | solution.py:370
  9.8 0.9 %copy-done.1 = bf16[64,3,3,64]{3,0,2,1:T(8,128)(2,1)S(1)} copy-done((bf16[64,3,3,64]{3,0,2,1:T(8,128)(2,1)S(1)}, bf16[64,3,3,64]{3,0,2,1:T(8,128)(2,1)}, u32[]{:S(2)}) %copy-start.1) | copy-done | bytes 73752
  10.9 1.2 %collective-permute-done.2.b_ref = bf16[144,128]{1,0:T(8,128)(2,1)S(1)} collective-permute-done((bf16[144,128]{1,0:T(8,128)(2,1)S(1)}, bf16[144,128]{1,0:T(8,128)(2,1)S(1)}, u32[]{:S(2)}, u32[]{:S(2)}) %collective-permute-start.2) | collective-permute-done | bytes 36896 | tf_op jit(solution)/shard_map/ppermute | solution.py:370
  13.0 2.0 %collective-permute-start.6 = (bf16[2,40,256]{2,1,0:T(8,128)(2,1)S(1)}, bf16[2,40,256]{2,1,0:T(8,128)(2,1)S(1)}, u32[]{:S(2)}, u32[]{:S(2)}) collective-permute-start(bf16[2,40,256]{2,1,0:T(8,128)(2,1)S(1)} %get-tuple-element.48.refs_0_), channel_id=1, source_target_pairs={{0,8},{4,12},{8,0},{12,4},{1,9},{5,13},{9,1},{13,5},{2,10},{6,14},... | collective-permute-start | bytes 122888 | tf_op jit(solution)/shard_map/ppermute | solution.py:374
  15.0 2.5 %collective-permute-start.5 = (bf16[2,40,256]{2,1,0:T(8,128)(2,1)S(1)}, bf16[2,40,256]{2,1,0:T(8,128)(2,1)S(1)}, u32[]{:S(2)}, u32[]{:S(2)}) collective-permute-start(bf16[2,40,256]{2,1,0:T(8,128)(2,1)S(1)} %get-tuple-element.48.refs_0_), channel_id=1, source_target_pairs={{0,12},{4,8},{8,4},{12,0},{1,13},{5,9},{9,5},{13,1},{2,14},{6,10},... | collective-permute-start | bytes 122888 | tf_op jit(solution)/shard_map/ppermute | solution.py:374
  17.6 1.4 %collective-permute-done.6.refs_3_ = bf16[2,40,256]{2,1,0:T(8,128)(2,1)S(1)} collective-permute-done((bf16[2,40,256]{2,1,0:T(8,128)(2,1)S(1)}, bf16[2,40,256]{2,1,0:T(8,128)(2,1)S(1)}, u32[]{:S(2)}, u32[]{:S(2)}) %collective-permute-start.6) | collective-permute-done | bytes 40992 | tf_op jit(solution)/shard_map/ppermute | solution.py:374
  19.0 1.8 %collective-permute-done.5.refs_2_ = bf16[2,40,256]{2,1,0:T(8,128)(2,1)S(1)} collective-permute-done((bf16[2,40,256]{2,1,0:T(8,128)(2,1)S(1)}, bf16[2,40,256]{2,1,0:T(8,128)(2,1)S(1)}, u32[]{:S(2)}, u32[]{:S(2)}) %collective-permute-start.5) | collective-permute-done | bytes 40992 | tf_op jit(solution)/shard_map/ppermute | solution.py:374
  21.5 1.0 %shard_map.71 = (bf16[72,256]{1,0:T(8,128)(2,1)S(1)}, bf16[72,256]{1,0:T(8,128)(2,1)S(1)}, bf16[72,256]{1,0:T(8,128)(2,1)S(1)}, bf16[72,256]{1,0:T(8,128)(2,1)S(...) custom-call(bf16[8,48,128]{2,1,0:T(8,128)(2,1)S(1)} %fusion.6.og_ref, ...), custom_call_target="tpu_custom_call" | custom-call | flops 452984832 | bytes 1368064 | tf_op jit(solution)/shard_map/pallas_call | solution.py:30
  22.9 2.5 %collective-permute-start.8 = (bf16[72,256]{1,0:T(8,128)(2,1)S(1)}, bf16[72,256]{1,0:T(8,128)(2,1)S(1)}, u32[]{:S(2)}, u32[]{:S(2)}) collective-permute-start(bf16[72,256]{1,0:T(8,128)(2,1)S(1)} %get-tuple-element.51), channel_id=1, source_target_pairs={{0,12},{4,8},{8,4},{12,0},{1,13},{5,9},{9,5},{13,1},{2,14},{6,10},... | collective-permute-start | bytes 110600 | tf_op jit(solution)/shard_map/ppermute | solution.py:374
  26.6 1.0 %collective-permute-done.7.refs_1_ = bf16[72,256]{1,0:T(8,128)(2,1)S(1)} collective-permute-done((bf16[72,256]{1,0:T(8,128)(2,1)S(1)}, bf16[72,256]{1,0:T(8,128)(2,1)S(1)}, u32[]{:S(2)}, u32[]{:S(2)}) %collective-permute-start.7) | collective-permute-done | bytes 36896 | tf_op jit(solution)/shard_map/ppermute | solution.py:374
  27.7 1.0 %collective-permute-done.8.refs_2_ = bf16[72,256]{1,0:T(8,128)(2,1)S(1)} collective-permute-done((bf16[72,256]{1,0:T(8,128)(2,1)S(1)}, bf16[72,256]{1,0:T(8,128)(2,1)S(1)}, u32[]{:S(2)}, u32[]{:S(2)}) %collective-permute-start.8) | collective-permute-done | bytes 36896 | tf_op jit(solution)/shard_map/ppermute | solution.py:374
  29.3 0.9 %shard_map.73 = (bf16[8,64,256]{2,1,0:T(8,128)(2,1)S(1)}, bf16[64,256]{1,0:T(8,128)(2,1)S(1)}, bf16[64,256]{1,0:T(8,128)(2,1)S(1)}, bf16[648,256]{1,0:T(8,128)(2,1)S(1)}, bf16[648,256]{1,0:T(8,128)(2,1)S(1)}) custom-call(bf16[72,256]{1,0:T(8,128)(2,1)S(1)} %get-tuple-element.49.refs_0_, bf16[72,256]{1,0:T(8,128)(2,1)S(1)} %collective-permute-done.7.refs_1_, ...), custom_call_target="tpu_custom_call" | custom-call | flops 150994944 | bytes 2498560 | tf_op jit(solution)/shard_map/pallas_call | solution.py:30
  30.3 1.6 %collective-permute-done.10.b_ref = bf16[648,256]{1,0:T(8,128)(2,1)S(1)} collective-permute-done((bf16[648,256]{1,0:T(8,128)(2,1)S(1)}, bf16[648,256]{1,0:T(8,128)(2,1)S(1)}, u32[]{:S(2)}, u32[]{:S(2)}) %collective-permute-start.10) | collective-permute-done | bytes 331808 | tf_op jit(solution)/shard_map/ppermute | solution.py:346
  32.0 1.0 %collective-permute-start.16 = (bf16[576,256]{1,0:T(8,128)(2,1)S(1)}, bf16[576,256]{1,0:T(8,128)(2,1)S(1)}, u32[]{:S(2)}, u32[]{:S(2)}) collective-permute-start(bf16[576,256]{1,0:T(8,128)(2,1)S(1)} %get-tuple-element.70.a_ref), channel_id=1, source_target_pairs={{0,2},{2,0},{1,3},{3,1},{4,6},{6,4},{5,7},{7,5},{8,10},{10,8},{9,1... | collective-permute-start | bytes 884744 | tf_op jit(solution)/shard_map/ppermute | solution.py:374
  33.0 1.0 %collective-permute-start.13 = (bf16[72,256]{1,0:T(8,128)(2,1)S(1)}, bf16[72,256]{1,0:T(8,128)(2,1)S(1)}, u32[]{:S(2)}, u32[]{:S(2)}) collective-permute-start(bf16[72,256]{1,0:T(8,128)(2,1)S(1)} %get-tuple-element.63.refs_0_), channel_id=1, source_target_pairs={{0,8},{4,12},{8,0},{12,4},{1,9},{5,13},{9,1},{13,5},{2,10},{6,14},... | collective-permute-start | bytes 110600 | tf_op jit(solution)/shard_map/ppermute | solution.py:374
  34.0 2.0 %collective-permute-start.12 = (bf16[72,256]{1,0:T(8,128)(2,1)S(1)}, bf16[72,256]{1,0:T(8,128)(2,1)S(1)}, u32[]{:S(2)}, u32[]{:S(2)}) collective-permute-start(bf16[72,256]{1,0:T(8,128)(2,1)S(1)} %get-tuple-element.63.refs_0_), channel_id=1, source_target_pairs={{0,12},{4,8},{8,4},{12,0},{1,13},{5,9},{9,5},{13,1},{2,14},{6,10},... | collective-permute-start | bytes 110600 | tf_op jit(solution)/shard_map/ppermute | solution.py:374
  36.4 2.3 %collective-permute-done.13.refs_3_ = bf16[72,256]{1,0:T(8,128)(2,1)S(1)} collective-permute-done((bf16[72,256]{1,0:T(8,128)(2,1)S(1)}, bf16[72,256]{1,0:T(8,128)(2,1)S(1)}, u32[]{:S(2)}, u32[]{:S(2)}) %collective-permute-start.13) | collective-permute-done | bytes 36896 | tf_op jit(solution)/shard_map/ppermute | solution.py:374
  38.8 1.0 %collective-permute-done.12.refs_2_ = bf16[72,256]{1,0:T(8,128)(2,1)S(1)} collective-permute-done((bf16[72,256]{1,0:T(8,128)(2,1)S(1)}, bf16[72,256]{1,0:T(8,128)(2,1)S(1)}, u32[]{:S(2)}, u32[]{:S(2)}) %collective-permute-start.12) | collective-permute-done | bytes 36896 | tf_op jit(solution)/shard_map/ppermute | solution.py:374
  40.2 1.2 %collective-permute-start.17 = (bf16[72,256]{1,0:T(8,128)(2,1)S(1)}, bf16[72,256]{1,0:T(8,128)(2,1)S(1)}, u32[]{:S(2)}, u32[]{:S(2)}) collective-permute-start(bf16[72,256]{1,0:T(8,128)(2,1)S(1)} %get-tuple-element.71.c_ref), channel_id=1, source_target_pairs={{0,2},{2,0},{1,3},{3,1},{4,6},{6,4},{5,7},{7,5},{8,10},{10,8},{9,1... | collective-permute-start | bytes 110600 | tf_op jit(solution)/shard_map/ppermute | solution.py:374
  41.6 3.6 %collective-permute-done.14.a_ref._ = bf16[64,256]{1,0:T(8,128)(2,1)S(1)} collective-permute-done((bf16[64,256]{1,0:T(8,128)(2,1)S(1)}, bf16[64,256]{1,0:T(8,128)(2,1)S(1)}, u32[]{:S(2)}, u32[]{:S(2)}) %collective-permute-start.14) | collective-permute-done | bytes 32800 | tf_op jit(solution)/shard_map/ppermute | solution.py:346
  45.4 1.2 %shard_map.76 = (bf16[64,8,128]{2,1,0:T(8,128)(2,1)}, f32[8,128]{1,0:T(8,128)S(1)}) custom-call(bf16[8,64,256]{2,1,0:T(8,128)(2,1)S(1)} %get-tuple-element.60.g_ref, bf16[64,256]{1,0:T(8,128)(2,1)S(1)} %collective-permute-done.14.a_ref._, bf16[64,256]{1,0:T(8,128)(2,1)S(1)} %collective-permute-done.15.b_ref.__, bf16[192,192]{1,0:T(8,128)(2,1)S(1)} %get-tuple-element.68.w_ref), custom_call_target="tpu_custom_call" | custom-call | flops 150994944 | bytes 536576 | tf_op jit(solution)/shard_map/pallas_call | solution.py:30
  47.1 1.2 %shard_map.78 = (f32[3,192,64]{2,1,0:T(8,128)}, f32[1152,256]{1,0:T(8,128)}) custom-call(bf16[648,256]{1,0:T(8,128)(2,1)S(1)} %shard_map.77.mine_ref, bf16[648,256]{1,0:T(8,128)(2,1)S(1)} %collective-permute-done.18.other_ref, f32[8,128]{1,0:T(8,128)S(1)} %get-tuple-element.72._), custom_call_target="tpu_custom_call" | custom-call | flops 1 | bytes 1994752 | tf_op jit(solution)/shard_map/pallas_call | solution.py:30
  (39 shorter events, 8.4 us)
Async XLA Ops:
  0.6 20.8 %copy-start = (bf16[128,3,3,256]{3,0,2,1:T(8,128)(2,1)S(1)}, bf16[128,3,3,256]{3,0,2,1:T(8,128)(2,1)}, u32[]{:S(2)}) copy-start(bf16[128,3,3,256]{3,0,2,1:T(8,128)(2,1)} %param.6) | copy-start | bytes 1769476
  1.7 5.7 %collective-permute-start.1 = (bf16[64,128]{1,0:T(8,128)(2,1)S(1)}, bf16[64,128]{1,0:T(8,128)(2,1)S(1)}, u32[]{:S(2)}, u32[]{:S(2)}) collective-permute-start(bf16[64,128]{1,0:T(8,128)(2,1)S(1)} %get-tuple-element.75), channel_id=1, source_target_pairs={{0,1},{1,0},{4,8},{5,9},{8,4},{9,5},{12,13},{13,12},{2,3},{3,2},{6... | collective-permute-start | bytes 49160 | tf_op jit(solution)/shard_map/ppermute | solution.py:360
  2.2 5.9 %collective-permute-start = (bf16[64,128]{1,0:T(8,128)(2,1)S(1)}, bf16[64,128]{1,0:T(8,128)(2,1)S(1)}, u32[]{:S(2)}, u32[]{:S(2)}) collective-permute-start(bf16[64,128]{1,0:T(8,128)(2,1)S(1)} %get-tuple-element.76), channel_id=1, source_target_pairs={{0,4},{4,0},{8,12},{12,8},{1,5},{5,1},{9,13},{13,9},{2,6},{6,2},{1... | collective-permute-start | bytes 49160 | tf_op jit(solution)/shard_map/ppermute | solution.py:346
  8.1 4.0 %collective-permute-start.2 = (bf16[144,128]{1,0:T(8,128)(2,1)S(1)}, bf16[144,128]{1,0:T(8,128)(2,1)S(1)}, u32[]{:S(2)}, u32[]{:S(2)}) collective-permute-start(bf16[144,128]{1,0:T(8,128)(2,1)S(1)} %get-tuple-element.41), channel_id=1, source_target_pairs={{0,16},{1,2},{2,1},{3,19},{16,0},{17,18},{18,17},{19,3},{4,20},{5,... | collective-permute-start | bytes 110600 | tf_op jit(solution)/shard_map/ppermute | solution.py:370
  9.7 2.4 %collective-permute-start.3 = (bf16[144,128]{1,0:T(8,128)(2,1)S(1)}, bf16[144,128]{1,0:T(8,128)(2,1)S(1)}, u32[]{:S(2)}, u32[]{:S(2)}) collective-permute-start(bf16[144,128]{1,0:T(8,128)(2,1)S(1)} %get-tuple-element.42), channel_id=1, source_target_pairs={{0,1},{1,0},{2,3},{3,2},{4,5},{5,4},{6,7},{7,6},{8,9},{9,8},{10,11... | collective-permute-start | bytes 110600 | tf_op jit(solution)/shard_map/ppermute | solution.py:346
  9.8 0.9 %copy-start.1 = (bf16[64,3,3,64]{3,0,2,1:T(8,128)(2,1)S(1)}, bf16[64,3,3,64]{3,0,2,1:T(8,128)(2,1)}, u32[]{:S(2)}) copy-start(bf16[64,3,3,64]{3,0,2,1:T(8,128)(2,1)} %param.5) | copy-start | bytes 221188
  13.0 6.0 %collective-permute-start.6 = (bf16[2,40,256]{2,1,0:T(8,128)(2,1)S(1)}, bf16[2,40,256]{2,1,0:T(8,128)(2,1)S(1)}, u32[]{:S(2)}, u32[]{:S(2)}) collective-permute-start(bf16[2,40,256]{2,1,0:T(8,128)(2,1)S(1)} %get-tuple-element.48.refs_0_), channel_id=1, source_target_pairs={{0,8},{4,12},{8,0},{12,4},{1,9},{5,13},{9,1},{13,5},{2,10},{6,14},... | collective-permute-start | bytes 122888 | tf_op jit(solution)/shard_map/ppermute | solution.py:374
  15.0 5.8 %collective-permute-start.5 = (bf16[2,40,256]{2,1,0:T(8,128)(2,1)S(1)}, bf16[2,40,256]{2,1,0:T(8,128)(2,1)S(1)}, u32[]{:S(2)}, u32[]{:S(2)}) collective-permute-start(bf16[2,40,256]{2,1,0:T(8,128)(2,1)S(1)} %get-tuple-element.48.refs_0_), channel_id=1, source_target_pairs={{0,12},{4,8},{8,4},{12,0},{1,13},{5,9},{9,5},{13,1},{2,14},{6,10},... | collective-permute-start | bytes 122888 | tf_op jit(solution)/shard_map/ppermute | solution.py:374
  17.5 4.0 %collective-permute-start.4 = (bf16[2,40,256]{2,1,0:T(8,128)(2,1)S(1)}, bf16[2,40,256]{2,1,0:T(8,128)(2,1)S(1)}, u32[]{:S(2)}, u32[]{:S(2)}) collective-permute-start(bf16[2,40,256]{2,1,0:T(8,128)(2,1)S(1)} %get-tuple-element.48.refs_0_), channel_id=1, source_target_pairs={{0,4},{4,0},{8,12},{12,8},{1,5},{5,1},{9,13},{13,9},{2,6},{6,2},{1... | collective-permute-start | bytes 122888 | tf_op jit(solution)/shard_map/ppermute | solution.py:374
  22.5 5.2 %collective-permute-start.7 = (bf16[72,256]{1,0:T(8,128)(2,1)S(1)}, bf16[72,256]{1,0:T(8,128)(2,1)S(1)}, u32[]{:S(2)}, u32[]{:S(2)}) collective-permute-start(bf16[72,256]{1,0:T(8,128)(2,1)S(1)} %get-tuple-element.50), channel_id=1, source_target_pairs={{0,8},{4,12},{8,0},{12,4},{1,9},{5,13},{9,1},{13,5},{2,10},{6,14},... | collective-permute-start | bytes 110600 | tf_op jit(solution)/shard_map/ppermute | solution.py:374
  22.9 5.8 %collective-permute-start.8 = (bf16[72,256]{1,0:T(8,128)(2,1)S(1)}, bf16[72,256]{1,0:T(8,128)(2,1)S(1)}, u32[]{:S(2)}, u32[]{:S(2)}) collective-permute-start(bf16[72,256]{1,0:T(8,128)(2,1)S(1)} %get-tuple-element.51), channel_id=1, source_target_pairs={{0,12},{4,8},{8,4},{12,0},{1,13},{5,9},{9,5},{13,1},{2,14},{6,10},... | collective-permute-start | bytes 110600 | tf_op jit(solution)/shard_map/ppermute | solution.py:374
  25.3 4.0 %collective-permute-start.9 = (bf16[72,256]{1,0:T(8,128)(2,1)S(1)}, bf16[72,256]{1,0:T(8,128)(2,1)S(1)}, u32[]{:S(2)}, u32[]{:S(2)}) collective-permute-start(bf16[72,256]{1,0:T(8,128)(2,1)S(1)} %get-tuple-element.52), channel_id=1, source_target_pairs={{0,4},{4,0},{8,12},{12,8},{1,5},{5,1},{9,13},{13,9},{2,6},{6,2},{1... | collective-permute-start | bytes 110600 | tf_op jit(solution)/shard_map/ppermute | solution.py:374
  30.2 1.7 %collective-permute-start.10 = (bf16[648,256]{1,0:T(8,128)(2,1)S(1)}, bf16[648,256]{1,0:T(8,128)(2,1)S(1)}, u32[]{:S(2)}, u32[]{:S(2)}) collective-permute-start(bf16[648,256]{1,0:T(8,128)(2,1)S(1)} %get-tuple-element.62), channel_id=1, source_target_pairs={{0,1},{1,0},{2,3},{3,2},{4,5},{5,4},{6,7},{7,6},{8,9},{9,8},{10,11... | collective-permute-start | bytes 995336 | tf_op jit(solution)/shard_map/ppermute | solution.py:346
  32.0 13.3 %collective-permute-start.16 = (bf16[576,256]{1,0:T(8,128)(2,1)S(1)}, bf16[576,256]{1,0:T(8,128)(2,1)S(1)}, u32[]{:S(2)}, u32[]{:S(2)}) collective-permute-start(bf16[576,256]{1,0:T(8,128)(2,1)S(1)} %get-tuple-element.70.a_ref), channel_id=1, source_target_pairs={{0,2},{2,0},{1,3},{3,1},{4,6},{6,4},{5,7},{7,5},{8,10},{10,8},{9,1... | collective-permute-start | bytes 884744 | tf_op jit(solution)/shard_map/ppermute | solution.py:374
  33.0 5.8 %collective-permute-start.13 = (bf16[72,256]{1,0:T(8,128)(2,1)S(1)}, bf16[72,256]{1,0:T(8,128)(2,1)S(1)}, u32[]{:S(2)}, u32[]{:S(2)}) collective-permute-start(bf16[72,256]{1,0:T(8,128)(2,1)S(1)} %get-tuple-element.63.refs_0_), channel_id=1, source_target_pairs={{0,8},{4,12},{8,0},{12,4},{1,9},{5,13},{9,1},{13,5},{2,10},{6,14},... | collective-permute-start | bytes 110600 | tf_op jit(solution)/shard_map/ppermute | solution.py:374
  34.0 5.8 %collective-permute-start.12 = (bf16[72,256]{1,0:T(8,128)(2,1)S(1)}, bf16[72,256]{1,0:T(8,128)(2,1)S(1)}, u32[]{:S(2)}, u32[]{:S(2)}) collective-permute-start(bf16[72,256]{1,0:T(8,128)(2,1)S(1)} %get-tuple-element.63.refs_0_), channel_id=1, source_target_pairs={{0,12},{4,8},{8,4},{12,0},{1,13},{5,9},{9,5},{13,1},{2,14},{6,10},... | collective-permute-start | bytes 110600 | tf_op jit(solution)/shard_map/ppermute | solution.py:374
  36.0 4.1 %collective-permute-start.11 = (bf16[72,256]{1,0:T(8,128)(2,1)S(1)}, bf16[72,256]{1,0:T(8,128)(2,1)S(1)}, u32[]{:S(2)}, u32[]{:S(2)}) collective-permute-start(bf16[72,256]{1,0:T(8,128)(2,1)S(1)} %get-tuple-element.63.refs_0_), channel_id=1, source_target_pairs={{0,4},{4,0},{8,12},{12,8},{1,5},{5,1},{9,13},{13,9},{2,6},{6,2},{1... | collective-permute-start | bytes 110600 | tf_op jit(solution)/shard_map/ppermute | solution.py:374
  40.2 5.1 %collective-permute-start.17 = (bf16[72,256]{1,0:T(8,128)(2,1)S(1)}, bf16[72,256]{1,0:T(8,128)(2,1)S(1)}, u32[]{:S(2)}, u32[]{:S(2)}) collective-permute-start(bf16[72,256]{1,0:T(8,128)(2,1)S(1)} %get-tuple-element.71.c_ref), channel_id=1, source_target_pairs={{0,2},{2,0},{1,3},{3,1},{4,6},{6,4},{5,7},{7,5},{8,10},{10,8},{9,1... | collective-permute-start | bytes 110600 | tf_op jit(solution)/shard_map/ppermute | solution.py:374
  41.3 3.9 %collective-permute-start.14 = (bf16[64,256]{1,0:T(8,128)(2,1)S(1)}, bf16[64,256]{1,0:T(8,128)(2,1)S(1)}, u32[]{:S(2)}, u32[]{:S(2)}) collective-permute-start(bf16[64,256]{1,0:T(8,128)(2,1)S(1)} %get-tuple-element.66), channel_id=1, source_target_pairs={{0,4},{4,0},{8,12},{12,8},{1,5},{5,1},{9,13},{13,9},{2,6},{6,2},{1... | collective-permute-start | bytes 98312 | tf_op jit(solution)/shard_map/ppermute | solution.py:346
  41.6 3.7 %collective-permute-start.15 = (bf16[64,256]{1,0:T(8,128)(2,1)S(1)}, bf16[64,256]{1,0:T(8,128)(2,1)S(1)}, u32[]{:S(2)}, u32[]{:S(2)}) collective-permute-start(bf16[64,256]{1,0:T(8,128)(2,1)S(1)} %get-tuple-element.67), channel_id=1, source_target_pairs={{0,1},{1,0},{4,8},{5,9},{8,4},{9,5},{12,13},{13,12},{2,3},{3,2},{6... | collective-permute-start | bytes 98312 | tf_op jit(solution)/shard_map/ppermute | solution.py:360
  45.4 1.7 %collective-permute-start.18 = (bf16[648,256]{1,0:T(8,128)(2,1)S(1)}, bf16[648,256]{1,0:T(8,128)(2,1)S(1)}, u32[]{:S(2)}, u32[]{:S(2)}) collective-permute-start(bf16[648,256]{1,0:T(8,128)(2,1)S(1)} %shard_map.77.mine_ref), channel_id=1, source_target_pairs={{0,1},{1,0},{2,3},{3,2},{4,5},{5,4},{6,7},{7,6},{8,9},{9,8},{10,11... | collective-permute-start | bytes 995336 | tf_op jit(solution)/shard_map/ppermute | solution.py:346

commit v14 on v13

--- a/solution.py
+++ b/solution.py
@@ -245,28 +245,29 @@
     refs[-1][...] = (a_ref[...].astype(F32) + b_ref[...].astype(F32)).astype(BF16)
 
 
-def add_halves(a_ref, b_ref, two_ref, one_ref):
-    half = two_ref.shape[0]
+def add_halves(a_ref, b_ref, border_ref, two_ref, one_ref, joined_ref):
+    half, border = two_ref.shape[0], border_ref.shape[0]
     total = (a_ref[...].astype(F32) + b_ref[...].astype(F32)).astype(BF16)
     two_ref[...] = total[:half]
     one_ref[...] = total[half:]
-
-
-def add_joined(a_ref, b_ref, c_ref, d_ref, _, __, out_ref):
+    joined_ref[:border] = border_ref[...]
+    joined_ref[border:] = total[half:]
+
+
+def add_joined(a_ref, b_ref, c_ref, d_ref, _, out_ref):
     half = a_ref.shape[0]
     out_ref[:half] = (a_ref[...].astype(F32) + b_ref[...].astype(F32)).astype(BF16)
     out_ref[half:] = (c_ref[...].astype(F32) + d_ref[...].astype(F32)).astype(BF16)
 
 
 def sum_rows(*refs):
-    *refs, a_ref, b_ref, out_ref, passed_a_ref, passed_b_ref = refs
-    terms = dict(zip(row_order(len(refs), near_first=True), (ref[...].astype(F32) for ref in refs)))
+    *refs, _, out_ref = refs
+    rows = out_ref.shape[0]
+    terms = dict(zip(row_order(len(refs), near_first=True), (ref[-rows:].astype(F32) for ref in refs)))
     terms = [terms[k] for k in range(len(refs))]
     while len(terms) > 1:
         terms = [a + b for a, b in zip(terms[::2], terms[1::2])]
     out_ref[...] = terms[0].astype(BF16)
-    passed_a_ref[...] = a_ref[...]
-    passed_b_ref[...] = b_ref[...]
 
 
 def grad_pre_one(*refs, bands):
@@ -308,7 +309,7 @@
 
 
 def layer_one_back(g_ref, a_ref, b_ref, w_ref, out_ref, done_ref, *, bands):
-    above, below = beside(a_ref, b_ref, lax.axis_index("row"), bands)
+    above, below = beside(a_ref.at[: b_ref.shape[0]], b_ref, lax.axis_index("row"), bands)
     done_ref[...] = jnp.zeros(done_ref.shape, F32)
     lines = [above] + [g_ref[h] for h in range(8)] + [below]
     rows = []
@@ -318,7 +319,7 @@
     out_ref[...] = jnp.swapaxes(jnp.stack(rows, 0), 0, 1).astype(BF16)
 
 
-def finish(mine_ref, other_ref, _, one_hbm, two_hbm, one_ref, two_ref, flat_ref, sems, *, scales):
+def finish(mine_ref, other_ref, one_hbm, two_hbm, one_ref, two_ref, flat_ref, sems, *, scales):
     pair, half = lax.axis_index("pair"), mine_ref.shape[0] - HALF_ONE
     halves = ((mine_ref, pair), (other_ref, 1 - pair))
     copies = []
@@ -482,39 +483,38 @@
         2 * 8 * 192 * 192 * 256,
         scratch=[pltpu.VMEM((144, 256), F32)],
     )
-    two, one = whole_call(
+    two, one, joined = whole_call(
         add_halves,
-        [shaped((half, 256)), shaped((HALF_ONE, 256))],
-        [keep, even_swap(send, "pair", 2)],
+        [shaped((half, 256)), shaped((HALF_ONE, 256)), shaped((channels + HALF_ONE, 256))],
+        [keep, even_swap(send, "pair", 2), up_a],
         0,
     )
     columns = lax.axis_size("col")
     two, two_more = sum_but_last(two, "col", columns)
-    ones = row_swaps([one] * bands, bands, near_first=True)
-    one, up_a, up_b = whole_call(
-        sum_rows, [shaped(a.shape) for a in (one, up_a, up_b)], ones + [up_a, up_b], 0
-    )
-    up_a, up_b = even_swap(up_a, "row", bands), odd_row_swap(up_b)
+    ones = row_swaps([one, joined] + [one] * (bands - 2), bands, near_first=True)
+    near = ones[row_order(bands, near_first=True).index(1)]
+    up_b = odd_row_swap(up_b)
+    (one,) = whole_call(sum_rows, [shaped(one.shape)], ones + [up_b], 0, after=1)
     input_grad, done = whole_call(
         functools.partial(layer_one_back, bands=bands),
         [shaped(features_in.shape), shaped((8, 128), F32)],
-        [g, up_a, up_b, back_one],
+        [g, near, up_b, back_one],
         2 * band_rows * 192 * 192 * 256,
     )
     one, one_more = sum_but_last(one, "col", columns)
     (mine,) = whole_call(
         add_joined,
         [shaped((half + HALF_ONE, 256))],
-        [two, two_more, one, one_more, up_a, up_b],
+        [two, two_more, one, one_more, done],
         0,
-        after=2,
+        after=1,
     )
     grad_one, grad_two = whole_call(
         functools.partial(
             finish, scales=(1.0 / math.sqrt(height * width), 1.0 / math.sqrt(pooled_rows * total))
         ),
         [shaped((3, 3 * channels, channels), F32), shaped((2 * half, 256), F32)],
-        [mine, even_swap(mine, "pair", 2), done],
+        [mine, even_swap(mine, "pair", 2)],
         1,
         scratch=[
             pltpu.VMEM((3, 3 * channels, channels), F32),
@@ -522,7 +522,6 @@
             pltpu.VMEM((144, 256), F32),
             pltpu.SemaphoreType.DMA((3,)),
         ],
-        after=1,
         out_spaces=[pl.ANY] * 2,
     )
     grad_two = jnp.transpose(grad_two.reshape(3, 3, filters, 4 * channels), (2, 0, 1, 3))

time: 48.5 us -> 48.3 us (level)
  waiting for transfers between devices: 17.9 us -> 17.1 us
  starting transfers between devices: 20.4 us -> 21 us
    ppermute x5 -> x4, waiting for transfers between devices: 6.43 us -> 3.96 us  [even_swap(): return lax.ppermute(values, axis, [(n, n ^ 1) for n in range(count)])]
    ppermute x2, waiting for transfers between devices: 0.01 us -> 1.21 us  [odd_row_swap(): return lax.ppermute(values, ('row', 'pair'), steps)]
    ppermute x11, starting transfers between devices: 13.7 us -> 14.5 us  [xor_swap(): return lax.ppermute(values, axis, [(n, n ^ k) for n in range(count)])]
    ppermute x11, waiting for transfers between devices: 10.3 us -> 10.8 us  [xor_swap(): return lax.ppermute(values, axis, [(n, n ^ k) for n in range(count)])]
    ppermute x5 -> x4, starting transfers between devices: 4.64 us -> 4.38 us  [even_swap(): return lax.ppermute(values, axis, [(n, n ^ 1) for n in range(count)])]
  transfers between devices with their start and end apart: 19 -> 18, of which waited for: 14 -> 14; matrix products, arithmetic and copies ran while one was open for 2% -> 2% of each run, Pallas kernels for 4% -> 4%
where the time goes in v14:
time: 48.3 us; the launch traced here: 48.1 us
  starting transfers between devices  21 us (43%)
  waiting for transfers between devices  17.1 us (35%)
  Pallas kernels  6.37 us (13%)
  local copies, waits for them, and re-layouts  2.77 us (6%)
  between operations  0.79 us (2%)
    ppermute x11, starting transfers between devices, xor_swap(): return lax.ppermute(values, axis, [(n, n ^ k) for n in range(count)])  14.5 us
    ppermute x11, waiting for transfers between devices, xor_swap(): return lax.ppermute(values, axis, [(n, n ^ k) for n in range(count)])  10.8 us
    pallas_call x12, Pallas kernels, whole_call(): pl.pallas_call(body, out_shape=outs, in_specs=specs, out_specs=[pl.BlockS...  6.37 us
    ppermute x4, starting transfers between devices, even_swap(): return lax.ppermute(values, axis, [(n, n ^ 1) for n in range(count)])  4.38 us
    ppermute x4, waiting for transfers between devices, even_swap(): return lax.ppermute(values, axis, [(n, n ^ 1) for n in range(count)])  3.96 us
    unnamed x6, local copies, waits for them, and re-layouts  2.75 us
    ppermute x1, starting transfers between devices, odd_strip_swap(): return lax.ppermute(values, ('grp',) + COLS, steps)  1.56 us
    ppermute x2, waiting for transfers between devices, odd_row_swap(): return lax.ppermute(values, ('row', 'pair'), steps)  1.21 us
  transfers between devices with their start and end apart: 18, of which 14 were waited for; matrix products, arithmetic and copies ran while one was open for 2% of the time, Pallas kernels for 4%

profile of v14, /device:TPU:0, one launch (start us, length us, event | category | flops | bytes accessed | tf_op | source)
XLA Modules:
  0.0 48.1 jit_solution(16439542430417686144)
XLA Ops:
  0.7 1.0 %copy.19 = bf16[64,8,128]{2,0,1:T(8,128)(2,1)S(1)} copy(bf16[64,8,128]{2,1,0:T(8,128)(2,1)} %param.4) | data formatting | bytes 262144 | tf_op args[0]
  2.2 4.1 %collective-permute-start = (bf16[64,128]{1,0:T(8,128)(2,1)S(1)}, bf16[64,128]{1,0:T(8,128)(2,1)S(1)}, u32[]{:S(2)}, u32[]{:S(2)}) collective-permute-start(bf16[64,128]{1,0:T(8,128)(2,1)S(1)} %get-tuple-element.72), channel_id=1, source_target_pairs={{0,4},{4,0},{8,12},{12,8},{1,5},{5,1},{9,13},{13,9},{2,6},{6,2},{1... | collective-permute-start | bytes 49160 | tf_op jit(solution)/shard_map/ppermute | solution.py:347
  8.1 1.6 %collective-permute-start.2 = (bf16[144,128]{1,0:T(8,128)(2,1)S(1)}, bf16[144,128]{1,0:T(8,128)(2,1)S(1)}, u32[]{:S(2)}, u32[]{:S(2)}) collective-permute-start(bf16[144,128]{1,0:T(8,128)(2,1)S(1)} %get-tuple-element.39), channel_id=1, source_target_pairs={{0,16},{1,2},{2,1},{3,19},{16,0},{17,18},{18,17},{19,3},{4,20},{5,... | collective-permute-start | bytes 110600 | tf_op jit(solution)/shard_map/ppermute | solution.py:371
  9.8 0.9 %copy-done.1 = bf16[64,3,3,64]{3,0,2,1:T(8,128)(2,1)S(1)} copy-done((bf16[64,3,3,64]{3,0,2,1:T(8,128)(2,1)S(1)}, bf16[64,3,3,64]{3,0,2,1:T(8,128)(2,1)}, u32[]{:S(2)}) %copy-start.1) | copy-done | bytes 73752
  10.9 1.2 %collective-permute-done.2.b_ref = bf16[144,128]{1,0:T(8,128)(2,1)S(1)} collective-permute-done((bf16[144,128]{1,0:T(8,128)(2,1)S(1)}, bf16[144,128]{1,0:T(8,128)(2,1)S(1)}, u32[]{:S(2)}, u32[]{:S(2)}) %collective-permute-start.2) | collective-permute-done | bytes 36896 | tf_op jit(solution)/shard_map/ppermute | solution.py:371
  13.0 2.0 %collective-permute-start.6 = (bf16[2,40,256]{2,1,0:T(8,128)(2,1)S(1)}, bf16[2,40,256]{2,1,0:T(8,128)(2,1)S(1)}, u32[]{:S(2)}, u32[]{:S(2)}) collective-permute-start(bf16[2,40,256]{2,1,0:T(8,128)(2,1)S(1)} %get-tuple-element.46.refs_0_), channel_id=1, source_target_pairs={{0,8},{4,12},{8,0},{12,4},{1,9},{5,13},{9,1},{13,5},{2,10},{6,14},... | collective-permute-start | bytes 122888 | tf_op jit(solution)/shard_map/ppermute | solution.py:375
  15.0 2.5 %collective-permute-start.5 = (bf16[2,40,256]{2,1,0:T(8,128)(2,1)S(1)}, bf16[2,40,256]{2,1,0:T(8,128)(2,1)S(1)}, u32[]{:S(2)}, u32[]{:S(2)}) collective-permute-start(bf16[2,40,256]{2,1,0:T(8,128)(2,1)S(1)} %get-tuple-element.46.refs_0_), channel_id=1, source_target_pairs={{0,12},{4,8},{8,4},{12,0},{1,13},{5,9},{9,5},{13,1},{2,14},{6,10},... | collective-permute-start | bytes 122888 | tf_op jit(solution)/shard_map/ppermute | solution.py:375
  17.6 1.4 %collective-permute-done.6.refs_3_ = bf16[2,40,256]{2,1,0:T(8,128)(2,1)S(1)} collective-permute-done((bf16[2,40,256]{2,1,0:T(8,128)(2,1)S(1)}, bf16[2,40,256]{2,1,0:T(8,128)(2,1)S(1)}, u32[]{:S(2)}, u32[]{:S(2)}) %collective-permute-start.6) | collective-permute-done | bytes 40992 | tf_op jit(solution)/shard_map/ppermute | solution.py:375
  19.0 1.8 %collective-permute-done.5.refs_2_ = bf16[2,40,256]{2,1,0:T(8,128)(2,1)S(1)} collective-permute-done((bf16[2,40,256]{2,1,0:T(8,128)(2,1)S(1)}, bf16[2,40,256]{2,1,0:T(8,128)(2,1)S(1)}, u32[]{:S(2)}, u32[]{:S(2)}) %collective-permute-start.5) | collective-permute-done | bytes 40992 | tf_op jit(solution)/shard_map/ppermute | solution.py:375
  21.5 1.0 %shard_map.71 = (bf16[72,256]{1,0:T(8,128)(2,1)S(1)}, bf16[72,256]{1,0:T(8,128)(2,1)S(1)}, bf16[72,256]{1,0:T(8,128)(2,1)S(1)}, bf16[72,256]{1,0:T(8,128)(2,1)S(...) custom-call(bf16[8,48,128]{2,1,0:T(8,128)(2,1)S(1)} %fusion.6.og_ref, ...), custom_call_target="tpu_custom_call" | custom-call | flops 452984832 | bytes 1368064 | tf_op jit(solution)/shard_map/pallas_call | solution.py:30
  22.9 2.5 %collective-permute-start.8 = (bf16[72,256]{1,0:T(8,128)(2,1)S(1)}, bf16[72,256]{1,0:T(8,128)(2,1)S(1)}, u32[]{:S(2)}, u32[]{:S(2)}) collective-permute-start(bf16[72,256]{1,0:T(8,128)(2,1)S(1)} %get-tuple-element.49), channel_id=1, source_target_pairs={{0,12},{4,8},{8,4},{12,0},{1,13},{5,9},{9,5},{13,1},{2,14},{6,10},... | collective-permute-start | bytes 110600 | tf_op jit(solution)/shard_map/ppermute | solution.py:375
  26.6 1.0 %collective-permute-done.7.refs_1_ = bf16[72,256]{1,0:T(8,128)(2,1)S(1)} collective-permute-done((bf16[72,256]{1,0:T(8,128)(2,1)S(1)}, bf16[72,256]{1,0:T(8,128)(2,1)S(1)}, u32[]{:S(2)}, u32[]{:S(2)}) %collective-permute-start.7) | collective-permute-done | bytes 36896 | tf_op jit(solution)/shard_map/ppermute | solution.py:375
  27.7 1.0 %collective-permute-done.8.refs_2_ = bf16[72,256]{1,0:T(8,128)(2,1)S(1)} collective-permute-done((bf16[72,256]{1,0:T(8,128)(2,1)S(1)}, bf16[72,256]{1,0:T(8,128)(2,1)S(1)}, u32[]{:S(2)}, u32[]{:S(2)}) %collective-permute-start.8) | collective-permute-done | bytes 36896 | tf_op jit(solution)/shard_map/ppermute | solution.py:375
  30.3 1.6 %collective-permute-done.10.b_ref = bf16[648,256]{1,0:T(8,128)(2,1)S(1)} collective-permute-done((bf16[648,256]{1,0:T(8,128)(2,1)S(1)}, bf16[648,256]{1,0:T(8,128)(2,1)S(1)}, u32[]{:S(2)}, u32[]{:S(2)}) %collective-permute-start.10) | collective-permute-done | bytes 331808 | tf_op jit(solution)/shard_map/ppermute | solution.py:347
  32.0 1.0 %collective-permute-start.13 = (bf16[576,256]{1,0:T(8,128)(2,1)S(1)}, bf16[576,256]{1,0:T(8,128)(2,1)S(1)}, u32[]{:S(2)}, u32[]{:S(2)}) collective-permute-start(bf16[576,256]{1,0:T(8,128)(2,1)S(1)} %get-tuple-element.66.a_ref), channel_id=1, source_target_pairs={{0,2},{2,0},{1,3},{3,1},{4,6},{6,4},{5,7},{7,5},{8,10},{10,8},{9,1... | collective-permute-start | bytes 884744 | tf_op jit(solution)/shard_map/ppermute | solution.py:375
  33.6 1.7 %collective-permute-start.15 = (bf16[72,256]{1,0:T(8,128)(2,1)S(1)}, bf16[72,256]{1,0:T(8,128)(2,1)S(1)}, u32[]{:S(2)}, u32[]{:S(2)}) collective-permute-start(bf16[72,256]{1,0:T(8,128)(2,1)S(1)} %get-tuple-element.67.refs_0_), channel_id=1, source_target_pairs={{0,8},{4,12},{8,0},{12,4},{1,9},{5,13},{9,1},{13,5},{2,10},{6,14},... | collective-permute-start | bytes 110600 | tf_op jit(solution)/shard_map/ppermute | solution.py:375
  35.3 2.0 %collective-permute-start.14 = (bf16[72,256]{1,0:T(8,128)(2,1)S(1)}, bf16[72,256]{1,0:T(8,128)(2,1)S(1)}, u32[]{:S(2)}, u32[]{:S(2)}) collective-permute-start(bf16[72,256]{1,0:T(8,128)(2,1)S(1)} %get-tuple-element.67.refs_0_), channel_id=1, source_target_pairs={{0,12},{4,8},{8,4},{12,0},{1,13},{5,9},{9,5},{13,1},{2,14},{6,10},... | collective-permute-start | bytes 110600 | tf_op jit(solution)/shard_map/ppermute | solution.py:375
  37.3 1.2 %collective-permute-done.12.b_ref.refs_4_ = bf16[64,256]{1,0:T(8,128)(2,1)S(1)} collective-permute-done((bf16[64,256]{1,0:T(8,128)(2,1)S(1)}, bf16[64,256]{1,0:T(8,128)(2,1)S(1)}, u32[]{:S(2)}, u32[]{:S(2)}) %collective-permute-start.12) | collective-permute-done | bytes 32800 | tf_op jit(solution)/shard_map/ppermute | solution.py:361
  38.9 2.2 %collective-permute-done.14.refs_2_ = bf16[72,256]{1,0:T(8,128)(2,1)S(1)} collective-permute-done((bf16[72,256]{1,0:T(8,128)(2,1)S(1)}, bf16[72,256]{1,0:T(8,128)(2,1)S(1)}, u32[]{:S(2)}, u32[]{:S(2)}) %collective-permute-start.14) | collective-permute-done | bytes 36896 | tf_op jit(solution)/shard_map/ppermute | solution.py:375
  41.1 1.2 %collective-permute-start.16 = (bf16[72,256]{1,0:T(8,128)(2,1)S(1)}, bf16[72,256]{1,0:T(8,128)(2,1)S(1)}, u32[]{:S(2)}, u32[]{:S(2)}) collective-permute-start(bf16[72,256]{1,0:T(8,128)(2,1)S(1)} %shard_map.76.c_ref), channel_id=1, source_target_pairs={{0,2},{2,0},{1,3},{3,1},{4,6},{6,4},{5,7},{7,5},{8,10},{10,8},{9,1... | collective-permute-start | bytes 110600 | tf_op jit(solution)/shard_map/ppermute | solution.py:375
  42.3 1.2 %shard_map.75 = (bf16[64,8,128]{2,1,0:T(8,128)(2,1)}, f32[8,128]{1,0:T(8,128)S(1)}) custom-call(bf16[8,64,256]{2,1,0:T(8,128)(2,1)S(1)} %get-tuple-element.58.g_ref, bf16[136,256]{1,0:T(8,128)(2,1)S(1)} %collective-permute-done.11.a_ref.refs_1_, bf16[64,256]{1,0:T(8,128)(2,1)S(1)} %collective-permute-done.12.b_ref.refs_4_, ...), custom_call_target="tpu_custom_call" | custom-call | flops 150994944 | bytes 573440 | tf_op jit(solution)/shard_map/pallas_call | solution.py:30
  43.5 1.7 %collective-permute-done.16.d_ref = bf16[72,256]{1,0:T(8,128)(2,1)S(1)} collective-permute-done((bf16[72,256]{1,0:T(8,128)(2,1)S(1)}, bf16[72,256]{1,0:T(8,128)(2,1)S(1)}, u32[]{:S(2)}, u32[]{:S(2)}) %collective-permute-start.16) | collective-permute-done | bytes 36896 | tf_op jit(solution)/shard_map/ppermute | solution.py:375
  45.3 1.6 %collective-permute-done.17.other_ref = bf16[648,256]{1,0:T(8,128)(2,1)S(1)} collective-permute-done((bf16[648,256]{1,0:T(8,128)(2,1)S(1)}, bf16[648,256]{1,0:T(8,128)(2,1)S(1)}, u32[]{:S(2)}, u32[]{:S(2)}) %collective-permute-start.17) | collective-permute-done | bytes 331808 | tf_op jit(solution)/shard_map/ppermute | solution.py:347
  46.9 1.2 %shard_map.78 = (f32[3,192,64]{2,1,0:T(8,128)}, f32[1152,256]{1,0:T(8,128)}) custom-call(bf16[648,256]{1,0:T(8,128)(2,1)S(1)} %shard_map.77.mine_ref, bf16[648,256]{1,0:T(8,128)(2,1)S(1)} %collective-permute-done.17.other_ref), custom_call_target="tpu_custom_call" | custom-call | flops 1 | bytes 1990656 | tf_op jit(solution)/shard_map/pallas_call | solution.py:30
  (37 shorter events, 8.8 us)
Async XLA Ops:
  0.6 20.8 %copy-start = (bf16[128,3,3,256]{3,0,2,1:T(8,128)(2,1)S(1)}, bf16[128,3,3,256]{3,0,2,1:T(8,128)(2,1)}, u32[]{:S(2)}) copy-start(bf16[128,3,3,256]{3,0,2,1:T(8,128)(2,1)} %param.6) | copy-start | bytes 1769476
  1.7 5.7 %collective-permute-start.1 = (bf16[64,128]{1,0:T(8,128)(2,1)S(1)}, bf16[64,128]{1,0:T(8,128)(2,1)S(1)}, u32[]{:S(2)}, u32[]{:S(2)}) collective-permute-start(bf16[64,128]{1,0:T(8,128)(2,1)S(1)} %get-tuple-element.71), channel_id=1, source_target_pairs={{0,1},{1,0},{4,8},{5,9},{8,4},{9,5},{12,13},{13,12},{2,3},{3,2},{6... | collective-permute-start | bytes 49160 | tf_op jit(solution)/shard_map/ppermute | solution.py:361
  2.2 5.9 %collective-permute-start = (bf16[64,128]{1,0:T(8,128)(2,1)S(1)}, bf16[64,128]{1,0:T(8,128)(2,1)S(1)}, u32[]{:S(2)}, u32[]{:S(2)}) collective-permute-start(bf16[64,128]{1,0:T(8,128)(2,1)S(1)} %get-tuple-element.72), channel_id=1, source_target_pairs={{0,4},{4,0},{8,12},{12,8},{1,5},{5,1},{9,13},{13,9},{2,6},{6,2},{1... | collective-permute-start | bytes 49160 | tf_op jit(solution)/shard_map/ppermute | solution.py:347
  8.1 4.0 %collective-permute-start.2 = (bf16[144,128]{1,0:T(8,128)(2,1)S(1)}, bf16[144,128]{1,0:T(8,128)(2,1)S(1)}, u32[]{:S(2)}, u32[]{:S(2)}) collective-permute-start(bf16[144,128]{1,0:T(8,128)(2,1)S(1)} %get-tuple-element.39), channel_id=1, source_target_pairs={{0,16},{1,2},{2,1},{3,19},{16,0},{17,18},{18,17},{19,3},{4,20},{5,... | collective-permute-start | bytes 110600 | tf_op jit(solution)/shard_map/ppermute | solution.py:371
  9.7 2.4 %collective-permute-start.3 = (bf16[144,128]{1,0:T(8,128)(2,1)S(1)}, bf16[144,128]{1,0:T(8,128)(2,1)S(1)}, u32[]{:S(2)}, u32[]{:S(2)}) collective-permute-start(bf16[144,128]{1,0:T(8,128)(2,1)S(1)} %get-tuple-element.40), channel_id=1, source_target_pairs={{0,1},{1,0},{2,3},{3,2},{4,5},{5,4},{6,7},{7,6},{8,9},{9,8},{10,11... | collective-permute-start | bytes 110600 | tf_op jit(solution)/shard_map/ppermute | solution.py:347
  9.8 0.9 %copy-start.1 = (bf16[64,3,3,64]{3,0,2,1:T(8,128)(2,1)S(1)}, bf16[64,3,3,64]{3,0,2,1:T(8,128)(2,1)}, u32[]{:S(2)}) copy-start(bf16[64,3,3,64]{3,0,2,1:T(8,128)(2,1)} %param.5) | copy-start | bytes 221188
  13.0 6.0 %collective-permute-start.6 = (bf16[2,40,256]{2,1,0:T(8,128)(2,1)S(1)}, bf16[2,40,256]{2,1,0:T(8,128)(2,1)S(1)}, u32[]{:S(2)}, u32[]{:S(2)}) collective-permute-start(bf16[2,40,256]{2,1,0:T(8,128)(2,1)S(1)} %get-tuple-element.46.refs_0_), channel_id=1, source_target_pairs={{0,8},{4,12},{8,0},{12,4},{1,9},{5,13},{9,1},{13,5},{2,10},{6,14},... | collective-permute-start | bytes 122888 | tf_op jit(solution)/shard_map/ppermute | solution.py:375
  15.0 5.8 %collective-permute-start.5 = (bf16[2,40,256]{2,1,0:T(8,128)(2,1)S(1)}, bf16[2,40,256]{2,1,0:T(8,128)(2,1)S(1)}, u32[]{:S(2)}, u32[]{:S(2)}) collective-permute-start(bf16[2,40,256]{2,1,0:T(8,128)(2,1)S(1)} %get-tuple-element.46.refs_0_), channel_id=1, source_target_pairs={{0,12},{4,8},{8,4},{12,0},{1,13},{5,9},{9,5},{13,1},{2,14},{6,10},... | collective-permute-start | bytes 122888 | tf_op jit(solution)/shard_map/ppermute | solution.py:375
  17.5 4.0 %collective-permute-start.4 = (bf16[2,40,256]{2,1,0:T(8,128)(2,1)S(1)}, bf16[2,40,256]{2,1,0:T(8,128)(2,1)S(1)}, u32[]{:S(2)}, u32[]{:S(2)}) collective-permute-start(bf16[2,40,256]{2,1,0:T(8,128)(2,1)S(1)} %get-tuple-element.46.refs_0_), channel_id=1, source_target_pairs={{0,4},{4,0},{8,12},{12,8},{1,5},{5,1},{9,13},{13,9},{2,6},{6,2},{1... | collective-permute-start | bytes 122888 | tf_op jit(solution)/shard_map/ppermute | solution.py:375
  22.5 5.2 %collective-permute-start.7 = (bf16[72,256]{1,0:T(8,128)(2,1)S(1)}, bf16[72,256]{1,0:T(8,128)(2,1)S(1)}, u32[]{:S(2)}, u32[]{:S(2)}) collective-permute-start(bf16[72,256]{1,0:T(8,128)(2,1)S(1)} %get-tuple-element.48), channel_id=1, source_target_pairs={{0,8},{4,12},{8,0},{12,4},{1,9},{5,13},{9,1},{13,5},{2,10},{6,14},... | collective-permute-start | bytes 110600 | tf_op jit(solution)/shard_map/ppermute | solution.py:375
  22.9 5.8 %collective-permute-start.8 = (bf16[72,256]{1,0:T(8,128)(2,1)S(1)}, bf16[72,256]{1,0:T(8,128)(2,1)S(1)}, u32[]{:S(2)}, u32[]{:S(2)}) collective-permute-start(bf16[72,256]{1,0:T(8,128)(2,1)S(1)} %get-tuple-element.49), channel_id=1, source_target_pairs={{0,12},{4,8},{8,4},{12,0},{1,13},{5,9},{9,5},{13,1},{2,14},{6,10},... | collective-permute-start | bytes 110600 | tf_op jit(solution)/shard_map/ppermute | solution.py:375
  25.3 4.0 %collective-permute-start.9 = (bf16[72,256]{1,0:T(8,128)(2,1)S(1)}, bf16[72,256]{1,0:T(8,128)(2,1)S(1)}, u32[]{:S(2)}, u32[]{:S(2)}) collective-permute-start(bf16[72,256]{1,0:T(8,128)(2,1)S(1)} %get-tuple-element.50), channel_id=1, source_target_pairs={{0,4},{4,0},{8,12},{12,8},{1,5},{5,1},{9,13},{13,9},{2,6},{6,2},{1... | collective-permute-start | bytes 110600 | tf_op jit(solution)/shard_map/ppermute | solution.py:375
  30.2 1.7 %collective-permute-start.10 = (bf16[648,256]{1,0:T(8,128)(2,1)S(1)}, bf16[648,256]{1,0:T(8,128)(2,1)S(1)}, u32[]{:S(2)}, u32[]{:S(2)}) collective-permute-start(bf16[648,256]{1,0:T(8,128)(2,1)S(1)} %get-tuple-element.60), channel_id=1, source_target_pairs={{0,1},{1,0},{2,3},{3,2},{4,5},{5,4},{6,7},{7,6},{8,9},{9,8},{10,11... | collective-permute-start | bytes 995336 | tf_op jit(solution)/shard_map/ppermute | solution.py:347
  32.0 13.2 %collective-permute-start.13 = (bf16[576,256]{1,0:T(8,128)(2,1)S(1)}, bf16[576,256]{1,0:T(8,128)(2,1)S(1)}, u32[]{:S(2)}, u32[]{:S(2)}) collective-permute-start(bf16[576,256]{1,0:T(8,128)(2,1)S(1)} %get-tuple-element.66.a_ref), channel_id=1, source_target_pairs={{0,2},{2,0},{1,3},{3,1},{4,6},{6,4},{5,7},{7,5},{8,10},{10,8},{9,1... | collective-permute-start | bytes 884744 | tf_op jit(solution)/shard_map/ppermute | solution.py:375
  33.0 8.1 %collective-permute-start.11 = (bf16[136,256]{1,0:T(8,128)(2,1)S(1)}, bf16[136,256]{1,0:T(8,128)(2,1)S(1)}, u32[]{:S(2)}, u32[]{:S(2)}) collective-permute-start(bf16[136,256]{1,0:T(8,128)(2,1)S(1)} %get-tuple-element.62), channel_id=1, source_target_pairs={{0,4},{4,0},{8,12},{12,8},{1,5},{5,1},{9,13},{13,9},{2,6},{6,2},{1... | collective-permute-start | bytes 208904 | tf_op jit(solution)/shard_map/ppermute | solution.py:375
  33.6 5.2 %collective-permute-start.15 = (bf16[72,256]{1,0:T(8,128)(2,1)S(1)}, bf16[72,256]{1,0:T(8,128)(2,1)S(1)}, u32[]{:S(2)}, u32[]{:S(2)}) collective-permute-start(bf16[72,256]{1,0:T(8,128)(2,1)S(1)} %get-tuple-element.67.refs_0_), channel_id=1, source_target_pairs={{0,8},{4,12},{8,0},{12,4},{1,9},{5,13},{9,1},{13,5},{2,10},{6,14},... | collective-permute-start | bytes 110600 | tf_op jit(solution)/shard_map/ppermute | solution.py:375
  35.3 5.8 %collective-permute-start.14 = (bf16[72,256]{1,0:T(8,128)(2,1)S(1)}, bf16[72,256]{1,0:T(8,128)(2,1)S(1)}, u32[]{:S(2)}, u32[]{:S(2)}) collective-permute-start(bf16[72,256]{1,0:T(8,128)(2,1)S(1)} %get-tuple-element.67.refs_0_), channel_id=1, source_target_pairs={{0,12},{4,8},{8,4},{12,0},{1,13},{5,9},{9,5},{13,1},{2,14},{6,10},... | collective-permute-start | bytes 110600 | tf_op jit(solution)/shard_map/ppermute | solution.py:375
  37.3 1.2 %collective-permute-start.12 = (bf16[64,256]{1,0:T(8,128)(2,1)S(1)}, bf16[64,256]{1,0:T(8,128)(2,1)S(1)}, u32[]{:S(2)}, u32[]{:S(2)}) collective-permute-start(bf16[64,256]{1,0:T(8,128)(2,1)S(1)} %get-tuple-element.63), channel_id=1, source_target_pairs={{0,1},{1,0},{4,8},{5,9},{8,4},{9,5},{12,13},{13,12},{2,3},{3,2},{6... | collective-permute-start | bytes 98312 | tf_op jit(solution)/shard_map/ppermute | solution.py:361
  41.1 4.0 %collective-permute-start.16 = (bf16[72,256]{1,0:T(8,128)(2,1)S(1)}, bf16[72,256]{1,0:T(8,128)(2,1)S(1)}, u32[]{:S(2)}, u32[]{:S(2)}) collective-permute-start(bf16[72,256]{1,0:T(8,128)(2,1)S(1)} %shard_map.76.c_ref), channel_id=1, source_target_pairs={{0,2},{2,0},{1,3},{3,1},{4,6},{6,4},{5,7},{7,5},{8,10},{10,8},{9,1... | collective-permute-start | bytes 110600 | tf_op jit(solution)/shard_map/ppermute | solution.py:375
  45.2 1.7 %collective-permute-start.17 = (bf16[648,256]{1,0:T(8,128)(2,1)S(1)}, bf16[648,256]{1,0:T(8,128)(2,1)S(1)}, u32[]{:S(2)}, u32[]{:S(2)}) collective-permute-start(bf16[648,256]{1,0:T(8,128)(2,1)S(1)} %shard_map.77.mine_ref), channel_id=1, source_target_pairs={{0,1},{1,0},{2,3},{3,2},{4,5},{5,4},{6,7},{7,6},{8,9},{9,8},{10,11... | collective-permute-start | bytes 995336 | tf_op jit(solution)/shard_map/ppermute | solution.py:347

commit v15 on v12

--- a/solution.py
+++ b/solution.py
@@ -245,22 +245,23 @@
     refs[-1][...] = (a_ref[...].astype(F32) + b_ref[...].astype(F32)).astype(BF16)
 
 
-def add_halves(a_ref, b_ref, two_ref, one_ref):
-    half = two_ref.shape[0]
+def add_halves(a_ref, b_ref, border_ref, two_ref, one_ref, joined_ref):
+    half, border = two_ref.shape[0], border_ref.shape[0]
     total = (a_ref[...].astype(F32) + b_ref[...].astype(F32)).astype(BF16)
     two_ref[...] = total[:half]
     one_ref[...] = total[half:]
+    joined_ref[:border] = border_ref[...]
+    joined_ref[border:] = total[half:]
 
 
 def sum_rows(*refs):
-    *refs, a_ref, b_ref, out_ref, passed_a_ref, passed_b_ref = refs
-    terms = dict(zip(row_order(len(refs), near_first=True), (ref[...].astype(F32) for ref in refs)))
+    *refs, _, out_ref = refs
+    rows = out_ref.shape[0]
+    terms = dict(zip(row_order(len(refs), near_first=True), (ref[-rows:].astype(F32) for ref in refs)))
     terms = [terms[k] for k in range(len(refs))]
     while len(terms) > 1:
         terms = [a + b for a, b in zip(terms[::2], terms[1::2])]
     out_ref[...] = terms[0].astype(BF16)
-    passed_a_ref[...] = a_ref[...]
-    passed_b_ref[...] = b_ref[...]
 
 
 def grad_pre_one(*refs, bands):
@@ -302,7 +303,7 @@
 
 
 def layer_one_back(g_ref, a_ref, b_ref, w_ref, out_ref, done_ref, *, bands):
-    above, below = beside(a_ref, b_ref, lax.axis_index("row"), bands)
+    above, below = beside(a_ref.at[: b_ref.shape[0]], b_ref, lax.axis_index("row"), bands)
     done_ref[...] = jnp.zeros(done_ref.shape, F32)
     lines = [above] + [g_ref[h] for h in range(8)] + [below]
     rows = []
@@ -325,7 +326,7 @@
         copy.wait()
 
 
-def finish_one(mine_ref, other_ref, _, out_ref, flat_ref, *, scale):
+def finish_one(mine_ref, other_ref, out_ref, flat_ref, *, scale):
     pair = lax.axis_index("pair")
     for ref, place in ((mine_ref, pair), (other_ref, 1 - pair)):
         flat_ref[pl.ds(pl.multiple_of(place * HALF_ONE, 8), HALF_ONE)] = ref[...].astype(F32) * scale
@@ -477,22 +478,22 @@
         2 * 8 * 192 * 192 * 256,
         scratch=[pltpu.VMEM((144, 256), F32)],
     )
-    two, one = whole_call(
+    two, one, joined = whole_call(
         add_halves,
-        [shaped((half, 256)), shaped((HALF_ONE, 256))],
-        [keep, even_swap(send, "pair", 2)],
+        [shaped((half, 256)), shaped((HALF_ONE, 256)), shaped((channels + HALF_ONE, 256))],
+        [keep, even_swap(send, "pair", 2), up_a],
         0,
     )
     columns = lax.axis_size("col")
     two, two_more = sum_but_last(two, "col", columns)
-    ones = row_swaps([one] * bands, bands, near_first=True)
-    one, up_a, up_b = whole_call(
-        sum_rows, [shaped(a.shape) for a in (one, up_a, up_b)], ones + [up_a, up_b], 0
-    )
+    ones = row_swaps([one, joined] + [one] * (bands - 2), bands, near_first=True)
+    near = ones[row_order(bands, near_first=True).index(1)]
+    up_b = odd_row_swap(up_b)
+    (one,) = whole_call(sum_rows, [shaped(one.shape)], ones + [up_b], 0, after=1)
     input_grad, done = whole_call(
         functools.partial(layer_one_back, bands=bands),
         [shaped(features_in.shape), shaped((8, 128), F32)],
-        [g, even_swap(up_a, "row", bands), odd_row_swap(up_b), back_one],
+        [g, near, up_b, back_one],
         2 * band_rows * 192 * 192 * 256,
     )
     mine_two = added(two, two_more, one)
@@ -504,14 +505,13 @@
         scratch=[pltpu.VMEM((2, half, 256), F32), pltpu.SemaphoreType.DMA((2,))],
         out_spaces=[pl.ANY, pltpu.VMEM],
     )
-    mine_one = added(*sum_but_last(one, "col", columns), wrote)
+    mine_one = added(*sum_but_last(one, "col", columns), wrote, done)
     (grad_one,) = whole_call(
         functools.partial(finish_one, scale=1.0 / math.sqrt(height * width)),
         [shaped((3, 3 * channels, channels), F32)],
-        [mine_one, even_swap(mine_one, "pair", 2), done],
+        [mine_one, even_swap(mine_one, "pair", 2)],
         1,
         scratch=[pltpu.VMEM((144, 256), F32)],
-        after=1,
     )
     grad_two = jnp.transpose(grad_two.reshape(3, 3, filters, 4 * channels), (2, 0, 1, 3))
     grad_one = jnp.transpose(grad_one.reshape(3, 3, channels, channels), (2, 0, 1, 3))

time: 48.3 us -> 47.6 us (0.986)
  waiting for transfers between devices: 16.8 us -> 15.6 us
    ppermute x11, waiting for transfers between devices: 12.5 us -> 9.72 us  [xor_swap(): return lax.ppermute(values, axis, [(n, n ^ k) for n in range(count)])]
    ppermute x2, waiting for transfers between devices: 0.01 us -> 1.21 us  [odd_row_swap(): return lax.ppermute(values, ('row', 'pair'), steps)]
    ppermute x11, starting transfers between devices: 13.5 us -> 14.5 us  [xor_swap(): return lax.ppermute(values, axis, [(n, n ^ k) for n in range(count)])]
    ppermute x6 -> x5, starting transfers between devices: 5.13 us -> 4.45 us  [even_swap(): return lax.ppermute(values, axis, [(n, n ^ 1) for n in range(count)])]
    ppermute x6 -> x5, waiting for transfers between devices: 3.12 us -> 3.54 us  [even_swap(): return lax.ppermute(values, axis, [(n, n ^ 1) for n in range(count)])]
  transfers between devices with their start and end apart: 20 -> 19, of which waited for: 15 -> 14; matrix products, arithmetic and copies ran while one was open for 2% -> 2% of each run, Pallas kernels for 7% -> 7%
where the time goes in v15:
time: 47.6 us; the launch traced here: 47.4 us
  starting transfers between devices  21.1 us (44%)
  waiting for transfers between devices  15.6 us (33%)
  Pallas kernels  7.05 us (15%)
  local copies, waits for them, and re-layouts  2.77 us (6%)
  between operations  0.82 us (2%)
    ppermute x11, starting transfers between devices, xor_swap(): return lax.ppermute(values, axis, [(n, n ^ k) for n in range(count)])  14.5 us
    ppermute x11, waiting for transfers between devices, xor_swap(): return lax.ppermute(values, axis, [(n, n ^ k) for n in range(count)])  9.72 us
    pallas_call x14, Pallas kernels, whole_call(): pl.pallas_call(body, out_shape=outs, in_specs=specs, out_specs=[pl.BlockS...  7.05 us
    ppermute x5, starting transfers between devices, even_swap(): return lax.ppermute(values, axis, [(n, n ^ 1) for n in range(count)])  4.45 us
    ppermute x5, waiting for transfers between devices, even_swap(): return lax.ppermute(values, axis, [(n, n ^ 1) for n in range(count)])  3.54 us
    unnamed x6, local copies, waits for them, and re-layouts  2.75 us
    ppermute x1, starting transfers between devices, odd_strip_swap(): return lax.ppermute(values, ('grp',) + COLS, steps)  1.56 us
    ppermute x2, waiting for transfers between devices, odd_row_swap(): return lax.ppermute(values, ('row', 'pair'), steps)  1.21 us
  transfers between devices with their start and end apart: 19, of which 14 were waited for; matrix products, arithmetic and copies ran while one was open for 2% of the time, Pallas kernels for 7%

profile of v15, /device:TPU:0, one launch (start us, length us, event | category | flops | bytes accessed | tf_op | source)
XLA Modules:
  0.0 47.4 jit_solution(5605508148118404088)
XLA Ops:
  0.7 1.0 %copy.19 = bf16[64,8,128]{2,0,1:T(8,128)(2,1)S(1)} copy(bf16[64,8,128]{2,1,0:T(8,128)(2,1)} %param.4) | data formatting | bytes 262144 | tf_op args[0]
  2.2 4.1 %collective-permute-start = (bf16[64,128]{1,0:T(8,128)(2,1)S(1)}, bf16[64,128]{1,0:T(8,128)(2,1)S(1)}, u32[]{:S(2)}, u32[]{:S(2)}) collective-permute-start(bf16[64,128]{1,0:T(8,128)(2,1)S(1)} %get-tuple-element.72), channel_id=1, source_target_pairs={{0,4},{4,0},{8,12},{12,8},{1,5},{5,1},{9,13},{13,9},{2,6},{6,2},{1... | collective-permute-start | bytes 49160 | tf_op jit(solution)/shard_map/ppermute | solution.py:342
  8.1 1.6 %collective-permute-start.2 = (bf16[144,128]{1,0:T(8,128)(2,1)S(1)}, bf16[144,128]{1,0:T(8,128)(2,1)S(1)}, u32[]{:S(2)}, u32[]{:S(2)}) collective-permute-start(bf16[144,128]{1,0:T(8,128)(2,1)S(1)} %get-tuple-element.39), channel_id=1, source_target_pairs={{0,16},{1,2},{2,1},{3,19},{16,0},{17,18},{18,17},{19,3},{4,20},{5,... | collective-permute-start | bytes 110600 | tf_op jit(solution)/shard_map/ppermute | solution.py:366
  9.8 0.9 %copy-done.1 = bf16[64,3,3,64]{3,0,2,1:T(8,128)(2,1)S(1)} copy-done((bf16[64,3,3,64]{3,0,2,1:T(8,128)(2,1)S(1)}, bf16[64,3,3,64]{3,0,2,1:T(8,128)(2,1)}, u32[]{:S(2)}) %copy-start.1) | copy-done | bytes 73752
  10.9 1.2 %collective-permute-done.2.b_ref = bf16[144,128]{1,0:T(8,128)(2,1)S(1)} collective-permute-done((bf16[144,128]{1,0:T(8,128)(2,1)S(1)}, bf16[144,128]{1,0:T(8,128)(2,1)S(1)}, u32[]{:S(2)}, u32[]{:S(2)}) %collective-permute-start.2) | collective-permute-done | bytes 36896 | tf_op jit(solution)/shard_map/ppermute | solution.py:366
  13.0 2.0 %collective-permute-start.6 = (bf16[2,40,256]{2,1,0:T(8,128)(2,1)S(1)}, bf16[2,40,256]{2,1,0:T(8,128)(2,1)S(1)}, u32[]{:S(2)}, u32[]{:S(2)}) collective-permute-start(bf16[2,40,256]{2,1,0:T(8,128)(2,1)S(1)} %get-tuple-element.46.refs_0_), channel_id=1, source_target_pairs={{0,8},{4,12},{8,0},{12,4},{1,9},{5,13},{9,1},{13,5},{2,10},{6,14},... | collective-permute-start | bytes 122888 | tf_op jit(solution)/shard_map/ppermute | solution.py:370
  15.0 2.5 %collective-permute-start.5 = (bf16[2,40,256]{2,1,0:T(8,128)(2,1)S(1)}, bf16[2,40,256]{2,1,0:T(8,128)(2,1)S(1)}, u32[]{:S(2)}, u32[]{:S(2)}) collective-permute-start(bf16[2,40,256]{2,1,0:T(8,128)(2,1)S(1)} %get-tuple-element.46.refs_0_), channel_id=1, source_target_pairs={{0,12},{4,8},{8,4},{12,0},{1,13},{5,9},{9,5},{13,1},{2,14},{6,10},... | collective-permute-start | bytes 122888 | tf_op jit(solution)/shard_map/ppermute | solution.py:370
  17.6 1.4 %collective-permute-done.6.refs_3_ = bf16[2,40,256]{2,1,0:T(8,128)(2,1)S(1)} collective-permute-done((bf16[2,40,256]{2,1,0:T(8,128)(2,1)S(1)}, bf16[2,40,256]{2,1,0:T(8,128)(2,1)S(1)}, u32[]{:S(2)}, u32[]{:S(2)}) %collective-permute-start.6) | collective-permute-done | bytes 40992 | tf_op jit(solution)/shard_map/ppermute | solution.py:370
  19.0 1.8 %collective-permute-done.5.refs_2_ = bf16[2,40,256]{2,1,0:T(8,128)(2,1)S(1)} collective-permute-done((bf16[2,40,256]{2,1,0:T(8,128)(2,1)S(1)}, bf16[2,40,256]{2,1,0:T(8,128)(2,1)S(1)}, u32[]{:S(2)}, u32[]{:S(2)}) %collective-permute-start.5) | collective-permute-done | bytes 40992 | tf_op jit(solution)/shard_map/ppermute | solution.py:370
  21.5 1.0 %shard_map.71 = (bf16[72,256]{1,0:T(8,128)(2,1)S(1)}, bf16[72,256]{1,0:T(8,128)(2,1)S(1)}, bf16[72,256]{1,0:T(8,128)(2,1)S(1)}, bf16[72,256]{1,0:T(8,128)(2,1)S(...) custom-call(bf16[8,48,128]{2,1,0:T(8,128)(2,1)S(1)} %fusion.6.og_ref, ...), custom_call_target="tpu_custom_call" | custom-call | flops 452984832 | bytes 1368064 | tf_op jit(solution)/shard_map/pallas_call | solution.py:30
  22.9 2.5 %collective-permute-start.8 = (bf16[72,256]{1,0:T(8,128)(2,1)S(1)}, bf16[72,256]{1,0:T(8,128)(2,1)S(1)}, u32[]{:S(2)}, u32[]{:S(2)}) collective-permute-start(bf16[72,256]{1,0:T(8,128)(2,1)S(1)} %get-tuple-element.49), channel_id=1, source_target_pairs={{0,12},{4,8},{8,4},{12,0},{1,13},{5,9},{9,5},{13,1},{2,14},{6,10},... | collective-permute-start | bytes 110600 | tf_op jit(solution)/shard_map/ppermute | solution.py:370
  26.6 1.0 %collective-permute-done.7.refs_1_ = bf16[72,256]{1,0:T(8,128)(2,1)S(1)} collective-permute-done((bf16[72,256]{1,0:T(8,128)(2,1)S(1)}, bf16[72,256]{1,0:T(8,128)(2,1)S(1)}, u32[]{:S(2)}, u32[]{:S(2)}) %collective-permute-start.7) | collective-permute-done | bytes 36896 | tf_op jit(solution)/shard_map/ppermute | solution.py:370
  27.7 1.0 %collective-permute-done.8.refs_2_ = bf16[72,256]{1,0:T(8,128)(2,1)S(1)} collective-permute-done((bf16[72,256]{1,0:T(8,128)(2,1)S(1)}, bf16[72,256]{1,0:T(8,128)(2,1)S(1)}, u32[]{:S(2)}, u32[]{:S(2)}) %collective-permute-start.8) | collective-permute-done | bytes 36896 | tf_op jit(solution)/shard_map/ppermute | solution.py:370
  29.3 0.9 %shard_map.73 = (bf16[8,64,256]{2,1,0:T(8,128)(2,1)S(1)}, bf16[64,256]{1,0:T(8,128)(2,1)S(1)}, bf16[64,256]{1,0:T(8,128)(2,1)S(1)}, bf16[648,256]{1,0:T(8,128)(2,1)S(1)}, bf16[648,256]{1,0:T(8,128)(2,1)S(1)}) custom-call(bf16[72,256]{1,0:T(8,128)(2,1)S(1)} %get-tuple-element.47.refs_0_, bf16[72,256]{1,0:T(8,128)(2,1)S(1)} %collective-permute-done.7.refs_1_, ...), custom_call_target="tpu_custom_call" | custom-call | flops 150994944 | bytes 2498560 | tf_op jit(solution)/shard_map/pallas_call | solution.py:30
  30.3 1.6 %collective-permute-done.10.b_ref = bf16[648,256]{1,0:T(8,128)(2,1)S(1)} collective-permute-done((bf16[648,256]{1,0:T(8,128)(2,1)S(1)}, bf16[648,256]{1,0:T(8,128)(2,1)S(1)}, u32[]{:S(2)}, u32[]{:S(2)}) %collective-permute-start.10) | collective-permute-done | bytes 331808 | tf_op jit(solution)/shard_map/ppermute | solution.py:342
  32.0 1.0 %collective-permute-start.16 = (bf16[576,256]{1,0:T(8,128)(2,1)S(1)}, bf16[576,256]{1,0:T(8,128)(2,1)S(1)}, u32[]{:S(2)}, u32[]{:S(2)}) collective-permute-start(bf16[576,256]{1,0:T(8,128)(2,1)S(1)} %get-tuple-element.67.a_ref), channel_id=1, source_target_pairs={{0,2},{2,0},{1,3},{3,1},{4,6},{6,4},{5,7},{7,5},{8,10},{10,8},{9,1... | collective-permute-start | bytes 884744 | tf_op jit(solution)/shard_map/ppermute | solution.py:370
  33.6 1.7 %collective-permute-start.14 = (bf16[72,256]{1,0:T(8,128)(2,1)S(1)}, bf16[72,256]{1,0:T(8,128)(2,1)S(1)}, u32[]{:S(2)}, u32[]{:S(2)}) collective-permute-start(bf16[72,256]{1,0:T(8,128)(2,1)S(1)} %get-tuple-element.66.refs_0_), channel_id=1, source_target_pairs={{0,8},{4,12},{8,0},{12,4},{1,9},{5,13},{9,1},{13,5},{2,10},{6,14},... | collective-permute-start | bytes 110600 | tf_op jit(solution)/shard_map/ppermute | solution.py:370
  35.3 2.0 %collective-permute-start.13 = (bf16[72,256]{1,0:T(8,128)(2,1)S(1)}, bf16[72,256]{1,0:T(8,128)(2,1)S(1)}, u32[]{:S(2)}, u32[]{:S(2)}) collective-permute-start(bf16[72,256]{1,0:T(8,128)(2,1)S(1)} %get-tuple-element.66.refs_0_), channel_id=1, source_target_pairs={{0,12},{4,8},{8,4},{12,0},{1,13},{5,9},{9,5},{13,1},{2,14},{6,10},... | collective-permute-start | bytes 110600 | tf_op jit(solution)/shard_map/ppermute | solution.py:370
  37.3 1.2 %collective-permute-done.12.b_ref.refs_4_ = bf16[64,256]{1,0:T(8,128)(2,1)S(1)} collective-permute-done((bf16[64,256]{1,0:T(8,128)(2,1)S(1)}, bf16[64,256]{1,0:T(8,128)(2,1)S(1)}, u32[]{:S(2)}, u32[]{:S(2)}) %collective-permute-start.12) | collective-permute-done | bytes 32800 | tf_op jit(solution)/shard_map/ppermute | solution.py:356
  38.9 2.2 %collective-permute-done.13.refs_2_ = bf16[72,256]{1,0:T(8,128)(2,1)S(1)} collective-permute-done((bf16[72,256]{1,0:T(8,128)(2,1)S(1)}, bf16[72,256]{1,0:T(8,128)(2,1)S(1)}, u32[]{:S(2)}, u32[]{:S(2)}) %collective-permute-start.13) | collective-permute-done | bytes 36896 | tf_op jit(solution)/shard_map/ppermute | solution.py:370
  41.3 1.2 %collective-permute-start.15 = (bf16[72,256]{1,0:T(8,128)(2,1)S(1)}, bf16[72,256]{1,0:T(8,128)(2,1)S(1)}, u32[]{:S(2)}, u32[]{:S(2)}) collective-permute-start(bf16[72,256]{1,0:T(8,128)(2,1)S(1)} %shard_map.76.refs_0_.a_ref), channel_id=1, source_target_pairs={{0,2},{2,0},{1,3},{3,1},{4,6},{6,4},{5,7},{7,5},{8,10},{10,8},{9,1... | collective-permute-start | bytes 110600 | tf_op jit(solution)/shard_map/ppermute | solution.py:370
  42.4 1.2 %shard_map.75 = (bf16[64,8,128]{2,1,0:T(8,128)(2,1)}, f32[8,128]{1,0:T(8,128)S(1)}) custom-call(bf16[8,64,256]{2,1,0:T(8,128)(2,1)S(1)} %get-tuple-element.58.g_ref, bf16[136,256]{1,0:T(8,128)(2,1)S(1)} %collective-permute-done.11.a_ref.refs_1_, bf16[64,256]{1,0:T(8,128)(2,1)S(1)} %collective-permute-done.12.b_ref.refs_4_, ...), custom_call_target="tpu_custom_call" | custom-call | flops 150994944 | bytes 573440 | tf_op jit(solution)/shard_map/pallas_call | solution.py:30
  43.6 1.1 %shard_map.78 = (f32[1152,256]{1,0:T(8,128)}, f32[8,128]{1,0:T(8,128)S(1)}) custom-call(bf16[576,256]{1,0:T(8,128)(2,1)S(1)} %shard_map.77.mine_ref, bf16[576,256]{1,0:T(8,128)(2,1)S(1)} %collective-permute-done.17.other_ref), custom_call_target="tpu_custom_call" | custom-call | flops 100000000 | bytes 1773568 | tf_op jit(solution)/shard_map/pallas_call | solution.py:30
  45.4 1.2 %collective-permute-done.18.other_ref = bf16[72,256]{1,0:T(8,128)(2,1)S(1)} collective-permute-done((bf16[72,256]{1,0:T(8,128)(2,1)S(1)}, bf16[72,256]{1,0:T(8,128)(2,1)S(1)}, u32[]{:S(2)}, u32[]{:S(2)}) %collective-permute-start.18) | collective-permute-done | bytes 36896 | tf_op jit(solution)/shard_map/ppermute | solution.py:342
  (41 shorter events, 9.4 us)
Async XLA Ops:
  0.6 20.8 %copy-start = (bf16[128,3,3,256]{3,0,2,1:T(8,128)(2,1)S(1)}, bf16[128,3,3,256]{3,0,2,1:T(8,128)(2,1)}, u32[]{:S(2)}) copy-start(bf16[128,3,3,256]{3,0,2,1:T(8,128)(2,1)} %param.6) | copy-start | bytes 1769476
  1.7 5.7 %collective-permute-start.1 = (bf16[64,128]{1,0:T(8,128)(2,1)S(1)}, bf16[64,128]{1,0:T(8,128)(2,1)S(1)}, u32[]{:S(2)}, u32[]{:S(2)}) collective-permute-start(bf16[64,128]{1,0:T(8,128)(2,1)S(1)} %get-tuple-element.71), channel_id=1, source_target_pairs={{0,1},{1,0},{4,8},{5,9},{8,4},{9,5},{12,13},{13,12},{2,3},{3,2},{6... | collective-permute-start | bytes 49160 | tf_op jit(solution)/shard_map/ppermute | solution.py:356
  2.2 5.9 %collective-permute-start = (bf16[64,128]{1,0:T(8,128)(2,1)S(1)}, bf16[64,128]{1,0:T(8,128)(2,1)S(1)}, u32[]{:S(2)}, u32[]{:S(2)}) collective-permute-start(bf16[64,128]{1,0:T(8,128)(2,1)S(1)} %get-tuple-element.72), channel_id=1, source_target_pairs={{0,4},{4,0},{8,12},{12,8},{1,5},{5,1},{9,13},{13,9},{2,6},{6,2},{1... | collective-permute-start | bytes 49160 | tf_op jit(solution)/shard_map/ppermute | solution.py:342
  8.1 4.0 %collective-permute-start.2 = (bf16[144,128]{1,0:T(8,128)(2,1)S(1)}, bf16[144,128]{1,0:T(8,128)(2,1)S(1)}, u32[]{:S(2)}, u32[]{:S(2)}) collective-permute-start(bf16[144,128]{1,0:T(8,128)(2,1)S(1)} %get-tuple-element.39), channel_id=1, source_target_pairs={{0,16},{1,2},{2,1},{3,19},{16,0},{17,18},{18,17},{19,3},{4,20},{5,... | collective-permute-start | bytes 110600 | tf_op jit(solution)/shard_map/ppermute | solution.py:366
  9.7 2.4 %collective-permute-start.3 = (bf16[144,128]{1,0:T(8,128)(2,1)S(1)}, bf16[144,128]{1,0:T(8,128)(2,1)S(1)}, u32[]{:S(2)}, u32[]{:S(2)}) collective-permute-start(bf16[144,128]{1,0:T(8,128)(2,1)S(1)} %get-tuple-element.40), channel_id=1, source_target_pairs={{0,1},{1,0},{2,3},{3,2},{4,5},{5,4},{6,7},{7,6},{8,9},{9,8},{10,11... | collective-permute-start | bytes 110600 | tf_op jit(solution)/shard_map/ppermute | solution.py:342
  9.8 0.9 %copy-start.1 = (bf16[64,3,3,64]{3,0,2,1:T(8,128)(2,1)S(1)}, bf16[64,3,3,64]{3,0,2,1:T(8,128)(2,1)}, u32[]{:S(2)}) copy-start(bf16[64,3,3,64]{3,0,2,1:T(8,128)(2,1)} %param.5) | copy-start | bytes 221188
  13.0 6.0 %collective-permute-start.6 = (bf16[2,40,256]{2,1,0:T(8,128)(2,1)S(1)}, bf16[2,40,256]{2,1,0:T(8,128)(2,1)S(1)}, u32[]{:S(2)}, u32[]{:S(2)}) collective-permute-start(bf16[2,40,256]{2,1,0:T(8,128)(2,1)S(1)} %get-tuple-element.46.refs_0_), channel_id=1, source_target_pairs={{0,8},{4,12},{8,0},{12,4},{1,9},{5,13},{9,1},{13,5},{2,10},{6,14},... | collective-permute-start | bytes 122888 | tf_op jit(solution)/shard_map/ppermute | solution.py:370
  15.0 5.8 %collective-permute-start.5 = (bf16[2,40,256]{2,1,0:T(8,128)(2,1)S(1)}, bf16[2,40,256]{2,1,0:T(8,128)(2,1)S(1)}, u32[]{:S(2)}, u32[]{:S(2)}) collective-permute-start(bf16[2,40,256]{2,1,0:T(8,128)(2,1)S(1)} %get-tuple-element.46.refs_0_), channel_id=1, source_target_pairs={{0,12},{4,8},{8,4},{12,0},{1,13},{5,9},{9,5},{13,1},{2,14},{6,10},... | collective-permute-start | bytes 122888 | tf_op jit(solution)/shard_map/ppermute | solution.py:370
  17.5 4.0 %collective-permute-start.4 = (bf16[2,40,256]{2,1,0:T(8,128)(2,1)S(1)}, bf16[2,40,256]{2,1,0:T(8,128)(2,1)S(1)}, u32[]{:S(2)}, u32[]{:S(2)}) collective-permute-start(bf16[2,40,256]{2,1,0:T(8,128)(2,1)S(1)} %get-tuple-element.46.refs_0_), channel_id=1, source_target_pairs={{0,4},{4,0},{8,12},{12,8},{1,5},{5,1},{9,13},{13,9},{2,6},{6,2},{1... | collective-permute-start | bytes 122888 | tf_op jit(solution)/shard_map/ppermute | solution.py:370
  22.5 5.2 %collective-permute-start.7 = (bf16[72,256]{1,0:T(8,128)(2,1)S(1)}, bf16[72,256]{1,0:T(8,128)(2,1)S(1)}, u32[]{:S(2)}, u32[]{:S(2)}) collective-permute-start(bf16[72,256]{1,0:T(8,128)(2,1)S(1)} %get-tuple-element.48), channel_id=1, source_target_pairs={{0,8},{4,12},{8,0},{12,4},{1,9},{5,13},{9,1},{13,5},{2,10},{6,14},... | collective-permute-start | bytes 110600 | tf_op jit(solution)/shard_map/ppermute | solution.py:370
  22.9 5.8 %collective-permute-start.8 = (bf16[72,256]{1,0:T(8,128)(2,1)S(1)}, bf16[72,256]{1,0:T(8,128)(2,1)S(1)}, u32[]{:S(2)}, u32[]{:S(2)}) collective-permute-start(bf16[72,256]{1,0:T(8,128)(2,1)S(1)} %get-tuple-element.49), channel_id=1, source_target_pairs={{0,12},{4,8},{8,4},{12,0},{1,13},{5,9},{9,5},{13,1},{2,14},{6,10},... | collective-permute-start | bytes 110600 | tf_op jit(solution)/shard_map/ppermute | solution.py:370
  25.3 4.0 %collective-permute-start.9 = (bf16[72,256]{1,0:T(8,128)(2,1)S(1)}, bf16[72,256]{1,0:T(8,128)(2,1)S(1)}, u32[]{:S(2)}, u32[]{:S(2)}) collective-permute-start(bf16[72,256]{1,0:T(8,128)(2,1)S(1)} %get-tuple-element.50), channel_id=1, source_target_pairs={{0,4},{4,0},{8,12},{12,8},{1,5},{5,1},{9,13},{13,9},{2,6},{6,2},{1... | collective-permute-start | bytes 110600 | tf_op jit(solution)/shard_map/ppermute | solution.py:370
  30.2 1.7 %collective-permute-start.10 = (bf16[648,256]{1,0:T(8,128)(2,1)S(1)}, bf16[648,256]{1,0:T(8,128)(2,1)S(1)}, u32[]{:S(2)}, u32[]{:S(2)}) collective-permute-start(bf16[648,256]{1,0:T(8,128)(2,1)S(1)} %get-tuple-element.60), channel_id=1, source_target_pairs={{0,1},{1,0},{2,3},{3,2},{4,5},{5,4},{6,7},{7,6},{8,9},{9,8},{10,11... | collective-permute-start | bytes 995336 | tf_op jit(solution)/shard_map/ppermute | solution.py:342
  32.0 9.1 %collective-permute-start.16 = (bf16[576,256]{1,0:T(8,128)(2,1)S(1)}, bf16[576,256]{1,0:T(8,128)(2,1)S(1)}, u32[]{:S(2)}, u32[]{:S(2)}) collective-permute-start(bf16[576,256]{1,0:T(8,128)(2,1)S(1)} %get-tuple-element.67.a_ref), channel_id=1, source_target_pairs={{0,2},{2,0},{1,3},{3,1},{4,6},{6,4},{5,7},{7,5},{8,10},{10,8},{9,1... | collective-permute-start | bytes 884744 | tf_op jit(solution)/shard_map/ppermute | solution.py:370
  33.0 8.1 %collective-permute-start.11 = (bf16[136,256]{1,0:T(8,128)(2,1)S(1)}, bf16[136,256]{1,0:T(8,128)(2,1)S(1)}, u32[]{:S(2)}, u32[]{:S(2)}) collective-permute-start(bf16[136,256]{1,0:T(8,128)(2,1)S(1)} %get-tuple-element.62), channel_id=1, source_target_pairs={{0,4},{4,0},{8,12},{12,8},{1,5},{5,1},{9,13},{13,9},{2,6},{6,2},{1... | collective-permute-start | bytes 208904 | tf_op jit(solution)/shard_map/ppermute | solution.py:370
  33.6 5.2 %collective-permute-start.14 = (bf16[72,256]{1,0:T(8,128)(2,1)S(1)}, bf16[72,256]{1,0:T(8,128)(2,1)S(1)}, u32[]{:S(2)}, u32[]{:S(2)}) collective-permute-start(bf16[72,256]{1,0:T(8,128)(2,1)S(1)} %get-tuple-element.66.refs_0_), channel_id=1, source_target_pairs={{0,8},{4,12},{8,0},{12,4},{1,9},{5,13},{9,1},{13,5},{2,10},{6,14},... | collective-permute-start | bytes 110600 | tf_op jit(solution)/shard_map/ppermute | solution.py:370
  35.3 5.8 %collective-permute-start.13 = (bf16[72,256]{1,0:T(8,128)(2,1)S(1)}, bf16[72,256]{1,0:T(8,128)(2,1)S(1)}, u32[]{:S(2)}, u32[]{:S(2)}) collective-permute-start(bf16[72,256]{1,0:T(8,128)(2,1)S(1)} %get-tuple-element.66.refs_0_), channel_id=1, source_target_pairs={{0,12},{4,8},{8,4},{12,0},{1,13},{5,9},{9,5},{13,1},{2,14},{6,10},... | collective-permute-start | bytes 110600 | tf_op jit(solution)/shard_map/ppermute | solution.py:370
  37.3 1.2 %collective-permute-start.12 = (bf16[64,256]{1,0:T(8,128)(2,1)S(1)}, bf16[64,256]{1,0:T(8,128)(2,1)S(1)}, u32[]{:S(2)}, u32[]{:S(2)}) collective-permute-start(bf16[64,256]{1,0:T(8,128)(2,1)S(1)} %get-tuple-element.63), channel_id=1, source_target_pairs={{0,1},{1,0},{4,8},{5,9},{8,4},{9,5},{12,13},{13,12},{2,3},{3,2},{6... | collective-permute-start | bytes 98312 | tf_op jit(solution)/shard_map/ppermute | solution.py:356
  41.2 2.4 %collective-permute-start.17 = (bf16[576,256]{1,0:T(8,128)(2,1)S(1)}, bf16[576,256]{1,0:T(8,128)(2,1)S(1)}, u32[]{:S(2)}, u32[]{:S(2)}) collective-permute-start(bf16[576,256]{1,0:T(8,128)(2,1)S(1)} %shard_map.77.mine_ref), channel_id=1, source_target_pairs={{0,1},{1,0},{2,3},{3,2},{4,5},{5,4},{6,7},{7,6},{8,9},{9,8},{10,11... | collective-permute-start | bytes 884744 | tf_op jit(solution)/shard_map/ppermute | solution.py:342
  41.3 4.0 %collective-permute-start.15 = (bf16[72,256]{1,0:T(8,128)(2,1)S(1)}, bf16[72,256]{1,0:T(8,128)(2,1)S(1)}, u32[]{:S(2)}, u32[]{:S(2)}) collective-permute-start(bf16[72,256]{1,0:T(8,128)(2,1)S(1)} %shard_map.76.refs_0_.a_ref), channel_id=1, source_target_pairs={{0,2},{2,0},{1,3},{3,1},{4,6},{6,4},{5,7},{7,5},{8,10},{10,8},{9,1... | collective-permute-start | bytes 110600 | tf_op jit(solution)/shard_map/ppermute | solution.py:370
  45.3 1.3 %collective-permute-start.18 = (bf16[72,256]{1,0:T(8,128)(2,1)S(1)}, bf16[72,256]{1,0:T(8,128)(2,1)S(1)}, u32[]{:S(2)}, u32[]{:S(2)}) collective-permute-start(bf16[72,256]{1,0:T(8,128)(2,1)S(1)} %shard_map.79.mine_ref), channel_id=1, source_target_pairs={{0,1},{1,0},{2,3},{3,2},{4,5},{5,4},{6,7},{7,6},{8,9},{9,8},{10,11... | collective-permute-start | bytes 110600 | tf_op jit(solution)/shard_map/ppermute | solution.py:342

commit v16 on v13

--- a/solution.py
+++ b/solution.py
@@ -12,7 +12,7 @@
 F32 = jnp.float32
 COLS = ("col", "pair")
 REACH = 3
-HALF_ONE = 72
+ROWS_ONE = 144
 PITCH = 48
 SENT = 40
 
@@ -252,28 +252,25 @@
     one_ref[...] = total[half:]
 
 
-def add_joined(a_ref, b_ref, c_ref, d_ref, _, __, out_ref):
+def add_joined(a_ref, b_ref, c_ref, d_ref, _, out_ref):
     half = a_ref.shape[0]
     out_ref[:half] = (a_ref[...].astype(F32) + b_ref[...].astype(F32)).astype(BF16)
     out_ref[half:] = (c_ref[...].astype(F32) + d_ref[...].astype(F32)).astype(BF16)
 
 
 def sum_rows(*refs):
-    *refs, a_ref, b_ref, out_ref, passed_a_ref, passed_b_ref = refs
+    *refs, _, _, out_ref = refs
     terms = dict(zip(row_order(len(refs), near_first=True), (ref[...].astype(F32) for ref in refs)))
     terms = [terms[k] for k in range(len(refs))]
     while len(terms) > 1:
         terms = [a + b for a, b in zip(terms[::2], terms[1::2])]
     out_ref[...] = terms[0].astype(BF16)
-    passed_a_ref[...] = a_ref[...]
-    passed_b_ref[...] = b_ref[...]
 
 
 def grad_pre_one(*refs, bands):
     terms, refs = refs[:bands], refs[bands:]
     slope_ref, wide_ref, pool_ref, order_ref, keep_two_ref, send_two_ref, *refs = refs
     g_ref, a_ref, b_ref, keep_ref, send_ref, part_ref = refs
-    pair = lax.axis_index("pair")
     summed = terms[0][...].astype(F32)
     for k in range(1, bands):
         summed = summed + terms[k][...].astype(F32)
@@ -302,9 +299,9 @@
     part_ref[:96] = jnp.concatenate([acc[:96, :128], acc[96:, :128]], 1)
     part_ref[96:] = jnp.concatenate([acc[48 * q : 48 * q + 48, 128:] for q in range(4)], 1)
     half = keep_two_ref.shape[0]
-    for ref, two_ref, place in ((keep_ref, keep_two_ref, pair), (send_ref, send_two_ref, 1 - pair)):
+    for ref, two_ref in ((keep_ref, keep_two_ref), (send_ref, send_two_ref)):
         ref[:half] = two_ref[...]
-        ref[half:] = part_ref[pl.ds(pl.multiple_of(place * HALF_ONE, 8), HALF_ONE)].astype(BF16)
+        ref[half:] = part_ref[...].astype(BF16)
 
 
 def layer_one_back(g_ref, a_ref, b_ref, w_ref, out_ref, done_ref, *, bands):
@@ -318,18 +315,16 @@
     out_ref[...] = jnp.swapaxes(jnp.stack(rows, 0), 0, 1).astype(BF16)
 
 
-def finish(mine_ref, other_ref, _, one_hbm, two_hbm, one_ref, two_ref, flat_ref, sems, *, scales):
-    pair, half = lax.axis_index("pair"), mine_ref.shape[0] - HALF_ONE
-    halves = ((mine_ref, pair), (other_ref, 1 - pair))
+def finish(mine_ref, other_ref, one_hbm, two_hbm, one_ref, two_ref, flat_ref, sems, *, scales):
+    pair, half = lax.axis_index("pair"), mine_ref.shape[0] - ROWS_ONE
     copies = []
-    for n, (ref, place) in enumerate(halves):
+    for n, (ref, place) in enumerate(((mine_ref, pair), (other_ref, 1 - pair))):
         rows = pl.ds(pl.multiple_of(place * half, 16), half)
         two_ref[n] = ref[:half].astype(F32) * scales[1]
         copies.append(pltpu.make_async_copy(two_ref.at[n], two_hbm.at[rows], sems.at[n]))
         copies[-1].start()
-    for ref, place in halves:
-        rows = pl.ds(pl.multiple_of(place * HALF_ONE, 8), HALF_ONE)
-        flat_ref[rows] = ref[half:].astype(F32) * scales[0]
+    last = pair == lax.axis_size("pair") - 1
+    flat_ref[...] = jnp.where(last, mine_ref[half:].astype(F32), other_ref[half:].astype(F32)) * scales[0]
     one_ref[0, :96] = flat_ref[:96, :64]
     one_ref[1, :96] = flat_ref[:96, 64:128]
     one_ref[0, 96:] = flat_ref[:96, 128:192]
@@ -372,6 +367,17 @@
 
 def xor_swap(values, axis, count, k):
     return lax.ppermute(values, axis, [(n, n ^ k) for n in range(count)])
+
+
+def last_core_swap(values, axis, k):
+    groups, count, cores = (lax.axis_size(name) for name in ("grp", axis, "pair"))
+    steps = []
+    for g in range(groups):
+        for n in range(count):
+            for p in range(cores):
+                to = (g, n ^ k) if p == cores - 1 else ((g + 1) % groups, n)
+                steps.append(((g * count + n) * cores + p, (to[0] * count + to[1]) * cores + p))
+    return lax.ppermute(values, ("grp", axis, "pair"), steps)
 
 
 def row_order(bands, near_first=False):
@@ -477,52 +483,52 @@
         functools.partial(grad_pre_one, bands=bands),
         [shaped((band_rows, channels, 256))]
         + [shaped((channels, 256))] * 2
-        + [shaped((half + HALF_ONE, 256))] * 2,
+        + [shaped((half + ROWS_ONE, 256))] * 2,
         received + [slope, wide, pool_back, order, keep_two, send_two],
         2 * 8 * 192 * 192 * 256,
         scratch=[pltpu.VMEM((144, 256), F32)],
     )
     two, one = whole_call(
         add_halves,
-        [shaped((half, 256)), shaped((HALF_ONE, 256))],
+        [shaped((half, 256)), shaped((ROWS_ONE, 256))],
         [keep, even_swap(send, "pair", 2)],
         0,
     )
     columns = lax.axis_size("col")
     two, two_more = sum_but_last(two, "col", columns)
-    ones = row_swaps([one] * bands, bands, near_first=True)
-    one, up_a, up_b = whole_call(
-        sum_rows, [shaped(a.shape) for a in (one, up_a, up_b)], ones + [up_a, up_b], 0
-    )
+    ones = [one] + [last_core_swap(one, "row", k) for k in row_order(bands, near_first=True)[1:]]
     up_a, up_b = even_swap(up_a, "row", bands), odd_row_swap(up_b)
+    (one,) = whole_call(sum_rows, [shaped(one.shape)], ones + [up_a, up_b], 0, after=2)
     input_grad, done = whole_call(
         functools.partial(layer_one_back, bands=bands),
         [shaped(features_in.shape), shaped((8, 128), F32)],
         [g, up_a, up_b, back_one],
         2 * band_rows * 192 * 192 * 256,
     )
-    one, one_more = sum_but_last(one, "col", columns)
+    step = 1
+    while 2 * step < columns:
+        one = added(one, last_core_swap(one, "col", step))
+        step *= 2
     (mine,) = whole_call(
         add_joined,
-        [shaped((half + HALF_ONE, 256))],
-        [two, two_more, one, one_more, up_a, up_b],
+        [shaped((half + ROWS_ONE, 256))],
+        [two, two_more, one, last_core_swap(one, "col", step), done],
         0,
-        after=2,
+        after=1,
     )
     grad_one, grad_two = whole_call(
         functools.partial(
             finish, scales=(1.0 / math.sqrt(height * width), 1.0 / math.sqrt(pooled_rows * total))
         ),
         [shaped((3, 3 * channels, channels), F32), shaped((2 * half, 256), F32)],
-        [mine, even_swap(mine, "pair", 2), done],
+        [mine, even_swap(mine, "pair", 2)],
         1,
         scratch=[
             pltpu.VMEM((3, 3 * channels, channels), F32),
             pltpu.VMEM((2, half, 256), F32),
-            pltpu.VMEM((144, 256), F32),
+            pltpu.VMEM((ROWS_ONE, 256), F32),
             pltpu.SemaphoreType.DMA((3,)),
         ],
-        after=1,
         out_spaces=[pl.ANY] * 2,
     )
     grad_two = jnp.transpose(grad_two.reshape(3, 3, filters, 4 * channels), (2, 0, 1, 3))

time: 48.5 us -> 50.1 us (1.033); the launches traced: 48.3 us -> 49.2 us
    ppermute x0 -> x4, starting transfers between devices: none -> 4.67 us  [last_core_swap(): return lax.ppermute(values, ('grp', axis, 'pair'), steps)]
    ppermute x11 -> x7, starting transfers between devices: 13.7 us -> 8.99 us  [xor_swap(): return lax.ppermute(values, axis, [(n, n ^ k) for n in range(count)])]
    ppermute x11 -> x7, waiting for transfers between devices: 10.3 us -> 6.58 us  [xor_swap(): return lax.ppermute(values, axis, [(n, n ^ k) for n in range(count)])]
    ppermute x0 -> x4, waiting for transfers between devices: none -> 2.13 us  [last_core_swap(): return lax.ppermute(values, ('grp', axis, 'pair'), steps)]
    ppermute x2, waiting for transfers between devices: 0.01 us -> 1.21 us  [odd_row_swap(): return lax.ppermute(values, ('row', 'pair'), steps)]
    ppermute x5, waiting for transfers between devices: 6.43 us -> 7.28 us  [even_swap(): return lax.ppermute(values, axis, [(n, n ^ 1) for n in range(count)])]
  transfers between devices with their start and end apart: 19 -> 19, of which waited for: 14 -> 13; matrix products, arithmetic and copies ran while one was open for 2% -> 2% of each run, Pallas kernels for 4% -> 4%
where the time goes in v16:
time: 50.1 us; the launch traced here: 49.2 us
  starting transfers between devices  20.8 us (42%)
  waiting for transfers between devices  18.4 us (37%)
  Pallas kernels  6.38 us (13%)
  local copies, waits for them, and re-layouts  2.77 us (6%)
  between operations  0.79 us (2%)
    ppermute x7, starting transfers between devices, xor_swap(): return lax.ppermute(values, axis, [(n, n ^ k) for n in range(count)])  8.99 us
    ppermute x5, waiting for transfers between devices, even_swap(): return lax.ppermute(values, axis, [(n, n ^ 1) for n in range(count)])  7.28 us
    ppermute x7, waiting for transfers between devices, xor_swap(): return lax.ppermute(values, axis, [(n, n ^ k) for n in range(count)])  6.58 us
    pallas_call x12, Pallas kernels, whole_call(): pl.pallas_call(body, out_shape=outs, in_specs=specs, out_specs=[pl.BlockS...  6.38 us
    ppermute x5, starting transfers between devices, even_swap(): return lax.ppermute(values, axis, [(n, n ^ 1) for n in range(count)])  5.07 us
    ppermute x4, starting transfers between devices, last_core_swap(): return lax.ppermute(values, ('grp', axis, 'pair'), steps)  4.67 us
    unnamed x6, local copies, waits for them, and re-layouts  2.75 us
    ppermute x4, waiting for transfers between devices, last_core_swap(): return lax.ppermute(values, ('grp', axis, 'pair'), steps)  2.13 us
  transfers between devices with their start and end apart: 19, of which 13 were waited for; matrix products, arithmetic and copies ran while one was open for 2% of the time, Pallas kernels for 4%

profile of v16, /device:TPU:0, one launch (start us, length us, event | category | flops | bytes accessed | tf_op | source)
XLA Modules:
  0.0 49.2 jit_solution(11490336814316122939)
XLA Ops:
  0.7 1.0 %copy.19 = bf16[64,8,128]{2,0,1:T(8,128)(2,1)S(1)} copy(bf16[64,8,128]{2,1,0:T(8,128)(2,1)} %param.4) | data formatting | bytes 262144 | tf_op args[0]
  2.2 4.1 %collective-permute-start = (bf16[64,128]{1,0:T(8,128)(2,1)S(1)}, bf16[64,128]{1,0:T(8,128)(2,1)S(1)}, u32[]{:S(2)}, u32[]{:S(2)}) collective-permute-start(bf16[64,128]{1,0:T(8,128)(2,1)S(1)} %get-tuple-element.70), channel_id=1, source_target_pairs={{0,4},{4,0},{8,12},{12,8},{1,5},{5,1},{9,13},{13,9},{2,6},{6,2},{1... | collective-permute-start | bytes 49160 | tf_op jit(solution)/shard_map/ppermute | solution.py:341
  8.1 1.6 %collective-permute-start.2 = (bf16[144,128]{1,0:T(8,128)(2,1)S(1)}, bf16[144,128]{1,0:T(8,128)(2,1)S(1)}, u32[]{:S(2)}, u32[]{:S(2)}) collective-permute-start(bf16[144,128]{1,0:T(8,128)(2,1)S(1)} %get-tuple-element.38), channel_id=1, source_target_pairs={{0,16},{1,2},{2,1},{3,19},{16,0},{17,18},{18,17},{19,3},{4,20},{5,... | collective-permute-start | bytes 110600 | tf_op jit(solution)/shard_map/ppermute | solution.py:365
  9.8 0.9 %copy-done.1 = bf16[64,3,3,64]{3,0,2,1:T(8,128)(2,1)S(1)} copy-done((bf16[64,3,3,64]{3,0,2,1:T(8,128)(2,1)S(1)}, bf16[64,3,3,64]{3,0,2,1:T(8,128)(2,1)}, u32[]{:S(2)}) %copy-start.1) | copy-done | bytes 73752
  10.9 1.2 %collective-permute-done.2.b_ref = bf16[144,128]{1,0:T(8,128)(2,1)S(1)} collective-permute-done((bf16[144,128]{1,0:T(8,128)(2,1)S(1)}, bf16[144,128]{1,0:T(8,128)(2,1)S(1)}, u32[]{:S(2)}, u32[]{:S(2)}) %collective-permute-start.2) | collective-permute-done | bytes 36896 | tf_op jit(solution)/shard_map/ppermute | solution.py:365
  13.0 2.0 %collective-permute-start.6 = (bf16[2,40,256]{2,1,0:T(8,128)(2,1)S(1)}, bf16[2,40,256]{2,1,0:T(8,128)(2,1)S(1)}, u32[]{:S(2)}, u32[]{:S(2)}) collective-permute-start(bf16[2,40,256]{2,1,0:T(8,128)(2,1)S(1)} %get-tuple-element.45.refs_0_), channel_id=1, source_target_pairs={{0,8},{4,12},{8,0},{12,4},{1,9},{5,13},{9,1},{13,5},{2,10},{6,14},... | collective-permute-start | bytes 122888 | tf_op jit(solution)/shard_map/ppermute | solution.py:369
  15.0 2.5 %collective-permute-start.5 = (bf16[2,40,256]{2,1,0:T(8,128)(2,1)S(1)}, bf16[2,40,256]{2,1,0:T(8,128)(2,1)S(1)}, u32[]{:S(2)}, u32[]{:S(2)}) collective-permute-start(bf16[2,40,256]{2,1,0:T(8,128)(2,1)S(1)} %get-tuple-element.45.refs_0_), channel_id=1, source_target_pairs={{0,12},{4,8},{8,4},{12,0},{1,13},{5,9},{9,5},{13,1},{2,14},{6,10},... | collective-permute-start | bytes 122888 | tf_op jit(solution)/shard_map/ppermute | solution.py:369
  17.6 1.4 %collective-permute-done.6.refs_3_ = bf16[2,40,256]{2,1,0:T(8,128)(2,1)S(1)} collective-permute-done((bf16[2,40,256]{2,1,0:T(8,128)(2,1)S(1)}, bf16[2,40,256]{2,1,0:T(8,128)(2,1)S(1)}, u32[]{:S(2)}, u32[]{:S(2)}) %collective-permute-start.6) | collective-permute-done | bytes 40992 | tf_op jit(solution)/shard_map/ppermute | solution.py:369
  19.0 1.8 %collective-permute-done.5.refs_2_ = bf16[2,40,256]{2,1,0:T(8,128)(2,1)S(1)} collective-permute-done((bf16[2,40,256]{2,1,0:T(8,128)(2,1)S(1)}, bf16[2,40,256]{2,1,0:T(8,128)(2,1)S(1)}, u32[]{:S(2)}, u32[]{:S(2)}) %collective-permute-start.5) | collective-permute-done | bytes 40992 | tf_op jit(solution)/shard_map/ppermute | solution.py:369
  21.5 1.0 %shard_map.71 = (bf16[72,256]{1,0:T(8,128)(2,1)S(1)}, bf16[72,256]{1,0:T(8,128)(2,1)S(1)}, bf16[72,256]{1,0:T(8,128)(2,1)S(1)}, bf16[72,256]{1,0:T(8,128)(2,1)S(...) custom-call(bf16[8,48,128]{2,1,0:T(8,128)(2,1)S(1)} %fusion.6.og_ref, ...), custom_call_target="tpu_custom_call" | custom-call | flops 452984832 | bytes 1368064 | tf_op jit(solution)/shard_map/pallas_call | solution.py:30
  22.9 2.5 %collective-permute-start.8 = (bf16[72,256]{1,0:T(8,128)(2,1)S(1)}, bf16[72,256]{1,0:T(8,128)(2,1)S(1)}, u32[]{:S(2)}, u32[]{:S(2)}) collective-permute-start(bf16[72,256]{1,0:T(8,128)(2,1)S(1)} %get-tuple-element.48), channel_id=1, source_target_pairs={{0,12},{4,8},{8,4},{12,0},{1,13},{5,9},{9,5},{13,1},{2,14},{6,10},... | collective-permute-start | bytes 110600 | tf_op jit(solution)/shard_map/ppermute | solution.py:369
  26.6 1.0 %collective-permute-done.7.refs_1_ = bf16[72,256]{1,0:T(8,128)(2,1)S(1)} collective-permute-done((bf16[72,256]{1,0:T(8,128)(2,1)S(1)}, bf16[72,256]{1,0:T(8,128)(2,1)S(1)}, u32[]{:S(2)}, u32[]{:S(2)}) %collective-permute-start.7) | collective-permute-done | bytes 36896 | tf_op jit(solution)/shard_map/ppermute | solution.py:369
  27.7 1.0 %collective-permute-done.8.refs_2_ = bf16[72,256]{1,0:T(8,128)(2,1)S(1)} collective-permute-done((bf16[72,256]{1,0:T(8,128)(2,1)S(1)}, bf16[72,256]{1,0:T(8,128)(2,1)S(1)}, u32[]{:S(2)}, u32[]{:S(2)}) %collective-permute-start.8) | collective-permute-done | bytes 36896 | tf_op jit(solution)/shard_map/ppermute | solution.py:369
  30.2 1.7 %collective-permute-done.12.b_ref = bf16[720,256]{1,0:T(8,128)(2,1)S(1)} collective-permute-done((bf16[720,256]{1,0:T(8,128)(2,1)S(1)}, bf16[720,256]{1,0:T(8,128)(2,1)S(1)}, u32[]{:S(2)}, u32[]{:S(2)}) %collective-permute-start.12) | collective-permute-done | bytes 368672 | tf_op jit(solution)/shard_map/ppermute | solution.py:341
  32.0 1.0 %collective-permute-start.13 = (bf16[576,256]{1,0:T(8,128)(2,1)S(1)}, bf16[576,256]{1,0:T(8,128)(2,1)S(1)}, u32[]{:S(2)}, u32[]{:S(2)}) collective-permute-start(bf16[576,256]{1,0:T(8,128)(2,1)S(1)} %get-tuple-element.64.a_ref), channel_id=1, source_target_pairs={{0,2},{2,0},{1,3},{3,1},{4,6},{6,4},{5,7},{7,5},{8,10},{10,8},{9,1... | collective-permute-start | bytes 884744 | tf_op jit(solution)/shard_map/ppermute | solution.py:369
  33.0 1.5 %collective-permute-start.16 = (bf16[144,256]{1,0:T(8,128)(2,1)S(1)}, bf16[144,256]{1,0:T(8,128)(2,1)S(1)}, u32[]{:S(2)}, u32[]{:S(2)}) collective-permute-start(bf16[144,256]{1,0:T(8,128)(2,1)S(1)} %get-tuple-element.65.refs_0_), channel_id=1, source_target_pairs={{0,16},{1,9},{4,20},{5,13},{8,24},{9,1},{12,28},{13,5},{16,0},{17,... | collective-permute-start | bytes 221192 | tf_op jit(solution)/shard_map/ppermute | solution.py:380
  35.0 1.5 %collective-permute-start.14 = (bf16[144,256]{1,0:T(8,128)(2,1)S(1)}, bf16[144,256]{1,0:T(8,128)(2,1)S(1)}, u32[]{:S(2)}, u32[]{:S(2)}) collective-permute-start(bf16[144,256]{1,0:T(8,128)(2,1)S(1)} %get-tuple-element.65.refs_0_), channel_id=1, source_target_pairs={{0,16},{1,5},{4,20},{5,1},{8,24},{9,13},{12,28},{13,9},{16,0},{17,... | collective-permute-start | bytes 221192 | tf_op jit(solution)/shard_map/ppermute | solution.py:380
  37.2 3.2 %collective-permute-done.10.a_ref.refs_4_ = bf16[64,256]{1,0:T(8,128)(2,1)S(1)} collective-permute-done((bf16[64,256]{1,0:T(8,128)(2,1)S(1)}, bf16[64,256]{1,0:T(8,128)(2,1)S(1)}, u32[]{:S(2)}, u32[]{:S(2)}) %collective-permute-start.10) | collective-permute-done | bytes 32800 | tf_op jit(solution)/shard_map/ppermute | solution.py:341
  40.5 1.2 %collective-permute-done.11.b_ref.refs_5_ = bf16[64,256]{1,0:T(8,128)(2,1)S(1)} collective-permute-done((bf16[64,256]{1,0:T(8,128)(2,1)S(1)}, bf16[64,256]{1,0:T(8,128)(2,1)S(1)}, u32[]{:S(2)}, u32[]{:S(2)}) %collective-permute-start.11) | collective-permute-done | bytes 32800 | tf_op jit(solution)/shard_map/ppermute | solution.py:355
  41.7 1.1 %collective-permute-start.17 = (bf16[144,256]{1,0:T(8,128)(2,1)S(1)}, bf16[144,256]{1,0:T(8,128)(2,1)S(1)}, u32[]{:S(2)}, u32[]{:S(2)}) collective-permute-start(bf16[144,256]{1,0:T(8,128)(2,1)S(1)} %shard_map.76.c_ref), channel_id=1, source_target_pairs={{0,16},{1,3},{2,18},{3,1},{16,0},{17,19},{18,2},{19,17},{4,20},{5,... | collective-permute-start | bytes 221192 | tf_op jit(solution)/shard_map/ppermute | solution.py:380
  42.8 1.2 %shard_map.74 = (bf16[64,8,128]{2,1,0:T(8,128)(2,1)}, f32[8,128]{1,0:T(8,128)S(1)}) custom-call(bf16[8,64,256]{2,1,0:T(8,128)(2,1)S(1)} %get-tuple-element.57.g_ref, bf16[64,256]{1,0:T(8,128)(2,1)S(1)} %collective-permute-done.10.a_ref.refs_4_, bf16[64,256]{1,0:T(8,128)(2,1)S(1)} %collective-permute-done.11.b_ref.refs_5_, ...), custom_call_target="tpu_custom_call" | custom-call | flops 150994944 | bytes 536576 | tf_op jit(solution)/shard_map/pallas_call | solution.py:30
  44.0 2.1 %collective-permute-done.17.d_ref = bf16[144,256]{1,0:T(8,128)(2,1)S(1)} collective-permute-done((bf16[144,256]{1,0:T(8,128)(2,1)S(1)}, bf16[144,256]{1,0:T(8,128)(2,1)S(1)}, u32[]{:S(2)}, u32[]{:S(2)}) %collective-permute-start.17) | collective-permute-done | bytes 73760 | tf_op jit(solution)/shard_map/ppermute | solution.py:380
  46.3 1.7 %collective-permute-done.18.other_ref = bf16[720,256]{1,0:T(8,128)(2,1)S(1)} collective-permute-done((bf16[720,256]{1,0:T(8,128)(2,1)S(1)}, bf16[720,256]{1,0:T(8,128)(2,1)S(1)}, u32[]{:S(2)}, u32[]{:S(2)}) %collective-permute-start.18) | collective-permute-done | bytes 368672 | tf_op jit(solution)/shard_map/ppermute | solution.py:341
  48.0 1.2 %shard_map.78 = (f32[3,192,64]{2,1,0:T(8,128)}, f32[1152,256]{1,0:T(8,128)}) custom-call(bf16[720,256]{1,0:T(8,128)(2,1)S(1)} %shard_map.77.mine_ref, bf16[720,256]{1,0:T(8,128)(2,1)S(1)} %collective-permute-done.18.other_ref), custom_call_target="tpu_custom_call" | custom-call | flops 1 | bytes 2064384 | tf_op jit(solution)/shard_map/pallas_call | solution.py:30
  (39 shorter events, 9.0 us)
Async XLA Ops:
  0.6 20.8 %copy-start = (bf16[128,3,3,256]{3,0,2,1:T(8,128)(2,1)S(1)}, bf16[128,3,3,256]{3,0,2,1:T(8,128)(2,1)}, u32[]{:S(2)}) copy-start(bf16[128,3,3,256]{3,0,2,1:T(8,128)(2,1)} %param.6) | copy-start | bytes 1769476
  1.7 5.7 %collective-permute-start.1 = (bf16[64,128]{1,0:T(8,128)(2,1)S(1)}, bf16[64,128]{1,0:T(8,128)(2,1)S(1)}, u32[]{:S(2)}, u32[]{:S(2)}) collective-permute-start(bf16[64,128]{1,0:T(8,128)(2,1)S(1)} %get-tuple-element.69), channel_id=1, source_target_pairs={{0,1},{1,0},{4,8},{5,9},{8,4},{9,5},{12,13},{13,12},{2,3},{3,2},{6... | collective-permute-start | bytes 49160 | tf_op jit(solution)/shard_map/ppermute | solution.py:355
  2.2 5.9 %collective-permute-start = (bf16[64,128]{1,0:T(8,128)(2,1)S(1)}, bf16[64,128]{1,0:T(8,128)(2,1)S(1)}, u32[]{:S(2)}, u32[]{:S(2)}) collective-permute-start(bf16[64,128]{1,0:T(8,128)(2,1)S(1)} %get-tuple-element.70), channel_id=1, source_target_pairs={{0,4},{4,0},{8,12},{12,8},{1,5},{5,1},{9,13},{13,9},{2,6},{6,2},{1... | collective-permute-start | bytes 49160 | tf_op jit(solution)/shard_map/ppermute | solution.py:341
  8.1 4.0 %collective-permute-start.2 = (bf16[144,128]{1,0:T(8,128)(2,1)S(1)}, bf16[144,128]{1,0:T(8,128)(2,1)S(1)}, u32[]{:S(2)}, u32[]{:S(2)}) collective-permute-start(bf16[144,128]{1,0:T(8,128)(2,1)S(1)} %get-tuple-element.38), channel_id=1, source_target_pairs={{0,16},{1,2},{2,1},{3,19},{16,0},{17,18},{18,17},{19,3},{4,20},{5,... | collective-permute-start | bytes 110600 | tf_op jit(solution)/shard_map/ppermute | solution.py:365
  9.7 2.4 %collective-permute-start.3 = (bf16[144,128]{1,0:T(8,128)(2,1)S(1)}, bf16[144,128]{1,0:T(8,128)(2,1)S(1)}, u32[]{:S(2)}, u32[]{:S(2)}) collective-permute-start(bf16[144,128]{1,0:T(8,128)(2,1)S(1)} %get-tuple-element.39), channel_id=1, source_target_pairs={{0,1},{1,0},{2,3},{3,2},{4,5},{5,4},{6,7},{7,6},{8,9},{9,8},{10,11... | collective-permute-start | bytes 110600 | tf_op jit(solution)/shard_map/ppermute | solution.py:341
  9.8 0.9 %copy-start.1 = (bf16[64,3,3,64]{3,0,2,1:T(8,128)(2,1)S(1)}, bf16[64,3,3,64]{3,0,2,1:T(8,128)(2,1)}, u32[]{:S(2)}) copy-start(bf16[64,3,3,64]{3,0,2,1:T(8,128)(2,1)} %param.5) | copy-start | bytes 221188
  13.0 6.0 %collective-permute-start.6 = (bf16[2,40,256]{2,1,0:T(8,128)(2,1)S(1)}, bf16[2,40,256]{2,1,0:T(8,128)(2,1)S(1)}, u32[]{:S(2)}, u32[]{:S(2)}) collective-permute-start(bf16[2,40,256]{2,1,0:T(8,128)(2,1)S(1)} %get-tuple-element.45.refs_0_), channel_id=1, source_target_pairs={{0,8},{4,12},{8,0},{12,4},{1,9},{5,13},{9,1},{13,5},{2,10},{6,14},... | collective-permute-start | bytes 122888 | tf_op jit(solution)/shard_map/ppermute | solution.py:369
  15.0 5.8 %collective-permute-start.5 = (bf16[2,40,256]{2,1,0:T(8,128)(2,1)S(1)}, bf16[2,40,256]{2,1,0:T(8,128)(2,1)S(1)}, u32[]{:S(2)}, u32[]{:S(2)}) collective-permute-start(bf16[2,40,256]{2,1,0:T(8,128)(2,1)S(1)} %get-tuple-element.45.refs_0_), channel_id=1, source_target_pairs={{0,12},{4,8},{8,4},{12,0},{1,13},{5,9},{9,5},{13,1},{2,14},{6,10},... | collective-permute-start | bytes 122888 | tf_op jit(solution)/shard_map/ppermute | solution.py:369
  17.5 4.0 %collective-permute-start.4 = (bf16[2,40,256]{2,1,0:T(8,128)(2,1)S(1)}, bf16[2,40,256]{2,1,0:T(8,128)(2,1)S(1)}, u32[]{:S(2)}, u32[]{:S(2)}) collective-permute-start(bf16[2,40,256]{2,1,0:T(8,128)(2,1)S(1)} %get-tuple-element.45.refs_0_), channel_id=1, source_target_pairs={{0,4},{4,0},{8,12},{12,8},{1,5},{5,1},{9,13},{13,9},{2,6},{6,2},{1... | collective-permute-start | bytes 122888 | tf_op jit(solution)/shard_map/ppermute | solution.py:369
  22.5 5.2 %collective-permute-start.7 = (bf16[72,256]{1,0:T(8,128)(2,1)S(1)}, bf16[72,256]{1,0:T(8,128)(2,1)S(1)}, u32[]{:S(2)}, u32[]{:S(2)}) collective-permute-start(bf16[72,256]{1,0:T(8,128)(2,1)S(1)} %get-tuple-element.47), channel_id=1, source_target_pairs={{0,8},{4,12},{8,0},{12,4},{1,9},{5,13},{9,1},{13,5},{2,10},{6,14},... | collective-permute-start | bytes 110600 | tf_op jit(solution)/shard_map/ppermute | solution.py:369
  22.9 5.8 %collective-permute-start.8 = (bf16[72,256]{1,0:T(8,128)(2,1)S(1)}, bf16[72,256]{1,0:T(8,128)(2,1)S(1)}, u32[]{:S(2)}, u32[]{:S(2)}) collective-permute-start(bf16[72,256]{1,0:T(8,128)(2,1)S(1)} %get-tuple-element.48), channel_id=1, source_target_pairs={{0,12},{4,8},{8,4},{12,0},{1,13},{5,9},{9,5},{13,1},{2,14},{6,10},... | collective-permute-start | bytes 110600 | tf_op jit(solution)/shard_map/ppermute | solution.py:369
  25.3 4.0 %collective-permute-start.9 = (bf16[72,256]{1,0:T(8,128)(2,1)S(1)}, bf16[72,256]{1,0:T(8,128)(2,1)S(1)}, u32[]{:S(2)}, u32[]{:S(2)}) collective-permute-start(bf16[72,256]{1,0:T(8,128)(2,1)S(1)} %get-tuple-element.49), channel_id=1, source_target_pairs={{0,4},{4,0},{8,12},{12,8},{1,5},{5,1},{9,13},{13,9},{2,6},{6,2},{1... | collective-permute-start | bytes 110600 | tf_op jit(solution)/shard_map/ppermute | solution.py:369
  30.2 1.8 %collective-permute-start.12 = (bf16[720,256]{1,0:T(8,128)(2,1)S(1)}, bf16[720,256]{1,0:T(8,128)(2,1)S(1)}, u32[]{:S(2)}, u32[]{:S(2)}) collective-permute-start(bf16[720,256]{1,0:T(8,128)(2,1)S(1)} %get-tuple-element.63), channel_id=1, source_target_pairs={{0,1},{1,0},{2,3},{3,2},{4,5},{5,4},{6,7},{7,6},{8,9},{9,8},{10,11... | collective-permute-start | bytes 1105928 | tf_op jit(solution)/shard_map/ppermute | solution.py:341
  32.0 14.1 %collective-permute-start.13 = (bf16[576,256]{1,0:T(8,128)(2,1)S(1)}, bf16[576,256]{1,0:T(8,128)(2,1)S(1)}, u32[]{:S(2)}, u32[]{:S(2)}) collective-permute-start(bf16[576,256]{1,0:T(8,128)(2,1)S(1)} %get-tuple-element.64.a_ref), channel_id=1, source_target_pairs={{0,2},{2,0},{1,3},{3,1},{4,6},{6,4},{5,7},{7,5},{8,10},{10,8},{9,1... | collective-permute-start | bytes 884744 | tf_op jit(solution)/shard_map/ppermute | solution.py:369
  33.0 8.7 %collective-permute-start.16 = (bf16[144,256]{1,0:T(8,128)(2,1)S(1)}, bf16[144,256]{1,0:T(8,128)(2,1)S(1)}, u32[]{:S(2)}, u32[]{:S(2)}) collective-permute-start(bf16[144,256]{1,0:T(8,128)(2,1)S(1)} %get-tuple-element.65.refs_0_), channel_id=1, source_target_pairs={{0,16},{1,9},{4,20},{5,13},{8,24},{9,1},{12,28},{13,5},{16,0},{17,... | collective-permute-start | bytes 221192 | tf_op jit(solution)/shard_map/ppermute | solution.py:380
  34.5 7.2 %collective-permute-start.15 = (bf16[144,256]{1,0:T(8,128)(2,1)S(1)}, bf16[144,256]{1,0:T(8,128)(2,1)S(1)}, u32[]{:S(2)}, u32[]{:S(2)}) collective-permute-start(bf16[144,256]{1,0:T(8,128)(2,1)S(1)} %get-tuple-element.65.refs_0_), channel_id=1, source_target_pairs={{0,16},{1,13},{4,20},{5,9},{8,24},{9,5},{12,28},{13,1},{16,0},{17,... | collective-permute-start | bytes 221192 | tf_op jit(solution)/shard_map/ppermute | solution.py:380
  35.0 6.7 %collective-permute-start.14 = (bf16[144,256]{1,0:T(8,128)(2,1)S(1)}, bf16[144,256]{1,0:T(8,128)(2,1)S(1)}, u32[]{:S(2)}, u32[]{:S(2)}) collective-permute-start(bf16[144,256]{1,0:T(8,128)(2,1)S(1)} %get-tuple-element.65.refs_0_), channel_id=1, source_target_pairs={{0,16},{1,5},{4,20},{5,1},{8,24},{9,13},{12,28},{13,9},{16,0},{17,... | collective-permute-start | bytes 221192 | tf_op jit(solution)/shard_map/ppermute | solution.py:380
  36.5 3.9 %collective-permute-start.10 = (bf16[64,256]{1,0:T(8,128)(2,1)S(1)}, bf16[64,256]{1,0:T(8,128)(2,1)S(1)}, u32[]{:S(2)}, u32[]{:S(2)}) collective-permute-start(bf16[64,256]{1,0:T(8,128)(2,1)S(1)} %get-tuple-element.58), channel_id=1, source_target_pairs={{0,4},{4,0},{8,12},{12,8},{1,5},{5,1},{9,13},{13,9},{2,6},{6,2},{1... | collective-permute-start | bytes 98312 | tf_op jit(solution)/shard_map/ppermute | solution.py:341
  40.5 1.2 %collective-permute-start.11 = (bf16[64,256]{1,0:T(8,128)(2,1)S(1)}, bf16[64,256]{1,0:T(8,128)(2,1)S(1)}, u32[]{:S(2)}, u32[]{:S(2)}) collective-permute-start(bf16[64,256]{1,0:T(8,128)(2,1)S(1)} %get-tuple-element.59), channel_id=1, source_target_pairs={{0,1},{1,0},{4,8},{5,9},{8,4},{9,5},{12,13},{13,12},{2,3},{3,2},{6... | collective-permute-start | bytes 98312 | tf_op jit(solution)/shard_map/ppermute | solution.py:355
  41.7 4.4 %collective-permute-start.17 = (bf16[144,256]{1,0:T(8,128)(2,1)S(1)}, bf16[144,256]{1,0:T(8,128)(2,1)S(1)}, u32[]{:S(2)}, u32[]{:S(2)}) collective-permute-start(bf16[144,256]{1,0:T(8,128)(2,1)S(1)} %shard_map.76.c_ref), channel_id=1, source_target_pairs={{0,16},{1,3},{2,18},{3,1},{16,0},{17,19},{18,2},{19,17},{4,20},{5,... | collective-permute-start | bytes 221192 | tf_op jit(solution)/shard_map/ppermute | solution.py:380
  46.2 1.8 %collective-permute-start.18 = (bf16[720,256]{1,0:T(8,128)(2,1)S(1)}, bf16[720,256]{1,0:T(8,128)(2,1)S(1)}, u32[]{:S(2)}, u32[]{:S(2)}) collective-permute-start(bf16[720,256]{1,0:T(8,128)(2,1)S(1)} %shard_map.77.mine_ref), channel_id=1, source_target_pairs={{0,1},{1,0},{2,3},{3,2},{4,5},{5,4},{6,7},{7,6},{8,9},{9,8},{10,11... | collective-permute-start | bytes 1105928 | tf_op jit(solution)/shard_map/ppermute | solution.py:341

commit v17 on v16

--- a/solution.py
+++ b/solution.py
@@ -252,19 +252,21 @@
     one_ref[...] = total[half:]
 
 
-def add_joined(a_ref, b_ref, c_ref, d_ref, _, out_ref):
+def add_joined(a_ref, b_ref, c_ref, d_ref, _, __, out_ref):
     half = a_ref.shape[0]
     out_ref[:half] = (a_ref[...].astype(F32) + b_ref[...].astype(F32)).astype(BF16)
     out_ref[half:] = (c_ref[...].astype(F32) + d_ref[...].astype(F32)).astype(BF16)
 
 
 def sum_rows(*refs):
-    *refs, _, _, out_ref = refs
+    *refs, a_ref, b_ref, out_ref, passed_a_ref, passed_b_ref = refs
     terms = dict(zip(row_order(len(refs), near_first=True), (ref[...].astype(F32) for ref in refs)))
     terms = [terms[k] for k in range(len(refs))]
     while len(terms) > 1:
         terms = [a + b for a, b in zip(terms[::2], terms[1::2])]
     out_ref[...] = terms[0].astype(BF16)
+    passed_a_ref[...] = a_ref[...]
+    passed_b_ref[...] = b_ref[...]
 
 
 def grad_pre_one(*refs, bands):
@@ -315,7 +317,7 @@
     out_ref[...] = jnp.swapaxes(jnp.stack(rows, 0), 0, 1).astype(BF16)
 
 
-def finish(mine_ref, other_ref, one_hbm, two_hbm, one_ref, two_ref, flat_ref, sems, *, scales):
+def finish(mine_ref, other_ref, _, one_hbm, two_hbm, one_ref, two_ref, flat_ref, sems, *, scales):
     pair, half = lax.axis_index("pair"), mine_ref.shape[0] - ROWS_ONE
     copies = []
     for n, (ref, place) in enumerate(((mine_ref, pair), (other_ref, 1 - pair))):
@@ -497,8 +499,10 @@
     columns = lax.axis_size("col")
     two, two_more = sum_but_last(two, "col", columns)
     ones = [one] + [last_core_swap(one, "row", k) for k in row_order(bands, near_first=True)[1:]]
+    one, up_a, up_b = whole_call(
+        sum_rows, [shaped(a.shape) for a in (one, up_a, up_b)], ones + [up_a, up_b], 0
+    )
     up_a, up_b = even_swap(up_a, "row", bands), odd_row_swap(up_b)
-    (one,) = whole_call(sum_rows, [shaped(one.shape)], ones + [up_a, up_b], 0, after=2)
     input_grad, done = whole_call(
         functools.partial(layer_one_back, bands=bands),
         [shaped(features_in.shape), shaped((8, 128), F32)],
@@ -512,16 +516,16 @@
     (mine,) = whole_call(
         add_joined,
         [shaped((half + ROWS_ONE, 256))],
-        [two, two_more, one, last_core_swap(one, "col", step), done],
+        [two, two_more, one, last_core_swap(one, "col", step), up_a, up_b],
         0,
-        after=1,
+        after=2,
     )
     grad_one, grad_two = whole_call(
         functools.partial(
             finish, scales=(1.0 / math.sqrt(height * width), 1.0 / math.sqrt(pooled_rows * total))
         ),
         [shaped((3, 3 * channels, channels), F32), shaped((2 * half, 256), F32)],
-        [mine, even_swap(mine, "pair", 2)],
+        [mine, even_swap(mine, "pair", 2), done],
         1,
         scratch=[
             pltpu.VMEM((3, 3 * channels, channels), F32),
@@ -529,6 +533,7 @@
             pltpu.VMEM((ROWS_ONE, 256), F32),
             pltpu.SemaphoreType.DMA((3,)),
         ],
+        after=1,
         out_spaces=[pl.ANY] * 2,
     )
     grad_two = jnp.transpose(grad_two.reshape(3, 3, filters, 4 * channels), (2, 0, 1, 3))

time: 50.1 us -> 48.2 us (0.962); the launches traced: 49.2 us -> 48 us
  waiting for transfers between devices: 18.4 us -> 17 us
    ppermute x2, waiting for transfers between devices: 1.21 us -> 0.01 us  [odd_row_swap(): return lax.ppermute(values, ('row', 'pair'), steps)]
    ppermute x5, waiting for transfers between devices: 7.28 us -> 6.1 us  [even_swap(): return lax.ppermute(values, axis, [(n, n ^ 1) for n in range(count)])]
    ppermute x4, waiting for transfers between devices: 2.13 us -> 3.12 us  [last_core_swap(): return lax.ppermute(values, ('grp', axis, 'pair'), steps)]
  transfers between devices with their start and end apart: 19 -> 19, of which waited for: 13 -> 14; matrix products, arithmetic and copies ran while one was open for 2% -> 2% of each run, Pallas kernels for 4% -> 5%
where the time goes in v17:
time: 48.2 us; the launch traced here: 48 us
  starting transfers between devices  21 us (44%)
  waiting for transfers between devices  17 us (35%)
  Pallas kernels  6.38 us (13%)
  local copies, waits for them, and re-layouts  2.77 us (6%)
  between operations  0.79 us (2%)
    ppermute x7, starting transfers between devices, xor_swap(): return lax.ppermute(values, axis, [(n, n ^ k) for n in range(count)])  8.99 us
    ppermute x7, waiting for transfers between devices, xor_swap(): return lax.ppermute(values, axis, [(n, n ^ k) for n in range(count)])  6.58 us
    pallas_call x12, Pallas kernels, whole_call(): pl.pallas_call(body, out_shape=outs, in_specs=specs, out_specs=[pl.BlockS...  6.38 us
    ppermute x5, waiting for transfers between devices, even_swap(): return lax.ppermute(values, axis, [(n, n ^ 1) for n in range(count)])  6.1 us
    ppermute x5, starting transfers between devices, even_swap(): return lax.ppermute(values, axis, [(n, n ^ 1) for n in range(count)])  5.07 us
    ppermute x4, starting transfers between devices, last_core_swap(): return lax.ppermute(values, ('grp', axis, 'pair'), steps)  4.85 us
    ppermute x4, waiting for transfers between devices, last_core_swap(): return lax.ppermute(values, ('grp', axis, 'pair'), steps)  3.12 us
    unnamed x6, local copies, waits for them, and re-layouts  2.75 us
  transfers between devices with their start and end apart: 19, of which 14 were waited for; matrix products, arithmetic and copies ran while one was open for 2% of the time, Pallas kernels for 5%

profile of v17, /device:TPU:0, one launch (start us, length us, event | category | flops | bytes accessed | tf_op | source)
XLA Modules:
  0.0 48.0 jit_solution(13218203896279648084)
XLA Ops:
  0.7 1.0 %copy.19 = bf16[64,8,128]{2,0,1:T(8,128)(2,1)S(1)} copy(bf16[64,8,128]{2,1,0:T(8,128)(2,1)} %param.4) | data formatting | bytes 262144 | tf_op args[0]
  2.2 4.1 %collective-permute-start = (bf16[64,128]{1,0:T(8,128)(2,1)S(1)}, bf16[64,128]{1,0:T(8,128)(2,1)S(1)}, u32[]{:S(2)}, u32[]{:S(2)}) collective-permute-start(bf16[64,128]{1,0:T(8,128)(2,1)S(1)} %get-tuple-element.76), channel_id=1, source_target_pairs={{0,4},{4,0},{8,12},{12,8},{1,5},{5,1},{9,13},{13,9},{2,6},{6,2},{1... | collective-permute-start | bytes 49160 | tf_op jit(solution)/shard_map/ppermute | solution.py:343
  8.1 1.6 %collective-permute-start.2 = (bf16[144,128]{1,0:T(8,128)(2,1)S(1)}, bf16[144,128]{1,0:T(8,128)(2,1)S(1)}, u32[]{:S(2)}, u32[]{:S(2)}) collective-permute-start(bf16[144,128]{1,0:T(8,128)(2,1)S(1)} %get-tuple-element.41), channel_id=1, source_target_pairs={{0,16},{1,2},{2,1},{3,19},{16,0},{17,18},{18,17},{19,3},{4,20},{5,... | collective-permute-start | bytes 110600 | tf_op jit(solution)/shard_map/ppermute | solution.py:367
  9.8 0.9 %copy-done.1 = bf16[64,3,3,64]{3,0,2,1:T(8,128)(2,1)S(1)} copy-done((bf16[64,3,3,64]{3,0,2,1:T(8,128)(2,1)S(1)}, bf16[64,3,3,64]{3,0,2,1:T(8,128)(2,1)}, u32[]{:S(2)}) %copy-start.1) | copy-done | bytes 73752
  10.9 1.2 %collective-permute-done.2.b_ref = bf16[144,128]{1,0:T(8,128)(2,1)S(1)} collective-permute-done((bf16[144,128]{1,0:T(8,128)(2,1)S(1)}, bf16[144,128]{1,0:T(8,128)(2,1)S(1)}, u32[]{:S(2)}, u32[]{:S(2)}) %collective-permute-start.2) | collective-permute-done | bytes 36896 | tf_op jit(solution)/shard_map/ppermute | solution.py:367
  12.1 0.9 %shard_map.70 = (bf16[2,40,256]{2,1,0:T(8,128)(2,1)S(1)}, bf16[8,64,256]{2,1,0:T(8,128)(2,1)S(1)}, bf16[10,64,256]{2,1,0:T(8,128)(2,1)S(1)}) custom-call(bf16[8,64,128]{2,1,0:T(8,128)(2,1)S(1)} %bitcast.34, bf16[64,128]{1,0:T(8,128)(2,1)S(1)} %get-tuple-element.43.above_ref, bf16[64,128]{1,0:T(8,128)(2,1)S(1)} %get-tuple-element.44.below_ref, ...), custom_call_target="tpu_custom_call" | custom-call | flops 150994944 | bytes 1122304 | tf_op jit(solution)/shard_map/pallas_call | solution.py:30
  13.0 2.0 %collective-permute-start.6 = (bf16[2,40,256]{2,1,0:T(8,128)(2,1)S(1)}, bf16[2,40,256]{2,1,0:T(8,128)(2,1)S(1)}, u32[]{:S(2)}, u32[]{:S(2)}) collective-permute-start(bf16[2,40,256]{2,1,0:T(8,128)(2,1)S(1)} %get-tuple-element.48.refs_0_), channel_id=1, source_target_pairs={{0,8},{4,12},{8,0},{12,4},{1,9},{5,13},{9,1},{13,5},{2,10},{6,14},... | collective-permute-start | bytes 122888 | tf_op jit(solution)/shard_map/ppermute | solution.py:371
  15.0 2.5 %collective-permute-start.5 = (bf16[2,40,256]{2,1,0:T(8,128)(2,1)S(1)}, bf16[2,40,256]{2,1,0:T(8,128)(2,1)S(1)}, u32[]{:S(2)}, u32[]{:S(2)}) collective-permute-start(bf16[2,40,256]{2,1,0:T(8,128)(2,1)S(1)} %get-tuple-element.48.refs_0_), channel_id=1, source_target_pairs={{0,12},{4,8},{8,4},{12,0},{1,13},{5,9},{9,5},{13,1},{2,14},{6,10},... | collective-permute-start | bytes 122888 | tf_op jit(solution)/shard_map/ppermute | solution.py:371
  17.6 1.4 %collective-permute-done.6.refs_3_ = bf16[2,40,256]{2,1,0:T(8,128)(2,1)S(1)} collective-permute-done((bf16[2,40,256]{2,1,0:T(8,128)(2,1)S(1)}, bf16[2,40,256]{2,1,0:T(8,128)(2,1)S(1)}, u32[]{:S(2)}, u32[]{:S(2)}) %collective-permute-start.6) | collective-permute-done | bytes 40992 | tf_op jit(solution)/shard_map/ppermute | solution.py:371
  19.0 1.8 %collective-permute-done.5.refs_2_ = bf16[2,40,256]{2,1,0:T(8,128)(2,1)S(1)} collective-permute-done((bf16[2,40,256]{2,1,0:T(8,128)(2,1)S(1)}, bf16[2,40,256]{2,1,0:T(8,128)(2,1)S(1)}, u32[]{:S(2)}, u32[]{:S(2)}) %collective-permute-start.5) | collective-permute-done | bytes 40992 | tf_op jit(solution)/shard_map/ppermute | solution.py:371
  21.5 1.0 %shard_map.71 = (bf16[72,256]{1,0:T(8,128)(2,1)S(1)}, bf16[72,256]{1,0:T(8,128)(2,1)S(1)}, bf16[72,256]{1,0:T(8,128)(2,1)S(1)}, bf16[72,256]{1,0:T(8,128)(2,1)S(...) custom-call(bf16[8,48,128]{2,1,0:T(8,128)(2,1)S(1)} %fusion.6.og_ref, ...), custom_call_target="tpu_custom_call" | custom-call | flops 452984832 | bytes 1368064 | tf_op jit(solution)/shard_map/pallas_call | solution.py:30
  22.9 2.5 %collective-permute-start.8 = (bf16[72,256]{1,0:T(8,128)(2,1)S(1)}, bf16[72,256]{1,0:T(8,128)(2,1)S(1)}, u32[]{:S(2)}, u32[]{:S(2)}) collective-permute-start(bf16[72,256]{1,0:T(8,128)(2,1)S(1)} %get-tuple-element.51), channel_id=1, source_target_pairs={{0,12},{4,8},{8,4},{12,0},{1,13},{5,9},{9,5},{13,1},{2,14},{6,10},... | collective-permute-start | bytes 110600 | tf_op jit(solution)/shard_map/ppermute | solution.py:371
  26.6 1.0 %collective-permute-done.7.refs_1_ = bf16[72,256]{1,0:T(8,128)(2,1)S(1)} collective-permute-done((bf16[72,256]{1,0:T(8,128)(2,1)S(1)}, bf16[72,256]{1,0:T(8,128)(2,1)S(1)}, u32[]{:S(2)}, u32[]{:S(2)}) %collective-permute-start.7) | collective-permute-done | bytes 36896 | tf_op jit(solution)/shard_map/ppermute | solution.py:371
  27.7 1.0 %collective-permute-done.8.refs_2_ = bf16[72,256]{1,0:T(8,128)(2,1)S(1)} collective-permute-done((bf16[72,256]{1,0:T(8,128)(2,1)S(1)}, bf16[72,256]{1,0:T(8,128)(2,1)S(1)}, u32[]{:S(2)}, u32[]{:S(2)}) %collective-permute-start.8) | collective-permute-done | bytes 36896 | tf_op jit(solution)/shard_map/ppermute | solution.py:371
  29.3 0.9 %shard_map.73 = (bf16[8,64,256]{2,1,0:T(8,128)(2,1)S(1)}, bf16[64,256]{1,0:T(8,128)(2,1)S(1)}, bf16[64,256]{1,0:T(8,128)(2,1)S(1)}, bf16[720,256]{1,0:T(8,128)(2,1)S(1)}, bf16[720,256]{1,0:T(8,128)(2,1)S(1)}) custom-call(bf16[72,256]{1,0:T(8,128)(2,1)S(1)} %get-tuple-element.49.refs_0_, bf16[72,256]{1,0:T(8,128)(2,1)S(1)} %collective-permute-done.7.refs_1_, ...), custom_call_target="tpu_custom_call" | custom-call | flops 150994944 | bytes 2572288 | tf_op jit(solution)/shard_map/pallas_call | solution.py:30
  30.2 1.7 %collective-permute-done.10.b_ref = bf16[720,256]{1,0:T(8,128)(2,1)S(1)} collective-permute-done((bf16[720,256]{1,0:T(8,128)(2,1)S(1)}, bf16[720,256]{1,0:T(8,128)(2,1)S(1)}, u32[]{:S(2)}, u32[]{:S(2)}) %collective-permute-start.10) | collective-permute-done | bytes 368672 | tf_op jit(solution)/shard_map/ppermute | solution.py:343
  32.0 1.0 %collective-permute-start.16 = (bf16[576,256]{1,0:T(8,128)(2,1)S(1)}, bf16[576,256]{1,0:T(8,128)(2,1)S(1)}, u32[]{:S(2)}, u32[]{:S(2)}) collective-permute-start(bf16[576,256]{1,0:T(8,128)(2,1)S(1)} %get-tuple-element.70.a_ref), channel_id=1, source_target_pairs={{0,2},{2,0},{1,3},{3,1},{4,6},{6,4},{5,7},{7,5},{8,10},{10,8},{9,1... | collective-permute-start | bytes 884744 | tf_op jit(solution)/shard_map/ppermute | solution.py:371
  33.0 1.5 %collective-permute-start.13 = (bf16[144,256]{1,0:T(8,128)(2,1)S(1)}, bf16[144,256]{1,0:T(8,128)(2,1)S(1)}, u32[]{:S(2)}, u32[]{:S(2)}) collective-permute-start(bf16[144,256]{1,0:T(8,128)(2,1)S(1)} %get-tuple-element.63.refs_0_), channel_id=1, source_target_pairs={{0,16},{1,9},{4,20},{5,13},{8,24},{9,1},{12,28},{13,5},{16,0},{17,... | collective-permute-start | bytes 221192 | tf_op jit(solution)/shard_map/ppermute | solution.py:382
  35.0 1.5 %collective-permute-start.11 = (bf16[144,256]{1,0:T(8,128)(2,1)S(1)}, bf16[144,256]{1,0:T(8,128)(2,1)S(1)}, u32[]{:S(2)}, u32[]{:S(2)}) collective-permute-start(bf16[144,256]{1,0:T(8,128)(2,1)S(1)} %get-tuple-element.63.refs_0_), channel_id=1, source_target_pairs={{0,16},{1,5},{4,20},{5,1},{8,24},{9,13},{12,28},{13,9},{16,0},{17,... | collective-permute-start | bytes 221192 | tf_op jit(solution)/shard_map/ppermute | solution.py:382
  37.3 1.5 %collective-permute-done.12.refs_2_ = bf16[144,256]{1,0:T(8,128)(2,1)S(1)} collective-permute-done((bf16[144,256]{1,0:T(8,128)(2,1)S(1)}, bf16[144,256]{1,0:T(8,128)(2,1)S(1)}, u32[]{:S(2)}, u32[]{:S(2)}) %collective-permute-start.12) | collective-permute-done | bytes 73760 | tf_op jit(solution)/shard_map/ppermute | solution.py:382
  39.7 1.3 %collective-permute-start.17 = (bf16[144,256]{1,0:T(8,128)(2,1)S(1)}, bf16[144,256]{1,0:T(8,128)(2,1)S(1)}, u32[]{:S(2)}, u32[]{:S(2)}) collective-permute-start(bf16[144,256]{1,0:T(8,128)(2,1)S(1)} %get-tuple-element.71.c_ref), channel_id=1, source_target_pairs={{0,16},{1,3},{2,18},{3,1},{16,0},{17,19},{18,2},{19,17},{4,20},{5,... | collective-permute-start | bytes 221192 | tf_op jit(solution)/shard_map/ppermute | solution.py:382
  41.7 3.2 %collective-permute-done.14.a_ref._ = bf16[64,256]{1,0:T(8,128)(2,1)S(1)} collective-permute-done((bf16[64,256]{1,0:T(8,128)(2,1)S(1)}, bf16[64,256]{1,0:T(8,128)(2,1)S(1)}, u32[]{:S(2)}, u32[]{:S(2)}) %collective-permute-start.14) | collective-permute-done | bytes 32800 | tf_op jit(solution)/shard_map/ppermute | solution.py:343
  45.1 1.2 %shard_map.76 = (bf16[64,8,128]{2,1,0:T(8,128)(2,1)}, f32[8,128]{1,0:T(8,128)S(1)}) custom-call(bf16[8,64,256]{2,1,0:T(8,128)(2,1)S(1)} %get-tuple-element.60.g_ref, bf16[64,256]{1,0:T(8,128)(2,1)S(1)} %collective-permute-done.14.a_ref._, bf16[64,256]{1,0:T(8,128)(2,1)S(1)} %collective-permute-done.15.b_ref.__, bf16[192,192]{1,0:T(8,128)(2,1)S(1)} %get-tuple-element.68.w_ref), custom_call_target="tpu_custom_call" | custom-call | flops 150994944 | bytes 536576 | tf_op jit(solution)/shard_map/pallas_call | solution.py:30
  46.8 1.2 %shard_map.78 = (f32[3,192,64]{2,1,0:T(8,128)}, f32[1152,256]{1,0:T(8,128)}) custom-call(bf16[720,256]{1,0:T(8,128)(2,1)S(1)} %shard_map.77.mine_ref, bf16[720,256]{1,0:T(8,128)(2,1)S(1)} %collective-permute-done.18.other_ref, f32[8,128]{1,0:T(8,128)S(1)} %get-tuple-element.72._), custom_call_target="tpu_custom_call" | custom-call | flops 1 | bytes 2068480 | tf_op jit(solution)/shard_map/pallas_call | solution.py:30
  (39 shorter events, 9.3 us)
Async XLA Ops:
  0.6 20.8 %copy-start = (bf16[128,3,3,256]{3,0,2,1:T(8,128)(2,1)S(1)}, bf16[128,3,3,256]{3,0,2,1:T(8,128)(2,1)}, u32[]{:S(2)}) copy-start(bf16[128,3,3,256]{3,0,2,1:T(8,128)(2,1)} %param.6) | copy-start | bytes 1769476
  1.7 5.7 %collective-permute-start.1 = (bf16[64,128]{1,0:T(8,128)(2,1)S(1)}, bf16[64,128]{1,0:T(8,128)(2,1)S(1)}, u32[]{:S(2)}, u32[]{:S(2)}) collective-permute-start(bf16[64,128]{1,0:T(8,128)(2,1)S(1)} %get-tuple-element.75), channel_id=1, source_target_pairs={{0,1},{1,0},{4,8},{5,9},{8,4},{9,5},{12,13},{13,12},{2,3},{3,2},{6... | collective-permute-start | bytes 49160 | tf_op jit(solution)/shard_map/ppermute | solution.py:357
  2.2 5.9 %collective-permute-start = (bf16[64,128]{1,0:T(8,128)(2,1)S(1)}, bf16[64,128]{1,0:T(8,128)(2,1)S(1)}, u32[]{:S(2)}, u32[]{:S(2)}) collective-permute-start(bf16[64,128]{1,0:T(8,128)(2,1)S(1)} %get-tuple-element.76), channel_id=1, source_target_pairs={{0,4},{4,0},{8,12},{12,8},{1,5},{5,1},{9,13},{13,9},{2,6},{6,2},{1... | collective-permute-start | bytes 49160 | tf_op jit(solution)/shard_map/ppermute | solution.py:343
  8.1 4.0 %collective-permute-start.2 = (bf16[144,128]{1,0:T(8,128)(2,1)S(1)}, bf16[144,128]{1,0:T(8,128)(2,1)S(1)}, u32[]{:S(2)}, u32[]{:S(2)}) collective-permute-start(bf16[144,128]{1,0:T(8,128)(2,1)S(1)} %get-tuple-element.41), channel_id=1, source_target_pairs={{0,16},{1,2},{2,1},{3,19},{16,0},{17,18},{18,17},{19,3},{4,20},{5,... | collective-permute-start | bytes 110600 | tf_op jit(solution)/shard_map/ppermute | solution.py:367
  9.7 2.4 %collective-permute-start.3 = (bf16[144,128]{1,0:T(8,128)(2,1)S(1)}, bf16[144,128]{1,0:T(8,128)(2,1)S(1)}, u32[]{:S(2)}, u32[]{:S(2)}) collective-permute-start(bf16[144,128]{1,0:T(8,128)(2,1)S(1)} %get-tuple-element.42), channel_id=1, source_target_pairs={{0,1},{1,0},{2,3},{3,2},{4,5},{5,4},{6,7},{7,6},{8,9},{9,8},{10,11... | collective-permute-start | bytes 110600 | tf_op jit(solution)/shard_map/ppermute | solution.py:343
  9.8 0.9 %copy-start.1 = (bf16[64,3,3,64]{3,0,2,1:T(8,128)(2,1)S(1)}, bf16[64,3,3,64]{3,0,2,1:T(8,128)(2,1)}, u32[]{:S(2)}) copy-start(bf16[64,3,3,64]{3,0,2,1:T(8,128)(2,1)} %param.5) | copy-start | bytes 221188
  13.0 6.0 %collective-permute-start.6 = (bf16[2,40,256]{2,1,0:T(8,128)(2,1)S(1)}, bf16[2,40,256]{2,1,0:T(8,128)(2,1)S(1)}, u32[]{:S(2)}, u32[]{:S(2)}) collective-permute-start(bf16[2,40,256]{2,1,0:T(8,128)(2,1)S(1)} %get-tuple-element.48.refs_0_), channel_id=1, source_target_pairs={{0,8},{4,12},{8,0},{12,4},{1,9},{5,13},{9,1},{13,5},{2,10},{6,14},... | collective-permute-start | bytes 122888 | tf_op jit(solution)/shard_map/ppermute | solution.py:371
  15.0 5.8 %collective-permute-start.5 = (bf16[2,40,256]{2,1,0:T(8,128)(2,1)S(1)}, bf16[2,40,256]{2,1,0:T(8,128)(2,1)S(1)}, u32[]{:S(2)}, u32[]{:S(2)}) collective-permute-start(bf16[2,40,256]{2,1,0:T(8,128)(2,1)S(1)} %get-tuple-element.48.refs_0_), channel_id=1, source_target_pairs={{0,12},{4,8},{8,4},{12,0},{1,13},{5,9},{9,5},{13,1},{2,14},{6,10},... | collective-permute-start | bytes 122888 | tf_op jit(solution)/shard_map/ppermute | solution.py:371
  17.5 4.0 %collective-permute-start.4 = (bf16[2,40,256]{2,1,0:T(8,128)(2,1)S(1)}, bf16[2,40,256]{2,1,0:T(8,128)(2,1)S(1)}, u32[]{:S(2)}, u32[]{:S(2)}) collective-permute-start(bf16[2,40,256]{2,1,0:T(8,128)(2,1)S(1)} %get-tuple-element.48.refs_0_), channel_id=1, source_target_pairs={{0,4},{4,0},{8,12},{12,8},{1,5},{5,1},{9,13},{13,9},{2,6},{6,2},{1... | collective-permute-start | bytes 122888 | tf_op jit(solution)/shard_map/ppermute | solution.py:371
  22.5 5.2 %collective-permute-start.7 = (bf16[72,256]{1,0:T(8,128)(2,1)S(1)}, bf16[72,256]{1,0:T(8,128)(2,1)S(1)}, u32[]{:S(2)}, u32[]{:S(2)}) collective-permute-start(bf16[72,256]{1,0:T(8,128)(2,1)S(1)} %get-tuple-element.50), channel_id=1, source_target_pairs={{0,8},{4,12},{8,0},{12,4},{1,9},{5,13},{9,1},{13,5},{2,10},{6,14},... | collective-permute-start | bytes 110600 | tf_op jit(solution)/shard_map/ppermute | solution.py:371
  22.9 5.8 %collective-permute-start.8 = (bf16[72,256]{1,0:T(8,128)(2,1)S(1)}, bf16[72,256]{1,0:T(8,128)(2,1)S(1)}, u32[]{:S(2)}, u32[]{:S(2)}) collective-permute-start(bf16[72,256]{1,0:T(8,128)(2,1)S(1)} %get-tuple-element.51), channel_id=1, source_target_pairs={{0,12},{4,8},{8,4},{12,0},{1,13},{5,9},{9,5},{13,1},{2,14},{6,10},... | collective-permute-start | bytes 110600 | tf_op jit(solution)/shard_map/ppermute | solution.py:371
  25.3 4.0 %collective-permute-start.9 = (bf16[72,256]{1,0:T(8,128)(2,1)S(1)}, bf16[72,256]{1,0:T(8,128)(2,1)S(1)}, u32[]{:S(2)}, u32[]{:S(2)}) collective-permute-start(bf16[72,256]{1,0:T(8,128)(2,1)S(1)} %get-tuple-element.52), channel_id=1, source_target_pairs={{0,4},{4,0},{8,12},{12,8},{1,5},{5,1},{9,13},{13,9},{2,6},{6,2},{1... | collective-permute-start | bytes 110600 | tf_op jit(solution)/shard_map/ppermute | solution.py:371
  30.2 1.8 %collective-permute-start.10 = (bf16[720,256]{1,0:T(8,128)(2,1)S(1)}, bf16[720,256]{1,0:T(8,128)(2,1)S(1)}, u32[]{:S(2)}, u32[]{:S(2)}) collective-permute-start(bf16[720,256]{1,0:T(8,128)(2,1)S(1)} %get-tuple-element.62), channel_id=1, source_target_pairs={{0,1},{1,0},{2,3},{3,2},{4,5},{5,4},{6,7},{7,6},{8,9},{9,8},{10,11... | collective-permute-start | bytes 1105928 | tf_op jit(solution)/shard_map/ppermute | solution.py:343
  32.0 12.9 %collective-permute-start.16 = (bf16[576,256]{1,0:T(8,128)(2,1)S(1)}, bf16[576,256]{1,0:T(8,128)(2,1)S(1)}, u32[]{:S(2)}, u32[]{:S(2)}) collective-permute-start(bf16[576,256]{1,0:T(8,128)(2,1)S(1)} %get-tuple-element.70.a_ref), channel_id=1, source_target_pairs={{0,2},{2,0},{1,3},{3,1},{4,6},{6,4},{5,7},{7,5},{8,10},{10,8},{9,1... | collective-permute-start | bytes 884744 | tf_op jit(solution)/shard_map/ppermute | solution.py:371
  33.0 4.4 %collective-permute-start.13 = (bf16[144,256]{1,0:T(8,128)(2,1)S(1)}, bf16[144,256]{1,0:T(8,128)(2,1)S(1)}, u32[]{:S(2)}, u32[]{:S(2)}) collective-permute-start(bf16[144,256]{1,0:T(8,128)(2,1)S(1)} %get-tuple-element.63.refs_0_), channel_id=1, source_target_pairs={{0,16},{1,9},{4,20},{5,13},{8,24},{9,1},{12,28},{13,5},{16,0},{17,... | collective-permute-start | bytes 221192 | tf_op jit(solution)/shard_map/ppermute | solution.py:382
  34.5 4.4 %collective-permute-start.12 = (bf16[144,256]{1,0:T(8,128)(2,1)S(1)}, bf16[144,256]{1,0:T(8,128)(2,1)S(1)}, u32[]{:S(2)}, u32[]{:S(2)}) collective-permute-start(bf16[144,256]{1,0:T(8,128)(2,1)S(1)} %get-tuple-element.63.refs_0_), channel_id=1, source_target_pairs={{0,16},{1,13},{4,20},{5,9},{8,24},{9,5},{12,28},{13,1},{16,0},{17,... | collective-permute-start | bytes 221192 | tf_op jit(solution)/shard_map/ppermute | solution.py:382
  35.0 4.6 %collective-permute-start.11 = (bf16[144,256]{1,0:T(8,128)(2,1)S(1)}, bf16[144,256]{1,0:T(8,128)(2,1)S(1)}, u32[]{:S(2)}, u32[]{:S(2)}) collective-permute-start(bf16[144,256]{1,0:T(8,128)(2,1)S(1)} %get-tuple-element.63.refs_0_), channel_id=1, source_target_pairs={{0,16},{1,5},{4,20},{5,1},{8,24},{9,13},{12,28},{13,9},{16,0},{17,... | collective-permute-start | bytes 221192 | tf_op jit(solution)/shard_map/ppermute | solution.py:382
  39.7 5.2 %collective-permute-start.17 = (bf16[144,256]{1,0:T(8,128)(2,1)S(1)}, bf16[144,256]{1,0:T(8,128)(2,1)S(1)}, u32[]{:S(2)}, u32[]{:S(2)}) collective-permute-start(bf16[144,256]{1,0:T(8,128)(2,1)S(1)} %get-tuple-element.71.c_ref), channel_id=1, source_target_pairs={{0,16},{1,3},{2,18},{3,1},{16,0},{17,19},{18,2},{19,17},{4,20},{5,... | collective-permute-start | bytes 221192 | tf_op jit(solution)/shard_map/ppermute | solution.py:382
  41.0 3.9 %collective-permute-start.14 = (bf16[64,256]{1,0:T(8,128)(2,1)S(1)}, bf16[64,256]{1,0:T(8,128)(2,1)S(1)}, u32[]{:S(2)}, u32[]{:S(2)}) collective-permute-start(bf16[64,256]{1,0:T(8,128)(2,1)S(1)} %get-tuple-element.66), channel_id=1, source_target_pairs={{0,4},{4,0},{8,12},{12,8},{1,5},{5,1},{9,13},{13,9},{2,6},{6,2},{1... | collective-permute-start | bytes 98312 | tf_op jit(solution)/shard_map/ppermute | solution.py:343
  41.7 3.2 %collective-permute-start.15 = (bf16[64,256]{1,0:T(8,128)(2,1)S(1)}, bf16[64,256]{1,0:T(8,128)(2,1)S(1)}, u32[]{:S(2)}, u32[]{:S(2)}) collective-permute-start(bf16[64,256]{1,0:T(8,128)(2,1)S(1)} %get-tuple-element.67), channel_id=1, source_target_pairs={{0,1},{1,0},{4,8},{5,9},{8,4},{9,5},{12,13},{13,12},{2,3},{3,2},{6... | collective-permute-start | bytes 98312 | tf_op jit(solution)/shard_map/ppermute | solution.py:357
  45.0 1.8 %collective-permute-start.18 = (bf16[720,256]{1,0:T(8,128)(2,1)S(1)}, bf16[720,256]{1,0:T(8,128)(2,1)S(1)}, u32[]{:S(2)}, u32[]{:S(2)}) collective-permute-start(bf16[720,256]{1,0:T(8,128)(2,1)S(1)} %shard_map.77.mine_ref), channel_id=1, source_target_pairs={{0,1},{1,0},{2,3},{3,2},{4,5},{5,4},{6,7},{7,6},{8,9},{9,8},{10,11... | collective-permute-start | bytes 1105928 | tf_op jit(solution)/shard_map/ppermute | solution.py:343

commit v18 on v12

--- a/solution.py
+++ b/solution.py
@@ -12,7 +12,7 @@
 F32 = jnp.float32
 COLS = ("col", "pair")
 REACH = 3
-HALF_ONE = 72
+ROWS_ONE = 144
 PITCH = 48
 SENT = 40
 
@@ -252,22 +252,10 @@
     one_ref[...] = total[half:]
 
 
-def sum_rows(*refs):
-    *refs, a_ref, b_ref, out_ref, passed_a_ref, passed_b_ref = refs
-    terms = dict(zip(row_order(len(refs), near_first=True), (ref[...].astype(F32) for ref in refs)))
-    terms = [terms[k] for k in range(len(refs))]
-    while len(terms) > 1:
-        terms = [a + b for a, b in zip(terms[::2], terms[1::2])]
-    out_ref[...] = terms[0].astype(BF16)
-    passed_a_ref[...] = a_ref[...]
-    passed_b_ref[...] = b_ref[...]
-
-
 def grad_pre_one(*refs, bands):
     terms, refs = refs[:bands], refs[bands:]
     slope_ref, wide_ref, pool_ref, order_ref, keep_two_ref, send_two_ref, *refs = refs
     g_ref, a_ref, b_ref, keep_ref, send_ref, part_ref = refs
-    pair = lax.axis_index("pair")
     summed = terms[0][...].astype(F32)
     for k in range(1, bands):
         summed = summed + terms[k][...].astype(F32)
@@ -296,9 +284,9 @@
     part_ref[:96] = jnp.concatenate([acc[:96, :128], acc[96:, :128]], 1)
     part_ref[96:] = jnp.concatenate([acc[48 * q : 48 * q + 48, 128:] for q in range(4)], 1)
     half = keep_two_ref.shape[0]
-    for ref, two_ref, place in ((keep_ref, keep_two_ref, pair), (send_ref, send_two_ref, 1 - pair)):
+    for ref, two_ref in ((keep_ref, keep_two_ref), (send_ref, send_two_ref)):
         ref[:half] = two_ref[...]
-        ref[half:] = part_ref[pl.ds(pl.multiple_of(place * HALF_ONE, 8), HALF_ONE)].astype(BF16)
+        ref[half:] = part_ref[...].astype(BF16)
 
 
 def layer_one_back(g_ref, a_ref, b_ref, w_ref, out_ref, done_ref, *, bands):
@@ -325,10 +313,9 @@
         copy.wait()
 
 
-def finish_one(mine_ref, other_ref, _, out_ref, flat_ref, *, scale):
-    pair = lax.axis_index("pair")
-    for ref, place in ((mine_ref, pair), (other_ref, 1 - pair)):
-        flat_ref[pl.ds(pl.multiple_of(place * HALF_ONE, 8), HALF_ONE)] = ref[...].astype(F32) * scale
+def finish_one(mine_ref, other_ref, out_ref, flat_ref, *, scale):
+    last = lax.axis_index("pair") == lax.axis_size("pair") - 1
+    flat_ref[...] = jnp.where(last, mine_ref[...].astype(F32), other_ref[...].astype(F32)) * scale
     out_ref[0, :96] = flat_ref[:96, :64]
     out_ref[1, :96] = flat_ref[:96, 64:128]
     out_ref[0, 96:] = flat_ref[:96, 128:192]
@@ -367,6 +354,17 @@
 
 def xor_swap(values, axis, count, k):
     return lax.ppermute(values, axis, [(n, n ^ k) for n in range(count)])
+
+
+def last_core_swap(values, axis, k):
+    groups, count, cores = (lax.axis_size(name) for name in ("grp", axis, "pair"))
+    steps = []
+    for g in range(groups):
+        for n in range(count):
+            for p in range(cores):
+                to = (g, n ^ k) if p == cores - 1 else ((g + 1) % groups, n)
+                steps.append(((g * count + n) * cores + p, (to[0] * count + to[1]) * cores + p))
+    return lax.ppermute(values, ("grp", axis, "pair"), steps)
 
 
 def row_order(bands, near_first=False):
@@ -472,27 +470,28 @@
         functools.partial(grad_pre_one, bands=bands),
         [shaped((band_rows, channels, 256))]
         + [shaped((channels, 256))] * 2
-        + [shaped((half + HALF_ONE, 256))] * 2,
+        + [shaped((half + ROWS_ONE, 256))] * 2,
         received + [slope, wide, pool_back, order, keep_two, send_two],
         2 * 8 * 192 * 192 * 256,
         scratch=[pltpu.VMEM((144, 256), F32)],
     )
     two, one = whole_call(
         add_halves,
-        [shaped((half, 256)), shaped((HALF_ONE, 256))],
+        [shaped((half, 256)), shaped((ROWS_ONE, 256))],
         [keep, even_swap(send, "pair", 2)],
         0,
     )
     columns = lax.axis_size("col")
     two, two_more = sum_but_last(two, "col", columns)
-    ones = row_swaps([one] * bands, bands, near_first=True)
-    one, up_a, up_b = whole_call(
-        sum_rows, [shaped(a.shape) for a in (one, up_a, up_b)], ones + [up_a, up_b], 0
-    )
+    up_a, up_b = even_swap(up_a, "row", bands), odd_row_swap(up_b)
+    step = 1
+    while step < bands:
+        one = added(one, last_core_swap(one, "row", step), *((up_a, up_b) if step == 1 else ()))
+        step *= 2
     input_grad, done = whole_call(
         functools.partial(layer_one_back, bands=bands),
         [shaped(features_in.shape), shaped((8, 128), F32)],
-        [g, even_swap(up_a, "row", bands), odd_row_swap(up_b), back_one],
+        [g, up_a, up_b, back_one],
         2 * band_rows * 192 * 192 * 256,
     )
     mine_two = added(two, two_more, one)
@@ -504,14 +503,17 @@
         scratch=[pltpu.VMEM((2, half, 256), F32), pltpu.SemaphoreType.DMA((2,))],
         out_spaces=[pl.ANY, pltpu.VMEM],
     )
-    mine_one = added(*sum_but_last(one, "col", columns), wrote)
+    step = 1
+    while step < columns:
+        last = 2 * step >= columns
+        one = added(one, last_core_swap(one, "col", step), *((wrote, done) if last else ()))
+        step *= 2
     (grad_one,) = whole_call(
         functools.partial(finish_one, scale=1.0 / math.sqrt(height * width)),
         [shaped((3, 3 * channels, channels), F32)],
-        [mine_one, even_swap(mine_one, "pair", 2), done],
+        [one, even_swap(one, "pair", 2)],
         1,
-        scratch=[pltpu.VMEM((144, 256), F32)],
-        after=1,
+        scratch=[pltpu.VMEM((ROWS_ONE, 256), F32)],
     )
     grad_two = jnp.transpose(grad_two.reshape(3, 3, filters, 4 * channels), (2, 0, 1, 3))
     grad_one = jnp.transpose(grad_one.reshape(3, 3, channels, channels), (2, 0, 1, 3))

time: 48.3 us -> 49.9 us (1.033)
  waiting for transfers between devices: 16.8 us -> 20.1 us
  starting transfers between devices: 20.7 us -> 18.9 us
    ppermute x11 -> x7, waiting for transfers between devices: 12.5 us -> 6.58 us  [xor_swap(): return lax.ppermute(values, axis, [(n, n ^ k) for n in range(count)])]
    ppermute x0 -> x3, waiting for transfers between devices: none -> 5.45 us  [last_core_swap(): return lax.ppermute(values, ('grp', axis, 'pair'), steps)]
    ppermute x11 -> x7, starting transfers between devices: 13.5 us -> 8.99 us  [xor_swap(): return lax.ppermute(values, axis, [(n, n ^ k) for n in range(count)])]
    ppermute x6, waiting for transfers between devices: 3.12 us -> 6.86 us  [even_swap(): return lax.ppermute(values, axis, [(n, n ^ 1) for n in range(count)])]
    ppermute x0 -> x3, starting transfers between devices: none -> 2.66 us  [last_core_swap(): return lax.ppermute(values, ('grp', axis, 'pair'), steps)]
    pallas_call x14 -> x15, Pallas kernels: 7.05 us -> 7.06 us  [whole_call(): pl.pallas_call(body, out_shape=outs, in_specs=specs, out_specs=[pl.BlockS...]
  transfers between devices with their start and end apart: 20 -> 19, of which waited for: 15 -> 13; matrix products, arithmetic and copies ran while one was open for 2% -> 2% of each run, Pallas kernels for 7% -> 6%
where the time goes in v18:
time: 49.9 us; the launch traced here: 49.7 us
  waiting for transfers between devices  20.1 us (40%)
  starting transfers between devices  18.9 us (38%)
  Pallas kernels  7.06 us (14%)
  local copies, waits for them, and re-layouts  2.77 us (6%)
  between operations  0.82 us (2%)
    ppermute x7, starting transfers between devices, xor_swap(): return lax.ppermute(values, axis, [(n, n ^ k) for n in range(count)])  8.99 us
    pallas_call x15, Pallas kernels, whole_call(): pl.pallas_call(body, out_shape=outs, in_specs=specs, out_specs=[pl.BlockS...  7.06 us
    ppermute x6, waiting for transfers between devices, even_swap(): return lax.ppermute(values, axis, [(n, n ^ 1) for n in range(count)])  6.86 us
    ppermute x7, waiting for transfers between devices, xor_swap(): return lax.ppermute(values, axis, [(n, n ^ k) for n in range(count)])  6.58 us
    ppermute x3, waiting for transfers between devices, last_core_swap(): return lax.ppermute(values, ('grp', axis, 'pair'), steps)  5.45 us
    ppermute x6, starting transfers between devices, even_swap(): return lax.ppermute(values, axis, [(n, n ^ 1) for n in range(count)])  5.14 us
    unnamed x6, local copies, waits for them, and re-layouts  2.75 us
    ppermute x3, starting transfers between devices, last_core_swap(): return lax.ppermute(values, ('grp', axis, 'pair'), steps)  2.66 us
  transfers between devices with their start and end apart: 19, of which 13 were waited for; matrix products, arithmetic and copies ran while one was open for 2% of the time, Pallas kernels for 6%

profile of v18, /device:TPU:0, one launch (start us, length us, event | category | flops | bytes accessed | tf_op | source)
XLA Modules:
  0.0 49.7 jit_solution(8591800974441052706)
XLA Ops:
  0.7 1.0 %copy.19 = bf16[64,8,128]{2,0,1:T(8,128)(2,1)S(1)} copy(bf16[64,8,128]{2,1,0:T(8,128)(2,1)} %param.4) | data formatting | bytes 262144 | tf_op args[0]
  2.2 4.1 %collective-permute-start = (bf16[64,128]{1,0:T(8,128)(2,1)S(1)}, bf16[64,128]{1,0:T(8,128)(2,1)S(1)}, u32[]{:S(2)}, u32[]{:S(2)}) collective-permute-start(bf16[64,128]{1,0:T(8,128)(2,1)S(1)} %get-tuple-element.70), channel_id=1, source_target_pairs={{0,4},{4,0},{8,12},{12,8},{1,5},{5,1},{9,13},{13,9},{2,6},{6,2},{1... | collective-permute-start | bytes 49160 | tf_op jit(solution)/shard_map/ppermute | solution.py:328
  8.1 1.6 %collective-permute-start.2 = (bf16[144,128]{1,0:T(8,128)(2,1)S(1)}, bf16[144,128]{1,0:T(8,128)(2,1)S(1)}, u32[]{:S(2)}, u32[]{:S(2)}) collective-permute-start(bf16[144,128]{1,0:T(8,128)(2,1)S(1)} %get-tuple-element.38), channel_id=1, source_target_pairs={{0,16},{1,2},{2,1},{3,19},{16,0},{17,18},{18,17},{19,3},{4,20},{5,... | collective-permute-start | bytes 110600 | tf_op jit(solution)/shard_map/ppermute | solution.py:352
  9.8 0.9 %copy-done.1 = bf16[64,3,3,64]{3,0,2,1:T(8,128)(2,1)S(1)} copy-done((bf16[64,3,3,64]{3,0,2,1:T(8,128)(2,1)S(1)}, bf16[64,3,3,64]{3,0,2,1:T(8,128)(2,1)}, u32[]{:S(2)}) %copy-start.1) | copy-done | bytes 73752
  10.9 1.2 %collective-permute-done.2.b_ref = bf16[144,128]{1,0:T(8,128)(2,1)S(1)} collective-permute-done((bf16[144,128]{1,0:T(8,128)(2,1)S(1)}, bf16[144,128]{1,0:T(8,128)(2,1)S(1)}, u32[]{:S(2)}, u32[]{:S(2)}) %collective-permute-start.2) | collective-permute-done | bytes 36896 | tf_op jit(solution)/shard_map/ppermute | solution.py:352
  12.1 0.9 %shard_map.70 = (bf16[2,40,256]{2,1,0:T(8,128)(2,1)S(1)}, bf16[8,64,256]{2,1,0:T(8,128)(2,1)S(1)}, bf16[10,64,256]{2,1,0:T(8,128)(2,1)S(1)}) custom-call(bf16[8,64,128]{2,1,0:T(8,128)(2,1)S(1)} %bitcast.34, bf16[64,128]{1,0:T(8,128)(2,1)S(1)} %get-tuple-element.40.above_ref, bf16[64,128]{1,0:T(8,128)(2,1)S(1)} %get-tuple-element.41.below_ref, ...), custom_call_target="tpu_custom_call" | custom-call | flops 150994944 | bytes 1122304 | tf_op jit(solution)/shard_map/pallas_call | solution.py:30
  13.0 2.0 %collective-permute-start.6 = (bf16[2,40,256]{2,1,0:T(8,128)(2,1)S(1)}, bf16[2,40,256]{2,1,0:T(8,128)(2,1)S(1)}, u32[]{:S(2)}, u32[]{:S(2)}) collective-permute-start(bf16[2,40,256]{2,1,0:T(8,128)(2,1)S(1)} %get-tuple-element.45.refs_0_), channel_id=1, source_target_pairs={{0,8},{4,12},{8,0},{12,4},{1,9},{5,13},{9,1},{13,5},{2,10},{6,14},... | collective-permute-start | bytes 122888 | tf_op jit(solution)/shard_map/ppermute | solution.py:356
  15.0 2.5 %collective-permute-start.5 = (bf16[2,40,256]{2,1,0:T(8,128)(2,1)S(1)}, bf16[2,40,256]{2,1,0:T(8,128)(2,1)S(1)}, u32[]{:S(2)}, u32[]{:S(2)}) collective-permute-start(bf16[2,40,256]{2,1,0:T(8,128)(2,1)S(1)} %get-tuple-element.45.refs_0_), channel_id=1, source_target_pairs={{0,12},{4,8},{8,4},{12,0},{1,13},{5,9},{9,5},{13,1},{2,14},{6,10},... | collective-permute-start | bytes 122888 | tf_op jit(solution)/shard_map/ppermute | solution.py:356
  17.6 1.4 %collective-permute-done.6.refs_3_ = bf16[2,40,256]{2,1,0:T(8,128)(2,1)S(1)} collective-permute-done((bf16[2,40,256]{2,1,0:T(8,128)(2,1)S(1)}, bf16[2,40,256]{2,1,0:T(8,128)(2,1)S(1)}, u32[]{:S(2)}, u32[]{:S(2)}) %collective-permute-start.6) | collective-permute-done | bytes 40992 | tf_op jit(solution)/shard_map/ppermute | solution.py:356
  19.0 1.8 %collective-permute-done.5.refs_2_ = bf16[2,40,256]{2,1,0:T(8,128)(2,1)S(1)} collective-permute-done((bf16[2,40,256]{2,1,0:T(8,128)(2,1)S(1)}, bf16[2,40,256]{2,1,0:T(8,128)(2,1)S(1)}, u32[]{:S(2)}, u32[]{:S(2)}) %collective-permute-start.5) | collective-permute-done | bytes 40992 | tf_op jit(solution)/shard_map/ppermute | solution.py:356
  21.5 1.0 %shard_map.71 = (bf16[72,256]{1,0:T(8,128)(2,1)S(1)}, bf16[72,256]{1,0:T(8,128)(2,1)S(1)}, bf16[72,256]{1,0:T(8,128)(2,1)S(1)}, bf16[72,256]{1,0:T(8,128)(2,1)S(...) custom-call(bf16[8,48,128]{2,1,0:T(8,128)(2,1)S(1)} %fusion.6.og_ref, ...), custom_call_target="tpu_custom_call" | custom-call | flops 452984832 | bytes 1368064 | tf_op jit(solution)/shard_map/pallas_call | solution.py:30
  22.9 2.5 %collective-permute-start.8 = (bf16[72,256]{1,0:T(8,128)(2,1)S(1)}, bf16[72,256]{1,0:T(8,128)(2,1)S(1)}, u32[]{:S(2)}, u32[]{:S(2)}) collective-permute-start(bf16[72,256]{1,0:T(8,128)(2,1)S(1)} %get-tuple-element.48), channel_id=1, source_target_pairs={{0,12},{4,8},{8,4},{12,0},{1,13},{5,9},{9,5},{13,1},{2,14},{6,10},... | collective-permute-start | bytes 110600 | tf_op jit(solution)/shard_map/ppermute | solution.py:356
  26.6 1.0 %collective-permute-done.7.refs_1_ = bf16[72,256]{1,0:T(8,128)(2,1)S(1)} collective-permute-done((bf16[72,256]{1,0:T(8,128)(2,1)S(1)}, bf16[72,256]{1,0:T(8,128)(2,1)S(1)}, u32[]{:S(2)}, u32[]{:S(2)}) %collective-permute-start.7) | collective-permute-done | bytes 36896 | tf_op jit(solution)/shard_map/ppermute | solution.py:356
  27.7 1.0 %collective-permute-done.8.refs_2_ = bf16[72,256]{1,0:T(8,128)(2,1)S(1)} collective-permute-done((bf16[72,256]{1,0:T(8,128)(2,1)S(1)}, bf16[72,256]{1,0:T(8,128)(2,1)S(1)}, u32[]{:S(2)}, u32[]{:S(2)}) %collective-permute-start.8) | collective-permute-done | bytes 36896 | tf_op jit(solution)/shard_map/ppermute | solution.py:356
  29.3 0.9 %shard_map.73 = (bf16[8,64,256]{2,1,0:T(8,128)(2,1)S(1)}, bf16[64,256]{1,0:T(8,128)(2,1)S(1)}, bf16[64,256]{1,0:T(8,128)(2,1)S(1)}, bf16[720,256]{1,0:T(8,128)(2,1)S(1)}, bf16[720,256]{1,0:T(8,128)(2,1)S(1)}) custom-call(bf16[72,256]{1,0:T(8,128)(2,1)S(1)} %get-tuple-element.46.refs_0_, bf16[72,256]{1,0:T(8,128)(2,1)S(1)} %collective-permute-done.7.refs_1_, ...), custom_call_target="tpu_custom_call" | custom-call | flops 150994944 | bytes 2572288 | tf_op jit(solution)/shard_map/pallas_call | solution.py:30
  30.2 1.7 %collective-permute-done.12.b_ref = bf16[720,256]{1,0:T(8,128)(2,1)S(1)} collective-permute-done((bf16[720,256]{1,0:T(8,128)(2,1)S(1)}, bf16[720,256]{1,0:T(8,128)(2,1)S(1)}, u32[]{:S(2)}, u32[]{:S(2)}) %collective-permute-start.12) | collective-permute-done | bytes 368672 | tf_op jit(solution)/shard_map/ppermute | solution.py:328
  32.0 1.0 %collective-permute-start.16 = (bf16[576,256]{1,0:T(8,128)(2,1)S(1)}, bf16[576,256]{1,0:T(8,128)(2,1)S(1)}, u32[]{:S(2)}, u32[]{:S(2)}) collective-permute-start(bf16[576,256]{1,0:T(8,128)(2,1)S(1)} %get-tuple-element.65.a_ref), channel_id=1, source_target_pairs={{0,2},{2,0},{1,3},{3,1},{4,6},{6,4},{5,7},{7,5},{8,10},{10,8},{9,1... | collective-permute-start | bytes 884744 | tf_op jit(solution)/shard_map/ppermute | solution.py:356
  33.0 1.5 %collective-permute-start.13 = (bf16[144,256]{1,0:T(8,128)(2,1)S(1)}, bf16[144,256]{1,0:T(8,128)(2,1)S(1)}, u32[]{:S(2)}, u32[]{:S(2)}) collective-permute-start(bf16[144,256]{1,0:T(8,128)(2,1)S(1)} %get-tuple-element.64.a_ref), channel_id=1, source_target_pairs={{0,16},{1,5},{4,20},{5,1},{8,24},{9,13},{12,28},{13,9},{16,0},{17,... | collective-permute-start | bytes 221192 | tf_op jit(solution)/shard_map/ppermute | solution.py:367
  35.2 3.2 %collective-permute-done.10.a_ref.refs_0_ = bf16[64,256]{1,0:T(8,128)(2,1)S(1)} collective-permute-done((bf16[64,256]{1,0:T(8,128)(2,1)S(1)}, bf16[64,256]{1,0:T(8,128)(2,1)S(1)}, u32[]{:S(2)}, u32[]{:S(2)}) %collective-permute-start.10) | collective-permute-done | bytes 32800 | tf_op jit(solution)/shard_map/ppermute | solution.py:328
  39.0 3.8 %collective-permute-done.14.b_ref = bf16[144,256]{1,0:T(8,128)(2,1)S(1)} collective-permute-done((bf16[144,256]{1,0:T(8,128)(2,1)S(1)}, bf16[144,256]{1,0:T(8,128)(2,1)S(1)}, u32[]{:S(2)}, u32[]{:S(2)}) %collective-permute-start.14) | collective-permute-done | bytes 73760 | tf_op jit(solution)/shard_map/ppermute | solution.py:367
  43.6 1.2 %shard_map.74 = (bf16[64,8,128]{2,1,0:T(8,128)(2,1)}, f32[8,128]{1,0:T(8,128)S(1)}) custom-call(bf16[8,64,256]{2,1,0:T(8,128)(2,1)S(1)} %get-tuple-element.57.g_ref, bf16[64,256]{1,0:T(8,128)(2,1)S(1)} %collective-permute-done.10.a_ref.refs_0_, bf16[64,256]{1,0:T(8,128)(2,1)S(1)} %collective-permute-done.11.b_ref.refs_1_, ...), custom_call_target="tpu_custom_call" | custom-call | flops 150994944 | bytes 536576 | tf_op jit(solution)/shard_map/pallas_call | solution.py:30
  44.8 1.1 %shard_map.79 = (f32[1152,256]{1,0:T(8,128)}, f32[8,128]{1,0:T(8,128)S(1)}) custom-call(bf16[576,256]{1,0:T(8,128)(2,1)S(1)} %shard_map.78.mine_ref, bf16[576,256]{1,0:T(8,128)(2,1)S(1)} %collective-permute-done.17.other_ref), custom_call_target="tpu_custom_call" | custom-call | flops 100000000 | bytes 1773568 | tf_op jit(solution)/shard_map/pallas_call | solution.py:30
  45.9 1.6 %collective-permute-done.15.b_ref = bf16[144,256]{1,0:T(8,128)(2,1)S(1)} collective-permute-done((bf16[144,256]{1,0:T(8,128)(2,1)S(1)}, bf16[144,256]{1,0:T(8,128)(2,1)S(1)}, u32[]{:S(2)}, u32[]{:S(2)}) %collective-permute-start.15) | collective-permute-done | bytes 73760 | tf_op jit(solution)/shard_map/ppermute | solution.py:367
  47.6 1.3 %collective-permute-done.18.other_ref = bf16[144,256]{1,0:T(8,128)(2,1)S(1)} collective-permute-done((bf16[144,256]{1,0:T(8,128)(2,1)S(1)}, bf16[144,256]{1,0:T(8,128)(2,1)S(1)}, u32[]{:S(2)}, u32[]{:S(2)}) %collective-permute-start.18) | collective-permute-done | bytes 73760 | tf_op jit(solution)/shard_map/ppermute | solution.py:328
  (42 shorter events, 8.8 us)
Async XLA Ops:
  0.6 20.8 %copy-start = (bf16[128,3,3,256]{3,0,2,1:T(8,128)(2,1)S(1)}, bf16[128,3,3,256]{3,0,2,1:T(8,128)(2,1)}, u32[]{:S(2)}) copy-start(bf16[128,3,3,256]{3,0,2,1:T(8,128)(2,1)} %param.6) | copy-start | bytes 1769476
  1.7 5.7 %collective-permute-start.1 = (bf16[64,128]{1,0:T(8,128)(2,1)S(1)}, bf16[64,128]{1,0:T(8,128)(2,1)S(1)}, u32[]{:S(2)}, u32[]{:S(2)}) collective-permute-start(bf16[64,128]{1,0:T(8,128)(2,1)S(1)} %get-tuple-element.69), channel_id=1, source_target_pairs={{0,1},{1,0},{4,8},{5,9},{8,4},{9,5},{12,13},{13,12},{2,3},{3,2},{6... | collective-permute-start | bytes 49160 | tf_op jit(solution)/shard_map/ppermute | solution.py:342
  2.2 5.9 %collective-permute-start = (bf16[64,128]{1,0:T(8,128)(2,1)S(1)}, bf16[64,128]{1,0:T(8,128)(2,1)S(1)}, u32[]{:S(2)}, u32[]{:S(2)}) collective-permute-start(bf16[64,128]{1,0:T(8,128)(2,1)S(1)} %get-tuple-element.70), channel_id=1, source_target_pairs={{0,4},{4,0},{8,12},{12,8},{1,5},{5,1},{9,13},{13,9},{2,6},{6,2},{1... | collective-permute-start | bytes 49160 | tf_op jit(solution)/shard_map/ppermute | solution.py:328
  8.1 4.0 %collective-permute-start.2 = (bf16[144,128]{1,0:T(8,128)(2,1)S(1)}, bf16[144,128]{1,0:T(8,128)(2,1)S(1)}, u32[]{:S(2)}, u32[]{:S(2)}) collective-permute-start(bf16[144,128]{1,0:T(8,128)(2,1)S(1)} %get-tuple-element.38), channel_id=1, source_target_pairs={{0,16},{1,2},{2,1},{3,19},{16,0},{17,18},{18,17},{19,3},{4,20},{5,... | collective-permute-start | bytes 110600 | tf_op jit(solution)/shard_map/ppermute | solution.py:352
  9.7 2.4 %collective-permute-start.3 = (bf16[144,128]{1,0:T(8,128)(2,1)S(1)}, bf16[144,128]{1,0:T(8,128)(2,1)S(1)}, u32[]{:S(2)}, u32[]{:S(2)}) collective-permute-start(bf16[144,128]{1,0:T(8,128)(2,1)S(1)} %get-tuple-element.39), channel_id=1, source_target_pairs={{0,1},{1,0},{2,3},{3,2},{4,5},{5,4},{6,7},{7,6},{8,9},{9,8},{10,11... | collective-permute-start | bytes 110600 | tf_op jit(solution)/shard_map/ppermute | solution.py:328
  9.8 0.9 %copy-start.1 = (bf16[64,3,3,64]{3,0,2,1:T(8,128)(2,1)S(1)}, bf16[64,3,3,64]{3,0,2,1:T(8,128)(2,1)}, u32[]{:S(2)}) copy-start(bf16[64,3,3,64]{3,0,2,1:T(8,128)(2,1)} %param.5) | copy-start | bytes 221188
  13.0 6.0 %collective-permute-start.6 = (bf16[2,40,256]{2,1,0:T(8,128)(2,1)S(1)}, bf16[2,40,256]{2,1,0:T(8,128)(2,1)S(1)}, u32[]{:S(2)}, u32[]{:S(2)}) collective-permute-start(bf16[2,40,256]{2,1,0:T(8,128)(2,1)S(1)} %get-tuple-element.45.refs_0_), channel_id=1, source_target_pairs={{0,8},{4,12},{8,0},{12,4},{1,9},{5,13},{9,1},{13,5},{2,10},{6,14},... | collective-permute-start | bytes 122888 | tf_op jit(solution)/shard_map/ppermute | solution.py:356
  15.0 5.8 %collective-permute-start.5 = (bf16[2,40,256]{2,1,0:T(8,128)(2,1)S(1)}, bf16[2,40,256]{2,1,0:T(8,128)(2,1)S(1)}, u32[]{:S(2)}, u32[]{:S(2)}) collective-permute-start(bf16[2,40,256]{2,1,0:T(8,128)(2,1)S(1)} %get-tuple-element.45.refs_0_), channel_id=1, source_target_pairs={{0,12},{4,8},{8,4},{12,0},{1,13},{5,9},{9,5},{13,1},{2,14},{6,10},... | collective-permute-start | bytes 122888 | tf_op jit(solution)/shard_map/ppermute | solution.py:356
  17.5 4.0 %collective-permute-start.4 = (bf16[2,40,256]{2,1,0:T(8,128)(2,1)S(1)}, bf16[2,40,256]{2,1,0:T(8,128)(2,1)S(1)}, u32[]{:S(2)}, u32[]{:S(2)}) collective-permute-start(bf16[2,40,256]{2,1,0:T(8,128)(2,1)S(1)} %get-tuple-element.45.refs_0_), channel_id=1, source_target_pairs={{0,4},{4,0},{8,12},{12,8},{1,5},{5,1},{9,13},{13,9},{2,6},{6,2},{1... | collective-permute-start | bytes 122888 | tf_op jit(solution)/shard_map/ppermute | solution.py:356
  22.5 5.2 %collective-permute-start.7 = (bf16[72,256]{1,0:T(8,128)(2,1)S(1)}, bf16[72,256]{1,0:T(8,128)(2,1)S(1)}, u32[]{:S(2)}, u32[]{:S(2)}) collective-permute-start(bf16[72,256]{1,0:T(8,128)(2,1)S(1)} %get-tuple-element.47), channel_id=1, source_target_pairs={{0,8},{4,12},{8,0},{12,4},{1,9},{5,13},{9,1},{13,5},{2,10},{6,14},... | collective-permute-start | bytes 110600 | tf_op jit(solution)/shard_map/ppermute | solution.py:356
  22.9 5.8 %collective-permute-start.8 = (bf16[72,256]{1,0:T(8,128)(2,1)S(1)}, bf16[72,256]{1,0:T(8,128)(2,1)S(1)}, u32[]{:S(2)}, u32[]{:S(2)}) collective-permute-start(bf16[72,256]{1,0:T(8,128)(2,1)S(1)} %get-tuple-element.48), channel_id=1, source_target_pairs={{0,12},{4,8},{8,4},{12,0},{1,13},{5,9},{9,5},{13,1},{2,14},{6,10},... | collective-permute-start | bytes 110600 | tf_op jit(solution)/shard_map/ppermute | solution.py:356
  25.3 4.0 %collective-permute-start.9 = (bf16[72,256]{1,0:T(8,128)(2,1)S(1)}, bf16[72,256]{1,0:T(8,128)(2,1)S(1)}, u32[]{:S(2)}, u32[]{:S(2)}) collective-permute-start(bf16[72,256]{1,0:T(8,128)(2,1)S(1)} %get-tuple-element.49), channel_id=1, source_target_pairs={{0,4},{4,0},{8,12},{12,8},{1,5},{5,1},{9,13},{13,9},{2,6},{6,2},{1... | collective-permute-start | bytes 110600 | tf_op jit(solution)/shard_map/ppermute | solution.py:356
  30.2 1.8 %collective-permute-start.12 = (bf16[720,256]{1,0:T(8,128)(2,1)S(1)}, bf16[720,256]{1,0:T(8,128)(2,1)S(1)}, u32[]{:S(2)}, u32[]{:S(2)}) collective-permute-start(bf16[720,256]{1,0:T(8,128)(2,1)S(1)} %get-tuple-element.63), channel_id=1, source_target_pairs={{0,1},{1,0},{2,3},{3,2},{4,5},{5,4},{6,7},{7,6},{8,9},{9,8},{10,11... | collective-permute-start | bytes 1105928 | tf_op jit(solution)/shard_map/ppermute | solution.py:328
  32.0 10.9 %collective-permute-start.16 = (bf16[576,256]{1,0:T(8,128)(2,1)S(1)}, bf16[576,256]{1,0:T(8,128)(2,1)S(1)}, u32[]{:S(2)}, u32[]{:S(2)}) collective-permute-start(bf16[576,256]{1,0:T(8,128)(2,1)S(1)} %get-tuple-element.65.a_ref), channel_id=1, source_target_pairs={{0,2},{2,0},{1,3},{3,1},{4,6},{6,4},{5,7},{7,5},{8,10},{10,8},{9,1... | collective-permute-start | bytes 884744 | tf_op jit(solution)/shard_map/ppermute | solution.py:356
  33.0 5.4 %collective-permute-start.13 = (bf16[144,256]{1,0:T(8,128)(2,1)S(1)}, bf16[144,256]{1,0:T(8,128)(2,1)S(1)}, u32[]{:S(2)}, u32[]{:S(2)}) collective-permute-start(bf16[144,256]{1,0:T(8,128)(2,1)S(1)} %get-tuple-element.64.a_ref), channel_id=1, source_target_pairs={{0,16},{1,5},{4,20},{5,1},{8,24},{9,13},{12,28},{13,9},{16,0},{17,... | collective-permute-start | bytes 221192 | tf_op jit(solution)/shard_map/ppermute | solution.py:367
  34.5 3.9 %collective-permute-start.10 = (bf16[64,256]{1,0:T(8,128)(2,1)S(1)}, bf16[64,256]{1,0:T(8,128)(2,1)S(1)}, u32[]{:S(2)}, u32[]{:S(2)}) collective-permute-start(bf16[64,256]{1,0:T(8,128)(2,1)S(1)} %get-tuple-element.58), channel_id=1, source_target_pairs={{0,4},{4,0},{8,12},{12,8},{1,5},{5,1},{9,13},{13,9},{2,6},{6,2},{1... | collective-permute-start | bytes 98312 | tf_op jit(solution)/shard_map/ppermute | solution.py:328
  35.2 3.2 %collective-permute-start.11 = (bf16[64,256]{1,0:T(8,128)(2,1)S(1)}, bf16[64,256]{1,0:T(8,128)(2,1)S(1)}, u32[]{:S(2)}, u32[]{:S(2)}) collective-permute-start(bf16[64,256]{1,0:T(8,128)(2,1)S(1)} %get-tuple-element.59), channel_id=1, source_target_pairs={{0,1},{1,0},{4,8},{5,9},{8,4},{9,5},{12,13},{13,12},{2,3},{3,2},{6... | collective-permute-start | bytes 98312 | tf_op jit(solution)/shard_map/ppermute | solution.py:342
  38.5 4.4 %collective-permute-start.14 = (bf16[144,256]{1,0:T(8,128)(2,1)S(1)}, bf16[144,256]{1,0:T(8,128)(2,1)S(1)}, u32[]{:S(2)}, u32[]{:S(2)}) collective-permute-start(bf16[144,256]{1,0:T(8,128)(2,1)S(1)} %shard_map.76.a_ref), channel_id=1, source_target_pairs={{0,16},{1,9},{4,20},{5,13},{8,24},{9,1},{12,28},{13,5},{16,0},{17,... | collective-permute-start | bytes 221192 | tf_op jit(solution)/shard_map/ppermute | solution.py:367
  43.0 1.8 %collective-permute-start.17 = (bf16[576,256]{1,0:T(8,128)(2,1)S(1)}, bf16[576,256]{1,0:T(8,128)(2,1)S(1)}, u32[]{:S(2)}, u32[]{:S(2)}) collective-permute-start(bf16[576,256]{1,0:T(8,128)(2,1)S(1)} %shard_map.78.mine_ref), channel_id=1, source_target_pairs={{0,1},{1,0},{2,3},{3,2},{4,5},{5,4},{6,7},{7,6},{8,9},{9,8},{10,11... | collective-permute-start | bytes 884744 | tf_op jit(solution)/shard_map/ppermute | solution.py:328
  43.1 4.4 %collective-permute-start.15 = (bf16[144,256]{1,0:T(8,128)(2,1)S(1)}, bf16[144,256]{1,0:T(8,128)(2,1)S(1)}, u32[]{:S(2)}, u32[]{:S(2)}) collective-permute-start(bf16[144,256]{1,0:T(8,128)(2,1)S(1)} %shard_map.77.refs_0_.a_ref), channel_id=1, source_target_pairs={{0,16},{1,3},{2,18},{3,1},{16,0},{17,19},{18,2},{19,17},{4,20},{5,... | collective-permute-start | bytes 221192 | tf_op jit(solution)/shard_map/ppermute | solution.py:367
  47.5 1.3 %collective-permute-start.18 = (bf16[144,256]{1,0:T(8,128)(2,1)S(1)}, bf16[144,256]{1,0:T(8,128)(2,1)S(1)}, u32[]{:S(2)}, u32[]{:S(2)}) collective-permute-start(bf16[144,256]{1,0:T(8,128)(2,1)S(1)} %shard_map.80.mine_ref), channel_id=1, source_target_pairs={{0,1},{1,0},{2,3},{3,2},{4,5},{5,4},{6,7},{7,6},{8,9},{9,8},{10,11... | collective-permute-start | bytes 221192 | tf_op jit(solution)/shard_map/ppermute | solution.py:328

commit v19 on v15

--- a/solution.py
+++ b/solution.py
@@ -407,12 +407,14 @@
     taps_one = jnp.transpose(filters_one, (1, 2, 0, 3)).reshape(3, 3 * channels, channels)
     taps_two = jnp.transpose(filters_two, (1, 2, 0, 3)).reshape(3, 3 * filters, 4 * channels)
 
-    og = jnp.transpose(out_grad, (1, 2, 0))
     edge = REACH - 1
-    x = jnp.transpose(features_in, (1, 0, 2))
     even = band % 2 == 0
-    to_a, to_b = jnp.where(even, x[-1], x[0]), jnp.where(even, x[0], x[-1])
-    head, tail = og[:edge], og[-edge:]
+    first, last = features_in[:, 0], features_in[:, -1]
+    to_a, to_b = jnp.where(even, last, first), jnp.where(even, first, last)
+    head, tail = (jnp.transpose(e, (1, 2, 0)) for e in (out_grad[:, :edge], out_grad[:, -edge:]))
+    whole_in, whole_grad = lax.optimization_barrier((features_in, out_grad))
+    x = jnp.transpose(whole_in, (1, 0, 2))
+    og = jnp.transpose(whole_grad, (1, 2, 0))
     joined_one, back_one, pool, pool_back, order = whole_call(
         functools.partial(constants, total=total),
         [shaped((3 * channels, 3 * channels))] * 2 + [shaped((2 * PITCH, 256))] * 2 + [shaped((256, 256))],

time: 47.6 us -> 47.8 us (level)
  local copies, waits for them, and re-layouts: 2.77 us -> 3.59 us
  waiting for transfers between devices: 15.6 us -> 15 us
    unnamed x6 -> x4, local copies, waits for them, and re-layouts: 2.75 us -> 0.01 us
    optimization_barrier x0 -> x2, local copies, waits for them, and re-layouts: none -> 1.77 us  [local(): whole_in, whole_grad = lax.optimization_barrier((features_in, out_grad))]
    slice x1, local copies, waits for them, and re-layouts: 0.01 us -> 1.09 us  [local(): first, last = (features_in[:, 0], features_in[:, -1])]
    ppermute x5, waiting for transfers between devices: 3.54 us -> 2.83 us  [even_swap(): return lax.ppermute(values, axis, [(n, n ^ 1) for n in range(count)])]
    reshape x1, local copies, waits for them, and re-layouts: 0.01 us -> 0.71 us  [local(): head, tail = (head.reshape(-1, 128), tail.reshape(-1, 128))]
  transfers between devices with their start and end apart: 19 -> 19, of which waited for: 14 -> 13; matrix products, arithmetic and copies ran while one was open for 2% -> 5% of each run, Pallas kernels for 7% -> 7%
where the time goes in v19:
time: 47.8 us; the launch traced here: 47.6 us
  starting transfers between devices  21 us (44%)
  waiting for transfers between devices  15 us (31%)
  Pallas kernels  7.07 us (15%)
  local copies, waits for them, and re-layouts  3.59 us (8%)
  between operations  0.83 us (2%)
    ppermute x11, starting transfers between devices, xor_swap(): return lax.ppermute(values, axis, [(n, n ^ k) for n in range(count)])  14.5 us
    ppermute x11, waiting for transfers between devices, xor_swap(): return lax.ppermute(values, axis, [(n, n ^ k) for n in range(count)])  9.71 us
    pallas_call x14, Pallas kernels, whole_call(): pl.pallas_call(body, out_shape=outs, in_specs=specs, out_specs=[pl.BlockS...  7.07 us
    ppermute x5, starting transfers between devices, even_swap(): return lax.ppermute(values, axis, [(n, n ^ 1) for n in range(count)])  4.45 us
    ppermute x5, waiting for transfers between devices, even_swap(): return lax.ppermute(values, axis, [(n, n ^ 1) for n in range(count)])  2.83 us
    optimization_barrier x2, local copies, waits for them, and re-layouts, local(): whole_in, whole_grad = lax.optimization_barrier((features_in, out_grad))  1.77 us
    ppermute x1, starting transfers between devices, odd_strip_swap(): return lax.ppermute(values, ('grp',) + COLS, steps)  1.57 us
    ppermute x1, waiting for transfers between devices, odd_strip_swap(): return lax.ppermute(values, ('grp',) + COLS, steps)  1.22 us
  transfers between devices with their start and end apart: 19, of which 13 were waited for; matrix products, arithmetic and copies ran while one was open for 5% of the time, Pallas kernels for 7%

profile of v19, /device:TPU:0, one launch (start us, length us, event | category | flops | bytes accessed | tf_op | source)
XLA Modules:
  0.0 47.6 jit_solution(6755437417124763272)
XLA Ops:
  0.7 1.1 %fusion.7 = (bf16[64,1,128]{2,1,0:T(2,128)(2,1)S(1)}, bf16[64,1,128]{2,1,0:T(2,128)(2,1)S(1)}) fusion(bf16[64,8,128]{2,1,0:T(8,128)(2,1)} %param.4), kind=kLoop, calls=%fused_computation.18 | loop fusion | bytes 65536 | tf_op jit(solution)/shard_map/slice | solution.py:412
  2.3 4.1 %collective-permute-start = (bf16[64,128]{1,0:T(8,128)(2,1)S(1)}, bf16[64,128]{1,0:T(8,128)(2,1)S(1)}, u32[]{:S(2)}, u32[]{:S(2)}) collective-permute-start(bf16[64,128]{1,0:T(8,128)(2,1)S(1)} %get-tuple-element.82), channel_id=1, source_target_pairs={{0,4},{4,0},{8,12},{12,8},{1,5},{5,1},{9,13},{13,9},{2,6},{6,2},{1... | collective-permute-start | bytes 49160 | tf_op jit(solution)/shard_map/ppermute | solution.py:342
  7.2 0.9 %copy.25 = bf16[64,8,128]{2,0,1:T(8,128)(2,1)S(1)} copy(bf16[64,8,128]{2,1,0:T(8,128)(2,1)} %param.4) | data formatting | bytes 262144 | tf_op jit(solution)/shard_map/optimization_barrier | solution.py:415
  8.3 1.6 %collective-permute-start.2 = (bf16[144,128]{1,0:T(8,128)(2,1)S(1)}, bf16[144,128]{1,0:T(8,128)(2,1)S(1)}, u32[]{:S(2)}, u32[]{:S(2)}) collective-permute-start(bf16[144,128]{1,0:T(8,128)(2,1)S(1)} %get-tuple-element.42), channel_id=1, source_target_pairs={{0,16},{1,2},{2,1},{3,19},{16,0},{17,18},{18,17},{19,3},{4,20},{5,... | collective-permute-start | bytes 110600 | tf_op jit(solution)/shard_map/ppermute | solution.py:366
  11.1 1.2 %collective-permute-done.2.b_ref = bf16[144,128]{1,0:T(8,128)(2,1)S(1)} collective-permute-done((bf16[144,128]{1,0:T(8,128)(2,1)S(1)}, bf16[144,128]{1,0:T(8,128)(2,1)S(1)}, u32[]{:S(2)}, u32[]{:S(2)}) %collective-permute-start.2) | collective-permute-done | bytes 36896 | tf_op jit(solution)/shard_map/ppermute | solution.py:366
  13.2 1.9 %collective-permute-start.6 = (bf16[2,40,256]{2,1,0:T(8,128)(2,1)S(1)}, bf16[2,40,256]{2,1,0:T(8,128)(2,1)S(1)}, u32[]{:S(2)}, u32[]{:S(2)}) collective-permute-start(bf16[2,40,256]{2,1,0:T(8,128)(2,1)S(1)} %get-tuple-element.50.refs_0_), channel_id=1, source_target_pairs={{0,8},{4,12},{8,0},{12,4},{1,9},{5,13},{9,1},{13,5},{2,10},{6,14},... | collective-permute-start | bytes 122888 | tf_op jit(solution)/shard_map/ppermute | solution.py:370
  15.1 2.5 %collective-permute-start.5 = (bf16[2,40,256]{2,1,0:T(8,128)(2,1)S(1)}, bf16[2,40,256]{2,1,0:T(8,128)(2,1)S(1)}, u32[]{:S(2)}, u32[]{:S(2)}) collective-permute-start(bf16[2,40,256]{2,1,0:T(8,128)(2,1)S(1)} %get-tuple-element.50.refs_0_), channel_id=1, source_target_pairs={{0,12},{4,8},{8,4},{12,0},{1,13},{5,9},{9,5},{13,1},{2,14},{6,10},... | collective-permute-start | bytes 122888 | tf_op jit(solution)/shard_map/ppermute | solution.py:370
  17.7 1.4 %collective-permute-done.6.refs_3_ = bf16[2,40,256]{2,1,0:T(8,128)(2,1)S(1)} collective-permute-done((bf16[2,40,256]{2,1,0:T(8,128)(2,1)S(1)}, bf16[2,40,256]{2,1,0:T(8,128)(2,1)S(1)}, u32[]{:S(2)}, u32[]{:S(2)}) %collective-permute-start.6) | collective-permute-done | bytes 40992 | tf_op jit(solution)/shard_map/ppermute | solution.py:370
  19.1 1.8 %collective-permute-done.5.refs_2_ = bf16[2,40,256]{2,1,0:T(8,128)(2,1)S(1)} collective-permute-done((bf16[2,40,256]{2,1,0:T(8,128)(2,1)S(1)}, bf16[2,40,256]{2,1,0:T(8,128)(2,1)S(1)}, u32[]{:S(2)}, u32[]{:S(2)}) %collective-permute-start.5) | collective-permute-done | bytes 40992 | tf_op jit(solution)/shard_map/ppermute | solution.py:370
  21.6 1.0 %shard_map.71 = (bf16[72,256]{1,0:T(8,128)(2,1)S(1)}, bf16[72,256]{1,0:T(8,128)(2,1)S(1)}, bf16[72,256]{1,0:T(8,128)(2,1)S(1)}, bf16[72,256]{1,0:T(8,128)(2,1)S(...) custom-call(bf16[8,48,128]{2,1,0:T(8,128)(2,1)S(1)} %fusion.6.og_ref, ...), custom_call_target="tpu_custom_call" | custom-call | flops 452984832 | bytes 1368064 | tf_op jit(solution)/shard_map/pallas_call | solution.py:30
  23.0 2.5 %collective-permute-start.8 = (bf16[72,256]{1,0:T(8,128)(2,1)S(1)}, bf16[72,256]{1,0:T(8,128)(2,1)S(1)}, u32[]{:S(2)}, u32[]{:S(2)}) collective-permute-start(bf16[72,256]{1,0:T(8,128)(2,1)S(1)} %get-tuple-element.53), channel_id=1, source_target_pairs={{0,12},{4,8},{8,4},{12,0},{1,13},{5,9},{9,5},{13,1},{2,14},{6,10},... | collective-permute-start | bytes 110600 | tf_op jit(solution)/shard_map/ppermute | solution.py:370
  26.8 1.0 %collective-permute-done.7.refs_1_ = bf16[72,256]{1,0:T(8,128)(2,1)S(1)} collective-permute-done((bf16[72,256]{1,0:T(8,128)(2,1)S(1)}, bf16[72,256]{1,0:T(8,128)(2,1)S(1)}, u32[]{:S(2)}, u32[]{:S(2)}) %collective-permute-start.7) | collective-permute-done | bytes 36896 | tf_op jit(solution)/shard_map/ppermute | solution.py:370
  27.8 1.0 %collective-permute-done.8.refs_2_ = bf16[72,256]{1,0:T(8,128)(2,1)S(1)} collective-permute-done((bf16[72,256]{1,0:T(8,128)(2,1)S(1)}, bf16[72,256]{1,0:T(8,128)(2,1)S(1)}, u32[]{:S(2)}, u32[]{:S(2)}) %collective-permute-start.8) | collective-permute-done | bytes 36896 | tf_op jit(solution)/shard_map/ppermute | solution.py:370
  29.4 0.9 %shard_map.73 = (bf16[8,64,256]{2,1,0:T(8,128)(2,1)S(1)}, bf16[64,256]{1,0:T(8,128)(2,1)S(1)}, bf16[64,256]{1,0:T(8,128)(2,1)S(1)}, bf16[648,256]{1,0:T(8,128)(2,1)S(1)}, bf16[648,256]{1,0:T(8,128)(2,1)S(1)}) custom-call(bf16[72,256]{1,0:T(8,128)(2,1)S(1)} %get-tuple-element.51.refs_0_, bf16[72,256]{1,0:T(8,128)(2,1)S(1)} %collective-permute-done.7.refs_1_, ...), custom_call_target="tpu_custom_call" | custom-call | flops 150994944 | bytes 2498560 | tf_op jit(solution)/shard_map/pallas_call | solution.py:30
  30.4 1.6 %collective-permute-done.10.b_ref = bf16[648,256]{1,0:T(8,128)(2,1)S(1)} collective-permute-done((bf16[648,256]{1,0:T(8,128)(2,1)S(1)}, bf16[648,256]{1,0:T(8,128)(2,1)S(1)}, u32[]{:S(2)}, u32[]{:S(2)}) %collective-permute-start.10) | collective-permute-done | bytes 331808 | tf_op jit(solution)/shard_map/ppermute | solution.py:342
  32.1 1.0 %collective-permute-start.16 = (bf16[576,256]{1,0:T(8,128)(2,1)S(1)}, bf16[576,256]{1,0:T(8,128)(2,1)S(1)}, u32[]{:S(2)}, u32[]{:S(2)}) collective-permute-start(bf16[576,256]{1,0:T(8,128)(2,1)S(1)} %get-tuple-element.71.a_ref), channel_id=1, source_target_pairs={{0,2},{2,0},{1,3},{3,1},{4,6},{6,4},{5,7},{7,5},{8,10},{10,8},{9,1... | collective-permute-start | bytes 884744 | tf_op jit(solution)/shard_map/ppermute | solution.py:370
  33.8 1.7 %collective-permute-start.14 = (bf16[72,256]{1,0:T(8,128)(2,1)S(1)}, bf16[72,256]{1,0:T(8,128)(2,1)S(1)}, u32[]{:S(2)}, u32[]{:S(2)}) collective-permute-start(bf16[72,256]{1,0:T(8,128)(2,1)S(1)} %get-tuple-element.70.refs_0_), channel_id=1, source_target_pairs={{0,8},{4,12},{8,0},{12,4},{1,9},{5,13},{9,1},{13,5},{2,10},{6,14},... | collective-permute-start | bytes 110600 | tf_op jit(solution)/shard_map/ppermute | solution.py:370
  35.4 2.0 %collective-permute-start.13 = (bf16[72,256]{1,0:T(8,128)(2,1)S(1)}, bf16[72,256]{1,0:T(8,128)(2,1)S(1)}, u32[]{:S(2)}, u32[]{:S(2)}) collective-permute-start(bf16[72,256]{1,0:T(8,128)(2,1)S(1)} %get-tuple-element.70.refs_0_), channel_id=1, source_target_pairs={{0,12},{4,8},{8,4},{12,0},{1,13},{5,9},{9,5},{13,1},{2,14},{6,10},... | collective-permute-start | bytes 110600 | tf_op jit(solution)/shard_map/ppermute | solution.py:370
  37.5 1.2 %collective-permute-done.12.b_ref.refs_4_ = bf16[64,256]{1,0:T(8,128)(2,1)S(1)} collective-permute-done((bf16[64,256]{1,0:T(8,128)(2,1)S(1)}, bf16[64,256]{1,0:T(8,128)(2,1)S(1)}, u32[]{:S(2)}, u32[]{:S(2)}) %collective-permute-start.12) | collective-permute-done | bytes 32800 | tf_op jit(solution)/shard_map/ppermute | solution.py:356
  39.0 2.2 %collective-permute-done.13.refs_2_ = bf16[72,256]{1,0:T(8,128)(2,1)S(1)} collective-permute-done((bf16[72,256]{1,0:T(8,128)(2,1)S(1)}, bf16[72,256]{1,0:T(8,128)(2,1)S(1)}, u32[]{:S(2)}, u32[]{:S(2)}) %collective-permute-start.13) | collective-permute-done | bytes 36896 | tf_op jit(solution)/shard_map/ppermute | solution.py:370
  41.4 1.2 %collective-permute-start.15 = (bf16[72,256]{1,0:T(8,128)(2,1)S(1)}, bf16[72,256]{1,0:T(8,128)(2,1)S(1)}, u32[]{:S(2)}, u32[]{:S(2)}) collective-permute-start(bf16[72,256]{1,0:T(8,128)(2,1)S(1)} %shard_map.76.refs_0_.a_ref), channel_id=1, source_target_pairs={{0,2},{2,0},{1,3},{3,1},{4,6},{6,4},{5,7},{7,5},{8,10},{10,8},{9,1... | collective-permute-start | bytes 110600 | tf_op jit(solution)/shard_map/ppermute | solution.py:370
  42.6 1.2 %shard_map.75 = (bf16[64,8,128]{2,1,0:T(8,128)(2,1)}, f32[8,128]{1,0:T(8,128)S(1)}) custom-call(bf16[8,64,256]{2,1,0:T(8,128)(2,1)S(1)} %get-tuple-element.62.g_ref, bf16[136,256]{1,0:T(8,128)(2,1)S(1)} %collective-permute-done.11.a_ref.refs_1_, bf16[64,256]{1,0:T(8,128)(2,1)S(1)} %collective-permute-done.12.b_ref.refs_4_, ...), custom_call_target="tpu_custom_call" | custom-call | flops 150994944 | bytes 573440 | tf_op jit(solution)/shard_map/pallas_call | solution.py:30
  43.7 1.1 %shard_map.78 = (f32[1152,256]{1,0:T(8,128)}, f32[8,128]{1,0:T(8,128)S(1)}) custom-call(bf16[576,256]{1,0:T(8,128)(2,1)S(1)} %shard_map.77.mine_ref, bf16[576,256]{1,0:T(8,128)(2,1)S(1)} %collective-permute-done.17.other_ref), custom_call_target="tpu_custom_call" | custom-call | flops 100000000 | bytes 1773568 | tf_op jit(solution)/shard_map/pallas_call | solution.py:30
  45.5 1.2 %collective-permute-done.18.other_ref = bf16[72,256]{1,0:T(8,128)(2,1)S(1)} collective-permute-done((bf16[72,256]{1,0:T(8,128)(2,1)S(1)}, bf16[72,256]{1,0:T(8,128)(2,1)S(1)}, u32[]{:S(2)}, u32[]{:S(2)}) %collective-permute-start.18) | collective-permute-done | bytes 36896 | tf_op jit(solution)/shard_map/ppermute | solution.py:342
  (41 shorter events, 9.4 us)
Async XLA Ops:
  0.6 10.2 %copy-start.1 = (bf16[64,3,3,64]{3,0,2,1:T(8,128)(2,1)S(1)}, bf16[64,3,3,64]{3,0,2,1:T(8,128)(2,1)}, u32[]{:S(2)}) copy-start(bf16[64,3,3,64]{3,0,2,1:T(8,128)(2,1)} %param.5) | copy-start | bytes 221188
  0.6 21.0 %copy-start = (bf16[128,3,3,256]{3,0,2,1:T(8,128)(2,1)S(1)}, bf16[128,3,3,256]{3,0,2,1:T(8,128)(2,1)}, u32[]{:S(2)}) copy-start(bf16[128,3,3,256]{3,0,2,1:T(8,128)(2,1)} %param.6) | copy-start | bytes 1769476
  1.8 6.4 %collective-permute-start.1 = (bf16[64,128]{1,0:T(8,128)(2,1)S(1)}, bf16[64,128]{1,0:T(8,128)(2,1)S(1)}, u32[]{:S(2)}, u32[]{:S(2)}) collective-permute-start(bf16[64,128]{1,0:T(8,128)(2,1)S(1)} %get-tuple-element.81), channel_id=1, source_target_pairs={{0,1},{1,0},{4,8},{5,9},{8,4},{9,5},{12,13},{13,12},{2,3},{3,2},{6... | collective-permute-start | bytes 49160 | tf_op jit(solution)/shard_map/ppermute | solution.py:356
  2.3 5.9 %collective-permute-start = (bf16[64,128]{1,0:T(8,128)(2,1)S(1)}, bf16[64,128]{1,0:T(8,128)(2,1)S(1)}, u32[]{:S(2)}, u32[]{:S(2)}) collective-permute-start(bf16[64,128]{1,0:T(8,128)(2,1)S(1)} %get-tuple-element.82), channel_id=1, source_target_pairs={{0,4},{4,0},{8,12},{12,8},{1,5},{5,1},{9,13},{13,9},{2,6},{6,2},{1... | collective-permute-start | bytes 49160 | tf_op jit(solution)/shard_map/ppermute | solution.py:342
  8.3 4.0 %collective-permute-start.2 = (bf16[144,128]{1,0:T(8,128)(2,1)S(1)}, bf16[144,128]{1,0:T(8,128)(2,1)S(1)}, u32[]{:S(2)}, u32[]{:S(2)}) collective-permute-start(bf16[144,128]{1,0:T(8,128)(2,1)S(1)} %get-tuple-element.42), channel_id=1, source_target_pairs={{0,16},{1,2},{2,1},{3,19},{16,0},{17,18},{18,17},{19,3},{4,20},{5,... | collective-permute-start | bytes 110600 | tf_op jit(solution)/shard_map/ppermute | solution.py:366
  9.9 2.4 %collective-permute-start.3 = (bf16[144,128]{1,0:T(8,128)(2,1)S(1)}, bf16[144,128]{1,0:T(8,128)(2,1)S(1)}, u32[]{:S(2)}, u32[]{:S(2)}) collective-permute-start(bf16[144,128]{1,0:T(8,128)(2,1)S(1)} %get-tuple-element.43), channel_id=1, source_target_pairs={{0,1},{1,0},{2,3},{3,2},{4,5},{5,4},{6,7},{7,6},{8,9},{9,8},{10,11... | collective-permute-start | bytes 110600 | tf_op jit(solution)/shard_map/ppermute | solution.py:342
  13.2 5.9 %collective-permute-start.6 = (bf16[2,40,256]{2,1,0:T(8,128)(2,1)S(1)}, bf16[2,40,256]{2,1,0:T(8,128)(2,1)S(1)}, u32[]{:S(2)}, u32[]{:S(2)}) collective-permute-start(bf16[2,40,256]{2,1,0:T(8,128)(2,1)S(1)} %get-tuple-element.50.refs_0_), channel_id=1, source_target_pairs={{0,8},{4,12},{8,0},{12,4},{1,9},{5,13},{9,1},{13,5},{2,10},{6,14},... | collective-permute-start | bytes 122888 | tf_op jit(solution)/shard_map/ppermute | solution.py:370
  15.1 5.8 %collective-permute-start.5 = (bf16[2,40,256]{2,1,0:T(8,128)(2,1)S(1)}, bf16[2,40,256]{2,1,0:T(8,128)(2,1)S(1)}, u32[]{:S(2)}, u32[]{:S(2)}) collective-permute-start(bf16[2,40,256]{2,1,0:T(8,128)(2,1)S(1)} %get-tuple-element.50.refs_0_), channel_id=1, source_target_pairs={{0,12},{4,8},{8,4},{12,0},{1,13},{5,9},{9,5},{13,1},{2,14},{6,10},... | collective-permute-start | bytes 122888 | tf_op jit(solution)/shard_map/ppermute | solution.py:370
  17.6 4.0 %collective-permute-start.4 = (bf16[2,40,256]{2,1,0:T(8,128)(2,1)S(1)}, bf16[2,40,256]{2,1,0:T(8,128)(2,1)S(1)}, u32[]{:S(2)}, u32[]{:S(2)}) collective-permute-start(bf16[2,40,256]{2,1,0:T(8,128)(2,1)S(1)} %get-tuple-element.50.refs_0_), channel_id=1, source_target_pairs={{0,4},{4,0},{8,12},{12,8},{1,5},{5,1},{9,13},{13,9},{2,6},{6,2},{1... | collective-permute-start | bytes 122888 | tf_op jit(solution)/shard_map/ppermute | solution.py:370
  22.6 5.2 %collective-permute-start.7 = (bf16[72,256]{1,0:T(8,128)(2,1)S(1)}, bf16[72,256]{1,0:T(8,128)(2,1)S(1)}, u32[]{:S(2)}, u32[]{:S(2)}) collective-permute-start(bf16[72,256]{1,0:T(8,128)(2,1)S(1)} %get-tuple-element.52), channel_id=1, source_target_pairs={{0,8},{4,12},{8,0},{12,4},{1,9},{5,13},{9,1},{13,5},{2,10},{6,14},... | collective-permute-start | bytes 110600 | tf_op jit(solution)/shard_map/ppermute | solution.py:370
  23.0 5.8 %collective-permute-start.8 = (bf16[72,256]{1,0:T(8,128)(2,1)S(1)}, bf16[72,256]{1,0:T(8,128)(2,1)S(1)}, u32[]{:S(2)}, u32[]{:S(2)}) collective-permute-start(bf16[72,256]{1,0:T(8,128)(2,1)S(1)} %get-tuple-element.53), channel_id=1, source_target_pairs={{0,12},{4,8},{8,4},{12,0},{1,13},{5,9},{9,5},{13,1},{2,14},{6,10},... | collective-permute-start | bytes 110600 | tf_op jit(solution)/shard_map/ppermute | solution.py:370
  25.5 4.0 %collective-permute-start.9 = (bf16[72,256]{1,0:T(8,128)(2,1)S(1)}, bf16[72,256]{1,0:T(8,128)(2,1)S(1)}, u32[]{:S(2)}, u32[]{:S(2)}) collective-permute-start(bf16[72,256]{1,0:T(8,128)(2,1)S(1)} %get-tuple-element.54), channel_id=1, source_target_pairs={{0,4},{4,0},{8,12},{12,8},{1,5},{5,1},{9,13},{13,9},{2,6},{6,2},{1... | collective-permute-start | bytes 110600 | tf_op jit(solution)/shard_map/ppermute | solution.py:370
  30.3 1.7 %collective-permute-start.10 = (bf16[648,256]{1,0:T(8,128)(2,1)S(1)}, bf16[648,256]{1,0:T(8,128)(2,1)S(1)}, u32[]{:S(2)}, u32[]{:S(2)}) collective-permute-start(bf16[648,256]{1,0:T(8,128)(2,1)S(1)} %get-tuple-element.64), channel_id=1, source_target_pairs={{0,1},{1,0},{2,3},{3,2},{4,5},{5,4},{6,7},{7,6},{8,9},{9,8},{10,11... | collective-permute-start | bytes 995336 | tf_op jit(solution)/shard_map/ppermute | solution.py:342
  32.1 9.1 %collective-permute-start.16 = (bf16[576,256]{1,0:T(8,128)(2,1)S(1)}, bf16[576,256]{1,0:T(8,128)(2,1)S(1)}, u32[]{:S(2)}, u32[]{:S(2)}) collective-permute-start(bf16[576,256]{1,0:T(8,128)(2,1)S(1)} %get-tuple-element.71.a_ref), channel_id=1, source_target_pairs={{0,2},{2,0},{1,3},{3,1},{4,6},{6,4},{5,7},{7,5},{8,10},{10,8},{9,1... | collective-permute-start | bytes 884744 | tf_op jit(solution)/shard_map/ppermute | solution.py:370
  33.1 8.1 %collective-permute-start.11 = (bf16[136,256]{1,0:T(8,128)(2,1)S(1)}, bf16[136,256]{1,0:T(8,128)(2,1)S(1)}, u32[]{:S(2)}, u32[]{:S(2)}) collective-permute-start(bf16[136,256]{1,0:T(8,128)(2,1)S(1)} %get-tuple-element.66), channel_id=1, source_target_pairs={{0,4},{4,0},{8,12},{12,8},{1,5},{5,1},{9,13},{13,9},{2,6},{6,2},{1... | collective-permute-start | bytes 208904 | tf_op jit(solution)/shard_map/ppermute | solution.py:370
  33.8 5.2 %collective-permute-start.14 = (bf16[72,256]{1,0:T(8,128)(2,1)S(1)}, bf16[72,256]{1,0:T(8,128)(2,1)S(1)}, u32[]{:S(2)}, u32[]{:S(2)}) collective-permute-start(bf16[72,256]{1,0:T(8,128)(2,1)S(1)} %get-tuple-element.70.refs_0_), channel_id=1, source_target_pairs={{0,8},{4,12},{8,0},{12,4},{1,9},{5,13},{9,1},{13,5},{2,10},{6,14},... | collective-permute-start | bytes 110600 | tf_op jit(solution)/shard_map/ppermute | solution.py:370
  35.4 5.8 %collective-permute-start.13 = (bf16[72,256]{1,0:T(8,128)(2,1)S(1)}, bf16[72,256]{1,0:T(8,128)(2,1)S(1)}, u32[]{:S(2)}, u32[]{:S(2)}) collective-permute-start(bf16[72,256]{1,0:T(8,128)(2,1)S(1)} %get-tuple-element.70.refs_0_), channel_id=1, source_target_pairs={{0,12},{4,8},{8,4},{12,0},{1,13},{5,9},{9,5},{13,1},{2,14},{6,10},... | collective-permute-start | bytes 110600 | tf_op jit(solution)/shard_map/ppermute | solution.py:370
  37.5 1.2 %collective-permute-start.12 = (bf16[64,256]{1,0:T(8,128)(2,1)S(1)}, bf16[64,256]{1,0:T(8,128)(2,1)S(1)}, u32[]{:S(2)}, u32[]{:S(2)}) collective-permute-start(bf16[64,256]{1,0:T(8,128)(2,1)S(1)} %get-tuple-element.67), channel_id=1, source_target_pairs={{0,1},{1,0},{4,8},{5,9},{8,4},{9,5},{12,13},{13,12},{2,3},{3,2},{6... | collective-permute-start | bytes 98312 | tf_op jit(solution)/shard_map/ppermute | solution.py:356
  41.3 2.4 %collective-permute-start.17 = (bf16[576,256]{1,0:T(8,128)(2,1)S(1)}, bf16[576,256]{1,0:T(8,128)(2,1)S(1)}, u32[]{:S(2)}, u32[]{:S(2)}) collective-permute-start(bf16[576,256]{1,0:T(8,128)(2,1)S(1)} %shard_map.77.mine_ref), channel_id=1, source_target_pairs={{0,1},{1,0},{2,3},{3,2},{4,5},{5,4},{6,7},{7,6},{8,9},{9,8},{10,11... | collective-permute-start | bytes 884744 | tf_op jit(solution)/shard_map/ppermute | solution.py:342
  41.4 4.0 %collective-permute-start.15 = (bf16[72,256]{1,0:T(8,128)(2,1)S(1)}, bf16[72,256]{1,0:T(8,128)(2,1)S(1)}, u32[]{:S(2)}, u32[]{:S(2)}) collective-permute-start(bf16[72,256]{1,0:T(8,128)(2,1)S(1)} %shard_map.76.refs_0_.a_ref), channel_id=1, source_target_pairs={{0,2},{2,0},{1,3},{3,1},{4,6},{6,4},{5,7},{7,5},{8,10},{10,8},{9,1... | collective-permute-start | bytes 110600 | tf_op jit(solution)/shard_map/ppermute | solution.py:370
  45.4 1.3 %collective-permute-start.18 = (bf16[72,256]{1,0:T(8,128)(2,1)S(1)}, bf16[72,256]{1,0:T(8,128)(2,1)S(1)}, u32[]{:S(2)}, u32[]{:S(2)}) collective-permute-start(bf16[72,256]{1,0:T(8,128)(2,1)S(1)} %shard_map.79.mine_ref), channel_id=1, source_target_pairs={{0,1},{1,0},{2,3},{3,2},{4,5},{5,4},{6,7},{7,6},{8,9},{9,8},{10,11... | collective-permute-start | bytes 110600 | tf_op jit(solution)/shard_map/ppermute | solution.py:342

commit v20 on v15

--- a/solution.py
+++ b/solution.py
@@ -371,7 +371,7 @@
 
 
 def row_order(bands, near_first=False):
-    far_first = sorted(range(1, bands), key=lambda k: (k < bands // 2, k))
+    far_first = list(range(bands - 1, 0, -1))
     return [0] + (far_first[::-1] if near_first else far_first)
 
 

time: 47.6 us -> 47.5 us (level)
  transfers between devices with their start and end apart: 19 -> 19, of which waited for: 14 -> 13; matrix products, arithmetic and copies ran while one was open for 2% -> 2% of each run, Pallas kernels for 7% -> 7%
where the time goes in v20:
time: 47.5 us; the launch traced here: 47.3 us
  starting transfers between devices  21 us (44%)
  waiting for transfers between devices  15.5 us (33%)
  Pallas kernels  7.06 us (15%)
  local copies, waits for them, and re-layouts  2.77 us (6%)
  between operations  0.81 us (2%)
    ppermute x11, starting transfers between devices, xor_swap(): return lax.ppermute(values, axis, [(n, n ^ k) for n in range(count)])  14.5 us
    ppermute x11, waiting for transfers between devices, xor_swap(): return lax.ppermute(values, axis, [(n, n ^ k) for n in range(count)])  9.62 us
    pallas_call x14, Pallas kernels, whole_call(): pl.pallas_call(body, out_shape=outs, in_specs=specs, out_specs=[pl.BlockS...  7.06 us
    ppermute x5, starting transfers between devices, even_swap(): return lax.ppermute(values, axis, [(n, n ^ 1) for n in range(count)])  4.45 us
    ppermute x5, waiting for transfers between devices, even_swap(): return lax.ppermute(values, axis, [(n, n ^ 1) for n in range(count)])  3.54 us
    unnamed x6, local copies, waits for them, and re-layouts  2.75 us
    ppermute x1, starting transfers between devices, odd_strip_swap(): return lax.ppermute(values, ('grp',) + COLS, steps)  1.56 us
    ppermute x2, waiting for transfers between devices, odd_row_swap(): return lax.ppermute(values, ('row', 'pair'), steps)  1.21 us
  transfers between devices with their start and end apart: 19, of which 13 were waited for; matrix products, arithmetic and copies ran while one was open for 2% of the time, Pallas kernels for 7%

profile of v20, /device:TPU:0, one launch (start us, length us, event | category | flops | bytes accessed | tf_op | source)
XLA Modules:
  0.0 47.3 jit_solution(294170757809407440)
XLA Ops:
  0.7 1.0 %copy.19 = bf16[64,8,128]{2,0,1:T(8,128)(2,1)S(1)} copy(bf16[64,8,128]{2,1,0:T(8,128)(2,1)} %param.4) | data formatting | bytes 262144 | tf_op args[0]
  2.2 4.1 %collective-permute-start = (bf16[64,128]{1,0:T(8,128)(2,1)S(1)}, bf16[64,128]{1,0:T(8,128)(2,1)S(1)}, u32[]{:S(2)}, u32[]{:S(2)}) collective-permute-start(bf16[64,128]{1,0:T(8,128)(2,1)S(1)} %get-tuple-element.72), channel_id=1, source_target_pairs={{0,4},{4,0},{8,12},{12,8},{1,5},{5,1},{9,13},{13,9},{2,6},{6,2},{1... | collective-permute-start | bytes 49160 | tf_op jit(solution)/shard_map/ppermute | solution.py:342
  8.1 1.6 %collective-permute-start.2 = (bf16[144,128]{1,0:T(8,128)(2,1)S(1)}, bf16[144,128]{1,0:T(8,128)(2,1)S(1)}, u32[]{:S(2)}, u32[]{:S(2)}) collective-permute-start(bf16[144,128]{1,0:T(8,128)(2,1)S(1)} %get-tuple-element.39), channel_id=1, source_target_pairs={{0,16},{1,2},{2,1},{3,19},{16,0},{17,18},{18,17},{19,3},{4,20},{5,... | collective-permute-start | bytes 110600 | tf_op jit(solution)/shard_map/ppermute | solution.py:366
  9.8 0.9 %copy-done.1 = bf16[64,3,3,64]{3,0,2,1:T(8,128)(2,1)S(1)} copy-done((bf16[64,3,3,64]{3,0,2,1:T(8,128)(2,1)S(1)}, bf16[64,3,3,64]{3,0,2,1:T(8,128)(2,1)}, u32[]{:S(2)}) %copy-start.1) | copy-done | bytes 73752
  10.9 1.2 %collective-permute-done.2.b_ref = bf16[144,128]{1,0:T(8,128)(2,1)S(1)} collective-permute-done((bf16[144,128]{1,0:T(8,128)(2,1)S(1)}, bf16[144,128]{1,0:T(8,128)(2,1)S(1)}, u32[]{:S(2)}, u32[]{:S(2)}) %collective-permute-start.2) | collective-permute-done | bytes 36896 | tf_op jit(solution)/shard_map/ppermute | solution.py:366
  13.0 2.6 %collective-permute-start.6 = (bf16[2,40,256]{2,1,0:T(8,128)(2,1)S(1)}, bf16[2,40,256]{2,1,0:T(8,128)(2,1)S(1)}, u32[]{:S(2)}, u32[]{:S(2)}) collective-permute-start(bf16[2,40,256]{2,1,0:T(8,128)(2,1)S(1)} %get-tuple-element.46.refs_0_), channel_id=1, source_target_pairs={{0,12},{4,8},{8,4},{12,0},{1,13},{5,9},{9,5},{13,1},{2,14},{6,10},... | collective-permute-start | bytes 122888 | tf_op jit(solution)/shard_map/ppermute | solution.py:370
  15.6 0.9 %collective-permute-start.5 = (bf16[2,40,256]{2,1,0:T(8,128)(2,1)S(1)}, bf16[2,40,256]{2,1,0:T(8,128)(2,1)S(1)}, u32[]{:S(2)}, u32[]{:S(2)}) collective-permute-start(bf16[2,40,256]{2,1,0:T(8,128)(2,1)S(1)} %get-tuple-element.46.refs_0_), channel_id=1, source_target_pairs={{0,8},{4,12},{8,0},{12,4},{1,9},{5,13},{9,1},{13,5},{2,10},{6,14},... | collective-permute-start | bytes 122888 | tf_op jit(solution)/shard_map/ppermute | solution.py:370
  16.6 0.9 %collective-permute-start.4 = (bf16[2,40,256]{2,1,0:T(8,128)(2,1)S(1)}, bf16[2,40,256]{2,1,0:T(8,128)(2,1)S(1)}, u32[]{:S(2)}, u32[]{:S(2)}) collective-permute-start(bf16[2,40,256]{2,1,0:T(8,128)(2,1)S(1)} %get-tuple-element.46.refs_0_), channel_id=1, source_target_pairs={{0,4},{4,0},{8,12},{12,8},{1,5},{5,1},{9,13},{13,9},{2,6},{6,2},{1... | collective-permute-start | bytes 122888 | tf_op jit(solution)/shard_map/ppermute | solution.py:370
  17.6 1.4 %collective-permute-done.6.refs_3_ = bf16[2,40,256]{2,1,0:T(8,128)(2,1)S(1)} collective-permute-done((bf16[2,40,256]{2,1,0:T(8,128)(2,1)S(1)}, bf16[2,40,256]{2,1,0:T(8,128)(2,1)S(1)}, u32[]{:S(2)}, u32[]{:S(2)}) %collective-permute-start.6) | collective-permute-done | bytes 40992 | tf_op jit(solution)/shard_map/ppermute | solution.py:370
  19.0 1.8 %collective-permute-done.5.refs_2_ = bf16[2,40,256]{2,1,0:T(8,128)(2,1)S(1)} collective-permute-done((bf16[2,40,256]{2,1,0:T(8,128)(2,1)S(1)}, bf16[2,40,256]{2,1,0:T(8,128)(2,1)S(1)}, u32[]{:S(2)}, u32[]{:S(2)}) %collective-permute-start.5) | collective-permute-done | bytes 40992 | tf_op jit(solution)/shard_map/ppermute | solution.py:370
  21.0 1.0 %shard_map.71 = (bf16[72,256]{1,0:T(8,128)(2,1)S(1)}, bf16[72,256]{1,0:T(8,128)(2,1)S(1)}, bf16[72,256]{1,0:T(8,128)(2,1)S(1)}, bf16[72,256]{1,0:T(8,128)(2,1)S(...) custom-call(bf16[8,48,128]{2,1,0:T(8,128)(2,1)S(1)} %fusion.6.og_ref, ...), custom_call_target="tpu_custom_call" | custom-call | flops 452984832 | bytes 1368064 | tf_op jit(solution)/shard_map/pallas_call | solution.py:30
  22.0 1.5 %collective-permute-start.7 = (bf16[72,256]{1,0:T(8,128)(2,1)S(1)}, bf16[72,256]{1,0:T(8,128)(2,1)S(1)}, u32[]{:S(2)}, u32[]{:S(2)}) collective-permute-start(bf16[72,256]{1,0:T(8,128)(2,1)S(1)} %get-tuple-element.48), channel_id=1, source_target_pairs={{0,12},{4,8},{8,4},{12,0},{1,13},{5,9},{9,5},{13,1},{2,14},{6,10},... | collective-permute-start | bytes 110600 | tf_op jit(solution)/shard_map/ppermute | solution.py:370
  24.0 2.5 %collective-permute-start.9 = (bf16[72,256]{1,0:T(8,128)(2,1)S(1)}, bf16[72,256]{1,0:T(8,128)(2,1)S(1)}, u32[]{:S(2)}, u32[]{:S(2)}) collective-permute-start(bf16[72,256]{1,0:T(8,128)(2,1)S(1)} %get-tuple-element.50), channel_id=1, source_target_pairs={{0,4},{4,0},{8,12},{12,8},{1,5},{5,1},{9,13},{13,9},{2,6},{6,2},{1... | collective-permute-start | bytes 110600 | tf_op jit(solution)/shard_map/ppermute | solution.py:370
  29.7 1.6 %collective-permute-done.10.b_ref = bf16[648,256]{1,0:T(8,128)(2,1)S(1)} collective-permute-done((bf16[648,256]{1,0:T(8,128)(2,1)S(1)}, bf16[648,256]{1,0:T(8,128)(2,1)S(1)}, u32[]{:S(2)}, u32[]{:S(2)}) %collective-permute-start.10) | collective-permute-done | bytes 331808 | tf_op jit(solution)/shard_map/ppermute | solution.py:342
  31.4 0.9 %collective-permute-start.16 = (bf16[576,256]{1,0:T(8,128)(2,1)S(1)}, bf16[576,256]{1,0:T(8,128)(2,1)S(1)}, u32[]{:S(2)}, u32[]{:S(2)}) collective-permute-start(bf16[576,256]{1,0:T(8,128)(2,1)S(1)} %get-tuple-element.67.a_ref), channel_id=1, source_target_pairs={{0,2},{2,0},{1,3},{3,1},{4,6},{6,4},{5,7},{7,5},{8,10},{10,8},{9,1... | collective-permute-start | bytes 884744 | tf_op jit(solution)/shard_map/ppermute | solution.py:370
  32.3 1.7 %collective-permute-start.11 = (bf16[136,256]{1,0:T(8,128)(2,1)S(1)}, bf16[136,256]{1,0:T(8,128)(2,1)S(1)}, u32[]{:S(2)}, u32[]{:S(2)}) collective-permute-start(bf16[136,256]{1,0:T(8,128)(2,1)S(1)} %get-tuple-element.62), channel_id=1, source_target_pairs={{0,4},{4,0},{8,12},{12,8},{1,5},{5,1},{9,13},{13,9},{2,6},{6,2},{1... | collective-permute-start | bytes 208904 | tf_op jit(solution)/shard_map/ppermute | solution.py:370
  34.0 1.3 %collective-permute-start.14 = (bf16[72,256]{1,0:T(8,128)(2,1)S(1)}, bf16[72,256]{1,0:T(8,128)(2,1)S(1)}, u32[]{:S(2)}, u32[]{:S(2)}) collective-permute-start(bf16[72,256]{1,0:T(8,128)(2,1)S(1)} %get-tuple-element.66.refs_0_), channel_id=1, source_target_pairs={{0,12},{4,8},{8,4},{12,0},{1,13},{5,9},{9,5},{13,1},{2,14},{6,10},... | collective-permute-start | bytes 110600 | tf_op jit(solution)/shard_map/ppermute | solution.py:370
  35.8 1.2 %collective-permute-done.12.b_ref.refs_4_ = bf16[64,256]{1,0:T(8,128)(2,1)S(1)} collective-permute-done((bf16[64,256]{1,0:T(8,128)(2,1)S(1)}, bf16[64,256]{1,0:T(8,128)(2,1)S(1)}, u32[]{:S(2)}, u32[]{:S(2)}) %collective-permute-start.12) | collective-permute-done | bytes 32800 | tf_op jit(solution)/shard_map/ppermute | solution.py:356
  37.0 2.8 %collective-permute-done.14.refs_3_ = bf16[72,256]{1,0:T(8,128)(2,1)S(1)} collective-permute-done((bf16[72,256]{1,0:T(8,128)(2,1)S(1)}, bf16[72,256]{1,0:T(8,128)(2,1)S(1)}, u32[]{:S(2)}, u32[]{:S(2)}) %collective-permute-start.14) | collective-permute-done | bytes 36896 | tf_op jit(solution)/shard_map/ppermute | solution.py:370
  39.8 1.1 %collective-permute-done.13.refs_2_ = bf16[72,256]{1,0:T(8,128)(2,1)S(1)} collective-permute-done((bf16[72,256]{1,0:T(8,128)(2,1)S(1)}, bf16[72,256]{1,0:T(8,128)(2,1)S(1)}, u32[]{:S(2)}, u32[]{:S(2)}) %collective-permute-start.13) | collective-permute-done | bytes 36896 | tf_op jit(solution)/shard_map/ppermute | solution.py:370
  41.1 1.2 %collective-permute-start.15 = (bf16[72,256]{1,0:T(8,128)(2,1)S(1)}, bf16[72,256]{1,0:T(8,128)(2,1)S(1)}, u32[]{:S(2)}, u32[]{:S(2)}) collective-permute-start(bf16[72,256]{1,0:T(8,128)(2,1)S(1)} %shard_map.76.refs_0_.a_ref), channel_id=1, source_target_pairs={{0,2},{2,0},{1,3},{3,1},{4,6},{6,4},{5,7},{7,5},{8,10},{10,8},{9,1... | collective-permute-start | bytes 110600 | tf_op jit(solution)/shard_map/ppermute | solution.py:370
  42.4 1.2 %shard_map.75 = (bf16[64,8,128]{2,1,0:T(8,128)(2,1)}, f32[8,128]{1,0:T(8,128)S(1)}) custom-call(bf16[8,64,256]{2,1,0:T(8,128)(2,1)S(1)} %get-tuple-element.58.g_ref, bf16[136,256]{1,0:T(8,128)(2,1)S(1)} %collective-permute-done.11.a_ref.refs_1_, bf16[64,256]{1,0:T(8,128)(2,1)S(1)} %collective-permute-done.12.b_ref.refs_4_, ...), custom_call_target="tpu_custom_call" | custom-call | flops 150994944 | bytes 573440 | tf_op jit(solution)/shard_map/pallas_call | solution.py:30
  43.5 1.1 %shard_map.78 = (f32[1152,256]{1,0:T(8,128)}, f32[8,128]{1,0:T(8,128)S(1)}) custom-call(bf16[576,256]{1,0:T(8,128)(2,1)S(1)} %shard_map.77.mine_ref, bf16[576,256]{1,0:T(8,128)(2,1)S(1)} %collective-permute-done.17.other_ref), custom_call_target="tpu_custom_call" | custom-call | flops 100000000 | bytes 1773568 | tf_op jit(solution)/shard_map/pallas_call | solution.py:30
  45.3 1.2 %collective-permute-done.18.other_ref = bf16[72,256]{1,0:T(8,128)(2,1)S(1)} collective-permute-done((bf16[72,256]{1,0:T(8,128)(2,1)S(1)}, bf16[72,256]{1,0:T(8,128)(2,1)S(1)}, u32[]{:S(2)}, u32[]{:S(2)}) %collective-permute-start.18) | collective-permute-done | bytes 36896 | tf_op jit(solution)/shard_map/ppermute | solution.py:342
  (41 shorter events, 9.7 us)
Async XLA Ops:
  0.6 20.4 %copy-start = (bf16[128,3,3,256]{3,0,2,1:T(8,128)(2,1)S(1)}, bf16[128,3,3,256]{3,0,2,1:T(8,128)(2,1)}, u32[]{:S(2)}) copy-start(bf16[128,3,3,256]{3,0,2,1:T(8,128)(2,1)} %param.6) | copy-start | bytes 1769476
  1.7 5.7 %collective-permute-start.1 = (bf16[64,128]{1,0:T(8,128)(2,1)S(1)}, bf16[64,128]{1,0:T(8,128)(2,1)S(1)}, u32[]{:S(2)}, u32[]{:S(2)}) collective-permute-start(bf16[64,128]{1,0:T(8,128)(2,1)S(1)} %get-tuple-element.71), channel_id=1, source_target_pairs={{0,1},{1,0},{4,8},{5,9},{8,4},{9,5},{12,13},{13,12},{2,3},{3,2},{6... | collective-permute-start | bytes 49160 | tf_op jit(solution)/shard_map/ppermute | solution.py:356
  2.2 5.9 %collective-permute-start = (bf16[64,128]{1,0:T(8,128)(2,1)S(1)}, bf16[64,128]{1,0:T(8,128)(2,1)S(1)}, u32[]{:S(2)}, u32[]{:S(2)}) collective-permute-start(bf16[64,128]{1,0:T(8,128)(2,1)S(1)} %get-tuple-element.72), channel_id=1, source_target_pairs={{0,4},{4,0},{8,12},{12,8},{1,5},{5,1},{9,13},{13,9},{2,6},{6,2},{1... | collective-permute-start | bytes 49160 | tf_op jit(solution)/shard_map/ppermute | solution.py:342
  8.1 4.0 %collective-permute-start.2 = (bf16[144,128]{1,0:T(8,128)(2,1)S(1)}, bf16[144,128]{1,0:T(8,128)(2,1)S(1)}, u32[]{:S(2)}, u32[]{:S(2)}) collective-permute-start(bf16[144,128]{1,0:T(8,128)(2,1)S(1)} %get-tuple-element.39), channel_id=1, source_target_pairs={{0,16},{1,2},{2,1},{3,19},{16,0},{17,18},{18,17},{19,3},{4,20},{5,... | collective-permute-start | bytes 110600 | tf_op jit(solution)/shard_map/ppermute | solution.py:366
  9.7 2.4 %collective-permute-start.3 = (bf16[144,128]{1,0:T(8,128)(2,1)S(1)}, bf16[144,128]{1,0:T(8,128)(2,1)S(1)}, u32[]{:S(2)}, u32[]{:S(2)}) collective-permute-start(bf16[144,128]{1,0:T(8,128)(2,1)S(1)} %get-tuple-element.40), channel_id=1, source_target_pairs={{0,1},{1,0},{2,3},{3,2},{4,5},{5,4},{6,7},{7,6},{8,9},{9,8},{10,11... | collective-permute-start | bytes 110600 | tf_op jit(solution)/shard_map/ppermute | solution.py:342
  9.8 0.9 %copy-start.1 = (bf16[64,3,3,64]{3,0,2,1:T(8,128)(2,1)S(1)}, bf16[64,3,3,64]{3,0,2,1:T(8,128)(2,1)}, u32[]{:S(2)}) copy-start(bf16[64,3,3,64]{3,0,2,1:T(8,128)(2,1)} %param.5) | copy-start | bytes 221188
  13.0 6.0 %collective-permute-start.6 = (bf16[2,40,256]{2,1,0:T(8,128)(2,1)S(1)}, bf16[2,40,256]{2,1,0:T(8,128)(2,1)S(1)}, u32[]{:S(2)}, u32[]{:S(2)}) collective-permute-start(bf16[2,40,256]{2,1,0:T(8,128)(2,1)S(1)} %get-tuple-element.46.refs_0_), channel_id=1, source_target_pairs={{0,12},{4,8},{8,4},{12,0},{1,13},{5,9},{9,5},{13,1},{2,14},{6,10},... | collective-permute-start | bytes 122888 | tf_op jit(solution)/shard_map/ppermute | solution.py:370
  15.6 5.1 %collective-permute-start.5 = (bf16[2,40,256]{2,1,0:T(8,128)(2,1)S(1)}, bf16[2,40,256]{2,1,0:T(8,128)(2,1)S(1)}, u32[]{:S(2)}, u32[]{:S(2)}) collective-permute-start(bf16[2,40,256]{2,1,0:T(8,128)(2,1)S(1)} %get-tuple-element.46.refs_0_), channel_id=1, source_target_pairs={{0,8},{4,12},{8,0},{12,4},{1,9},{5,13},{9,1},{13,5},{2,10},{6,14},... | collective-permute-start | bytes 122888 | tf_op jit(solution)/shard_map/ppermute | solution.py:370
  16.6 4.4 %collective-permute-start.4 = (bf16[2,40,256]{2,1,0:T(8,128)(2,1)S(1)}, bf16[2,40,256]{2,1,0:T(8,128)(2,1)S(1)}, u32[]{:S(2)}, u32[]{:S(2)}) collective-permute-start(bf16[2,40,256]{2,1,0:T(8,128)(2,1)S(1)} %get-tuple-element.46.refs_0_), channel_id=1, source_target_pairs={{0,4},{4,0},{8,12},{12,8},{1,5},{5,1},{9,13},{13,9},{2,6},{6,2},{1... | collective-permute-start | bytes 122888 | tf_op jit(solution)/shard_map/ppermute | solution.py:370
  22.0 5.8 %collective-permute-start.7 = (bf16[72,256]{1,0:T(8,128)(2,1)S(1)}, bf16[72,256]{1,0:T(8,128)(2,1)S(1)}, u32[]{:S(2)}, u32[]{:S(2)}) collective-permute-start(bf16[72,256]{1,0:T(8,128)(2,1)S(1)} %get-tuple-element.48), channel_id=1, source_target_pairs={{0,12},{4,8},{8,4},{12,0},{1,13},{5,9},{9,5},{13,1},{2,14},{6,10},... | collective-permute-start | bytes 110600 | tf_op jit(solution)/shard_map/ppermute | solution.py:370
  23.5 5.3 %collective-permute-start.8 = (bf16[72,256]{1,0:T(8,128)(2,1)S(1)}, bf16[72,256]{1,0:T(8,128)(2,1)S(1)}, u32[]{:S(2)}, u32[]{:S(2)}) collective-permute-start(bf16[72,256]{1,0:T(8,128)(2,1)S(1)} %get-tuple-element.49), channel_id=1, source_target_pairs={{0,8},{4,12},{8,0},{12,4},{1,9},{5,13},{9,1},{13,5},{2,10},{6,14},... | collective-permute-start | bytes 110600 | tf_op jit(solution)/shard_map/ppermute | solution.py:370
  24.0 4.7 %collective-permute-start.9 = (bf16[72,256]{1,0:T(8,128)(2,1)S(1)}, bf16[72,256]{1,0:T(8,128)(2,1)S(1)}, u32[]{:S(2)}, u32[]{:S(2)}) collective-permute-start(bf16[72,256]{1,0:T(8,128)(2,1)S(1)} %get-tuple-element.50), channel_id=1, source_target_pairs={{0,4},{4,0},{8,12},{12,8},{1,5},{5,1},{9,13},{13,9},{2,6},{6,2},{1... | collective-permute-start | bytes 110600 | tf_op jit(solution)/shard_map/ppermute | solution.py:370
  29.6 1.7 %collective-permute-start.10 = (bf16[648,256]{1,0:T(8,128)(2,1)S(1)}, bf16[648,256]{1,0:T(8,128)(2,1)S(1)}, u32[]{:S(2)}, u32[]{:S(2)}) collective-permute-start(bf16[648,256]{1,0:T(8,128)(2,1)S(1)} %get-tuple-element.60), channel_id=1, source_target_pairs={{0,1},{1,0},{2,3},{3,2},{4,5},{5,4},{6,7},{7,6},{8,9},{9,8},{10,11... | collective-permute-start | bytes 995336 | tf_op jit(solution)/shard_map/ppermute | solution.py:342
  31.4 9.6 %collective-permute-start.16 = (bf16[576,256]{1,0:T(8,128)(2,1)S(1)}, bf16[576,256]{1,0:T(8,128)(2,1)S(1)}, u32[]{:S(2)}, u32[]{:S(2)}) collective-permute-start(bf16[576,256]{1,0:T(8,128)(2,1)S(1)} %get-tuple-element.67.a_ref), channel_id=1, source_target_pairs={{0,2},{2,0},{1,3},{3,1},{4,6},{6,4},{5,7},{7,5},{8,10},{10,8},{9,1... | collective-permute-start | bytes 884744 | tf_op jit(solution)/shard_map/ppermute | solution.py:370
  32.3 8.6 %collective-permute-start.11 = (bf16[136,256]{1,0:T(8,128)(2,1)S(1)}, bf16[136,256]{1,0:T(8,128)(2,1)S(1)}, u32[]{:S(2)}, u32[]{:S(2)}) collective-permute-start(bf16[136,256]{1,0:T(8,128)(2,1)S(1)} %get-tuple-element.62), channel_id=1, source_target_pairs={{0,4},{4,0},{8,12},{12,8},{1,5},{5,1},{9,13},{13,9},{2,6},{6,2},{1... | collective-permute-start | bytes 208904 | tf_op jit(solution)/shard_map/ppermute | solution.py:370
  34.0 5.8 %collective-permute-start.14 = (bf16[72,256]{1,0:T(8,128)(2,1)S(1)}, bf16[72,256]{1,0:T(8,128)(2,1)S(1)}, u32[]{:S(2)}, u32[]{:S(2)}) collective-permute-start(bf16[72,256]{1,0:T(8,128)(2,1)S(1)} %get-tuple-element.66.refs_0_), channel_id=1, source_target_pairs={{0,12},{4,8},{8,4},{12,0},{1,13},{5,9},{9,5},{13,1},{2,14},{6,10},... | collective-permute-start | bytes 110600 | tf_op jit(solution)/shard_map/ppermute | solution.py:370
  35.4 5.5 %collective-permute-start.13 = (bf16[72,256]{1,0:T(8,128)(2,1)S(1)}, bf16[72,256]{1,0:T(8,128)(2,1)S(1)}, u32[]{:S(2)}, u32[]{:S(2)}) collective-permute-start(bf16[72,256]{1,0:T(8,128)(2,1)S(1)} %get-tuple-element.66.refs_0_), channel_id=1, source_target_pairs={{0,8},{4,12},{8,0},{12,4},{1,9},{5,13},{9,1},{13,5},{2,10},{6,14},... | collective-permute-start | bytes 110600 | tf_op jit(solution)/shard_map/ppermute | solution.py:370
  35.8 1.2 %collective-permute-start.12 = (bf16[64,256]{1,0:T(8,128)(2,1)S(1)}, bf16[64,256]{1,0:T(8,128)(2,1)S(1)}, u32[]{:S(2)}, u32[]{:S(2)}) collective-permute-start(bf16[64,256]{1,0:T(8,128)(2,1)S(1)} %get-tuple-element.63), channel_id=1, source_target_pairs={{0,1},{1,0},{4,8},{5,9},{8,4},{9,5},{12,13},{13,12},{2,3},{3,2},{6... | collective-permute-start | bytes 98312 | tf_op jit(solution)/shard_map/ppermute | solution.py:356
  41.1 2.5 %collective-permute-start.17 = (bf16[576,256]{1,0:T(8,128)(2,1)S(1)}, bf16[576,256]{1,0:T(8,128)(2,1)S(1)}, u32[]{:S(2)}, u32[]{:S(2)}) collective-permute-start(bf16[576,256]{1,0:T(8,128)(2,1)S(1)} %shard_map.77.mine_ref), channel_id=1, source_target_pairs={{0,1},{1,0},{2,3},{3,2},{4,5},{5,4},{6,7},{7,6},{8,9},{9,8},{10,11... | collective-permute-start | bytes 884744 | tf_op jit(solution)/shard_map/ppermute | solution.py:342
  41.1 4.0 %collective-permute-start.15 = (bf16[72,256]{1,0:T(8,128)(2,1)S(1)}, bf16[72,256]{1,0:T(8,128)(2,1)S(1)}, u32[]{:S(2)}, u32[]{:S(2)}) collective-permute-start(bf16[72,256]{1,0:T(8,128)(2,1)S(1)} %shard_map.76.refs_0_.a_ref), channel_id=1, source_target_pairs={{0,2},{2,0},{1,3},{3,1},{4,6},{6,4},{5,7},{7,5},{8,10},{10,8},{9,1... | collective-permute-start | bytes 110600 | tf_op jit(solution)/shard_map/ppermute | solution.py:370
  45.2 1.3 %collective-permute-start.18 = (bf16[72,256]{1,0:T(8,128)(2,1)S(1)}, bf16[72,256]{1,0:T(8,128)(2,1)S(1)}, u32[]{:S(2)}, u32[]{:S(2)}) collective-permute-start(bf16[72,256]{1,0:T(8,128)(2,1)S(1)} %shard_map.79.mine_ref), channel_id=1, source_target_pairs={{0,1},{1,0},{2,3},{3,2},{4,5},{5,4},{6,7},{7,6},{8,9},{9,8},{10,11... | collective-permute-start | bytes 110600 | tf_op jit(solution)/shard_map/ppermute | solution.py:342

commit v21 on v20

--- a/solution.py
+++ b/solution.py
@@ -254,14 +254,8 @@
     joined_ref[border:] = total[half:]
 
 
-def sum_rows(*refs):
-    *refs, _, out_ref = refs
-    rows = out_ref.shape[0]
-    terms = dict(zip(row_order(len(refs), near_first=True), (ref[-rows:].astype(F32) for ref in refs)))
-    terms = [terms[k] for k in range(len(refs))]
-    while len(terms) > 1:
-        terms = [a + b for a, b in zip(terms[::2], terms[1::2])]
-    out_ref[...] = terms[0].astype(BF16)
+def add_near(a_ref, near_ref, _, out_ref):
+    out_ref[...] = (a_ref[...].astype(F32) + near_ref[-a_ref.shape[0] :].astype(F32)).astype(BF16)
 
 
 def grad_pre_one(*refs, bands):
@@ -486,10 +480,12 @@
     )
     columns = lax.axis_size("col")
     two, two_more = sum_but_last(two, "col", columns)
-    ones = row_swaps([one, joined] + [one] * (bands - 2), bands, near_first=True)
-    near = ones[row_order(bands, near_first=True).index(1)]
-    up_b = odd_row_swap(up_b)
-    (one,) = whole_call(sum_rows, [shaped(one.shape)], ones + [up_b], 0, after=1)
+    near, up_b = xor_swap(joined, "row", bands, 1), odd_row_swap(up_b)
+    (one,) = whole_call(add_near, [shaped(one.shape)], [one, near, up_b], 0, after=1)
+    step = 2
+    while step < bands:
+        one = added(one, xor_swap(one, "row", bands, step))
+        step *= 2
     input_grad, done = whole_call(
         functools.partial(layer_one_back, bands=bands),
         [shaped(features_in.shape), shaped((8, 128), F32)],

time: 47.5 us -> 48.1 us (1.013)
  starting transfers between devices: 21 us -> 21.8 us
    ppermute x11 -> x10, starting transfers between devices: 14.5 us -> 15.3 us  [xor_swap(): return lax.ppermute(values, axis, [(n, n ^ k) for n in range(count)])]
    ppermute x11 -> x10, waiting for transfers between devices: 9.62 us -> 9.4 us  [xor_swap(): return lax.ppermute(values, axis, [(n, n ^ k) for n in range(count)])]
    pallas_call x14 -> x15, Pallas kernels: 7.06 us -> 7.07 us  [whole_call(): pl.pallas_call(body, out_shape=outs, in_specs=specs, out_specs=[pl.BlockS...]
  transfers between devices with their start and end apart: 19 -> 18, of which waited for: 13 -> 13; matrix products, arithmetic and copies ran while one was open for 2% -> 2% of each run, Pallas kernels for 7% -> 7%
where the time goes in v21:
time: 48.1 us; the launch traced here: 47.9 us
  starting transfers between devices  21.8 us (45%)
  waiting for transfers between devices  15.3 us (32%)
  Pallas kernels  7.07 us (15%)
  local copies, waits for them, and re-layouts  2.77 us (6%)
  between operations  0.81 us (2%)
    ppermute x10, starting transfers between devices, xor_swap(): return lax.ppermute(values, axis, [(n, n ^ k) for n in range(count)])  15.3 us
    ppermute x10, waiting for transfers between devices, xor_swap(): return lax.ppermute(values, axis, [(n, n ^ k) for n in range(count)])  9.4 us
    pallas_call x15, Pallas kernels, whole_call(): pl.pallas_call(body, out_shape=outs, in_specs=specs, out_specs=[pl.BlockS...  7.07 us
    ppermute x5, starting transfers between devices, even_swap(): return lax.ppermute(values, axis, [(n, n ^ 1) for n in range(count)])  4.45 us
    ppermute x5, waiting for transfers between devices, even_swap(): return lax.ppermute(values, axis, [(n, n ^ 1) for n in range(count)])  3.54 us
    unnamed x6, local copies, waits for them, and re-layouts  2.75 us
    ppermute x1, starting transfers between devices, odd_strip_swap(): return lax.ppermute(values, ('grp',) + COLS, steps)  1.56 us
    ppermute x2, waiting for transfers between devices, odd_row_swap(): return lax.ppermute(values, ('row', 'pair'), steps)  1.21 us
  transfers between devices with their start and end apart: 18, of which 13 were waited for; matrix products, arithmetic and copies ran while one was open for 2% of the time, Pallas kernels for 7%

profile of v21, /device:TPU:0, one launch (start us, length us, event | category | flops | bytes accessed | tf_op | source)
XLA Modules:
  0.0 47.9 jit_solution(12251760400038501660)
XLA Ops:
  0.7 1.0 %copy.19 = bf16[64,8,128]{2,0,1:T(8,128)(2,1)S(1)} copy(bf16[64,8,128]{2,1,0:T(8,128)(2,1)} %param.4) | data formatting | bytes 262144 | tf_op args[0]
  2.2 4.1 %collective-permute-start = (bf16[64,128]{1,0:T(8,128)(2,1)S(1)}, bf16[64,128]{1,0:T(8,128)(2,1)S(1)}, u32[]{:S(2)}, u32[]{:S(2)}) collective-permute-start(bf16[64,128]{1,0:T(8,128)(2,1)S(1)} %get-tuple-element.72), channel_id=1, source_target_pairs={{0,4},{4,0},{8,12},{12,8},{1,5},{5,1},{9,13},{13,9},{2,6},{6,2},{1... | collective-permute-start | bytes 49160 | tf_op jit(solution)/shard_map/ppermute | solution.py:336
  8.1 1.6 %collective-permute-start.2 = (bf16[144,128]{1,0:T(8,128)(2,1)S(1)}, bf16[144,128]{1,0:T(8,128)(2,1)S(1)}, u32[]{:S(2)}, u32[]{:S(2)}) collective-permute-start(bf16[144,128]{1,0:T(8,128)(2,1)S(1)} %get-tuple-element.39), channel_id=1, source_target_pairs={{0,16},{1,2},{2,1},{3,19},{16,0},{17,18},{18,17},{19,3},{4,20},{5,... | collective-permute-start | bytes 110600 | tf_op jit(solution)/shard_map/ppermute | solution.py:360
  9.8 0.9 %copy-done.1 = bf16[64,3,3,64]{3,0,2,1:T(8,128)(2,1)S(1)} copy-done((bf16[64,3,3,64]{3,0,2,1:T(8,128)(2,1)S(1)}, bf16[64,3,3,64]{3,0,2,1:T(8,128)(2,1)}, u32[]{:S(2)}) %copy-start.1) | copy-done | bytes 73752
  10.9 1.2 %collective-permute-done.2.b_ref = bf16[144,128]{1,0:T(8,128)(2,1)S(1)} collective-permute-done((bf16[144,128]{1,0:T(8,128)(2,1)S(1)}, bf16[144,128]{1,0:T(8,128)(2,1)S(1)}, u32[]{:S(2)}, u32[]{:S(2)}) %collective-permute-start.2) | collective-permute-done | bytes 36896 | tf_op jit(solution)/shard_map/ppermute | solution.py:360
  13.0 2.6 %collective-permute-start.6 = (bf16[2,40,256]{2,1,0:T(8,128)(2,1)S(1)}, bf16[2,40,256]{2,1,0:T(8,128)(2,1)S(1)}, u32[]{:S(2)}, u32[]{:S(2)}) collective-permute-start(bf16[2,40,256]{2,1,0:T(8,128)(2,1)S(1)} %get-tuple-element.46.refs_0_), channel_id=1, source_target_pairs={{0,12},{4,8},{8,4},{12,0},{1,13},{5,9},{9,5},{13,1},{2,14},{6,10},... | collective-permute-start | bytes 122888 | tf_op jit(solution)/shard_map/ppermute | solution.py:364
  15.6 0.9 %collective-permute-start.5 = (bf16[2,40,256]{2,1,0:T(8,128)(2,1)S(1)}, bf16[2,40,256]{2,1,0:T(8,128)(2,1)S(1)}, u32[]{:S(2)}, u32[]{:S(2)}) collective-permute-start(bf16[2,40,256]{2,1,0:T(8,128)(2,1)S(1)} %get-tuple-element.46.refs_0_), channel_id=1, source_target_pairs={{0,8},{4,12},{8,0},{12,4},{1,9},{5,13},{9,1},{13,5},{2,10},{6,14},... | collective-permute-start | bytes 122888 | tf_op jit(solution)/shard_map/ppermute | solution.py:364
  16.6 0.9 %collective-permute-start.4 = (bf16[2,40,256]{2,1,0:T(8,128)(2,1)S(1)}, bf16[2,40,256]{2,1,0:T(8,128)(2,1)S(1)}, u32[]{:S(2)}, u32[]{:S(2)}) collective-permute-start(bf16[2,40,256]{2,1,0:T(8,128)(2,1)S(1)} %get-tuple-element.46.refs_0_), channel_id=1, source_target_pairs={{0,4},{4,0},{8,12},{12,8},{1,5},{5,1},{9,13},{13,9},{2,6},{6,2},{1... | collective-permute-start | bytes 122888 | tf_op jit(solution)/shard_map/ppermute | solution.py:364
  17.6 1.4 %collective-permute-done.6.refs_3_ = bf16[2,40,256]{2,1,0:T(8,128)(2,1)S(1)} collective-permute-done((bf16[2,40,256]{2,1,0:T(8,128)(2,1)S(1)}, bf16[2,40,256]{2,1,0:T(8,128)(2,1)S(1)}, u32[]{:S(2)}, u32[]{:S(2)}) %collective-permute-start.6) | collective-permute-done | bytes 40992 | tf_op jit(solution)/shard_map/ppermute | solution.py:364
  19.0 1.8 %collective-permute-done.5.refs_2_ = bf16[2,40,256]{2,1,0:T(8,128)(2,1)S(1)} collective-permute-done((bf16[2,40,256]{2,1,0:T(8,128)(2,1)S(1)}, bf16[2,40,256]{2,1,0:T(8,128)(2,1)S(1)}, u32[]{:S(2)}, u32[]{:S(2)}) %collective-permute-start.5) | collective-permute-done | bytes 40992 | tf_op jit(solution)/shard_map/ppermute | solution.py:364
  21.0 1.0 %shard_map.71 = (bf16[72,256]{1,0:T(8,128)(2,1)S(1)}, bf16[72,256]{1,0:T(8,128)(2,1)S(1)}, bf16[72,256]{1,0:T(8,128)(2,1)S(1)}, bf16[72,256]{1,0:T(8,128)(2,1)S(...) custom-call(bf16[8,48,128]{2,1,0:T(8,128)(2,1)S(1)} %fusion.6.og_ref, ...), custom_call_target="tpu_custom_call" | custom-call | flops 452984832 | bytes 1368064 | tf_op jit(solution)/shard_map/pallas_call | solution.py:30
  22.0 1.5 %collective-permute-start.7 = (bf16[72,256]{1,0:T(8,128)(2,1)S(1)}, bf16[72,256]{1,0:T(8,128)(2,1)S(1)}, u32[]{:S(2)}, u32[]{:S(2)}) collective-permute-start(bf16[72,256]{1,0:T(8,128)(2,1)S(1)} %get-tuple-element.48), channel_id=1, source_target_pairs={{0,12},{4,8},{8,4},{12,0},{1,13},{5,9},{9,5},{13,1},{2,14},{6,10},... | collective-permute-start | bytes 110600 | tf_op jit(solution)/shard_map/ppermute | solution.py:364
  24.0 2.5 %collective-permute-start.9 = (bf16[72,256]{1,0:T(8,128)(2,1)S(1)}, bf16[72,256]{1,0:T(8,128)(2,1)S(1)}, u32[]{:S(2)}, u32[]{:S(2)}) collective-permute-start(bf16[72,256]{1,0:T(8,128)(2,1)S(1)} %get-tuple-element.50), channel_id=1, source_target_pairs={{0,4},{4,0},{8,12},{12,8},{1,5},{5,1},{9,13},{13,9},{2,6},{6,2},{1... | collective-permute-start | bytes 110600 | tf_op jit(solution)/shard_map/ppermute | solution.py:364
  29.7 1.6 %collective-permute-done.10.b_ref = bf16[648,256]{1,0:T(8,128)(2,1)S(1)} collective-permute-done((bf16[648,256]{1,0:T(8,128)(2,1)S(1)}, bf16[648,256]{1,0:T(8,128)(2,1)S(1)}, u32[]{:S(2)}, u32[]{:S(2)}) %collective-permute-start.10) | collective-permute-done | bytes 331808 | tf_op jit(solution)/shard_map/ppermute | solution.py:336
  31.4 0.9 %collective-permute-start.15 = (bf16[576,256]{1,0:T(8,128)(2,1)S(1)}, bf16[576,256]{1,0:T(8,128)(2,1)S(1)}, u32[]{:S(2)}, u32[]{:S(2)}) collective-permute-start(bf16[576,256]{1,0:T(8,128)(2,1)S(1)} %get-tuple-element.67.a_ref), channel_id=1, source_target_pairs={{0,2},{2,0},{1,3},{3,1},{4,6},{6,4},{5,7},{7,5},{8,10},{10,8},{9,1... | collective-permute-start | bytes 884744 | tf_op jit(solution)/shard_map/ppermute | solution.py:364
  32.3 1.7 %collective-permute-start.11 = (bf16[136,256]{1,0:T(8,128)(2,1)S(1)}, bf16[136,256]{1,0:T(8,128)(2,1)S(1)}, u32[]{:S(2)}, u32[]{:S(2)}) collective-permute-start(bf16[136,256]{1,0:T(8,128)(2,1)S(1)} %get-tuple-element.62), channel_id=1, source_target_pairs={{0,4},{4,0},{8,12},{12,8},{1,5},{5,1},{9,13},{13,9},{2,6},{6,2},{1... | collective-permute-start | bytes 208904 | tf_op jit(solution)/shard_map/ppermute | solution.py:364
  34.0 1.2 %collective-permute-done.12.b_ref._ = bf16[64,256]{1,0:T(8,128)(2,1)S(1)} collective-permute-done((bf16[64,256]{1,0:T(8,128)(2,1)S(1)}, bf16[64,256]{1,0:T(8,128)(2,1)S(1)}, u32[]{:S(2)}, u32[]{:S(2)}) %collective-permute-start.12) | collective-permute-done | bytes 32800 | tf_op jit(solution)/shard_map/ppermute | solution.py:350
  35.2 1.4 %collective-permute-done.11.a_ref.near_ref = bf16[136,256]{1,0:T(8,128)(2,1)S(1)} collective-permute-done((bf16[136,256]{1,0:T(8,128)(2,1)S(1)}, bf16[136,256]{1,0:T(8,128)(2,1)S(1)}, u32[]{:S(2)}, u32[]{:S(2)}) %collective-permute-start.11) | collective-permute-done | bytes 69664 | tf_op jit(solution)/shard_map/ppermute | solution.py:364
  36.6 2.5 %collective-permute-start.13 = (bf16[72,256]{1,0:T(8,128)(2,1)S(1)}, bf16[72,256]{1,0:T(8,128)(2,1)S(1)}, u32[]{:S(2)}, u32[]{:S(2)}) collective-permute-start(bf16[72,256]{1,0:T(8,128)(2,1)S(1)} %shard_map.76.a_ref), channel_id=1, source_target_pairs={{0,8},{4,12},{8,0},{12,4},{1,9},{5,13},{9,1},{13,5},{2,10},{6,14},... | collective-permute-start | bytes 110600 | tf_op jit(solution)/shard_map/ppermute | solution.py:364
  39.1 2.4 %collective-permute-done.13.b_ref = bf16[72,256]{1,0:T(8,128)(2,1)S(1)} collective-permute-done((bf16[72,256]{1,0:T(8,128)(2,1)S(1)}, bf16[72,256]{1,0:T(8,128)(2,1)S(1)}, u32[]{:S(2)}, u32[]{:S(2)}) %collective-permute-start.13) | collective-permute-done | bytes 36896 | tf_op jit(solution)/shard_map/ppermute | solution.py:364
  41.7 1.3 %collective-permute-start.14 = (bf16[72,256]{1,0:T(8,128)(2,1)S(1)}, bf16[72,256]{1,0:T(8,128)(2,1)S(1)}, u32[]{:S(2)}, u32[]{:S(2)}) collective-permute-start(bf16[72,256]{1,0:T(8,128)(2,1)S(1)} %shard_map.77.refs_0_.a_ref), channel_id=1, source_target_pairs={{0,2},{2,0},{1,3},{3,1},{4,6},{6,4},{5,7},{7,5},{8,10},{10,8},{9,1... | collective-permute-start | bytes 110600 | tf_op jit(solution)/shard_map/ppermute | solution.py:364
  43.0 1.2 %shard_map.75 = (bf16[64,8,128]{2,1,0:T(8,128)(2,1)}, f32[8,128]{1,0:T(8,128)S(1)}) custom-call(bf16[8,64,256]{2,1,0:T(8,128)(2,1)S(1)} %get-tuple-element.58.g_ref, bf16[136,256]{1,0:T(8,128)(2,1)S(1)} %collective-permute-done.11.a_ref.near_ref, bf16[64,256]{1,0:T(8,128)(2,1)S(1)} %collective-permute-done.12.b_ref._, ...), custom_call_target="tpu_custom_call" | custom-call | flops 150994944 | bytes 573440 | tf_op jit(solution)/shard_map/pallas_call | solution.py:30
  44.2 1.1 %shard_map.79 = (f32[1152,256]{1,0:T(8,128)}, f32[8,128]{1,0:T(8,128)S(1)}) custom-call(bf16[576,256]{1,0:T(8,128)(2,1)S(1)} %shard_map.78.mine_ref, bf16[576,256]{1,0:T(8,128)(2,1)S(1)} %collective-permute-done.16.other_ref), custom_call_target="tpu_custom_call" | custom-call | flops 100000000 | bytes 1773568 | tf_op jit(solution)/shard_map/pallas_call | solution.py:30
  45.8 1.2 %collective-permute-done.17.other_ref = bf16[72,256]{1,0:T(8,128)(2,1)S(1)} collective-permute-done((bf16[72,256]{1,0:T(8,128)(2,1)S(1)}, bf16[72,256]{1,0:T(8,128)(2,1)S(1)}, u32[]{:S(2)}, u32[]{:S(2)}) %collective-permute-start.17) | collective-permute-done | bytes 36896 | tf_op jit(solution)/shard_map/ppermute | solution.py:336
  (40 shorter events, 9.3 us)
Async XLA Ops:
  0.6 20.4 %copy-start = (bf16[128,3,3,256]{3,0,2,1:T(8,128)(2,1)S(1)}, bf16[128,3,3,256]{3,0,2,1:T(8,128)(2,1)}, u32[]{:S(2)}) copy-start(bf16[128,3,3,256]{3,0,2,1:T(8,128)(2,1)} %param.6) | copy-start | bytes 1769476
  1.7 5.7 %collective-permute-start.1 = (bf16[64,128]{1,0:T(8,128)(2,1)S(1)}, bf16[64,128]{1,0:T(8,128)(2,1)S(1)}, u32[]{:S(2)}, u32[]{:S(2)}) collective-permute-start(bf16[64,128]{1,0:T(8,128)(2,1)S(1)} %get-tuple-element.71), channel_id=1, source_target_pairs={{0,1},{1,0},{4,8},{5,9},{8,4},{9,5},{12,13},{13,12},{2,3},{3,2},{6... | collective-permute-start | bytes 49160 | tf_op jit(solution)/shard_map/ppermute | solution.py:350
  2.2 5.9 %collective-permute-start = (bf16[64,128]{1,0:T(8,128)(2,1)S(1)}, bf16[64,128]{1,0:T(8,128)(2,1)S(1)}, u32[]{:S(2)}, u32[]{:S(2)}) collective-permute-start(bf16[64,128]{1,0:T(8,128)(2,1)S(1)} %get-tuple-element.72), channel_id=1, source_target_pairs={{0,4},{4,0},{8,12},{12,8},{1,5},{5,1},{9,13},{13,9},{2,6},{6,2},{1... | collective-permute-start | bytes 49160 | tf_op jit(solution)/shard_map/ppermute | solution.py:336
  8.1 4.0 %collective-permute-start.2 = (bf16[144,128]{1,0:T(8,128)(2,1)S(1)}, bf16[144,128]{1,0:T(8,128)(2,1)S(1)}, u32[]{:S(2)}, u32[]{:S(2)}) collective-permute-start(bf16[144,128]{1,0:T(8,128)(2,1)S(1)} %get-tuple-element.39), channel_id=1, source_target_pairs={{0,16},{1,2},{2,1},{3,19},{16,0},{17,18},{18,17},{19,3},{4,20},{5,... | collective-permute-start | bytes 110600 | tf_op jit(solution)/shard_map/ppermute | solution.py:360
  9.7 2.4 %collective-permute-start.3 = (bf16[144,128]{1,0:T(8,128)(2,1)S(1)}, bf16[144,128]{1,0:T(8,128)(2,1)S(1)}, u32[]{:S(2)}, u32[]{:S(2)}) collective-permute-start(bf16[144,128]{1,0:T(8,128)(2,1)S(1)} %get-tuple-element.40), channel_id=1, source_target_pairs={{0,1},{1,0},{2,3},{3,2},{4,5},{5,4},{6,7},{7,6},{8,9},{9,8},{10,11... | collective-permute-start | bytes 110600 | tf_op jit(solution)/shard_map/ppermute | solution.py:336
  9.8 0.9 %copy-start.1 = (bf16[64,3,3,64]{3,0,2,1:T(8,128)(2,1)S(1)}, bf16[64,3,3,64]{3,0,2,1:T(8,128)(2,1)}, u32[]{:S(2)}) copy-start(bf16[64,3,3,64]{3,0,2,1:T(8,128)(2,1)} %param.5) | copy-start | bytes 221188
  13.0 6.0 %collective-permute-start.6 = (bf16[2,40,256]{2,1,0:T(8,128)(2,1)S(1)}, bf16[2,40,256]{2,1,0:T(8,128)(2,1)S(1)}, u32[]{:S(2)}, u32[]{:S(2)}) collective-permute-start(bf16[2,40,256]{2,1,0:T(8,128)(2,1)S(1)} %get-tuple-element.46.refs_0_), channel_id=1, source_target_pairs={{0,12},{4,8},{8,4},{12,0},{1,13},{5,9},{9,5},{13,1},{2,14},{6,10},... | collective-permute-start | bytes 122888 | tf_op jit(solution)/shard_map/ppermute | solution.py:364
  15.6 5.1 %collective-permute-start.5 = (bf16[2,40,256]{2,1,0:T(8,128)(2,1)S(1)}, bf16[2,40,256]{2,1,0:T(8,128)(2,1)S(1)}, u32[]{:S(2)}, u32[]{:S(2)}) collective-permute-start(bf16[2,40,256]{2,1,0:T(8,128)(2,1)S(1)} %get-tuple-element.46.refs_0_), channel_id=1, source_target_pairs={{0,8},{4,12},{8,0},{12,4},{1,9},{5,13},{9,1},{13,5},{2,10},{6,14},... | collective-permute-start | bytes 122888 | tf_op jit(solution)/shard_map/ppermute | solution.py:364
  16.6 4.4 %collective-permute-start.4 = (bf16[2,40,256]{2,1,0:T(8,128)(2,1)S(1)}, bf16[2,40,256]{2,1,0:T(8,128)(2,1)S(1)}, u32[]{:S(2)}, u32[]{:S(2)}) collective-permute-start(bf16[2,40,256]{2,1,0:T(8,128)(2,1)S(1)} %get-tuple-element.46.refs_0_), channel_id=1, source_target_pairs={{0,4},{4,0},{8,12},{12,8},{1,5},{5,1},{9,13},{13,9},{2,6},{6,2},{1... | collective-permute-start | bytes 122888 | tf_op jit(solution)/shard_map/ppermute | solution.py:364
  22.0 5.8 %collective-permute-start.7 = (bf16[72,256]{1,0:T(8,128)(2,1)S(1)}, bf16[72,256]{1,0:T(8,128)(2,1)S(1)}, u32[]{:S(2)}, u32[]{:S(2)}) collective-permute-start(bf16[72,256]{1,0:T(8,128)(2,1)S(1)} %get-tuple-element.48), channel_id=1, source_target_pairs={{0,12},{4,8},{8,4},{12,0},{1,13},{5,9},{9,5},{13,1},{2,14},{6,10},... | collective-permute-start | bytes 110600 | tf_op jit(solution)/shard_map/ppermute | solution.py:364
  23.5 5.3 %collective-permute-start.8 = (bf16[72,256]{1,0:T(8,128)(2,1)S(1)}, bf16[72,256]{1,0:T(8,128)(2,1)S(1)}, u32[]{:S(2)}, u32[]{:S(2)}) collective-permute-start(bf16[72,256]{1,0:T(8,128)(2,1)S(1)} %get-tuple-element.49), channel_id=1, source_target_pairs={{0,8},{4,12},{8,0},{12,4},{1,9},{5,13},{9,1},{13,5},{2,10},{6,14},... | collective-permute-start | bytes 110600 | tf_op jit(solution)/shard_map/ppermute | solution.py:364
  24.0 4.7 %collective-permute-start.9 = (bf16[72,256]{1,0:T(8,128)(2,1)S(1)}, bf16[72,256]{1,0:T(8,128)(2,1)S(1)}, u32[]{:S(2)}, u32[]{:S(2)}) collective-permute-start(bf16[72,256]{1,0:T(8,128)(2,1)S(1)} %get-tuple-element.50), channel_id=1, source_target_pairs={{0,4},{4,0},{8,12},{12,8},{1,5},{5,1},{9,13},{13,9},{2,6},{6,2},{1... | collective-permute-start | bytes 110600 | tf_op jit(solution)/shard_map/ppermute | solution.py:364
  29.6 1.7 %collective-permute-start.10 = (bf16[648,256]{1,0:T(8,128)(2,1)S(1)}, bf16[648,256]{1,0:T(8,128)(2,1)S(1)}, u32[]{:S(2)}, u32[]{:S(2)}) collective-permute-start(bf16[648,256]{1,0:T(8,128)(2,1)S(1)} %get-tuple-element.60), channel_id=1, source_target_pairs={{0,1},{1,0},{2,3},{3,2},{4,5},{5,4},{6,7},{7,6},{8,9},{9,8},{10,11... | collective-permute-start | bytes 995336 | tf_op jit(solution)/shard_map/ppermute | solution.py:336
  31.4 10.2 %collective-permute-start.15 = (bf16[576,256]{1,0:T(8,128)(2,1)S(1)}, bf16[576,256]{1,0:T(8,128)(2,1)S(1)}, u32[]{:S(2)}, u32[]{:S(2)}) collective-permute-start(bf16[576,256]{1,0:T(8,128)(2,1)S(1)} %get-tuple-element.67.a_ref), channel_id=1, source_target_pairs={{0,2},{2,0},{1,3},{3,1},{4,6},{6,4},{5,7},{7,5},{8,10},{10,8},{9,1... | collective-permute-start | bytes 884744 | tf_op jit(solution)/shard_map/ppermute | solution.py:364
  32.3 4.3 %collective-permute-start.11 = (bf16[136,256]{1,0:T(8,128)(2,1)S(1)}, bf16[136,256]{1,0:T(8,128)(2,1)S(1)}, u32[]{:S(2)}, u32[]{:S(2)}) collective-permute-start(bf16[136,256]{1,0:T(8,128)(2,1)S(1)} %get-tuple-element.62), channel_id=1, source_target_pairs={{0,4},{4,0},{8,12},{12,8},{1,5},{5,1},{9,13},{13,9},{2,6},{6,2},{1... | collective-permute-start | bytes 208904 | tf_op jit(solution)/shard_map/ppermute | solution.py:364
  34.0 1.2 %collective-permute-start.12 = (bf16[64,256]{1,0:T(8,128)(2,1)S(1)}, bf16[64,256]{1,0:T(8,128)(2,1)S(1)}, u32[]{:S(2)}, u32[]{:S(2)}) collective-permute-start(bf16[64,256]{1,0:T(8,128)(2,1)S(1)} %get-tuple-element.63), channel_id=1, source_target_pairs={{0,1},{1,0},{4,8},{5,9},{8,4},{9,5},{12,13},{13,12},{2,3},{3,2},{6... | collective-permute-start | bytes 98312 | tf_op jit(solution)/shard_map/ppermute | solution.py:350
  36.6 4.9 %collective-permute-start.13 = (bf16[72,256]{1,0:T(8,128)(2,1)S(1)}, bf16[72,256]{1,0:T(8,128)(2,1)S(1)}, u32[]{:S(2)}, u32[]{:S(2)}) collective-permute-start(bf16[72,256]{1,0:T(8,128)(2,1)S(1)} %shard_map.76.a_ref), channel_id=1, source_target_pairs={{0,8},{4,12},{8,0},{12,4},{1,9},{5,13},{9,1},{13,5},{2,10},{6,14},... | collective-permute-start | bytes 110600 | tf_op jit(solution)/shard_map/ppermute | solution.py:364
  41.6 2.5 %collective-permute-start.16 = (bf16[576,256]{1,0:T(8,128)(2,1)S(1)}, bf16[576,256]{1,0:T(8,128)(2,1)S(1)}, u32[]{:S(2)}, u32[]{:S(2)}) collective-permute-start(bf16[576,256]{1,0:T(8,128)(2,1)S(1)} %shard_map.78.mine_ref), channel_id=1, source_target_pairs={{0,1},{1,0},{2,3},{3,2},{4,5},{5,4},{6,7},{7,6},{8,9},{9,8},{10,11... | collective-permute-start | bytes 884744 | tf_op jit(solution)/shard_map/ppermute | solution.py:336
  41.7 4.0 %collective-permute-start.14 = (bf16[72,256]{1,0:T(8,128)(2,1)S(1)}, bf16[72,256]{1,0:T(8,128)(2,1)S(1)}, u32[]{:S(2)}, u32[]{:S(2)}) collective-permute-start(bf16[72,256]{1,0:T(8,128)(2,1)S(1)} %shard_map.77.refs_0_.a_ref), channel_id=1, source_target_pairs={{0,2},{2,0},{1,3},{3,1},{4,6},{6,4},{5,7},{7,5},{8,10},{10,8},{9,1... | collective-permute-start | bytes 110600 | tf_op jit(solution)/shard_map/ppermute | solution.py:364
  45.8 1.3 %collective-permute-start.17 = (bf16[72,256]{1,0:T(8,128)(2,1)S(1)}, bf16[72,256]{1,0:T(8,128)(2,1)S(1)}, u32[]{:S(2)}, u32[]{:S(2)}) collective-permute-start(bf16[72,256]{1,0:T(8,128)(2,1)S(1)} %shard_map.80.mine_ref), channel_id=1, source_target_pairs={{0,1},{1,0},{2,3},{3,2},{4,5},{5,4},{6,7},{7,6},{8,9},{9,8},{10,11... | collective-permute-start | bytes 110600 | tf_op jit(solution)/shard_map/ppermute | solution.py:336

commit v22 on v20

--- a/solution.py
+++ b/solution.py
@@ -326,10 +326,11 @@
         copy.wait()
 
 
-def finish_one(mine_ref, other_ref, out_ref, flat_ref, *, scale):
+def finish_one(mine_ref, across_ref, beside_ref, corner_ref, _, __, out_ref, flat_ref, *, scale):
     pair = lax.axis_index("pair")
-    for ref, place in ((mine_ref, pair), (other_ref, 1 - pair)):
-        flat_ref[pl.ds(pl.multiple_of(place * HALF_ONE, 8), HALF_ONE)] = ref[...].astype(F32) * scale
+    for refs, place in (((mine_ref, across_ref), pair), ((beside_ref, corner_ref), 1 - pair)):
+        total = refs[0][...].astype(F32) + refs[1][...].astype(F32)
+        flat_ref[pl.ds(pl.multiple_of(place * HALF_ONE, 8), HALF_ONE)] = total * scale
     out_ref[0, :96] = flat_ref[:96, :64]
     out_ref[1, :96] = flat_ref[:96, 64:128]
     out_ref[0, 96:] = flat_ref[:96, 128:192]
@@ -368,6 +369,12 @@
 
 def xor_swap(values, axis, count, k):
     return lax.ppermute(values, axis, [(n, n ^ k) for n in range(count)])
+
+
+def corner_swap(values, k):
+    columns, cores = lax.axis_size("col"), lax.axis_size("pair")
+    steps = [(c * cores + p, (c ^ k) * cores + (p ^ 1)) for c in range(columns) for p in range(cores)]
+    return lax.ppermute(values, COLS, steps)
 
 
 def row_order(bands, near_first=False):
@@ -505,13 +512,16 @@
         scratch=[pltpu.VMEM((2, half, 256), F32), pltpu.SemaphoreType.DMA((2,))],
         out_spaces=[pl.ANY, pltpu.VMEM],
     )
-    mine_one = added(*sum_but_last(one, "col", columns), wrote, done)
+    one, across = sum_but_last(one, "col", columns)
+    beside_one = even_swap(one, "pair", 2)
+    corner = corner_swap(one, columns // 2)
     (grad_one,) = whole_call(
         functools.partial(finish_one, scale=1.0 / math.sqrt(height * width)),
         [shaped((3, 3 * channels, channels), F32)],
-        [mine_one, even_swap(mine_one, "pair", 2)],
+        [one, across, beside_one, corner, wrote, done],
         1,
         scratch=[pltpu.VMEM((144, 256), F32)],
+        after=2,
     )
     grad_two = jnp.transpose(grad_two.reshape(3, 3, filters, 4 * channels), (2, 0, 1, 3))
     grad_one = jnp.transpose(grad_one.reshape(3, 3, channels, channels), (2, 0, 1, 3))

time: 47.5 us -> 47.5 us (level)
  starting transfers between devices: 21 us -> 22 us
  waiting for transfers between devices: 15.5 us -> 14.6 us
    ppermute x0 -> x1, starting transfers between devices: none -> 1.27 us  [corner_swap(): return lax.ppermute(values, COLS, steps)]
    ppermute x5, waiting for transfers between devices: 3.54 us -> 2.34 us  [even_swap(): return lax.ppermute(values, axis, [(n, n ^ 1) for n in range(count)])]
    pallas_call x14 -> x13, Pallas kernels: 7.06 us -> 7.08 us  [whole_call(): pl.pallas_call(body, out_shape=outs, in_specs=specs, out_specs=[pl.BlockS...]
  transfers between devices with their start and end apart: 19 -> 20, of which waited for: 13 -> 12; matrix products, arithmetic and copies ran while one was open for 2% -> 2% of each run, Pallas kernels for 7% -> 7%
where the time goes in v22:
time: 47.5 us; the launch traced here: 47.3 us
  starting transfers between devices  22 us (46%)
  waiting for transfers between devices  14.6 us (31%)
  Pallas kernels  7.08 us (15%)
  local copies, waits for them, and re-layouts  2.77 us (6%)
  between operations  0.81 us (2%)
    ppermute x11, starting transfers between devices, xor_swap(): return lax.ppermute(values, axis, [(n, n ^ k) for n in range(count)])  14.2 us
    ppermute x11, waiting for transfers between devices, xor_swap(): return lax.ppermute(values, axis, [(n, n ^ k) for n in range(count)])  9.88 us
    pallas_call x13, Pallas kernels, whole_call(): pl.pallas_call(body, out_shape=outs, in_specs=specs, out_specs=[pl.BlockS...  7.08 us
    ppermute x5, starting transfers between devices, even_swap(): return lax.ppermute(values, axis, [(n, n ^ 1) for n in range(count)])  4.44 us
    unnamed x6, local copies, waits for them, and re-layouts  2.75 us
    ppermute x5, waiting for transfers between devices, even_swap(): return lax.ppermute(values, axis, [(n, n ^ 1) for n in range(count)])  2.34 us
    ppermute x1, starting transfers between devices, odd_strip_swap(): return lax.ppermute(values, ('grp',) + COLS, steps)  1.56 us
    ppermute x1, starting transfers between devices, corner_swap(): return lax.ppermute(values, COLS, steps)  1.27 us
  transfers between devices with their start and end apart: 20, of which 12 were waited for; matrix products, arithmetic and copies ran while one was open for 2% of the time, Pallas kernels for 7%

profile of v22, /device:TPU:0, one launch (start us, length us, event | category | flops | bytes accessed | tf_op | source)
XLA Modules:
  0.0 47.3 jit_solution(12515484734678068810)
XLA Ops:
  0.7 1.0 %copy.19 = bf16[64,8,128]{2,0,1:T(8,128)(2,1)S(1)} copy(bf16[64,8,128]{2,1,0:T(8,128)(2,1)} %param.4) | data formatting | bytes 262144 | tf_op args[0]
  2.2 4.1 %collective-permute-start = (bf16[64,128]{1,0:T(8,128)(2,1)S(1)}, bf16[64,128]{1,0:T(8,128)(2,1)S(1)}, u32[]{:S(2)}, u32[]{:S(2)}) collective-permute-start(bf16[64,128]{1,0:T(8,128)(2,1)S(1)} %get-tuple-element.72), channel_id=1, source_target_pairs={{0,4},{4,0},{8,12},{12,8},{1,5},{5,1},{9,13},{13,9},{2,6},{6,2},{1... | collective-permute-start | bytes 49160 | tf_op jit(solution)/shard_map/ppermute | solution.py:343
  8.1 1.6 %collective-permute-start.2 = (bf16[144,128]{1,0:T(8,128)(2,1)S(1)}, bf16[144,128]{1,0:T(8,128)(2,1)S(1)}, u32[]{:S(2)}, u32[]{:S(2)}) collective-permute-start(bf16[144,128]{1,0:T(8,128)(2,1)S(1)} %get-tuple-element.39), channel_id=1, source_target_pairs={{0,16},{1,2},{2,1},{3,19},{16,0},{17,18},{18,17},{19,3},{4,20},{5,... | collective-permute-start | bytes 110600 | tf_op jit(solution)/shard_map/ppermute | solution.py:367
  9.8 0.9 %copy-done.1 = bf16[64,3,3,64]{3,0,2,1:T(8,128)(2,1)S(1)} copy-done((bf16[64,3,3,64]{3,0,2,1:T(8,128)(2,1)S(1)}, bf16[64,3,3,64]{3,0,2,1:T(8,128)(2,1)}, u32[]{:S(2)}) %copy-start.1) | copy-done | bytes 73752
  10.9 1.2 %collective-permute-done.2.b_ref = bf16[144,128]{1,0:T(8,128)(2,1)S(1)} collective-permute-done((bf16[144,128]{1,0:T(8,128)(2,1)S(1)}, bf16[144,128]{1,0:T(8,128)(2,1)S(1)}, u32[]{:S(2)}, u32[]{:S(2)}) %collective-permute-start.2) | collective-permute-done | bytes 36896 | tf_op jit(solution)/shard_map/ppermute | solution.py:367
  13.0 2.6 %collective-permute-start.6 = (bf16[2,40,256]{2,1,0:T(8,128)(2,1)S(1)}, bf16[2,40,256]{2,1,0:T(8,128)(2,1)S(1)}, u32[]{:S(2)}, u32[]{:S(2)}) collective-permute-start(bf16[2,40,256]{2,1,0:T(8,128)(2,1)S(1)} %get-tuple-element.46.refs_0_), channel_id=1, source_target_pairs={{0,12},{4,8},{8,4},{12,0},{1,13},{5,9},{9,5},{13,1},{2,14},{6,10},... | collective-permute-start | bytes 122888 | tf_op jit(solution)/shard_map/ppermute | solution.py:371
  15.6 0.9 %collective-permute-start.5 = (bf16[2,40,256]{2,1,0:T(8,128)(2,1)S(1)}, bf16[2,40,256]{2,1,0:T(8,128)(2,1)S(1)}, u32[]{:S(2)}, u32[]{:S(2)}) collective-permute-start(bf16[2,40,256]{2,1,0:T(8,128)(2,1)S(1)} %get-tuple-element.46.refs_0_), channel_id=1, source_target_pairs={{0,8},{4,12},{8,0},{12,4},{1,9},{5,13},{9,1},{13,5},{2,10},{6,14},... | collective-permute-start | bytes 122888 | tf_op jit(solution)/shard_map/ppermute | solution.py:371
  16.6 0.9 %collective-permute-start.4 = (bf16[2,40,256]{2,1,0:T(8,128)(2,1)S(1)}, bf16[2,40,256]{2,1,0:T(8,128)(2,1)S(1)}, u32[]{:S(2)}, u32[]{:S(2)}) collective-permute-start(bf16[2,40,256]{2,1,0:T(8,128)(2,1)S(1)} %get-tuple-element.46.refs_0_), channel_id=1, source_target_pairs={{0,4},{4,0},{8,12},{12,8},{1,5},{5,1},{9,13},{13,9},{2,6},{6,2},{1... | collective-permute-start | bytes 122888 | tf_op jit(solution)/shard_map/ppermute | solution.py:371
  17.6 1.4 %collective-permute-done.6.refs_3_ = bf16[2,40,256]{2,1,0:T(8,128)(2,1)S(1)} collective-permute-done((bf16[2,40,256]{2,1,0:T(8,128)(2,1)S(1)}, bf16[2,40,256]{2,1,0:T(8,128)(2,1)S(1)}, u32[]{:S(2)}, u32[]{:S(2)}) %collective-permute-start.6) | collective-permute-done | bytes 40992 | tf_op jit(solution)/shard_map/ppermute | solution.py:371
  19.0 1.8 %collective-permute-done.5.refs_2_ = bf16[2,40,256]{2,1,0:T(8,128)(2,1)S(1)} collective-permute-done((bf16[2,40,256]{2,1,0:T(8,128)(2,1)S(1)}, bf16[2,40,256]{2,1,0:T(8,128)(2,1)S(1)}, u32[]{:S(2)}, u32[]{:S(2)}) %collective-permute-start.5) | collective-permute-done | bytes 40992 | tf_op jit(solution)/shard_map/ppermute | solution.py:371
  21.0 1.0 %shard_map.71 = (bf16[72,256]{1,0:T(8,128)(2,1)S(1)}, bf16[72,256]{1,0:T(8,128)(2,1)S(1)}, bf16[72,256]{1,0:T(8,128)(2,1)S(1)}, bf16[72,256]{1,0:T(8,128)(2,1)S(...) custom-call(bf16[8,48,128]{2,1,0:T(8,128)(2,1)S(1)} %fusion.6.og_ref, ...), custom_call_target="tpu_custom_call" | custom-call | flops 452984832 | bytes 1368064 | tf_op jit(solution)/shard_map/pallas_call | solution.py:30
  22.0 1.5 %collective-permute-start.7 = (bf16[72,256]{1,0:T(8,128)(2,1)S(1)}, bf16[72,256]{1,0:T(8,128)(2,1)S(1)}, u32[]{:S(2)}, u32[]{:S(2)}) collective-permute-start(bf16[72,256]{1,0:T(8,128)(2,1)S(1)} %get-tuple-element.48), channel_id=1, source_target_pairs={{0,12},{4,8},{8,4},{12,0},{1,13},{5,9},{9,5},{13,1},{2,14},{6,10},... | collective-permute-start | bytes 110600 | tf_op jit(solution)/shard_map/ppermute | solution.py:371
  24.0 2.5 %collective-permute-start.9 = (bf16[72,256]{1,0:T(8,128)(2,1)S(1)}, bf16[72,256]{1,0:T(8,128)(2,1)S(1)}, u32[]{:S(2)}, u32[]{:S(2)}) collective-permute-start(bf16[72,256]{1,0:T(8,128)(2,1)S(1)} %get-tuple-element.50), channel_id=1, source_target_pairs={{0,4},{4,0},{8,12},{12,8},{1,5},{5,1},{9,13},{13,9},{2,6},{6,2},{1... | collective-permute-start | bytes 110600 | tf_op jit(solution)/shard_map/ppermute | solution.py:371
  27.8 0.9 %collective-permute-done.8.refs_2_ = bf16[72,256]{1,0:T(8,128)(2,1)S(1)} collective-permute-done((bf16[72,256]{1,0:T(8,128)(2,1)S(1)}, bf16[72,256]{1,0:T(8,128)(2,1)S(1)}, u32[]{:S(2)}, u32[]{:S(2)}) %collective-permute-start.8) | collective-permute-done | bytes 36896 | tf_op jit(solution)/shard_map/ppermute | solution.py:371
  29.7 1.6 %collective-permute-done.10.b_ref = bf16[648,256]{1,0:T(8,128)(2,1)S(1)} collective-permute-done((bf16[648,256]{1,0:T(8,128)(2,1)S(1)}, bf16[648,256]{1,0:T(8,128)(2,1)S(1)}, u32[]{:S(2)}, u32[]{:S(2)}) %collective-permute-start.10) | collective-permute-done | bytes 331808 | tf_op jit(solution)/shard_map/ppermute | solution.py:343
  31.4 0.9 %collective-permute-start.18 = (bf16[576,256]{1,0:T(8,128)(2,1)S(1)}, bf16[576,256]{1,0:T(8,128)(2,1)S(1)}, u32[]{:S(2)}, u32[]{:S(2)}) collective-permute-start(bf16[576,256]{1,0:T(8,128)(2,1)S(1)} %get-tuple-element.67.a_ref), channel_id=1, source_target_pairs={{0,2},{2,0},{1,3},{3,1},{4,6},{6,4},{5,7},{7,5},{8,10},{10,8},{9,1... | collective-permute-start | bytes 884744 | tf_op jit(solution)/shard_map/ppermute | solution.py:371
  32.3 1.7 %collective-permute-start.11 = (bf16[136,256]{1,0:T(8,128)(2,1)S(1)}, bf16[136,256]{1,0:T(8,128)(2,1)S(1)}, u32[]{:S(2)}, u32[]{:S(2)}) collective-permute-start(bf16[136,256]{1,0:T(8,128)(2,1)S(1)} %get-tuple-element.62), channel_id=1, source_target_pairs={{0,4},{4,0},{8,12},{12,8},{1,5},{5,1},{9,13},{13,9},{2,6},{6,2},{1... | collective-permute-start | bytes 208904 | tf_op jit(solution)/shard_map/ppermute | solution.py:371
  34.0 1.3 %collective-permute-start.14 = (bf16[72,256]{1,0:T(8,128)(2,1)S(1)}, bf16[72,256]{1,0:T(8,128)(2,1)S(1)}, u32[]{:S(2)}, u32[]{:S(2)}) collective-permute-start(bf16[72,256]{1,0:T(8,128)(2,1)S(1)} %get-tuple-element.66.refs_0_), channel_id=1, source_target_pairs={{0,12},{4,8},{8,4},{12,0},{1,13},{5,9},{9,5},{13,1},{2,14},{6,10},... | collective-permute-start | bytes 110600 | tf_op jit(solution)/shard_map/ppermute | solution.py:371
  35.8 1.2 %collective-permute-done.12.b_ref.refs_4_ = bf16[64,256]{1,0:T(8,128)(2,1)S(1)} collective-permute-done((bf16[64,256]{1,0:T(8,128)(2,1)S(1)}, bf16[64,256]{1,0:T(8,128)(2,1)S(1)}, u32[]{:S(2)}, u32[]{:S(2)}) %collective-permute-start.12) | collective-permute-done | bytes 32800 | tf_op jit(solution)/shard_map/ppermute | solution.py:357
  37.0 2.8 %collective-permute-done.14.refs_3_ = bf16[72,256]{1,0:T(8,128)(2,1)S(1)} collective-permute-done((bf16[72,256]{1,0:T(8,128)(2,1)S(1)}, bf16[72,256]{1,0:T(8,128)(2,1)S(1)}, u32[]{:S(2)}, u32[]{:S(2)}) %collective-permute-start.14) | collective-permute-done | bytes 36896 | tf_op jit(solution)/shard_map/ppermute | solution.py:371
  39.8 1.1 %collective-permute-done.13.refs_2_ = bf16[72,256]{1,0:T(8,128)(2,1)S(1)} collective-permute-done((bf16[72,256]{1,0:T(8,128)(2,1)S(1)}, bf16[72,256]{1,0:T(8,128)(2,1)S(1)}, u32[]{:S(2)}, u32[]{:S(2)}) %collective-permute-start.13) | collective-permute-done | bytes 36896 | tf_op jit(solution)/shard_map/ppermute | solution.py:371
  41.1 1.3 %collective-permute-start.17 = (bf16[72,256]{1,0:T(8,128)(2,1)S(1)}, bf16[72,256]{1,0:T(8,128)(2,1)S(1)}, u32[]{:S(2)}, u32[]{:S(2)}) collective-permute-start(bf16[72,256]{1,0:T(8,128)(2,1)S(1)} %shard_map.76.refs_0_.mine_ref), channel_id=1, source_target_pairs={{0,3},{1,2},{2,1},{3,0},{4,7},{5,6},{6,5},{7,4},{8,11},{9,10},{10,... | collective-permute-start | bytes 110600 | tf_op jit(solution)/shard_map/ppermute | solution.py:377
  43.3 1.2 %shard_map.75 = (bf16[64,8,128]{2,1,0:T(8,128)(2,1)}, f32[8,128]{1,0:T(8,128)S(1)}) custom-call(bf16[8,64,256]{2,1,0:T(8,128)(2,1)S(1)} %get-tuple-element.58.g_ref, bf16[136,256]{1,0:T(8,128)(2,1)S(1)} %collective-permute-done.11.a_ref.refs_1_, bf16[64,256]{1,0:T(8,128)(2,1)S(1)} %collective-permute-done.12.b_ref.refs_4_, ...), custom_call_target="tpu_custom_call" | custom-call | flops 150994944 | bytes 573440 | tf_op jit(solution)/shard_map/pallas_call | solution.py:30
  44.5 1.1 %shard_map.78 = (f32[1152,256]{1,0:T(8,128)}, f32[8,128]{1,0:T(8,128)S(1)}) custom-call(bf16[576,256]{1,0:T(8,128)(2,1)S(1)} %shard_map.77.mine_ref, bf16[576,256]{1,0:T(8,128)(2,1)S(1)} %collective-permute-done.19.other_ref), custom_call_target="tpu_custom_call" | custom-call | flops 100000000 | bytes 1773568 | tf_op jit(solution)/shard_map/pallas_call | solution.py:30
  (42 shorter events, 10.0 us)
Async XLA Ops:
  0.6 20.4 %copy-start = (bf16[128,3,3,256]{3,0,2,1:T(8,128)(2,1)S(1)}, bf16[128,3,3,256]{3,0,2,1:T(8,128)(2,1)}, u32[]{:S(2)}) copy-start(bf16[128,3,3,256]{3,0,2,1:T(8,128)(2,1)} %param.6) | copy-start | bytes 1769476
  1.7 5.7 %collective-permute-start.1 = (bf16[64,128]{1,0:T(8,128)(2,1)S(1)}, bf16[64,128]{1,0:T(8,128)(2,1)S(1)}, u32[]{:S(2)}, u32[]{:S(2)}) collective-permute-start(bf16[64,128]{1,0:T(8,128)(2,1)S(1)} %get-tuple-element.71), channel_id=1, source_target_pairs={{0,1},{1,0},{4,8},{5,9},{8,4},{9,5},{12,13},{13,12},{2,3},{3,2},{6... | collective-permute-start | bytes 49160 | tf_op jit(solution)/shard_map/ppermute | solution.py:357
  2.2 5.9 %collective-permute-start = (bf16[64,128]{1,0:T(8,128)(2,1)S(1)}, bf16[64,128]{1,0:T(8,128)(2,1)S(1)}, u32[]{:S(2)}, u32[]{:S(2)}) collective-permute-start(bf16[64,128]{1,0:T(8,128)(2,1)S(1)} %get-tuple-element.72), channel_id=1, source_target_pairs={{0,4},{4,0},{8,12},{12,8},{1,5},{5,1},{9,13},{13,9},{2,6},{6,2},{1... | collective-permute-start | bytes 49160 | tf_op jit(solution)/shard_map/ppermute | solution.py:343
  8.1 4.0 %collective-permute-start.2 = (bf16[144,128]{1,0:T(8,128)(2,1)S(1)}, bf16[144,128]{1,0:T(8,128)(2,1)S(1)}, u32[]{:S(2)}, u32[]{:S(2)}) collective-permute-start(bf16[144,128]{1,0:T(8,128)(2,1)S(1)} %get-tuple-element.39), channel_id=1, source_target_pairs={{0,16},{1,2},{2,1},{3,19},{16,0},{17,18},{18,17},{19,3},{4,20},{5,... | collective-permute-start | bytes 110600 | tf_op jit(solution)/shard_map/ppermute | solution.py:367
  9.7 2.4 %collective-permute-start.3 = (bf16[144,128]{1,0:T(8,128)(2,1)S(1)}, bf16[144,128]{1,0:T(8,128)(2,1)S(1)}, u32[]{:S(2)}, u32[]{:S(2)}) collective-permute-start(bf16[144,128]{1,0:T(8,128)(2,1)S(1)} %get-tuple-element.40), channel_id=1, source_target_pairs={{0,1},{1,0},{2,3},{3,2},{4,5},{5,4},{6,7},{7,6},{8,9},{9,8},{10,11... | collective-permute-start | bytes 110600 | tf_op jit(solution)/shard_map/ppermute | solution.py:343
  9.8 0.9 %copy-start.1 = (bf16[64,3,3,64]{3,0,2,1:T(8,128)(2,1)S(1)}, bf16[64,3,3,64]{3,0,2,1:T(8,128)(2,1)}, u32[]{:S(2)}) copy-start(bf16[64,3,3,64]{3,0,2,1:T(8,128)(2,1)} %param.5) | copy-start | bytes 221188
  13.0 6.0 %collective-permute-start.6 = (bf16[2,40,256]{2,1,0:T(8,128)(2,1)S(1)}, bf16[2,40,256]{2,1,0:T(8,128)(2,1)S(1)}, u32[]{:S(2)}, u32[]{:S(2)}) collective-permute-start(bf16[2,40,256]{2,1,0:T(8,128)(2,1)S(1)} %get-tuple-element.46.refs_0_), channel_id=1, source_target_pairs={{0,12},{4,8},{8,4},{12,0},{1,13},{5,9},{9,5},{13,1},{2,14},{6,10},... | collective-permute-start | bytes 122888 | tf_op jit(solution)/shard_map/ppermute | solution.py:371
  15.6 5.1 %collective-permute-start.5 = (bf16[2,40,256]{2,1,0:T(8,128)(2,1)S(1)}, bf16[2,40,256]{2,1,0:T(8,128)(2,1)S(1)}, u32[]{:S(2)}, u32[]{:S(2)}) collective-permute-start(bf16[2,40,256]{2,1,0:T(8,128)(2,1)S(1)} %get-tuple-element.46.refs_0_), channel_id=1, source_target_pairs={{0,8},{4,12},{8,0},{12,4},{1,9},{5,13},{9,1},{13,5},{2,10},{6,14},... | collective-permute-start | bytes 122888 | tf_op jit(solution)/shard_map/ppermute | solution.py:371
  16.6 4.4 %collective-permute-start.4 = (bf16[2,40,256]{2,1,0:T(8,128)(2,1)S(1)}, bf16[2,40,256]{2,1,0:T(8,128)(2,1)S(1)}, u32[]{:S(2)}, u32[]{:S(2)}) collective-permute-start(bf16[2,40,256]{2,1,0:T(8,128)(2,1)S(1)} %get-tuple-element.46.refs_0_), channel_id=1, source_target_pairs={{0,4},{4,0},{8,12},{12,8},{1,5},{5,1},{9,13},{13,9},{2,6},{6,2},{1... | collective-permute-start | bytes 122888 | tf_op jit(solution)/shard_map/ppermute | solution.py:371
  22.0 5.8 %collective-permute-start.7 = (bf16[72,256]{1,0:T(8,128)(2,1)S(1)}, bf16[72,256]{1,0:T(8,128)(2,1)S(1)}, u32[]{:S(2)}, u32[]{:S(2)}) collective-permute-start(bf16[72,256]{1,0:T(8,128)(2,1)S(1)} %get-tuple-element.48), channel_id=1, source_target_pairs={{0,12},{4,8},{8,4},{12,0},{1,13},{5,9},{9,5},{13,1},{2,14},{6,10},... | collective-permute-start | bytes 110600 | tf_op jit(solution)/shard_map/ppermute | solution.py:371
  23.5 5.3 %collective-permute-start.8 = (bf16[72,256]{1,0:T(8,128)(2,1)S(1)}, bf16[72,256]{1,0:T(8,128)(2,1)S(1)}, u32[]{:S(2)}, u32[]{:S(2)}) collective-permute-start(bf16[72,256]{1,0:T(8,128)(2,1)S(1)} %get-tuple-element.49), channel_id=1, source_target_pairs={{0,8},{4,12},{8,0},{12,4},{1,9},{5,13},{9,1},{13,5},{2,10},{6,14},... | collective-permute-start | bytes 110600 | tf_op jit(solution)/shard_map/ppermute | solution.py:371
  24.0 4.7 %collective-permute-start.9 = (bf16[72,256]{1,0:T(8,128)(2,1)S(1)}, bf16[72,256]{1,0:T(8,128)(2,1)S(1)}, u32[]{:S(2)}, u32[]{:S(2)}) collective-permute-start(bf16[72,256]{1,0:T(8,128)(2,1)S(1)} %get-tuple-element.50), channel_id=1, source_target_pairs={{0,4},{4,0},{8,12},{12,8},{1,5},{5,1},{9,13},{13,9},{2,6},{6,2},{1... | collective-permute-start | bytes 110600 | tf_op jit(solution)/shard_map/ppermute | solution.py:371
  29.6 1.7 %collective-permute-start.10 = (bf16[648,256]{1,0:T(8,128)(2,1)S(1)}, bf16[648,256]{1,0:T(8,128)(2,1)S(1)}, u32[]{:S(2)}, u32[]{:S(2)}) collective-permute-start(bf16[648,256]{1,0:T(8,128)(2,1)S(1)} %get-tuple-element.60), channel_id=1, source_target_pairs={{0,1},{1,0},{2,3},{3,2},{4,5},{5,4},{6,7},{7,6},{8,9},{9,8},{10,11... | collective-permute-start | bytes 995336 | tf_op jit(solution)/shard_map/ppermute | solution.py:343
  31.4 9.6 %collective-permute-start.18 = (bf16[576,256]{1,0:T(8,128)(2,1)S(1)}, bf16[576,256]{1,0:T(8,128)(2,1)S(1)}, u32[]{:S(2)}, u32[]{:S(2)}) collective-permute-start(bf16[576,256]{1,0:T(8,128)(2,1)S(1)} %get-tuple-element.67.a_ref), channel_id=1, source_target_pairs={{0,2},{2,0},{1,3},{3,1},{4,6},{6,4},{5,7},{7,5},{8,10},{10,8},{9,1... | collective-permute-start | bytes 884744 | tf_op jit(solution)/shard_map/ppermute | solution.py:371
  32.3 8.6 %collective-permute-start.11 = (bf16[136,256]{1,0:T(8,128)(2,1)S(1)}, bf16[136,256]{1,0:T(8,128)(2,1)S(1)}, u32[]{:S(2)}, u32[]{:S(2)}) collective-permute-start(bf16[136,256]{1,0:T(8,128)(2,1)S(1)} %get-tuple-element.62), channel_id=1, source_target_pairs={{0,4},{4,0},{8,12},{12,8},{1,5},{5,1},{9,13},{13,9},{2,6},{6,2},{1... | collective-permute-start | bytes 208904 | tf_op jit(solution)/shard_map/ppermute | solution.py:371
  34.0 5.8 %collective-permute-start.14 = (bf16[72,256]{1,0:T(8,128)(2,1)S(1)}, bf16[72,256]{1,0:T(8,128)(2,1)S(1)}, u32[]{:S(2)}, u32[]{:S(2)}) collective-permute-start(bf16[72,256]{1,0:T(8,128)(2,1)S(1)} %get-tuple-element.66.refs_0_), channel_id=1, source_target_pairs={{0,12},{4,8},{8,4},{12,0},{1,13},{5,9},{9,5},{13,1},{2,14},{6,10},... | collective-permute-start | bytes 110600 | tf_op jit(solution)/shard_map/ppermute | solution.py:371
  35.4 5.5 %collective-permute-start.13 = (bf16[72,256]{1,0:T(8,128)(2,1)S(1)}, bf16[72,256]{1,0:T(8,128)(2,1)S(1)}, u32[]{:S(2)}, u32[]{:S(2)}) collective-permute-start(bf16[72,256]{1,0:T(8,128)(2,1)S(1)} %get-tuple-element.66.refs_0_), channel_id=1, source_target_pairs={{0,8},{4,12},{8,0},{12,4},{1,9},{5,13},{9,1},{13,5},{2,10},{6,14},... | collective-permute-start | bytes 110600 | tf_op jit(solution)/shard_map/ppermute | solution.py:371
  35.8 1.2 %collective-permute-start.12 = (bf16[64,256]{1,0:T(8,128)(2,1)S(1)}, bf16[64,256]{1,0:T(8,128)(2,1)S(1)}, u32[]{:S(2)}, u32[]{:S(2)}) collective-permute-start(bf16[64,256]{1,0:T(8,128)(2,1)S(1)} %get-tuple-element.63), channel_id=1, source_target_pairs={{0,1},{1,0},{4,8},{5,9},{8,4},{9,5},{12,13},{13,12},{2,3},{3,2},{6... | collective-permute-start | bytes 98312 | tf_op jit(solution)/shard_map/ppermute | solution.py:357
  41.1 3.5 %collective-permute-start.19 = (bf16[576,256]{1,0:T(8,128)(2,1)S(1)}, bf16[576,256]{1,0:T(8,128)(2,1)S(1)}, u32[]{:S(2)}, u32[]{:S(2)}) collective-permute-start(bf16[576,256]{1,0:T(8,128)(2,1)S(1)} %shard_map.77.mine_ref), channel_id=1, source_target_pairs={{0,1},{1,0},{2,3},{3,2},{4,5},{5,4},{6,7},{7,6},{8,9},{9,8},{10,11... | collective-permute-start | bytes 884744 | tf_op jit(solution)/shard_map/ppermute | solution.py:343
  41.1 4.5 %collective-permute-start.17 = (bf16[72,256]{1,0:T(8,128)(2,1)S(1)}, bf16[72,256]{1,0:T(8,128)(2,1)S(1)}, u32[]{:S(2)}, u32[]{:S(2)}) collective-permute-start(bf16[72,256]{1,0:T(8,128)(2,1)S(1)} %shard_map.76.refs_0_.mine_ref), channel_id=1, source_target_pairs={{0,3},{1,2},{2,1},{3,0},{4,7},{5,6},{6,5},{7,4},{8,11},{9,10},{10,... | collective-permute-start | bytes 110600 | tf_op jit(solution)/shard_map/ppermute | solution.py:377
  42.4 3.2 %collective-permute-start.16 = (bf16[72,256]{1,0:T(8,128)(2,1)S(1)}, bf16[72,256]{1,0:T(8,128)(2,1)S(1)}, u32[]{:S(2)}, u32[]{:S(2)}) collective-permute-start(bf16[72,256]{1,0:T(8,128)(2,1)S(1)} %shard_map.76.refs_0_.mine_ref), channel_id=1, source_target_pairs={{0,1},{1,0},{2,3},{3,2},{4,5},{5,4},{6,7},{7,6},{8,9},{9,8},{10,11... | collective-permute-start | bytes 110600 | tf_op jit(solution)/shard_map/ppermute | solution.py:343
  42.5 4.0 %collective-permute-start.15 = (bf16[72,256]{1,0:T(8,128)(2,1)S(1)}, bf16[72,256]{1,0:T(8,128)(2,1)S(1)}, u32[]{:S(2)}, u32[]{:S(2)}) collective-permute-start(bf16[72,256]{1,0:T(8,128)(2,1)S(1)} %shard_map.76.refs_0_.mine_ref), channel_id=1, source_target_pairs={{0,2},{2,0},{1,3},{3,1},{4,6},{6,4},{5,7},{7,5},{8,10},{10,8},{9,1... | collective-permute-start | bytes 110600 | tf_op jit(solution)/shard_map/ppermute | solution.py:371

commit v23 on v22

--- a/solution.py
+++ b/solution.py
@@ -257,7 +257,7 @@
 def sum_rows(*refs):
     *refs, _, out_ref = refs
     rows = out_ref.shape[0]
-    terms = dict(zip(row_order(len(refs), near_first=True), (ref[-rows:].astype(F32) for ref in refs)))
+    terms = dict(zip(row_order(len(refs), near_first=True, by_half=True), (ref[-rows:].astype(F32) for ref in refs)))
     terms = [terms[k] for k in range(len(refs))]
     while len(terms) > 1:
         terms = [a + b for a, b in zip(terms[::2], terms[1::2])]
@@ -326,7 +326,7 @@
         copy.wait()
 
 
-def finish_one(mine_ref, across_ref, beside_ref, corner_ref, _, __, out_ref, flat_ref, *, scale):
+def finish_one(mine_ref, corner_ref, beside_ref, across_ref, _, __, out_ref, flat_ref, *, scale):
     pair = lax.axis_index("pair")
     for refs, place in (((mine_ref, across_ref), pair), ((beside_ref, corner_ref), 1 - pair)):
         total = refs[0][...].astype(F32) + refs[1][...].astype(F32)
@@ -377,13 +377,13 @@
     return lax.ppermute(values, COLS, steps)
 
 
-def row_order(bands, near_first=False):
-    far_first = list(range(bands - 1, 0, -1))
+def row_order(bands, near_first=False, by_half=False):
+    far_first = sorted(range(1, bands), key=lambda k: (k < bands // 2, k if by_half else -k))
     return [0] + (far_first[::-1] if near_first else far_first)
 
 
-def row_swaps(values, bands, near_first=False):
-    order = row_order(bands, near_first)
+def row_swaps(values, bands, near_first=False, by_half=False):
+    order = row_order(bands, near_first, by_half)
     return [values[0]] + [xor_swap(values[k], "row", bands, k) for k in order[1:]]
 
 
@@ -493,8 +493,8 @@
     )
     columns = lax.axis_size("col")
     two, two_more = sum_but_last(two, "col", columns)
-    ones = row_swaps([one, joined] + [one] * (bands - 2), bands, near_first=True)
-    near = ones[row_order(bands, near_first=True).index(1)]
+    ones = row_swaps([one, joined] + [one] * (bands - 2), bands, near_first=True, by_half=True)
+    near = ones[row_order(bands, near_first=True, by_half=True).index(1)]
     up_b = odd_row_swap(up_b)
     (one,) = whole_call(sum_rows, [shaped(one.shape)], ones + [up_b], 0, after=1)
     input_grad, done = whole_call(
@@ -518,7 +518,7 @@
     (grad_one,) = whole_call(
         functools.partial(finish_one, scale=1.0 / math.sqrt(height * width)),
         [shaped((3, 3 * channels, channels), F32)],
-        [one, across, beside_one, corner, wrote, done],
+        [one, corner, beside_one, across, wrote, done],
         1,
         scratch=[pltpu.VMEM((144, 256), F32)],
         after=2,

time: 47.5 us -> 46.9 us (0.987)
  waiting for transfers between devices: 14.6 us -> 13.1 us
  starting transfers between devices: 22 us -> 22.9 us
    ppermute x11, waiting for transfers between devices: 9.88 us -> 8.14 us  [xor_swap(): return lax.ppermute(values, axis, [(n, n ^ k) for n in range(count)])]
    ppermute x11, starting transfers between devices: 14.2 us -> 15.4 us  [xor_swap(): return lax.ppermute(values, axis, [(n, n ^ k) for n in range(count)])]
where the time goes in v23:
time: 46.9 us; the launch traced here: 46.7 us
  starting transfers between devices  22.9 us (49%)
  waiting for transfers between devices  13.1 us (28%)
  Pallas kernels  7.08 us (15%)
  local copies, waits for them, and re-layouts  2.77 us (6%)
  between operations  0.81 us (2%)
    ppermute x11, starting transfers between devices, xor_swap(): return lax.ppermute(values, axis, [(n, n ^ k) for n in range(count)])  15.4 us
    ppermute x11, waiting for transfers between devices, xor_swap(): return lax.ppermute(values, axis, [(n, n ^ k) for n in range(count)])  8.14 us
    pallas_call x13, Pallas kernels, whole_call(): pl.pallas_call(body, out_shape=outs, in_specs=specs, out_specs=[pl.BlockS...  7.08 us
    ppermute x5, starting transfers between devices, even_swap(): return lax.ppermute(values, axis, [(n, n ^ 1) for n in range(count)])  4.54 us
    unnamed x6, local copies, waits for them, and re-layouts  2.75 us
    ppermute x5, waiting for transfers between devices, even_swap(): return lax.ppermute(values, axis, [(n, n ^ 1) for n in range(count)])  2.34 us
    ppermute x1, starting transfers between devices, odd_strip_swap(): return lax.ppermute(values, ('grp',) + COLS, steps)  1.56 us
    ppermute x2, waiting for transfers between devices, odd_row_swap(): return lax.ppermute(values, ('row', 'pair'), steps)  1.21 us
  transfers between devices with their start and end apart: 20, of which 12 were waited for; matrix products, arithmetic and copies ran while one was open for 2% of the time, Pallas kernels for 7%

profile of v23, /device:TPU:0, one launch (start us, length us, event | category | flops | bytes accessed | tf_op | source)
XLA Modules:
  0.0 46.7 jit_solution(722132869905800184)
XLA Ops:
  0.7 1.0 %copy.19 = bf16[64,8,128]{2,0,1:T(8,128)(2,1)S(1)} copy(bf16[64,8,128]{2,1,0:T(8,128)(2,1)} %param.4) | data formatting | bytes 262144 | tf_op args[0]
  2.2 4.1 %collective-permute-start = (bf16[64,128]{1,0:T(8,128)(2,1)S(1)}, bf16[64,128]{1,0:T(8,128)(2,1)S(1)}, u32[]{:S(2)}, u32[]{:S(2)}) collective-permute-start(bf16[64,128]{1,0:T(8,128)(2,1)S(1)} %get-tuple-element.72), channel_id=1, source_target_pairs={{0,4},{4,0},{8,12},{12,8},{1,5},{5,1},{9,13},{13,9},{2,6},{6,2},{1... | collective-permute-start | bytes 49160 | tf_op jit(solution)/shard_map/ppermute | solution.py:343
  8.1 1.6 %collective-permute-start.2 = (bf16[144,128]{1,0:T(8,128)(2,1)S(1)}, bf16[144,128]{1,0:T(8,128)(2,1)S(1)}, u32[]{:S(2)}, u32[]{:S(2)}) collective-permute-start(bf16[144,128]{1,0:T(8,128)(2,1)S(1)} %get-tuple-element.39), channel_id=1, source_target_pairs={{0,16},{1,2},{2,1},{3,19},{16,0},{17,18},{18,17},{19,3},{4,20},{5,... | collective-permute-start | bytes 110600 | tf_op jit(solution)/shard_map/ppermute | solution.py:367
  9.8 0.9 %copy-done.1 = bf16[64,3,3,64]{3,0,2,1:T(8,128)(2,1)S(1)} copy-done((bf16[64,3,3,64]{3,0,2,1:T(8,128)(2,1)S(1)}, bf16[64,3,3,64]{3,0,2,1:T(8,128)(2,1)}, u32[]{:S(2)}) %copy-start.1) | copy-done | bytes 73752
  10.9 1.2 %collective-permute-done.2.b_ref = bf16[144,128]{1,0:T(8,128)(2,1)S(1)} collective-permute-done((bf16[144,128]{1,0:T(8,128)(2,1)S(1)}, bf16[144,128]{1,0:T(8,128)(2,1)S(1)}, u32[]{:S(2)}, u32[]{:S(2)}) %collective-permute-start.2) | collective-permute-done | bytes 36896 | tf_op jit(solution)/shard_map/ppermute | solution.py:367
  13.0 2.6 %collective-permute-start.6 = (bf16[2,40,256]{2,1,0:T(8,128)(2,1)S(1)}, bf16[2,40,256]{2,1,0:T(8,128)(2,1)S(1)}, u32[]{:S(2)}, u32[]{:S(2)}) collective-permute-start(bf16[2,40,256]{2,1,0:T(8,128)(2,1)S(1)} %get-tuple-element.46.refs_0_), channel_id=1, source_target_pairs={{0,12},{4,8},{8,4},{12,0},{1,13},{5,9},{9,5},{13,1},{2,14},{6,10},... | collective-permute-start | bytes 122888 | tf_op jit(solution)/shard_map/ppermute | solution.py:371
  15.6 0.9 %collective-permute-start.5 = (bf16[2,40,256]{2,1,0:T(8,128)(2,1)S(1)}, bf16[2,40,256]{2,1,0:T(8,128)(2,1)S(1)}, u32[]{:S(2)}, u32[]{:S(2)}) collective-permute-start(bf16[2,40,256]{2,1,0:T(8,128)(2,1)S(1)} %get-tuple-element.46.refs_0_), channel_id=1, source_target_pairs={{0,8},{4,12},{8,0},{12,4},{1,9},{5,13},{9,1},{13,5},{2,10},{6,14},... | collective-permute-start | bytes 122888 | tf_op jit(solution)/shard_map/ppermute | solution.py:371
  16.6 0.9 %collective-permute-start.4 = (bf16[2,40,256]{2,1,0:T(8,128)(2,1)S(1)}, bf16[2,40,256]{2,1,0:T(8,128)(2,1)S(1)}, u32[]{:S(2)}, u32[]{:S(2)}) collective-permute-start(bf16[2,40,256]{2,1,0:T(8,128)(2,1)S(1)} %get-tuple-element.46.refs_0_), channel_id=1, source_target_pairs={{0,4},{4,0},{8,12},{12,8},{1,5},{5,1},{9,13},{13,9},{2,6},{6,2},{1... | collective-permute-start | bytes 122888 | tf_op jit(solution)/shard_map/ppermute | solution.py:371
  17.6 1.4 %collective-permute-done.6.refs_3_ = bf16[2,40,256]{2,1,0:T(8,128)(2,1)S(1)} collective-permute-done((bf16[2,40,256]{2,1,0:T(8,128)(2,1)S(1)}, bf16[2,40,256]{2,1,0:T(8,128)(2,1)S(1)}, u32[]{:S(2)}, u32[]{:S(2)}) %collective-permute-start.6) | collective-permute-done | bytes 40992 | tf_op jit(solution)/shard_map/ppermute | solution.py:371
  19.0 1.8 %collective-permute-done.5.refs_2_ = bf16[2,40,256]{2,1,0:T(8,128)(2,1)S(1)} collective-permute-done((bf16[2,40,256]{2,1,0:T(8,128)(2,1)S(1)}, bf16[2,40,256]{2,1,0:T(8,128)(2,1)S(1)}, u32[]{:S(2)}, u32[]{:S(2)}) %collective-permute-start.5) | collective-permute-done | bytes 40992 | tf_op jit(solution)/shard_map/ppermute | solution.py:371
  21.0 1.0 %shard_map.71 = (bf16[72,256]{1,0:T(8,128)(2,1)S(1)}, bf16[72,256]{1,0:T(8,128)(2,1)S(1)}, bf16[72,256]{1,0:T(8,128)(2,1)S(1)}, bf16[72,256]{1,0:T(8,128)(2,1)S(...) custom-call(bf16[8,48,128]{2,1,0:T(8,128)(2,1)S(1)} %fusion.6.og_ref, ...), custom_call_target="tpu_custom_call" | custom-call | flops 452984832 | bytes 1368064 | tf_op jit(solution)/shard_map/pallas_call | solution.py:30
  22.0 1.5 %collective-permute-start.7 = (bf16[72,256]{1,0:T(8,128)(2,1)S(1)}, bf16[72,256]{1,0:T(8,128)(2,1)S(1)}, u32[]{:S(2)}, u32[]{:S(2)}) collective-permute-start(bf16[72,256]{1,0:T(8,128)(2,1)S(1)} %get-tuple-element.48), channel_id=1, source_target_pairs={{0,12},{4,8},{8,4},{12,0},{1,13},{5,9},{9,5},{13,1},{2,14},{6,10},... | collective-permute-start | bytes 110600 | tf_op jit(solution)/shard_map/ppermute | solution.py:371
  24.0 2.5 %collective-permute-start.9 = (bf16[72,256]{1,0:T(8,128)(2,1)S(1)}, bf16[72,256]{1,0:T(8,128)(2,1)S(1)}, u32[]{:S(2)}, u32[]{:S(2)}) collective-permute-start(bf16[72,256]{1,0:T(8,128)(2,1)S(1)} %get-tuple-element.50), channel_id=1, source_target_pairs={{0,4},{4,0},{8,12},{12,8},{1,5},{5,1},{9,13},{13,9},{2,6},{6,2},{1... | collective-permute-start | bytes 110600 | tf_op jit(solution)/shard_map/ppermute | solution.py:371
  29.7 1.6 %collective-permute-done.10.b_ref = bf16[648,256]{1,0:T(8,128)(2,1)S(1)} collective-permute-done((bf16[648,256]{1,0:T(8,128)(2,1)S(1)}, bf16[648,256]{1,0:T(8,128)(2,1)S(1)}, u32[]{:S(2)}, u32[]{:S(2)}) %collective-permute-start.10) | collective-permute-done | bytes 331808 | tf_op jit(solution)/shard_map/ppermute | solution.py:343
  31.4 0.9 %collective-permute-start.18 = (bf16[576,256]{1,0:T(8,128)(2,1)S(1)}, bf16[576,256]{1,0:T(8,128)(2,1)S(1)}, u32[]{:S(2)}, u32[]{:S(2)}) collective-permute-start(bf16[576,256]{1,0:T(8,128)(2,1)S(1)} %get-tuple-element.67.a_ref), channel_id=1, source_target_pairs={{0,2},{2,0},{1,3},{3,1},{4,6},{6,4},{5,7},{7,5},{8,10},{10,8},{9,1... | collective-permute-start | bytes 884744 | tf_op jit(solution)/shard_map/ppermute | solution.py:371
  32.3 1.7 %collective-permute-start.11 = (bf16[136,256]{1,0:T(8,128)(2,1)S(1)}, bf16[136,256]{1,0:T(8,128)(2,1)S(1)}, u32[]{:S(2)}, u32[]{:S(2)}) collective-permute-start(bf16[136,256]{1,0:T(8,128)(2,1)S(1)} %get-tuple-element.62), channel_id=1, source_target_pairs={{0,4},{4,0},{8,12},{12,8},{1,5},{5,1},{9,13},{13,9},{2,6},{6,2},{1... | collective-permute-start | bytes 208904 | tf_op jit(solution)/shard_map/ppermute | solution.py:371
  34.0 1.1 %collective-permute-start.14 = (bf16[72,256]{1,0:T(8,128)(2,1)S(1)}, bf16[72,256]{1,0:T(8,128)(2,1)S(1)}, u32[]{:S(2)}, u32[]{:S(2)}) collective-permute-start(bf16[72,256]{1,0:T(8,128)(2,1)S(1)} %get-tuple-element.66.refs_0_), channel_id=1, source_target_pairs={{0,8},{4,12},{8,0},{12,4},{1,9},{5,13},{9,1},{13,5},{2,10},{6,14},... | collective-permute-start | bytes 110600 | tf_op jit(solution)/shard_map/ppermute | solution.py:371
  35.1 1.6 %collective-permute-start.13 = (bf16[72,256]{1,0:T(8,128)(2,1)S(1)}, bf16[72,256]{1,0:T(8,128)(2,1)S(1)}, u32[]{:S(2)}, u32[]{:S(2)}) collective-permute-start(bf16[72,256]{1,0:T(8,128)(2,1)S(1)} %get-tuple-element.66.refs_0_), channel_id=1, source_target_pairs={{0,12},{4,8},{8,4},{12,0},{1,13},{5,9},{9,5},{13,1},{2,14},{6,10},... | collective-permute-start | bytes 110600 | tf_op jit(solution)/shard_map/ppermute | solution.py:371
  36.7 1.2 %collective-permute-done.12.b_ref.refs_4_ = bf16[64,256]{1,0:T(8,128)(2,1)S(1)} collective-permute-done((bf16[64,256]{1,0:T(8,128)(2,1)S(1)}, bf16[64,256]{1,0:T(8,128)(2,1)S(1)}, u32[]{:S(2)}, u32[]{:S(2)}) %collective-permute-start.12) | collective-permute-done | bytes 32800 | tf_op jit(solution)/shard_map/ppermute | solution.py:357
  37.9 1.9 %collective-permute-done.14.refs_3_ = bf16[72,256]{1,0:T(8,128)(2,1)S(1)} collective-permute-done((bf16[72,256]{1,0:T(8,128)(2,1)S(1)}, bf16[72,256]{1,0:T(8,128)(2,1)S(1)}, u32[]{:S(2)}, u32[]{:S(2)}) %collective-permute-start.14) | collective-permute-done | bytes 36896 | tf_op jit(solution)/shard_map/ppermute | solution.py:371
  39.8 1.2 %collective-permute-done.13.refs_2_ = bf16[72,256]{1,0:T(8,128)(2,1)S(1)} collective-permute-done((bf16[72,256]{1,0:T(8,128)(2,1)S(1)}, bf16[72,256]{1,0:T(8,128)(2,1)S(1)}, u32[]{:S(2)}, u32[]{:S(2)}) %collective-permute-start.13) | collective-permute-done | bytes 36896 | tf_op jit(solution)/shard_map/ppermute | solution.py:371
  41.1 1.2 %collective-permute-start.17 = (bf16[72,256]{1,0:T(8,128)(2,1)S(1)}, bf16[72,256]{1,0:T(8,128)(2,1)S(1)}, u32[]{:S(2)}, u32[]{:S(2)}) collective-permute-start(bf16[72,256]{1,0:T(8,128)(2,1)S(1)} %shard_map.76.refs_0_.mine_ref), channel_id=1, source_target_pairs={{0,2},{2,0},{1,3},{3,1},{4,6},{6,4},{5,7},{7,5},{8,10},{10,8},{9,1... | collective-permute-start | bytes 110600 | tf_op jit(solution)/shard_map/ppermute | solution.py:371
  43.3 1.2 %shard_map.75 = (bf16[64,8,128]{2,1,0:T(8,128)(2,1)}, f32[8,128]{1,0:T(8,128)S(1)}) custom-call(bf16[8,64,256]{2,1,0:T(8,128)(2,1)S(1)} %get-tuple-element.58.g_ref, bf16[136,256]{1,0:T(8,128)(2,1)S(1)} %collective-permute-done.11.a_ref.refs_1_, bf16[64,256]{1,0:T(8,128)(2,1)S(1)} %collective-permute-done.12.b_ref.refs_4_, ...), custom_call_target="tpu_custom_call" | custom-call | flops 150994944 | bytes 573440 | tf_op jit(solution)/shard_map/pallas_call | solution.py:30
  44.5 1.1 %shard_map.78 = (f32[1152,256]{1,0:T(8,128)}, f32[8,128]{1,0:T(8,128)S(1)}) custom-call(bf16[576,256]{1,0:T(8,128)(2,1)S(1)} %shard_map.77.mine_ref, bf16[576,256]{1,0:T(8,128)(2,1)S(1)} %collective-permute-done.19.other_ref), custom_call_target="tpu_custom_call" | custom-call | flops 100000000 | bytes 1773568 | tf_op jit(solution)/shard_map/pallas_call | solution.py:30
  (42 shorter events, 10.0 us)
Async XLA Ops:
  0.6 20.4 %copy-start = (bf16[128,3,3,256]{3,0,2,1:T(8,128)(2,1)S(1)}, bf16[128,3,3,256]{3,0,2,1:T(8,128)(2,1)}, u32[]{:S(2)}) copy-start(bf16[128,3,3,256]{3,0,2,1:T(8,128)(2,1)} %param.6) | copy-start | bytes 1769476
  1.7 5.7 %collective-permute-start.1 = (bf16[64,128]{1,0:T(8,128)(2,1)S(1)}, bf16[64,128]{1,0:T(8,128)(2,1)S(1)}, u32[]{:S(2)}, u32[]{:S(2)}) collective-permute-start(bf16[64,128]{1,0:T(8,128)(2,1)S(1)} %get-tuple-element.71), channel_id=1, source_target_pairs={{0,1},{1,0},{4,8},{5,9},{8,4},{9,5},{12,13},{13,12},{2,3},{3,2},{6... | collective-permute-start | bytes 49160 | tf_op jit(solution)/shard_map/ppermute | solution.py:357
  2.2 5.9 %collective-permute-start = (bf16[64,128]{1,0:T(8,128)(2,1)S(1)}, bf16[64,128]{1,0:T(8,128)(2,1)S(1)}, u32[]{:S(2)}, u32[]{:S(2)}) collective-permute-start(bf16[64,128]{1,0:T(8,128)(2,1)S(1)} %get-tuple-element.72), channel_id=1, source_target_pairs={{0,4},{4,0},{8,12},{12,8},{1,5},{5,1},{9,13},{13,9},{2,6},{6,2},{1... | collective-permute-start | bytes 49160 | tf_op jit(solution)/shard_map/ppermute | solution.py:343
  8.1 4.0 %collective-permute-start.2 = (bf16[144,128]{1,0:T(8,128)(2,1)S(1)}, bf16[144,128]{1,0:T(8,128)(2,1)S(1)}, u32[]{:S(2)}, u32[]{:S(2)}) collective-permute-start(bf16[144,128]{1,0:T(8,128)(2,1)S(1)} %get-tuple-element.39), channel_id=1, source_target_pairs={{0,16},{1,2},{2,1},{3,19},{16,0},{17,18},{18,17},{19,3},{4,20},{5,... | collective-permute-start | bytes 110600 | tf_op jit(solution)/shard_map/ppermute | solution.py:367
  9.7 2.4 %collective-permute-start.3 = (bf16[144,128]{1,0:T(8,128)(2,1)S(1)}, bf16[144,128]{1,0:T(8,128)(2,1)S(1)}, u32[]{:S(2)}, u32[]{:S(2)}) collective-permute-start(bf16[144,128]{1,0:T(8,128)(2,1)S(1)} %get-tuple-element.40), channel_id=1, source_target_pairs={{0,1},{1,0},{2,3},{3,2},{4,5},{5,4},{6,7},{7,6},{8,9},{9,8},{10,11... | collective-permute-start | bytes 110600 | tf_op jit(solution)/shard_map/ppermute | solution.py:343
  9.8 0.9 %copy-start.1 = (bf16[64,3,3,64]{3,0,2,1:T(8,128)(2,1)S(1)}, bf16[64,3,3,64]{3,0,2,1:T(8,128)(2,1)}, u32[]{:S(2)}) copy-start(bf16[64,3,3,64]{3,0,2,1:T(8,128)(2,1)} %param.5) | copy-start | bytes 221188
  13.0 6.0 %collective-permute-start.6 = (bf16[2,40,256]{2,1,0:T(8,128)(2,1)S(1)}, bf16[2,40,256]{2,1,0:T(8,128)(2,1)S(1)}, u32[]{:S(2)}, u32[]{:S(2)}) collective-permute-start(bf16[2,40,256]{2,1,0:T(8,128)(2,1)S(1)} %get-tuple-element.46.refs_0_), channel_id=1, source_target_pairs={{0,12},{4,8},{8,4},{12,0},{1,13},{5,9},{9,5},{13,1},{2,14},{6,10},... | collective-permute-start | bytes 122888 | tf_op jit(solution)/shard_map/ppermute | solution.py:371
  15.6 5.1 %collective-permute-start.5 = (bf16[2,40,256]{2,1,0:T(8,128)(2,1)S(1)}, bf16[2,40,256]{2,1,0:T(8,128)(2,1)S(1)}, u32[]{:S(2)}, u32[]{:S(2)}) collective-permute-start(bf16[2,40,256]{2,1,0:T(8,128)(2,1)S(1)} %get-tuple-element.46.refs_0_), channel_id=1, source_target_pairs={{0,8},{4,12},{8,0},{12,4},{1,9},{5,13},{9,1},{13,5},{2,10},{6,14},... | collective-permute-start | bytes 122888 | tf_op jit(solution)/shard_map/ppermute | solution.py:371
  16.6 4.4 %collective-permute-start.4 = (bf16[2,40,256]{2,1,0:T(8,128)(2,1)S(1)}, bf16[2,40,256]{2,1,0:T(8,128)(2,1)S(1)}, u32[]{:S(2)}, u32[]{:S(2)}) collective-permute-start(bf16[2,40,256]{2,1,0:T(8,128)(2,1)S(1)} %get-tuple-element.46.refs_0_), channel_id=1, source_target_pairs={{0,4},{4,0},{8,12},{12,8},{1,5},{5,1},{9,13},{13,9},{2,6},{6,2},{1... | collective-permute-start | bytes 122888 | tf_op jit(solution)/shard_map/ppermute | solution.py:371
  22.0 5.8 %collective-permute-start.7 = (bf16[72,256]{1,0:T(8,128)(2,1)S(1)}, bf16[72,256]{1,0:T(8,128)(2,1)S(1)}, u32[]{:S(2)}, u32[]{:S(2)}) collective-permute-start(bf16[72,256]{1,0:T(8,128)(2,1)S(1)} %get-tuple-element.48), channel_id=1, source_target_pairs={{0,12},{4,8},{8,4},{12,0},{1,13},{5,9},{9,5},{13,1},{2,14},{6,10},... | collective-permute-start | bytes 110600 | tf_op jit(solution)/shard_map/ppermute | solution.py:371
  23.5 5.3 %collective-permute-start.8 = (bf16[72,256]{1,0:T(8,128)(2,1)S(1)}, bf16[72,256]{1,0:T(8,128)(2,1)S(1)}, u32[]{:S(2)}, u32[]{:S(2)}) collective-permute-start(bf16[72,256]{1,0:T(8,128)(2,1)S(1)} %get-tuple-element.49), channel_id=1, source_target_pairs={{0,8},{4,12},{8,0},{12,4},{1,9},{5,13},{9,1},{13,5},{2,10},{6,14},... | collective-permute-start | bytes 110600 | tf_op jit(solution)/shard_map/ppermute | solution.py:371
  24.0 4.7 %collective-permute-start.9 = (bf16[72,256]{1,0:T(8,128)(2,1)S(1)}, bf16[72,256]{1,0:T(8,128)(2,1)S(1)}, u32[]{:S(2)}, u32[]{:S(2)}) collective-permute-start(bf16[72,256]{1,0:T(8,128)(2,1)S(1)} %get-tuple-element.50), channel_id=1, source_target_pairs={{0,4},{4,0},{8,12},{12,8},{1,5},{5,1},{9,13},{13,9},{2,6},{6,2},{1... | collective-permute-start | bytes 110600 | tf_op jit(solution)/shard_map/ppermute | solution.py:371
  29.6 1.7 %collective-permute-start.10 = (bf16[648,256]{1,0:T(8,128)(2,1)S(1)}, bf16[648,256]{1,0:T(8,128)(2,1)S(1)}, u32[]{:S(2)}, u32[]{:S(2)}) collective-permute-start(bf16[648,256]{1,0:T(8,128)(2,1)S(1)} %get-tuple-element.60), channel_id=1, source_target_pairs={{0,1},{1,0},{2,3},{3,2},{4,5},{5,4},{6,7},{7,6},{8,9},{9,8},{10,11... | collective-permute-start | bytes 995336 | tf_op jit(solution)/shard_map/ppermute | solution.py:343
  31.4 9.5 %collective-permute-start.18 = (bf16[576,256]{1,0:T(8,128)(2,1)S(1)}, bf16[576,256]{1,0:T(8,128)(2,1)S(1)}, u32[]{:S(2)}, u32[]{:S(2)}) collective-permute-start(bf16[576,256]{1,0:T(8,128)(2,1)S(1)} %get-tuple-element.67.a_ref), channel_id=1, source_target_pairs={{0,2},{2,0},{1,3},{3,1},{4,6},{6,4},{5,7},{7,5},{8,10},{10,8},{9,1... | collective-permute-start | bytes 884744 | tf_op jit(solution)/shard_map/ppermute | solution.py:371
  32.3 8.6 %collective-permute-start.11 = (bf16[136,256]{1,0:T(8,128)(2,1)S(1)}, bf16[136,256]{1,0:T(8,128)(2,1)S(1)}, u32[]{:S(2)}, u32[]{:S(2)}) collective-permute-start(bf16[136,256]{1,0:T(8,128)(2,1)S(1)} %get-tuple-element.62), channel_id=1, source_target_pairs={{0,4},{4,0},{8,12},{12,8},{1,5},{5,1},{9,13},{13,9},{2,6},{6,2},{1... | collective-permute-start | bytes 208904 | tf_op jit(solution)/shard_map/ppermute | solution.py:371
  34.0 5.7 %collective-permute-start.14 = (bf16[72,256]{1,0:T(8,128)(2,1)S(1)}, bf16[72,256]{1,0:T(8,128)(2,1)S(1)}, u32[]{:S(2)}, u32[]{:S(2)}) collective-permute-start(bf16[72,256]{1,0:T(8,128)(2,1)S(1)} %get-tuple-element.66.refs_0_), channel_id=1, source_target_pairs={{0,8},{4,12},{8,0},{12,4},{1,9},{5,13},{9,1},{13,5},{2,10},{6,14},... | collective-permute-start | bytes 110600 | tf_op jit(solution)/shard_map/ppermute | solution.py:371
  35.1 5.8 %collective-permute-start.13 = (bf16[72,256]{1,0:T(8,128)(2,1)S(1)}, bf16[72,256]{1,0:T(8,128)(2,1)S(1)}, u32[]{:S(2)}, u32[]{:S(2)}) collective-permute-start(bf16[72,256]{1,0:T(8,128)(2,1)S(1)} %get-tuple-element.66.refs_0_), channel_id=1, source_target_pairs={{0,12},{4,8},{8,4},{12,0},{1,13},{5,9},{9,5},{13,1},{2,14},{6,10},... | collective-permute-start | bytes 110600 | tf_op jit(solution)/shard_map/ppermute | solution.py:371
  36.7 1.2 %collective-permute-start.12 = (bf16[64,256]{1,0:T(8,128)(2,1)S(1)}, bf16[64,256]{1,0:T(8,128)(2,1)S(1)}, u32[]{:S(2)}, u32[]{:S(2)}) collective-permute-start(bf16[64,256]{1,0:T(8,128)(2,1)S(1)} %get-tuple-element.63), channel_id=1, source_target_pairs={{0,1},{1,0},{4,8},{5,9},{8,4},{9,5},{12,13},{13,12},{2,3},{3,2},{6... | collective-permute-start | bytes 98312 | tf_op jit(solution)/shard_map/ppermute | solution.py:357
  41.0 3.5 %collective-permute-start.19 = (bf16[576,256]{1,0:T(8,128)(2,1)S(1)}, bf16[576,256]{1,0:T(8,128)(2,1)S(1)}, u32[]{:S(2)}, u32[]{:S(2)}) collective-permute-start(bf16[576,256]{1,0:T(8,128)(2,1)S(1)} %shard_map.77.mine_ref), channel_id=1, source_target_pairs={{0,1},{1,0},{2,3},{3,2},{4,5},{5,4},{6,7},{7,6},{8,9},{9,8},{10,11... | collective-permute-start | bytes 884744 | tf_op jit(solution)/shard_map/ppermute | solution.py:343
  41.1 4.5 %collective-permute-start.17 = (bf16[72,256]{1,0:T(8,128)(2,1)S(1)}, bf16[72,256]{1,0:T(8,128)(2,1)S(1)}, u32[]{:S(2)}, u32[]{:S(2)}) collective-permute-start(bf16[72,256]{1,0:T(8,128)(2,1)S(1)} %shard_map.76.refs_0_.mine_ref), channel_id=1, source_target_pairs={{0,2},{2,0},{1,3},{3,1},{4,6},{6,4},{5,7},{7,5},{8,10},{10,8},{9,1... | collective-permute-start | bytes 110600 | tf_op jit(solution)/shard_map/ppermute | solution.py:371
  42.3 3.3 %collective-permute-start.16 = (bf16[72,256]{1,0:T(8,128)(2,1)S(1)}, bf16[72,256]{1,0:T(8,128)(2,1)S(1)}, u32[]{:S(2)}, u32[]{:S(2)}) collective-permute-start(bf16[72,256]{1,0:T(8,128)(2,1)S(1)} %shard_map.76.refs_0_.mine_ref), channel_id=1, source_target_pairs={{0,1},{1,0},{2,3},{3,2},{4,5},{5,4},{6,7},{7,6},{8,9},{9,8},{10,11... | collective-permute-start | bytes 110600 | tf_op jit(solution)/shard_map/ppermute | solution.py:343
  42.5 3.4 %collective-permute-start.15 = (bf16[72,256]{1,0:T(8,128)(2,1)S(1)}, bf16[72,256]{1,0:T(8,128)(2,1)S(1)}, u32[]{:S(2)}, u32[]{:S(2)}) collective-permute-start(bf16[72,256]{1,0:T(8,128)(2,1)S(1)} %shard_map.76.refs_0_.mine_ref), channel_id=1, source_target_pairs={{0,3},{1,2},{2,1},{3,0},{4,7},{5,6},{6,5},{7,4},{8,11},{9,10},{10,... | collective-permute-start | bytes 110600 | tf_op jit(solution)/shard_map/ppermute | solution.py:377

commit v24 on v23

--- a/solution.py
+++ b/solution.py
@@ -116,7 +116,7 @@
     b_ref[64:] = jnp.where(even, first, last).astype(BF16)
 
 
-def pack_borders(up_a_ref, up_b_ref, own_a_ref, own_b_ref, a_ref, b_ref, above_ref, below_ref, *, bands):
+def pack_borders(up_b_ref, up_a_ref, own_a_ref, own_b_ref, a_ref, b_ref, above_ref, below_ref, *, bands):
     even = (strip_index() & 1) == 0
     above_ref[...], below_ref[...] = beside(up_a_ref, up_b_ref, lax.axis_index("row"), bands)
     slot = lax.broadcasted_iota(jnp.int32, (64, 128), 1) >> 4
@@ -326,7 +326,7 @@
         copy.wait()
 
 
-def finish_one(mine_ref, corner_ref, beside_ref, across_ref, _, __, out_ref, flat_ref, *, scale):
+def finish_one(mine_ref, beside_ref, corner_ref, across_ref, _, __, out_ref, flat_ref, *, scale):
     pair = lax.axis_index("pair")
     for refs, place in (((mine_ref, across_ref), pair), ((beside_ref, corner_ref), 1 - pair)):
         total = refs[0][...].astype(F32) + refs[1][...].astype(F32)
@@ -433,7 +433,7 @@
     to_a, to_b, above, below = whole_call(
         functools.partial(pack_borders, bands=bands),
         [shaped((2 * channels + head.shape[0], 128))] * 2 + [shaped((channels, strip_cols))] * 2,
-        [even_swap(to_a, "row", bands), odd_row_swap(to_b), own_a, own_b],
+        [odd_row_swap(to_b), even_swap(to_a, "row", bands), own_a, own_b],
         1,
     )
     side_a, side_b = even_swap(to_a, COLS, strips), odd_strip_swap(to_b)
@@ -518,7 +518,7 @@
     (grad_one,) = whole_call(
         functools.partial(finish_one, scale=1.0 / math.sqrt(height * width)),
         [shaped((3, 3 * channels, channels), F32)],
-        [one, corner, beside_one, across, wrote, done],
+        [one, beside_one, corner, across, wrote, done],
         1,
         scratch=[pltpu.VMEM((144, 256), F32)],
         after=2,

time: 46.9 us -> 46.8 us (level)
    ppermute x5, starting transfers between devices: 4.54 us -> 3.66 us  [even_swap(): return lax.ppermute(values, axis, [(n, n ^ 1) for n in range(count)])]
    ppermute x11, starting transfers between devices: 15.4 us -> 16.2 us  [xor_swap(): return lax.ppermute(values, axis, [(n, n ^ k) for n in range(count)])]
    ppermute x11, waiting for transfers between devices: 8.14 us -> 8.85 us  [xor_swap(): return lax.ppermute(values, axis, [(n, n ^ k) for n in range(count)])]
    ppermute x2, starting transfers between devices: 0.52 us -> 0.01 us  [odd_row_swap(): return lax.ppermute(values, ('row', 'pair'), steps)]
where the time goes in v24:
time: 46.8 us; the launch traced here: 46.6 us
  starting transfers between devices  22.6 us (48%)
  waiting for transfers between devices  13.3 us (28%)
  Pallas kernels  7.08 us (15%)
  local copies, waits for them, and re-layouts  2.78 us (6%)
  between operations  0.8 us (2%)
    ppermute x11, starting transfers between devices, xor_swap(): return lax.ppermute(values, axis, [(n, n ^ k) for n in range(count)])  16.2 us
    ppermute x11, waiting for transfers between devices, xor_swap(): return lax.ppermute(values, axis, [(n, n ^ k) for n in range(count)])  8.85 us
    pallas_call x13, Pallas kernels, whole_call(): pl.pallas_call(body, out_shape=outs, in_specs=specs, out_specs=[pl.BlockS...  7.08 us
    ppermute x5, starting transfers between devices, even_swap(): return lax.ppermute(values, axis, [(n, n ^ 1) for n in range(count)])  3.66 us
    unnamed x6, local copies, waits for them, and re-layouts  2.75 us
    ppermute x5, waiting for transfers between devices, even_swap(): return lax.ppermute(values, axis, [(n, n ^ 1) for n in range(count)])  2.35 us
    ppermute x1, starting transfers between devices, odd_strip_swap(): return lax.ppermute(values, ('grp',) + COLS, steps)  2.01 us
    ppermute x2, waiting for transfers between devices, odd_row_swap(): return lax.ppermute(values, ('row', 'pair'), steps)  1.21 us
  transfers between devices with their start and end apart: 20, of which 12 were waited for; matrix products, arithmetic and copies ran while one was open for 2% of the time, Pallas kernels for 7%

profile of v24, /device:TPU:0, one launch (start us, length us, event | category | flops | bytes accessed | tf_op | source)
XLA Modules:
  0.0 46.6 jit_solution(18169496402788171894)
XLA Ops:
  0.7 1.0 %copy.19 = bf16[64,8,128]{2,0,1:T(8,128)(2,1)S(1)} copy(bf16[64,8,128]{2,1,0:T(8,128)(2,1)} %param.4) | data formatting | bytes 262144 | tf_op args[0]
  1.7 3.1 %collective-permute-start.1 = (bf16[64,128]{1,0:T(8,128)(2,1)S(1)}, bf16[64,128]{1,0:T(8,128)(2,1)S(1)}, u32[]{:S(2)}, u32[]{:S(2)}) collective-permute-start(bf16[64,128]{1,0:T(8,128)(2,1)S(1)} %get-tuple-element.71), channel_id=1, source_target_pairs={{0,4},{4,0},{8,12},{12,8},{1,5},{5,1},{9,13},{13,9},{2,6},{6,2},{1... | collective-permute-start | bytes 49160 | tf_op jit(solution)/shard_map/ppermute | solution.py:343
  6.6 2.0 %collective-permute-start.2 = (bf16[144,128]{1,0:T(8,128)(2,1)S(1)}, bf16[144,128]{1,0:T(8,128)(2,1)S(1)}, u32[]{:S(2)}, u32[]{:S(2)}) collective-permute-start(bf16[144,128]{1,0:T(8,128)(2,1)S(1)} %get-tuple-element.39), channel_id=1, source_target_pairs={{0,16},{1,2},{2,1},{3,19},{16,0},{17,18},{18,17},{19,3},{4,20},{5,... | collective-permute-start | bytes 110600 | tf_op jit(solution)/shard_map/ppermute | solution.py:367
  8.7 0.9 %copy-done.1 = bf16[64,3,3,64]{3,0,2,1:T(8,128)(2,1)S(1)} copy-done((bf16[64,3,3,64]{3,0,2,1:T(8,128)(2,1)S(1)}, bf16[64,3,3,64]{3,0,2,1:T(8,128)(2,1)}, u32[]{:S(2)}) %copy-start.1) | copy-done | bytes 73752
  10.6 0.9 %shard_map.70 = (bf16[2,40,256]{2,1,0:T(8,128)(2,1)S(1)}, bf16[8,64,256]{2,1,0:T(8,128)(2,1)S(1)}, bf16[10,64,256]{2,1,0:T(8,128)(2,1)S(1)}) custom-call(bf16[8,64,128]{2,1,0:T(8,128)(2,1)S(1)} %bitcast.34, bf16[64,128]{1,0:T(8,128)(2,1)S(1)} %get-tuple-element.41.above_ref, bf16[64,128]{1,0:T(8,128)(2,1)S(1)} %get-tuple-element.42.below_ref, ...), custom_call_target="tpu_custom_call" | custom-call | flops 150994944 | bytes 1122304 | tf_op jit(solution)/shard_map/pallas_call | solution.py:30
  11.4 4.1 %collective-permute-start.6 = (bf16[2,40,256]{2,1,0:T(8,128)(2,1)S(1)}, bf16[2,40,256]{2,1,0:T(8,128)(2,1)S(1)}, u32[]{:S(2)}, u32[]{:S(2)}) collective-permute-start(bf16[2,40,256]{2,1,0:T(8,128)(2,1)S(1)} %get-tuple-element.46.refs_0_), channel_id=1, source_target_pairs={{0,12},{4,8},{8,4},{12,0},{1,13},{5,9},{9,5},{13,1},{2,14},{6,10},... | collective-permute-start | bytes 122888 | tf_op jit(solution)/shard_map/ppermute | solution.py:371
  17.5 3.0 %collective-permute-done.5.refs_2_ = bf16[2,40,256]{2,1,0:T(8,128)(2,1)S(1)} collective-permute-done((bf16[2,40,256]{2,1,0:T(8,128)(2,1)S(1)}, bf16[2,40,256]{2,1,0:T(8,128)(2,1)S(1)}, u32[]{:S(2)}, u32[]{:S(2)}) %collective-permute-start.5) | collective-permute-done | bytes 40992 | tf_op jit(solution)/shard_map/ppermute | solution.py:371
  20.6 1.0 %shard_map.71 = (bf16[72,256]{1,0:T(8,128)(2,1)S(1)}, bf16[72,256]{1,0:T(8,128)(2,1)S(1)}, bf16[72,256]{1,0:T(8,128)(2,1)S(1)}, bf16[72,256]{1,0:T(8,128)(2,1)S(...) custom-call(bf16[8,48,128]{2,1,0:T(8,128)(2,1)S(1)} %fusion.6.og_ref, ...), custom_call_target="tpu_custom_call" | custom-call | flops 452984832 | bytes 1368064 | tf_op jit(solution)/shard_map/pallas_call | solution.py:30
  21.7 2.5 %collective-permute-start.7 = (bf16[72,256]{1,0:T(8,128)(2,1)S(1)}, bf16[72,256]{1,0:T(8,128)(2,1)S(1)}, u32[]{:S(2)}, u32[]{:S(2)}) collective-permute-start(bf16[72,256]{1,0:T(8,128)(2,1)S(1)} %get-tuple-element.48), channel_id=1, source_target_pairs={{0,12},{4,8},{8,4},{12,0},{1,13},{5,9},{9,5},{13,1},{2,14},{6,10},... | collective-permute-start | bytes 110600 | tf_op jit(solution)/shard_map/ppermute | solution.py:371
  24.1 2.0 %collective-permute-start.9 = (bf16[72,256]{1,0:T(8,128)(2,1)S(1)}, bf16[72,256]{1,0:T(8,128)(2,1)S(1)}, u32[]{:S(2)}, u32[]{:S(2)}) collective-permute-start(bf16[72,256]{1,0:T(8,128)(2,1)S(1)} %get-tuple-element.50), channel_id=1, source_target_pairs={{0,4},{4,0},{8,12},{12,8},{1,5},{5,1},{9,13},{13,9},{2,6},{6,2},{1... | collective-permute-start | bytes 110600 | tf_op jit(solution)/shard_map/ppermute | solution.py:371
  26.7 1.0 %collective-permute-done.7.refs_1_ = bf16[72,256]{1,0:T(8,128)(2,1)S(1)} collective-permute-done((bf16[72,256]{1,0:T(8,128)(2,1)S(1)}, bf16[72,256]{1,0:T(8,128)(2,1)S(1)}, u32[]{:S(2)}, u32[]{:S(2)}) %collective-permute-start.7) | collective-permute-done | bytes 36896 | tf_op jit(solution)/shard_map/ppermute | solution.py:371
  27.7 1.2 %collective-permute-done.8.refs_2_ = bf16[72,256]{1,0:T(8,128)(2,1)S(1)} collective-permute-done((bf16[72,256]{1,0:T(8,128)(2,1)S(1)}, bf16[72,256]{1,0:T(8,128)(2,1)S(1)}, u32[]{:S(2)}, u32[]{:S(2)}) %collective-permute-start.8) | collective-permute-done | bytes 36896 | tf_op jit(solution)/shard_map/ppermute | solution.py:371
  29.0 0.9 %shard_map.73 = (bf16[8,64,256]{2,1,0:T(8,128)(2,1)S(1)}, bf16[64,256]{1,0:T(8,128)(2,1)S(1)}, bf16[64,256]{1,0:T(8,128)(2,1)S(1)}, bf16[648,256]{1,0:T(8,128)(2,1)S(1)}, bf16[648,256]{1,0:T(8,128)(2,1)S(1)}) custom-call(bf16[72,256]{1,0:T(8,128)(2,1)S(1)} %get-tuple-element.47.refs_0_, bf16[72,256]{1,0:T(8,128)(2,1)S(1)} %collective-permute-done.7.refs_1_, ...), custom_call_target="tpu_custom_call" | custom-call | flops 150994944 | bytes 2498560 | tf_op jit(solution)/shard_map/pallas_call | solution.py:30
  30.0 1.6 %collective-permute-done.10.b_ref = bf16[648,256]{1,0:T(8,128)(2,1)S(1)} collective-permute-done((bf16[648,256]{1,0:T(8,128)(2,1)S(1)}, bf16[648,256]{1,0:T(8,128)(2,1)S(1)}, u32[]{:S(2)}, u32[]{:S(2)}) %collective-permute-start.10) | collective-permute-done | bytes 331808 | tf_op jit(solution)/shard_map/ppermute | solution.py:343
  31.7 1.0 %collective-permute-start.18 = (bf16[576,256]{1,0:T(8,128)(2,1)S(1)}, bf16[576,256]{1,0:T(8,128)(2,1)S(1)}, u32[]{:S(2)}, u32[]{:S(2)}) collective-permute-start(bf16[576,256]{1,0:T(8,128)(2,1)S(1)} %get-tuple-element.67.a_ref), channel_id=1, source_target_pairs={{0,2},{2,0},{1,3},{3,1},{4,6},{6,4},{5,7},{7,5},{8,10},{10,8},{9,1... | collective-permute-start | bytes 884744 | tf_op jit(solution)/shard_map/ppermute | solution.py:371
  32.6 1.1 %collective-permute-start.11 = (bf16[136,256]{1,0:T(8,128)(2,1)S(1)}, bf16[136,256]{1,0:T(8,128)(2,1)S(1)}, u32[]{:S(2)}, u32[]{:S(2)}) collective-permute-start(bf16[136,256]{1,0:T(8,128)(2,1)S(1)} %get-tuple-element.62), channel_id=1, source_target_pairs={{0,4},{4,0},{8,12},{12,8},{1,5},{5,1},{9,13},{13,9},{2,6},{6,2},{1... | collective-permute-start | bytes 208904 | tf_op jit(solution)/shard_map/ppermute | solution.py:371
  33.7 1.3 %collective-permute-start.14 = (bf16[72,256]{1,0:T(8,128)(2,1)S(1)}, bf16[72,256]{1,0:T(8,128)(2,1)S(1)}, u32[]{:S(2)}, u32[]{:S(2)}) collective-permute-start(bf16[72,256]{1,0:T(8,128)(2,1)S(1)} %get-tuple-element.66.refs_0_), channel_id=1, source_target_pairs={{0,8},{4,12},{8,0},{12,4},{1,9},{5,13},{9,1},{13,5},{2,10},{6,14},... | collective-permute-start | bytes 110600 | tf_op jit(solution)/shard_map/ppermute | solution.py:371
  35.1 2.0 %collective-permute-start.13 = (bf16[72,256]{1,0:T(8,128)(2,1)S(1)}, bf16[72,256]{1,0:T(8,128)(2,1)S(1)}, u32[]{:S(2)}, u32[]{:S(2)}) collective-permute-start(bf16[72,256]{1,0:T(8,128)(2,1)S(1)} %get-tuple-element.66.refs_0_), channel_id=1, source_target_pairs={{0,12},{4,8},{8,4},{12,0},{1,13},{5,9},{9,5},{13,1},{2,14},{6,10},... | collective-permute-start | bytes 110600 | tf_op jit(solution)/shard_map/ppermute | solution.py:371
  37.0 1.2 %collective-permute-done.12.b_ref.refs_4_ = bf16[64,256]{1,0:T(8,128)(2,1)S(1)} collective-permute-done((bf16[64,256]{1,0:T(8,128)(2,1)S(1)}, bf16[64,256]{1,0:T(8,128)(2,1)S(1)}, u32[]{:S(2)}, u32[]{:S(2)}) %collective-permute-start.12) | collective-permute-done | bytes 32800 | tf_op jit(solution)/shard_map/ppermute | solution.py:357
  38.2 1.5 %collective-permute-done.14.refs_3_ = bf16[72,256]{1,0:T(8,128)(2,1)S(1)} collective-permute-done((bf16[72,256]{1,0:T(8,128)(2,1)S(1)}, bf16[72,256]{1,0:T(8,128)(2,1)S(1)}, u32[]{:S(2)}, u32[]{:S(2)}) %collective-permute-start.14) | collective-permute-done | bytes 36896 | tf_op jit(solution)/shard_map/ppermute | solution.py:371
  39.8 1.2 %collective-permute-done.13.refs_2_ = bf16[72,256]{1,0:T(8,128)(2,1)S(1)} collective-permute-done((bf16[72,256]{1,0:T(8,128)(2,1)S(1)}, bf16[72,256]{1,0:T(8,128)(2,1)S(1)}, u32[]{:S(2)}, u32[]{:S(2)}) %collective-permute-start.13) | collective-permute-done | bytes 36896 | tf_op jit(solution)/shard_map/ppermute | solution.py:371
  41.1 1.2 %collective-permute-start.17 = (bf16[72,256]{1,0:T(8,128)(2,1)S(1)}, bf16[72,256]{1,0:T(8,128)(2,1)S(1)}, u32[]{:S(2)}, u32[]{:S(2)}) collective-permute-start(bf16[72,256]{1,0:T(8,128)(2,1)S(1)} %shard_map.76.refs_0_.mine_ref), channel_id=1, source_target_pairs={{0,2},{2,0},{1,3},{3,1},{4,6},{6,4},{5,7},{7,5},{8,10},{10,8},{9,1... | collective-permute-start | bytes 110600 | tf_op jit(solution)/shard_map/ppermute | solution.py:371
  43.3 1.2 %shard_map.75 = (bf16[64,8,128]{2,1,0:T(8,128)(2,1)}, f32[8,128]{1,0:T(8,128)S(1)}) custom-call(bf16[8,64,256]{2,1,0:T(8,128)(2,1)S(1)} %get-tuple-element.58.g_ref, bf16[136,256]{1,0:T(8,128)(2,1)S(1)} %collective-permute-done.11.a_ref.refs_1_, bf16[64,256]{1,0:T(8,128)(2,1)S(1)} %collective-permute-done.12.b_ref.refs_4_, ...), custom_call_target="tpu_custom_call" | custom-call | flops 150994944 | bytes 573440 | tf_op jit(solution)/shard_map/pallas_call | solution.py:30
  44.5 1.1 %shard_map.78 = (f32[1152,256]{1,0:T(8,128)}, f32[8,128]{1,0:T(8,128)S(1)}) custom-call(bf16[576,256]{1,0:T(8,128)(2,1)S(1)} %shard_map.77.mine_ref, bf16[576,256]{1,0:T(8,128)(2,1)S(1)} %collective-permute-done.19.other_ref), custom_call_target="tpu_custom_call" | custom-call | flops 100000000 | bytes 1773568 | tf_op jit(solution)/shard_map/pallas_call | solution.py:30
  (42 shorter events, 7.9 us)
Async XLA Ops:
  0.6 20.0 %copy-start = (bf16[128,3,3,256]{3,0,2,1:T(8,128)(2,1)S(1)}, bf16[128,3,3,256]{3,0,2,1:T(8,128)(2,1)}, u32[]{:S(2)}) copy-start(bf16[128,3,3,256]{3,0,2,1:T(8,128)(2,1)} %param.6) | copy-start | bytes 1769476
  1.7 4.8 %collective-permute-start.1 = (bf16[64,128]{1,0:T(8,128)(2,1)S(1)}, bf16[64,128]{1,0:T(8,128)(2,1)S(1)}, u32[]{:S(2)}, u32[]{:S(2)}) collective-permute-start(bf16[64,128]{1,0:T(8,128)(2,1)S(1)} %get-tuple-element.71), channel_id=1, source_target_pairs={{0,4},{4,0},{8,12},{12,8},{1,5},{5,1},{9,13},{13,9},{2,6},{6,2},{1... | collective-permute-start | bytes 49160 | tf_op jit(solution)/shard_map/ppermute | solution.py:343
  4.7 1.7 %collective-permute-start = (bf16[64,128]{1,0:T(8,128)(2,1)S(1)}, bf16[64,128]{1,0:T(8,128)(2,1)S(1)}, u32[]{:S(2)}, u32[]{:S(2)}) collective-permute-start(bf16[64,128]{1,0:T(8,128)(2,1)S(1)} %get-tuple-element.72), channel_id=1, source_target_pairs={{0,1},{1,0},{4,8},{5,9},{8,4},{9,5},{12,13},{13,12},{2,3},{3,2},{6... | collective-permute-start | bytes 49160 | tf_op jit(solution)/shard_map/ppermute | solution.py:357
  6.6 4.0 %collective-permute-start.2 = (bf16[144,128]{1,0:T(8,128)(2,1)S(1)}, bf16[144,128]{1,0:T(8,128)(2,1)S(1)}, u32[]{:S(2)}, u32[]{:S(2)}) collective-permute-start(bf16[144,128]{1,0:T(8,128)(2,1)S(1)} %get-tuple-element.39), channel_id=1, source_target_pairs={{0,16},{1,2},{2,1},{3,19},{16,0},{17,18},{18,17},{19,3},{4,20},{5,... | collective-permute-start | bytes 110600 | tf_op jit(solution)/shard_map/ppermute | solution.py:367
  8.6 2.0 %collective-permute-start.3 = (bf16[144,128]{1,0:T(8,128)(2,1)S(1)}, bf16[144,128]{1,0:T(8,128)(2,1)S(1)}, u32[]{:S(2)}, u32[]{:S(2)}) collective-permute-start(bf16[144,128]{1,0:T(8,128)(2,1)S(1)} %get-tuple-element.40), channel_id=1, source_target_pairs={{0,1},{1,0},{2,3},{3,2},{4,5},{5,4},{6,7},{7,6},{8,9},{9,8},{10,11... | collective-permute-start | bytes 110600 | tf_op jit(solution)/shard_map/ppermute | solution.py:343
  8.7 0.9 %copy-start.1 = (bf16[64,3,3,64]{3,0,2,1:T(8,128)(2,1)S(1)}, bf16[64,3,3,64]{3,0,2,1:T(8,128)(2,1)}, u32[]{:S(2)}) copy-start(bf16[64,3,3,64]{3,0,2,1:T(8,128)(2,1)} %param.5) | copy-start | bytes 221188
  11.4 6.1 %collective-permute-start.6 = (bf16[2,40,256]{2,1,0:T(8,128)(2,1)S(1)}, bf16[2,40,256]{2,1,0:T(8,128)(2,1)S(1)}, u32[]{:S(2)}, u32[]{:S(2)}) collective-permute-start(bf16[2,40,256]{2,1,0:T(8,128)(2,1)S(1)} %get-tuple-element.46.refs_0_), channel_id=1, source_target_pairs={{0,12},{4,8},{8,4},{12,0},{1,13},{5,9},{9,5},{13,1},{2,14},{6,10},... | collective-permute-start | bytes 122888 | tf_op jit(solution)/shard_map/ppermute | solution.py:371
  15.6 5.0 %collective-permute-start.5 = (bf16[2,40,256]{2,1,0:T(8,128)(2,1)S(1)}, bf16[2,40,256]{2,1,0:T(8,128)(2,1)S(1)}, u32[]{:S(2)}, u32[]{:S(2)}) collective-permute-start(bf16[2,40,256]{2,1,0:T(8,128)(2,1)S(1)} %get-tuple-element.46.refs_0_), channel_id=1, source_target_pairs={{0,8},{4,12},{8,0},{12,4},{1,9},{5,13},{9,1},{13,5},{2,10},{6,14},... | collective-permute-start | bytes 122888 | tf_op jit(solution)/shard_map/ppermute | solution.py:371
  16.2 4.4 %collective-permute-start.4 = (bf16[2,40,256]{2,1,0:T(8,128)(2,1)S(1)}, bf16[2,40,256]{2,1,0:T(8,128)(2,1)S(1)}, u32[]{:S(2)}, u32[]{:S(2)}) collective-permute-start(bf16[2,40,256]{2,1,0:T(8,128)(2,1)S(1)} %get-tuple-element.46.refs_0_), channel_id=1, source_target_pairs={{0,4},{4,0},{8,12},{12,8},{1,5},{5,1},{9,13},{13,9},{2,6},{6,2},{1... | collective-permute-start | bytes 122888 | tf_op jit(solution)/shard_map/ppermute | solution.py:371
  21.7 6.1 %collective-permute-start.7 = (bf16[72,256]{1,0:T(8,128)(2,1)S(1)}, bf16[72,256]{1,0:T(8,128)(2,1)S(1)}, u32[]{:S(2)}, u32[]{:S(2)}) collective-permute-start(bf16[72,256]{1,0:T(8,128)(2,1)S(1)} %get-tuple-element.48), channel_id=1, source_target_pairs={{0,12},{4,8},{8,4},{12,0},{1,13},{5,9},{9,5},{13,1},{2,14},{6,10},... | collective-permute-start | bytes 110600 | tf_op jit(solution)/shard_map/ppermute | solution.py:371
  24.1 4.9 %collective-permute-start.8 = (bf16[72,256]{1,0:T(8,128)(2,1)S(1)}, bf16[72,256]{1,0:T(8,128)(2,1)S(1)}, u32[]{:S(2)}, u32[]{:S(2)}) collective-permute-start(bf16[72,256]{1,0:T(8,128)(2,1)S(1)} %get-tuple-element.49), channel_id=1, source_target_pairs={{0,8},{4,12},{8,0},{12,4},{1,9},{5,13},{9,1},{13,5},{2,10},{6,14},... | collective-permute-start | bytes 110600 | tf_op jit(solution)/shard_map/ppermute | solution.py:371
  24.1 4.9 %collective-permute-start.9 = (bf16[72,256]{1,0:T(8,128)(2,1)S(1)}, bf16[72,256]{1,0:T(8,128)(2,1)S(1)}, u32[]{:S(2)}, u32[]{:S(2)}) collective-permute-start(bf16[72,256]{1,0:T(8,128)(2,1)S(1)} %get-tuple-element.50), channel_id=1, source_target_pairs={{0,4},{4,0},{8,12},{12,8},{1,5},{5,1},{9,13},{13,9},{2,6},{6,2},{1... | collective-permute-start | bytes 110600 | tf_op jit(solution)/shard_map/ppermute | solution.py:371
  29.9 1.7 %collective-permute-start.10 = (bf16[648,256]{1,0:T(8,128)(2,1)S(1)}, bf16[648,256]{1,0:T(8,128)(2,1)S(1)}, u32[]{:S(2)}, u32[]{:S(2)}) collective-permute-start(bf16[648,256]{1,0:T(8,128)(2,1)S(1)} %get-tuple-element.60), channel_id=1, source_target_pairs={{0,1},{1,0},{2,3},{3,2},{4,5},{5,4},{6,7},{7,6},{8,9},{9,8},{10,11... | collective-permute-start | bytes 995336 | tf_op jit(solution)/shard_map/ppermute | solution.py:343
  31.7 9.3 %collective-permute-start.18 = (bf16[576,256]{1,0:T(8,128)(2,1)S(1)}, bf16[576,256]{1,0:T(8,128)(2,1)S(1)}, u32[]{:S(2)}, u32[]{:S(2)}) collective-permute-start(bf16[576,256]{1,0:T(8,128)(2,1)S(1)} %get-tuple-element.67.a_ref), channel_id=1, source_target_pairs={{0,2},{2,0},{1,3},{3,1},{4,6},{6,4},{5,7},{7,5},{8,10},{10,8},{9,1... | collective-permute-start | bytes 884744 | tf_op jit(solution)/shard_map/ppermute | solution.py:371
  32.6 8.3 %collective-permute-start.11 = (bf16[136,256]{1,0:T(8,128)(2,1)S(1)}, bf16[136,256]{1,0:T(8,128)(2,1)S(1)}, u32[]{:S(2)}, u32[]{:S(2)}) collective-permute-start(bf16[136,256]{1,0:T(8,128)(2,1)S(1)} %get-tuple-element.62), channel_id=1, source_target_pairs={{0,4},{4,0},{8,12},{12,8},{1,5},{5,1},{9,13},{13,9},{2,6},{6,2},{1... | collective-permute-start | bytes 208904 | tf_op jit(solution)/shard_map/ppermute | solution.py:371
  33.7 6.0 %collective-permute-start.14 = (bf16[72,256]{1,0:T(8,128)(2,1)S(1)}, bf16[72,256]{1,0:T(8,128)(2,1)S(1)}, u32[]{:S(2)}, u32[]{:S(2)}) collective-permute-start(bf16[72,256]{1,0:T(8,128)(2,1)S(1)} %get-tuple-element.66.refs_0_), channel_id=1, source_target_pairs={{0,8},{4,12},{8,0},{12,4},{1,9},{5,13},{9,1},{13,5},{2,10},{6,14},... | collective-permute-start | bytes 110600 | tf_op jit(solution)/shard_map/ppermute | solution.py:371
  35.1 5.9 %collective-permute-start.13 = (bf16[72,256]{1,0:T(8,128)(2,1)S(1)}, bf16[72,256]{1,0:T(8,128)(2,1)S(1)}, u32[]{:S(2)}, u32[]{:S(2)}) collective-permute-start(bf16[72,256]{1,0:T(8,128)(2,1)S(1)} %get-tuple-element.66.refs_0_), channel_id=1, source_target_pairs={{0,12},{4,8},{8,4},{12,0},{1,13},{5,9},{9,5},{13,1},{2,14},{6,10},... | collective-permute-start | bytes 110600 | tf_op jit(solution)/shard_map/ppermute | solution.py:371
  37.0 1.2 %collective-permute-start.12 = (bf16[64,256]{1,0:T(8,128)(2,1)S(1)}, bf16[64,256]{1,0:T(8,128)(2,1)S(1)}, u32[]{:S(2)}, u32[]{:S(2)}) collective-permute-start(bf16[64,256]{1,0:T(8,128)(2,1)S(1)} %get-tuple-element.63), channel_id=1, source_target_pairs={{0,1},{1,0},{4,8},{5,9},{8,4},{9,5},{12,13},{13,12},{2,3},{3,2},{6... | collective-permute-start | bytes 98312 | tf_op jit(solution)/shard_map/ppermute | solution.py:357
  41.0 3.5 %collective-permute-start.19 = (bf16[576,256]{1,0:T(8,128)(2,1)S(1)}, bf16[576,256]{1,0:T(8,128)(2,1)S(1)}, u32[]{:S(2)}, u32[]{:S(2)}) collective-permute-start(bf16[576,256]{1,0:T(8,128)(2,1)S(1)} %shard_map.77.mine_ref), channel_id=1, source_target_pairs={{0,1},{1,0},{2,3},{3,2},{4,5},{5,4},{6,7},{7,6},{8,9},{9,8},{10,11... | collective-permute-start | bytes 884744 | tf_op jit(solution)/shard_map/ppermute | solution.py:343
  41.1 4.5 %collective-permute-start.17 = (bf16[72,256]{1,0:T(8,128)(2,1)S(1)}, bf16[72,256]{1,0:T(8,128)(2,1)S(1)}, u32[]{:S(2)}, u32[]{:S(2)}) collective-permute-start(bf16[72,256]{1,0:T(8,128)(2,1)S(1)} %shard_map.76.refs_0_.mine_ref), channel_id=1, source_target_pairs={{0,2},{2,0},{1,3},{3,1},{4,6},{6,4},{5,7},{7,5},{8,10},{10,8},{9,1... | collective-permute-start | bytes 110600 | tf_op jit(solution)/shard_map/ppermute | solution.py:371
  42.3 3.4 %collective-permute-start.16 = (bf16[72,256]{1,0:T(8,128)(2,1)S(1)}, bf16[72,256]{1,0:T(8,128)(2,1)S(1)}, u32[]{:S(2)}, u32[]{:S(2)}) collective-permute-start(bf16[72,256]{1,0:T(8,128)(2,1)S(1)} %shard_map.76.refs_0_.mine_ref), channel_id=1, source_target_pairs={{0,3},{1,2},{2,1},{3,0},{4,7},{5,6},{6,5},{7,4},{8,11},{9,10},{10,... | collective-permute-start | bytes 110600 | tf_op jit(solution)/shard_map/ppermute | solution.py:377
  43.0 2.7 %collective-permute-start.15 = (bf16[72,256]{1,0:T(8,128)(2,1)S(1)}, bf16[72,256]{1,0:T(8,128)(2,1)S(1)}, u32[]{:S(2)}, u32[]{:S(2)}) collective-permute-start(bf16[72,256]{1,0:T(8,128)(2,1)S(1)} %shard_map.76.refs_0_.mine_ref), channel_id=1, source_target_pairs={{0,1},{1,0},{2,3},{3,2},{4,5},{5,4},{6,7},{7,6},{8,9},{9,8},{10,11... | collective-permute-start | bytes 110600 | tf_op jit(solution)/shard_map/ppermute | solution.py:343

commit v25 on v24

--- a/solution.py
+++ b/solution.py
@@ -302,7 +302,16 @@
         ref[half:] = part_ref[pl.ds(pl.multiple_of(place * HALF_ONE, 8), HALF_ONE)].astype(BF16)
 
 
-def layer_one_back(g_ref, a_ref, b_ref, w_ref, out_ref, done_ref, *, bands):
+def last_outputs(
+    g_ref, a_ref, b_ref, w_ref, mine_ref, other_ref, out_ref, two_hbm, done_ref, two_ref, sems, *, bands, scale
+):
+    pair, half = lax.axis_index("pair"), mine_ref.shape[0]
+    copies = []
+    for n, (ref, place) in enumerate(((mine_ref, pair), (other_ref, 1 - pair))):
+        target = pl.ds(pl.multiple_of(place * half, 16), half)
+        two_ref[n] = ref[...].astype(F32) * scale
+        copies.append(pltpu.make_async_copy(two_ref.at[n], two_hbm.at[target], sems.at[n]))
+        copies[-1].start()
     above, below = beside(a_ref.at[: b_ref.shape[0]], b_ref, lax.axis_index("row"), bands)
     done_ref[...] = jnp.zeros(done_ref.shape, F32)
     lines = [above] + [g_ref[h] for h in range(8)] + [below]
@@ -311,22 +320,11 @@
         z = dot(w_ref[...], jnp.concatenate(lines[h : h + 3], 0), (1, 0))
         rows.append((roll(z[:64], -1, 1) + z[64:128] + roll(z[128:], 1, 1))[:, :128])
     out_ref[...] = jnp.swapaxes(jnp.stack(rows, 0), 0, 1).astype(BF16)
-
-
-def finish_two(mine_ref, other_ref, two_hbm, done_ref, two_ref, sems, *, scale):
-    pair, half = lax.axis_index("pair"), mine_ref.shape[0]
-    done_ref[...] = jnp.zeros(done_ref.shape, F32)
-    copies = []
-    for n, (ref, place) in enumerate(((mine_ref, pair), (other_ref, 1 - pair))):
-        rows = pl.ds(pl.multiple_of(place * half, 16), half)
-        two_ref[n] = ref[...].astype(F32) * scale
-        copies.append(pltpu.make_async_copy(two_ref.at[n], two_hbm.at[rows], sems.at[n]))
-        copies[-1].start()
     for copy in copies:
         copy.wait()
 
 
-def finish_one(mine_ref, beside_ref, corner_ref, across_ref, _, __, out_ref, flat_ref, *, scale):
+def finish_one(mine_ref, beside_ref, corner_ref, across_ref, _, out_ref, flat_ref, *, scale):
     pair = lax.axis_index("pair")
     for refs, place in (((mine_ref, across_ref), pair), ((beside_ref, corner_ref), 1 - pair)):
         total = refs[0][...].astype(F32) + refs[1][...].astype(F32)
@@ -497,20 +495,14 @@
     near = ones[row_order(bands, near_first=True, by_half=True).index(1)]
     up_b = odd_row_swap(up_b)
     (one,) = whole_call(sum_rows, [shaped(one.shape)], ones + [up_b], 0, after=1)
-    input_grad, done = whole_call(
-        functools.partial(layer_one_back, bands=bands),
-        [shaped(features_in.shape), shaped((8, 128), F32)],
-        [g, near, up_b, back_one],
+    mine_two = added(two, two_more, one)
+    input_grad, grad_two, done = whole_call(
+        functools.partial(last_outputs, bands=bands, scale=1.0 / math.sqrt(pooled_rows * total)),
+        [shaped(features_in.shape), shaped((2 * half, 256), F32), shaped((8, 128), F32)],
+        [g, near, up_b, back_one, mine_two, even_swap(mine_two, "pair", 2)],
         2 * band_rows * 192 * 192 * 256,
-    )
-    mine_two = added(two, two_more, one)
-    grad_two, wrote = whole_call(
-        functools.partial(finish_two, scale=1.0 / math.sqrt(pooled_rows * total)),
-        [shaped((2 * half, 256), F32), shaped((8, 128), F32)],
-        [mine_two, even_swap(mine_two, "pair", 2)],
-        10**8,
         scratch=[pltpu.VMEM((2, half, 256), F32), pltpu.SemaphoreType.DMA((2,))],
-        out_spaces=[pl.ANY, pltpu.VMEM],
+        out_spaces=[pltpu.VMEM, pl.ANY, pltpu.VMEM],
     )
     one, across = sum_but_last(one, "col", columns)
     beside_one = even_swap(one, "pair", 2)
@@ -518,10 +510,10 @@
     (grad_one,) = whole_call(
         functools.partial(finish_one, scale=1.0 / math.sqrt(height * width)),
         [shaped((3, 3 * channels, channels), F32)],
-        [one, beside_one, corner, across, wrote, done],
+        [one, beside_one, corner, across, done],
         1,
         scratch=[pltpu.VMEM((144, 256), F32)],
-        after=2,
+        after=1,
     )
     grad_two = jnp.transpose(grad_two.reshape(3, 3, filters, 4 * channels), (2, 0, 1, 3))
     grad_one = jnp.transpose(grad_one.reshape(3, 3, channels, channels), (2, 0, 1, 3))

time: 46.8 us -> 46.8 us (level)
    pallas_call x13 -> x12, Pallas kernels: 7.08 us -> 7.07 us  [whole_call(): pl.pallas_call(body, out_shape=outs, in_specs=specs, out_specs=[pl.BlockS...]
where the time goes in v25:
time: 46.8 us; the launch traced here: 46.6 us
  starting transfers between devices  22.6 us (48%)
  waiting for transfers between devices  13.3 us (28%)
  Pallas kernels  7.07 us (15%)
  local copies, waits for them, and re-layouts  2.78 us (6%)
  between operations  0.8 us (2%)
    ppermute x11, starting transfers between devices, xor_swap(): return lax.ppermute(values, axis, [(n, n ^ k) for n in range(count)])  16.2 us
    ppermute x11, waiting for transfers between devices, xor_swap(): return lax.ppermute(values, axis, [(n, n ^ k) for n in range(count)])  8.85 us
    pallas_call x12, Pallas kernels, whole_call(): pl.pallas_call(body, out_shape=outs, in_specs=specs, out_specs=[pl.BlockS...  7.07 us
    ppermute x5, starting transfers between devices, even_swap(): return lax.ppermute(values, axis, [(n, n ^ 1) for n in range(count)])  3.66 us
    unnamed x6, local copies, waits for them, and re-layouts  2.75 us
    ppermute x5, waiting for transfers between devices, even_swap(): return lax.ppermute(values, axis, [(n, n ^ 1) for n in range(count)])  2.35 us
    ppermute x1, starting transfers between devices, odd_strip_swap(): return lax.ppermute(values, ('grp',) + COLS, steps)  2.01 us
    ppermute x2, waiting for transfers between devices, odd_row_swap(): return lax.ppermute(values, ('row', 'pair'), steps)  1.21 us
  transfers between devices with their start and end apart: 20, of which 12 were waited for; matrix products, arithmetic and copies ran while one was open for 2% of the time, Pallas kernels for 7%

profile of v25, /device:TPU:0, one launch (start us, length us, event | category | flops | bytes accessed | tf_op | source)
XLA Modules:
  0.0 46.6 jit_solution(8466115726329358905)
XLA Ops:
  0.7 1.0 %copy.19 = bf16[64,8,128]{2,0,1:T(8,128)(2,1)S(1)} copy(bf16[64,8,128]{2,1,0:T(8,128)(2,1)} %param.4) | data formatting | bytes 262144 | tf_op args[0]
  1.7 3.1 %collective-permute-start.1 = (bf16[64,128]{1,0:T(8,128)(2,1)S(1)}, bf16[64,128]{1,0:T(8,128)(2,1)S(1)}, u32[]{:S(2)}, u32[]{:S(2)}) collective-permute-start(bf16[64,128]{1,0:T(8,128)(2,1)S(1)} %get-tuple-element.69), channel_id=1, source_target_pairs={{0,4},{4,0},{8,12},{12,8},{1,5},{5,1},{9,13},{13,9},{2,6},{6,2},{1... | collective-permute-start | bytes 49160 | tf_op jit(solution)/shard_map/ppermute | solution.py:341
  6.6 2.0 %collective-permute-start.2 = (bf16[144,128]{1,0:T(8,128)(2,1)S(1)}, bf16[144,128]{1,0:T(8,128)(2,1)S(1)}, u32[]{:S(2)}, u32[]{:S(2)}) collective-permute-start(bf16[144,128]{1,0:T(8,128)(2,1)S(1)} %get-tuple-element.38), channel_id=1, source_target_pairs={{0,16},{1,2},{2,1},{3,19},{16,0},{17,18},{18,17},{19,3},{4,20},{5,... | collective-permute-start | bytes 110600 | tf_op jit(solution)/shard_map/ppermute | solution.py:365
  8.7 0.9 %copy-done.1 = bf16[64,3,3,64]{3,0,2,1:T(8,128)(2,1)S(1)} copy-done((bf16[64,3,3,64]{3,0,2,1:T(8,128)(2,1)S(1)}, bf16[64,3,3,64]{3,0,2,1:T(8,128)(2,1)}, u32[]{:S(2)}) %copy-start.1) | copy-done | bytes 73752
  10.6 0.9 %shard_map.70 = (bf16[2,40,256]{2,1,0:T(8,128)(2,1)S(1)}, bf16[8,64,256]{2,1,0:T(8,128)(2,1)S(1)}, bf16[10,64,256]{2,1,0:T(8,128)(2,1)S(1)}) custom-call(bf16[8,64,128]{2,1,0:T(8,128)(2,1)S(1)} %bitcast.34, bf16[64,128]{1,0:T(8,128)(2,1)S(1)} %get-tuple-element.40.above_ref, bf16[64,128]{1,0:T(8,128)(2,1)S(1)} %get-tuple-element.41.below_ref, ...), custom_call_target="tpu_custom_call" | custom-call | flops 150994944 | bytes 1122304 | tf_op jit(solution)/shard_map/pallas_call | solution.py:30
  11.4 4.1 %collective-permute-start.6 = (bf16[2,40,256]{2,1,0:T(8,128)(2,1)S(1)}, bf16[2,40,256]{2,1,0:T(8,128)(2,1)S(1)}, u32[]{:S(2)}, u32[]{:S(2)}) collective-permute-start(bf16[2,40,256]{2,1,0:T(8,128)(2,1)S(1)} %get-tuple-element.45.refs_0_), channel_id=1, source_target_pairs={{0,12},{4,8},{8,4},{12,0},{1,13},{5,9},{9,5},{13,1},{2,14},{6,10},... | collective-permute-start | bytes 122888 | tf_op jit(solution)/shard_map/ppermute | solution.py:369
  17.5 3.0 %collective-permute-done.5.refs_2_ = bf16[2,40,256]{2,1,0:T(8,128)(2,1)S(1)} collective-permute-done((bf16[2,40,256]{2,1,0:T(8,128)(2,1)S(1)}, bf16[2,40,256]{2,1,0:T(8,128)(2,1)S(1)}, u32[]{:S(2)}, u32[]{:S(2)}) %collective-permute-start.5) | collective-permute-done | bytes 40992 | tf_op jit(solution)/shard_map/ppermute | solution.py:369
  20.6 1.0 %shard_map.71 = (bf16[72,256]{1,0:T(8,128)(2,1)S(1)}, bf16[72,256]{1,0:T(8,128)(2,1)S(1)}, bf16[72,256]{1,0:T(8,128)(2,1)S(1)}, bf16[72,256]{1,0:T(8,128)(2,1)S(...) custom-call(bf16[8,48,128]{2,1,0:T(8,128)(2,1)S(1)} %fusion.6.og_ref, ...), custom_call_target="tpu_custom_call" | custom-call | flops 452984832 | bytes 1368064 | tf_op jit(solution)/shard_map/pallas_call | solution.py:30
  21.7 2.5 %collective-permute-start.7 = (bf16[72,256]{1,0:T(8,128)(2,1)S(1)}, bf16[72,256]{1,0:T(8,128)(2,1)S(1)}, u32[]{:S(2)}, u32[]{:S(2)}) collective-permute-start(bf16[72,256]{1,0:T(8,128)(2,1)S(1)} %get-tuple-element.47), channel_id=1, source_target_pairs={{0,12},{4,8},{8,4},{12,0},{1,13},{5,9},{9,5},{13,1},{2,14},{6,10},... | collective-permute-start | bytes 110600 | tf_op jit(solution)/shard_map/ppermute | solution.py:369
  24.1 2.0 %collective-permute-start.9 = (bf16[72,256]{1,0:T(8,128)(2,1)S(1)}, bf16[72,256]{1,0:T(8,128)(2,1)S(1)}, u32[]{:S(2)}, u32[]{:S(2)}) collective-permute-start(bf16[72,256]{1,0:T(8,128)(2,1)S(1)} %get-tuple-element.49), channel_id=1, source_target_pairs={{0,4},{4,0},{8,12},{12,8},{1,5},{5,1},{9,13},{13,9},{2,6},{6,2},{1... | collective-permute-start | bytes 110600 | tf_op jit(solution)/shard_map/ppermute | solution.py:369
  26.7 1.0 %collective-permute-done.7.refs_1_ = bf16[72,256]{1,0:T(8,128)(2,1)S(1)} collective-permute-done((bf16[72,256]{1,0:T(8,128)(2,1)S(1)}, bf16[72,256]{1,0:T(8,128)(2,1)S(1)}, u32[]{:S(2)}, u32[]{:S(2)}) %collective-permute-start.7) | collective-permute-done | bytes 36896 | tf_op jit(solution)/shard_map/ppermute | solution.py:369
  27.7 1.3 %collective-permute-done.8.refs_2_ = bf16[72,256]{1,0:T(8,128)(2,1)S(1)} collective-permute-done((bf16[72,256]{1,0:T(8,128)(2,1)S(1)}, bf16[72,256]{1,0:T(8,128)(2,1)S(1)}, u32[]{:S(2)}, u32[]{:S(2)}) %collective-permute-start.8) | collective-permute-done | bytes 36896 | tf_op jit(solution)/shard_map/ppermute | solution.py:369
  29.0 0.9 %shard_map.73 = (bf16[8,64,256]{2,1,0:T(8,128)(2,1)S(1)}, bf16[64,256]{1,0:T(8,128)(2,1)S(1)}, bf16[64,256]{1,0:T(8,128)(2,1)S(1)}, bf16[648,256]{1,0:T(8,128)(2,1)S(1)}, bf16[648,256]{1,0:T(8,128)(2,1)S(1)}) custom-call(bf16[72,256]{1,0:T(8,128)(2,1)S(1)} %get-tuple-element.46.refs_0_, bf16[72,256]{1,0:T(8,128)(2,1)S(1)} %collective-permute-done.7.refs_1_, ...), custom_call_target="tpu_custom_call" | custom-call | flops 150994944 | bytes 2498560 | tf_op jit(solution)/shard_map/pallas_call | solution.py:30
  30.0 1.6 %collective-permute-done.10.b_ref = bf16[648,256]{1,0:T(8,128)(2,1)S(1)} collective-permute-done((bf16[648,256]{1,0:T(8,128)(2,1)S(1)}, bf16[648,256]{1,0:T(8,128)(2,1)S(1)}, u32[]{:S(2)}, u32[]{:S(2)}) %collective-permute-start.10) | collective-permute-done | bytes 331808 | tf_op jit(solution)/shard_map/ppermute | solution.py:341
  31.7 1.0 %collective-permute-start.13 = (bf16[576,256]{1,0:T(8,128)(2,1)S(1)}, bf16[576,256]{1,0:T(8,128)(2,1)S(1)}, u32[]{:S(2)}, u32[]{:S(2)}) collective-permute-start(bf16[576,256]{1,0:T(8,128)(2,1)S(1)} %get-tuple-element.64.a_ref), channel_id=1, source_target_pairs={{0,2},{2,0},{1,3},{3,1},{4,6},{6,4},{5,7},{7,5},{8,10},{10,8},{9,1... | collective-permute-start | bytes 884744 | tf_op jit(solution)/shard_map/ppermute | solution.py:369
  32.6 1.1 %collective-permute-start.11 = (bf16[136,256]{1,0:T(8,128)(2,1)S(1)}, bf16[136,256]{1,0:T(8,128)(2,1)S(1)}, u32[]{:S(2)}, u32[]{:S(2)}) collective-permute-start(bf16[136,256]{1,0:T(8,128)(2,1)S(1)} %get-tuple-element.61), channel_id=1, source_target_pairs={{0,4},{4,0},{8,12},{12,8},{1,5},{5,1},{9,13},{13,9},{2,6},{6,2},{1... | collective-permute-start | bytes 208904 | tf_op jit(solution)/shard_map/ppermute | solution.py:369
  33.7 1.3 %collective-permute-start.15 = (bf16[72,256]{1,0:T(8,128)(2,1)S(1)}, bf16[72,256]{1,0:T(8,128)(2,1)S(1)}, u32[]{:S(2)}, u32[]{:S(2)}) collective-permute-start(bf16[72,256]{1,0:T(8,128)(2,1)S(1)} %get-tuple-element.65.refs_0_), channel_id=1, source_target_pairs={{0,8},{4,12},{8,0},{12,4},{1,9},{5,13},{9,1},{13,5},{2,10},{6,14},... | collective-permute-start | bytes 110600 | tf_op jit(solution)/shard_map/ppermute | solution.py:369
  35.1 2.0 %collective-permute-start.14 = (bf16[72,256]{1,0:T(8,128)(2,1)S(1)}, bf16[72,256]{1,0:T(8,128)(2,1)S(1)}, u32[]{:S(2)}, u32[]{:S(2)}) collective-permute-start(bf16[72,256]{1,0:T(8,128)(2,1)S(1)} %get-tuple-element.65.refs_0_), channel_id=1, source_target_pairs={{0,12},{4,8},{8,4},{12,0},{1,13},{5,9},{9,5},{13,1},{2,14},{6,10},... | collective-permute-start | bytes 110600 | tf_op jit(solution)/shard_map/ppermute | solution.py:369
  37.0 1.2 %collective-permute-done.12.refs_4_.b_ref = bf16[64,256]{1,0:T(8,128)(2,1)S(1)} collective-permute-done((bf16[64,256]{1,0:T(8,128)(2,1)S(1)}, bf16[64,256]{1,0:T(8,128)(2,1)S(1)}, u32[]{:S(2)}, u32[]{:S(2)}) %collective-permute-start.12) | collective-permute-done | bytes 32800 | tf_op jit(solution)/shard_map/ppermute | solution.py:355
  38.2 1.5 %collective-permute-done.15.refs_3_ = bf16[72,256]{1,0:T(8,128)(2,1)S(1)} collective-permute-done((bf16[72,256]{1,0:T(8,128)(2,1)S(1)}, bf16[72,256]{1,0:T(8,128)(2,1)S(1)}, u32[]{:S(2)}, u32[]{:S(2)}) %collective-permute-start.15) | collective-permute-done | bytes 36896 | tf_op jit(solution)/shard_map/ppermute | solution.py:369
  39.8 1.2 %collective-permute-done.14.refs_2_ = bf16[72,256]{1,0:T(8,128)(2,1)S(1)} collective-permute-done((bf16[72,256]{1,0:T(8,128)(2,1)S(1)}, bf16[72,256]{1,0:T(8,128)(2,1)S(1)}, u32[]{:S(2)}, u32[]{:S(2)}) %collective-permute-start.14) | collective-permute-done | bytes 36896 | tf_op jit(solution)/shard_map/ppermute | solution.py:369
  41.1 1.2 %collective-permute-start.19 = (bf16[72,256]{1,0:T(8,128)(2,1)S(1)}, bf16[72,256]{1,0:T(8,128)(2,1)S(1)}, u32[]{:S(2)}, u32[]{:S(2)}) collective-permute-start(bf16[72,256]{1,0:T(8,128)(2,1)S(1)} %shard_map.75.refs_0_.mine_ref), channel_id=1, source_target_pairs={{0,2},{2,0},{1,3},{3,1},{4,6},{6,4},{5,7},{7,5},{8,10},{10,8},{9,1... | collective-permute-start | bytes 110600 | tf_op jit(solution)/shard_map/ppermute | solution.py:369
  43.3 2.2 %shard_map.77 = (bf16[64,8,128]{2,1,0:T(8,128)(2,1)}, f32[1152,256]{1,0:T(8,128)}, f32[8,128]{1,0:T(8,128)S(1)}) custom-call(bf16[8,64,256]{2,1,0:T(8,128)(2,1)S(1)} %get-tuple-element.57.g_ref, bf16[136,256]{1,0:T(8,128)(2,1)S(1)} %collective-permute-done.11.refs_1_.a_ref, bf16[64,256]{1,0:T(8,128)(2,1)S(1)} %collective-permute-done.12.refs_4_.b_ref, ...), custom_call_target="tpu_custom_call" | custom-call | flops 150994944 | bytes 2342912 | tf_op jit(solution)/shard_map/pallas_call | solution.py:30
  45.7 0.9 %shard_map.78 = f32[3,192,64]{2,1,0:T(8,128)} custom-call(bf16[72,256]{1,0:T(8,128)(2,1)S(1)} %shard_map.75.refs_0_.mine_ref, bf16[72,256]{1,0:T(8,128)(2,1)S(1)} %collective-permute-done.17.beside_ref, bf16[72,256]{1,0:T(8,128)(2,1)S(1)} %collective-permute-done.18.corner_ref, bf16[72,256]{1,0:T(8,128)(2,1)S(1)} %collective-permute-done.19.across_ref, ...), custom_call_target="tpu_custom_call" | custom-call | flops 1 | bytes 299008 | tf_op jit(solution)/shard_map/pallas_call | solution.py:30
  (41 shorter events, 7.0 us)
Async XLA Ops:
  0.6 20.0 %copy-start = (bf16[128,3,3,256]{3,0,2,1:T(8,128)(2,1)S(1)}, bf16[128,3,3,256]{3,0,2,1:T(8,128)(2,1)}, u32[]{:S(2)}) copy-start(bf16[128,3,3,256]{3,0,2,1:T(8,128)(2,1)} %param.6) | copy-start | bytes 1769476
  1.7 4.8 %collective-permute-start.1 = (bf16[64,128]{1,0:T(8,128)(2,1)S(1)}, bf16[64,128]{1,0:T(8,128)(2,1)S(1)}, u32[]{:S(2)}, u32[]{:S(2)}) collective-permute-start(bf16[64,128]{1,0:T(8,128)(2,1)S(1)} %get-tuple-element.69), channel_id=1, source_target_pairs={{0,4},{4,0},{8,12},{12,8},{1,5},{5,1},{9,13},{13,9},{2,6},{6,2},{1... | collective-permute-start | bytes 49160 | tf_op jit(solution)/shard_map/ppermute | solution.py:341
  4.7 1.7 %collective-permute-start = (bf16[64,128]{1,0:T(8,128)(2,1)S(1)}, bf16[64,128]{1,0:T(8,128)(2,1)S(1)}, u32[]{:S(2)}, u32[]{:S(2)}) collective-permute-start(bf16[64,128]{1,0:T(8,128)(2,1)S(1)} %get-tuple-element.70), channel_id=1, source_target_pairs={{0,1},{1,0},{4,8},{5,9},{8,4},{9,5},{12,13},{13,12},{2,3},{3,2},{6... | collective-permute-start | bytes 49160 | tf_op jit(solution)/shard_map/ppermute | solution.py:355
  6.6 4.0 %collective-permute-start.2 = (bf16[144,128]{1,0:T(8,128)(2,1)S(1)}, bf16[144,128]{1,0:T(8,128)(2,1)S(1)}, u32[]{:S(2)}, u32[]{:S(2)}) collective-permute-start(bf16[144,128]{1,0:T(8,128)(2,1)S(1)} %get-tuple-element.38), channel_id=1, source_target_pairs={{0,16},{1,2},{2,1},{3,19},{16,0},{17,18},{18,17},{19,3},{4,20},{5,... | collective-permute-start | bytes 110600 | tf_op jit(solution)/shard_map/ppermute | solution.py:365
  8.6 2.0 %collective-permute-start.3 = (bf16[144,128]{1,0:T(8,128)(2,1)S(1)}, bf16[144,128]{1,0:T(8,128)(2,1)S(1)}, u32[]{:S(2)}, u32[]{:S(2)}) collective-permute-start(bf16[144,128]{1,0:T(8,128)(2,1)S(1)} %get-tuple-element.39), channel_id=1, source_target_pairs={{0,1},{1,0},{2,3},{3,2},{4,5},{5,4},{6,7},{7,6},{8,9},{9,8},{10,11... | collective-permute-start | bytes 110600 | tf_op jit(solution)/shard_map/ppermute | solution.py:341
  8.7 0.9 %copy-start.1 = (bf16[64,3,3,64]{3,0,2,1:T(8,128)(2,1)S(1)}, bf16[64,3,3,64]{3,0,2,1:T(8,128)(2,1)}, u32[]{:S(2)}) copy-start(bf16[64,3,3,64]{3,0,2,1:T(8,128)(2,1)} %param.5) | copy-start | bytes 221188
  11.4 6.1 %collective-permute-start.6 = (bf16[2,40,256]{2,1,0:T(8,128)(2,1)S(1)}, bf16[2,40,256]{2,1,0:T(8,128)(2,1)S(1)}, u32[]{:S(2)}, u32[]{:S(2)}) collective-permute-start(bf16[2,40,256]{2,1,0:T(8,128)(2,1)S(1)} %get-tuple-element.45.refs_0_), channel_id=1, source_target_pairs={{0,12},{4,8},{8,4},{12,0},{1,13},{5,9},{9,5},{13,1},{2,14},{6,10},... | collective-permute-start | bytes 122888 | tf_op jit(solution)/shard_map/ppermute | solution.py:369
  15.6 5.0 %collective-permute-start.5 = (bf16[2,40,256]{2,1,0:T(8,128)(2,1)S(1)}, bf16[2,40,256]{2,1,0:T(8,128)(2,1)S(1)}, u32[]{:S(2)}, u32[]{:S(2)}) collective-permute-start(bf16[2,40,256]{2,1,0:T(8,128)(2,1)S(1)} %get-tuple-element.45.refs_0_), channel_id=1, source_target_pairs={{0,8},{4,12},{8,0},{12,4},{1,9},{5,13},{9,1},{13,5},{2,10},{6,14},... | collective-permute-start | bytes 122888 | tf_op jit(solution)/shard_map/ppermute | solution.py:369
  16.2 4.4 %collective-permute-start.4 = (bf16[2,40,256]{2,1,0:T(8,128)(2,1)S(1)}, bf16[2,40,256]{2,1,0:T(8,128)(2,1)S(1)}, u32[]{:S(2)}, u32[]{:S(2)}) collective-permute-start(bf16[2,40,256]{2,1,0:T(8,128)(2,1)S(1)} %get-tuple-element.45.refs_0_), channel_id=1, source_target_pairs={{0,4},{4,0},{8,12},{12,8},{1,5},{5,1},{9,13},{13,9},{2,6},{6,2},{1... | collective-permute-start | bytes 122888 | tf_op jit(solution)/shard_map/ppermute | solution.py:369
  21.7 6.1 %collective-permute-start.7 = (bf16[72,256]{1,0:T(8,128)(2,1)S(1)}, bf16[72,256]{1,0:T(8,128)(2,1)S(1)}, u32[]{:S(2)}, u32[]{:S(2)}) collective-permute-start(bf16[72,256]{1,0:T(8,128)(2,1)S(1)} %get-tuple-element.47), channel_id=1, source_target_pairs={{0,12},{4,8},{8,4},{12,0},{1,13},{5,9},{9,5},{13,1},{2,14},{6,10},... | collective-permute-start | bytes 110600 | tf_op jit(solution)/shard_map/ppermute | solution.py:369
  24.1 4.9 %collective-permute-start.8 = (bf16[72,256]{1,0:T(8,128)(2,1)S(1)}, bf16[72,256]{1,0:T(8,128)(2,1)S(1)}, u32[]{:S(2)}, u32[]{:S(2)}) collective-permute-start(bf16[72,256]{1,0:T(8,128)(2,1)S(1)} %get-tuple-element.48), channel_id=1, source_target_pairs={{0,8},{4,12},{8,0},{12,4},{1,9},{5,13},{9,1},{13,5},{2,10},{6,14},... | collective-permute-start | bytes 110600 | tf_op jit(solution)/shard_map/ppermute | solution.py:369
  24.1 4.9 %collective-permute-start.9 = (bf16[72,256]{1,0:T(8,128)(2,1)S(1)}, bf16[72,256]{1,0:T(8,128)(2,1)S(1)}, u32[]{:S(2)}, u32[]{:S(2)}) collective-permute-start(bf16[72,256]{1,0:T(8,128)(2,1)S(1)} %get-tuple-element.49), channel_id=1, source_target_pairs={{0,4},{4,0},{8,12},{12,8},{1,5},{5,1},{9,13},{13,9},{2,6},{6,2},{1... | collective-permute-start | bytes 110600 | tf_op jit(solution)/shard_map/ppermute | solution.py:369
  29.9 1.7 %collective-permute-start.10 = (bf16[648,256]{1,0:T(8,128)(2,1)S(1)}, bf16[648,256]{1,0:T(8,128)(2,1)S(1)}, u32[]{:S(2)}, u32[]{:S(2)}) collective-permute-start(bf16[648,256]{1,0:T(8,128)(2,1)S(1)} %get-tuple-element.59), channel_id=1, source_target_pairs={{0,1},{1,0},{2,3},{3,2},{4,5},{5,4},{6,7},{7,6},{8,9},{9,8},{10,11... | collective-permute-start | bytes 995336 | tf_op jit(solution)/shard_map/ppermute | solution.py:341
  31.7 9.3 %collective-permute-start.13 = (bf16[576,256]{1,0:T(8,128)(2,1)S(1)}, bf16[576,256]{1,0:T(8,128)(2,1)S(1)}, u32[]{:S(2)}, u32[]{:S(2)}) collective-permute-start(bf16[576,256]{1,0:T(8,128)(2,1)S(1)} %get-tuple-element.64.a_ref), channel_id=1, source_target_pairs={{0,2},{2,0},{1,3},{3,1},{4,6},{6,4},{5,7},{7,5},{8,10},{10,8},{9,1... | collective-permute-start | bytes 884744 | tf_op jit(solution)/shard_map/ppermute | solution.py:369
  32.6 8.3 %collective-permute-start.11 = (bf16[136,256]{1,0:T(8,128)(2,1)S(1)}, bf16[136,256]{1,0:T(8,128)(2,1)S(1)}, u32[]{:S(2)}, u32[]{:S(2)}) collective-permute-start(bf16[136,256]{1,0:T(8,128)(2,1)S(1)} %get-tuple-element.61), channel_id=1, source_target_pairs={{0,4},{4,0},{8,12},{12,8},{1,5},{5,1},{9,13},{13,9},{2,6},{6,2},{1... | collective-permute-start | bytes 208904 | tf_op jit(solution)/shard_map/ppermute | solution.py:369
  33.7 6.0 %collective-permute-start.15 = (bf16[72,256]{1,0:T(8,128)(2,1)S(1)}, bf16[72,256]{1,0:T(8,128)(2,1)S(1)}, u32[]{:S(2)}, u32[]{:S(2)}) collective-permute-start(bf16[72,256]{1,0:T(8,128)(2,1)S(1)} %get-tuple-element.65.refs_0_), channel_id=1, source_target_pairs={{0,8},{4,12},{8,0},{12,4},{1,9},{5,13},{9,1},{13,5},{2,10},{6,14},... | collective-permute-start | bytes 110600 | tf_op jit(solution)/shard_map/ppermute | solution.py:369
  35.1 5.9 %collective-permute-start.14 = (bf16[72,256]{1,0:T(8,128)(2,1)S(1)}, bf16[72,256]{1,0:T(8,128)(2,1)S(1)}, u32[]{:S(2)}, u32[]{:S(2)}) collective-permute-start(bf16[72,256]{1,0:T(8,128)(2,1)S(1)} %get-tuple-element.65.refs_0_), channel_id=1, source_target_pairs={{0,12},{4,8},{8,4},{12,0},{1,13},{5,9},{9,5},{13,1},{2,14},{6,10},... | collective-permute-start | bytes 110600 | tf_op jit(solution)/shard_map/ppermute | solution.py:369
  37.0 1.2 %collective-permute-start.12 = (bf16[64,256]{1,0:T(8,128)(2,1)S(1)}, bf16[64,256]{1,0:T(8,128)(2,1)S(1)}, u32[]{:S(2)}, u32[]{:S(2)}) collective-permute-start(bf16[64,256]{1,0:T(8,128)(2,1)S(1)} %get-tuple-element.62), channel_id=1, source_target_pairs={{0,1},{1,0},{4,8},{5,9},{8,4},{9,5},{12,13},{13,12},{2,3},{3,2},{6... | collective-permute-start | bytes 98312 | tf_op jit(solution)/shard_map/ppermute | solution.py:355
  41.1 2.3 %collective-permute-start.16 = (bf16[576,256]{1,0:T(8,128)(2,1)S(1)}, bf16[576,256]{1,0:T(8,128)(2,1)S(1)}, u32[]{:S(2)}, u32[]{:S(2)}) collective-permute-start(bf16[576,256]{1,0:T(8,128)(2,1)S(1)} %shard_map.76.mine_ref), channel_id=1, source_target_pairs={{0,1},{1,0},{2,3},{3,2},{4,5},{5,4},{6,7},{7,6},{8,9},{9,8},{10,11... | collective-permute-start | bytes 884744 | tf_op jit(solution)/shard_map/ppermute | solution.py:341
  41.1 4.4 %collective-permute-start.19 = (bf16[72,256]{1,0:T(8,128)(2,1)S(1)}, bf16[72,256]{1,0:T(8,128)(2,1)S(1)}, u32[]{:S(2)}, u32[]{:S(2)}) collective-permute-start(bf16[72,256]{1,0:T(8,128)(2,1)S(1)} %shard_map.75.refs_0_.mine_ref), channel_id=1, source_target_pairs={{0,2},{2,0},{1,3},{3,1},{4,6},{6,4},{5,7},{7,5},{8,10},{10,8},{9,1... | collective-permute-start | bytes 110600 | tf_op jit(solution)/shard_map/ppermute | solution.py:369
  42.3 3.4 %collective-permute-start.18 = (bf16[72,256]{1,0:T(8,128)(2,1)S(1)}, bf16[72,256]{1,0:T(8,128)(2,1)S(1)}, u32[]{:S(2)}, u32[]{:S(2)}) collective-permute-start(bf16[72,256]{1,0:T(8,128)(2,1)S(1)} %shard_map.75.refs_0_.mine_ref), channel_id=1, source_target_pairs={{0,3},{1,2},{2,1},{3,0},{4,7},{5,6},{6,5},{7,4},{8,11},{9,10},{10,... | collective-permute-start | bytes 110600 | tf_op jit(solution)/shard_map/ppermute | solution.py:375
  43.0 2.7 %collective-permute-start.17 = (bf16[72,256]{1,0:T(8,128)(2,1)S(1)}, bf16[72,256]{1,0:T(8,128)(2,1)S(1)}, u32[]{:S(2)}, u32[]{:S(2)}) collective-permute-start(bf16[72,256]{1,0:T(8,128)(2,1)S(1)} %shard_map.75.refs_0_.mine_ref), channel_id=1, source_target_pairs={{0,1},{1,0},{2,3},{3,2},{4,5},{5,4},{6,7},{7,6},{8,9},{9,8},{10,11... | collective-permute-start | bytes 110600 | tf_op jit(solution)/shard_map/ppermute | solution.py:341

commit v26 on v24

--- a/solution.py
+++ b/solution.py
@@ -466,7 +466,7 @@
         4 * count * 9 * filters * 4 * channels,
         scratch=[pltpu.VMEM((bands, 72, 4 * channels), BF16)],
     )
-    received = row_swaps(terms, bands)
+    received = row_swaps(terms, bands, by_half=True)
 
     half = 9 * filters // 2
     keep_two, send_two = whole_call(

time: 46.8 us -> 47.2 us (level)
  waiting for transfers between devices: 13.3 us -> 14.6 us
  starting transfers between devices: 22.6 us -> 21.7 us
    ppermute x11, waiting for transfers between devices: 8.85 us -> 10.1 us  [xor_swap(): return lax.ppermute(values, axis, [(n, n ^ k) for n in range(count)])]
    ppermute x11, starting transfers between devices: 16.2 us -> 15.3 us  [xor_swap(): return lax.ppermute(values, axis, [(n, n ^ k) for n in range(count)])]
  transfers between devices with their start and end apart: 20 -> 20, of which waited for: 12 -> 11; matrix products, arithmetic and copies ran while one was open for 2% -> 2% of each run, Pallas kernels for 7% -> 7%
where the time goes in v26:
time: 47.2 us; the launch traced here: 47 us
  starting transfers between devices  21.7 us (46%)
  waiting for transfers between devices  14.6 us (31%)
  Pallas kernels  7.09 us (15%)
  local copies, waits for them, and re-layouts  2.78 us (6%)
  between operations  0.8 us (2%)
    ppermute x11, starting transfers between devices, xor_swap(): return lax.ppermute(values, axis, [(n, n ^ k) for n in range(count)])  15.3 us
    ppermute x11, waiting for transfers between devices, xor_swap(): return lax.ppermute(values, axis, [(n, n ^ k) for n in range(count)])  10.1 us
    pallas_call x13, Pallas kernels, whole_call(): pl.pallas_call(body, out_shape=outs, in_specs=specs, out_specs=[pl.BlockS...  7.09 us
    ppermute x5, starting transfers between devices, even_swap(): return lax.ppermute(values, axis, [(n, n ^ 1) for n in range(count)])  3.66 us
    unnamed x6, local copies, waits for them, and re-layouts  2.75 us
    ppermute x5, waiting for transfers between devices, even_swap(): return lax.ppermute(values, axis, [(n, n ^ 1) for n in range(count)])  2.35 us
    ppermute x1, starting transfers between devices, odd_strip_swap(): return lax.ppermute(values, ('grp',) + COLS, steps)  2.01 us
    ppermute x2, waiting for transfers between devices, odd_row_swap(): return lax.ppermute(values, ('row', 'pair'), steps)  1.21 us
  transfers between devices with their start and end apart: 20, of which 11 were waited for; matrix products, arithmetic and copies ran while one was open for 2% of the time, Pallas kernels for 7%

profile of v26, /device:TPU:0, one launch (start us, length us, event | category | flops | bytes accessed | tf_op | source)
XLA Modules:
  0.0 47.0 jit_solution(13389223552359347176)
XLA Ops:
  0.7 1.0 %copy.19 = bf16[64,8,128]{2,0,1:T(8,128)(2,1)S(1)} copy(bf16[64,8,128]{2,1,0:T(8,128)(2,1)} %param.4) | data formatting | bytes 262144 | tf_op args[0]
  1.7 3.1 %collective-permute-start.1 = (bf16[64,128]{1,0:T(8,128)(2,1)S(1)}, bf16[64,128]{1,0:T(8,128)(2,1)S(1)}, u32[]{:S(2)}, u32[]{:S(2)}) collective-permute-start(bf16[64,128]{1,0:T(8,128)(2,1)S(1)} %get-tuple-element.71), channel_id=1, source_target_pairs={{0,4},{4,0},{8,12},{12,8},{1,5},{5,1},{9,13},{13,9},{2,6},{6,2},{1... | collective-permute-start | bytes 49160 | tf_op jit(solution)/shard_map/ppermute | solution.py:343
  4.7 0.8 %copy.20 = bf16[128,32,8]{0,1,2:T(8,128)(2,1)S(1)} copy(bf16[128,32,8]{0,2,1:T(8,128)(2,1)} %param.7) | data formatting | bytes 131072 | tf_op args[3]
  6.6 2.0 %collective-permute-start.2 = (bf16[144,128]{1,0:T(8,128)(2,1)S(1)}, bf16[144,128]{1,0:T(8,128)(2,1)S(1)}, u32[]{:S(2)}, u32[]{:S(2)}) collective-permute-start(bf16[144,128]{1,0:T(8,128)(2,1)S(1)} %get-tuple-element.39), channel_id=1, source_target_pairs={{0,16},{1,2},{2,1},{3,19},{16,0},{17,18},{18,17},{19,3},{4,20},{5,... | collective-permute-start | bytes 110600 | tf_op jit(solution)/shard_map/ppermute | solution.py:367
  8.7 0.9 %copy-done.1 = bf16[64,3,3,64]{3,0,2,1:T(8,128)(2,1)S(1)} copy-done((bf16[64,3,3,64]{3,0,2,1:T(8,128)(2,1)S(1)}, bf16[64,3,3,64]{3,0,2,1:T(8,128)(2,1)}, u32[]{:S(2)}) %copy-start.1) | copy-done | bytes 73752
  10.6 0.9 %shard_map.70 = (bf16[2,40,256]{2,1,0:T(8,128)(2,1)S(1)}, bf16[8,64,256]{2,1,0:T(8,128)(2,1)S(1)}, bf16[10,64,256]{2,1,0:T(8,128)(2,1)S(1)}) custom-call(bf16[8,64,128]{2,1,0:T(8,128)(2,1)S(1)} %bitcast.34, bf16[64,128]{1,0:T(8,128)(2,1)S(1)} %get-tuple-element.41.above_ref, bf16[64,128]{1,0:T(8,128)(2,1)S(1)} %get-tuple-element.42.below_ref, ...), custom_call_target="tpu_custom_call" | custom-call | flops 150994944 | bytes 1122304 | tf_op jit(solution)/shard_map/pallas_call | solution.py:30
  11.4 4.1 %collective-permute-start.6 = (bf16[2,40,256]{2,1,0:T(8,128)(2,1)S(1)}, bf16[2,40,256]{2,1,0:T(8,128)(2,1)S(1)}, u32[]{:S(2)}, u32[]{:S(2)}) collective-permute-start(bf16[2,40,256]{2,1,0:T(8,128)(2,1)S(1)} %get-tuple-element.46.refs_0_), channel_id=1, source_target_pairs={{0,12},{4,8},{8,4},{12,0},{1,13},{5,9},{9,5},{13,1},{2,14},{6,10},... | collective-permute-start | bytes 122888 | tf_op jit(solution)/shard_map/ppermute | solution.py:371
  17.5 3.0 %collective-permute-done.5.refs_2_ = bf16[2,40,256]{2,1,0:T(8,128)(2,1)S(1)} collective-permute-done((bf16[2,40,256]{2,1,0:T(8,128)(2,1)S(1)}, bf16[2,40,256]{2,1,0:T(8,128)(2,1)S(1)}, u32[]{:S(2)}, u32[]{:S(2)}) %collective-permute-start.5) | collective-permute-done | bytes 40992 | tf_op jit(solution)/shard_map/ppermute | solution.py:371
  20.6 1.0 %shard_map.71 = (bf16[72,256]{1,0:T(8,128)(2,1)S(1)}, bf16[72,256]{1,0:T(8,128)(2,1)S(1)}, bf16[72,256]{1,0:T(8,128)(2,1)S(1)}, bf16[72,256]{1,0:T(8,128)(2,1)S(...) custom-call(bf16[8,48,128]{2,1,0:T(8,128)(2,1)S(1)} %fusion.6.og_ref, ...), custom_call_target="tpu_custom_call" | custom-call | flops 452984832 | bytes 1368064 | tf_op jit(solution)/shard_map/pallas_call | solution.py:30
  21.7 1.9 %collective-permute-start.7 = (bf16[72,256]{1,0:T(8,128)(2,1)S(1)}, bf16[72,256]{1,0:T(8,128)(2,1)S(1)}, u32[]{:S(2)}, u32[]{:S(2)}) collective-permute-start(bf16[72,256]{1,0:T(8,128)(2,1)S(1)} %get-tuple-element.48), channel_id=1, source_target_pairs={{0,8},{4,12},{8,0},{12,4},{1,9},{5,13},{9,1},{13,5},{2,10},{6,14},... | collective-permute-start | bytes 110600 | tf_op jit(solution)/shard_map/ppermute | solution.py:371
  23.6 1.5 %collective-permute-start.8 = (bf16[72,256]{1,0:T(8,128)(2,1)S(1)}, bf16[72,256]{1,0:T(8,128)(2,1)S(1)}, u32[]{:S(2)}, u32[]{:S(2)}) collective-permute-start(bf16[72,256]{1,0:T(8,128)(2,1)S(1)} %get-tuple-element.49), channel_id=1, source_target_pairs={{0,12},{4,8},{8,4},{12,0},{1,13},{5,9},{9,5},{13,1},{2,14},{6,10},... | collective-permute-start | bytes 110600 | tf_op jit(solution)/shard_map/ppermute | solution.py:371
  25.8 0.8 %collective-permute-done.7.refs_1_ = bf16[72,256]{1,0:T(8,128)(2,1)S(1)} collective-permute-done((bf16[72,256]{1,0:T(8,128)(2,1)S(1)}, bf16[72,256]{1,0:T(8,128)(2,1)S(1)}, u32[]{:S(2)}, u32[]{:S(2)}) %collective-permute-start.7) | collective-permute-done | bytes 36896 | tf_op jit(solution)/shard_map/ppermute | solution.py:371
  26.6 2.8 %collective-permute-done.8.refs_2_ = bf16[72,256]{1,0:T(8,128)(2,1)S(1)} collective-permute-done((bf16[72,256]{1,0:T(8,128)(2,1)S(1)}, bf16[72,256]{1,0:T(8,128)(2,1)S(1)}, u32[]{:S(2)}, u32[]{:S(2)}) %collective-permute-start.8) | collective-permute-done | bytes 36896 | tf_op jit(solution)/shard_map/ppermute | solution.py:371
  29.4 0.9 %shard_map.73 = (bf16[8,64,256]{2,1,0:T(8,128)(2,1)S(1)}, bf16[64,256]{1,0:T(8,128)(2,1)S(1)}, bf16[64,256]{1,0:T(8,128)(2,1)S(1)}, bf16[648,256]{1,0:T(8,128)(2,1)S(1)}, bf16[648,256]{1,0:T(8,128)(2,1)S(1)}) custom-call(bf16[72,256]{1,0:T(8,128)(2,1)S(1)} %get-tuple-element.47.refs_0_, bf16[72,256]{1,0:T(8,128)(2,1)S(1)} %collective-permute-done.7.refs_1_, ...), custom_call_target="tpu_custom_call" | custom-call | flops 150994944 | bytes 2498560 | tf_op jit(solution)/shard_map/pallas_call | solution.py:30
  30.3 1.6 %collective-permute-done.10.b_ref = bf16[648,256]{1,0:T(8,128)(2,1)S(1)} collective-permute-done((bf16[648,256]{1,0:T(8,128)(2,1)S(1)}, bf16[648,256]{1,0:T(8,128)(2,1)S(1)}, u32[]{:S(2)}, u32[]{:S(2)}) %collective-permute-start.10) | collective-permute-done | bytes 331808 | tf_op jit(solution)/shard_map/ppermute | solution.py:343
  32.0 1.0 %collective-permute-start.18 = (bf16[576,256]{1,0:T(8,128)(2,1)S(1)}, bf16[576,256]{1,0:T(8,128)(2,1)S(1)}, u32[]{:S(2)}, u32[]{:S(2)}) collective-permute-start(bf16[576,256]{1,0:T(8,128)(2,1)S(1)} %get-tuple-element.67.a_ref), channel_id=1, source_target_pairs={{0,2},{2,0},{1,3},{3,1},{4,6},{6,4},{5,7},{7,5},{8,10},{10,8},{9,1... | collective-permute-start | bytes 884744 | tf_op jit(solution)/shard_map/ppermute | solution.py:371
  33.0 2.5 %collective-permute-start.14 = (bf16[72,256]{1,0:T(8,128)(2,1)S(1)}, bf16[72,256]{1,0:T(8,128)(2,1)S(1)}, u32[]{:S(2)}, u32[]{:S(2)}) collective-permute-start(bf16[72,256]{1,0:T(8,128)(2,1)S(1)} %get-tuple-element.66.refs_0_), channel_id=1, source_target_pairs={{0,8},{4,12},{8,0},{12,4},{1,9},{5,13},{9,1},{13,5},{2,10},{6,14},... | collective-permute-start | bytes 110600 | tf_op jit(solution)/shard_map/ppermute | solution.py:371
  35.6 1.9 %collective-permute-start.13 = (bf16[72,256]{1,0:T(8,128)(2,1)S(1)}, bf16[72,256]{1,0:T(8,128)(2,1)S(1)}, u32[]{:S(2)}, u32[]{:S(2)}) collective-permute-start(bf16[72,256]{1,0:T(8,128)(2,1)S(1)} %get-tuple-element.66.refs_0_), channel_id=1, source_target_pairs={{0,12},{4,8},{8,4},{12,0},{1,13},{5,9},{9,5},{13,1},{2,14},{6,10},... | collective-permute-start | bytes 110600 | tf_op jit(solution)/shard_map/ppermute | solution.py:371
  37.4 1.2 %collective-permute-done.12.b_ref.refs_4_ = bf16[64,256]{1,0:T(8,128)(2,1)S(1)} collective-permute-done((bf16[64,256]{1,0:T(8,128)(2,1)S(1)}, bf16[64,256]{1,0:T(8,128)(2,1)S(1)}, u32[]{:S(2)}, u32[]{:S(2)}) %collective-permute-start.12) | collective-permute-done | bytes 32800 | tf_op jit(solution)/shard_map/ppermute | solution.py:357
  38.7 2.6 %collective-permute-done.13.refs_2_ = bf16[72,256]{1,0:T(8,128)(2,1)S(1)} collective-permute-done((bf16[72,256]{1,0:T(8,128)(2,1)S(1)}, bf16[72,256]{1,0:T(8,128)(2,1)S(1)}, u32[]{:S(2)}, u32[]{:S(2)}) %collective-permute-start.13) | collective-permute-done | bytes 36896 | tf_op jit(solution)/shard_map/ppermute | solution.py:371
  41.5 1.2 %collective-permute-start.17 = (bf16[72,256]{1,0:T(8,128)(2,1)S(1)}, bf16[72,256]{1,0:T(8,128)(2,1)S(1)}, u32[]{:S(2)}, u32[]{:S(2)}) collective-permute-start(bf16[72,256]{1,0:T(8,128)(2,1)S(1)} %shard_map.76.refs_0_.mine_ref), channel_id=1, source_target_pairs={{0,2},{2,0},{1,3},{3,1},{4,6},{6,4},{5,7},{7,5},{8,10},{10,8},{9,1... | collective-permute-start | bytes 110600 | tf_op jit(solution)/shard_map/ppermute | solution.py:371
  43.7 1.2 %shard_map.75 = (bf16[64,8,128]{2,1,0:T(8,128)(2,1)}, f32[8,128]{1,0:T(8,128)S(1)}) custom-call(bf16[8,64,256]{2,1,0:T(8,128)(2,1)S(1)} %get-tuple-element.58.g_ref, bf16[136,256]{1,0:T(8,128)(2,1)S(1)} %collective-permute-done.11.a_ref.refs_1_, bf16[64,256]{1,0:T(8,128)(2,1)S(1)} %collective-permute-done.12.b_ref.refs_4_, ...), custom_call_target="tpu_custom_call" | custom-call | flops 150994944 | bytes 573440 | tf_op jit(solution)/shard_map/pallas_call | solution.py:30
  44.9 1.1 %shard_map.78 = (f32[1152,256]{1,0:T(8,128)}, f32[8,128]{1,0:T(8,128)S(1)}) custom-call(bf16[576,256]{1,0:T(8,128)(2,1)S(1)} %shard_map.77.mine_ref, bf16[576,256]{1,0:T(8,128)(2,1)S(1)} %collective-permute-done.19.other_ref), custom_call_target="tpu_custom_call" | custom-call | flops 100000000 | bytes 1773568 | tf_op jit(solution)/shard_map/pallas_call | solution.py:30
  46.1 0.9 %shard_map.79 = f32[3,192,64]{2,1,0:T(8,128)} custom-call(bf16[72,256]{1,0:T(8,128)(2,1)S(1)} %shard_map.76.refs_0_.mine_ref, bf16[72,256]{1,0:T(8,128)(2,1)S(1)} %collective-permute-done.15.beside_ref, bf16[72,256]{1,0:T(8,128)(2,1)S(1)} %collective-permute-done.16.corner_ref, bf16[72,256]{1,0:T(8,128)(2,1)S(1)} %collective-permute-done.17.across_ref, ...), custom_call_target="tpu_custom_call" | custom-call | flops 1 | bytes 303104 | tf_op jit(solution)/shard_map/pallas_call | solution.py:30
  (42 shorter events, 6.4 us)
Async XLA Ops:
  0.6 20.0 %copy-start = (bf16[128,3,3,256]{3,0,2,1:T(8,128)(2,1)S(1)}, bf16[128,3,3,256]{3,0,2,1:T(8,128)(2,1)}, u32[]{:S(2)}) copy-start(bf16[128,3,3,256]{3,0,2,1:T(8,128)(2,1)} %param.6) | copy-start | bytes 1769476
  1.7 4.8 %collective-permute-start.1 = (bf16[64,128]{1,0:T(8,128)(2,1)S(1)}, bf16[64,128]{1,0:T(8,128)(2,1)S(1)}, u32[]{:S(2)}, u32[]{:S(2)}) collective-permute-start(bf16[64,128]{1,0:T(8,128)(2,1)S(1)} %get-tuple-element.71), channel_id=1, source_target_pairs={{0,4},{4,0},{8,12},{12,8},{1,5},{5,1},{9,13},{13,9},{2,6},{6,2},{1... | collective-permute-start | bytes 49160 | tf_op jit(solution)/shard_map/ppermute | solution.py:343
  4.7 1.7 %collective-permute-start = (bf16[64,128]{1,0:T(8,128)(2,1)S(1)}, bf16[64,128]{1,0:T(8,128)(2,1)S(1)}, u32[]{:S(2)}, u32[]{:S(2)}) collective-permute-start(bf16[64,128]{1,0:T(8,128)(2,1)S(1)} %get-tuple-element.72), channel_id=1, source_target_pairs={{0,1},{1,0},{4,8},{5,9},{8,4},{9,5},{12,13},{13,12},{2,3},{3,2},{6... | collective-permute-start | bytes 49160 | tf_op jit(solution)/shard_map/ppermute | solution.py:357
  6.6 4.0 %collective-permute-start.2 = (bf16[144,128]{1,0:T(8,128)(2,1)S(1)}, bf16[144,128]{1,0:T(8,128)(2,1)S(1)}, u32[]{:S(2)}, u32[]{:S(2)}) collective-permute-start(bf16[144,128]{1,0:T(8,128)(2,1)S(1)} %get-tuple-element.39), channel_id=1, source_target_pairs={{0,16},{1,2},{2,1},{3,19},{16,0},{17,18},{18,17},{19,3},{4,20},{5,... | collective-permute-start | bytes 110600 | tf_op jit(solution)/shard_map/ppermute | solution.py:367
  8.6 2.0 %collective-permute-start.3 = (bf16[144,128]{1,0:T(8,128)(2,1)S(1)}, bf16[144,128]{1,0:T(8,128)(2,1)S(1)}, u32[]{:S(2)}, u32[]{:S(2)}) collective-permute-start(bf16[144,128]{1,0:T(8,128)(2,1)S(1)} %get-tuple-element.40), channel_id=1, source_target_pairs={{0,1},{1,0},{2,3},{3,2},{4,5},{5,4},{6,7},{7,6},{8,9},{9,8},{10,11... | collective-permute-start | bytes 110600 | tf_op jit(solution)/shard_map/ppermute | solution.py:343
  8.7 0.9 %copy-start.1 = (bf16[64,3,3,64]{3,0,2,1:T(8,128)(2,1)S(1)}, bf16[64,3,3,64]{3,0,2,1:T(8,128)(2,1)}, u32[]{:S(2)}) copy-start(bf16[64,3,3,64]{3,0,2,1:T(8,128)(2,1)} %param.5) | copy-start | bytes 221188
  11.4 6.1 %collective-permute-start.6 = (bf16[2,40,256]{2,1,0:T(8,128)(2,1)S(1)}, bf16[2,40,256]{2,1,0:T(8,128)(2,1)S(1)}, u32[]{:S(2)}, u32[]{:S(2)}) collective-permute-start(bf16[2,40,256]{2,1,0:T(8,128)(2,1)S(1)} %get-tuple-element.46.refs_0_), channel_id=1, source_target_pairs={{0,12},{4,8},{8,4},{12,0},{1,13},{5,9},{9,5},{13,1},{2,14},{6,10},... | collective-permute-start | bytes 122888 | tf_op jit(solution)/shard_map/ppermute | solution.py:371
  15.6 5.0 %collective-permute-start.5 = (bf16[2,40,256]{2,1,0:T(8,128)(2,1)S(1)}, bf16[2,40,256]{2,1,0:T(8,128)(2,1)S(1)}, u32[]{:S(2)}, u32[]{:S(2)}) collective-permute-start(bf16[2,40,256]{2,1,0:T(8,128)(2,1)S(1)} %get-tuple-element.46.refs_0_), channel_id=1, source_target_pairs={{0,8},{4,12},{8,0},{12,4},{1,9},{5,13},{9,1},{13,5},{2,10},{6,14},... | collective-permute-start | bytes 122888 | tf_op jit(solution)/shard_map/ppermute | solution.py:371
  16.2 4.4 %collective-permute-start.4 = (bf16[2,40,256]{2,1,0:T(8,128)(2,1)S(1)}, bf16[2,40,256]{2,1,0:T(8,128)(2,1)S(1)}, u32[]{:S(2)}, u32[]{:S(2)}) collective-permute-start(bf16[2,40,256]{2,1,0:T(8,128)(2,1)S(1)} %get-tuple-element.46.refs_0_), channel_id=1, source_target_pairs={{0,4},{4,0},{8,12},{12,8},{1,5},{5,1},{9,13},{13,9},{2,6},{6,2},{1... | collective-permute-start | bytes 122888 | tf_op jit(solution)/shard_map/ppermute | solution.py:371
  21.7 4.9 %collective-permute-start.7 = (bf16[72,256]{1,0:T(8,128)(2,1)S(1)}, bf16[72,256]{1,0:T(8,128)(2,1)S(1)}, u32[]{:S(2)}, u32[]{:S(2)}) collective-permute-start(bf16[72,256]{1,0:T(8,128)(2,1)S(1)} %get-tuple-element.48), channel_id=1, source_target_pairs={{0,8},{4,12},{8,0},{12,4},{1,9},{5,13},{9,1},{13,5},{2,10},{6,14},... | collective-permute-start | bytes 110600 | tf_op jit(solution)/shard_map/ppermute | solution.py:371
  23.6 5.8 %collective-permute-start.8 = (bf16[72,256]{1,0:T(8,128)(2,1)S(1)}, bf16[72,256]{1,0:T(8,128)(2,1)S(1)}, u32[]{:S(2)}, u32[]{:S(2)}) collective-permute-start(bf16[72,256]{1,0:T(8,128)(2,1)S(1)} %get-tuple-element.49), channel_id=1, source_target_pairs={{0,12},{4,8},{8,4},{12,0},{1,13},{5,9},{9,5},{13,1},{2,14},{6,10},... | collective-permute-start | bytes 110600 | tf_op jit(solution)/shard_map/ppermute | solution.py:371
  25.0 4.4 %collective-permute-start.9 = (bf16[72,256]{1,0:T(8,128)(2,1)S(1)}, bf16[72,256]{1,0:T(8,128)(2,1)S(1)}, u32[]{:S(2)}, u32[]{:S(2)}) collective-permute-start(bf16[72,256]{1,0:T(8,128)(2,1)S(1)} %get-tuple-element.50), channel_id=1, source_target_pairs={{0,4},{4,0},{8,12},{12,8},{1,5},{5,1},{9,13},{13,9},{2,6},{6,2},{1... | collective-permute-start | bytes 110600 | tf_op jit(solution)/shard_map/ppermute | solution.py:371
  30.3 1.7 %collective-permute-start.10 = (bf16[648,256]{1,0:T(8,128)(2,1)S(1)}, bf16[648,256]{1,0:T(8,128)(2,1)S(1)}, u32[]{:S(2)}, u32[]{:S(2)}) collective-permute-start(bf16[648,256]{1,0:T(8,128)(2,1)S(1)} %get-tuple-element.60), channel_id=1, source_target_pairs={{0,1},{1,0},{2,3},{3,2},{4,5},{5,4},{6,7},{7,6},{8,9},{9,8},{10,11... | collective-permute-start | bytes 995336 | tf_op jit(solution)/shard_map/ppermute | solution.py:343
  32.0 9.3 %collective-permute-start.18 = (bf16[576,256]{1,0:T(8,128)(2,1)S(1)}, bf16[576,256]{1,0:T(8,128)(2,1)S(1)}, u32[]{:S(2)}, u32[]{:S(2)}) collective-permute-start(bf16[576,256]{1,0:T(8,128)(2,1)S(1)} %get-tuple-element.67.a_ref), channel_id=1, source_target_pairs={{0,2},{2,0},{1,3},{3,1},{4,6},{6,4},{5,7},{7,5},{8,10},{10,8},{9,1... | collective-permute-start | bytes 884744 | tf_op jit(solution)/shard_map/ppermute | solution.py:371
  33.0 8.3 %collective-permute-start.11 = (bf16[136,256]{1,0:T(8,128)(2,1)S(1)}, bf16[136,256]{1,0:T(8,128)(2,1)S(1)}, u32[]{:S(2)}, u32[]{:S(2)}) collective-permute-start(bf16[136,256]{1,0:T(8,128)(2,1)S(1)} %get-tuple-element.62), channel_id=1, source_target_pairs={{0,4},{4,0},{8,12},{12,8},{1,5},{5,1},{9,13},{13,9},{2,6},{6,2},{1... | collective-permute-start | bytes 208904 | tf_op jit(solution)/shard_map/ppermute | solution.py:371
  33.0 5.6 %collective-permute-start.14 = (bf16[72,256]{1,0:T(8,128)(2,1)S(1)}, bf16[72,256]{1,0:T(8,128)(2,1)S(1)}, u32[]{:S(2)}, u32[]{:S(2)}) collective-permute-start(bf16[72,256]{1,0:T(8,128)(2,1)S(1)} %get-tuple-element.66.refs_0_), channel_id=1, source_target_pairs={{0,8},{4,12},{8,0},{12,4},{1,9},{5,13},{9,1},{13,5},{2,10},{6,14},... | collective-permute-start | bytes 110600 | tf_op jit(solution)/shard_map/ppermute | solution.py:371
  35.6 5.8 %collective-permute-start.13 = (bf16[72,256]{1,0:T(8,128)(2,1)S(1)}, bf16[72,256]{1,0:T(8,128)(2,1)S(1)}, u32[]{:S(2)}, u32[]{:S(2)}) collective-permute-start(bf16[72,256]{1,0:T(8,128)(2,1)S(1)} %get-tuple-element.66.refs_0_), channel_id=1, source_target_pairs={{0,12},{4,8},{8,4},{12,0},{1,13},{5,9},{9,5},{13,1},{2,14},{6,10},... | collective-permute-start | bytes 110600 | tf_op jit(solution)/shard_map/ppermute | solution.py:371
  37.4 1.2 %collective-permute-start.12 = (bf16[64,256]{1,0:T(8,128)(2,1)S(1)}, bf16[64,256]{1,0:T(8,128)(2,1)S(1)}, u32[]{:S(2)}, u32[]{:S(2)}) collective-permute-start(bf16[64,256]{1,0:T(8,128)(2,1)S(1)} %get-tuple-element.63), channel_id=1, source_target_pairs={{0,1},{1,0},{4,8},{5,9},{8,4},{9,5},{12,13},{13,12},{2,3},{3,2},{6... | collective-permute-start | bytes 98312 | tf_op jit(solution)/shard_map/ppermute | solution.py:357
  41.4 3.5 %collective-permute-start.19 = (bf16[576,256]{1,0:T(8,128)(2,1)S(1)}, bf16[576,256]{1,0:T(8,128)(2,1)S(1)}, u32[]{:S(2)}, u32[]{:S(2)}) collective-permute-start(bf16[576,256]{1,0:T(8,128)(2,1)S(1)} %shard_map.77.mine_ref), channel_id=1, source_target_pairs={{0,1},{1,0},{2,3},{3,2},{4,5},{5,4},{6,7},{7,6},{8,9},{9,8},{10,11... | collective-permute-start | bytes 884744 | tf_op jit(solution)/shard_map/ppermute | solution.py:343
  41.5 4.5 %collective-permute-start.17 = (bf16[72,256]{1,0:T(8,128)(2,1)S(1)}, bf16[72,256]{1,0:T(8,128)(2,1)S(1)}, u32[]{:S(2)}, u32[]{:S(2)}) collective-permute-start(bf16[72,256]{1,0:T(8,128)(2,1)S(1)} %shard_map.76.refs_0_.mine_ref), channel_id=1, source_target_pairs={{0,2},{2,0},{1,3},{3,1},{4,6},{6,4},{5,7},{7,5},{8,10},{10,8},{9,1... | collective-permute-start | bytes 110600 | tf_op jit(solution)/shard_map/ppermute | solution.py:371
  42.7 3.4 %collective-permute-start.16 = (bf16[72,256]{1,0:T(8,128)(2,1)S(1)}, bf16[72,256]{1,0:T(8,128)(2,1)S(1)}, u32[]{:S(2)}, u32[]{:S(2)}) collective-permute-start(bf16[72,256]{1,0:T(8,128)(2,1)S(1)} %shard_map.76.refs_0_.mine_ref), channel_id=1, source_target_pairs={{0,3},{1,2},{2,1},{3,0},{4,7},{5,6},{6,5},{7,4},{8,11},{9,10},{10,... | collective-permute-start | bytes 110600 | tf_op jit(solution)/shard_map/ppermute | solution.py:377
  43.4 2.7 %collective-permute-start.15 = (bf16[72,256]{1,0:T(8,128)(2,1)S(1)}, bf16[72,256]{1,0:T(8,128)(2,1)S(1)}, u32[]{:S(2)}, u32[]{:S(2)}) collective-permute-start(bf16[72,256]{1,0:T(8,128)(2,1)S(1)} %shard_map.76.refs_0_.mine_ref), channel_id=1, source_target_pairs={{0,1},{1,0},{2,3},{3,2},{4,5},{5,4},{6,7},{7,6},{8,9},{9,8},{10,11... | collective-permute-start | bytes 110600 | tf_op jit(solution)/shard_map/ppermute | solution.py:343

commit v27 on v24

--- a/solution.py
+++ b/solution.py
@@ -257,7 +257,7 @@
 def sum_rows(*refs):
     *refs, _, out_ref = refs
     rows = out_ref.shape[0]
-    terms = dict(zip(row_order(len(refs), near_first=True, by_half=True), (ref[-rows:].astype(F32) for ref in refs)))
+    terms = dict(zip(row_order(len(refs), near_first=True, by_half=False), (ref[-rows:].astype(F32) for ref in refs)))
     terms = [terms[k] for k in range(len(refs))]
     while len(terms) > 1:
         terms = [a + b for a, b in zip(terms[::2], terms[1::2])]
@@ -493,8 +493,8 @@
     )
     columns = lax.axis_size("col")
     two, two_more = sum_but_last(two, "col", columns)
-    ones = row_swaps([one, joined] + [one] * (bands - 2), bands, near_first=True, by_half=True)
-    near = ones[row_order(bands, near_first=True, by_half=True).index(1)]
+    ones = row_swaps([one, joined] + [one] * (bands - 2), bands, near_first=True, by_half=False)
+    near = ones[row_order(bands, near_first=True, by_half=False).index(1)]
     up_b = odd_row_swap(up_b)
     (one,) = whole_call(sum_rows, [shaped(one.shape)], ones + [up_b], 0, after=1)
     input_grad, done = whole_call(

time: 46.8 us -> 46.9 us (level)
  waiting for transfers between devices: 13.3 us -> 14.3 us
  starting transfers between devices: 22.6 us -> 21.7 us
    ppermute x11, waiting for transfers between devices: 8.85 us -> 9.84 us  [xor_swap(): return lax.ppermute(values, axis, [(n, n ^ k) for n in range(count)])]
    ppermute x11, starting transfers between devices: 16.2 us -> 15.3 us  [xor_swap(): return lax.ppermute(values, axis, [(n, n ^ k) for n in range(count)])]
where the time goes in v27:
time: 46.9 us; the launch traced here: 46.7 us
  starting transfers between devices  21.7 us (46%)
  waiting for transfers between devices  14.3 us (30%)
  Pallas kernels  7.08 us (15%)
  local copies, waits for them, and re-layouts  2.78 us (6%)
  between operations  0.8 us (2%)
    ppermute x11, starting transfers between devices, xor_swap(): return lax.ppermute(values, axis, [(n, n ^ k) for n in range(count)])  15.3 us
    ppermute x11, waiting for transfers between devices, xor_swap(): return lax.ppermute(values, axis, [(n, n ^ k) for n in range(count)])  9.84 us
    pallas_call x13, Pallas kernels, whole_call(): pl.pallas_call(body, out_shape=outs, in_specs=specs, out_specs=[pl.BlockS...  7.08 us
    ppermute x5, starting transfers between devices, even_swap(): return lax.ppermute(values, axis, [(n, n ^ 1) for n in range(count)])  3.66 us
    unnamed x6, local copies, waits for them, and re-layouts  2.75 us
    ppermute x5, waiting for transfers between devices, even_swap(): return lax.ppermute(values, axis, [(n, n ^ 1) for n in range(count)])  2.35 us
    ppermute x1, starting transfers between devices, odd_strip_swap(): return lax.ppermute(values, ('grp',) + COLS, steps)  2.01 us
    ppermute x2, waiting for transfers between devices, odd_row_swap(): return lax.ppermute(values, ('row', 'pair'), steps)  1.21 us
  transfers between devices with their start and end apart: 20, of which 12 were waited for; matrix products, arithmetic and copies ran while one was open for 2% of the time, Pallas kernels for 7%

profile of v27, /device:TPU:0, one launch (start us, length us, event | category | flops | bytes accessed | tf_op | source)
XLA Modules:
  0.0 46.7 jit_solution(12878643810264306819)
XLA Ops:
  0.7 1.0 %copy.19 = bf16[64,8,128]{2,0,1:T(8,128)(2,1)S(1)} copy(bf16[64,8,128]{2,1,0:T(8,128)(2,1)} %param.4) | data formatting | bytes 262144 | tf_op args[0]
  1.7 3.1 %collective-permute-start.1 = (bf16[64,128]{1,0:T(8,128)(2,1)S(1)}, bf16[64,128]{1,0:T(8,128)(2,1)S(1)}, u32[]{:S(2)}, u32[]{:S(2)}) collective-permute-start(bf16[64,128]{1,0:T(8,128)(2,1)S(1)} %get-tuple-element.71), channel_id=1, source_target_pairs={{0,4},{4,0},{8,12},{12,8},{1,5},{5,1},{9,13},{13,9},{2,6},{6,2},{1... | collective-permute-start | bytes 49160 | tf_op jit(solution)/shard_map/ppermute | solution.py:343
  6.6 2.0 %collective-permute-start.2 = (bf16[144,128]{1,0:T(8,128)(2,1)S(1)}, bf16[144,128]{1,0:T(8,128)(2,1)S(1)}, u32[]{:S(2)}, u32[]{:S(2)}) collective-permute-start(bf16[144,128]{1,0:T(8,128)(2,1)S(1)} %get-tuple-element.39), channel_id=1, source_target_pairs={{0,16},{1,2},{2,1},{3,19},{16,0},{17,18},{18,17},{19,3},{4,20},{5,... | collective-permute-start | bytes 110600 | tf_op jit(solution)/shard_map/ppermute | solution.py:367
  8.7 0.9 %copy-done.1 = bf16[64,3,3,64]{3,0,2,1:T(8,128)(2,1)S(1)} copy-done((bf16[64,3,3,64]{3,0,2,1:T(8,128)(2,1)S(1)}, bf16[64,3,3,64]{3,0,2,1:T(8,128)(2,1)}, u32[]{:S(2)}) %copy-start.1) | copy-done | bytes 73752
  10.6 0.9 %shard_map.70 = (bf16[2,40,256]{2,1,0:T(8,128)(2,1)S(1)}, bf16[8,64,256]{2,1,0:T(8,128)(2,1)S(1)}, bf16[10,64,256]{2,1,0:T(8,128)(2,1)S(1)}) custom-call(bf16[8,64,128]{2,1,0:T(8,128)(2,1)S(1)} %bitcast.34, bf16[64,128]{1,0:T(8,128)(2,1)S(1)} %get-tuple-element.41.above_ref, bf16[64,128]{1,0:T(8,128)(2,1)S(1)} %get-tuple-element.42.below_ref, ...), custom_call_target="tpu_custom_call" | custom-call | flops 150994944 | bytes 1122304 | tf_op jit(solution)/shard_map/pallas_call | solution.py:30
  11.4 4.1 %collective-permute-start.6 = (bf16[2,40,256]{2,1,0:T(8,128)(2,1)S(1)}, bf16[2,40,256]{2,1,0:T(8,128)(2,1)S(1)}, u32[]{:S(2)}, u32[]{:S(2)}) collective-permute-start(bf16[2,40,256]{2,1,0:T(8,128)(2,1)S(1)} %get-tuple-element.46.refs_0_), channel_id=1, source_target_pairs={{0,12},{4,8},{8,4},{12,0},{1,13},{5,9},{9,5},{13,1},{2,14},{6,10},... | collective-permute-start | bytes 122888 | tf_op jit(solution)/shard_map/ppermute | solution.py:371
  17.5 3.0 %collective-permute-done.5.refs_2_ = bf16[2,40,256]{2,1,0:T(8,128)(2,1)S(1)} collective-permute-done((bf16[2,40,256]{2,1,0:T(8,128)(2,1)S(1)}, bf16[2,40,256]{2,1,0:T(8,128)(2,1)S(1)}, u32[]{:S(2)}, u32[]{:S(2)}) %collective-permute-start.5) | collective-permute-done | bytes 40992 | tf_op jit(solution)/shard_map/ppermute | solution.py:371
  20.6 1.0 %shard_map.71 = (bf16[72,256]{1,0:T(8,128)(2,1)S(1)}, bf16[72,256]{1,0:T(8,128)(2,1)S(1)}, bf16[72,256]{1,0:T(8,128)(2,1)S(1)}, bf16[72,256]{1,0:T(8,128)(2,1)S(...) custom-call(bf16[8,48,128]{2,1,0:T(8,128)(2,1)S(1)} %fusion.6.og_ref, ...), custom_call_target="tpu_custom_call" | custom-call | flops 452984832 | bytes 1368064 | tf_op jit(solution)/shard_map/pallas_call | solution.py:30
  21.7 2.5 %collective-permute-start.7 = (bf16[72,256]{1,0:T(8,128)(2,1)S(1)}, bf16[72,256]{1,0:T(8,128)(2,1)S(1)}, u32[]{:S(2)}, u32[]{:S(2)}) collective-permute-start(bf16[72,256]{1,0:T(8,128)(2,1)S(1)} %get-tuple-element.48), channel_id=1, source_target_pairs={{0,12},{4,8},{8,4},{12,0},{1,13},{5,9},{9,5},{13,1},{2,14},{6,10},... | collective-permute-start | bytes 110600 | tf_op jit(solution)/shard_map/ppermute | solution.py:371
  24.1 2.0 %collective-permute-start.9 = (bf16[72,256]{1,0:T(8,128)(2,1)S(1)}, bf16[72,256]{1,0:T(8,128)(2,1)S(1)}, u32[]{:S(2)}, u32[]{:S(2)}) collective-permute-start(bf16[72,256]{1,0:T(8,128)(2,1)S(1)} %get-tuple-element.50), channel_id=1, source_target_pairs={{0,4},{4,0},{8,12},{12,8},{1,5},{5,1},{9,13},{13,9},{2,6},{6,2},{1... | collective-permute-start | bytes 110600 | tf_op jit(solution)/shard_map/ppermute | solution.py:371
  26.7 1.0 %collective-permute-done.7.refs_1_ = bf16[72,256]{1,0:T(8,128)(2,1)S(1)} collective-permute-done((bf16[72,256]{1,0:T(8,128)(2,1)S(1)}, bf16[72,256]{1,0:T(8,128)(2,1)S(1)}, u32[]{:S(2)}, u32[]{:S(2)}) %collective-permute-start.7) | collective-permute-done | bytes 36896 | tf_op jit(solution)/shard_map/ppermute | solution.py:371
  27.7 1.2 %collective-permute-done.8.refs_2_ = bf16[72,256]{1,0:T(8,128)(2,1)S(1)} collective-permute-done((bf16[72,256]{1,0:T(8,128)(2,1)S(1)}, bf16[72,256]{1,0:T(8,128)(2,1)S(1)}, u32[]{:S(2)}, u32[]{:S(2)}) %collective-permute-start.8) | collective-permute-done | bytes 36896 | tf_op jit(solution)/shard_map/ppermute | solution.py:371
  29.0 0.9 %shard_map.73 = (bf16[8,64,256]{2,1,0:T(8,128)(2,1)S(1)}, bf16[64,256]{1,0:T(8,128)(2,1)S(1)}, bf16[64,256]{1,0:T(8,128)(2,1)S(1)}, bf16[648,256]{1,0:T(8,128)(2,1)S(1)}, bf16[648,256]{1,0:T(8,128)(2,1)S(1)}) custom-call(bf16[72,256]{1,0:T(8,128)(2,1)S(1)} %get-tuple-element.47.refs_0_, bf16[72,256]{1,0:T(8,128)(2,1)S(1)} %collective-permute-done.7.refs_1_, ...), custom_call_target="tpu_custom_call" | custom-call | flops 150994944 | bytes 2498560 | tf_op jit(solution)/shard_map/pallas_call | solution.py:30
  30.0 1.6 %collective-permute-done.10.b_ref = bf16[648,256]{1,0:T(8,128)(2,1)S(1)} collective-permute-done((bf16[648,256]{1,0:T(8,128)(2,1)S(1)}, bf16[648,256]{1,0:T(8,128)(2,1)S(1)}, u32[]{:S(2)}, u32[]{:S(2)}) %collective-permute-start.10) | collective-permute-done | bytes 331808 | tf_op jit(solution)/shard_map/ppermute | solution.py:343
  31.7 1.0 %collective-permute-start.18 = (bf16[576,256]{1,0:T(8,128)(2,1)S(1)}, bf16[576,256]{1,0:T(8,128)(2,1)S(1)}, u32[]{:S(2)}, u32[]{:S(2)}) collective-permute-start(bf16[576,256]{1,0:T(8,128)(2,1)S(1)} %get-tuple-element.67.a_ref), channel_id=1, source_target_pairs={{0,2},{2,0},{1,3},{3,1},{4,6},{6,4},{5,7},{7,5},{8,10},{10,8},{9,1... | collective-permute-start | bytes 884744 | tf_op jit(solution)/shard_map/ppermute | solution.py:371
  32.6 1.1 %collective-permute-start.11 = (bf16[136,256]{1,0:T(8,128)(2,1)S(1)}, bf16[136,256]{1,0:T(8,128)(2,1)S(1)}, u32[]{:S(2)}, u32[]{:S(2)}) collective-permute-start(bf16[136,256]{1,0:T(8,128)(2,1)S(1)} %get-tuple-element.62), channel_id=1, source_target_pairs={{0,4},{4,0},{8,12},{12,8},{1,5},{5,1},{9,13},{13,9},{2,6},{6,2},{1... | collective-permute-start | bytes 208904 | tf_op jit(solution)/shard_map/ppermute | solution.py:371
  33.7 2.4 %collective-permute-start.14 = (bf16[72,256]{1,0:T(8,128)(2,1)S(1)}, bf16[72,256]{1,0:T(8,128)(2,1)S(1)}, u32[]{:S(2)}, u32[]{:S(2)}) collective-permute-start(bf16[72,256]{1,0:T(8,128)(2,1)S(1)} %get-tuple-element.66.refs_0_), channel_id=1, source_target_pairs={{0,12},{4,8},{8,4},{12,0},{1,13},{5,9},{9,5},{13,1},{2,14},{6,10},... | collective-permute-start | bytes 110600 | tf_op jit(solution)/shard_map/ppermute | solution.py:371
  36.1 1.2 %collective-permute-done.12.b_ref.refs_4_ = bf16[64,256]{1,0:T(8,128)(2,1)S(1)} collective-permute-done((bf16[64,256]{1,0:T(8,128)(2,1)S(1)}, bf16[64,256]{1,0:T(8,128)(2,1)S(1)}, u32[]{:S(2)}, u32[]{:S(2)}) %collective-permute-start.12) | collective-permute-done | bytes 32800 | tf_op jit(solution)/shard_map/ppermute | solution.py:357
  37.3 2.4 %collective-permute-done.14.refs_3_ = bf16[72,256]{1,0:T(8,128)(2,1)S(1)} collective-permute-done((bf16[72,256]{1,0:T(8,128)(2,1)S(1)}, bf16[72,256]{1,0:T(8,128)(2,1)S(1)}, u32[]{:S(2)}, u32[]{:S(2)}) %collective-permute-start.14) | collective-permute-done | bytes 36896 | tf_op jit(solution)/shard_map/ppermute | solution.py:371
  39.7 1.3 %collective-permute-done.13.refs_2_ = bf16[72,256]{1,0:T(8,128)(2,1)S(1)} collective-permute-done((bf16[72,256]{1,0:T(8,128)(2,1)S(1)}, bf16[72,256]{1,0:T(8,128)(2,1)S(1)}, u32[]{:S(2)}, u32[]{:S(2)}) %collective-permute-start.13) | collective-permute-done | bytes 36896 | tf_op jit(solution)/shard_map/ppermute | solution.py:371
  41.2 1.2 %collective-permute-start.17 = (bf16[72,256]{1,0:T(8,128)(2,1)S(1)}, bf16[72,256]{1,0:T(8,128)(2,1)S(1)}, u32[]{:S(2)}, u32[]{:S(2)}) collective-permute-start(bf16[72,256]{1,0:T(8,128)(2,1)S(1)} %shard_map.76.refs_0_.mine_ref), channel_id=1, source_target_pairs={{0,2},{2,0},{1,3},{3,1},{4,6},{6,4},{5,7},{7,5},{8,10},{10,8},{9,1... | collective-permute-start | bytes 110600 | tf_op jit(solution)/shard_map/ppermute | solution.py:371
  43.4 1.2 %shard_map.75 = (bf16[64,8,128]{2,1,0:T(8,128)(2,1)}, f32[8,128]{1,0:T(8,128)S(1)}) custom-call(bf16[8,64,256]{2,1,0:T(8,128)(2,1)S(1)} %get-tuple-element.58.g_ref, bf16[136,256]{1,0:T(8,128)(2,1)S(1)} %collective-permute-done.11.a_ref.refs_1_, bf16[64,256]{1,0:T(8,128)(2,1)S(1)} %collective-permute-done.12.b_ref.refs_4_, ...), custom_call_target="tpu_custom_call" | custom-call | flops 150994944 | bytes 573440 | tf_op jit(solution)/shard_map/pallas_call | solution.py:30
  44.6 1.1 %shard_map.78 = (f32[1152,256]{1,0:T(8,128)}, f32[8,128]{1,0:T(8,128)S(1)}) custom-call(bf16[576,256]{1,0:T(8,128)(2,1)S(1)} %shard_map.77.mine_ref, bf16[576,256]{1,0:T(8,128)(2,1)S(1)} %collective-permute-done.19.other_ref), custom_call_target="tpu_custom_call" | custom-call | flops 100000000 | bytes 1773568 | tf_op jit(solution)/shard_map/pallas_call | solution.py:30
  45.8 0.9 %shard_map.79 = f32[3,192,64]{2,1,0:T(8,128)} custom-call(bf16[72,256]{1,0:T(8,128)(2,1)S(1)} %shard_map.76.refs_0_.mine_ref, bf16[72,256]{1,0:T(8,128)(2,1)S(1)} %collective-permute-done.15.beside_ref, bf16[72,256]{1,0:T(8,128)(2,1)S(1)} %collective-permute-done.16.corner_ref, bf16[72,256]{1,0:T(8,128)(2,1)S(1)} %collective-permute-done.17.across_ref, ...), custom_call_target="tpu_custom_call" | custom-call | flops 1 | bytes 303104 | tf_op jit(solution)/shard_map/pallas_call | solution.py:30
  (42 shorter events, 7.0 us)
Async XLA Ops:
  0.6 20.0 %copy-start = (bf16[128,3,3,256]{3,0,2,1:T(8,128)(2,1)S(1)}, bf16[128,3,3,256]{3,0,2,1:T(8,128)(2,1)}, u32[]{:S(2)}) copy-start(bf16[128,3,3,256]{3,0,2,1:T(8,128)(2,1)} %param.6) | copy-start | bytes 1769476
  1.7 4.8 %collective-permute-start.1 = (bf16[64,128]{1,0:T(8,128)(2,1)S(1)}, bf16[64,128]{1,0:T(8,128)(2,1)S(1)}, u32[]{:S(2)}, u32[]{:S(2)}) collective-permute-start(bf16[64,128]{1,0:T(8,128)(2,1)S(1)} %get-tuple-element.71), channel_id=1, source_target_pairs={{0,4},{4,0},{8,12},{12,8},{1,5},{5,1},{9,13},{13,9},{2,6},{6,2},{1... | collective-permute-start | bytes 49160 | tf_op jit(solution)/shard_map/ppermute | solution.py:343
  4.7 1.7 %collective-permute-start = (bf16[64,128]{1,0:T(8,128)(2,1)S(1)}, bf16[64,128]{1,0:T(8,128)(2,1)S(1)}, u32[]{:S(2)}, u32[]{:S(2)}) collective-permute-start(bf16[64,128]{1,0:T(8,128)(2,1)S(1)} %get-tuple-element.72), channel_id=1, source_target_pairs={{0,1},{1,0},{4,8},{5,9},{8,4},{9,5},{12,13},{13,12},{2,3},{3,2},{6... | collective-permute-start | bytes 49160 | tf_op jit(solution)/shard_map/ppermute | solution.py:357
  6.6 4.0 %collective-permute-start.2 = (bf16[144,128]{1,0:T(8,128)(2,1)S(1)}, bf16[144,128]{1,0:T(8,128)(2,1)S(1)}, u32[]{:S(2)}, u32[]{:S(2)}) collective-permute-start(bf16[144,128]{1,0:T(8,128)(2,1)S(1)} %get-tuple-element.39), channel_id=1, source_target_pairs={{0,16},{1,2},{2,1},{3,19},{16,0},{17,18},{18,17},{19,3},{4,20},{5,... | collective-permute-start | bytes 110600 | tf_op jit(solution)/shard_map/ppermute | solution.py:367
  8.6 2.0 %collective-permute-start.3 = (bf16[144,128]{1,0:T(8,128)(2,1)S(1)}, bf16[144,128]{1,0:T(8,128)(2,1)S(1)}, u32[]{:S(2)}, u32[]{:S(2)}) collective-permute-start(bf16[144,128]{1,0:T(8,128)(2,1)S(1)} %get-tuple-element.40), channel_id=1, source_target_pairs={{0,1},{1,0},{2,3},{3,2},{4,5},{5,4},{6,7},{7,6},{8,9},{9,8},{10,11... | collective-permute-start | bytes 110600 | tf_op jit(solution)/shard_map/ppermute | solution.py:343
  8.7 0.9 %copy-start.1 = (bf16[64,3,3,64]{3,0,2,1:T(8,128)(2,1)S(1)}, bf16[64,3,3,64]{3,0,2,1:T(8,128)(2,1)}, u32[]{:S(2)}) copy-start(bf16[64,3,3,64]{3,0,2,1:T(8,128)(2,1)} %param.5) | copy-start | bytes 221188
  11.4 6.1 %collective-permute-start.6 = (bf16[2,40,256]{2,1,0:T(8,128)(2,1)S(1)}, bf16[2,40,256]{2,1,0:T(8,128)(2,1)S(1)}, u32[]{:S(2)}, u32[]{:S(2)}) collective-permute-start(bf16[2,40,256]{2,1,0:T(8,128)(2,1)S(1)} %get-tuple-element.46.refs_0_), channel_id=1, source_target_pairs={{0,12},{4,8},{8,4},{12,0},{1,13},{5,9},{9,5},{13,1},{2,14},{6,10},... | collective-permute-start | bytes 122888 | tf_op jit(solution)/shard_map/ppermute | solution.py:371
  15.6 5.0 %collective-permute-start.5 = (bf16[2,40,256]{2,1,0:T(8,128)(2,1)S(1)}, bf16[2,40,256]{2,1,0:T(8,128)(2,1)S(1)}, u32[]{:S(2)}, u32[]{:S(2)}) collective-permute-start(bf16[2,40,256]{2,1,0:T(8,128)(2,1)S(1)} %get-tuple-element.46.refs_0_), channel_id=1, source_target_pairs={{0,8},{4,12},{8,0},{12,4},{1,9},{5,13},{9,1},{13,5},{2,10},{6,14},... | collective-permute-start | bytes 122888 | tf_op jit(solution)/shard_map/ppermute | solution.py:371
  16.2 4.4 %collective-permute-start.4 = (bf16[2,40,256]{2,1,0:T(8,128)(2,1)S(1)}, bf16[2,40,256]{2,1,0:T(8,128)(2,1)S(1)}, u32[]{:S(2)}, u32[]{:S(2)}) collective-permute-start(bf16[2,40,256]{2,1,0:T(8,128)(2,1)S(1)} %get-tuple-element.46.refs_0_), channel_id=1, source_target_pairs={{0,4},{4,0},{8,12},{12,8},{1,5},{5,1},{9,13},{13,9},{2,6},{6,2},{1... | collective-permute-start | bytes 122888 | tf_op jit(solution)/shard_map/ppermute | solution.py:371
  21.7 6.1 %collective-permute-start.7 = (bf16[72,256]{1,0:T(8,128)(2,1)S(1)}, bf16[72,256]{1,0:T(8,128)(2,1)S(1)}, u32[]{:S(2)}, u32[]{:S(2)}) collective-permute-start(bf16[72,256]{1,0:T(8,128)(2,1)S(1)} %get-tuple-element.48), channel_id=1, source_target_pairs={{0,12},{4,8},{8,4},{12,0},{1,13},{5,9},{9,5},{13,1},{2,14},{6,10},... | collective-permute-start | bytes 110600 | tf_op jit(solution)/shard_map/ppermute | solution.py:371
  24.1 4.9 %collective-permute-start.8 = (bf16[72,256]{1,0:T(8,128)(2,1)S(1)}, bf16[72,256]{1,0:T(8,128)(2,1)S(1)}, u32[]{:S(2)}, u32[]{:S(2)}) collective-permute-start(bf16[72,256]{1,0:T(8,128)(2,1)S(1)} %get-tuple-element.49), channel_id=1, source_target_pairs={{0,8},{4,12},{8,0},{12,4},{1,9},{5,13},{9,1},{13,5},{2,10},{6,14},... | collective-permute-start | bytes 110600 | tf_op jit(solution)/shard_map/ppermute | solution.py:371
  24.1 4.9 %collective-permute-start.9 = (bf16[72,256]{1,0:T(8,128)(2,1)S(1)}, bf16[72,256]{1,0:T(8,128)(2,1)S(1)}, u32[]{:S(2)}, u32[]{:S(2)}) collective-permute-start(bf16[72,256]{1,0:T(8,128)(2,1)S(1)} %get-tuple-element.50), channel_id=1, source_target_pairs={{0,4},{4,0},{8,12},{12,8},{1,5},{5,1},{9,13},{13,9},{2,6},{6,2},{1... | collective-permute-start | bytes 110600 | tf_op jit(solution)/shard_map/ppermute | solution.py:371
  29.9 1.7 %collective-permute-start.10 = (bf16[648,256]{1,0:T(8,128)(2,1)S(1)}, bf16[648,256]{1,0:T(8,128)(2,1)S(1)}, u32[]{:S(2)}, u32[]{:S(2)}) collective-permute-start(bf16[648,256]{1,0:T(8,128)(2,1)S(1)} %get-tuple-element.60), channel_id=1, source_target_pairs={{0,1},{1,0},{2,3},{3,2},{4,5},{5,4},{6,7},{7,6},{8,9},{9,8},{10,11... | collective-permute-start | bytes 995336 | tf_op jit(solution)/shard_map/ppermute | solution.py:343
  31.7 9.4 %collective-permute-start.18 = (bf16[576,256]{1,0:T(8,128)(2,1)S(1)}, bf16[576,256]{1,0:T(8,128)(2,1)S(1)}, u32[]{:S(2)}, u32[]{:S(2)}) collective-permute-start(bf16[576,256]{1,0:T(8,128)(2,1)S(1)} %get-tuple-element.67.a_ref), channel_id=1, source_target_pairs={{0,2},{2,0},{1,3},{3,1},{4,6},{6,4},{5,7},{7,5},{8,10},{10,8},{9,1... | collective-permute-start | bytes 884744 | tf_op jit(solution)/shard_map/ppermute | solution.py:371
  32.6 8.4 %collective-permute-start.11 = (bf16[136,256]{1,0:T(8,128)(2,1)S(1)}, bf16[136,256]{1,0:T(8,128)(2,1)S(1)}, u32[]{:S(2)}, u32[]{:S(2)}) collective-permute-start(bf16[136,256]{1,0:T(8,128)(2,1)S(1)} %get-tuple-element.62), channel_id=1, source_target_pairs={{0,4},{4,0},{8,12},{12,8},{1,5},{5,1},{9,13},{13,9},{2,6},{6,2},{1... | collective-permute-start | bytes 208904 | tf_op jit(solution)/shard_map/ppermute | solution.py:371
  33.7 6.0 %collective-permute-start.14 = (bf16[72,256]{1,0:T(8,128)(2,1)S(1)}, bf16[72,256]{1,0:T(8,128)(2,1)S(1)}, u32[]{:S(2)}, u32[]{:S(2)}) collective-permute-start(bf16[72,256]{1,0:T(8,128)(2,1)S(1)} %get-tuple-element.66.refs_0_), channel_id=1, source_target_pairs={{0,12},{4,8},{8,4},{12,0},{1,13},{5,9},{9,5},{13,1},{2,14},{6,10},... | collective-permute-start | bytes 110600 | tf_op jit(solution)/shard_map/ppermute | solution.py:371
  36.1 4.9 %collective-permute-start.13 = (bf16[72,256]{1,0:T(8,128)(2,1)S(1)}, bf16[72,256]{1,0:T(8,128)(2,1)S(1)}, u32[]{:S(2)}, u32[]{:S(2)}) collective-permute-start(bf16[72,256]{1,0:T(8,128)(2,1)S(1)} %get-tuple-element.66.refs_0_), channel_id=1, source_target_pairs={{0,8},{4,12},{8,0},{12,4},{1,9},{5,13},{9,1},{13,5},{2,10},{6,14},... | collective-permute-start | bytes 110600 | tf_op jit(solution)/shard_map/ppermute | solution.py:371
  36.1 1.2 %collective-permute-start.12 = (bf16[64,256]{1,0:T(8,128)(2,1)S(1)}, bf16[64,256]{1,0:T(8,128)(2,1)S(1)}, u32[]{:S(2)}, u32[]{:S(2)}) collective-permute-start(bf16[64,256]{1,0:T(8,128)(2,1)S(1)} %get-tuple-element.63), channel_id=1, source_target_pairs={{0,1},{1,0},{4,8},{5,9},{8,4},{9,5},{12,13},{13,12},{2,3},{3,2},{6... | collective-permute-start | bytes 98312 | tf_op jit(solution)/shard_map/ppermute | solution.py:357
  41.1 3.5 %collective-permute-start.19 = (bf16[576,256]{1,0:T(8,128)(2,1)S(1)}, bf16[576,256]{1,0:T(8,128)(2,1)S(1)}, u32[]{:S(2)}, u32[]{:S(2)}) collective-permute-start(bf16[576,256]{1,0:T(8,128)(2,1)S(1)} %shard_map.77.mine_ref), channel_id=1, source_target_pairs={{0,1},{1,0},{2,3},{3,2},{4,5},{5,4},{6,7},{7,6},{8,9},{9,8},{10,11... | collective-permute-start | bytes 884744 | tf_op jit(solution)/shard_map/ppermute | solution.py:343
  41.2 4.5 %collective-permute-start.17 = (bf16[72,256]{1,0:T(8,128)(2,1)S(1)}, bf16[72,256]{1,0:T(8,128)(2,1)S(1)}, u32[]{:S(2)}, u32[]{:S(2)}) collective-permute-start(bf16[72,256]{1,0:T(8,128)(2,1)S(1)} %shard_map.76.refs_0_.mine_ref), channel_id=1, source_target_pairs={{0,2},{2,0},{1,3},{3,1},{4,6},{6,4},{5,7},{7,5},{8,10},{10,8},{9,1... | collective-permute-start | bytes 110600 | tf_op jit(solution)/shard_map/ppermute | solution.py:371
  42.4 3.4 %collective-permute-start.16 = (bf16[72,256]{1,0:T(8,128)(2,1)S(1)}, bf16[72,256]{1,0:T(8,128)(2,1)S(1)}, u32[]{:S(2)}, u32[]{:S(2)}) collective-permute-start(bf16[72,256]{1,0:T(8,128)(2,1)S(1)} %shard_map.76.refs_0_.mine_ref), channel_id=1, source_target_pairs={{0,3},{1,2},{2,1},{3,0},{4,7},{5,6},{6,5},{7,4},{8,11},{9,10},{10,... | collective-permute-start | bytes 110600 | tf_op jit(solution)/shard_map/ppermute | solution.py:377
  43.1 2.7 %collective-permute-start.15 = (bf16[72,256]{1,0:T(8,128)(2,1)S(1)}, bf16[72,256]{1,0:T(8,128)(2,1)S(1)}, u32[]{:S(2)}, u32[]{:S(2)}) collective-permute-start(bf16[72,256]{1,0:T(8,128)(2,1)S(1)} %shard_map.76.refs_0_.mine_ref), channel_id=1, source_target_pairs={{0,1},{1,0},{2,3},{3,2},{4,5},{5,4},{6,7},{7,6},{8,9},{9,8},{10,11... | collective-permute-start | bytes 110600 | tf_op jit(solution)/shard_map/ppermute | solution.py:343

commit v28 on v24

--- a/solution.py
+++ b/solution.py
@@ -133,8 +133,8 @@
     x_ref,
     above_ref,
     below_ref,
+    b_ref,
     a_ref,
-    b_ref,
     w_ref,
     pool_ref,
     order_ref,
@@ -444,7 +444,7 @@
             shaped((band_rows, channels, 256)),
             shaped((band_rows + 2, channels, 256)),
         ],
-        [x, above, below, side_a, side_b, joined_one, pool, order],
+        [x, above, below, side_b, side_a, joined_one, pool, order],
         2 * band_rows * 192 * 192 * 256,
     )
     pieces = row_swaps([pooled] * bands, bands, near_first=True)

time: 46.8 us -> 46.8 us (level)
  no operation moved by 1% of the time
where the time goes in v28:
time: 46.8 us; the launch traced here: 46.6 us
  starting transfers between devices  22.6 us (48%)
  waiting for transfers between devices  13.3 us (28%)
  Pallas kernels  7.08 us (15%)
  local copies, waits for them, and re-layouts  2.78 us (6%)
  between operations  0.8 us (2%)
    ppermute x11, starting transfers between devices, xor_swap(): return lax.ppermute(values, axis, [(n, n ^ k) for n in range(count)])  16.2 us
    ppermute x11, waiting for transfers between devices, xor_swap(): return lax.ppermute(values, axis, [(n, n ^ k) for n in range(count)])  8.85 us
    pallas_call x13, Pallas kernels, whole_call(): pl.pallas_call(body, out_shape=outs, in_specs=specs, out_specs=[pl.BlockS...  7.08 us
    ppermute x5, starting transfers between devices, even_swap(): return lax.ppermute(values, axis, [(n, n ^ 1) for n in range(count)])  3.66 us
    unnamed x6, local copies, waits for them, and re-layouts  2.75 us
    ppermute x5, waiting for transfers between devices, even_swap(): return lax.ppermute(values, axis, [(n, n ^ 1) for n in range(count)])  2.35 us
    ppermute x1, starting transfers between devices, odd_strip_swap(): return lax.ppermute(values, ('grp',) + COLS, steps)  2.01 us
    ppermute x2, waiting for transfers between devices, odd_row_swap(): return lax.ppermute(values, ('row', 'pair'), steps)  1.21 us
  transfers between devices with their start and end apart: 20, of which 12 were waited for; matrix products, arithmetic and copies ran while one was open for 2% of the time, Pallas kernels for 7%

profile of v28, /device:TPU:0, one launch (start us, length us, event | category | flops | bytes accessed | tf_op | source)
XLA Modules:
  0.0 46.6 jit_solution(7863854784834896744)
XLA Ops:
  0.7 1.0 %copy.19 = bf16[64,8,128]{2,0,1:T(8,128)(2,1)S(1)} copy(bf16[64,8,128]{2,1,0:T(8,128)(2,1)} %param.4) | data formatting | bytes 262144 | tf_op args[0]
  1.7 3.1 %collective-permute-start.1 = (bf16[64,128]{1,0:T(8,128)(2,1)S(1)}, bf16[64,128]{1,0:T(8,128)(2,1)S(1)}, u32[]{:S(2)}, u32[]{:S(2)}) collective-permute-start(bf16[64,128]{1,0:T(8,128)(2,1)S(1)} %get-tuple-element.71), channel_id=1, source_target_pairs={{0,4},{4,0},{8,12},{12,8},{1,5},{5,1},{9,13},{13,9},{2,6},{6,2},{1... | collective-permute-start | bytes 49160 | tf_op jit(solution)/shard_map/ppermute | solution.py:343
  6.6 2.0 %collective-permute-start.2 = (bf16[144,128]{1,0:T(8,128)(2,1)S(1)}, bf16[144,128]{1,0:T(8,128)(2,1)S(1)}, u32[]{:S(2)}, u32[]{:S(2)}) collective-permute-start(bf16[144,128]{1,0:T(8,128)(2,1)S(1)} %get-tuple-element.39), channel_id=1, source_target_pairs={{0,16},{1,2},{2,1},{3,19},{16,0},{17,18},{18,17},{19,3},{4,20},{5,... | collective-permute-start | bytes 110600 | tf_op jit(solution)/shard_map/ppermute | solution.py:367
  8.7 0.9 %copy-done.1 = bf16[64,3,3,64]{3,0,2,1:T(8,128)(2,1)S(1)} copy-done((bf16[64,3,3,64]{3,0,2,1:T(8,128)(2,1)S(1)}, bf16[64,3,3,64]{3,0,2,1:T(8,128)(2,1)}, u32[]{:S(2)}) %copy-start.1) | copy-done | bytes 73752
  10.6 0.9 %shard_map.70 = (bf16[2,40,256]{2,1,0:T(8,128)(2,1)S(1)}, bf16[8,64,256]{2,1,0:T(8,128)(2,1)S(1)}, bf16[10,64,256]{2,1,0:T(8,128)(2,1)S(1)}) custom-call(bf16[8,64,128]{2,1,0:T(8,128)(2,1)S(1)} %bitcast.34, bf16[64,128]{1,0:T(8,128)(2,1)S(1)} %get-tuple-element.41.above_ref, bf16[64,128]{1,0:T(8,128)(2,1)S(1)} %get-tuple-element.42.below_ref, ...), custom_call_target="tpu_custom_call" | custom-call | flops 150994944 | bytes 1122304 | tf_op jit(solution)/shard_map/pallas_call | solution.py:30
  11.4 4.1 %collective-permute-start.6 = (bf16[2,40,256]{2,1,0:T(8,128)(2,1)S(1)}, bf16[2,40,256]{2,1,0:T(8,128)(2,1)S(1)}, u32[]{:S(2)}, u32[]{:S(2)}) collective-permute-start(bf16[2,40,256]{2,1,0:T(8,128)(2,1)S(1)} %get-tuple-element.46.refs_0_), channel_id=1, source_target_pairs={{0,12},{4,8},{8,4},{12,0},{1,13},{5,9},{9,5},{13,1},{2,14},{6,10},... | collective-permute-start | bytes 122888 | tf_op jit(solution)/shard_map/ppermute | solution.py:371
  17.5 3.0 %collective-permute-done.5.refs_2_ = bf16[2,40,256]{2,1,0:T(8,128)(2,1)S(1)} collective-permute-done((bf16[2,40,256]{2,1,0:T(8,128)(2,1)S(1)}, bf16[2,40,256]{2,1,0:T(8,128)(2,1)S(1)}, u32[]{:S(2)}, u32[]{:S(2)}) %collective-permute-start.5) | collective-permute-done | bytes 40992 | tf_op jit(solution)/shard_map/ppermute | solution.py:371
  20.6 1.0 %shard_map.71 = (bf16[72,256]{1,0:T(8,128)(2,1)S(1)}, bf16[72,256]{1,0:T(8,128)(2,1)S(1)}, bf16[72,256]{1,0:T(8,128)(2,1)S(1)}, bf16[72,256]{1,0:T(8,128)(2,1)S(...) custom-call(bf16[8,48,128]{2,1,0:T(8,128)(2,1)S(1)} %fusion.6.og_ref, ...), custom_call_target="tpu_custom_call" | custom-call | flops 452984832 | bytes 1368064 | tf_op jit(solution)/shard_map/pallas_call | solution.py:30
  21.7 2.5 %collective-permute-start.7 = (bf16[72,256]{1,0:T(8,128)(2,1)S(1)}, bf16[72,256]{1,0:T(8,128)(2,1)S(1)}, u32[]{:S(2)}, u32[]{:S(2)}) collective-permute-start(bf16[72,256]{1,0:T(8,128)(2,1)S(1)} %get-tuple-element.48), channel_id=1, source_target_pairs={{0,12},{4,8},{8,4},{12,0},{1,13},{5,9},{9,5},{13,1},{2,14},{6,10},... | collective-permute-start | bytes 110600 | tf_op jit(solution)/shard_map/ppermute | solution.py:371
  24.1 2.0 %collective-permute-start.9 = (bf16[72,256]{1,0:T(8,128)(2,1)S(1)}, bf16[72,256]{1,0:T(8,128)(2,1)S(1)}, u32[]{:S(2)}, u32[]{:S(2)}) collective-permute-start(bf16[72,256]{1,0:T(8,128)(2,1)S(1)} %get-tuple-element.50), channel_id=1, source_target_pairs={{0,4},{4,0},{8,12},{12,8},{1,5},{5,1},{9,13},{13,9},{2,6},{6,2},{1... | collective-permute-start | bytes 110600 | tf_op jit(solution)/shard_map/ppermute | solution.py:371
  26.7 1.0 %collective-permute-done.7.refs_1_ = bf16[72,256]{1,0:T(8,128)(2,1)S(1)} collective-permute-done((bf16[72,256]{1,0:T(8,128)(2,1)S(1)}, bf16[72,256]{1,0:T(8,128)(2,1)S(1)}, u32[]{:S(2)}, u32[]{:S(2)}) %collective-permute-start.7) | collective-permute-done | bytes 36896 | tf_op jit(solution)/shard_map/ppermute | solution.py:371
  27.7 1.2 %collective-permute-done.8.refs_2_ = bf16[72,256]{1,0:T(8,128)(2,1)S(1)} collective-permute-done((bf16[72,256]{1,0:T(8,128)(2,1)S(1)}, bf16[72,256]{1,0:T(8,128)(2,1)S(1)}, u32[]{:S(2)}, u32[]{:S(2)}) %collective-permute-start.8) | collective-permute-done | bytes 36896 | tf_op jit(solution)/shard_map/ppermute | solution.py:371
  29.0 0.9 %shard_map.73 = (bf16[8,64,256]{2,1,0:T(8,128)(2,1)S(1)}, bf16[64,256]{1,0:T(8,128)(2,1)S(1)}, bf16[64,256]{1,0:T(8,128)(2,1)S(1)}, bf16[648,256]{1,0:T(8,128)(2,1)S(1)}, bf16[648,256]{1,0:T(8,128)(2,1)S(1)}) custom-call(bf16[72,256]{1,0:T(8,128)(2,1)S(1)} %get-tuple-element.47.refs_0_, bf16[72,256]{1,0:T(8,128)(2,1)S(1)} %collective-permute-done.7.refs_1_, ...), custom_call_target="tpu_custom_call" | custom-call | flops 150994944 | bytes 2498560 | tf_op jit(solution)/shard_map/pallas_call | solution.py:30
  30.0 1.6 %collective-permute-done.10.b_ref = bf16[648,256]{1,0:T(8,128)(2,1)S(1)} collective-permute-done((bf16[648,256]{1,0:T(8,128)(2,1)S(1)}, bf16[648,256]{1,0:T(8,128)(2,1)S(1)}, u32[]{:S(2)}, u32[]{:S(2)}) %collective-permute-start.10) | collective-permute-done | bytes 331808 | tf_op jit(solution)/shard_map/ppermute | solution.py:343
  31.7 1.0 %collective-permute-start.18 = (bf16[576,256]{1,0:T(8,128)(2,1)S(1)}, bf16[576,256]{1,0:T(8,128)(2,1)S(1)}, u32[]{:S(2)}, u32[]{:S(2)}) collective-permute-start(bf16[576,256]{1,0:T(8,128)(2,1)S(1)} %get-tuple-element.67.a_ref), channel_id=1, source_target_pairs={{0,2},{2,0},{1,3},{3,1},{4,6},{6,4},{5,7},{7,5},{8,10},{10,8},{9,1... | collective-permute-start | bytes 884744 | tf_op jit(solution)/shard_map/ppermute | solution.py:371
  32.6 1.1 %collective-permute-start.11 = (bf16[136,256]{1,0:T(8,128)(2,1)S(1)}, bf16[136,256]{1,0:T(8,128)(2,1)S(1)}, u32[]{:S(2)}, u32[]{:S(2)}) collective-permute-start(bf16[136,256]{1,0:T(8,128)(2,1)S(1)} %get-tuple-element.62), channel_id=1, source_target_pairs={{0,4},{4,0},{8,12},{12,8},{1,5},{5,1},{9,13},{13,9},{2,6},{6,2},{1... | collective-permute-start | bytes 208904 | tf_op jit(solution)/shard_map/ppermute | solution.py:371
  33.7 1.3 %collective-permute-start.14 = (bf16[72,256]{1,0:T(8,128)(2,1)S(1)}, bf16[72,256]{1,0:T(8,128)(2,1)S(1)}, u32[]{:S(2)}, u32[]{:S(2)}) collective-permute-start(bf16[72,256]{1,0:T(8,128)(2,1)S(1)} %get-tuple-element.66.refs_0_), channel_id=1, source_target_pairs={{0,8},{4,12},{8,0},{12,4},{1,9},{5,13},{9,1},{13,5},{2,10},{6,14},... | collective-permute-start | bytes 110600 | tf_op jit(solution)/shard_map/ppermute | solution.py:371
  35.1 2.0 %collective-permute-start.13 = (bf16[72,256]{1,0:T(8,128)(2,1)S(1)}, bf16[72,256]{1,0:T(8,128)(2,1)S(1)}, u32[]{:S(2)}, u32[]{:S(2)}) collective-permute-start(bf16[72,256]{1,0:T(8,128)(2,1)S(1)} %get-tuple-element.66.refs_0_), channel_id=1, source_target_pairs={{0,12},{4,8},{8,4},{12,0},{1,13},{5,9},{9,5},{13,1},{2,14},{6,10},... | collective-permute-start | bytes 110600 | tf_op jit(solution)/shard_map/ppermute | solution.py:371
  37.0 1.2 %collective-permute-done.12.b_ref.refs_4_ = bf16[64,256]{1,0:T(8,128)(2,1)S(1)} collective-permute-done((bf16[64,256]{1,0:T(8,128)(2,1)S(1)}, bf16[64,256]{1,0:T(8,128)(2,1)S(1)}, u32[]{:S(2)}, u32[]{:S(2)}) %collective-permute-start.12) | collective-permute-done | bytes 32800 | tf_op jit(solution)/shard_map/ppermute | solution.py:357
  38.2 1.5 %collective-permute-done.14.refs_3_ = bf16[72,256]{1,0:T(8,128)(2,1)S(1)} collective-permute-done((bf16[72,256]{1,0:T(8,128)(2,1)S(1)}, bf16[72,256]{1,0:T(8,128)(2,1)S(1)}, u32[]{:S(2)}, u32[]{:S(2)}) %collective-permute-start.14) | collective-permute-done | bytes 36896 | tf_op jit(solution)/shard_map/ppermute | solution.py:371
  39.8 1.2 %collective-permute-done.13.refs_2_ = bf16[72,256]{1,0:T(8,128)(2,1)S(1)} collective-permute-done((bf16[72,256]{1,0:T(8,128)(2,1)S(1)}, bf16[72,256]{1,0:T(8,128)(2,1)S(1)}, u32[]{:S(2)}, u32[]{:S(2)}) %collective-permute-start.13) | collective-permute-done | bytes 36896 | tf_op jit(solution)/shard_map/ppermute | solution.py:371
  41.1 1.2 %collective-permute-start.17 = (bf16[72,256]{1,0:T(8,128)(2,1)S(1)}, bf16[72,256]{1,0:T(8,128)(2,1)S(1)}, u32[]{:S(2)}, u32[]{:S(2)}) collective-permute-start(bf16[72,256]{1,0:T(8,128)(2,1)S(1)} %shard_map.76.refs_0_.mine_ref), channel_id=1, source_target_pairs={{0,2},{2,0},{1,3},{3,1},{4,6},{6,4},{5,7},{7,5},{8,10},{10,8},{9,1... | collective-permute-start | bytes 110600 | tf_op jit(solution)/shard_map/ppermute | solution.py:371
  43.3 1.2 %shard_map.75 = (bf16[64,8,128]{2,1,0:T(8,128)(2,1)}, f32[8,128]{1,0:T(8,128)S(1)}) custom-call(bf16[8,64,256]{2,1,0:T(8,128)(2,1)S(1)} %get-tuple-element.58.g_ref, bf16[136,256]{1,0:T(8,128)(2,1)S(1)} %collective-permute-done.11.a_ref.refs_1_, bf16[64,256]{1,0:T(8,128)(2,1)S(1)} %collective-permute-done.12.b_ref.refs_4_, ...), custom_call_target="tpu_custom_call" | custom-call | flops 150994944 | bytes 573440 | tf_op jit(solution)/shard_map/pallas_call | solution.py:30
  44.5 1.1 %shard_map.78 = (f32[1152,256]{1,0:T(8,128)}, f32[8,128]{1,0:T(8,128)S(1)}) custom-call(bf16[576,256]{1,0:T(8,128)(2,1)S(1)} %shard_map.77.mine_ref, bf16[576,256]{1,0:T(8,128)(2,1)S(1)} %collective-permute-done.19.other_ref), custom_call_target="tpu_custom_call" | custom-call | flops 100000000 | bytes 1773568 | tf_op jit(solution)/shard_map/pallas_call | solution.py:30
  (42 shorter events, 7.9 us)
Async XLA Ops:
  0.6 20.0 %copy-start = (bf16[128,3,3,256]{3,0,2,1:T(8,128)(2,1)S(1)}, bf16[128,3,3,256]{3,0,2,1:T(8,128)(2,1)}, u32[]{:S(2)}) copy-start(bf16[128,3,3,256]{3,0,2,1:T(8,128)(2,1)} %param.6) | copy-start | bytes 1769476
  1.7 4.8 %collective-permute-start.1 = (bf16[64,128]{1,0:T(8,128)(2,1)S(1)}, bf16[64,128]{1,0:T(8,128)(2,1)S(1)}, u32[]{:S(2)}, u32[]{:S(2)}) collective-permute-start(bf16[64,128]{1,0:T(8,128)(2,1)S(1)} %get-tuple-element.71), channel_id=1, source_target_pairs={{0,4},{4,0},{8,12},{12,8},{1,5},{5,1},{9,13},{13,9},{2,6},{6,2},{1... | collective-permute-start | bytes 49160 | tf_op jit(solution)/shard_map/ppermute | solution.py:343
  4.7 1.7 %collective-permute-start = (bf16[64,128]{1,0:T(8,128)(2,1)S(1)}, bf16[64,128]{1,0:T(8,128)(2,1)S(1)}, u32[]{:S(2)}, u32[]{:S(2)}) collective-permute-start(bf16[64,128]{1,0:T(8,128)(2,1)S(1)} %get-tuple-element.72), channel_id=1, source_target_pairs={{0,1},{1,0},{4,8},{5,9},{8,4},{9,5},{12,13},{13,12},{2,3},{3,2},{6... | collective-permute-start | bytes 49160 | tf_op jit(solution)/shard_map/ppermute | solution.py:357
  6.6 4.0 %collective-permute-start.2 = (bf16[144,128]{1,0:T(8,128)(2,1)S(1)}, bf16[144,128]{1,0:T(8,128)(2,1)S(1)}, u32[]{:S(2)}, u32[]{:S(2)}) collective-permute-start(bf16[144,128]{1,0:T(8,128)(2,1)S(1)} %get-tuple-element.39), channel_id=1, source_target_pairs={{0,16},{1,2},{2,1},{3,19},{16,0},{17,18},{18,17},{19,3},{4,20},{5,... | collective-permute-start | bytes 110600 | tf_op jit(solution)/shard_map/ppermute | solution.py:367
  8.6 2.0 %collective-permute-start.3 = (bf16[144,128]{1,0:T(8,128)(2,1)S(1)}, bf16[144,128]{1,0:T(8,128)(2,1)S(1)}, u32[]{:S(2)}, u32[]{:S(2)}) collective-permute-start(bf16[144,128]{1,0:T(8,128)(2,1)S(1)} %get-tuple-element.40), channel_id=1, source_target_pairs={{0,1},{1,0},{2,3},{3,2},{4,5},{5,4},{6,7},{7,6},{8,9},{9,8},{10,11... | collective-permute-start | bytes 110600 | tf_op jit(solution)/shard_map/ppermute | solution.py:343
  8.7 0.9 %copy-start.1 = (bf16[64,3,3,64]{3,0,2,1:T(8,128)(2,1)S(1)}, bf16[64,3,3,64]{3,0,2,1:T(8,128)(2,1)}, u32[]{:S(2)}) copy-start(bf16[64,3,3,64]{3,0,2,1:T(8,128)(2,1)} %param.5) | copy-start | bytes 221188
  11.4 6.1 %collective-permute-start.6 = (bf16[2,40,256]{2,1,0:T(8,128)(2,1)S(1)}, bf16[2,40,256]{2,1,0:T(8,128)(2,1)S(1)}, u32[]{:S(2)}, u32[]{:S(2)}) collective-permute-start(bf16[2,40,256]{2,1,0:T(8,128)(2,1)S(1)} %get-tuple-element.46.refs_0_), channel_id=1, source_target_pairs={{0,12},{4,8},{8,4},{12,0},{1,13},{5,9},{9,5},{13,1},{2,14},{6,10},... | collective-permute-start | bytes 122888 | tf_op jit(solution)/shard_map/ppermute | solution.py:371
  15.6 5.0 %collective-permute-start.5 = (bf16[2,40,256]{2,1,0:T(8,128)(2,1)S(1)}, bf16[2,40,256]{2,1,0:T(8,128)(2,1)S(1)}, u32[]{:S(2)}, u32[]{:S(2)}) collective-permute-start(bf16[2,40,256]{2,1,0:T(8,128)(2,1)S(1)} %get-tuple-element.46.refs_0_), channel_id=1, source_target_pairs={{0,8},{4,12},{8,0},{12,4},{1,9},{5,13},{9,1},{13,5},{2,10},{6,14},... | collective-permute-start | bytes 122888 | tf_op jit(solution)/shard_map/ppermute | solution.py:371
  16.2 4.4 %collective-permute-start.4 = (bf16[2,40,256]{2,1,0:T(8,128)(2,1)S(1)}, bf16[2,40,256]{2,1,0:T(8,128)(2,1)S(1)}, u32[]{:S(2)}, u32[]{:S(2)}) collective-permute-start(bf16[2,40,256]{2,1,0:T(8,128)(2,1)S(1)} %get-tuple-element.46.refs_0_), channel_id=1, source_target_pairs={{0,4},{4,0},{8,12},{12,8},{1,5},{5,1},{9,13},{13,9},{2,6},{6,2},{1... | collective-permute-start | bytes 122888 | tf_op jit(solution)/shard_map/ppermute | solution.py:371
  21.7 6.1 %collective-permute-start.7 = (bf16[72,256]{1,0:T(8,128)(2,1)S(1)}, bf16[72,256]{1,0:T(8,128)(2,1)S(1)}, u32[]{:S(2)}, u32[]{:S(2)}) collective-permute-start(bf16[72,256]{1,0:T(8,128)(2,1)S(1)} %get-tuple-element.48), channel_id=1, source_target_pairs={{0,12},{4,8},{8,4},{12,0},{1,13},{5,9},{9,5},{13,1},{2,14},{6,10},... | collective-permute-start | bytes 110600 | tf_op jit(solution)/shard_map/ppermute | solution.py:371
  24.1 4.9 %collective-permute-start.8 = (bf16[72,256]{1,0:T(8,128)(2,1)S(1)}, bf16[72,256]{1,0:T(8,128)(2,1)S(1)}, u32[]{:S(2)}, u32[]{:S(2)}) collective-permute-start(bf16[72,256]{1,0:T(8,128)(2,1)S(1)} %get-tuple-element.49), channel_id=1, source_target_pairs={{0,8},{4,12},{8,0},{12,4},{1,9},{5,13},{9,1},{13,5},{2,10},{6,14},... | collective-permute-start | bytes 110600 | tf_op jit(solution)/shard_map/ppermute | solution.py:371
  24.1 4.9 %collective-permute-start.9 = (bf16[72,256]{1,0:T(8,128)(2,1)S(1)}, bf16[72,256]{1,0:T(8,128)(2,1)S(1)}, u32[]{:S(2)}, u32[]{:S(2)}) collective-permute-start(bf16[72,256]{1,0:T(8,128)(2,1)S(1)} %get-tuple-element.50), channel_id=1, source_target_pairs={{0,4},{4,0},{8,12},{12,8},{1,5},{5,1},{9,13},{13,9},{2,6},{6,2},{1... | collective-permute-start | bytes 110600 | tf_op jit(solution)/shard_map/ppermute | solution.py:371
  29.9 1.7 %collective-permute-start.10 = (bf16[648,256]{1,0:T(8,128)(2,1)S(1)}, bf16[648,256]{1,0:T(8,128)(2,1)S(1)}, u32[]{:S(2)}, u32[]{:S(2)}) collective-permute-start(bf16[648,256]{1,0:T(8,128)(2,1)S(1)} %get-tuple-element.60), channel_id=1, source_target_pairs={{0,1},{1,0},{2,3},{3,2},{4,5},{5,4},{6,7},{7,6},{8,9},{9,8},{10,11... | collective-permute-start | bytes 995336 | tf_op jit(solution)/shard_map/ppermute | solution.py:343
  31.7 9.3 %collective-permute-start.18 = (bf16[576,256]{1,0:T(8,128)(2,1)S(1)}, bf16[576,256]{1,0:T(8,128)(2,1)S(1)}, u32[]{:S(2)}, u32[]{:S(2)}) collective-permute-start(bf16[576,256]{1,0:T(8,128)(2,1)S(1)} %get-tuple-element.67.a_ref), channel_id=1, source_target_pairs={{0,2},{2,0},{1,3},{3,1},{4,6},{6,4},{5,7},{7,5},{8,10},{10,8},{9,1... | collective-permute-start | bytes 884744 | tf_op jit(solution)/shard_map/ppermute | solution.py:371
  32.6 8.3 %collective-permute-start.11 = (bf16[136,256]{1,0:T(8,128)(2,1)S(1)}, bf16[136,256]{1,0:T(8,128)(2,1)S(1)}, u32[]{:S(2)}, u32[]{:S(2)}) collective-permute-start(bf16[136,256]{1,0:T(8,128)(2,1)S(1)} %get-tuple-element.62), channel_id=1, source_target_pairs={{0,4},{4,0},{8,12},{12,8},{1,5},{5,1},{9,13},{13,9},{2,6},{6,2},{1... | collective-permute-start | bytes 208904 | tf_op jit(solution)/shard_map/ppermute | solution.py:371
  33.7 6.0 %collective-permute-start.14 = (bf16[72,256]{1,0:T(8,128)(2,1)S(1)}, bf16[72,256]{1,0:T(8,128)(2,1)S(1)}, u32[]{:S(2)}, u32[]{:S(2)}) collective-permute-start(bf16[72,256]{1,0:T(8,128)(2,1)S(1)} %get-tuple-element.66.refs_0_), channel_id=1, source_target_pairs={{0,8},{4,12},{8,0},{12,4},{1,9},{5,13},{9,1},{13,5},{2,10},{6,14},... | collective-permute-start | bytes 110600 | tf_op jit(solution)/shard_map/ppermute | solution.py:371
  35.1 5.9 %collective-permute-start.13 = (bf16[72,256]{1,0:T(8,128)(2,1)S(1)}, bf16[72,256]{1,0:T(8,128)(2,1)S(1)}, u32[]{:S(2)}, u32[]{:S(2)}) collective-permute-start(bf16[72,256]{1,0:T(8,128)(2,1)S(1)} %get-tuple-element.66.refs_0_), channel_id=1, source_target_pairs={{0,12},{4,8},{8,4},{12,0},{1,13},{5,9},{9,5},{13,1},{2,14},{6,10},... | collective-permute-start | bytes 110600 | tf_op jit(solution)/shard_map/ppermute | solution.py:371
  37.0 1.2 %collective-permute-start.12 = (bf16[64,256]{1,0:T(8,128)(2,1)S(1)}, bf16[64,256]{1,0:T(8,128)(2,1)S(1)}, u32[]{:S(2)}, u32[]{:S(2)}) collective-permute-start(bf16[64,256]{1,0:T(8,128)(2,1)S(1)} %get-tuple-element.63), channel_id=1, source_target_pairs={{0,1},{1,0},{4,8},{5,9},{8,4},{9,5},{12,13},{13,12},{2,3},{3,2},{6... | collective-permute-start | bytes 98312 | tf_op jit(solution)/shard_map/ppermute | solution.py:357
  41.0 3.5 %collective-permute-start.19 = (bf16[576,256]{1,0:T(8,128)(2,1)S(1)}, bf16[576,256]{1,0:T(8,128)(2,1)S(1)}, u32[]{:S(2)}, u32[]{:S(2)}) collective-permute-start(bf16[576,256]{1,0:T(8,128)(2,1)S(1)} %shard_map.77.mine_ref), channel_id=1, source_target_pairs={{0,1},{1,0},{2,3},{3,2},{4,5},{5,4},{6,7},{7,6},{8,9},{9,8},{10,11... | collective-permute-start | bytes 884744 | tf_op jit(solution)/shard_map/ppermute | solution.py:343
  41.1 4.5 %collective-permute-start.17 = (bf16[72,256]{1,0:T(8,128)(2,1)S(1)}, bf16[72,256]{1,0:T(8,128)(2,1)S(1)}, u32[]{:S(2)}, u32[]{:S(2)}) collective-permute-start(bf16[72,256]{1,0:T(8,128)(2,1)S(1)} %shard_map.76.refs_0_.mine_ref), channel_id=1, source_target_pairs={{0,2},{2,0},{1,3},{3,1},{4,6},{6,4},{5,7},{7,5},{8,10},{10,8},{9,1... | collective-permute-start | bytes 110600 | tf_op jit(solution)/shard_map/ppermute | solution.py:371
  42.3 3.4 %collective-permute-start.16 = (bf16[72,256]{1,0:T(8,128)(2,1)S(1)}, bf16[72,256]{1,0:T(8,128)(2,1)S(1)}, u32[]{:S(2)}, u32[]{:S(2)}) collective-permute-start(bf16[72,256]{1,0:T(8,128)(2,1)S(1)} %shard_map.76.refs_0_.mine_ref), channel_id=1, source_target_pairs={{0,3},{1,2},{2,1},{3,0},{4,7},{5,6},{6,5},{7,4},{8,11},{9,10},{10,... | collective-permute-start | bytes 110600 | tf_op jit(solution)/shard_map/ppermute | solution.py:377
  43.0 2.7 %collective-permute-start.15 = (bf16[72,256]{1,0:T(8,128)(2,1)S(1)}, bf16[72,256]{1,0:T(8,128)(2,1)S(1)}, u32[]{:S(2)}, u32[]{:S(2)}) collective-permute-start(bf16[72,256]{1,0:T(8,128)(2,1)S(1)} %shard_map.76.refs_0_.mine_ref), channel_id=1, source_target_pairs={{0,1},{1,0},{2,3},{3,2},{4,5},{5,4},{6,7},{7,6},{8,9},{9,8},{10,11... | collective-permute-start | bytes 110600 | tf_op jit(solution)/shard_map/ppermute | solution.py:343
